TPU v7x, 32 devices: a whole 2x2x4 slice. The times are simulated.
32 devices in a mesh: batch: 8 (over z, x), height: 4 (over y, core).
Axes of the slice: x: 2, y: 2, z: 4, core: 2. Of those that a mesh axis runs over, the one named last changes fastest.
Arguments:
- inputs: bfloat16 [16, 24, 32, 512], P('batch', 'height'), may hold values from -13 to 13
- bucket: int32 [16], P('batch'), may hold values from 0 to 2, as said below
- norm1_gain: float32 [512], replicated, may hold values from 0.1 to 1.9
- norm1_shift: float32 [512], replicated, may hold values from -3 to 3
- conv1_weight: bfloat16 [4608, 512], replicated, may hold values from -0.09375 to 0.09375
- conv1_bias: float32 [512], replicated, may hold values from -3 to 3
- norm2_gain: float32 [512], replicated, may hold values from 0.1 to 1.9
- norm2_shift: float32 [512], replicated, may hold values from -3 to 3
- conv2_weight: bfloat16 [4608, 512], replicated, may hold values from -0.09375 to 0.09375
- conv2_bias: float32 [512], replicated, may hold values from -3 to 3
- norm3_gain: float32 [512], replicated, may hold values from 0.1 to 1.9
- norm3_shift: float32 [512], replicated, may hold values from -3 to 3
- query_weight: bfloat16 [512, 512], replicated, may hold values from -0.375 to 0.375
- query_bias: float32 [512], replicated, may hold values from -3 to 3
- key_weight: bfloat16 [512, 512], replicated, may hold values from -0.375 to 0.375
- value_weight: bfloat16 [512, 512], replicated, may hold values from -0.25 to 0.25
- value_bias: float32 [512], replicated, may hold values from -3 to 3
- proj_weight: bfloat16 [512, 512], replicated, may hold values from -1 to 1
- proj_bias: float32 [512], replicated, may hold values from -1.75 to 1.75
- cotangent: bfloat16 [16, 24, 32, 512], P('batch', 'height'), may hold values from -6 to 6
Outputs:
- outputs: bfloat16 [16, 24, 32, 512], P('batch', 'height')
- input_grad: bfloat16 [16, 24, 32, 512], P('batch', 'height')
- grad_norm1_gain: float32 [512], P('batch')
- grad_norm1_shift: float32 [512], P('batch')
- grad_conv1_weight: float32 [4608, 512], P('batch')
- grad_conv1_bias: float32 [512], P('batch')
- grad_norm2_gain: float32 [512], P('batch')
- grad_norm2_shift: float32 [512], P('batch')
- grad_conv2_weight: float32 [4608, 512], P('batch')
- grad_conv2_bias: float32 [512], P('batch')
- grad_norm3_gain: float32 [512], P('batch')
- grad_norm3_shift: float32 [512], P('batch')
- grad_query_weight: float32 [512, 512], P('batch')
- grad_query_bias: float32 [512], P('batch')
- grad_key_weight: float32 [512, 512], P('batch')
- grad_value_weight: float32 [512, 512], P('batch')
- grad_value_bias: float32 [512], P('batch')
- grad_proj_weight: float32 [512, 512], P('batch')
- grad_proj_bias: float32 [512], P('batch')
Inputs may be any that keep to these rules, and one draw needn't show every extreme that they name: Among the 2 images on each index of batch, at least one is of bucket 1.
All inputs are finite; a program needn't handle non-finite values.
Results may differ from a plain program's by a relative error of at most 0.025.
Values may be sent and summed in bfloat16 or wider, within the bound.
No kernel may reach another device: no remote copies, remote signals or barrier semaphores. Data moves between devices by JAX's collectives and lax.ppermute only.
A program may use at most 128 MiB of HBM per device.

v0:
```python
import jax
import jax.numpy as jnp
from jax import lax
from jax.sharding import PartitionSpec as P

GROUPS = 32
UNIT = 8


epsilon = 1e-05


def with_halo(block, sides, width):
    for axis, dim in sides:
        count = lax.axis_size(axis)
        forward = [(i, i + 1) for i in range(count - 1)]
        backward = [(target, source) for source, target in forward]
        low = lax.ppermute(
            lax.slice_in_dim(block, block.shape[dim] - width, None, axis=dim), axis, forward
        )
        high = lax.ppermute(lax.slice_in_dim(block, 0, width, axis=dim), axis, backward)
        block = jnp.concatenate([low, block, high], axis=dim)
    return block


def shortened(x):

    def short(part):
        return part.astype(jnp.bfloat16) if part.dtype == jnp.float32 else part

    return jax.tree.map(short, x)


def pixel_inside(bucket, first_row, row_count, col_count):
    heights = jnp.where(bucket == 1, 3 * UNIT, 2 * UNIT)
    widths = jnp.where(bucket == 0, 3 * UNIT, jnp.where(bucket == 1, 2 * UNIT, 4 * UNIT))
    row_ids = first_row + lax.broadcasted_iota(jnp.int32, (1, row_count, 1), 1)
    col_ids = lax.broadcasted_iota(jnp.int32, (1, 1, col_count), 2)
    inside = (row_ids < heights[:, None, None]) & (col_ids < widths[:, None, None])
    return (inside.astype(jnp.float32), (heights * widths).astype(jnp.float32))


def group_sums(values, inside4):
    images, row_count, col_count, channels = values.shape
    grouped = (values * inside4).reshape(images, row_count * col_count, GROUPS, channels // GROUPS)
    return jnp.sum(grouped, axis=(1, 3))


def spread_out(statistic, channels):
    return jnp.repeat(statistic, channels // GROUPS, axis=1)[:, None, None, :]


def norm_forward(values, inside4, group_size, norm_gain, norm_shift):
    channels = values.shape[-1]
    mean_value = lax.psum(group_sums(values, inside4), "height") / group_size
    centered = values - spread_out(mean_value, channels)
    variance = lax.psum(group_sums(centered * centered, inside4), "height") / group_size
    inverse = lax.rsqrt(variance + epsilon)
    normal = centered * spread_out(inverse, channels)
    return (normal * norm_gain + norm_shift, normal, inverse)


def norm_backward(grad_out, normal, inverse, inside4, group_size, norm_gain):
    channels = grad_out.shape[-1]
    scaled = grad_out * norm_gain
    plain_sum, cross_sum = lax.psum(
        (group_sums(scaled, inside4), group_sums(scaled * normal, inside4)), "height"
    )
    correction = spread_out(plain_sum / group_size, channels) + normal * spread_out(
        cross_sum / group_size, channels
    )
    grad_in = spread_out(inverse, channels) * (scaled - inside4 * correction)
    return (grad_in, jnp.sum(grad_out * normal, axis=(0, 1, 2)), jnp.sum(grad_out, axis=(0, 1, 2)))


def conv_apply(activation, weight):
    images, row_count, col_count, channels = activation.shape
    padded = with_halo(activation, (("height", 1),), 1)
    padded = jnp.pad(padded, ((0, 0), (0, 0), (1, 1), (0, 0)))
    stacked = jnp.concatenate(
        [
            padded[:, row_step : row_step + row_count, col_step : col_step + col_count, :]
            for row_step in range(3)
            for col_step in range(3)
        ],
        axis=-1,
    )
    result = jnp.einsum("ihwk,kc->ihwc", stacked, weight, preferred_element_type=jnp.float32)
    return (result, stacked)


def flipped(weight):
    channels = weight.shape[1]
    turned = weight.reshape(3, 3, channels, channels)[::-1, ::-1]
    return jnp.transpose(turned, (0, 1, 3, 2)).reshape(9 * channels, channels)


def silu_slope(preact):
    sigmoid_value = jax.nn.sigmoid(preact)
    return sigmoid_value * (1.0 + preact * (1.0 - sigmoid_value))


def residual_block(start_act, inside4, group_size, params):
    (
        norm1_gain,
        norm1_shift,
        conv1_weight,
        conv1_bias,
        norm2_gain,
        norm2_shift,
        conv2_weight,
        conv2_bias,
    ) = params
    normed1, normal1, inverse1 = norm_forward(
        start_act, inside4, group_size, norm1_gain, norm1_shift
    )
    first_act = (inside4 * jax.nn.silu(normed1)).astype(jnp.bfloat16)
    first_conv, first_stack = conv_apply(first_act, conv1_weight)
    first_conv = first_conv + conv1_bias
    normed2, normal2, inverse2 = norm_forward(
        first_conv, inside4, group_size, norm2_gain, norm2_shift
    )
    second_act = (inside4 * jax.nn.silu(normed2)).astype(jnp.bfloat16)
    second_conv, second_stack = conv_apply(second_act, conv2_weight)
    middle = inside4 * (start_act + (second_conv + conv2_bias))
    return (
        middle,
        (normed1, normal1, inverse1, first_stack, normed2, normal2, inverse2, second_stack),
    )


def on_device(
    inputs,
    bucket,
    norm1_gain,
    norm1_shift,
    conv1_weight,
    conv1_bias,
    norm2_gain,
    norm2_shift,
    conv2_weight,
    conv2_bias,
    norm3_gain,
    norm3_shift,
    query_weight,
    query_bias,
    key_weight,
    value_weight,
    value_bias,
    proj_weight,
    proj_bias,
    cotangent,
):
    images, row_count, col_count, channels = inputs.shape
    height_parts = lax.axis_size("height")
    inside, area_size = pixel_inside(
        bucket, lax.axis_index("height") * row_count, row_count, col_count
    )
    whole_inside, unused = pixel_inside(bucket, 0, row_count * height_parts, col_count)
    inside4 = inside[..., None]
    group_size = area_size[:, None] * (channels // GROUPS)
    start_act = inside4 * inputs.astype(jnp.float32)
    first_params = (
        norm1_gain,
        norm1_shift,
        conv1_weight,
        conv1_bias,
        norm2_gain,
        norm2_shift,
        conv2_weight,
        conv2_bias,
    )
    middle = residual_block(start_act, inside4, group_size, first_params)[0]
    local_rows = row_count * col_count
    scaling = channels ** (-0.5)
    normed3, normal3, inverse3 = norm_forward(middle, inside4, group_size, norm3_gain, norm3_shift)
    flat_rows = normed3.astype(jnp.bfloat16).reshape(images, local_rows, channels)
    queries = (
        jnp.einsum("ipc,cd->ipd", flat_rows, query_weight, preferred_element_type=jnp.float32)
        + query_bias
    ).astype(jnp.bfloat16)
    key_rows = jnp.einsum(
        "ipc,cd->ipd", flat_rows, key_weight, preferred_element_type=jnp.float32
    ).astype(jnp.bfloat16)
    values = (
        jnp.einsum("ipc,cd->ipd", flat_rows, value_weight, preferred_element_type=jnp.float32)
        + value_bias
    ).astype(jnp.bfloat16)
    all_keys, all_values = (
        lax.all_gather(key_rows, "height", axis=1, tiled=True),
        lax.all_gather(values, "height", axis=1, tiled=True),
    )
    key_valid = whole_inside.reshape(images, 1, local_rows * height_parts) > 0.5

    def score_block(query_block):
        raw_scores = (
            jnp.einsum("iqc,ikc->iqk", query_block, all_keys, preferred_element_type=jnp.float32)
            * scaling
        )
        return jnp.where(key_valid, raw_scores, -1000000000.0)

    scores = score_block(queries)
    highest_score = jnp.max(scores, axis=-1, keepdims=True)
    raised = jnp.exp(scores - highest_score)
    row_total = jnp.sum(raised, axis=-1, keepdims=True)
    log_total = highest_score + jnp.log(row_total)
    soft_weights = (raised / row_total).astype(jnp.bfloat16)
    mixed_rows = jnp.einsum(
        "iqk,ikc->iqc", soft_weights, all_values, preferred_element_type=jnp.float32
    ).astype(jnp.bfloat16)
    projected = (
        jnp.einsum("iqc,cd->iqd", mixed_rows, proj_weight, preferred_element_type=jnp.float32)
        + proj_bias
    )
    outputs = (inside4 * (middle + projected.reshape(inputs.shape))).astype(jnp.bfloat16)
    grad_top = inside4 * cotangent.astype(jnp.float32)
    grad_rows = grad_top.astype(jnp.bfloat16).reshape(images, local_rows, channels)
    proj_weight_grad = jnp.einsum(
        "iqc,iqd->cd", mixed_rows, grad_rows, preferred_element_type=jnp.float32
    )
    proj_bias_grad = jnp.sum(grad_top, axis=(0, 1, 2))
    grad_mixed = jnp.einsum(
        "iqd,cd->iqc", grad_rows, proj_weight, preferred_element_type=jnp.float32
    ).astype(jnp.bfloat16)
    soft_again = jnp.exp(score_block(queries) - log_total)
    grad_soft = jnp.einsum(
        "iqc,ikc->iqk", grad_mixed, all_values, preferred_element_type=jnp.float32
    )
    value_part = jnp.einsum(
        "iqk,iqc->ikc",
        soft_again.astype(jnp.bfloat16),
        grad_mixed,
        preferred_element_type=jnp.float32,
    )
    grad_scores = soft_again * (grad_soft - jnp.sum(soft_again * grad_soft, axis=-1, keepdims=True))
    grad_scores = grad_scores.astype(jnp.bfloat16)
    grad_queries = (
        jnp.einsum("iqk,ikc->iqc", grad_scores, all_keys, preferred_element_type=jnp.float32)
        * scaling
    ).astype(jnp.bfloat16)
    key_part = (
        jnp.einsum("iqk,iqc->ikc", grad_scores, queries, preferred_element_type=jnp.float32)
        * scaling
    )
    key_sum, value_sum = (
        lax.psum_scatter(
            key_part.astype(jnp.bfloat16), "height", scatter_dimension=1, tiled=True
        ).astype(jnp.float32),
        lax.psum_scatter(
            value_part.astype(jnp.bfloat16), "height", scatter_dimension=1, tiled=True
        ).astype(jnp.float32),
    )
    grad_keys = key_sum.astype(jnp.bfloat16)
    grad_values = value_sum.astype(jnp.bfloat16)
    query_weight_grad = jnp.einsum(
        "ipc,ipd->cd", flat_rows, grad_queries, preferred_element_type=jnp.float32
    )
    query_bias_grad = jnp.sum(grad_queries.astype(jnp.float32), axis=(0, 1))
    key_weight_grad = jnp.einsum(
        "ipc,ipd->cd", flat_rows, grad_keys, preferred_element_type=jnp.float32
    )
    value_weight_grad = jnp.einsum(
        "ipc,ipd->cd", flat_rows, grad_values, preferred_element_type=jnp.float32
    )
    value_bias_grad = jnp.sum(grad_values.astype(jnp.float32), axis=(0, 1))
    grad_flat = (
        jnp.einsum("ipd,cd->ipc", grad_queries, query_weight, preferred_element_type=jnp.float32)
        + jnp.einsum("ipd,cd->ipc", grad_keys, key_weight, preferred_element_type=jnp.float32)
        + jnp.einsum("ipd,cd->ipc", grad_values, value_weight, preferred_element_type=jnp.float32)
    )
    grad_normed, norm3_gain_grad, norm3_shift_grad = norm_backward(
        grad_flat.reshape(inputs.shape), normal3, inverse3, inside4, group_size, norm3_gain
    )
    grad_middle = inside4 * (grad_top + grad_normed)
    record = residual_block(start_act, inside4, group_size, first_params)[1]
    normed1, normal1, inverse1, first_stack, normed2, normal2, inverse2, second_stack = record
    grad_second = grad_middle.astype(jnp.bfloat16)
    conv2_weight_grad = jnp.einsum(
        "ihwk,ihwc->kc", second_stack, grad_second, preferred_element_type=jnp.float32
    )
    conv2_bias_grad = jnp.sum(grad_second.astype(jnp.float32), axis=(0, 1, 2))
    grad_act2 = conv_apply(grad_second, flipped(conv2_weight))[0]
    grad_first, norm2_gain_grad, norm2_shift_grad = norm_backward(
        inside4 * grad_act2 * silu_slope(normed2),
        normal2,
        inverse2,
        inside4,
        group_size,
        norm2_gain,
    )
    grad_first = grad_first.astype(jnp.bfloat16)
    conv1_weight_grad = jnp.einsum(
        "ihwk,ihwc->kc", first_stack, grad_first, preferred_element_type=jnp.float32
    )
    conv1_bias_grad = jnp.sum(grad_first.astype(jnp.float32), axis=(0, 1, 2))
    grad_act1 = conv_apply(grad_first, flipped(conv1_weight))[0]
    grad_start, norm1_gain_grad, norm1_shift_grad = norm_backward(
        inside4 * grad_act1 * silu_slope(normed1),
        normal1,
        inverse1,
        inside4,
        group_size,
        norm1_gain,
    )
    input_grad = (inside4 * (grad_middle + grad_start)).astype(jnp.bfloat16)
    slices = (
        lax.psum_scatter(norm1_gain_grad, "batch", scatter_dimension=0, tiled=True),
        lax.psum_scatter(norm1_shift_grad, "batch", scatter_dimension=0, tiled=True),
        lax.psum_scatter(conv1_weight_grad, "batch", scatter_dimension=0, tiled=True),
        lax.psum_scatter(conv1_bias_grad, "batch", scatter_dimension=0, tiled=True),
        lax.psum_scatter(norm2_gain_grad, "batch", scatter_dimension=0, tiled=True),
        lax.psum_scatter(norm2_shift_grad, "batch", scatter_dimension=0, tiled=True),
        lax.psum_scatter(conv2_weight_grad, "batch", scatter_dimension=0, tiled=True),
        lax.psum_scatter(conv2_bias_grad, "batch", scatter_dimension=0, tiled=True),
        lax.psum_scatter(norm3_gain_grad, "batch", scatter_dimension=0, tiled=True),
        lax.psum_scatter(norm3_shift_grad, "batch", scatter_dimension=0, tiled=True),
        lax.psum_scatter(query_weight_grad, "batch", scatter_dimension=0, tiled=True),
        lax.psum_scatter(query_bias_grad, "batch", scatter_dimension=0, tiled=True),
        lax.psum_scatter(key_weight_grad, "batch", scatter_dimension=0, tiled=True),
        lax.psum_scatter(value_weight_grad, "batch", scatter_dimension=0, tiled=True),
        lax.psum_scatter(value_bias_grad, "batch", scatter_dimension=0, tiled=True),
        lax.psum_scatter(proj_weight_grad, "batch", scatter_dimension=0, tiled=True),
        lax.psum_scatter(proj_bias_grad, "batch", scatter_dimension=0, tiled=True),
    )
    summed = jax.tree.map(
        lambda part: part.astype(jnp.float32), lax.psum(shortened(tuple(slices)), "height")
    )
    return (outputs, input_grad) + tuple(summed)


def solution(mesh):
    placed = (
        P("batch", "height", None, None),
        P("batch"),
        P(),
        P(),
        P(),
        P(),
        P(),
        P(),
        P(),
        P(),
        P(),
        P(),
        P(),
        P(),
        P(),
        P(),
        P(),
        P(),
        P(),
        P("batch", "height", None, None),
    )
    return jax.shard_map(
        on_device,
        mesh=mesh,
        in_specs=placed,
        out_specs=(
            P("batch", "height", None, None),
            P("batch", "height", None, None),
            P("batch"),
            P("batch"),
            P("batch", None),
            P("batch"),
            P("batch"),
            P("batch"),
            P("batch", None),
            P("batch"),
            P("batch"),
            P("batch"),
            P("batch", None),
            P("batch"),
            P("batch", None),
            P("batch", None),
            P("batch"),
            P("batch", None),
            P("batch"),
        ),
        check_vma=False,
    )
```

profile of v0, /device:TPU:0, one launch (start us, length us, event | category | flops | bytes accessed | tf_op | source)
XLA Modules:
  0.0 869.7 jit_solution(8951114740814492323)
XLA Ops:
  10.3 8.3 psum.215
  20.3 5.7 psum.216
  27.7 1.7 collective-permute-start
  30.7 2.0 collective-permute-done.1
  35.2 2.0 multiply_reduce_fusion.13
  37.4 8.6 psum.217
  46.7 5.6 psum.218
  52.9 1.8 collective-permute-start.2
  56.0 3.3 collective-permute-done.3
  60.4 5.7 multiply_reduce_fusion.11
  66.3 8.6 psum.219
  75.5 5.6 psum.220
  84.2 2.2 convolution_convert_fusion.1
  86.4 2.2 fusion.22
  88.6 15.5 %all-gather.3.cloned.1.call-done = bf16[2,768,512]{2,1,0:T(8,128)(2,1)} async-done(((bf16[2,192,512]{2,1,0:T(8,128)(2,1)}), bf16[2,768,512]{2,1,0:T(8,128)(2,1)}) %all-gather.3.cloned.1.call-update) | async-done | bytes 1572880 | tf_op jit(solution)/shard_map/all_gather | solution.py:190
  104.1 2.3 fusion.66
  106.8 1.9 convolution_convert_fusion
  108.8 17.1 %all-gather.5.cloned.1.call-done = bf16[2,768,512]{2,1,0:T(8,128)(2,1)} async-done(((bf16[2,192,512]{2,1,0:T(8,128)(2,1)}), bf16[2,768,512]{2,1,0:T(8,128)(2,1)}) %all-gather.5.cloned.1.call-update) | async-done | bytes 1572880 | tf_op jit(solution)/shard_map/all_gather | solution.py:191
  125.9 2.4 multiply_reduce_fusion
  129.4 1.8 multiply_convert_fusion
  131.5 2.0 convolution_convert_fusion.2
  135.8 2.2 convert_reduce_fusion.1
  139.5 17.1 %reduce-scatter.11.cloned.1.call-done = bf16[2,192,512]{2,1,0:T(8,128)(2,1)} async-done(((bf16[2,768,512]{2,1,0:T(8,128)(2,1)}), bf16[2,192,512]{2,1,0:T(8,128)(2,1)}) %reduce-scatter.11.cloned.1.call-update) | async-done | bytes 393232 | tf_op jit(solution)/shard_map/reduce_scatter | solution.py:249
  156.6 2.4 convolution_bitcast_fusion.3
  159.2 2.4 fusion.46
  161.6 25.8 %reduce-scatter.9.cloned.1.call-done = bf16[2,192,512]{2,1,0:T(8,128)(2,1)} async-done(((bf16[2,768,512]{2,1,0:T(8,128)(2,1)}), bf16[2,192,512]{2,1,0:T(8,128)(2,1)}) %reduce-scatter.9.cloned.1.call-update) | async-done | bytes 393232 | tf_op jit(solution)/shard_map/reduce_scatter | solution.py:246
  187.4 2.4 convolution_bitcast_fusion.4
  189.9 1.8 convolution_add_fusion.1
  192.8 5.7 all-reduce.18
  200.3 7.2 convolution_bitcast_fusion
  207.6 1.7 collective-permute-start.4
  210.6 4.9 reverse_bitcast_fusion.1
  215.5 6.7 copy.51
  223.0 1.7 copy-done.7
  224.8 3.4 multiply_reduce_fusion.2
  228.5 8.3 all-reduce.17
  238.6 7.1 convolution_bitcast_fusion.1
  245.8 4.9 reverse_bitcast_fusion
  250.7 6.7 copy.52
  258.7 2.3 convolution_add_fusion.2
  261.0 1.5 convert_element_type.275
  262.5 58.4 %reduce-scatter.17.cloned.1.call-done = f32[64,512]{1,0:T(8,128)} async-done(((f32[512,512]{1,0:T(8,128)}), f32[64,512]{1,0:T(8,128)}) %reduce-scatter.17.cloned.1.call-update) | async-done | bytes 131088 | tf_op jit(solution)/shard_map/reduce_scatter | solution.py:317
  320.9 1.5 convert_element_type.263
  323.8 1.5 collective-permute-start.7
  325.4 3.2 collective-permute-done.7
  336.4 50.4 %reduce-scatter.21.cloned.1.call-done = f32[64,512]{1,0:T(8,128)} async-done(((f32[512,512]{1,0:T(8,128)}), f32[64,512]{1,0:T(8,128)}) %reduce-scatter.21.cloned.1.call-update) | async-done | bytes 131088 | tf_op jit(solution)/shard_map/reduce_scatter | solution.py:320
  386.9 1.5 convert_element_type.270
  388.4 65.4 %reduce-scatter.19.cloned.1.call-done = f32[64,512]{1,0:T(8,128)} async-done(((f32[512,512]{1,0:T(8,128)}), f32[64,512]{1,0:T(8,128)}) %reduce-scatter.19.cloned.1.call-update) | async-done | bytes 131088 | tf_op jit(solution)/shard_map/reduce_scatter | solution.py:319
  453.8 1.5 convert_element_type.268
  455.4 164.4 %reduce-scatter.15.cloned.1.call-done = f32[576,512]{1,0:T(8,128)} async-done(((f32[4608,512]{1,0:T(8,128)}), f32[576,512]{1,0:T(8,128)}) %reduce-scatter.15.cloned.1.call-update) | async-done | bytes 1179664 | tf_op jit(solution)/shard_map/reduce_scatter | solution.py:313
  619.8 2.2 convert_element_type.254
  622.0 163.9 %reduce-scatter.13.cloned.1.call-done = f32[576,512]{1,0:T(8,128)} async-done(((f32[4608,512]{1,0:T(8,128)}), f32[576,512]{1,0:T(8,128)}) %reduce-scatter.13.cloned.1.call-update) | async-done | bytes 1179664 | tf_op jit(solution)/shard_map/reduce_scatter | solution.py:309
  785.8 2.2 convert_element_type.245
  788.0 6.8 multiply_reduce_fusion.3
  794.9 35.2 %all-reduce.15 = (bf16[512]{0:T(512)(128)(2,1)S(1)}, bf16[512]{0:T(512)(128)(2,1)S(1)}, bf16[512]{0:T(512)(128)(2,1)S(1)}, bf16[512]{0:T(512)(128)(2,1)S(1)}, bf...) all-reduce(f32[512]{0:T(512)S(1)} %get-tuple-element.23, ...), channel_id=4, replica_groups=mesh['batch'=8,'height'=4] {'batch'}, use_global_device_ids=true, to_apply=%region_42.43.clone | all-reduce | flops 5632 | bytes 33792
  830.9 5.7 all-reduce.19
  842.7 6.5 all-reduce.16
  849.6 3.1 multiply_convert_fusion.2
  852.7 1.5 convert_element_type.264
  854.2 1.5 convert_element_type.269
  855.7 1.5 convert_element_type.271
  857.2 1.5 convert_element_type.276
  858.7 2.2 convert_element_type.246
  861.0 2.2 convert_element_type.255
  (251 shorter events, 47.5 us)
Async XLA Ops:
  7.2 75.6 %copy-start = (bf16[512,512]{1,0:T(8,128)(2,1)S(1)}, bf16[512,512]{1,0:T(8,128)(2,1)}, u32[]{:S(2)}) copy-start(bf16[512,512]{1,0:T(8,128)(2,1)} %param.35) | copy-start | bytes 1572868
  7.2 25.9 %copy-start.4 = (bf16[2,6,32,512]{3,2,1,0:T(8,128)(2,1)S(1)}, bf16[2,6,32,512]{3,2,1,0:T(8,128)(2,1)}, u32[]{:S(2)}) copy-start(bf16[2,6,32,512]{3,2,1,0:T(8,128)(2,1)} %param.20) | copy-start | bytes 1179652
  7.2 25.9 %copy-start.22 = (f32[512]{0:T(512)S(1)}, f32[512]{0:T(512)}, u32[]{:S(2)}) copy-start(f32[512]{0:T(512)} %param.22) | copy-start | bytes 6148
  7.2 25.9 %copy-start.25 = (f32[512]{0:T(512)S(1)}, f32[512]{0:T(512)}, u32[]{:S(2)}) copy-start(f32[512]{0:T(512)} %param.23) | copy-start | bytes 6148
  7.2 96.8 %all-gather.3.cloned.1.call-start = ((), (), s32[]{:S(2)}) async-start(), calls=%async_computation.8 | async-start | bytes 1966080 | tf_op jit(solution)/shard_map/all_gather | solution.py:190
  27.7 3.0 collective-permute-start
  29.4 3.3 collective-permute-start.1
  32.9 2.3 copy-start.6
  32.9 2.3 copy-start.28
  35.2 2.0 copy-start.20
  35.2 11.0 %copy-start.12 = (bf16[2,6,32,512]{3,2,1,0:T(8,128)(2,1)S(1)}, bf16[2,6,32,512]{3,2,1,0:T(8,128)(2,1)}, u32[]{:S(2)}) copy-start(bf16[2,6,32,512]{3,2,1,0:T(8,128)(2,1)} %param.39) | copy-start | bytes 1179652
  35.2 17.3 %copy-start.23 = (f32[512]{0:T(512)S(1)}, f32[512]{0:T(512)}, u32[]{:S(2)}) copy-start(f32[512]{0:T(512)} %param.26) | copy-start | bytes 6148
  35.2 17.3 %copy-start.24 = (f32[512]{0:T(512)S(1)}, f32[512]{0:T(512)}, u32[]{:S(2)}) copy-start(f32[512]{0:T(512)} %param.27) | copy-start | bytes 6148
  46.5 37.7 %copy-start.8 = (bf16[2,6,32,512]{3,2,1,0:T(8,128)(2,1)}, bf16[2,6,32,512]{3,2,1,0:T(8,128)(2,1)S(1)}, u32[]{:S(2)}) copy-start(bf16[2,6,32,512]{3,2,1,0:T(8,128)(2,1)S(1)} %get-tuple-element.80) | copy-start | bytes 1179652
  52.9 3.1 collective-permute-start.2
  54.7 4.6 collective-permute-start.3
  59.6 0.8 copy-start.29
  60.4 5.7 copy-start.21
  60.4 21.0 %copy-start.19 = (f32[512]{0:T(512)S(1)}, f32[512]{0:T(512)}, u32[]{:S(2)}) copy-start(f32[512]{0:T(512)} %param.30) | copy-start | bytes 6148
  60.4 21.0 %copy-start.26 = (f32[512]{0:T(512)S(1)}, f32[512]{0:T(512)}, u32[]{:S(2)}) copy-start(f32[512]{0:T(512)} %param.31) | copy-start | bytes 6148
  60.4 21.1 %copy-start.15 = (bf16[512,512]{1,0:T(8,128)(2,1)S(1)}, bf16[512,512]{1,0:T(8,128)(2,1)}, u32[]{:S(2)}) copy-start(bf16[512,512]{1,0:T(8,128)(2,1)} %param.34) | copy-start | bytes 1572868
  66.1 16.6 %copy-start.30 = (f32[512]{0:T(512)S(1)}, f32[512]{0:T(512)}, u32[]{:S(2)}) copy-start(f32[512]{0:T(512)} %param.36) | copy-start | bytes 6148
  75.1 11.3 %copy-start.31 = (f32[512]{0:T(512)S(1)}, f32[512]{0:T(512)}, u32[]{:S(2)}) copy-start(f32[512]{0:T(512)} %param.33) | copy-start | bytes 6148
  81.5 7.0 copy-start.2
  82.7 43.2 %all-gather.5.cloned.1.call-start = ((), (), s32[]{:S(2)}) async-start(), calls=%async_computation.9 | async-start | bytes 1966080 | tf_op jit(solution)/shard_map/all_gather | solution.py:191
  83.9 72.7 %reduce-scatter.11.cloned.1.call-start = ((), (), s32[]{:S(2)}) async-start(), calls=%async_computation.11 | async-start | bytes 1966080 | tf_op jit(solution)/shard_map/reduce_scatter | solution.py:249
  104.1 2.7 copy-start.11
  108.7 78.7 %reduce-scatter.9.cloned.1.call-start = ((), (), s32[]{:S(2)}) async-start(), calls=%async_computation.10 | async-start | bytes 1966080 | tf_op jit(solution)/shard_map/reduce_scatter | solution.py:246
  125.9 3.5 copy-start.18
  128.6 0.8 copy-start.14
  131.3 129.7 %reduce-scatter.23.cloned.1.call-start = ((), (), s32[]{:S(2)}) async-start(), calls=%async_computation.17 | async-start | bytes 1179648 | tf_op jit(solution)/shard_map/reduce_scatter | solution.py:322
  131.5 2.8 copy-start.9
  133.5 0.7 copy-start.17
  134.3 3.7 copy-start.3
  135.7 185.2 %reduce-scatter.17.cloned.1.call-start = ((), (), s32[]{:S(2)}) async-start(), calls=%async_computation.14 | async-start | bytes 1179648 | tf_op jit(solution)/shard_map/reduce_scatter | solution.py:317
  139.5 247.4 %reduce-scatter.21.cloned.1.call-start = ((), (), s32[]{:S(2)}) async-start(), calls=%async_computation.16 | async-start | bytes 1179648 | tf_op jit(solution)/shard_map/reduce_scatter | solution.py:320
  159.1 294.7 %reduce-scatter.19.cloned.1.call-start = ((), (), s32[]{:S(2)}) async-start(), calls=%async_computation.15 | async-start | bytes 1179648 | tf_op jit(solution)/shard_map/reduce_scatter | solution.py:319
  159.2 32.5 %copy-start.10 = (bf16[2,192,512]{2,1,0:T(8,128)(2,1)S(1)}, bf16[2,192,512]{2,1,0:T(8,128)(2,1)}, u32[]{:S(2)}) copy-start(bf16[2,192,512]{2,1,0:T(8,128)(2,1)} %reduce-scatter.11.cloned.1.call-done) | copy-start | bytes 1179652
  189.8 430.0 %reduce-scatter.15.cloned.1.call-start = ((), (), s32[]{:S(2)}) async-start(), calls=%async_computation.13 | async-start | bytes 10616832 | tf_op jit(solution)/shard_map/reduce_scatter | solution.py:313
  207.6 578.3 %reduce-scatter.13.cloned.1.call-start = ((), (), s32[]{:S(2)}) async-start(), calls=%async_computation.12 | async-start | bytes 10616832 | tf_op jit(solution)/shard_map/reduce_scatter | solution.py:309
  207.6 14.6 %collective-permute-start.4 = (bf16[2,1,32,512]{3,2,1,0:T(8,128)(2,1)S(1)}, bf16[2,1,32,512]{3,2,1,0:T(8,128)(2,1)S(1)}, u32[]{:S(2)}, u32[]{:S(2)}) collective-permute-start(bf16[2,1,32,512]{3,2,1,0:T(8,128)(2,1)S(1)} %get-tuple-element.74), channel_id=1, source_target_pairs={{0,1},{1,2},{2,3},{4,5},{5,6},{6,7},{8,9},{9,10},{10,11},{12,13},{... | collective-permute-start | bytes 196616 | tf_op jit(solution)/shard_map/ppermute | solution.py:18
  209.3 12.9 %collective-permute-start.5 = (bf16[2,1,32,512]{3,2,1,0:T(8,128)(2,1)S(1)}, bf16[2,1,32,512]{3,2,1,0:T(8,128)(2,1)S(1)}, u32[]{:S(2)}, u32[]{:S(2)}) collective-permute-start(bf16[2,1,32,512]{3,2,1,0:T(8,128)(2,1)S(1)} %get-tuple-element.75), channel_id=1, source_target_pairs={{1,0},{2,1},{3,2},{5,4},{6,5},{7,6},{9,8},{10,9},{11,10},{13,12},{... | collective-permute-start | bytes 196616 | tf_op jit(solution)/shard_map/ppermute | solution.py:21
  222.4 2.3 copy-start.7
  245.7 607.0 %all-reduce.23.cloned.1.call-start = ((), (), s32[]{:S(2)}) async-start(), calls=%async_computation.18 | async-start | bytes 2883584 | tf_op jit(solution)/shard_map/psum | solution.py:326
  250.7 6.7 copy-start.32
  250.7 8.0 copy-start.16
  250.7 8.0 copy-start.27
  322.5 2.9 collective-permute-start.6
  323.8 4.8 collective-permute-start.7
  334.8 453.3 %copy-start.5 = (bf16[2,6,32,512]{3,2,1,0:T(8,128)(2,1)S(1)}, bf16[2,6,32,512]{3,2,1,0:T(8,128)(2,1)}, u32[]{:S(2)}) copy-start(bf16[2,6,32,512]{3,2,1,0:T(8,128)(2,1)} %param.20) | copy-start | bytes 1179652
  334.8 453.3 %copy-start.13 = (bf16[2,6,32,512]{3,2,1,0:T(8,128)(2,1)S(1)}, bf16[2,6,32,512]{3,2,1,0:T(8,128)(2,1)}, u32[]{:S(2)}) copy-start(bf16[2,6,32,512]{3,2,1,0:T(8,128)(2,1)} %param.39) | copy-start | bytes 1179652
  849.6 13.6 %copy-start.1 = (bf16[512,512]{1,0:T(8,128)(2,1)S(1)}, bf16[512,512]{1,0:T(8,128)(2,1)}, u32[]{:S(2)}) copy-start(bf16[512,512]{1,0:T(8,128)(2,1)} %param.35) | copy-start | bytes 1572868
Sparse Core Ops, SparseCore 0:
  82.8 21.2 all-gather.2
  106.2 19.6 all-gather.4
  128.4 28.1 reduce-scatter.10
  159.2 28.1 reduce-scatter.8
  190.6 63.5 reduce-scatter.22
  258.4 62.4 reduce-scatter.16
  324.3 62.4 reduce-scatter.20
  391.2 62.5 reduce-scatter.18
  457.4 162.3 reduce-scatter.14
  623.2 162.5 reduce-scatter.12
  790.3 40.8 all-reduce.22
where the time goes:
time: 872 us; the launch traced here: 870 us
  waiting for transfers between devices  587 us (67%)
  blocking collectives  104 us (12%)
  matrix products  66.1 us (8%)
  other arithmetic  45 us (5%)
  local copies, waits for them, and re-layouts  39.9 us (5%)
  between operations  15.4 us (2%)
  starting transfers between devices  12.4 us (1%)
    reduce_scatter x1, waiting for transfers between devices, on_device(): lax.psum_scatter(conv2_weight_grad, 'batch', scatter_dimension=0, tiled=T...  164 us
    reduce_scatter x1, waiting for transfers between devices, on_device(): lax.psum_scatter(conv1_weight_grad, 'batch', scatter_dimension=0, tiled=T...  164 us
    reduce_scatter x1, waiting for transfers between devices, on_device(): lax.psum_scatter(key_weight_grad, 'batch', scatter_dimension=0, tiled=True)  65.4 us
    reduce_scatter x1, waiting for transfers between devices, on_device(): lax.psum_scatter(query_weight_grad, 'batch', scatter_dimension=0, tiled=T...  58.4 us
    reduce_scatter x1, waiting for transfers between devices, on_device(): lax.psum_scatter(value_weight_grad, 'batch', scatter_dimension=0, tiled=T...  50.4 us
    unnamed x1, blocking collectives  35.2 us
    reduce_scatter x1, waiting for transfers between devices, on_device(): lax.psum_scatter(key_part.astype(jnp.bfloat16), 'height', scatter_dimensi...  25.8 us
    psum x3, blocking collectives, norm_forward(): mean_value = lax.psum(group_sums(values, inside4), 'height') / group_size  25.5 us
  transfers between devices with their start and end apart: 19, of which 12 were waited for; matrix products, arithmetic and copies ran while one was open for 13% of the time, Pallas kernels for 0%

commit v1 on v0

v1 whole, which is shorter than its diff:
```python
import functools

import jax
import jax.numpy as jnp
from jax import lax
from jax.experimental import pallas as pl
from jax.experimental.pallas import tpu as pltpu
from jax.sharding import PartitionSpec as P

GROUPS = 32
UNIT = 8
PIX = 512
PAD = 32
BLK = 128
F32 = jnp.float32
BF16 = jnp.bfloat16
epsilon = 1e-05

VM = pl.BlockSpec(memory_space=pltpu.VMEM)
SM = pl.BlockSpec(memory_space=pltpu.SMEM)


def place(bucket_ref):
    h = lax.axis_index("height")
    upper = lax.div(h, 2)
    tall_first = bucket_ref[0] == 1
    tall_image = jnp.where(tall_first, 0, 1)
    home = jnp.where(upper == 1, tall_image, 1 - tall_image)
    away = 1 - home

    def facts(image):
        kind = bucket_ref[image]
        tall = kind == 1
        stride = jnp.where(tall, 2 * UNIT, 4 * UNIT)
        width = jnp.where(kind == 0, 3 * UNIT, stride)
        return (image, tall, stride, width)

    return h, facts(home), facts(away)


def pixel_col(stride, lanes=1):
    rows = lax.broadcasted_iota(jnp.int32, (PIX, lanes), 0)
    return rows, rows & (stride - 1)


def pixel_mask(facts):
    unused, tall, stride, width = facts
    rows, cols = pixel_col(stride)
    limit = jnp.where(tall, 6 * UNIT * UNIT, 8 * UNIT * UNIT)
    mask = jnp.where((cols < width) & (rows < limit), 1.0, 0.0).astype(F32)
    size = jnp.where(tall | (width == 3 * UNIT), 6 * UNIT * UNIT, 8 * UNIT * UNIT)
    return mask, size.astype(F32)


def group_total(row):
    channels = row.shape[-1]
    lane = lax.broadcasted_iota(jnp.int32, row.shape, 1)
    step = 1
    while step < channels // GROUPS:
        up = pltpu.roll(row, channels - step, 1)
        down = pltpu.roll(row, step, 1)
        row = row + jnp.where((lane & step) == 0, up, down)
        step *= 2
    return row


def total(values):
    return jnp.sum(values, axis=0, keepdims=True)


def wide_total(row):
    return group_total(jnp.broadcast_to(row, (8, row.shape[-1])))[0:1]


def norm_stats(values, mask, group_size):
    mean = wide_total(total(values * mask)) / group_size
    centered = values - mean
    variance = wide_total(total(centered * centered * mask)) / group_size
    return mean, lax.rsqrt(variance + epsilon)


def norm_back(grad, normal, inverse, mask, group_size, gain):
    scaled = grad * gain
    plain = wide_total(total(scaled)) / group_size
    cross = wide_total(total(scaled * normal)) / group_size
    grad_in = inverse * (scaled - mask * (plain + normal * cross))
    return grad_in, total(grad * normal), total(grad)


def sigmoid(u):
    return 1.0 / (1.0 + jnp.exp(-u))


def silu_slope(u):
    s = sigmoid(u)
    return s * (1.0 + u * (1.0 - s))


def mm(a, b):
    return jnp.dot(a, b, preferred_element_type=F32)


def mm_nt(a, b):
    return lax.dot_general(a, b, (((1,), (1,)), ((), ())), preferred_element_type=F32)


def mm_tn(a, b):
    return lax.dot_general(a, b, (((0,), (0,)), ((), ())), preferred_element_type=F32)


def fill_shifts(shift_ref, values, stride):
    unused, cols = pixel_col(stride)
    lanes = values.shape[1]
    zeros = jnp.zeros((PAD, lanes), BF16)
    for q in range(3):
        shift_ref[q, 0:PAD, :] = zeros
        shift_ref[q, PAD + PIX : 2 * PAD + PIX, :] = zeros
    left = jnp.where(cols == 0, 0.0, pltpu.roll(values, 1, 0))
    right = jnp.where(cols == stride - 1, 0.0, pltpu.roll(values, PIX - 1, 0))
    shift_ref[0, PAD : PAD + PIX, :] = left.astype(BF16)
    shift_ref[1, PAD : PAD + PIX, :] = values.astype(BF16)
    shift_ref[2, PAD : PAD + PIX, :] = right.astype(BF16)


def tap(shift_ref, p, q, stride, first=0, count=PIX):
    start = pl.multiple_of(PAD + first + (p - 1) * stride, 16)
    return shift_ref[q, pl.ds(start, count), :]


def conv_forward(shift_ref, weight_ref, stride, out_ref, tile=256):
    for first in range(0, PIX, tile):
        stacked = jnp.concatenate(
            [tap(shift_ref, p, q, stride, first, tile) for p in range(3) for q in range(3)], axis=1
        )
        out_ref[first : first + tile, :] = mm(stacked, weight_ref[...])


def conv_backward(shift_ref, weight_ref, stride, out_ref, tile=256):
    channels = weight_ref.shape[1]
    for first in range(0, PIX, tile):
        acc = None
        for p in range(3):
            for q in range(3):
                row = (8 - (3 * p + q)) * channels
                part = mm_nt(
                    tap(shift_ref, p, q, stride, first, tile), weight_ref[row : row + channels, :]
                )
                acc = part if acc is None else acc + part
        out_ref[first : first + tile, :] = acc


def assemble(out_ref, facts, h, pieces):
    unused, tall, stride, width = facts
    own, partner, received, partner_received = pieces
    other = h ^ 1

    @pl.when(tall)
    def _():
        for ref, index in (
            (own, h),
            (partner, other),
            (received, h ^ 2),
            (partner_received, other ^ 2),
        ):
            out_ref[pl.ds(pl.multiple_of(96 * index, 16), 96), :] = ref[0:96, :]
        out_ref[384:512, :] = jnp.zeros((128, out_ref.shape[1]), out_ref.dtype)

    @pl.when(jnp.logical_not(tall))
    def _():
        low = h & 1
        out_ref[pl.ds(pl.multiple_of(192 * low, 16), 192), :] = own[...]
        out_ref[pl.ds(pl.multiple_of(192 * (1 - low), 16), 192), :] = partner[...]

        @pl.when(low == 0)
        def _():
            out_ref[384:512, :] = received[...]

        @pl.when(low == 1)
        def _():
            out_ref[384:512, :] = partner_received[...]


def split_out(full_ref, facts, h, own_ref, send_ref):
    unused, tall, stride, width = facts
    send_h = h ^ 2

    @pl.when(tall)
    def _():
        own_ref[0:96, :] = full_ref[pl.ds(pl.multiple_of(96 * h, 16), 96), :]
        own_ref[96:192, :] = jnp.zeros((96, own_ref.shape[1]), own_ref.dtype)
        send_ref[0:96, :] = full_ref[pl.ds(pl.multiple_of(96 * send_h, 16), 96), :]
        send_ref[96:128, :] = jnp.zeros((32, own_ref.shape[1]), own_ref.dtype)

    @pl.when(jnp.logical_not(tall))
    def _():
        own_ref[...] = full_ref[pl.ds(pl.multiple_of(192 * (h & 1), 16), 192), :]
        send_ref[...] = full_ref[384:512, :]


def pack_kernel(bucket_ref, x_ref, cot_ref, away_x, home_x, away_c, home_c):
    h, home, away = place(bucket_ref)
    for src, away_ref, home_ref in ((x_ref, away_x, home_x), (cot_ref, away_c, home_c)):
        for facts, dst, wide_rows in ((away, away_ref, 4), (home, home_ref, 6)):
            image, tall, stride, width = facts

            @pl.when(tall)
            def _():
                for row in range(6):
                    dst[16 * row : 16 * row + 16, :] = src[image, row, 0:16, :]
                dst[96 : dst.shape[0], :] = jnp.zeros((dst.shape[0] - 96, dst.shape[1]), dst.dtype)

            @pl.when(jnp.logical_not(tall))
            def _():
                for row in range(wide_rows):
                    dst[32 * row : 32 * row + 32, :] = src[image, row]


def first_kernel(
    bucket_ref, own, partner, received, partner_received,
    gain1, shift1, weight1, bias1, gain2, shift2,
    image_ref, conv_ref, act1_t, act2_t, act2_ref, stats_ref, send_t,
    shift_ref,
):
    h, home, away = place(bucket_ref)
    stride = home[2]
    mask, pixels = pixel_mask(home)
    channels = gain1.shape[1]
    group_size = pixels * (channels // GROUPS)
    assemble(image_ref, home, h, (own, partner, received, partner_received))
    values = image_ref[...].astype(F32) * mask
    mean1, inverse1 = norm_stats(values, mask, group_size)
    u = (values - mean1) * inverse1 * gain1[...] + shift1[...]
    act = u * sigmoid(u) * mask
    fill_shifts(shift_ref, act, stride)
    act1_t[...] = act.astype(BF16).T
    conv_forward(shift_ref, weight1, stride, conv_ref)
    values = conv_ref[...] + bias1[...]
    conv_ref[...] = values
    mean2, inverse2 = norm_stats(values, mask, group_size)
    u = (values - mean2) * inverse2 * gain2[...] + shift2[...]
    act = (u * sigmoid(u) * mask).astype(BF16)
    act2_ref[...] = act
    act2_t[...] = act.T
    half = pl.multiple_of((h & 1) * (channels // 2), 16)
    send_t[0] = act1_t[pl.ds(half, channels // 2), :]
    send_t[1] = act2_t[pl.ds(half, channels // 2), :]
    stats_ref[0:1, :] = mean1
    stats_ref[1:2, :] = inverse1
    stats_ref[2:3, :] = mean2
    stats_ref[3:4, :] = inverse2
    stats_ref[4:8, :] = jnp.zeros((4, channels), F32)


def second_kernel(
    bucket_ref, image_ref, act2_ref, own, partner, received, partner_received,
    weight2, bias2, gain3, shift3, wq, bq, wk, wv, bv, wp, bp,
    out_own, out_send, grad2_ref, grad_middle_ref, attn_keep, attn_send, vec_ref,
    block_keep, block_send,
    shift_ref, full_ref, middle_ref, scratch,
):
    h, home, away = place(bucket_ref)
    stride = home[2]
    mask, pixels = pixel_mask(home)
    channels = gain3.shape[1]
    group_size = pixels * (channels // GROUPS)
    scaling = channels ** (-0.5)
    fill_shifts(shift_ref, act2_ref[...].astype(F32), stride)
    conv_forward(shift_ref, weight2, stride, middle_ref)
    middle = mask * (image_ref[...].astype(F32) + (middle_ref[...] + bias2[...]))
    middle_ref[...] = middle
    mean3, inverse3 = norm_stats(middle, mask, group_size)
    normal = (middle - mean3) * inverse3
    normed = (normal * gain3[...] + shift3[...]).astype(BF16)
    queries = (mm(normed, wq[...]) + bq[...]).astype(BF16)
    keys = mm(normed, wk[...]).astype(BF16)
    values = (mm(normed, wv[...]) + bv[...]).astype(BF16)
    lanes = lax.broadcasted_iota(jnp.int32, (1, PIX), 1)
    key_cols = lanes & (stride - 1)
    key_valid = (key_cols < home[3]) & (lanes < jnp.where(home[1], 384, 512))
    scores = jnp.where(key_valid, mm_nt(queries, keys) * scaling, -1000000000.0)
    raised = jnp.exp(scores - jnp.max(scores, axis=1, keepdims=True))
    soft = raised * (1.0 / jnp.sum(raised, axis=1, keepdims=True))
    soft16 = soft.astype(BF16)
    mixed = mm(soft16, values).astype(BF16)
    projected = mm(mixed, wp[...]) + bp[...]
    full_ref[...] = (mask * (middle_ref[...] + projected)).astype(BF16)
    split_out(full_ref, home, h, out_own, out_send)

    assemble(full_ref, home, h, (own, partner, received, partner_received))
    grad_top = full_ref[...].astype(F32) * mask
    grad_rows = grad_top.astype(BF16)
    grad_mixed = mm_nt(grad_rows, wp[...]).astype(BF16)
    grad_soft = mm_nt(grad_mixed, values)
    grad_values = mm_tn(soft16, grad_mixed).astype(BF16)
    grad_scores = soft * (grad_soft - jnp.sum(soft * grad_soft, axis=1, keepdims=True))
    grad_scores = grad_scores.astype(BF16)
    grad_queries = (mm(grad_scores, keys) * scaling).astype(BF16)
    grad_keys = (mm_tn(grad_scores, queries) * scaling).astype(BF16)
    grad_normed = (
        mm_nt(grad_queries, wq[...]) + mm_nt(grad_keys, wk[...]) + mm_nt(grad_values, wv[...])
    )
    grad_in, gain_grad, shift_grad = norm_back(
        grad_normed, normal, inverse3, mask, group_size, gain3[...]
    )
    grad_middle = mask * (grad_top + grad_in)
    grad_middle_ref[...] = grad_middle
    grad2 = grad_middle.astype(BF16)
    grad2_ref[...] = grad2
    vec_ref[0:1, :] = gain_grad
    vec_ref[1:2, :] = shift_grad
    vec_ref[2:3, :] = total(grad_queries.astype(F32))
    vec_ref[3:4, :] = total(grad_values.astype(F32))
    vec_ref[4:5, :] = total(grad_top)
    vec_ref[5:6, :] = total(grad2.astype(F32))
    vec_ref[6:8, :] = jnp.zeros((2, channels), F32)

    keep_at = pl.multiple_of(BLK * h, BLK)
    send_at = pl.multiple_of(BLK * (h ^ 2), BLK)
    block_keep[...] = grad2_ref[:, pl.ds(keep_at, BLK)]
    block_send[...] = grad2_ref[:, pl.ds(send_at, BLK)]
    for index, grad in enumerate((grad_queries, grad_keys, grad_values, grad_rows)):
        scratch[...] = grad
        column = (index % 3) * 2 * BLK
        full_ref[:, 0:BLK] = scratch[:, pl.ds(keep_at, BLK)]
        full_ref[:, BLK : 2 * BLK] = scratch[:, pl.ds(send_at, BLK)]
        result = mm_tn(mixed if index == 3 else normed, full_ref[:, 0 : 2 * BLK]).astype(BF16)
        attn_keep[index] = result[:, 0:BLK]
        attn_send[index] = result[:, BLK : 2 * BLK]


def third_kernel(
    bucket_ref, grad2_ref, conv_ref, stats_ref, weight2, gain2, shift2,
    grad1_ref, block_keep, block_send, vec_ref,
    shift_ref, acc_ref,
):
    h, home, away = place(bucket_ref)
    stride = home[2]
    mask, pixels = pixel_mask(home)
    channels = gain2.shape[1]
    group_size = pixels * (channels // GROUPS)
    fill_shifts(shift_ref, grad2_ref[...].astype(F32), stride)
    conv_backward(shift_ref, weight2, stride, acc_ref)
    inverse = stats_ref[3:4, :]
    normal = (conv_ref[...] - stats_ref[2:3, :]) * inverse
    u = normal * gain2[...] + shift2[...]
    grad = mask * acc_ref[...] * silu_slope(u)
    grad_in, gain_grad, shift_grad = norm_back(grad, normal, inverse, mask, group_size, gain2[...])
    grad1 = grad_in.astype(BF16)
    grad1_ref[...] = grad1
    vec_ref[0:1, :] = gain_grad
    vec_ref[1:2, :] = shift_grad
    vec_ref[2:3, :] = total(grad1.astype(F32))
    vec_ref[3:8, :] = jnp.zeros((5, channels), F32)
    block_keep[...] = grad1_ref[:, pl.ds(pl.multiple_of(BLK * h, BLK), BLK)]
    block_send[...] = grad1_ref[:, pl.ds(pl.multiple_of(BLK * (h ^ 2), BLK), BLK)]


def fourth_kernel(
    bucket_ref, grad1_ref, image_ref, stats_ref, grad_middle_ref, weight1, gain1, shift1,
    grad_own, grad_send, vec_ref,
    shift_ref, acc_ref, full_ref,
):
    h, home, away = place(bucket_ref)
    stride = home[2]
    mask, pixels = pixel_mask(home)
    channels = gain1.shape[1]
    group_size = pixels * (channels // GROUPS)
    fill_shifts(shift_ref, grad1_ref[...].astype(F32), stride)
    conv_backward(shift_ref, weight1, stride, acc_ref)
    inverse = stats_ref[1:2, :]
    normal = (image_ref[...].astype(F32) * mask - stats_ref[0:1, :]) * inverse
    u = normal * gain1[...] + shift1[...]
    grad = mask * acc_ref[...] * silu_slope(u)
    grad_in, gain_grad, shift_grad = norm_back(grad, normal, inverse, mask, group_size, gain1[...])
    full_ref[...] = (mask * (grad_middle_ref[...] + grad_in)).astype(BF16)
    vec_ref[0:1, :] = gain_grad
    vec_ref[1:2, :] = shift_grad
    vec_ref[2:8, :] = jnp.zeros((6, channels), F32)
    split_out(full_ref, home, h, grad_own, grad_send)


def weight_kernel(
    bucket_ref, act_t, half_t, partner_half_t, block_own, block_away,
    keep_ref, send_ref,
    left_ref, right_ref, shift_ref, sum_ref,
):
    h, home, away = place(bucket_ref)
    channels = act_t.shape[0]
    half = channels // 2
    left_ref[:, 0:PIX] = act_t[...]
    left_ref[pl.ds(pl.multiple_of((h & 1) * half, 16), half), PIX : 2 * PIX] = half_t[...]
    left_ref[pl.ds(pl.multiple_of((1 - (h & 1)) * half, 16), half), PIX : 2 * PIX] = partner_half_t[...]
    for index, (facts, block) in enumerate(((home, block_own), (away, block_away))):
        stride = facts[2]
        fill_shifts(shift_ref, block[...].astype(F32), stride)
        for p in range(3):
            for q in range(3):
                column = (3 * p + q) * BLK
                right_ref[index * PIX : (index + 1) * PIX, column : column + BLK] = tap(
                    shift_ref, 2 - p, 2 - q, stride
                )
    for t in range(0, 9):
        sum_ref[t * channels : (t + 1) * channels, :] = mm(
            left_ref[...], right_ref[:, t * BLK : (t + 1) * BLK]
        )
    mine = lax.axis_index("batch") & 1
    pairs, rows = keep_ref.shape[0], keep_ref.shape[1]
    for pair in range(pairs):
        keep_ref[pair] = sum_ref[pl.ds(pl.multiple_of((2 * pair + mine) * rows, 8), rows), :].astype(BF16)
        send_ref[pair] = sum_ref[pl.ds(pl.multiple_of((2 * pair + 1 - mine) * rows, 8), rows), :].astype(BF16)


def unpack_kernel(bucket_ref, out_own, out_away, grad_own, grad_away, out_ref, grad_ref):
    h, home, away = place(bucket_ref)
    for own, received, dst in ((out_own, out_away, out_ref), (grad_own, grad_away, grad_ref)):
        channels = dst.shape[3]
        for facts, src, wide_rows in ((away, received, 4), (home, own, 6)):
            image, tall, stride, width = facts

            @pl.when(tall)
            def _():
                for row in range(6):
                    dst[image, row, 0:16, :] = src[16 * row : 16 * row + 16, :]
                    dst[image, row, 16:32, :] = jnp.zeros((16, channels), dst.dtype)

            @pl.when(jnp.logical_not(tall))
            def _():
                for row in range(wide_rows):
                    dst[image, row] = src[32 * row : 32 * row + 32, :]
                for row in range(wide_rows, 6):
                    dst[image, row] = jnp.zeros((32, channels), dst.dtype)

            if wide_rows == 4:

                @pl.when(jnp.logical_not(tall) & (h == 3))
                def _():
                    for row in range(6):
                        dst[image, row] = jnp.zeros((32, channels), dst.dtype)


def call(kernel, name, outs, scratch, flops, nbytes, *operands):
    return pl.pallas_call(
        kernel,
        name=name,
        out_shape=[jax.ShapeDtypeStruct(shape, dtype) for shape, dtype in outs],
        in_specs=[SM] + [VM] * (len(operands) - 1),
        out_specs=[VM] * len(outs),
        scratch_shapes=[pltpu.VMEM(shape, dtype) for shape, dtype in scratch],
        compiler_params=pltpu.CompilerParams(vmem_limit_bytes=48 * 1024 * 1024),
        cost_estimate=pl.CostEstimate(flops=flops, bytes_accessed=nbytes, transcendentals=0),
    )(*operands)


def on_device(
    inputs,
    bucket,
    norm1_gain,
    norm1_shift,
    conv1_weight,
    conv1_bias,
    norm2_gain,
    norm2_shift,
    conv2_weight,
    conv2_bias,
    norm3_gain,
    norm3_shift,
    query_weight,
    query_bias,
    key_weight,
    value_weight,
    value_bias,
    proj_weight,
    proj_bias,
    cotangent,
):
    channels = inputs.shape[-1]
    batches = lax.axis_size("batch")
    bits = batches.bit_length() - 1
    shard_rows = 9 * channels // batches
    small_rows = channels // batches
    C = channels

    def row(v):
        return v.reshape(1, channels)

    def to_core(v):
        return lax.ppermute(v, "height", [(i, i ^ 1) for i in range(4)])

    def to_chip(v):
        return lax.ppermute(v, "height", [(i, i ^ 2) for i in range(4)])

    def to_batch(v, bit):
        return lax.ppermute(v, "batch", [(i, i ^ (1 << bit)) for i in range(batches)])

    img16 = ((PIX, C), BF16)
    img32 = ((PIX, C), F32)
    vec = ((8, C), F32)
    block = ((PIX, BLK), BF16)
    shifts = ((3, PIX + 2 * PAD, C), BF16)
    unit = 2 * PIX * C * C

    away_x, home_x, away_c, home_c = call(
        pack_kernel, "pack",
        [((128, C), BF16), ((192, C), BF16), ((128, C), BF16), ((192, C), BF16)],
        [], 0, 1 << 21, bucket, inputs, cotangent,
    )
    recv_x = to_chip(away_x)
    core_x = to_core(home_x)
    recv_c = to_chip(away_c)
    core_c = to_core(home_c)
    core_recv_x = to_core(recv_x)
    core_recv_c = to_core(recv_c)

    image, conv, act1_t, act2_t, act2, stats, send_t = call(
        first_kernel, "first",
        [img16, img32, ((C, PIX), BF16), ((C, PIX), BF16), img16, vec, ((2, C // 2, PIX), BF16)],
        [shifts], 9 * unit, 9 << 20,
        bucket, home_x, core_x, recv_x, core_recv_x, row(norm1_gain), row(norm1_shift),
        conv1_weight, row(conv1_bias), row(norm2_gain), row(norm2_shift),
    )
    half_t = to_chip(send_t)
    core_half_t = to_core(half_t)

    out_own, out_send, grad2, grad_middle, attn_keep, attn_send, vec_a, block2, block2_send = call(
        second_kernel, "second",
        [((192, C), BF16), ((128, C), BF16), img16, img32, ((4, C, BLK), BF16), ((4, C, BLK), BF16),
         vec, block, block],
        [shifts, img16, img32, img16], 32 * unit, 12 << 20,
        bucket, image, act2, home_c, core_c, recv_c, core_recv_c,
        conv2_weight, row(conv2_bias), row(norm3_gain), row(norm3_shift),
        query_weight, row(query_bias), key_weight, value_weight, row(value_bias),
        proj_weight, row(proj_bias),
    )
    block2_away = to_chip(block2_send)
    attn_recv = to_chip(attn_send)
    out_away = to_chip(out_send)

    grad1, block1, block1_send, vec_b = call(
        third_kernel, "third",
        [img16, block, block, vec],
        [shifts, img32], 9 * unit, 9 << 20,
        bucket, grad2, conv, stats, conv2_weight, row(norm2_gain), row(norm2_shift),
    )
    block1_away = to_chip(block1_send)

    def weight_grad(name, act_t, index, own, away):
        return call(
            weight_kernel, name,
            [((batches // 2, shard_rows, BLK), BF16)] * 2,
            [((C, 2 * PIX), BF16), ((2 * PIX, 9 * BLK), BF16), ((3, PIX + 2 * PAD, BLK), BF16),
             ((9 * C, BLK), F32)],
            5 * unit, 4 << 20,
            bucket, act_t, half_t[index], core_half_t[index], own, away,
        )

    keep2, send2 = weight_grad("weight2", act2_t, 1, block2, block2_away)
    attn = attn_keep.astype(F32) + attn_recv.astype(F32)
    attn = attn.astype(BF16).reshape(4, batches // 2, 2, small_rows, BLK)
    me = lax.axis_index("batch")

    def pick(v, axis, bit):
        mine = (me >> bit) & 1
        return (
            lax.dynamic_index_in_dim(v, mine, axis, keepdims=False),
            lax.dynamic_index_in_dim(v, 1 - mine, axis, keepdims=False),
        )

    attn_mine, attn_other = pick(attn, 2, 0)

    def lay(v):
        return jnp.transpose(v, (1, 0, 2, 3)).reshape(batches // 2, 4 * small_rows, BLK)

    def scatter(keep, send):
        bit = 0
        while True:
            got = to_batch(send, bit)
            added = (keep.astype(F32) + got.astype(F32)).astype(BF16)
            bit += 1
            if bit == bits:
                return added[0]
            added = added.reshape(added.shape[0] // 2, 2, *added.shape[1:])
            keep, send = pick(added, 1, bit)

    shard2 = scatter(
        jnp.concatenate([keep2, lay(attn_mine)], axis=1),
        jnp.concatenate([send2, lay(attn_other)], axis=1),
    )

    grad_own, grad_send, vec_c = call(
        fourth_kernel, "fourth",
        [((192, C), BF16), ((128, C), BF16), vec],
        [shifts, img32, img16], 9 * unit, 9 << 20,
        bucket, grad1, image, stats, grad_middle, conv1_weight, row(norm1_gain), row(norm1_shift),
    )
    grad_away = to_chip(grad_send)

    keep1, send1 = weight_grad("weight1", act1_t, 0, block1, block1_away)
    vectors = jnp.concatenate([vec_a[:6], vec_b[:3], vec_c[:2]], axis=0)
    count = vectors.shape[0]
    vec_rows = -(-count * small_rows // BLK)
    vec_rows = -(-vec_rows // 8) * 8
    vectors = jnp.transpose(vectors.reshape(count, batches, small_rows), (1, 0, 2))
    vectors = vectors.reshape(batches, count * small_rows)
    vectors = jnp.pad(vectors, ((0, 0), (0, vec_rows * BLK - count * small_rows)))
    vectors = vectors.astype(BF16).reshape(batches // 2, 2, vec_rows, BLK)
    vec_mine, vec_other = pick(vectors, 1, 0)
    shard1 = scatter(
        jnp.concatenate([keep1, vec_mine], axis=1),
        jnp.concatenate([send1, vec_other], axis=1),
    )

    def gather(shard):
        h = lax.axis_index("height")
        far = to_chip(shard)
        near_pair = jnp.where(h < 2, jnp.stack([shard, far]), jnp.stack([far, shard]))
        core_pair = to_core(near_pair)
        odd = (h & 1) == 1
        even_part = jnp.where(odd, core_pair, near_pair)
        odd_part = jnp.where(odd, near_pair, core_pair)
        return jnp.concatenate([even_part[0], odd_part[0], even_part[1], odd_part[1]], axis=-1).astype(F32)

    whole2 = gather(shard2)
    whole1 = gather(shard1)
    tail = whole1[shard_rows:].reshape(vec_rows, 4, BLK)
    sums = (tail[:, 0] + tail[:, 2]).reshape(vec_rows * BLK)
    v = [sums[i * small_rows : (i + 1) * small_rows] for i in range(count)]
    small = [whole2[shard_rows + i * small_rows : shard_rows + (i + 1) * small_rows] for i in range(4)]

    outputs, input_grad = call(
        unpack_kernel, "unpack",
        [(inputs.shape, BF16)] * 2, [], 0, 1 << 21,
        bucket, out_own, out_away, grad_own, grad_away,
    )
    return (
        outputs, input_grad,
        v[9], v[10], whole1[:shard_rows], v[8],
        v[6], v[7], whole2[:shard_rows], v[5],
        v[0], v[1],
        small[0], v[2], small[1], small[2], v[3], small[3], v[4],
    )


def solution(mesh):
    image = P("batch", "height", None, None)
    vector = P("batch")
    matrix = P("batch", None)
    return jax.shard_map(
        on_device,
        mesh=mesh,
        in_specs=(image, vector) + (P(),) * 17 + (image,),
        out_specs=(
            image, image,
            vector, vector, matrix, vector,
            vector, vector, matrix, vector,
            vector, vector,
            matrix, vector, matrix, matrix, vector, matrix, vector,
        ),
        check_vma=False,
    )
```

time: 872 us -> 138 us (0.16)
  waiting for transfers between devices: 587 us -> 46.5 us
  blocking collectives: 104 us -> 0 us
  matrix products: 66.1 us -> 0 us
  Pallas kernels: 0 us -> 45.1 us
  other arithmetic: 45 us -> 9.29 us
  local copies, waits for them, and re-layouts: 39.9 us -> 11 us
  between operations: 15.4 us -> 1.16 us
  starting transfers between devices: 12.4 us -> 24.2 us
    reduce_scatter x8 -> x0, waiting for transfers between devices: 545 us -> none  [the longest x1 164 us: on_device(): lax.psum_scatter(conv2_weight_grad, 'batch', scatter_dimension=0, tiled=T...]
    psum x10 -> x0, blocking collectives: 68.8 us -> none  [the longest x3 25.5 us: norm_forward(): mean_value = lax.psum(group_sums(values, inside4), 'height') / group_size]
    dot_general x24 -> x0, matrix products: 66.1 us -> none  [the longest x4 17.9 us: conv_apply(): jnp.einsum('ihwk,kc->ihwc', stacked, weight, preferred_element_type=jnp.f...]
    pallas_call x0 -> x8, Pallas kernels: none -> 45.1 us  [call(): pl.pallas_call(kernel, name=name, out_shape=[jax.ShapeDtypeStruct(shape,...]
    ppermute x8 -> x23, waiting for transfers between devices: 8.53 us -> 46.5 us  [the longest x6 29.8 us: to_batch(): return lax.ppermute(v, 'batch', [(i, i ^ 1 << bit) for i in range(batches)])]
    unnamed x1 -> x0, blocking collectives: 35.2 us -> none
    all_gather x2 -> x0, waiting for transfers between devices: 32.7 us -> none  [the longest x1 17.1 us: on_device(): lax.all_gather(values, 'height', axis=1, tiled=True)]
    convert_element_type x30 -> x9, other arithmetic: 32.1 us -> 6.3 us  [the longest x6 3.91 us: scatter(): added = (keep.astype(F32) + got.astype(F32)).astype(BF16)]
  transfers between devices with their start and end apart: 19 -> 23, of which waited for: 12 -> 10; matrix products, arithmetic and copies ran while one was open for 13% -> 8% of each run, Pallas kernels for 0% -> 32%
where the time goes in v1:
time: 138 us; the launch traced here: 137 us
  waiting for transfers between devices  46.5 us (34%)
  Pallas kernels  45.1 us (33%)
  starting transfers between devices  24.2 us (18%)
  local copies, waits for them, and re-layouts  11 us (8%)
  other arithmetic  9.29 us (7%)
    pallas_call x8, Pallas kernels, call(): pl.pallas_call(kernel, name=name, out_shape=[jax.ShapeDtypeStruct(shape,...  45.1 us
    ppermute x6, waiting for transfers between devices, to_batch(): return lax.ppermute(v, 'batch', [(i, i ^ 1 << bit) for i in range(batches)])  29.8 us
    ppermute x10, waiting for transfers between devices, to_chip(): return lax.ppermute(v, 'height', [(i, i ^ 2) for i in range(4)])  15.6 us
    ppermute x6, starting transfers between devices, to_batch(): return lax.ppermute(v, 'batch', [(i, i ^ 1 << bit) for i in range(batches)])  11.9 us
    ppermute x10, starting transfers between devices, to_chip(): return lax.ppermute(v, 'height', [(i, i ^ 2) for i in range(4)])  11.6 us
    unnamed x60, local copies, waits for them, and re-layouts  7.6 us
    convert_element_type x6, other arithmetic, scatter(): added = (keep.astype(F32) + got.astype(F32)).astype(BF16)  3.91 us
  transfers between devices with their start and end apart: 23, of which 10 were waited for; matrix products, arithmetic and copies ran while one was open for 8% of the time, Pallas kernels for 32%

profile of v1, /device:TPU:0, one launch (start us, length us, event | category | flops | bytes accessed | tf_op | source)
XLA Modules:
  0.0 137.3 jit_solution(13869873996365574059)
XLA Ops:
  0.7 1.0 copy-done
  1.7 1.0 copy-done.1
  2.7 0.7 copy-done.2
  3.3 0.6 pack.1
  3.9 3.0 %collective-permute-start.1 = (bf16[128,512]{1,0:T(8,128)(2,1)S(1)}, bf16[128,512]{1,0:T(8,128)(2,1)S(1)}, u32[]{:S(2)}, u32[]{:S(2)}) collective-permute-start(bf16[128,512]{1,0:T(8,128)(2,1)S(1)} %get-tuple-element.53), channel_id=1, source_target_pairs={{0,2},{1,3},{2,0},{3,1},{4,6},{5,7},{6,4},{7,5},{8,10},{9,11},{10,... | collective-permute-start | bytes 393224 | tf_op jit(solution)/shard_map/ppermute | solution.py:490
  7.0 0.2 collective-permute-start.4
  7.1 3.7 %collective-permute-done.1.received = bf16[128,512]{1,0:T(8,128)(2,1)S(1)} collective-permute-done((bf16[128,512]{1,0:T(8,128)(2,1)S(1)}, bf16[128,512]{1,0:T(8,128)(2,1)S(1)}, u32[]{:S(2)}, u32[]{:S(2)}) %collective-permute-start.1) | collective-permute-done | bytes 131104 | tf_op jit(solution)/shard_map/ppermute | solution.py:490
  10.9 0.5 collective-permute-start.3
  11.4 1.9 %collective-permute-done.4.received = bf16[128,512]{1,0:T(8,128)(2,1)S(1)} collective-permute-done((bf16[128,512]{1,0:T(8,128)(2,1)S(1)}, bf16[128,512]{1,0:T(8,128)(2,1)S(1)}, u32[]{:S(2)}, u32[]{:S(2)}) %collective-permute-start.4) | collective-permute-done | bytes 131104 | tf_op jit(solution)/shard_map/ppermute | solution.py:490
  13.3 0.6 copy-done.3
  13.9 0.7 copy-done.9
  14.6 0.7 copy-done.16
  15.3 0.7 copy-done.18
  16.0 0.7 copy-done.20
  16.7 0.7 copy-done.22
  17.4 8.0 %first.1 = (bf16[512,512]{1,0:T(8,128)(2,1)S(1)}, f32[512,512]{1,0:T(8,128)S(1)}, bf16[512,512]{1,0:T(8,128)(2,1)S(1)}, bf16[512,512]{1,0:T(8,128)(2,1)S(1)}, bf...) custom-call(s32[2]{0:T(128)S(1)} %copy-done.3, ...), custom_call_target="tpu_custom_call" | custom-call | flops 2415919104 | bytes 9437184 | tf_op jit(solution)/shard_map/first/pallas_call | solution.py:442
  25.4 0.8 copy-done.27
  26.2 1.7 %collective-permute-start.8 = (bf16[2,256,512]{2,1,0:T(8,128)(2,1)S(1)}, bf16[2,256,512]{2,1,0:T(8,128)(2,1)}, u32[]{:S(2)}, u32[]{:S(2)}) collective-permute-start(bf16[2,256,512]{2,1,0:T(8,128)(2,1)S(1)} %get-tuple-element.70), channel_id=1, source_target_pairs={{0,2},{1,3},{2,0},{3,1},{4,6},{5,7},{6,4},{7,5},{8,10},{9,11},{10,... | collective-permute-start | bytes 1572872 | tf_op jit(solution)/shard_map/ppermute | solution.py:490
  28.1 13.3 %second.1 = (bf16[192,512]{1,0:T(8,128)(2,1)S(1)}, bf16[128,512]{1,0:T(8,128)(2,1)S(1)}, bf16[512,512]{1,0:T(8,128)(2,1)S(1)}, f32[512,512]{1,0:T(8,128)}, bf16[...) custom-call(s32[2]{0:T(128)S(1)} %copy-done.3, ...), custom_call_target="tpu_custom_call" | custom-call | flops 8589934592 | bytes 12582912 | tf_op jit(solution)/shard_map/second/pallas_call | solution.py:442
  41.4 0.3 collective-permute-start.17
  41.7 6.6 %third.1 = (bf16[512,512]{1,0:T(8,128)(2,1)S(1)}, bf16[512,128]{1,0:T(8,128)(2,1)S(1)}, bf16[512,128]{1,0:T(8,128)(2,1)S(1)}, f32[8,512]{1,0:T(8,128)S(1)}) custom-call(s32[2]{0:T(128)S(1)} %copy-done.3, bf16[512,512]{1,0:T(8,128)(2,1)S(1)} %get-tuple-element.60.grad2_ref, f32[512,512]{1,0:T(8,128)S(1)} %get-tuple-element.61.conv_ref, ...), custom_call_target="tpu_custom_call" | custom-call | flops 2415919104 | bytes 9437184 | tf_op jit(solution)/shard_map/third/pallas_call | solution.py:442
  48.3 6.8 %fourth.1 = (bf16[192,512]{1,0:T(8,128)(2,1)S(1)}, bf16[128,512]{1,0:T(8,128)(2,1)S(1)}, f32[8,512]{1,0:T(8,128)S(1)}) custom-call(s32[2]{0:T(128)S(1)} %copy-done.3, bf16[512,512]{1,0:T(8,128)(2,1)S(1)} %get-tuple-element.63.grad1_ref, bf16[512,512]{1,0:T(8,128)(2,1)S(1)} %get-tuple-element.54.image_ref, f32[8,512]{1,0:T(8,128)S(1)} %get-tuple-element.62.stats_ref, ...), custom_call_target="tpu_custom_call" | custom-call | flops 2415919104 | bytes 9437184 | tf_op jit(solution)/shard_map/fourth/pallas_call | solution.py:442
  55.2 0.1 reshape.137
  55.3 0.1 reshape.138
  55.5 1.8 %collective-permute-start.10 = (bf16[512,128]{1,0:T(8,128)(2,1)S(1)}, bf16[512,128]{1,0:T(8,128)(2,1)S(1)}, u32[]{:S(2)}, u32[]{:S(2)}) collective-permute-start(bf16[512,128]{1,0:T(8,128)(2,1)S(1)} %get-tuple-element.72), channel_id=1, source_target_pairs={{0,2},{1,3},{2,0},{3,1},{4,6},{5,7},{6,4},{7,5},{8,10},{9,11},{10,... | collective-permute-start | bytes 393224 | tf_op jit(solution)/shard_map/ppermute | solution.py:490
  57.3 0.3 collective-permute-start.16
  57.6 1.2 add_convert_fusion.2
  58.9 1.1 slice_bitcast_fusion.1
  60.1 1.8 %collective-permute-done.10.block_away = bf16[512,128]{1,0:T(8,128)(2,1)S(1)} collective-permute-done((bf16[512,128]{1,0:T(8,128)(2,1)S(1)}, bf16[512,128]{1,0:T(8,128)(2,1)S(1)}, u32[]{:S(2)}, u32[]{:S(2)}) %collective-permute-start.10) | collective-permute-done | bytes 131104 | tf_op jit(solution)/shard_map/ppermute | solution.py:490
  61.9 4.1 %weight1.5 = (bf16[4,576,128]{2,1,0:T(8,128)(2,1)S(1)}, bf16[4,576,128]{2,1,0:T(8,128)(2,1)S(1)}) custom-call(s32[2]{0:T(128)S(1)} %copy-done.4, bf16[512,512]{1,0:T(8,128)(2,1)S(1)} %copy-done.28, bf16[256,512]{1,0:T(8,128)(2,1)S(1)} %get-tuple-element.98.half_t, bf16[256,512]{1,0:T(8,128)(2,1)S(1)} %get-tuple-element.96.partner_half_t, ...), custom_call_target="tpu_custom_call" | custom-call | flops 1342177280 | bytes 4194304 | tf_op jit(solution)/shard_map/weight1/pallas_call | solution.py:442
  66.0 0.9 pad_maximum_fusion.1
  66.9 1.8 %collective-permute-start.11 = (bf16[4,584,128]{2,1,0:T(8,128)(2,1)}, bf16[4,584,128]{2,1,0:T(8,128)(2,1)}, u32[]{:S(2)}, u32[]{:S(2)}) collective-permute-start(bf16[4,584,128]{2,1,0:T(8,128)(2,1)} %pad_maximum_fusion.1), channel_id=1, source_target_pairs={{0,4},{4,0},{8,12},{12,8},{16,20},{20,16},{24,28},{28,24},{1,5},{5... | collective-permute-start | bytes 1794056 | tf_op jit(solution)/shard_map/ppermute | solution.py:493
  68.7 4.1 %weight2.5 = (bf16[4,576,128]{2,1,0:T(8,128)(2,1)S(1)}, bf16[4,576,128]{2,1,0:T(8,128)(2,1)S(1)}) custom-call(s32[2]{0:T(128)S(1)} %copy-done.4, bf16[512,512]{1,0:T(8,128)(2,1)S(1)} %copy-done.26, bf16[256,512]{1,0:T(8,128)(2,1)S(1)} %get-tuple-element.97.half_t, bf16[256,512]{1,0:T(8,128)(2,1)S(1)} %get-tuple-element.95.partner_half_t, ...), custom_call_target="tpu_custom_call" | custom-call | flops 1342177280 | bytes 4194304 | tf_op jit(solution)/shard_map/weight2/pallas_call | solution.py:442
  72.8 1.0 pad_maximum_fusion
  73.8 0.3 collective-permute-start.18
  74.1 9.6 %collective-permute-done.11 = bf16[4,584,128]{2,1,0:T(8,128)(2,1)} collective-permute-done((bf16[4,584,128]{2,1,0:T(8,128)(2,1)}, bf16[4,584,128]{2,1,0:T(8,128)(2,1)}, u32[]{:S(2)}, u32[]{:S(2)}) %collective-permute-start.11) | collective-permute-done | bytes 598048 | tf_op jit(solution)/shard_map/ppermute | solution.py:493
  83.7 1.2 add_convert_fusion.1
  84.9 1.9 %collective-permute-start.12 = (bf16[2,584,128]{2,1,0:T(8,128)(2,1)S(1)}, bf16[2,584,128]{2,1,0:T(8,128)(2,1)S(1)}, u32[]{:S(2)}, u32[]{:S(2)}) collective-permute-start(bf16[2,584,128]{2,1,0:T(8,128)(2,1)S(1)} %dynamic-slice_bitcast_fusion.1), channel_id=1, source_target_pairs={{0,8},{4,12},{8,0},{12,4},{16,24},{20,28},{24,16},{28,20},{1,9},{5... | collective-permute-start | bytes 897032 | tf_op jit(solution)/shard_map/ppermute | solution.py:493
  86.8 12.8 %collective-permute-done.18 = bf16[4,832,128]{2,1,0:T(8,128)(2,1)} collective-permute-done((bf16[4,832,128]{2,1,0:T(8,128)(2,1)}, bf16[4,832,128]{2,1,0:T(8,128)(2,1)}, u32[]{:S(2)}, u32[]{:S(2)}) %collective-permute-start.18) | collective-permute-done | bytes 852000 | tf_op jit(solution)/shard_map/ppermute | solution.py:493
  99.6 1.4 %add_convert_fusion = bf16[4,832,128]{2,1,0:T(8,128)(2,1)S(1)} fusion(bf16[4,832,128]{2,1,0:T(8,128)(2,1)} %collective-permute-done.18, bf16[4,256,128]{2,1,0:T(8,128)(2,1)S(1)} %bitcast.103, bf16[4,576,128]{2,1,0:T(8,128)(2,1)S(1)} %get-tuple-element.81), kind=kLoop, calls=%fused_computation | loop fusion | flops 2981888 | bytes 2555904 | tf_op jit(solution)/shard_map/convert_element_type | solution.py:577
  101.0 1.9 %collective-permute-start.19 = (bf16[2,832,128]{2,1,0:T(8,128)(2,1)S(1)}, bf16[2,832,128]{2,1,0:T(8,128)(2,1)}, u32[]{:S(2)}, u32[]{:S(2)}) collective-permute-start(bf16[2,832,128]{2,1,0:T(8,128)(2,1)S(1)} %dynamic-slice_bitcast_fusion), channel_id=1, source_target_pairs={{0,8},{4,12},{8,0},{12,4},{16,24},{20,28},{24,16},{28,20},{1,9},{5... | collective-permute-start | bytes 1277960 | tf_op jit(solution)/shard_map/ppermute | solution.py:493
  102.9 0.1 fusion.1
  103.0 2.7 %collective-permute-start.13 = (bf16[1,584,128]{2,1,0:T(8,128)(2,1)S(1)}, bf16[1,584,128]{2,1,0:T(8,128)(2,1)S(1)}, u32[]{:S(2)}, u32[]{:S(2)}) collective-permute-start(bf16[1,584,128]{2,1,0:T(8,128)(2,1)S(1)} %constant_dynamic-slice_fusion.3), channel_id=1, source_target_pairs={{0,16},{4,20},{8,24},{12,28},{16,0},{20,4},{24,8},{28,12},{1,17},{... | collective-permute-start | bytes 448520 | tf_op jit(solution)/shard_map/ppermute | solution.py:493
  105.6 7.4 %collective-permute-done.13 = bf16[1,584,128]{2,1,0:T(8,128)(2,1)S(1)} collective-permute-done((bf16[1,584,128]{2,1,0:T(8,128)(2,1)S(1)}, bf16[1,584,128]{2,1,0:T(8,128)(2,1)S(1)}, u32[]{:S(2)}, u32[]{:S(2)}) %collective-permute-start.13) | collective-permute-done | bytes 149536 | tf_op jit(solution)/shard_map/ppermute | solution.py:493
  113.1 1.6 %collective-permute-start.14 = (bf16[584,128]{1,0:T(8,128)(2,1)S(1)}, bf16[584,128]{1,0:T(8,128)(2,1)S(1)}, u32[]{:S(2)}, u32[]{:S(2)}) collective-permute-start(bf16[584,128]{1,0:T(8,128)(2,1)S(1)} %bitcast.102), channel_id=1, source_target_pairs={{0,2},{1,3},{2,0},{3,1},{4,6},{5,7},{6,4},{7,5},{8,10},{9,11},{10,... | collective-permute-start | bytes 448520 | tf_op jit(solution)/shard_map/ppermute | solution.py:490
  114.7 1.1 fusion
  115.9 3.4 %collective-permute-start.20 = (bf16[1,832,128]{2,1,0:T(8,128)(2,1)S(1)}, bf16[1,832,128]{2,1,0:T(8,128)(2,1)S(1)}, u32[]{:S(2)}, u32[]{:S(2)}) collective-permute-start(bf16[1,832,128]{2,1,0:T(8,128)(2,1)S(1)} %constant_dynamic-slice_fusion), channel_id=1, source_target_pairs={{0,16},{4,20},{8,24},{12,28},{16,0},{20,4},{24,8},{28,12},{1,17},{... | collective-permute-start | bytes 638984 | tf_op jit(solution)/shard_map/ppermute | solution.py:493
  119.3 0.5 collective-permute-start.6
  119.8 1.5 %collective-permute-start.7 = (bf16[128,512]{1,0:T(8,128)(2,1)S(1)}, bf16[128,512]{1,0:T(8,128)(2,1)S(1)}, u32[]{:S(2)}, u32[]{:S(2)}) collective-permute-start(bf16[128,512]{1,0:T(8,128)(2,1)S(1)} %get-tuple-element.66), channel_id=1, source_target_pairs={{0,2},{1,3},{2,0},{3,1},{4,6},{5,7},{6,4},{7,5},{8,10},{9,11},{10,... | collective-permute-start | bytes 393224 | tf_op jit(solution)/shard_map/ppermute | solution.py:490
  121.4 0.1 maximum_select_fusion.1
  121.4 0.1 collective-permute-start.15
  121.5 2.8 %collective-permute-done.6.out_away = bf16[128,512]{1,0:T(8,128)(2,1)S(1)} collective-permute-done((bf16[128,512]{1,0:T(8,128)(2,1)S(1)}, bf16[128,512]{1,0:T(8,128)(2,1)S(1)}, u32[]{:S(2)}, u32[]{:S(2)}) %collective-permute-start.6) | collective-permute-done | bytes 131104 | tf_op jit(solution)/shard_map/ppermute | solution.py:490
  124.3 1.4 %collective-permute-done.7.grad_away = bf16[128,512]{1,0:T(8,128)(2,1)S(1)} collective-permute-done((bf16[128,512]{1,0:T(8,128)(2,1)S(1)}, bf16[128,512]{1,0:T(8,128)(2,1)S(1)}, u32[]{:S(2)}, u32[]{:S(2)}) %collective-permute-start.7) | collective-permute-done | bytes 131104 | tf_op jit(solution)/shard_map/ppermute | solution.py:490
  125.7 1.5 %unpack.1 = (bf16[2,6,32,512]{3,2,1,0:T(8,128)(2,1)}, bf16[2,6,32,512]{3,2,1,0:T(8,128)(2,1)}) custom-call(s32[2]{0:T(128)S(1)} %copy-done.4, bf16[192,512]{1,0:T(8,128)(2,1)S(1)} %get-tuple-element.58.out_own, bf16[128,512]{1,0:T(8,128)(2,1)S(1)} %collective-permute-done.6.out_away, bf16[192,512]{1,0:T(8,128)(2,1)S(1)} %get-tuple-element.65.grad_own, ...), custom_call_target="tpu_custom_call" | custom-call | bytes 2097152 | tf_op jit(solution)/shard_map/unpack/pallas_call | solution.py:442
  127.3 0.7 collective-permute-start.21
  128.0 0.1 broadcast_select_fusion.3
  128.2 1.1 fusion.2
  129.3 3.9 %collective-permute-done.21 = bf16[832,128]{1,0:T(8,128)(2,1)S(1)} collective-permute-done((bf16[832,128]{1,0:T(8,128)(2,1)S(1)}, bf16[832,128]{1,0:T(8,128)(2,1)S(1)}, u32[]{:S(2)}, u32[]{:S(2)}) %collective-permute-start.21) | collective-permute-done | bytes 213024 | tf_op jit(solution)/shard_map/ppermute | solution.py:490
  133.3 0.6 fusion.4
  134.0 1.1 collective-permute-done.22
  135.1 0.1 broadcast_select_fusion.1
  135.2 0.1 maximum_convert_fusion
  135.4 0.8 maximum_convert_fusion.1
  136.2 1.1 slice.160
  (89 shorter events, 0.8 us)
Async XLA Ops:
  0.7 1.0 copy-start
  1.7 1.0 copy-start.1
  2.6 0.7 copy-start.2
  3.9 6.9 %collective-permute-start.1 = (bf16[128,512]{1,0:T(8,128)(2,1)S(1)}, bf16[128,512]{1,0:T(8,128)(2,1)S(1)}, u32[]{:S(2)}, u32[]{:S(2)}) collective-permute-start(bf16[128,512]{1,0:T(8,128)(2,1)S(1)} %get-tuple-element.53), channel_id=1, source_target_pairs={{0,2},{1,3},{2,0},{3,1},{4,6},{5,7},{6,4},{7,5},{8,10},{9,11},{10,... | collective-permute-start | bytes 393224 | tf_op jit(solution)/shard_map/ppermute | solution.py:490
  7.0 6.3 %collective-permute-start = (bf16[192,512]{1,0:T(8,128)(2,1)S(1)}, bf16[192,512]{1,0:T(8,128)(2,1)S(1)}, u32[]{:S(2)}, u32[]{:S(2)}) collective-permute-start(bf16[192,512]{1,0:T(8,128)(2,1)S(1)} %get-tuple-element.52.own), channel_id=1, source_target_pairs={{0,1},{1,0},{2,3},{3,2},{4,5},{5,4},{6,7},{7,6},{8,9},{9,8},{10,11... | collective-permute-start | bytes 589832 | tf_op jit(solution)/shard_map/ppermute | solution.py:487
  7.0 6.3 %collective-permute-start.4 = (bf16[128,512]{1,0:T(8,128)(2,1)S(1)}, bf16[128,512]{1,0:T(8,128)(2,1)S(1)}, u32[]{:S(2)}, u32[]{:S(2)}) collective-permute-start(bf16[128,512]{1,0:T(8,128)(2,1)S(1)} %get-tuple-element.57), channel_id=1, source_target_pairs={{0,2},{1,3},{2,0},{3,1},{4,6},{5,7},{6,4},{7,5},{8,10},{9,11},{10,... | collective-permute-start | bytes 393224 | tf_op jit(solution)/shard_map/ppermute | solution.py:490
  10.9 2.4 %collective-permute-start.2 = (bf16[128,512]{1,0:T(8,128)(2,1)S(1)}, bf16[128,512]{1,0:T(8,128)(2,1)S(1)}, u32[]{:S(2)}, u32[]{:S(2)}) collective-permute-start(bf16[128,512]{1,0:T(8,128)(2,1)S(1)} %collective-permute-done.1.received), channel_id=1, source_target_pairs={{0,1},{1,0},{2,3},{3,2},{4,5},{5,4},{6,7},{7,6},{8,9},{9,8},{10,11... | collective-permute-start | bytes 393224 | tf_op jit(solution)/shard_map/ppermute | solution.py:487
  10.9 17.1 %collective-permute-start.3 = (bf16[192,512]{1,0:T(8,128)(2,1)S(1)}, bf16[192,512]{1,0:T(8,128)(2,1)S(1)}, u32[]{:S(2)}, u32[]{:S(2)}) collective-permute-start(bf16[192,512]{1,0:T(8,128)(2,1)S(1)} %get-tuple-element.56.own), channel_id=1, source_target_pairs={{0,1},{1,0},{2,3},{3,2},{4,5},{5,4},{6,7},{7,6},{8,9},{9,8},{10,11... | collective-permute-start | bytes 589832 | tf_op jit(solution)/shard_map/ppermute | solution.py:487
  13.3 14.7 %collective-permute-start.5 = (bf16[128,512]{1,0:T(8,128)(2,1)S(1)}, bf16[128,512]{1,0:T(8,128)(2,1)S(1)}, u32[]{:S(2)}, u32[]{:S(2)}) collective-permute-start(bf16[128,512]{1,0:T(8,128)(2,1)S(1)} %collective-permute-done.4.received), channel_id=1, source_target_pairs={{0,1},{1,0},{2,3},{3,2},{4,5},{5,4},{6,7},{7,6},{8,9},{9,8},{10,11... | collective-permute-start | bytes 393224 | tf_op jit(solution)/shard_map/ppermute | solution.py:487
  13.3 0.7 copy-start.3
  13.9 0.7 copy-start.9
  14.6 0.7 copy-start.16
  15.3 0.7 copy-start.18
  16.0 0.7 copy-start.20
  16.7 0.7 copy-start.22
  17.4 10.6 %copy-start.5 = (bf16[512,512]{1,0:T(8,128)(2,1)S(1)}, bf16[512,512]{1,0:T(8,128)(2,1)}, u32[]{:S(2)}) copy-start(bf16[512,512]{1,0:T(8,128)(2,1)} %wq.1) | copy-start | bytes 1572868
  17.4 10.6 %copy-start.6 = (bf16[512,512]{1,0:T(8,128)(2,1)S(1)}, bf16[512,512]{1,0:T(8,128)(2,1)}, u32[]{:S(2)}) copy-start(bf16[512,512]{1,0:T(8,128)(2,1)} %wk.1) | copy-start | bytes 1572868
  17.4 10.6 %copy-start.7 = (bf16[512,512]{1,0:T(8,128)(2,1)S(1)}, bf16[512,512]{1,0:T(8,128)(2,1)}, u32[]{:S(2)}) copy-start(bf16[512,512]{1,0:T(8,128)(2,1)} %wv.1) | copy-start | bytes 1572868
  17.4 10.6 %copy-start.8 = (bf16[512,512]{1,0:T(8,128)(2,1)S(1)}, bf16[512,512]{1,0:T(8,128)(2,1)}, u32[]{:S(2)}) copy-start(bf16[512,512]{1,0:T(8,128)(2,1)} %wp.1) | copy-start | bytes 1572868
  17.4 10.6 %copy-start.10 = (f32[512]{0:T(512)S(1)}, f32[512]{0:T(512)}, u32[]{:S(2)}) copy-start(f32[512]{0:T(512)} %param.29) | copy-start | bytes 6148
  17.4 10.6 %copy-start.11 = (f32[512]{0:T(512)S(1)}, f32[512]{0:T(512)}, u32[]{:S(2)}) copy-start(f32[512]{0:T(512)} %param.30) | copy-start | bytes 6148
  17.4 10.6 %copy-start.12 = (f32[512]{0:T(512)S(1)}, f32[512]{0:T(512)}, u32[]{:S(2)}) copy-start(f32[512]{0:T(512)} %param.31) | copy-start | bytes 6148
  17.4 10.6 %copy-start.13 = (f32[512]{0:T(512)S(1)}, f32[512]{0:T(512)}, u32[]{:S(2)}) copy-start(f32[512]{0:T(512)} %param.33) | copy-start | bytes 6148
  17.4 10.6 %copy-start.14 = (f32[512]{0:T(512)S(1)}, f32[512]{0:T(512)}, u32[]{:S(2)}) copy-start(f32[512]{0:T(512)} %param.36) | copy-start | bytes 6148
  17.4 10.6 %copy-start.15 = (f32[512]{0:T(512)S(1)}, f32[512]{0:T(512)}, u32[]{:S(2)}) copy-start(f32[512]{0:T(512)} %param.38) | copy-start | bytes 6148
  25.4 0.8 copy-start.27
  26.2 15.2 %copy-start.25 = (bf16[512,512]{1,0:T(8,128)(2,1)}, bf16[512,512]{1,0:T(8,128)(2,1)S(1)}, u32[]{:S(2)}) copy-start(bf16[512,512]{1,0:T(8,128)(2,1)S(1)} %get-tuple-element.78.act_t) | copy-start | bytes 1572868
  26.2 31.3 %collective-permute-start.8 = (bf16[2,256,512]{2,1,0:T(8,128)(2,1)S(1)}, bf16[2,256,512]{2,1,0:T(8,128)(2,1)}, u32[]{:S(2)}, u32[]{:S(2)}) collective-permute-start(bf16[2,256,512]{2,1,0:T(8,128)(2,1)S(1)} %get-tuple-element.70), channel_id=1, source_target_pairs={{0,2},{1,3},{2,0},{3,1},{4,6},{5,7},{6,4},{7,5},{8,10},{9,11},{10,... | collective-permute-start | bytes 1572872 | tf_op jit(solution)/shard_map/ppermute | solution.py:490
  28.1 13.7 %copy-start.17 = (f32[512]{0:T(512)S(1)}, f32[512]{0:T(512)}, u32[]{:S(2)}) copy-start(f32[512]{0:T(512)} %param.26) | copy-start | bytes 6148
  28.1 13.6 %copy-start.19 = (f32[512]{0:T(512)S(1)}, f32[512]{0:T(512)}, u32[]{:S(2)}) copy-start(f32[512]{0:T(512)} %param.27) | copy-start | bytes 6148
  41.4 16.1 %collective-permute-start.17 = (bf16[4,512,128]{2,1,0:T(8,128)(2,1)S(1)}, bf16[4,512,128]{2,1,0:T(8,128)(2,1)}, u32[]{:S(2)}, u32[]{:S(2)}) collective-permute-start(bf16[4,512,128]{2,1,0:T(8,128)(2,1)S(1)} %get-tuple-element.83), channel_id=1, source_target_pairs={{0,2},{1,3},{2,0},{3,1},{4,6},{5,7},{6,4},{7,5},{8,10},{9,11},{10,... | collective-permute-start | bytes 1572872 | tf_op jit(solution)/shard_map/ppermute | solution.py:490
  41.7 6.6 %copy-start.21 = (f32[512]{0:T(512)S(1)}, f32[512]{0:T(512)}, u32[]{:S(2)}) copy-start(f32[512]{0:T(512)} %param.22) | copy-start | bytes 6148
  41.7 6.6 %copy-start.23 = (f32[512]{0:T(512)S(1)}, f32[512]{0:T(512)}, u32[]{:S(2)}) copy-start(f32[512]{0:T(512)} %param.23) | copy-start | bytes 6148
  41.7 6.6 %copy-start.24 = (f32[512,512]{1,0:T(8,128)S(1)}, f32[512,512]{1,0:T(8,128)}, u32[]{:S(2)}) copy-start(f32[512,512]{1,0:T(8,128)} %get-tuple-element.64.grad_middle_ref) | copy-start | bytes 3145732
  55.5 6.4 %collective-permute-start.10 = (bf16[512,128]{1,0:T(8,128)(2,1)S(1)}, bf16[512,128]{1,0:T(8,128)(2,1)S(1)}, u32[]{:S(2)}, u32[]{:S(2)}) collective-permute-start(bf16[512,128]{1,0:T(8,128)(2,1)S(1)} %get-tuple-element.72), channel_id=1, source_target_pairs={{0,2},{1,3},{2,0},{3,1},{4,6},{5,7},{6,4},{7,5},{8,10},{9,11},{10,... | collective-permute-start | bytes 393224 | tf_op jit(solution)/shard_map/ppermute | solution.py:490
  57.3 11.4 %collective-permute-start.16 = (bf16[512,128]{1,0:T(8,128)(2,1)S(1)}, bf16[512,128]{1,0:T(8,128)(2,1)S(1)}, u32[]{:S(2)}, u32[]{:S(2)}) collective-permute-start(bf16[512,128]{1,0:T(8,128)(2,1)S(1)} %get-tuple-element.80), channel_id=1, source_target_pairs={{0,2},{1,3},{2,0},{3,1},{4,6},{5,7},{6,4},{7,5},{8,10},{9,11},{10,... | collective-permute-start | bytes 393224 | tf_op jit(solution)/shard_map/ppermute | solution.py:490
  57.6 2.4 %collective-permute-start.9 = (bf16[2,256,512]{2,1,0:T(8,128)(2,1)}, bf16[2,256,512]{2,1,0:T(8,128)(2,1)S(1)}, u32[]{:S(2)}, u32[]{:S(2)}) collective-permute-start(bf16[2,256,512]{2,1,0:T(8,128)(2,1)} %collective-permute-done.8), channel_id=1, source_target_pairs={{0,1},{1,0},{2,3},{3,2},{4,5},{5,4},{6,7},{7,6},{8,9},{9,8},{10,11... | collective-permute-start | bytes 1572872 | tf_op jit(solution)/shard_map/ppermute | solution.py:487
  58.8 3.1 %copy-start.4 = (s32[2]{0:T(128)S(1)}, s32[2]{0:T(128)}, u32[]{:S(2)}) copy-start(s32[2]{0:T(128)} %bucket_ref.15) | copy-start | bytes 28
  58.8 3.1 %copy-start.28 = (bf16[512,512]{1,0:T(8,128)(2,1)S(1)}, bf16[512,512]{1,0:T(8,128)(2,1)}, u32[]{:S(2)}) copy-start(bf16[512,512]{1,0:T(8,128)(2,1)} %copy-done.27) | copy-start | bytes 1572868
  61.9 6.8 %copy-start.26 = (bf16[512,512]{1,0:T(8,128)(2,1)S(1)}, bf16[512,512]{1,0:T(8,128)(2,1)}, u32[]{:S(2)}) copy-start(bf16[512,512]{1,0:T(8,128)(2,1)} %copy-done.25) | copy-start | bytes 1572868
  66.9 16.8 %collective-permute-start.11 = (bf16[4,584,128]{2,1,0:T(8,128)(2,1)}, bf16[4,584,128]{2,1,0:T(8,128)(2,1)}, u32[]{:S(2)}, u32[]{:S(2)}) collective-permute-start(bf16[4,584,128]{2,1,0:T(8,128)(2,1)} %pad_maximum_fusion.1), channel_id=1, source_target_pairs={{0,4},{4,0},{8,12},{12,8},{16,20},{20,16},{24,28},{28,24},{1,5},{5... | collective-permute-start | bytes 1794056 | tf_op jit(solution)/shard_map/ppermute | solution.py:493
  73.8 25.8 %collective-permute-start.18 = (bf16[4,832,128]{2,1,0:T(8,128)(2,1)}, bf16[4,832,128]{2,1,0:T(8,128)(2,1)}, u32[]{:S(2)}, u32[]{:S(2)}) collective-permute-start(bf16[4,832,128]{2,1,0:T(8,128)(2,1)} %pad_maximum_fusion), channel_id=1, source_target_pairs={{0,4},{4,0},{8,12},{12,8},{16,20},{20,16},{24,28},{28,24},{1,5},{5... | collective-permute-start | bytes 2555912 | tf_op jit(solution)/shard_map/ppermute | solution.py:493
  84.9 17.9 %collective-permute-start.12 = (bf16[2,584,128]{2,1,0:T(8,128)(2,1)S(1)}, bf16[2,584,128]{2,1,0:T(8,128)(2,1)S(1)}, u32[]{:S(2)}, u32[]{:S(2)}) collective-permute-start(bf16[2,584,128]{2,1,0:T(8,128)(2,1)S(1)} %dynamic-slice_bitcast_fusion.1), channel_id=1, source_target_pairs={{0,8},{4,12},{8,0},{12,4},{16,24},{20,28},{24,16},{28,20},{1,9},{5... | collective-permute-start | bytes 897032 | tf_op jit(solution)/shard_map/ppermute | solution.py:493
  101.0 13.7 %collective-permute-start.19 = (bf16[2,832,128]{2,1,0:T(8,128)(2,1)S(1)}, bf16[2,832,128]{2,1,0:T(8,128)(2,1)}, u32[]{:S(2)}, u32[]{:S(2)}) collective-permute-start(bf16[2,832,128]{2,1,0:T(8,128)(2,1)S(1)} %dynamic-slice_bitcast_fusion), channel_id=1, source_target_pairs={{0,8},{4,12},{8,0},{12,4},{16,24},{20,28},{24,16},{28,20},{1,9},{5... | collective-permute-start | bytes 1277960 | tf_op jit(solution)/shard_map/ppermute | solution.py:493
  103.0 10.1 %collective-permute-start.13 = (bf16[1,584,128]{2,1,0:T(8,128)(2,1)S(1)}, bf16[1,584,128]{2,1,0:T(8,128)(2,1)S(1)}, u32[]{:S(2)}, u32[]{:S(2)}) collective-permute-start(bf16[1,584,128]{2,1,0:T(8,128)(2,1)S(1)} %constant_dynamic-slice_fusion.3), channel_id=1, source_target_pairs={{0,16},{4,20},{8,24},{12,28},{16,0},{20,4},{24,8},{28,12},{1,17},{... | collective-permute-start | bytes 448520 | tf_op jit(solution)/shard_map/ppermute | solution.py:493
  113.1 8.3 %collective-permute-start.14 = (bf16[584,128]{1,0:T(8,128)(2,1)S(1)}, bf16[584,128]{1,0:T(8,128)(2,1)S(1)}, u32[]{:S(2)}, u32[]{:S(2)}) collective-permute-start(bf16[584,128]{1,0:T(8,128)(2,1)S(1)} %bitcast.102), channel_id=1, source_target_pairs={{0,2},{1,3},{2,0},{3,1},{4,6},{5,7},{6,4},{7,5},{8,10},{9,11},{10,... | collective-permute-start | bytes 448520 | tf_op jit(solution)/shard_map/ppermute | solution.py:490
  115.9 11.3 %collective-permute-start.20 = (bf16[1,832,128]{2,1,0:T(8,128)(2,1)S(1)}, bf16[1,832,128]{2,1,0:T(8,128)(2,1)S(1)}, u32[]{:S(2)}, u32[]{:S(2)}) collective-permute-start(bf16[1,832,128]{2,1,0:T(8,128)(2,1)S(1)} %constant_dynamic-slice_fusion), channel_id=1, source_target_pairs={{0,16},{4,20},{8,24},{12,28},{16,0},{20,4},{24,8},{28,12},{1,17},{... | collective-permute-start | bytes 638984 | tf_op jit(solution)/shard_map/ppermute | solution.py:493
  119.3 5.0 %collective-permute-start.6 = (bf16[128,512]{1,0:T(8,128)(2,1)S(1)}, bf16[128,512]{1,0:T(8,128)(2,1)S(1)}, u32[]{:S(2)}, u32[]{:S(2)}) collective-permute-start(bf16[128,512]{1,0:T(8,128)(2,1)S(1)} %get-tuple-element.59), channel_id=1, source_target_pairs={{0,2},{1,3},{2,0},{3,1},{4,6},{5,7},{6,4},{7,5},{8,10},{9,11},{10,... | collective-permute-start | bytes 393224 | tf_op jit(solution)/shard_map/ppermute | solution.py:490
  119.8 5.9 %collective-permute-start.7 = (bf16[128,512]{1,0:T(8,128)(2,1)S(1)}, bf16[128,512]{1,0:T(8,128)(2,1)S(1)}, u32[]{:S(2)}, u32[]{:S(2)}) collective-permute-start(bf16[128,512]{1,0:T(8,128)(2,1)S(1)} %get-tuple-element.66), channel_id=1, source_target_pairs={{0,2},{1,3},{2,0},{3,1},{4,6},{5,7},{6,4},{7,5},{8,10},{9,11},{10,... | collective-permute-start | bytes 393224 | tf_op jit(solution)/shard_map/ppermute | solution.py:490
  121.4 6.5 %collective-permute-start.15 = (bf16[2,584,128]{2,1,0:T(8,128)(2,1)S(1)}, bf16[2,584,128]{2,1,0:T(8,128)(2,1)S(1)}, u32[]{:S(2)}, u32[]{:S(2)}) collective-permute-start(bf16[2,584,128]{2,1,0:T(8,128)(2,1)S(1)} %maximum_select_fusion.1), channel_id=1, source_target_pairs={{0,1},{1,0},{2,3},{3,2},{4,5},{5,4},{6,7},{7,6},{8,9},{9,8},{10,11... | collective-permute-start | bytes 897032 | tf_op jit(solution)/shard_map/ppermute | solution.py:487
  127.3 5.9 %collective-permute-start.21 = (bf16[832,128]{1,0:T(8,128)(2,1)S(1)}, bf16[832,128]{1,0:T(8,128)(2,1)S(1)}, u32[]{:S(2)}, u32[]{:S(2)}) collective-permute-start(bf16[832,128]{1,0:T(8,128)(2,1)S(1)} %bitcast.101), channel_id=1, source_target_pairs={{0,2},{1,3},{2,0},{3,1},{4,6},{5,7},{6,4},{7,5},{8,10},{9,11},{10,... | collective-permute-start | bytes 638984 | tf_op jit(solution)/shard_map/ppermute | solution.py:490
  133.3 1.8 %collective-permute-start.22 = (bf16[2,832,128]{2,1,0:T(8,128)(2,1)S(1)}, bf16[2,832,128]{2,1,0:T(8,128)(2,1)S(1)}, u32[]{:S(2)}, u32[]{:S(2)}) collective-permute-start(bf16[2,832,128]{2,1,0:T(8,128)(2,1)S(1)} %maximum_select_fusion), channel_id=1, source_target_pairs={{0,1},{1,0},{2,3},{3,2},{4,5},{5,4},{6,7},{7,6},{8,9},{9,8},{10,11... | collective-permute-start | bytes 1277960 | tf_op jit(solution)/shard_map/ppermute | solution.py:487

commit v2 on v1

v2 whole, which is shorter than its diff:
```python
import functools

import jax
import jax.numpy as jnp
from jax import lax
from jax.experimental import pallas as pl
from jax.experimental.pallas import tpu as pltpu
from jax.sharding import PartitionSpec as P

GROUPS = 32
UNIT = 8
PIX = 512
PAD = 32
BLK = 128
F32 = jnp.float32
BF16 = jnp.bfloat16
epsilon = 1e-05

VM = pl.BlockSpec(memory_space=pltpu.VMEM)
SM = pl.BlockSpec(memory_space=pltpu.SMEM)
HB = pl.BlockSpec(memory_space=pl.ANY)
RATE = 1 << 30
LENGTH = {
    "pack": 1, "first": 6, "second": 11, "third": 5, "fourth": 5, "weight2": 3, "weight1": 3, "unpack": 2,
}


def place(bucket_ref):
    h = lax.axis_index("height")
    upper = lax.div(h, 2)
    tall_first = bucket_ref[0] == 1
    tall_image = jnp.where(tall_first, 0, 1)
    home = jnp.where(upper == 1, tall_image, 1 - tall_image)
    away = 1 - home

    def facts(image):
        kind = bucket_ref[image]
        tall = kind == 1
        stride = jnp.where(tall, 2 * UNIT, 4 * UNIT)
        width = jnp.where(kind == 0, 3 * UNIT, stride)
        return (image, tall, stride, width)

    return h, facts(home), facts(away)


def pixel_col(stride, lanes=1):
    rows = lax.broadcasted_iota(jnp.int32, (PIX, lanes), 0)
    return rows, rows & (stride - 1)


def pixel_mask(facts):
    unused, tall, stride, width = facts
    rows, cols = pixel_col(stride)
    limit = jnp.where(tall, 6 * UNIT * UNIT, 8 * UNIT * UNIT)
    mask = jnp.where((cols < width) & (rows < limit), 1.0, 0.0).astype(F32)
    size = jnp.where(tall | (width == 3 * UNIT), 6 * UNIT * UNIT, 8 * UNIT * UNIT)
    return mask, size.astype(F32)


def group_total(row):
    channels = row.shape[-1]
    lane = lax.broadcasted_iota(jnp.int32, row.shape, 1)
    step = 1
    while step < channels // GROUPS:
        up = pltpu.roll(row, channels - step, 1)
        down = pltpu.roll(row, step, 1)
        row = row + jnp.where((lane & step) == 0, up, down)
        step *= 2
    return row


def total(values):
    return jnp.sum(values, axis=0, keepdims=True)


def wide_total(row):
    return group_total(jnp.broadcast_to(row, (8, row.shape[-1])))[0:1]


def norm_stats(values, mask, group_size):
    mean = wide_total(total(values)) / group_size
    centered = (values - mean) * mask
    variance = wide_total(total(centered * centered)) / group_size
    return mean, lax.rsqrt(variance + epsilon)


def silu_norm(values, mean, inverse, gain, shift, mask):
    scale = 0.5 * inverse * gain
    half = values * scale + (0.5 * shift - mean * scale)
    return (half + half * jnp.tanh(half)) * mask


def norm_back(grad, normal, inverse, mask, group_size, gain):
    plain_row = total(grad)
    cross_row = total(grad * normal)
    plain = wide_total(plain_row * gain) / group_size
    cross = wide_total(cross_row * gain) / group_size
    grad_in = grad * (inverse * gain) - mask * (plain * inverse + normal * (cross * inverse))
    return grad_in, cross_row, plain_row


def silu_slope(u):
    half = 0.5 * u
    t = jnp.tanh(half)
    return (0.5 + 0.5 * t) * (1.0 + half * (1.0 - t))


def mm(a, b):
    return jnp.dot(a, b, preferred_element_type=F32)


def mm_nt(a, b):
    return lax.dot_general(a, b, (((1,), (1,)), ((), ())), preferred_element_type=F32)


def mm_tn(a, b):
    return lax.dot_general(a, b, (((0,), (0,)), ((), ())), preferred_element_type=F32)


def fill_shifts(shift_ref, values, stride):
    unused, cols = pixel_col(stride)
    lanes = values.shape[1]
    zeros = jnp.zeros((PAD, lanes), BF16)
    for q in range(3):
        shift_ref[q, 0:PAD, :] = zeros
        shift_ref[q, PAD + PIX : 2 * PAD + PIX, :] = zeros
    left = jnp.where(cols == 0, 0.0, pltpu.roll(values, 1, 0))
    right = jnp.where(cols == stride - 1, 0.0, pltpu.roll(values, PIX - 1, 0))
    shift_ref[0, PAD : PAD + PIX, :] = left.astype(BF16)
    shift_ref[1, PAD : PAD + PIX, :] = values.astype(BF16)
    shift_ref[2, PAD : PAD + PIX, :] = right.astype(BF16)


def tap(shift_ref, p, q, stride, first=0, count=PIX):
    start = pl.multiple_of(PAD + first + (p - 1) * stride, 16)
    return shift_ref[q, pl.ds(start, count), :]


def conv_forward(shift_ref, weight_ref, stride, out_ref, tile=256):
    for first in range(0, PIX, tile):
        stacked = jnp.concatenate(
            [tap(shift_ref, p, q, stride, first, tile) for p in range(3) for q in range(3)], axis=1
        )
        out_ref[first : first + tile, :] = mm(stacked, weight_ref[...])


def conv_backward(shift_ref, weight_ref, stride, out_ref, tile=256):
    channels = weight_ref.shape[1]
    for first in range(0, PIX, tile):
        acc = None
        for p in range(3):
            for q in range(3):
                row = (8 - (3 * p + q)) * channels
                part = mm_nt(
                    tap(shift_ref, p, q, stride, first, tile), weight_ref[row : row + channels, :]
                )
                acc = part if acc is None else acc + part
        out_ref[first : first + tile, :] = acc


def assemble(out_ref, facts, h, pieces):
    unused, tall, stride, width = facts
    own, partner, received, partner_received = pieces
    other = h ^ 1

    @pl.when(tall)
    def _():
        for ref, index in (
            (own, h),
            (partner, other),
            (received, h ^ 2),
            (partner_received, other ^ 2),
        ):
            out_ref[pl.ds(pl.multiple_of(96 * index, 16), 96), :] = ref[0:96, :]
        out_ref[384:512, :] = jnp.zeros((128, out_ref.shape[1]), out_ref.dtype)

    @pl.when(jnp.logical_not(tall))
    def _():
        low = h & 1
        out_ref[pl.ds(pl.multiple_of(192 * low, 16), 192), :] = own[...]
        out_ref[pl.ds(pl.multiple_of(192 * (1 - low), 16), 192), :] = partner[...]

        @pl.when(low == 0)
        def _():
            out_ref[384:512, :] = received[...]

        @pl.when(low == 1)
        def _():
            out_ref[384:512, :] = partner_received[...]


def split_out(full_ref, facts, h, own_ref, send_ref):
    unused, tall, stride, width = facts
    send_h = h ^ 2

    @pl.when(tall)
    def _():
        own_ref[0:96, :] = full_ref[pl.ds(pl.multiple_of(96 * h, 16), 96), :]
        own_ref[96:192, :] = jnp.zeros((96, own_ref.shape[1]), own_ref.dtype)
        send_ref[0:96, :] = full_ref[pl.ds(pl.multiple_of(96 * send_h, 16), 96), :]
        send_ref[96:128, :] = jnp.zeros((32, own_ref.shape[1]), own_ref.dtype)

    @pl.when(jnp.logical_not(tall))
    def _():
        own_ref[...] = full_ref[pl.ds(pl.multiple_of(192 * (h & 1), 16), 192), :]
        send_ref[...] = full_ref[384:512, :]


GAIN1, SHIFT1, BIAS1, GAIN2, SHIFT2, BIAS2, GAIN3, SHIFT3, QB, VB, PB = range(11)
VECS = 16


def vec(vec_ref, index):
    return vec_ref[index : index + 1, :]


def pack_kernel(bucket_ref, x_ref, cot_ref, kinds, away_x, home_x, away_c, home_c, sems):
    h, home, away = place(bucket_ref)
    kinds[0] = bucket_ref[0]
    kinds[1] = bucket_ref[1]

    def each(act):
        slot = 0
        for src, away_ref, home_ref in ((x_ref, away_x, home_x), (cot_ref, away_c, home_c)):
            for facts, dst, wide_rows in ((away, away_ref, 4), (home, home_ref, 6)):
                image, tall, stride, width = facts

                @pl.when(tall)
                def _():
                    for row in range(6):
                        act(
                            src.at[image, row, pl.ds(0, 16), :],
                            dst.at[pl.ds(16 * row, 16), :],
                            sems.at[slot + row],
                        )

                @pl.when(jnp.logical_not(tall))
                def _():
                    for row in range(wide_rows):
                        act(src.at[image, row], dst.at[pl.ds(32 * row, 32), :], sems.at[slot + row])

                slot += 6

    each(lambda a, b, sem: pltpu.make_async_copy(a, b, sem).start())
    each(lambda a, b, sem: pltpu.make_async_copy(a, b, sem).wait())


def first_kernel(
    bucket_ref, own, partner, received, partner_received, vecs, weight1,
    image_ref, conv_ref, act2_ref, stats_ref, act1_t, act2_t, send1_t, send2_t,
    shift_ref,
):
    h, home, away = place(bucket_ref)
    stride = home[2]
    mask, pixels = pixel_mask(home)
    channels = vecs.shape[1]
    group_size = pixels * (channels // GROUPS)
    assemble(image_ref, home, h, (own, partner, received, partner_received))
    values = image_ref[...].astype(F32) * mask
    mean1, inverse1 = norm_stats(values, mask, group_size)
    act = silu_norm(values, mean1, inverse1, vec(vecs, GAIN1), vec(vecs, SHIFT1), mask)
    fill_shifts(shift_ref, act, stride)
    act1_t[...] = act.astype(BF16).T
    conv_forward(shift_ref, weight1, stride, conv_ref)
    values = (conv_ref[...] + vec(vecs, BIAS1)) * mask
    conv_ref[...] = values
    mean2, inverse2 = norm_stats(values, mask, group_size)
    act = silu_norm(values, mean2, inverse2, vec(vecs, GAIN2), vec(vecs, SHIFT2), mask)
    act = act.astype(BF16)
    act2_ref[...] = act
    act2_t[...] = act.T
    half = pl.multiple_of((h & 1) * (channels // 2), 16)
    send1_t[...] = act1_t[pl.ds(half, channels // 2), :]
    send2_t[...] = act2_t[pl.ds(half, channels // 2), :]
    stats_ref[0:1, :] = mean1
    stats_ref[1:2, :] = inverse1
    stats_ref[2:3, :] = mean2
    stats_ref[3:4, :] = inverse2
    stats_ref[4:8, :] = jnp.zeros((4, channels), F32)


def second_kernel(
    bucket_ref, image_ref, act2_ref, own, partner, received, partner_received, vecs,
    weight2, wq, wk, wv, wp,
    out_own, out_send, grad2_ref, grad_middle_ref, attn_keep, attn_send, vec_ref,
    block_keep, block_send,
    shift_ref, full_ref, middle_ref, grads_ref, sum_ref,
):
    h, home, away = place(bucket_ref)
    stride = home[2]
    mask, pixels = pixel_mask(home)
    channels = vecs.shape[1]
    group_size = pixels * (channels // GROUPS)
    scaling = channels ** (-0.5)
    fill_shifts(shift_ref, act2_ref[...].astype(F32), stride)
    conv_forward(shift_ref, weight2, stride, middle_ref)
    middle = mask * (image_ref[...].astype(F32) + (middle_ref[...] + vec(vecs, BIAS2)))
    middle_ref[...] = middle
    mean3, inverse3 = norm_stats(middle, mask, group_size)
    normal = (middle - mean3) * inverse3
    normed = (normal * vec(vecs, GAIN3) + vec(vecs, SHIFT3)).astype(BF16)
    wide = jnp.concatenate([wq[...], wk[...], wv[...]], axis=1)
    joint = mm(normed, wide)
    queries = (joint[:, 0:channels] + vec(vecs, QB)).astype(BF16)
    keys = joint[:, channels : 2 * channels].astype(BF16)
    values = (joint[:, 2 * channels :] + vec(vecs, VB)).astype(BF16)
    lanes = lax.broadcasted_iota(jnp.int32, (1, PIX), 1)
    key_cols = lanes & (stride - 1)
    key_valid = (key_cols < home[3]) & (lanes < jnp.where(home[1], 384, 512))
    scores = jnp.where(key_valid, mm_nt(queries, keys) * scaling, -1000000000.0)
    raised = jnp.exp(scores - jnp.max(scores, axis=1, keepdims=True))
    soft = raised * (1.0 / jnp.sum(raised, axis=1, keepdims=True))
    soft16 = soft.astype(BF16)
    mixed = mm(soft16, values).astype(BF16)
    projected = mm(mixed, wp[...]) + vec(vecs, PB)
    full_ref[...] = (mask * (middle_ref[...] + projected)).astype(BF16)
    split_out(full_ref, home, h, out_own, out_send)

    assemble(full_ref, home, h, (own, partner, received, partner_received))
    grad_top = full_ref[...].astype(F32) * mask
    grad_rows = grad_top.astype(BF16)
    grad_mixed = mm_nt(grad_rows, wp[...]).astype(BF16)
    grad_soft = mm_nt(grad_mixed, values)
    grad_values = mm_tn(soft16, grad_mixed).astype(BF16)
    grad_scores = soft * (grad_soft - jnp.sum(soft * grad_soft, axis=1, keepdims=True))
    grad_scores = grad_scores.astype(BF16)
    grad_queries = (mm(grad_scores, keys) * scaling).astype(BF16)
    grad_keys = (mm_tn(grad_scores, queries) * scaling).astype(BF16)
    grads_ref[:, 0:channels] = grad_queries
    grads_ref[:, channels : 2 * channels] = grad_keys
    grads_ref[:, 2 * channels : 3 * channels] = grad_values
    grads_ref[:, 3 * channels : 4 * channels] = grad_rows
    grad_normed = mm_nt(grads_ref[:, 0 : 3 * channels], wide)
    grad_in, gain_grad, shift_grad = norm_back(
        grad_normed, normal, inverse3, mask, group_size, vec(vecs, GAIN3)
    )
    grad_middle = mask * (grad_top + grad_in)
    grad_middle_ref[...] = grad_middle
    grad2 = grad_middle.astype(BF16)
    grad2_ref[...] = grad2
    vec_ref[0:1, :] = gain_grad
    vec_ref[1:2, :] = shift_grad
    vec_ref[2:3, :] = total(grad_queries.astype(F32))
    vec_ref[3:4, :] = total(grad_values.astype(F32))
    vec_ref[4:5, :] = total(grad_top)
    vec_ref[5:6, :] = total(grad2.astype(F32))
    vec_ref[6:8, :] = jnp.zeros((2, channels), F32)

    keep_at = pl.multiple_of(BLK * h, BLK)
    send_at = pl.multiple_of(BLK * (h ^ 2), BLK)
    block_keep[...] = grad2_ref[:, pl.ds(keep_at, BLK)]
    block_send[...] = grad2_ref[:, pl.ds(send_at, BLK)]

    def blocks(index):
        start = index * channels
        return [
            grads_ref[:, pl.ds(pl.multiple_of(start + BLK * h, BLK), BLK)],
            grads_ref[:, pl.ds(pl.multiple_of(start + BLK * (h ^ 2), BLK), BLK)],
        ]

    sum_ref[:, 0 : 6 * BLK] = mm_tn(normed, jnp.concatenate(blocks(0) + blocks(1) + blocks(2), axis=1))
    sum_ref[:, 6 * BLK : 8 * BLK] = mm_tn(mixed, jnp.concatenate(blocks(3), axis=1))
    mine = lax.axis_index("batch") & 1
    pairs = attn_keep.shape[0]
    rows = channels // (2 * pairs)
    for pair in range(pairs):
        for dst, which in ((attn_keep, mine), (attn_send, 1 - mine)):
            part = sum_ref[pl.ds(pl.multiple_of((2 * pair + which) * rows, 8), rows), :].astype(BF16)
            for index in range(4):
                dst[pair, index * rows : (index + 1) * rows, :] = part[:, index * 2 * BLK : (index + 1) * 2 * BLK]


def third_kernel(
    bucket_ref, grad2_ref, conv_ref, stats_ref, vecs, weight2,
    grad1_ref, block_keep, block_send, vec_ref,
    shift_ref, acc_ref,
):
    h, home, away = place(bucket_ref)
    stride = home[2]
    mask, pixels = pixel_mask(home)
    channels = vecs.shape[1]
    group_size = pixels * (channels // GROUPS)
    fill_shifts(shift_ref, grad2_ref[...].astype(F32), stride)
    conv_backward(shift_ref, weight2, stride, acc_ref)
    inverse = stats_ref[3:4, :]
    normal = (conv_ref[...] - stats_ref[2:3, :]) * inverse
    u = normal * vec(vecs, GAIN2) + vec(vecs, SHIFT2)
    grad = mask * acc_ref[...] * silu_slope(u)
    grad_in, gain_grad, shift_grad = norm_back(
        grad, normal, inverse, mask, group_size, vec(vecs, GAIN2)
    )
    grad1 = grad_in.astype(BF16)
    grad1_ref[...] = grad1
    vec_ref[0:1, :] = gain_grad
    vec_ref[1:2, :] = shift_grad
    vec_ref[2:3, :] = total(grad1.astype(F32))
    vec_ref[3:8, :] = jnp.zeros((5, channels), F32)
    block_keep[...] = grad1_ref[:, pl.ds(pl.multiple_of(BLK * h, BLK), BLK)]
    block_send[...] = grad1_ref[:, pl.ds(pl.multiple_of(BLK * (h ^ 2), BLK), BLK)]


def fourth_kernel(
    bucket_ref, grad1_ref, image_ref, stats_ref, grad_middle_ref, vecs, weight1, vec_a, vec_b,
    grad_own, grad_send, vec_out,
    shift_ref, acc_ref, full_ref, vec_ref,
):
    h, home, away = place(bucket_ref)
    stride = home[2]
    mask, pixels = pixel_mask(home)
    channels = vecs.shape[1]
    group_size = pixels * (channels // GROUPS)
    fill_shifts(shift_ref, grad1_ref[...].astype(F32), stride)
    conv_backward(shift_ref, weight1, stride, acc_ref)
    inverse = stats_ref[1:2, :]
    normal = (image_ref[...].astype(F32) * mask - stats_ref[0:1, :]) * inverse
    u = normal * vec(vecs, GAIN1) + vec(vecs, SHIFT1)
    grad = mask * acc_ref[...] * silu_slope(u)
    grad_in, gain_grad, shift_grad = norm_back(
        grad, normal, inverse, mask, group_size, vec(vecs, GAIN1)
    )
    full_ref[...] = (mask * (grad_middle_ref[...] + grad_in)).astype(BF16)
    split_out(full_ref, home, h, grad_own, grad_send)
    vec_ref[0:6, :] = vec_a[0:6, :]
    vec_ref[6:9, :] = vec_b[0:3, :]
    vec_ref[9:10, :] = gain_grad
    vec_ref[10:11, :] = shift_grad
    vec_ref[11:VECS, :] = jnp.zeros((VECS - 11, channels), F32)
    batches = vec_out.shape[0]
    rows = channels // batches
    for shard in range(batches):
        start = shard * rows
        tile = start // BLK * BLK
        part = vec_ref[:, tile : tile + BLK]
        if start > tile:
            part = pltpu.roll(part, BLK - (start - tile), 1)
        vec_out[shard] = part


def weight_kernel(
    bucket_ref, act_t, half_t, partner_half_t, block_own, block_away, *rest, tail
):
    vec_in = rest[0] if tail else None
    keep_ref, send_ref, left_ref, right_ref, shift_ref, sum_ref = rest[tail:]
    h, home, away = place(bucket_ref)
    channels = act_t.shape[0]
    half = channels // 2
    left_ref[:, 0:PIX] = act_t[...]
    left_ref[pl.ds(pl.multiple_of((h & 1) * half, 16), half), PIX : 2 * PIX] = half_t[...]
    left_ref[pl.ds(pl.multiple_of((1 - (h & 1)) * half, 16), half), PIX : 2 * PIX] = (
        partner_half_t[...]
    )
    for index, (facts, block) in enumerate(((home, block_own), (away, block_away))):
        stride = facts[2]
        fill_shifts(shift_ref, block[...].astype(F32), stride)
        for p in range(3):
            for q in range(3):
                column = (3 * p + q) * BLK
                right_ref[index * PIX : (index + 1) * PIX, column : column + BLK] = tap(
                    shift_ref, 2 - p, 2 - q, stride
                )
    joint = mm(left_ref[...], right_ref[...])
    for t in range(9):
        sum_ref[t * channels : (t + 1) * channels, :] = joint[:, t * BLK : (t + 1) * BLK]
    mine = lax.axis_index("batch") & 1
    pairs = keep_ref.shape[0]
    rows = 9 * channels // (2 * pairs)
    for pair in range(pairs):
        for dst, which in ((keep_ref, mine), (send_ref, 1 - mine)):
            shard = 2 * pair + which
            dst[pair, 0:rows, :] = sum_ref[pl.ds(pl.multiple_of(shard * rows, 8), rows), :].astype(BF16)
            if tail:
                dst[pair, rows : rows + VECS, :] = vec_in[shard].astype(BF16)


def route_kernel(bit, keep_ref, got_ref, own_ref, *out_refs):
    group = (lax.axis_index("batch") >> bit) & (len(out_refs))
    count = own_ref.shape[0]
    for step, dst in enumerate((own_ref,) + out_refs):
        which = group ^ step
        for index in range(count):
            at = index * (len(out_refs) + 1) + which
            dst[index] = (keep_ref[at].astype(F32) + got_ref[at].astype(F32)).astype(BF16)


def join_kernel(own_ref, far_ref, near_ref, diagonal_ref, out_ref, *tail_ref):
    h = lax.axis_index("height")
    rows = out_ref.shape[0]
    for ref, index in ((own_ref, h), (far_ref, h ^ 2), (near_ref, h ^ 1), (diagonal_ref, h ^ 3)):
        out_ref[:, pl.ds(pl.multiple_of(BLK * index, BLK), BLK)] = ref[0:rows, :].astype(F32)
    if tail_ref:
        own, far = own_ref[rows:, :].astype(F32), far_ref[rows:, :].astype(F32)
        near, diagonal = near_ref[rows:, :].astype(F32), diagonal_ref[rows:, :].astype(F32)
        tail_ref[0][...] = 0.5 * ((own + near) + (far + diagonal))


def join_attn_kernel(own_ref, far_ref, near_ref, diagonal_ref, *out_refs):
    h = lax.axis_index("height")
    rows = out_refs[0].shape[0]
    for first, second, index in ((own_ref, far_ref, h), (near_ref, diagonal_ref, h ^ 1)):
        for position in range(2):
            lane, other = position * BLK, (1 - position) * BLK
            column = pl.multiple_of(BLK * (index ^ (2 * position)), BLK)
            for number, dst in enumerate(out_refs):
                at = number * rows
                dst[:, pl.ds(column, BLK)] = first[at : at + rows, lane : lane + BLK].astype(
                    F32
                ) + second[at : at + rows, other : other + BLK].astype(F32)


def unpack_kernel(bucket_ref, out_own, out_away, grad_own, grad_away, out_ref, grad_ref):
    h, home, away = place(bucket_ref)
    for own, received, dst in ((out_own, out_away, out_ref), (grad_own, grad_away, grad_ref)):
        channels = dst.shape[3]
        for facts, src, wide_rows in ((away, received, 4), (home, own, 6)):
            image, tall, stride, width = facts

            @pl.when(tall)
            def _():
                for row in range(6):
                    dst[image, row, 0:16, :] = src[16 * row : 16 * row + 16, :]
                    dst[image, row, 16:32, :] = jnp.zeros((16, channels), dst.dtype)

            @pl.when(jnp.logical_not(tall))
            def _():
                for row in range(wide_rows):
                    dst[image, row] = src[32 * row : 32 * row + 32, :]
                for row in range(wide_rows, 6):
                    dst[image, row] = jnp.zeros((32, channels), dst.dtype)

            if wide_rows == 4:

                @pl.when(jnp.logical_not(tall) & (h == 3))
                def _():
                    for row in range(6):
                        dst[image, row] = jnp.zeros((32, channels), dst.dtype)


def call(kernel, name, outs, scratch, vmem, *operands, smem=1, any_from=99):
    specs = [SM] * smem + [VM] * (len(operands) - smem)
    specs = [HB if i >= any_from else spec for i, spec in enumerate(specs)]
    return pl.pallas_call(
        kernel,
        name=name,
        out_shape=[jax.ShapeDtypeStruct(shape, dtype) for shape, dtype in outs],
        in_specs=specs,
        out_specs=[SM if dtype == jnp.int32 else VM for shape, dtype in outs],
        scratch_shapes=[
            pltpu.SemaphoreType.DMA(shape) if dtype is None else pltpu.VMEM(shape, dtype)
            for shape, dtype in scratch
        ],
        compiler_params=pltpu.CompilerParams(vmem_limit_bytes=vmem << 20),
        cost_estimate=pl.CostEstimate(
            flops=LENGTH.get(name, 1) * RATE, bytes_accessed=1024, transcendentals=0
        ),
    )(*operands)


def on_device(
    inputs,
    bucket,
    norm1_gain,
    norm1_shift,
    conv1_weight,
    conv1_bias,
    norm2_gain,
    norm2_shift,
    conv2_weight,
    conv2_bias,
    norm3_gain,
    norm3_shift,
    query_weight,
    query_bias,
    key_weight,
    value_weight,
    value_bias,
    proj_weight,
    proj_bias,
    cotangent,
):
    C = inputs.shape[-1]
    batches = lax.axis_size("batch")
    bits = batches.bit_length() - 1
    shard_rows = 9 * C // batches
    small_rows = C // batches

    def to_core(v):
        return lax.ppermute(v, "height", [(i, i ^ 1) for i in range(4)])

    def to_chip(v):
        return lax.ppermute(v, "height", [(i, i ^ 2) for i in range(4)])

    def to_batch(v, change):
        return lax.ppermute(v, "batch", [(i, i ^ change) for i in range(batches)])

    def after(v, *others):
        return lax.optimization_barrier((v,) + others)[0]

    img16 = ((PIX, C), BF16)
    img32 = ((PIX, C), F32)
    rows8 = ((8, C), F32)
    block = ((PIX, BLK), BF16)
    turned = ((C, PIX), BF16)
    half = ((C // 2, PIX), BF16)
    shifts = ((3, PIX + 2 * PAD, C), BF16)

    kinds, away_x, home_x, away_c, home_c = call(
        pack_kernel, "pack",
        [((2,), jnp.int32), ((128, C), BF16), ((192, C), BF16), ((128, C), BF16), ((192, C), BF16)],
        [((24,), None)], 8, bucket, inputs, cotangent, any_from=1,
    )
    vecs = jnp.stack(
        [
            norm1_gain, norm1_shift, conv1_bias, norm2_gain, norm2_shift, conv2_bias,
            norm3_gain, norm3_shift, query_bias, value_bias, proj_bias,
        ]
    )
    recv_x = to_chip(away_x)
    core_x = to_core(home_x)
    recv_c = to_chip(away_c)
    core_c = to_core(home_c)
    core_recv_x = to_core(recv_x)
    core_recv_c = to_core(recv_c)

    image, conv, act2, stats, act1_t, act2_t, send1_t, send2_t = call(
        first_kernel, "first",
        [img16, img32, img16, rows8, turned, turned, half, half],
        [shifts], 24,
        kinds, home_x, core_x, recv_x, core_recv_x, vecs, conv1_weight,
    )
    half_t = [to_chip(v) for v in (send1_t, send2_t)]
    core_half_t = [to_core(v) for v in half_t]

    attn_out = ((batches // 2, 4 * small_rows, 2 * BLK), BF16)
    out_own, out_send, grad2, grad_middle, attn_keep, attn_send, vec_a, block2, block2_send = call(
        second_kernel, "second",
        [((192, C), BF16), ((128, C), BF16), img16, img32, attn_out, attn_out, rows8, block, block],
        [shifts, img16, img32, ((PIX, 4 * C), BF16), ((C, 8 * BLK), F32)], 32,
        kinds, image, act2, home_c, core_c, recv_c, core_recv_c, vecs,
        conv2_weight, query_weight, key_weight, value_weight, proj_weight,
    )
    block2_away = to_chip(block2_send)
    out_away = to_chip(out_send)
    attn_got = to_batch(attn_send, 1)

    grad1, block1, block1_send, vec_b = call(
        third_kernel, "third",
        [img16, block, block, rows8],
        [shifts, img32], 24,
        kinds, grad2, conv, stats, vecs, conv2_weight,
    )
    block1_away = to_chip(block1_send)

    def weight_grad(name, act_t, index, own, away, *tail):
        rows = shard_rows + (VECS if tail else 0)
        return call(
            functools.partial(weight_kernel, tail=len(tail)), name,
            [((batches // 2, rows, BLK), BF16)] * 2,
            [((C, 2 * PIX), BF16), ((2 * PIX, 9 * BLK), BF16), ((3, PIX + 2 * PAD, BLK), BF16),
             ((9 * C, BLK), F32)],
            24, kinds, act_t, half_t[index], core_half_t[index], own, away, *tail,
        )

    keep2, send2 = weight_grad("weight2", act2_t, 1, after(block2, block1), block2_away)
    got2 = to_batch(send2, 1)

    grad_own, grad_send, vec_c = call(
        fourth_kernel, "fourth",
        [((192, C), BF16), ((128, C), BF16), ((batches, VECS, BLK), F32)],
        [shifts, img32, img16, ((VECS, C), F32)], 24,
        kinds, after(grad1, send2), image, stats, grad_middle, vecs, conv1_weight, vec_a, vec_b,
    )
    grad_away = to_chip(grad_send)
    keep1, send1 = weight_grad("weight1", act1_t, 0, block1, block1_away, vec_c)
    got1 = to_batch(send1, 1)

    def scatter(name, keep, got):
        bit = 1
        while bit < bits:
            width = min(2, bits - bit)
            ways = 1 << width
            shape = (keep.shape[0] // ways,) + keep.shape[1:]
            parts = call(
                functools.partial(route_kernel, bit), name + str(bit),
                [(shape, BF16)] * ways, [], 16, keep, got, smem=0,
            )
            got = [to_batch(parts[j], j << bit) for j in range(1, ways)]
            bit += width
            if bit < bits:
                keep = parts[0]
                got = functools.reduce(lambda a, b: a + b, [g.astype(F32) for g in got]).astype(BF16)
            else:
                added = parts[0].astype(F32)
                for g in got:
                    added = added + g.astype(F32)
                return added.astype(BF16)[0]

    def gather(shard):
        far = to_chip(shard)
        near = to_core(shard)
        return shard, far, near, to_core(far)

    attn_parts = gather(scatter("routea", after(attn_keep, send1), attn_got))
    parts2 = gather(scatter("routeb", keep2, got2))
    parts1 = gather(scatter("routec", keep1, got1))
    small = call(
        join_attn_kernel, "joina", [((small_rows, C), F32)] * 4, [], 8, *attn_parts, smem=0
    )
    (whole2,) = call(join_kernel, "joinb", [((shard_rows, C), F32)], [], 8, *parts2, smem=0)
    whole1, sums = call(
        join_kernel, "joinc", [((shard_rows, C), F32), ((VECS, BLK), F32)], [], 8, *parts1, smem=0
    )
    v = [sums[i, :small_rows] for i in range(11)]

    outputs, input_grad = call(
        unpack_kernel, "unpack",
        [(inputs.shape, BF16)] * 2, [], 8,
        kinds, out_own, out_away, grad_own, grad_away,
    )
    return (
        outputs, input_grad,
        v[9], v[10], whole1, v[8],
        v[6], v[7], whole2, v[5],
        v[0], v[1],
        small[0], v[2], small[1], small[2], v[3], small[3], v[4],
    )


def solution(mesh):
    image = P("batch", "height", None, None)
    vector = P("batch")
    matrix = P("batch", None)
    return jax.shard_map(
        on_device,
        mesh=mesh,
        in_specs=(image, vector) + (P(),) * 17 + (image,),
        out_specs=(
            image, image,
            vector, vector, matrix, vector,
            vector, vector, matrix, vector,
            vector, vector,
            matrix, vector, matrix, matrix, vector, matrix, vector,
        ),
        check_vma=False,
    )
```

time: 138 us -> 115 us (0.83)
  waiting for transfers between devices: 46.5 us -> 32.9 us
  starting transfers between devices: 24.2 us -> 33.7 us
  other arithmetic: 9.29 us -> 0.25 us
  Pallas kernels: 45.1 us -> 39.6 us
  local copies, waits for them, and re-layouts: 11 us -> 7.12 us
    ppermute x6 -> x12, waiting for transfers between devices: 29.8 us -> 20.3 us  [to_batch(): return lax.ppermute(v, 'batch', [(i, i ^ change) for i in range(batches)])]
    convert_element_type x9 -> x0, other arithmetic: 6.3 us -> none  [the longest x6 3.91 us: scatter(): added = (keep.astype(F32) + got.astype(F32)).astype(BF16)]
    ppermute x6 -> x12, starting transfers between devices: 11.9 us -> 17.7 us  [to_batch(): return lax.ppermute(v, 'batch', [(i, i ^ change) for i in range(batches)])]
    pallas_call x8 -> x14, Pallas kernels: 45.1 us -> 39.6 us  [call(): pl.pallas_call(kernel, name=name, out_shape=[jax.ShapeDtypeStruct(shape,...]
    ppermute x10 -> x11, waiting for transfers between devices: 15.6 us -> 12.6 us  [to_chip(): return lax.ppermute(v, 'height', [(i, i ^ 2) for i in range(4)])]
    ppermute x10 -> x11, starting transfers between devices: 11.6 us -> 14.6 us  [to_chip(): return lax.ppermute(v, 'height', [(i, i ^ 2) for i in range(4)])]
    unnamed x60 -> x22, local copies, waits for them, and re-layouts: 7.6 us -> 5.01 us
    concatenate x3 -> x0, other arithmetic: 1.84 us -> none  [the longest x1 0.96 us: on_device(): jnp.concatenate([send2, lay(attn_other)], axis=1)]
  transfers between devices with their start and end apart: 23 -> 35, of which waited for: 10 -> 10; matrix products, arithmetic and copies ran while one was open for 8% -> 2% of each run, Pallas kernels for 32% -> 32%
where the time goes in v2:
time: 115 us; the launch traced here: 114 us
  Pallas kernels  39.6 us (34%)
  starting transfers between devices  33.7 us (29%)
  waiting for transfers between devices  32.9 us (29%)
  local copies, waits for them, and re-layouts  7.12 us (6%)
    pallas_call x14, Pallas kernels, call(): pl.pallas_call(kernel, name=name, out_shape=[jax.ShapeDtypeStruct(shape,...  39.6 us
    ppermute x12, waiting for transfers between devices, to_batch(): return lax.ppermute(v, 'batch', [(i, i ^ change) for i in range(batches)])  20.3 us
    ppermute x12, starting transfers between devices, to_batch(): return lax.ppermute(v, 'batch', [(i, i ^ change) for i in range(batches)])  17.7 us
    ppermute x11, starting transfers between devices, to_chip(): return lax.ppermute(v, 'height', [(i, i ^ 2) for i in range(4)])  14.6 us
    ppermute x11, waiting for transfers between devices, to_chip(): return lax.ppermute(v, 'height', [(i, i ^ 2) for i in range(4)])  12.6 us
    unnamed x22, local copies, waits for them, and re-layouts  5.01 us
  transfers between devices with their start and end apart: 35, of which 10 were waited for; matrix products, arithmetic and copies ran while one was open for 2% of the time, Pallas kernels for 32%

profile of v2, /device:TPU:0, one launch (start us, length us, event | category | flops | bytes accessed | tf_op | source)
XLA Modules:
  0.0 114.4 jit_solution(9867175186484612406)
XLA Ops:
  0.7 1.0 copy-done.6
  1.7 1.0 copy-done.7
  2.7 0.7 copy-done.8
  3.3 2.2 %pack.1 = (s32[2]{0:T(128)S(1)}, bf16[128,512]{1,0:T(8,128)(2,1)S(1)}, bf16[192,512]{1,0:T(8,128)(2,1)S(1)}, bf16[128,512]{1,0:T(8,128)(2,1)S(1)}, bf16[192,512]{1,0:T(8,128)(2,1)S(1)}) custom-call(s32[2]{0:T(128)S(1)} %copy-done.8, bf16[2,6,32,512]{3,2,1,0:T(8,128)(2,1)S(1)} %copy-done.6, bf16[2,6,32,512]{3,2,1,0:T(8,128)(2,1)S(1)} %copy-done.7), custom_call_target="tpu_custom_call" | custom-call | flops 1073741824 | bytes 1024 | tf_op jit(solution)/shard_map/pack/pallas_call | solution.py:541
  5.5 2.9 %collective-permute-start.1 = (bf16[128,512]{1,0:T(8,128)(2,1)S(1)}, bf16[128,512]{1,0:T(8,128)(2,1)S(1)}, u32[]{:S(2)}, u32[]{:S(2)}) collective-permute-start(bf16[128,512]{1,0:T(8,128)(2,1)S(1)} %get-tuple-element.77), channel_id=1, source_target_pairs={{0,2},{1,3},{2,0},{3,1},{4,6},{5,7},{6,4},{7,5},{8,10},{9,11},{10,... | collective-permute-start | bytes 393224 | tf_op jit(solution)/shard_map/ppermute | solution.py:590
  8.4 0.0 collective-permute-start
  8.4 0.2 collective-permute-start.4
  8.5 3.7 %collective-permute-done.1.received = bf16[128,512]{1,0:T(8,128)(2,1)S(1)} collective-permute-done((bf16[128,512]{1,0:T(8,128)(2,1)S(1)}, bf16[128,512]{1,0:T(8,128)(2,1)S(1)}, u32[]{:S(2)}, u32[]{:S(2)}) %collective-permute-start.1) | collective-permute-done | bytes 131104 | tf_op jit(solution)/shard_map/ppermute | solution.py:590
  12.3 0.5 collective-permute-start.3
  12.8 1.6 %stack.47.vecs = f32[11,512]{1,0:T(8,128)S(1)} concatenate(f32[1,512]{1,0:T(1,128)} %bitcast.41, f32[1,512]{1,0:T(1,128)} %bitcast.42, f32[1,512]{1,0:T(1,128)} %bitcast.43, f32[1,512]{1,0:T(1,128)} %bitcast.44, f32[1,512]{1,0:T(1,128)} %bitcast.45, f32[1,512]{1,0:T(1,128)} %bitcast.46, f32[1,512]{1,0:T(1,128)} %bitcast.47, f32[1,512]{1,0:T(1,128)} %bitcast.48, ...), dimensions={0} | concatenate | bytes 45056 | tf_op jit(solution)/shard_map/stack | solution.py:611
  14.4 0.3 collective-permute-done.4.received
  14.7 0.0 copy-start.1
  14.7 2.3 %copy-done.1 = bf16[4608,512]{1,0:T(8,128)(2,1)S(1)} copy-done((bf16[4608,512]{1,0:T(8,128)(2,1)S(1)}, bf16[4608,512]{1,0:T(8,128)(2,1)}, u32[]{:S(2)}) %copy-start.1) | copy-done | bytes 4718616
  17.0 0.0 copy-start.5
  17.1 0.0 slice-start
  17.1 5.9 %first.1 = (bf16[512,512]{1,0:T(8,128)(2,1)S(1)}, f32[512,512]{1,0:T(8,128)S(1)}, bf16[512,512]{1,0:T(8,128)(2,1)S(1)}, f32[8,512]{1,0:T(8,128)S(1)}, bf16[512,5...) custom-call(s32[2]{0:T(128)S(1)} %get-tuple-element.75.bucket_ref, ...), custom_call_target="tpu_custom_call" | custom-call | flops 6442450944 | bytes 1024 | tf_op jit(solution)/shard_map/first/pallas_call | solution.py:541
  23.0 2.3 %collective-permute-start.7 = (bf16[256,512]{1,0:T(8,128)(2,1)S(1)}, bf16[256,512]{1,0:T(8,128)(2,1)S(1)}, u32[]{:S(2)}, u32[]{:S(2)}) collective-permute-start(bf16[256,512]{1,0:T(8,128)(2,1)S(1)} %get-tuple-element.89), channel_id=1, source_target_pairs={{0,2},{1,3},{2,0},{3,1},{4,6},{5,7},{6,4},{7,5},{8,10},{9,11},{10,... | collective-permute-start | bytes 786440 | tf_op jit(solution)/shard_map/ppermute | solution.py:590
  25.3 0.0 slice-start.1
  25.3 10.5 %second.1 = (bf16[192,512]{1,0:T(8,128)(2,1)S(1)}, bf16[128,512]{1,0:T(8,128)(2,1)S(1)}, bf16[512,512]{1,0:T(8,128)(2,1)S(1)}, f32[512,512]{1,0:T(8,128)S(1)}, b...) custom-call(s32[2]{0:T(128)S(1)} %get-tuple-element.75.bucket_ref, ...), custom_call_target="tpu_custom_call" | custom-call | flops 11811160064 | bytes 1024 | tf_op jit(solution)/shard_map/second/pallas_call | solution.py:541
  35.9 0.1 collective-permute-start.9
  35.9 2.0 %collective-permute-start.11 = (bf16[256,512]{1,0:T(8,128)(2,1)S(1)}, bf16[256,512]{1,0:T(8,128)(2,1)S(1)}, u32[]{:S(2)}, u32[]{:S(2)}) collective-permute-start(bf16[256,512]{1,0:T(8,128)(2,1)S(1)} %get-tuple-element.104), channel_id=1, source_target_pairs={{0,2},{1,3},{2,0},{3,1},{4,6},{5,7},{6,4},{7,5},{8,10},{9,11},{10,... | collective-permute-start | bytes 786440 | tf_op jit(solution)/shard_map/ppermute | solution.py:590
  38.0 4.6 %third.1 = (bf16[512,512]{1,0:T(8,128)(2,1)S(1)}, bf16[512,128]{1,0:T(8,128)(2,1)S(1)}, bf16[512,128]{1,0:T(8,128)(2,1)S(1)}, f32[8,512]{1,0:T(8,128)S(1)}) custom-call(s32[2]{0:T(128)S(1)} %get-tuple-element.75.bucket_ref, bf16[512,512]{1,0:T(8,128)(2,1)S(1)} %get-tuple-element.84.grad2_ref, f32[512,512]{1,0:T(8,128)S(1)} %get-tuple-element.85.conv_ref, ...), custom_call_target="tpu_custom_call" | custom-call | flops 5368709120 | bytes 1024 | tf_op jit(solution)/shard_map/third/pallas_call | solution.py:541
  42.5 0.2 collective-permute-start.13
  42.7 1.7 %collective-permute-start.28 = (bf16[4,256,256]{2,1,0:T(8,128)(2,1)S(1)}, bf16[4,256,256]{2,1,0:T(8,128)(2,1)S(1)}, u32[]{:S(2)}, u32[]{:S(2)}) collective-permute-start(bf16[4,256,256]{2,1,0:T(8,128)(2,1)S(1)} %get-tuple-element.122), channel_id=1, source_target_pairs={{0,4},{4,0},{8,12},{12,8},{16,20},{20,16},{24,28},{28,24},{1,5},{5... | collective-permute-start | bytes 1572872 | tf_op jit(solution)/shard_map/ppermute | solution.py:593
  44.4 3.4 %collective-permute-done.11.half_t = bf16[256,512]{1,0:T(8,128)(2,1)S(1)} collective-permute-done((bf16[256,512]{1,0:T(8,128)(2,1)S(1)}, bf16[256,512]{1,0:T(8,128)(2,1)S(1)}, u32[]{:S(2)}, u32[]{:S(2)}) %collective-permute-start.11) | collective-permute-done | bytes 262176 | tf_op jit(solution)/shard_map/ppermute | solution.py:590
  47.9 3.1 %weight2.5 = (bf16[4,576,128]{2,1,0:T(8,128)(2,1)S(1)}, bf16[4,576,128]{2,1,0:T(8,128)(2,1)S(1)}) custom-call(s32[2]{0:T(128)S(1)} %get-tuple-element.75.bucket_ref, bf16[512,512]{1,0:T(8,128)(2,1)S(1)} %get-tuple-element.88.act_t, bf16[256,512]{1,0:T(8,128)(2,1)S(1)} %collective-permute-done.7.half_t, ...), custom_call_target="tpu_custom_call" | custom-call | flops 3221225472 | bytes 1024 | tf_op jit(solution)/shard_map/weight2/pallas_call | solution.py:541
  51.0 1.6 %collective-permute-start.21 = (bf16[4,576,128]{2,1,0:T(8,128)(2,1)S(1)}, bf16[4,576,128]{2,1,0:T(8,128)(2,1)S(1)}, u32[]{:S(2)}, u32[]{:S(2)}) collective-permute-start(bf16[4,576,128]{2,1,0:T(8,128)(2,1)S(1)} %get-tuple-element.94), channel_id=1, source_target_pairs={{0,4},{4,0},{8,12},{12,8},{16,20},{20,16},{24,28},{28,24},{1,5},{5... | collective-permute-start | bytes 1769480 | tf_op jit(solution)/shard_map/ppermute | solution.py:593
  52.6 5.0 %fourth.1 = (bf16[192,512]{1,0:T(8,128)(2,1)S(1)}, bf16[128,512]{1,0:T(8,128)(2,1)S(1)}, f32[8,16,128]{2,1,0:T(8,128)S(1)}) custom-call(s32[2]{0:T(128)S(1)} %get-tuple-element.75.bucket_ref, bf16[512,512]{1,0:T(8,128)(2,1)S(1)} %get-tuple-element.95.grad1_ref, bf16[512,512]{1,0:T(8,128)(2,1)S(1)} %get-tuple-element.78.image_ref, ...), custom_call_target="tpu_custom_call" | custom-call | flops 5368709120 | bytes 1024 | tf_op jit(solution)/shard_map/fourth/pallas_call | solution.py:541
  57.6 3.1 %weight1.5 = (bf16[4,592,128]{2,1,0:T(8,128)(2,1)S(1)}, bf16[4,592,128]{2,1,0:T(8,128)(2,1)S(1)}) custom-call(s32[2]{0:T(128)S(1)} %get-tuple-element.75.bucket_ref, bf16[512,512]{1,0:T(8,128)(2,1)S(1)} %get-tuple-element.103.act_t, bf16[256,512]{1,0:T(8,128)(2,1)S(1)} %collective-permute-done.11.half_t, ...), custom_call_target="tpu_custom_call" | custom-call | flops 3221225472 | bytes 1024 | tf_op jit(solution)/shard_map/weight1/pallas_call | solution.py:541
  60.7 0.6 collective-permute-start.14
  61.3 0.1 routea1.1
  61.4 1.7 %collective-permute-start.29 = (bf16[1,256,256]{2,1,0:T(8,128)(2,1)S(1)}, bf16[1,256,256]{2,1,0:T(8,128)(2,1)S(1)}, u32[]{:S(2)}, u32[]{:S(2)}) collective-permute-start(bf16[1,256,256]{2,1,0:T(8,128)(2,1)S(1)} %get-tuple-element.124), channel_id=1, source_target_pairs={{0,8},{4,12},{8,0},{12,4},{16,24},{20,28},{24,16},{28,20},{1,9},{5... | collective-permute-start | bytes 393224 | tf_op jit(solution)/shard_map/ppermute | solution.py:593
  63.1 2.6 %collective-permute-start.30 = (bf16[1,256,256]{2,1,0:T(8,128)(2,1)S(1)}, bf16[1,256,256]{2,1,0:T(8,128)(2,1)S(1)}, u32[]{:S(2)}, u32[]{:S(2)}) collective-permute-start(bf16[1,256,256]{2,1,0:T(8,128)(2,1)S(1)} %get-tuple-element.125), channel_id=1, source_target_pairs={{0,16},{4,20},{8,24},{12,28},{16,0},{20,4},{24,8},{28,12},{1,17},{... | collective-permute-start | bytes 393224 | tf_op jit(solution)/shard_map/ppermute | solution.py:593
  65.7 0.2 collective-permute-start.31
  65.9 4.1 %collective-permute-done.21.got_ref = bf16[4,576,128]{2,1,0:T(8,128)(2,1)S(1)} collective-permute-done((bf16[4,576,128]{2,1,0:T(8,128)(2,1)S(1)}, bf16[4,576,128]{2,1,0:T(8,128)(2,1)S(1)}, u32[]{:S(2)}, u32[]{:S(2)}) %collective-permute-start.21) | collective-permute-done | bytes 589856 | tf_op jit(solution)/shard_map/ppermute | solution.py:593
  70.0 2.0 %collective-permute-start.6 = (bf16[128,512]{1,0:T(8,128)(2,1)S(1)}, bf16[128,512]{1,0:T(8,128)(2,1)S(1)}, u32[]{:S(2)}, u32[]{:S(2)}) collective-permute-start(bf16[128,512]{1,0:T(8,128)(2,1)S(1)} %get-tuple-element.83), channel_id=1, source_target_pairs={{0,2},{1,3},{2,0},{3,1},{4,6},{5,7},{6,4},{7,5},{8,10},{9,11},{10,... | collective-permute-start | bytes 393224 | tf_op jit(solution)/shard_map/ppermute | solution.py:590
  72.0 0.1 routeb1.1
  72.2 1.6 %collective-permute-start.22 = (bf16[1,576,128]{2,1,0:T(8,128)(2,1)S(1)}, bf16[1,576,128]{2,1,0:T(8,128)(2,1)S(1)}, u32[]{:S(2)}, u32[]{:S(2)}) collective-permute-start(bf16[1,576,128]{2,1,0:T(8,128)(2,1)S(1)} %get-tuple-element.117), channel_id=1, source_target_pairs={{0,8},{4,12},{8,0},{12,4},{16,24},{20,28},{24,16},{28,20},{1,9},{5... | collective-permute-start | bytes 442376 | tf_op jit(solution)/shard_map/ppermute | solution.py:593
  73.8 2.2 %collective-permute-done.30 = bf16[1,256,256]{2,1,0:T(8,128)(2,1)S(1)} collective-permute-done((bf16[1,256,256]{2,1,0:T(8,128)(2,1)S(1)}, bf16[1,256,256]{2,1,0:T(8,128)(2,1)S(1)}, u32[]{:S(2)}, u32[]{:S(2)}) %collective-permute-start.30) | collective-permute-done | bytes 131104 | tf_op jit(solution)/shard_map/ppermute | solution.py:593
  76.0 0.4 collective-permute-start.23
  76.4 1.9 %collective-permute-start.24 = (bf16[1,576,128]{2,1,0:T(8,128)(2,1)S(1)}, bf16[1,576,128]{2,1,0:T(8,128)(2,1)S(1)}, u32[]{:S(2)}, u32[]{:S(2)}) collective-permute-start(bf16[1,576,128]{2,1,0:T(8,128)(2,1)S(1)} %get-tuple-element.119), channel_id=1, source_target_pairs={{0,24},{4,28},{8,16},{12,20},{16,8},{20,12},{24,0},{28,4},{1,25},{... | collective-permute-start | bytes 442376 | tf_op jit(solution)/shard_map/ppermute | solution.py:593
  78.3 0.1 fusion.2.own_ref
  78.4 4.2 %collective-permute-done.14.got_ref = bf16[4,592,128]{2,1,0:T(8,128)(2,1)S(1)} collective-permute-done((bf16[4,592,128]{2,1,0:T(8,128)(2,1)S(1)}, bf16[4,592,128]{2,1,0:T(8,128)(2,1)S(1)}, u32[]{:S(2)}, u32[]{:S(2)}) %collective-permute-start.14) | collective-permute-done | bytes 606240 | tf_op jit(solution)/shard_map/ppermute | solution.py:593
  82.6 1.7 %collective-permute-start.32 = (bf16[256,256]{1,0:T(8,128)(2,1)S(1)}, bf16[256,256]{1,0:T(8,128)(2,1)S(1)}, u32[]{:S(2)}, u32[]{:S(2)}) collective-permute-start(bf16[256,256]{1,0:T(8,128)(2,1)S(1)} %fusion.2.own_ref), channel_id=1, source_target_pairs={{0,2},{1,3},{2,0},{3,1},{4,6},{5,7},{6,4},{7,5},{8,10},{9,11},{10,... | collective-permute-start | bytes 393224 | tf_op jit(solution)/shard_map/ppermute | solution.py:590
  84.3 0.1 routec1.1
  84.5 3.1 %collective-permute-start.15 = (bf16[1,592,128]{2,1,0:T(8,128)(2,1)S(1)}, bf16[1,592,128]{2,1,0:T(8,128)(2,1)S(1)}, u32[]{:S(2)}, u32[]{:S(2)}) collective-permute-start(bf16[1,592,128]{2,1,0:T(8,128)(2,1)S(1)} %get-tuple-element.110), channel_id=1, source_target_pairs={{0,8},{4,12},{8,0},{12,4},{16,24},{20,28},{24,16},{28,20},{1,9},{5... | collective-permute-start | bytes 454664 | tf_op jit(solution)/shard_map/ppermute | solution.py:593
  87.5 0.8 collective-permute-done.23
  88.3 0.4 collective-permute-start.16
  88.7 1.9 %collective-permute-start.17 = (bf16[1,592,128]{2,1,0:T(8,128)(2,1)S(1)}, bf16[1,592,128]{2,1,0:T(8,128)(2,1)S(1)}, u32[]{:S(2)}, u32[]{:S(2)}) collective-permute-start(bf16[1,592,128]{2,1,0:T(8,128)(2,1)S(1)} %get-tuple-element.112), channel_id=1, source_target_pairs={{0,24},{4,28},{8,16},{12,20},{16,8},{20,12},{24,0},{28,4},{1,25},{... | collective-permute-start | bytes 454664 | tf_op jit(solution)/shard_map/ppermute | solution.py:593
  90.6 0.1 fusion.1.own_ref
  90.7 1.4 %collective-permute-start.10 = (bf16[128,512]{1,0:T(8,128)(2,1)S(1)}, bf16[128,512]{1,0:T(8,128)(2,1)S(1)}, u32[]{:S(2)}, u32[]{:S(2)}) collective-permute-start(bf16[128,512]{1,0:T(8,128)(2,1)S(1)} %get-tuple-element.100), channel_id=1, source_target_pairs={{0,2},{1,3},{2,0},{3,1},{4,6},{5,7},{6,4},{7,5},{8,10},{9,11},{10,... | collective-permute-start | bytes 393224 | tf_op jit(solution)/shard_map/ppermute | solution.py:590
  92.1 8.9 %collective-permute-done.16 = bf16[1,592,128]{2,1,0:T(8,128)(2,1)S(1)} collective-permute-done((bf16[1,592,128]{2,1,0:T(8,128)(2,1)S(1)}, bf16[1,592,128]{2,1,0:T(8,128)(2,1)S(1)}, u32[]{:S(2)}, u32[]{:S(2)}) %collective-permute-start.16) | collective-permute-done | bytes 151584 | tf_op jit(solution)/shard_map/ppermute | solution.py:593
  101.1 0.3 collective-permute-start.25
  101.4 0.1 fusion.own_ref
  101.5 0.3 collective-permute-start.26
  101.8 1.7 %collective-permute-start.18 = (bf16[592,128]{1,0:T(8,128)(2,1)S(1)}, bf16[592,128]{1,0:T(8,128)(2,1)S(1)}, u32[]{:S(2)}, u32[]{:S(2)}) collective-permute-start(bf16[592,128]{1,0:T(8,128)(2,1)S(1)} %fusion.own_ref), channel_id=1, source_target_pairs={{0,2},{1,3},{2,0},{3,1},{4,6},{5,7},{6,4},{7,5},{8,10},{9,11},{10,... | collective-permute-start | bytes 454664 | tf_op jit(solution)/shard_map/ppermute | solution.py:590
  103.5 4.2 %collective-permute-done.25.far_ref = bf16[576,128]{1,0:T(8,128)(2,1)S(1)} collective-permute-done((bf16[576,128]{1,0:T(8,128)(2,1)S(1)}, bf16[576,128]{1,0:T(8,128)(2,1)S(1)}, u32[]{:S(2)}, u32[]{:S(2)}) %collective-permute-start.25) | collective-permute-done | bytes 147488 | tf_op jit(solution)/shard_map/ppermute | solution.py:590
  107.7 1.5 %unpack.1 = (bf16[2,6,32,512]{3,2,1,0:T(8,128)(2,1)}, bf16[2,6,32,512]{3,2,1,0:T(8,128)(2,1)}) custom-call(s32[2]{0:T(128)S(1)} %get-tuple-element.75.bucket_ref, bf16[192,512]{1,0:T(8,128)(2,1)S(1)} %get-tuple-element.82.out_own, bf16[128,512]{1,0:T(8,128)(2,1)S(1)} %collective-permute-done.6.out_away, bf16[192,512]{1,0:T(8,128)(2,1)S(1)} %get-tuple-element.99.grad_own, ...), custom_call_target="tpu_custom_call" | custom-call | flops 2147483648 | bytes 1024 | tf_op jit(solution)/shard_map/unpack/pallas_call | solution.py:541
  109.2 0.5 collective-permute-start.19
  109.7 0.8 collective-permute-done.18.far_ref
  110.6 0.9 joina.1
  111.4 1.2 %joinb.1 = f32[576,512]{1,0:T(8,128)} custom-call(bf16[576,128]{1,0:T(8,128)(2,1)S(1)} %fusion.1.own_ref, bf16[576,128]{1,0:T(8,128)(2,1)S(1)} %collective-permute-done.25.far_ref, bf16[576,128]{1,0:T(8,128)(2,1)S(1)} %collective-permute-done.26.near_ref, bf16[576,128]{1,0:T(8,128)(2,1)S(1)} %collective-permute-done.27.diagonal_ref), custom_call_target="tpu_custom_call" | custom-call | flops 1073741824 | bytes 1024 | tf_op jit(solution)/shard_map/joinb/pallas_call | solution.py:541
  112.6 1.2 %joinc.1 = (f32[576,512]{1,0:T(8,128)}, f32[16,128]{1,0:T(8,128)S(1)}) custom-call(bf16[592,128]{1,0:T(8,128)(2,1)S(1)} %fusion.own_ref, bf16[592,128]{1,0:T(8,128)(2,1)S(1)} %collective-permute-done.18.far_ref, bf16[592,128]{1,0:T(8,128)(2,1)S(1)} %collective-permute-done.19.near_ref, bf16[592,128]{1,0:T(8,128)(2,1)S(1)} %collective-permute-done.20.diagonal_ref), custom_call_target="tpu_custom_call" | custom-call | flops 1073741824 | bytes 1024 | tf_op jit(solution)/shard_map/joinc/pallas_call | solution.py:541
  113.8 0.6 slice_bitcast_fusion
  (48 shorter events, 0.1 us)
Async XLA Ops:
  0.7 1.0 copy-start.6
  1.7 1.0 copy-start.7
  2.6 0.7 copy-start.8
  5.5 6.8 %collective-permute-start.1 = (bf16[128,512]{1,0:T(8,128)(2,1)S(1)}, bf16[128,512]{1,0:T(8,128)(2,1)S(1)}, u32[]{:S(2)}, u32[]{:S(2)}) collective-permute-start(bf16[128,512]{1,0:T(8,128)(2,1)S(1)} %get-tuple-element.77), channel_id=1, source_target_pairs={{0,2},{1,3},{2,0},{3,1},{4,6},{5,7},{6,4},{7,5},{8,10},{9,11},{10,... | collective-permute-start | bytes 393224 | tf_op jit(solution)/shard_map/ppermute | solution.py:590
  8.4 6.3 %collective-permute-start = (bf16[192,512]{1,0:T(8,128)(2,1)S(1)}, bf16[192,512]{1,0:T(8,128)(2,1)S(1)}, u32[]{:S(2)}, u32[]{:S(2)}) collective-permute-start(bf16[192,512]{1,0:T(8,128)(2,1)S(1)} %get-tuple-element.76.own), channel_id=1, source_target_pairs={{0,1},{1,0},{2,3},{3,2},{4,5},{5,4},{6,7},{7,6},{8,9},{9,8},{10,11... | collective-permute-start | bytes 589832 | tf_op jit(solution)/shard_map/ppermute | solution.py:587
  8.4 6.3 %collective-permute-start.4 = (bf16[128,512]{1,0:T(8,128)(2,1)S(1)}, bf16[128,512]{1,0:T(8,128)(2,1)S(1)}, u32[]{:S(2)}, u32[]{:S(2)}) collective-permute-start(bf16[128,512]{1,0:T(8,128)(2,1)S(1)} %get-tuple-element.81), channel_id=1, source_target_pairs={{0,2},{1,3},{2,0},{3,1},{4,6},{5,7},{6,4},{7,5},{8,10},{9,11},{10,... | collective-permute-start | bytes 393224 | tf_op jit(solution)/shard_map/ppermute | solution.py:590
  12.3 2.4 %collective-permute-start.2 = (bf16[128,512]{1,0:T(8,128)(2,1)S(1)}, bf16[128,512]{1,0:T(8,128)(2,1)S(1)}, u32[]{:S(2)}, u32[]{:S(2)}) collective-permute-start(bf16[128,512]{1,0:T(8,128)(2,1)S(1)} %collective-permute-done.1.received), channel_id=1, source_target_pairs={{0,1},{1,0},{2,3},{3,2},{4,5},{5,4},{6,7},{7,6},{8,9},{9,8},{10,11... | collective-permute-start | bytes 393224 | tf_op jit(solution)/shard_map/ppermute | solution.py:587
  12.3 13.0 %collective-permute-start.3 = (bf16[192,512]{1,0:T(8,128)(2,1)S(1)}, bf16[192,512]{1,0:T(8,128)(2,1)S(1)}, u32[]{:S(2)}, u32[]{:S(2)}) collective-permute-start(bf16[192,512]{1,0:T(8,128)(2,1)S(1)} %get-tuple-element.80.own), channel_id=1, source_target_pairs={{0,1},{1,0},{2,3},{3,2},{4,5},{5,4},{6,7},{7,6},{8,9},{9,8},{10,11... | collective-permute-start | bytes 589832 | tf_op jit(solution)/shard_map/ppermute | solution.py:587
  14.7 10.6 %collective-permute-start.5 = (bf16[128,512]{1,0:T(8,128)(2,1)S(1)}, bf16[128,512]{1,0:T(8,128)(2,1)S(1)}, u32[]{:S(2)}, u32[]{:S(2)}) collective-permute-start(bf16[128,512]{1,0:T(8,128)(2,1)S(1)} %collective-permute-done.4.received), channel_id=1, source_target_pairs={{0,1},{1,0},{2,3},{3,2},{4,5},{5,4},{6,7},{7,6},{8,9},{9,8},{10,11... | collective-permute-start | bytes 393224 | tf_op jit(solution)/shard_map/ppermute | solution.py:587
  14.7 2.3 %copy-start.1 = (bf16[4608,512]{1,0:T(8,128)(2,1)S(1)}, bf16[4608,512]{1,0:T(8,128)(2,1)}, u32[]{:S(2)}) copy-start(bf16[4608,512]{1,0:T(8,128)(2,1)} %weight1.4) | copy-start | bytes 14155780
  17.0 8.2 %copy-start = (bf16[4608,512]{1,0:T(8,128)(2,1)S(1)}, bf16[4608,512]{1,0:T(8,128)(2,1)}, u32[]{:S(2)}) copy-start(bf16[4608,512]{1,0:T(8,128)(2,1)} %weight2.4) | copy-start | bytes 14155780
  17.0 8.2 %copy-start.2 = (bf16[512,512]{1,0:T(8,128)(2,1)S(1)}, bf16[512,512]{1,0:T(8,128)(2,1)}, u32[]{:S(2)}) copy-start(bf16[512,512]{1,0:T(8,128)(2,1)} %wq.1) | copy-start | bytes 1572868
  17.0 8.2 %copy-start.3 = (bf16[512,512]{1,0:T(8,128)(2,1)S(1)}, bf16[512,512]{1,0:T(8,128)(2,1)}, u32[]{:S(2)}) copy-start(bf16[512,512]{1,0:T(8,128)(2,1)} %wk.1) | copy-start | bytes 1572868
  17.0 8.2 %copy-start.4 = (bf16[512,512]{1,0:T(8,128)(2,1)S(1)}, bf16[512,512]{1,0:T(8,128)(2,1)}, u32[]{:S(2)}) copy-start(bf16[512,512]{1,0:T(8,128)(2,1)} %wv.1) | copy-start | bytes 1572868
  17.0 8.3 %copy-start.5 = (bf16[512,512]{1,0:T(8,128)(2,1)S(1)}, bf16[512,512]{1,0:T(8,128)(2,1)}, u32[]{:S(2)}) copy-start(bf16[512,512]{1,0:T(8,128)(2,1)} %wp.1) | copy-start | bytes 1572868
  17.1 35.5 %slice-start = ((s8[4718592]{0:T(1024)(128)(4,1)}), s8[4194304]{0:T(1024)(128)(4,1)S(1)}, s32[]{:S(2)}) async-start(s8[4718592]{0:T(1024)(128)(4,1)} %bitcast.39), calls=%async_computation | async-start | bytes 8388608
  23.0 15.0 %collective-permute-start.7 = (bf16[256,512]{1,0:T(8,128)(2,1)S(1)}, bf16[256,512]{1,0:T(8,128)(2,1)S(1)}, u32[]{:S(2)}, u32[]{:S(2)}) collective-permute-start(bf16[256,512]{1,0:T(8,128)(2,1)S(1)} %get-tuple-element.89), channel_id=1, source_target_pairs={{0,2},{1,3},{2,0},{3,1},{4,6},{5,7},{6,4},{7,5},{8,10},{9,11},{10,... | collective-permute-start | bytes 786440 | tf_op jit(solution)/shard_map/ppermute | solution.py:590
  25.3 27.3 %slice-start.1 = ((s8[4718592]{0:T(1024)(128)(4,1)}), s8[524288]{0:T(1024)(128)(4,1)S(1)}, s32[]{:S(2)}) async-start(s8[4718592]{0:T(1024)(128)(4,1)} %bitcast.39), calls=%async_computation.1 | async-start | bytes 1048576
  35.9 12.0 %collective-permute-start.9 = (bf16[512,128]{1,0:T(8,128)(2,1)S(1)}, bf16[512,128]{1,0:T(8,128)(2,1)S(1)}, u32[]{:S(2)}, u32[]{:S(2)}) collective-permute-start(bf16[512,128]{1,0:T(8,128)(2,1)S(1)} %get-tuple-element.93), channel_id=1, source_target_pairs={{0,2},{1,3},{2,0},{3,1},{4,6},{5,7},{6,4},{7,5},{8,10},{9,11},{10,... | collective-permute-start | bytes 393224 | tf_op jit(solution)/shard_map/ppermute | solution.py:590
  35.9 11.9 %collective-permute-start.11 = (bf16[256,512]{1,0:T(8,128)(2,1)S(1)}, bf16[256,512]{1,0:T(8,128)(2,1)S(1)}, u32[]{:S(2)}, u32[]{:S(2)}) collective-permute-start(bf16[256,512]{1,0:T(8,128)(2,1)S(1)} %get-tuple-element.104), channel_id=1, source_target_pairs={{0,2},{1,3},{2,0},{3,1},{4,6},{5,7},{6,4},{7,5},{8,10},{9,11},{10,... | collective-permute-start | bytes 786440 | tf_op jit(solution)/shard_map/ppermute | solution.py:590
  38.0 9.9 %collective-permute-start.8 = (bf16[256,512]{1,0:T(8,128)(2,1)S(1)}, bf16[256,512]{1,0:T(8,128)(2,1)S(1)}, u32[]{:S(2)}, u32[]{:S(2)}) collective-permute-start(bf16[256,512]{1,0:T(8,128)(2,1)S(1)} %collective-permute-done.7.half_t), channel_id=1, source_target_pairs={{0,1},{1,0},{2,3},{3,2},{4,5},{5,4},{6,7},{7,6},{8,9},{9,8},{10,11... | collective-permute-start | bytes 786440 | tf_op jit(solution)/shard_map/ppermute | solution.py:587
  42.5 15.1 %collective-permute-start.13 = (bf16[512,128]{1,0:T(8,128)(2,1)S(1)}, bf16[512,128]{1,0:T(8,128)(2,1)S(1)}, u32[]{:S(2)}, u32[]{:S(2)}) collective-permute-start(bf16[512,128]{1,0:T(8,128)(2,1)S(1)} %get-tuple-element.105), channel_id=1, source_target_pairs={{0,2},{1,3},{2,0},{3,1},{4,6},{5,7},{6,4},{7,5},{8,10},{9,11},{10,... | collective-permute-start | bytes 393224 | tf_op jit(solution)/shard_map/ppermute | solution.py:590
  42.7 18.6 %collective-permute-start.28 = (bf16[4,256,256]{2,1,0:T(8,128)(2,1)S(1)}, bf16[4,256,256]{2,1,0:T(8,128)(2,1)S(1)}, u32[]{:S(2)}, u32[]{:S(2)}) collective-permute-start(bf16[4,256,256]{2,1,0:T(8,128)(2,1)S(1)} %get-tuple-element.122), channel_id=1, source_target_pairs={{0,4},{4,0},{8,12},{12,8},{16,20},{20,16},{24,28},{28,24},{1,5},{5... | collective-permute-start | bytes 1572872 | tf_op jit(solution)/shard_map/ppermute | solution.py:593
  47.9 9.7 %collective-permute-start.12 = (bf16[256,512]{1,0:T(8,128)(2,1)S(1)}, bf16[256,512]{1,0:T(8,128)(2,1)S(1)}, u32[]{:S(2)}, u32[]{:S(2)}) collective-permute-start(bf16[256,512]{1,0:T(8,128)(2,1)S(1)} %collective-permute-done.11.half_t), channel_id=1, source_target_pairs={{0,1},{1,0},{2,3},{3,2},{4,5},{5,4},{6,7},{7,6},{8,9},{9,8},{10,11... | collective-permute-start | bytes 786440 | tf_op jit(solution)/shard_map/ppermute | solution.py:587
  51.0 19.1 %collective-permute-start.21 = (bf16[4,576,128]{2,1,0:T(8,128)(2,1)S(1)}, bf16[4,576,128]{2,1,0:T(8,128)(2,1)S(1)}, u32[]{:S(2)}, u32[]{:S(2)}) collective-permute-start(bf16[4,576,128]{2,1,0:T(8,128)(2,1)S(1)} %get-tuple-element.94), channel_id=1, source_target_pairs={{0,4},{4,0},{8,12},{12,8},{16,20},{20,16},{24,28},{28,24},{1,5},{5... | collective-permute-start | bytes 1769480 | tf_op jit(solution)/shard_map/ppermute | solution.py:593
  60.7 21.9 %collective-permute-start.14 = (bf16[4,592,128]{2,1,0:T(8,128)(2,1)S(1)}, bf16[4,592,128]{2,1,0:T(8,128)(2,1)S(1)}, u32[]{:S(2)}, u32[]{:S(2)}) collective-permute-start(bf16[4,592,128]{2,1,0:T(8,128)(2,1)S(1)} %get-tuple-element.108), channel_id=1, source_target_pairs={{0,4},{4,0},{8,12},{12,8},{16,20},{20,16},{24,28},{28,24},{1,5},{5... | collective-permute-start | bytes 1818632 | tf_op jit(solution)/shard_map/ppermute | solution.py:593
  61.4 10.7 %collective-permute-start.29 = (bf16[1,256,256]{2,1,0:T(8,128)(2,1)S(1)}, bf16[1,256,256]{2,1,0:T(8,128)(2,1)S(1)}, u32[]{:S(2)}, u32[]{:S(2)}) collective-permute-start(bf16[1,256,256]{2,1,0:T(8,128)(2,1)S(1)} %get-tuple-element.124), channel_id=1, source_target_pairs={{0,8},{4,12},{8,0},{12,4},{16,24},{20,28},{24,16},{28,20},{1,9},{5... | collective-permute-start | bytes 393224 | tf_op jit(solution)/shard_map/ppermute | solution.py:593
  63.1 12.9 %collective-permute-start.30 = (bf16[1,256,256]{2,1,0:T(8,128)(2,1)S(1)}, bf16[1,256,256]{2,1,0:T(8,128)(2,1)S(1)}, u32[]{:S(2)}, u32[]{:S(2)}) collective-permute-start(bf16[1,256,256]{2,1,0:T(8,128)(2,1)S(1)} %get-tuple-element.125), channel_id=1, source_target_pairs={{0,16},{4,20},{8,24},{12,28},{16,0},{20,4},{24,8},{28,12},{1,17},{... | collective-permute-start | bytes 393224 | tf_op jit(solution)/shard_map/ppermute | solution.py:593
  65.7 10.7 %collective-permute-start.31 = (bf16[1,256,256]{2,1,0:T(8,128)(2,1)S(1)}, bf16[1,256,256]{2,1,0:T(8,128)(2,1)S(1)}, u32[]{:S(2)}, u32[]{:S(2)}) collective-permute-start(bf16[1,256,256]{2,1,0:T(8,128)(2,1)S(1)} %get-tuple-element.126), channel_id=1, source_target_pairs={{0,24},{4,28},{8,16},{12,20},{16,8},{20,12},{24,0},{28,4},{1,25},{... | collective-permute-start | bytes 393224 | tf_op jit(solution)/shard_map/ppermute | solution.py:593
  70.0 31.4 %collective-permute-start.6 = (bf16[128,512]{1,0:T(8,128)(2,1)S(1)}, bf16[128,512]{1,0:T(8,128)(2,1)S(1)}, u32[]{:S(2)}, u32[]{:S(2)}) collective-permute-start(bf16[128,512]{1,0:T(8,128)(2,1)S(1)} %get-tuple-element.83), channel_id=1, source_target_pairs={{0,2},{1,3},{2,0},{3,1},{4,6},{5,7},{6,4},{7,5},{8,10},{9,11},{10,... | collective-permute-start | bytes 393224 | tf_op jit(solution)/shard_map/ppermute | solution.py:590
  72.2 12.3 %collective-permute-start.22 = (bf16[1,576,128]{2,1,0:T(8,128)(2,1)S(1)}, bf16[1,576,128]{2,1,0:T(8,128)(2,1)S(1)}, u32[]{:S(2)}, u32[]{:S(2)}) collective-permute-start(bf16[1,576,128]{2,1,0:T(8,128)(2,1)S(1)} %get-tuple-element.117), channel_id=1, source_target_pairs={{0,8},{4,12},{8,0},{12,4},{16,24},{20,28},{24,16},{28,20},{1,9},{5... | collective-permute-start | bytes 442376 | tf_op jit(solution)/shard_map/ppermute | solution.py:593
  76.0 12.3 %collective-permute-start.23 = (bf16[1,576,128]{2,1,0:T(8,128)(2,1)S(1)}, bf16[1,576,128]{2,1,0:T(8,128)(2,1)S(1)}, u32[]{:S(2)}, u32[]{:S(2)}) collective-permute-start(bf16[1,576,128]{2,1,0:T(8,128)(2,1)S(1)} %get-tuple-element.118), channel_id=1, source_target_pairs={{0,16},{4,20},{8,24},{12,28},{16,0},{20,4},{24,8},{28,12},{1,17},{... | collective-permute-start | bytes 442376 | tf_op jit(solution)/shard_map/ppermute | solution.py:593
  76.4 12.3 %collective-permute-start.24 = (bf16[1,576,128]{2,1,0:T(8,128)(2,1)S(1)}, bf16[1,576,128]{2,1,0:T(8,128)(2,1)S(1)}, u32[]{:S(2)}, u32[]{:S(2)}) collective-permute-start(bf16[1,576,128]{2,1,0:T(8,128)(2,1)S(1)} %get-tuple-element.119), channel_id=1, source_target_pairs={{0,24},{4,28},{8,16},{12,20},{16,8},{20,12},{24,0},{28,4},{1,25},{... | collective-permute-start | bytes 442376 | tf_op jit(solution)/shard_map/ppermute | solution.py:593
  82.6 8.1 %collective-permute-start.32 = (bf16[256,256]{1,0:T(8,128)(2,1)S(1)}, bf16[256,256]{1,0:T(8,128)(2,1)S(1)}, u32[]{:S(2)}, u32[]{:S(2)}) collective-permute-start(bf16[256,256]{1,0:T(8,128)(2,1)S(1)} %fusion.2.own_ref), channel_id=1, source_target_pairs={{0,2},{1,3},{2,0},{3,1},{4,6},{5,7},{6,4},{7,5},{8,10},{9,11},{10,... | collective-permute-start | bytes 393224 | tf_op jit(solution)/shard_map/ppermute | solution.py:590
  84.5 7.7 %collective-permute-start.15 = (bf16[1,592,128]{2,1,0:T(8,128)(2,1)S(1)}, bf16[1,592,128]{2,1,0:T(8,128)(2,1)S(1)}, u32[]{:S(2)}, u32[]{:S(2)}) collective-permute-start(bf16[1,592,128]{2,1,0:T(8,128)(2,1)S(1)} %get-tuple-element.110), channel_id=1, source_target_pairs={{0,8},{4,12},{8,0},{12,4},{16,24},{20,28},{24,16},{28,20},{1,9},{5... | collective-permute-start | bytes 454664 | tf_op jit(solution)/shard_map/ppermute | solution.py:593
  88.3 12.8 %collective-permute-start.16 = (bf16[1,592,128]{2,1,0:T(8,128)(2,1)S(1)}, bf16[1,592,128]{2,1,0:T(8,128)(2,1)S(1)}, u32[]{:S(2)}, u32[]{:S(2)}) collective-permute-start(bf16[1,592,128]{2,1,0:T(8,128)(2,1)S(1)} %get-tuple-element.111), channel_id=1, source_target_pairs={{0,16},{4,20},{8,24},{12,28},{16,0},{20,4},{24,8},{28,12},{1,17},{... | collective-permute-start | bytes 454664 | tf_op jit(solution)/shard_map/ppermute | solution.py:593
  88.7 12.4 %collective-permute-start.17 = (bf16[1,592,128]{2,1,0:T(8,128)(2,1)S(1)}, bf16[1,592,128]{2,1,0:T(8,128)(2,1)S(1)}, u32[]{:S(2)}, u32[]{:S(2)}) collective-permute-start(bf16[1,592,128]{2,1,0:T(8,128)(2,1)S(1)} %get-tuple-element.112), channel_id=1, source_target_pairs={{0,24},{4,28},{8,16},{12,20},{16,8},{20,12},{24,0},{28,4},{1,25},{... | collective-permute-start | bytes 454664 | tf_op jit(solution)/shard_map/ppermute | solution.py:593
  90.7 11.1 %collective-permute-start.10 = (bf16[128,512]{1,0:T(8,128)(2,1)S(1)}, bf16[128,512]{1,0:T(8,128)(2,1)S(1)}, u32[]{:S(2)}, u32[]{:S(2)}) collective-permute-start(bf16[128,512]{1,0:T(8,128)(2,1)S(1)} %get-tuple-element.100), channel_id=1, source_target_pairs={{0,2},{1,3},{2,0},{3,1},{4,6},{5,7},{6,4},{7,5},{8,10},{9,11},{10,... | collective-permute-start | bytes 393224 | tf_op jit(solution)/shard_map/ppermute | solution.py:590
  92.1 17.1 %collective-permute-start.33 = (bf16[256,256]{1,0:T(8,128)(2,1)S(1)}, bf16[256,256]{1,0:T(8,128)(2,1)S(1)}, u32[]{:S(2)}, u32[]{:S(2)}) collective-permute-start(bf16[256,256]{1,0:T(8,128)(2,1)S(1)} %fusion.2.own_ref), channel_id=1, source_target_pairs={{0,1},{1,0},{2,3},{3,2},{4,5},{5,4},{6,7},{7,6},{8,9},{9,8},{10,11... | collective-permute-start | bytes 393224 | tf_op jit(solution)/shard_map/ppermute | solution.py:587
  101.1 9.5 %collective-permute-start.34 = (bf16[256,256]{1,0:T(8,128)(2,1)S(1)}, bf16[256,256]{1,0:T(8,128)(2,1)S(1)}, u32[]{:S(2)}, u32[]{:S(2)}) collective-permute-start(bf16[256,256]{1,0:T(8,128)(2,1)S(1)} %collective-permute-done.32.far_ref), channel_id=1, source_target_pairs={{0,1},{1,0},{2,3},{3,2},{4,5},{5,4},{6,7},{7,6},{8,9},{9,8},{10,11... | collective-permute-start | bytes 393224 | tf_op jit(solution)/shard_map/ppermute | solution.py:587
  101.1 6.6 %collective-permute-start.25 = (bf16[576,128]{1,0:T(8,128)(2,1)S(1)}, bf16[576,128]{1,0:T(8,128)(2,1)S(1)}, u32[]{:S(2)}, u32[]{:S(2)}) collective-permute-start(bf16[576,128]{1,0:T(8,128)(2,1)S(1)} %fusion.1.own_ref), channel_id=1, source_target_pairs={{0,2},{1,3},{2,0},{3,1},{4,6},{5,7},{6,4},{7,5},{8,10},{9,11},{10,... | collective-permute-start | bytes 442376 | tf_op jit(solution)/shard_map/ppermute | solution.py:590
  101.5 10.0 %collective-permute-start.26 = (bf16[576,128]{1,0:T(8,128)(2,1)S(1)}, bf16[576,128]{1,0:T(8,128)(2,1)S(1)}, u32[]{:S(2)}, u32[]{:S(2)}) collective-permute-start(bf16[576,128]{1,0:T(8,128)(2,1)S(1)} %fusion.1.own_ref), channel_id=1, source_target_pairs={{0,1},{1,0},{2,3},{3,2},{4,5},{5,4},{6,7},{7,6},{8,9},{9,8},{10,11... | collective-permute-start | bytes 442376 | tf_op jit(solution)/shard_map/ppermute | solution.py:587
  101.8 8.8 %collective-permute-start.18 = (bf16[592,128]{1,0:T(8,128)(2,1)S(1)}, bf16[592,128]{1,0:T(8,128)(2,1)S(1)}, u32[]{:S(2)}, u32[]{:S(2)}) collective-permute-start(bf16[592,128]{1,0:T(8,128)(2,1)S(1)} %fusion.own_ref), channel_id=1, source_target_pairs={{0,2},{1,3},{2,0},{3,1},{4,6},{5,7},{6,4},{7,5},{8,10},{9,11},{10,... | collective-permute-start | bytes 454664 | tf_op jit(solution)/shard_map/ppermute | solution.py:590
  107.7 3.7 %collective-permute-start.27 = (bf16[576,128]{1,0:T(8,128)(2,1)S(1)}, bf16[576,128]{1,0:T(8,128)(2,1)S(1)}, u32[]{:S(2)}, u32[]{:S(2)}) collective-permute-start(bf16[576,128]{1,0:T(8,128)(2,1)S(1)} %collective-permute-done.25.far_ref), channel_id=1, source_target_pairs={{0,1},{1,0},{2,3},{3,2},{4,5},{5,4},{6,7},{7,6},{8,9},{9,8},{10,11... | collective-permute-start | bytes 442376 | tf_op jit(solution)/shard_map/ppermute | solution.py:587
  109.2 3.4 %collective-permute-start.19 = (bf16[592,128]{1,0:T(8,128)(2,1)S(1)}, bf16[592,128]{1,0:T(8,128)(2,1)S(1)}, u32[]{:S(2)}, u32[]{:S(2)}) collective-permute-start(bf16[592,128]{1,0:T(8,128)(2,1)S(1)} %fusion.own_ref), channel_id=1, source_target_pairs={{0,1},{1,0},{2,3},{3,2},{4,5},{5,4},{6,7},{7,6},{8,9},{9,8},{10,11... | collective-permute-start | bytes 454664 | tf_op jit(solution)/shard_map/ppermute | solution.py:587
  110.6 2.1 %collective-permute-start.20 = (bf16[592,128]{1,0:T(8,128)(2,1)S(1)}, bf16[592,128]{1,0:T(8,128)(2,1)S(1)}, u32[]{:S(2)}, u32[]{:S(2)}) collective-permute-start(bf16[592,128]{1,0:T(8,128)(2,1)S(1)} %collective-permute-done.18.far_ref), channel_id=1, source_target_pairs={{0,1},{1,0},{2,3},{3,2},{4,5},{5,4},{6,7},{7,6},{8,9},{9,8},{10,11... | collective-permute-start | bytes 454664 | tf_op jit(solution)/shard_map/ppermute | solution.py:587

commit v3 on v2

--- a/solution.py
+++ b/solution.py
@@ -18,10 +18,10 @@
 
 VM = pl.BlockSpec(memory_space=pltpu.VMEM)
 SM = pl.BlockSpec(memory_space=pltpu.SMEM)
-HB = pl.BlockSpec(memory_space=pl.ANY)
+HB = pl.BlockSpec(memory_space=pltpu.HBM)
 RATE = 1 << 30
 LENGTH = {
-    "pack": 1, "first": 6, "second": 11, "third": 5, "fourth": 5, "weight2": 3, "weight1": 3, "unpack": 2,
+    "pack": 10, "stack": 10, "first": 8, "second": 30, "third": 20, "fourth": 0.02, "weight2": 0.02, "weight1": 0.02,
 }
 
 
@@ -214,10 +214,13 @@
     return vec_ref[index : index + 1, :]
 
 
-def pack_kernel(bucket_ref, x_ref, cot_ref, kinds, away_x, home_x, away_c, home_c, sems):
+def pack_kernel(
+    bucket_hbm, x_ref, cot_ref, kinds, away_x, home_x, away_c, home_c, bucket_ref, bucket_sem, sems
+):
+    copy = pltpu.make_async_copy(bucket_hbm, bucket_ref, bucket_sem.at[0])
+    copy.start()
+    copy.wait()
     h, home, away = place(bucket_ref)
-    kinds[0] = bucket_ref[0]
-    kinds[1] = bucket_ref[1]
 
     def each(act):
         slot = 0
@@ -242,12 +245,21 @@
                 slot += 6
 
     each(lambda a, b, sem: pltpu.make_async_copy(a, b, sem).start())
+    kinds[0] = bucket_ref[0]
+    kinds[1] = bucket_ref[1]
     each(lambda a, b, sem: pltpu.make_async_copy(a, b, sem).wait())
+
+
+def stack_kernel(*refs):
+    out_ref = refs[-1]
+    for index, ref in enumerate(refs[:-1]):
+        out_ref[index : index + 1, :] = ref[...]
+    out_ref[len(refs) - 1 :, :] = jnp.zeros((VECS - len(refs) + 1, out_ref.shape[1]), F32)
 
 
 def first_kernel(
     bucket_ref, own, partner, received, partner_received, vecs, weight1,
-    image_ref, conv_ref, act2_ref, stats_ref, act1_t, act2_t, send1_t, send2_t,
+    image_ref, conv_ref, act2_ref, stats_ref, act1_t, act2_t, send_t,
     shift_ref,
 ):
     h, home, away = place(bucket_ref)
@@ -270,8 +282,8 @@
     act2_ref[...] = act
     act2_t[...] = act.T
     half = pl.multiple_of((h & 1) * (channels // 2), 16)
-    send1_t[...] = act1_t[pl.ds(half, channels // 2), :]
-    send2_t[...] = act2_t[pl.ds(half, channels // 2), :]
+    send_t[0] = act1_t[pl.ds(half, channels // 2), :]
+    send_t[1] = act2_t[pl.ds(half, channels // 2), :]
     stats_ref[0:1, :] = mean1
     stats_ref[1:2, :] = inverse1
     stats_ref[2:3, :] = mean2
@@ -437,7 +449,7 @@
 
 
 def weight_kernel(
-    bucket_ref, act_t, half_t, partner_half_t, block_own, block_away, *rest, tail
+    bucket_ref, act_t, half_t, partner_half_t, block_own, block_away, *rest, layer, tail
 ):
     vec_in = rest[0] if tail else None
     keep_ref, send_ref, left_ref, right_ref, shift_ref, sum_ref = rest[tail:]
@@ -445,9 +457,9 @@
     channels = act_t.shape[0]
     half = channels // 2
     left_ref[:, 0:PIX] = act_t[...]
-    left_ref[pl.ds(pl.multiple_of((h & 1) * half, 16), half), PIX : 2 * PIX] = half_t[...]
+    left_ref[pl.ds(pl.multiple_of((h & 1) * half, 16), half), PIX : 2 * PIX] = half_t[layer]
     left_ref[pl.ds(pl.multiple_of((1 - (h & 1)) * half, 16), half), PIX : 2 * PIX] = (
-        partner_half_t[...]
+        partner_half_t[layer]
     )
     for index, (facts, block) in enumerate(((home, block_own), (away, block_away))):
         stride = facts[2]
@@ -545,12 +557,14 @@
         in_specs=specs,
         out_specs=[SM if dtype == jnp.int32 else VM for shape, dtype in outs],
         scratch_shapes=[
-            pltpu.SemaphoreType.DMA(shape) if dtype is None else pltpu.VMEM(shape, dtype)
+            pltpu.SemaphoreType.DMA(shape)
+            if dtype is None
+            else (pltpu.SMEM if dtype == jnp.int32 else pltpu.VMEM)(shape, dtype)
             for shape, dtype in scratch
         ],
         compiler_params=pltpu.CompilerParams(vmem_limit_bytes=vmem << 20),
         cost_estimate=pl.CostEstimate(
-            flops=LENGTH.get(name, 1) * RATE, bytes_accessed=1024, transcendentals=0
+            flops=int(LENGTH.get(name, 1) * RATE), bytes_accessed=1024, transcendentals=0
         ),
     )(*operands)
 
@@ -583,6 +597,9 @@
     shard_rows = 9 * C // batches
     small_rows = C // batches
 
+    def row(v):
+        return v.reshape(1, C)
+
     def to_core(v):
         return lax.ppermute(v, "height", [(i, i ^ 1) for i in range(4)])
 
@@ -600,35 +617,38 @@
     rows8 = ((8, C), F32)
     block = ((PIX, BLK), BF16)
     turned = ((C, PIX), BF16)
-    half = ((C // 2, PIX), BF16)
     shifts = ((3, PIX + 2 * PAD, C), BF16)
 
     kinds, away_x, home_x, away_c, home_c = call(
         pack_kernel, "pack",
         [((2,), jnp.int32), ((128, C), BF16), ((192, C), BF16), ((128, C), BF16), ((192, C), BF16)],
-        [((24,), None)], 8, bucket, inputs, cotangent, any_from=1,
-    )
-    vecs = jnp.stack(
-        [
-            norm1_gain, norm1_shift, conv1_bias, norm2_gain, norm2_shift, conv2_bias,
-            norm3_gain, norm3_shift, query_bias, value_bias, proj_bias,
-        ]
+        [((2,), jnp.int32), ((1,), None), ((24,), None)], 54, bucket, inputs, cotangent,
+        smem=0, any_from=0,
+    )
+    vectors = (
+        norm1_gain, norm1_shift, conv1_bias, norm2_gain, norm2_shift, conv2_bias,
+        norm3_gain, norm3_shift, query_bias, value_bias, proj_bias,
+    )
+    (vecs,) = call(
+        stack_kernel, "stack", [((VECS, C), F32)], [], 8,
+        after(row(vectors[0]), away_x), *[row(v) for v in vectors[1:]], smem=0,
     )
     recv_x = to_chip(away_x)
     core_x = to_core(home_x)
-    recv_c = to_chip(away_c)
+    recv_x = after(recv_x, vecs)
+    recv_c = to_chip(after(away_c, recv_x))
     core_c = to_core(home_c)
     core_recv_x = to_core(recv_x)
-    core_recv_c = to_core(recv_c)
-
-    image, conv, act2, stats, act1_t, act2_t, send1_t, send2_t = call(
+    core_recv_c = lax.ppermute(after(away_c, recv_x), "height", [(i, i ^ 3) for i in range(4)])
+
+    image, conv, act2, stats, act1_t, act2_t, send_t = call(
         first_kernel, "first",
-        [img16, img32, img16, rows8, turned, turned, half, half],
+        [img16, img32, img16, rows8, turned, turned, ((2, C // 2, PIX), BF16)],
         [shifts], 24,
         kinds, home_x, core_x, recv_x, core_recv_x, vecs, conv1_weight,
     )
-    half_t = [to_chip(v) for v in (send1_t, send2_t)]
-    core_half_t = [to_core(v) for v in half_t]
+    half_t = to_chip(send_t)
+    core_half_t = to_core(half_t)
 
     attn_out = ((batches // 2, 4 * small_rows, 2 * BLK), BF16)
     out_own, out_send, grad2, grad_middle, attn_keep, attn_send, vec_a, block2, block2_send = call(
@@ -653,11 +673,11 @@
     def weight_grad(name, act_t, index, own, away, *tail):
         rows = shard_rows + (VECS if tail else 0)
         return call(
-            functools.partial(weight_kernel, tail=len(tail)), name,
+            functools.partial(weight_kernel, layer=index, tail=len(tail)), name,
             [((batches // 2, rows, BLK), BF16)] * 2,
             [((C, 2 * PIX), BF16), ((2 * PIX, 9 * BLK), BF16), ((3, PIX + 2 * PAD, BLK), BF16),
              ((9 * C, BLK), F32)],
-            24, kinds, act_t, half_t[index], core_half_t[index], own, away, *tail,
+            24, kinds, act_t, half_t, core_half_t, own, away, *tail,
         )
 
     keep2, send2 = weight_grad("weight2", act2_t, 1, after(block2, block1), block2_away)
@@ -701,21 +721,22 @@
 
     attn_parts = gather(scatter("routea", after(attn_keep, send1), attn_got))
     parts2 = gather(scatter("routeb", keep2, got2))
-    parts1 = gather(scatter("routec", keep1, got1))
     small = call(
         join_attn_kernel, "joina", [((small_rows, C), F32)] * 4, [], 8, *attn_parts, smem=0
     )
     (whole2,) = call(join_kernel, "joinb", [((shard_rows, C), F32)], [], 8, *parts2, smem=0)
-    whole1, sums = call(
-        join_kernel, "joinc", [((shard_rows, C), F32), ((VECS, BLK), F32)], [], 8, *parts1, smem=0
-    )
-    v = [sums[i, :small_rows] for i in range(11)]
-
     outputs, input_grad = call(
         unpack_kernel, "unpack",
         [(inputs.shape, BF16)] * 2, [], 8,
         kinds, out_own, out_away, grad_own, grad_away,
     )
+    shard1 = scatter("routec", keep1, got1)
+    parts1 = gather(after(shard1, whole2, small[0], outputs))
+    whole1, sums = call(
+        join_kernel, "joinc", [((shard_rows, C), F32), ((VECS, BLK), F32)], [], 8, *parts1, smem=0
+    )
+    v = [sums[i, :small_rows] for i in range(11)]
+
     return (
         outputs, input_grad,
         v[9], v[10], whole1, v[8],

time: 115 us -> 108 us (0.939)
  local copies, waits for them, and re-layouts: 7.12 us -> 0.68 us
  waiting for transfers between devices: 32.9 us -> 28.3 us
  starting transfers between devices: 33.7 us -> 36.8 us
    ppermute x12, waiting for transfers between devices: 20.3 us -> 14.3 us  [to_batch(): return lax.ppermute(v, 'batch', [(i, i ^ change) for i in range(batches)])]
    unnamed x22 -> x46, local copies, waits for them, and re-layouts: 5.01 us -> 0.12 us
    ppermute x12, starting transfers between devices: 17.7 us -> 21.8 us  [to_batch(): return lax.ppermute(v, 'batch', [(i, i ^ change) for i in range(batches)])]
    another operation x1 -> x0, local copies, waits for them, and re-layouts: 1.56 us -> none  [on_device(): jnp.stack([norm1_gain, norm1_shift, conv1_bias, norm2_gain, norm2_shift,...]
    ppermute x12 -> x10, waiting for transfers between devices: 0.03 us -> 1.39 us  [to_core(): return lax.ppermute(v, 'height', [(i, i ^ 1) for i in range(4)])]
    pallas_call x14 -> x15, Pallas kernels: 39.6 us -> 40.4 us  [call(): pl.pallas_call(kernel, name=name, out_shape=[jax.ShapeDtypeStruct(shape,...]
    ppermute x11 -> x10, starting transfers between devices: 14.6 us -> 14.4 us  [to_chip(): return lax.ppermute(v, 'height', [(i, i ^ 2) for i in range(4)])]
    ppermute x11 -> x10, waiting for transfers between devices: 12.6 us -> 12.6 us  [to_chip(): return lax.ppermute(v, 'height', [(i, i ^ 2) for i in range(4)])]
  transfers between devices with their start and end apart: 35 -> 33, of which waited for: 10 -> 10; matrix products, arithmetic and copies ran while one was open for 2% -> 0% of each run, Pallas kernels for 32% -> 32%
where the time goes in v3:
time: 108 us; the launch traced here: 107 us
  Pallas kernels  40.4 us (37%)
  starting transfers between devices  36.8 us (34%)
  waiting for transfers between devices  28.3 us (26%)
  between operations  1.14 us (1%)
    pallas_call x15, Pallas kernels, call(): pl.pallas_call(kernel, name=name, out_shape=[jax.ShapeDtypeStruct(shape,...  40.4 us
    ppermute x12, starting transfers between devices, to_batch(): return lax.ppermute(v, 'batch', [(i, i ^ change) for i in range(batches)])  21.8 us
    ppermute x10, starting transfers between devices, to_chip(): return lax.ppermute(v, 'height', [(i, i ^ 2) for i in range(4)])  14.4 us
    ppermute x12, waiting for transfers between devices, to_batch(): return lax.ppermute(v, 'batch', [(i, i ^ change) for i in range(batches)])  14.3 us
    ppermute x10, waiting for transfers between devices, to_chip(): return lax.ppermute(v, 'height', [(i, i ^ 2) for i in range(4)])  12.6 us
  transfers between devices with their start and end apart: 33, of which 10 were waited for; matrix products, arithmetic and copies ran while one was open for 0% of the time, Pallas kernels for 32%

profile of v3, /device:TPU:0, one launch (start us, length us, event | category | flops | bytes accessed | tf_op | source)
XLA Modules:
  0.0 107.5 jit_solution(12023132361609876985)
XLA Ops:
  0.8 0.0 slice-start
  0.8 0.0 slice-start.2
  0.8 3.2 %pack.1 = (s32[2]{0:T(128)}, bf16[128,512]{1,0:T(8,128)(2,1)}, bf16[192,512]{1,0:T(8,128)(2,1)}, bf16[128,512]{1,0:T(8,128)(2,1)}, bf16[192,512]{1,0:T(8,128)(2,1)}) custom-call(s32[2]{0:T(128)} %bucket_hbm.1, bf16[2,6,32,512]{3,2,1,0:T(8,128)(2,1)} %x_ref.1, bf16[2,6,32,512]{3,2,1,0:T(8,128)(2,1)} %cot_ref.1), custom_call_target="tpu_custom_call" | custom-call | flops 10737418240 | bytes 1024 | tf_op jit(solution)/shard_map/pack/pallas_call | solution.py:553
  4.1 3.0 %collective-permute-start.1 = (bf16[128,512]{1,0:T(8,128)(2,1)}, bf16[128,512]{1,0:T(8,128)(2,1)S(1)}, u32[]{:S(2)}, u32[]{:S(2)}) collective-permute-start(bf16[128,512]{1,0:T(8,128)(2,1)} %get-tuple-element.80), channel_id=1, source_target_pairs={{0,2},{1,3},{2,0},{3,1},{4,6},{5,7},{6,4},{7,5},{8,10},{9,11},{10,... | collective-permute-start | bytes 393224 | tf_op jit(solution)/shard_map/ppermute | solution.py:607
  7.1 0.0 collective-permute-start
  7.2 0.0 copy-start.5
  7.2 0.0 copy-start.18
  7.2 0.0 copy-start
  7.2 0.0 copy-start.6
  7.2 0.0 slice-start.3
  7.3 3.5 %collective-permute-done.1.received = bf16[128,512]{1,0:T(8,128)(2,1)S(1)} collective-permute-done((bf16[128,512]{1,0:T(8,128)(2,1)}, bf16[128,512]{1,0:T(8,128)(2,1)S(1)}, u32[]{:S(2)}, u32[]{:S(2)}) %collective-permute-start.1) | collective-permute-done | bytes 131104 | tf_op jit(solution)/shard_map/ppermute | solution.py:607
  10.8 0.0 collective-permute-start.2
  10.8 0.5 collective-permute-start.3
  11.3 1.7 %collective-permute-start.4 = (bf16[128,512]{1,0:T(8,128)(2,1)S(1)}, bf16[128,512]{1,0:T(8,128)(2,1)S(1)}, u32[]{:S(2)}, u32[]{:S(2)}) collective-permute-start(bf16[128,512]{1,0:T(8,128)(2,1)S(1)} %copy-done.18), channel_id=1, source_target_pairs={{0,2},{1,3},{2,0},{3,1},{4,6},{5,7},{6,4},{7,5},{8,10},{9,11},{10,... | collective-permute-start | bytes 393224 | tf_op jit(solution)/shard_map/ppermute | solution.py:607
  13.1 0.0 copy-start.1
  13.1 0.0 copy-start.2
  13.1 0.0 copy-start.3
  13.1 0.0 copy-start.4
  13.2 5.8 %first.1 = (bf16[512,512]{1,0:T(8,128)(2,1)S(1)}, f32[512,512]{1,0:T(8,128)S(1)}, bf16[512,512]{1,0:T(8,128)(2,1)S(1)}, f32[8,512]{1,0:T(8,128)S(1)}, bf16[512,5...) custom-call(s32[2]{0:T(128)S(1)} %copy-done, bf16[192,512]{1,0:T(8,128)(2,1)S(1)} %copy-done.6, ...), custom_call_target="tpu_custom_call" | custom-call | flops 8589934592 | bytes 1024 | tf_op jit(solution)/shard_map/first/pallas_call | solution.py:553
  19.0 1.5 %collective-permute-start.7 = (bf16[2,256,512]{2,1,0:T(8,128)(2,1)S(1)}, bf16[2,256,512]{2,1,0:T(8,128)(2,1)S(1)}, u32[]{:S(2)}, u32[]{:S(2)}) collective-permute-start(bf16[2,256,512]{2,1,0:T(8,128)(2,1)S(1)} %get-tuple-element.95), channel_id=1, source_target_pairs={{0,2},{1,3},{2,0},{3,1},{4,6},{5,7},{6,4},{7,5},{8,10},{9,11},{10,... | collective-permute-start | bytes 1572872 | tf_op jit(solution)/shard_map/ppermute | solution.py:607
  20.5 10.5 %second.1 = (bf16[192,512]{1,0:T(8,128)(2,1)S(1)}, bf16[128,512]{1,0:T(8,128)(2,1)S(1)}, bf16[512,512]{1,0:T(8,128)(2,1)S(1)}, f32[512,512]{1,0:T(8,128)S(1)}, b...) custom-call(s32[2]{0:T(128)S(1)} %copy-done, ...), custom_call_target="tpu_custom_call" | custom-call | flops 32212254720 | bytes 1024 | tf_op jit(solution)/shard_map/second/pallas_call | solution.py:553
  31.0 0.7 collective-permute-start.9
  31.7 1.6 %collective-permute-start.23 = (bf16[4,256,256]{2,1,0:T(8,128)(2,1)S(1)}, bf16[4,256,256]{2,1,0:T(8,128)(2,1)S(1)}, u32[]{:S(2)}, u32[]{:S(2)}) collective-permute-start(bf16[4,256,256]{2,1,0:T(8,128)(2,1)S(1)} %get-tuple-element.125), channel_id=1, source_target_pairs={{0,4},{4,0},{8,12},{12,8},{16,20},{20,16},{24,28},{28,24},{1,5},{5... | collective-permute-start | bytes 1572872 | tf_op jit(solution)/shard_map/ppermute | solution.py:610
  33.2 0.1 collective-permute-done.7.half_t
  33.3 4.5 %third.1 = (bf16[512,512]{1,0:T(8,128)(2,1)S(1)}, bf16[512,128]{1,0:T(8,128)(2,1)S(1)}, bf16[512,128]{1,0:T(8,128)(2,1)S(1)}, f32[8,512]{1,0:T(8,128)S(1)}) custom-call(s32[2]{0:T(128)S(1)} %copy-done, bf16[512,512]{1,0:T(8,128)(2,1)S(1)} %get-tuple-element.90.grad2_ref, f32[512,512]{1,0:T(8,128)S(1)} %get-tuple-element.91.conv_ref, ...), custom_call_target="tpu_custom_call" | custom-call | flops 21474836480 | bytes 1024 | tf_op jit(solution)/shard_map/third/pallas_call | solution.py:553
  37.9 3.1 %weight2.5 = (bf16[4,576,128]{2,1,0:T(8,128)(2,1)S(1)}, bf16[4,576,128]{2,1,0:T(8,128)(2,1)S(1)}) custom-call(s32[2]{0:T(128)S(1)} %copy-done, bf16[512,512]{1,0:T(8,128)(2,1)S(1)} %get-tuple-element.94.act_t, bf16[2,256,512]{2,1,0:T(8,128)(2,1)S(1)} %collective-permute-done.7.half_t, bf16[2,256,512]{2,1,0:T(8,128)(2,1)S(1)} %collective-permute-done.8.partner_half_t, ...), custom_call_target="tpu_custom_call" | custom-call | flops 21474836 | bytes 1024 | tf_op jit(solution)/shard_map/weight2/pallas_call | solution.py:553
  41.0 1.9 %collective-permute-start.16 = (bf16[4,576,128]{2,1,0:T(8,128)(2,1)S(1)}, bf16[4,576,128]{2,1,0:T(8,128)(2,1)S(1)}, u32[]{:S(2)}, u32[]{:S(2)}) collective-permute-start(bf16[4,576,128]{2,1,0:T(8,128)(2,1)S(1)} %get-tuple-element.100), channel_id=1, source_target_pairs={{0,4},{4,0},{8,12},{12,8},{16,20},{20,16},{24,28},{28,24},{1,5},{5... | collective-permute-start | bytes 1769480 | tf_op jit(solution)/shard_map/ppermute | solution.py:610
  42.8 1.7 %collective-permute-start.11 = (bf16[512,128]{1,0:T(8,128)(2,1)S(1)}, bf16[512,128]{1,0:T(8,128)(2,1)S(1)}, u32[]{:S(2)}, u32[]{:S(2)}) collective-permute-start(bf16[512,128]{1,0:T(8,128)(2,1)S(1)} %get-tuple-element.110), channel_id=1, source_target_pairs={{0,2},{1,3},{2,0},{3,1},{4,6},{5,7},{6,4},{7,5},{8,10},{9,11},{10,... | collective-permute-start | bytes 393224 | tf_op jit(solution)/shard_map/ppermute | solution.py:607
  44.5 5.0 %fourth.1 = (bf16[192,512]{1,0:T(8,128)(2,1)S(1)}, bf16[128,512]{1,0:T(8,128)(2,1)S(1)}, f32[8,16,128]{2,1,0:T(8,128)S(1)}) custom-call(s32[2]{0:T(128)S(1)} %copy-done, bf16[512,512]{1,0:T(8,128)(2,1)S(1)} %get-tuple-element.101.grad1_ref, bf16[512,512]{1,0:T(8,128)(2,1)S(1)} %get-tuple-element.83.image_ref, f32[8,512]{1,0:T(8,128)S(1)} %get-tuple-element.92.stats_ref, ...), custom_call_target="tpu_custom_call" | custom-call | flops 21474836 | bytes 1024 | tf_op jit(solution)/shard_map/fourth/pallas_call | solution.py:553
  49.5 3.1 %weight1.5 = (bf16[4,592,128]{2,1,0:T(8,128)(2,1)S(1)}, bf16[4,592,128]{2,1,0:T(8,128)(2,1)S(1)}) custom-call(s32[2]{0:T(128)S(1)} %copy-done, bf16[512,512]{1,0:T(8,128)(2,1)S(1)} %get-tuple-element.109.act_t, bf16[2,256,512]{2,1,0:T(8,128)(2,1)S(1)} %collective-permute-done.7.half_t, bf16[2,256,512]{2,1,0:T(8,128)(2,1)S(1)} %collective-permute-done.8.partner_half_t, ...), custom_call_target="tpu_custom_call" | custom-call | flops 21474836 | bytes 1024 | tf_op jit(solution)/shard_map/weight1/pallas_call | solution.py:553
  52.6 0.6 collective-permute-start.12
  53.2 0.1 routea1.1
  53.3 1.7 %collective-permute-start.24 = (bf16[1,256,256]{2,1,0:T(8,128)(2,1)S(1)}, bf16[1,256,256]{2,1,0:T(8,128)(2,1)S(1)}, u32[]{:S(2)}, u32[]{:S(2)}) collective-permute-start(bf16[1,256,256]{2,1,0:T(8,128)(2,1)S(1)} %get-tuple-element.127), channel_id=1, source_target_pairs={{0,8},{4,12},{8,0},{12,4},{16,24},{20,28},{24,16},{28,20},{1,9},{5... | collective-permute-start | bytes 393224 | tf_op jit(solution)/shard_map/ppermute | solution.py:610
  55.0 2.6 %collective-permute-start.25 = (bf16[1,256,256]{2,1,0:T(8,128)(2,1)S(1)}, bf16[1,256,256]{2,1,0:T(8,128)(2,1)S(1)}, u32[]{:S(2)}, u32[]{:S(2)}) collective-permute-start(bf16[1,256,256]{2,1,0:T(8,128)(2,1)S(1)} %get-tuple-element.128), channel_id=1, source_target_pairs={{0,16},{4,20},{8,24},{12,28},{16,0},{20,4},{24,8},{28,12},{1,17},{... | collective-permute-start | bytes 393224 | tf_op jit(solution)/shard_map/ppermute | solution.py:610
  57.6 0.2 collective-permute-start.26
  57.8 1.4 %collective-permute-done.16.got_ref = bf16[4,576,128]{2,1,0:T(8,128)(2,1)S(1)} collective-permute-done((bf16[4,576,128]{2,1,0:T(8,128)(2,1)S(1)}, bf16[4,576,128]{2,1,0:T(8,128)(2,1)S(1)}, u32[]{:S(2)}, u32[]{:S(2)}) %collective-permute-start.16) | collective-permute-done | bytes 589856 | tf_op jit(solution)/shard_map/ppermute | solution.py:610
  59.1 0.1 routeb1.1
  59.3 1.7 %collective-permute-start.17 = (bf16[1,576,128]{2,1,0:T(8,128)(2,1)S(1)}, bf16[1,576,128]{2,1,0:T(8,128)(2,1)S(1)}, u32[]{:S(2)}, u32[]{:S(2)}) collective-permute-start(bf16[1,576,128]{2,1,0:T(8,128)(2,1)S(1)} %get-tuple-element.120), channel_id=1, source_target_pairs={{0,8},{4,12},{8,0},{12,4},{16,24},{20,28},{24,16},{28,20},{1,9},{5... | collective-permute-start | bytes 442376 | tf_op jit(solution)/shard_map/ppermute | solution.py:610
  60.9 2.6 %collective-permute-start.18 = (bf16[1,576,128]{2,1,0:T(8,128)(2,1)S(1)}, bf16[1,576,128]{2,1,0:T(8,128)(2,1)S(1)}, u32[]{:S(2)}, u32[]{:S(2)}) collective-permute-start(bf16[1,576,128]{2,1,0:T(8,128)(2,1)S(1)} %get-tuple-element.121), channel_id=1, source_target_pairs={{0,16},{4,20},{8,24},{12,28},{16,0},{20,4},{24,8},{28,12},{1,17},{... | collective-permute-start | bytes 442376 | tf_op jit(solution)/shard_map/ppermute | solution.py:610
  63.5 4.3 %collective-permute-done.25 = bf16[1,256,256]{2,1,0:T(8,128)(2,1)S(1)} collective-permute-done((bf16[1,256,256]{2,1,0:T(8,128)(2,1)S(1)}, bf16[1,256,256]{2,1,0:T(8,128)(2,1)S(1)}, u32[]{:S(2)}, u32[]{:S(2)}) %collective-permute-start.25) | collective-permute-done | bytes 131104 | tf_op jit(solution)/shard_map/ppermute | solution.py:610
  67.8 2.9 %collective-permute-start.19 = (bf16[1,576,128]{2,1,0:T(8,128)(2,1)S(1)}, bf16[1,576,128]{2,1,0:T(8,128)(2,1)S(1)}, u32[]{:S(2)}, u32[]{:S(2)}) collective-permute-start(bf16[1,576,128]{2,1,0:T(8,128)(2,1)S(1)} %get-tuple-element.122), channel_id=1, source_target_pairs={{0,24},{4,28},{8,16},{12,20},{16,8},{20,12},{24,0},{28,4},{1,25},{... | collective-permute-start | bytes 442376 | tf_op jit(solution)/shard_map/ppermute | solution.py:610
  70.7 0.1 fusion.2.own_ref
  70.8 0.7 collective-permute-start.27
  71.5 1.4 %collective-permute-start.6 = (bf16[128,512]{1,0:T(8,128)(2,1)S(1)}, bf16[128,512]{1,0:T(8,128)(2,1)S(1)}, u32[]{:S(2)}, u32[]{:S(2)}) collective-permute-start(bf16[128,512]{1,0:T(8,128)(2,1)S(1)} %get-tuple-element.89), channel_id=1, source_target_pairs={{0,2},{1,3},{2,0},{3,1},{4,6},{5,7},{6,4},{7,5},{8,10},{9,11},{10,... | collective-permute-start | bytes 393224 | tf_op jit(solution)/shard_map/ppermute | solution.py:607
  72.9 0.1 routec1.1
  73.0 4.0 %collective-permute-done.27.far_ref = bf16[256,256]{1,0:T(8,128)(2,1)S(1)} collective-permute-done((bf16[256,256]{1,0:T(8,128)(2,1)S(1)}, bf16[256,256]{1,0:T(8,128)(2,1)S(1)}, u32[]{:S(2)}, u32[]{:S(2)}) %collective-permute-start.27) | collective-permute-done | bytes 131104 | tf_op jit(solution)/shard_map/ppermute | solution.py:607
  77.1 0.7 collective-permute-start.10
  77.8 2.3 %collective-permute-done.18 = bf16[1,576,128]{2,1,0:T(8,128)(2,1)S(1)} collective-permute-done((bf16[1,576,128]{2,1,0:T(8,128)(2,1)S(1)}, bf16[1,576,128]{2,1,0:T(8,128)(2,1)S(1)}, u32[]{:S(2)}, u32[]{:S(2)}) %collective-permute-start.18) | collective-permute-done | bytes 147488 | tf_op jit(solution)/shard_map/ppermute | solution.py:610
  80.1 3.4 %collective-permute-start.13 = (bf16[1,592,128]{2,1,0:T(8,128)(2,1)S(1)}, bf16[1,592,128]{2,1,0:T(8,128)(2,1)S(1)}, u32[]{:S(2)}, u32[]{:S(2)}) collective-permute-start(bf16[1,592,128]{2,1,0:T(8,128)(2,1)S(1)} %get-tuple-element.115), channel_id=1, source_target_pairs={{0,8},{4,12},{8,0},{12,4},{16,24},{20,28},{24,16},{28,20},{1,9},{5... | collective-permute-start | bytes 454664 | tf_op jit(solution)/shard_map/ppermute | solution.py:610
  83.5 0.1 fusion.1.own_ref
  83.6 1.3 %collective-permute-start.14 = (bf16[1,592,128]{2,1,0:T(8,128)(2,1)S(1)}, bf16[1,592,128]{2,1,0:T(8,128)(2,1)S(1)}, u32[]{:S(2)}, u32[]{:S(2)}) collective-permute-start(bf16[1,592,128]{2,1,0:T(8,128)(2,1)S(1)} %get-tuple-element.116), channel_id=1, source_target_pairs={{0,16},{4,20},{8,24},{12,28},{16,0},{20,4},{24,8},{28,12},{1,17},{... | collective-permute-start | bytes 454664 | tf_op jit(solution)/shard_map/ppermute | solution.py:610
  84.9 1.5 %collective-permute-start.15 = (bf16[1,592,128]{2,1,0:T(8,128)(2,1)S(1)}, bf16[1,592,128]{2,1,0:T(8,128)(2,1)S(1)}, u32[]{:S(2)}, u32[]{:S(2)}) collective-permute-start(bf16[1,592,128]{2,1,0:T(8,128)(2,1)S(1)} %get-tuple-element.117), channel_id=1, source_target_pairs={{0,24},{4,28},{8,16},{12,20},{16,8},{20,12},{24,0},{28,4},{1,25},{... | collective-permute-start | bytes 454664 | tf_op jit(solution)/shard_map/ppermute | solution.py:610
  86.4 1.4 %collective-permute-start.20 = (bf16[576,128]{1,0:T(8,128)(2,1)S(1)}, bf16[576,128]{1,0:T(8,128)(2,1)S(1)}, u32[]{:S(2)}, u32[]{:S(2)}) collective-permute-start(bf16[576,128]{1,0:T(8,128)(2,1)S(1)} %fusion.1.own_ref), channel_id=1, source_target_pairs={{0,2},{1,3},{2,0},{3,1},{4,6},{5,7},{6,4},{7,5},{8,10},{9,11},{10,... | collective-permute-start | bytes 442376 | tf_op jit(solution)/shard_map/ppermute | solution.py:607
  87.7 1.5 %unpack.1 = (bf16[2,6,32,512]{3,2,1,0:T(8,128)(2,1)}, bf16[2,6,32,512]{3,2,1,0:T(8,128)(2,1)}) custom-call(s32[2]{0:T(128)S(1)} %copy-done, bf16[192,512]{1,0:T(8,128)(2,1)S(1)} %get-tuple-element.88.out_own, bf16[128,512]{1,0:T(8,128)(2,1)S(1)} %collective-permute-done.6.out_away, bf16[192,512]{1,0:T(8,128)(2,1)S(1)} %get-tuple-element.105.grad_own, ...), custom_call_target="tpu_custom_call" | custom-call | flops 1073741824 | bytes 1024 | tf_op jit(solution)/shard_map/unpack/pallas_call | solution.py:553
  89.3 0.9 joina.1
  90.1 1.4 %collective-permute-done.20.far_ref = bf16[576,128]{1,0:T(8,128)(2,1)S(1)} collective-permute-done((bf16[576,128]{1,0:T(8,128)(2,1)S(1)}, bf16[576,128]{1,0:T(8,128)(2,1)S(1)}, u32[]{:S(2)}, u32[]{:S(2)}) %collective-permute-start.20) | collective-permute-done | bytes 147488 | tf_op jit(solution)/shard_map/ppermute | solution.py:607
  91.5 6.4 %collective-permute-done.14 = bf16[1,592,128]{2,1,0:T(8,128)(2,1)S(1)} collective-permute-done((bf16[1,592,128]{2,1,0:T(8,128)(2,1)S(1)}, bf16[1,592,128]{2,1,0:T(8,128)(2,1)S(1)}, u32[]{:S(2)}, u32[]{:S(2)}) %collective-permute-start.14) | collective-permute-done | bytes 151584 | tf_op jit(solution)/shard_map/ppermute | solution.py:610
  97.9 0.1 fusion.own_ref
  98.0 1.2 %joinb.1 = f32[576,512]{1,0:T(8,128)} custom-call(bf16[576,128]{1,0:T(8,128)(2,1)S(1)} %fusion.1.own_ref, bf16[576,128]{1,0:T(8,128)(2,1)S(1)} %collective-permute-done.20.far_ref, bf16[576,128]{1,0:T(8,128)(2,1)S(1)} %collective-permute-done.21.near_ref, bf16[576,128]{1,0:T(8,128)(2,1)S(1)} %collective-permute-done.22.diagonal_ref), custom_call_target="tpu_custom_call" | custom-call | flops 1073741824 | bytes 1024 | tf_op jit(solution)/shard_map/joinb/pallas_call | solution.py:553
  99.2 1.7 %collective-permute-start.30 = (bf16[592,128]{1,0:T(8,128)(2,1)S(1)}, bf16[592,128]{1,0:T(8,128)(2,1)S(1)}, u32[]{:S(2)}, u32[]{:S(2)}) collective-permute-start(bf16[592,128]{1,0:T(8,128)(2,1)S(1)} %fusion.own_ref), channel_id=1, source_target_pairs={{0,2},{1,3},{2,0},{3,1},{4,6},{5,7},{6,4},{7,5},{8,10},{9,11},{10,... | collective-permute-start | bytes 454664 | tf_op jit(solution)/shard_map/ppermute | solution.py:607
  100.8 3.5 %collective-permute-done.30.far_ref = bf16[592,128]{1,0:T(8,128)(2,1)S(1)} collective-permute-done((bf16[592,128]{1,0:T(8,128)(2,1)S(1)}, bf16[592,128]{1,0:T(8,128)(2,1)S(1)}, u32[]{:S(2)}, u32[]{:S(2)}) %collective-permute-start.30) | collective-permute-done | bytes 151584 | tf_op jit(solution)/shard_map/ppermute | solution.py:607
  104.4 1.4 %collective-permute-done.32.diagonal_ref = bf16[592,128]{1,0:T(8,128)(2,1)S(1)} collective-permute-done((bf16[592,128]{1,0:T(8,128)(2,1)S(1)}, bf16[592,128]{1,0:T(8,128)(2,1)S(1)}, u32[]{:S(2)}, u32[]{:S(2)}) %collective-permute-start.32) | collective-permute-done | bytes 151584 | tf_op jit(solution)/shard_map/ppermute | solution.py:604
  105.7 1.2 %joinc.1 = (f32[576,512]{1,0:T(8,128)}, f32[16,128]{1,0:T(8,128)S(1)}) custom-call(bf16[592,128]{1,0:T(8,128)(2,1)S(1)} %fusion.own_ref, bf16[592,128]{1,0:T(8,128)(2,1)S(1)} %collective-permute-done.30.far_ref, bf16[592,128]{1,0:T(8,128)(2,1)S(1)} %collective-permute-done.31.near_ref, bf16[592,128]{1,0:T(8,128)(2,1)S(1)} %collective-permute-done.32.diagonal_ref), custom_call_target="tpu_custom_call" | custom-call | flops 1073741824 | bytes 1024 | tf_op jit(solution)/shard_map/joinc/pallas_call | solution.py:553
  106.9 0.6 slice_bitcast_fusion
  (69 shorter events, 0.2 us)
Async XLA Ops:
  0.7 6.4 %copy-start.7 = (f32[512]{0:T(512)S(1)}, f32[512]{0:T(512)}, u32[]{:S(2)}) copy-start(f32[512]{0:T(512)} %param.22) | copy-start | bytes 6148
  0.7 6.4 %copy-start.8 = (f32[512]{0:T(512)S(1)}, f32[512]{0:T(512)}, u32[]{:S(2)}) copy-start(f32[512]{0:T(512)} %param.23) | copy-start | bytes 6148
  0.7 6.4 %copy-start.17 = (f32[512]{0:T(512)S(1)}, f32[512]{0:T(512)}, u32[]{:S(2)}) copy-start(f32[512]{0:T(512)} %param.38) | copy-start | bytes 6148
  0.7 6.4 %copy-start.9 = (f32[512]{0:T(512)S(1)}, f32[512]{0:T(512)}, u32[]{:S(2)}) copy-start(f32[512]{0:T(512)} %param.25) | copy-start | bytes 6148
  0.7 6.4 %copy-start.10 = (f32[512]{0:T(512)S(1)}, f32[512]{0:T(512)}, u32[]{:S(2)}) copy-start(f32[512]{0:T(512)} %param.26) | copy-start | bytes 6148
  0.7 6.4 %copy-start.11 = (f32[512]{0:T(512)S(1)}, f32[512]{0:T(512)}, u32[]{:S(2)}) copy-start(f32[512]{0:T(512)} %param.27) | copy-start | bytes 6148
  0.7 6.4 %copy-start.12 = (f32[512]{0:T(512)S(1)}, f32[512]{0:T(512)}, u32[]{:S(2)}) copy-start(f32[512]{0:T(512)} %param.29) | copy-start | bytes 6148
  0.7 6.4 %copy-start.13 = (f32[512]{0:T(512)S(1)}, f32[512]{0:T(512)}, u32[]{:S(2)}) copy-start(f32[512]{0:T(512)} %param.30) | copy-start | bytes 6148
  0.7 6.4 %copy-start.14 = (f32[512]{0:T(512)S(1)}, f32[512]{0:T(512)}, u32[]{:S(2)}) copy-start(f32[512]{0:T(512)} %param.31) | copy-start | bytes 6148
  0.8 6.4 %copy-start.15 = (f32[512]{0:T(512)S(1)}, f32[512]{0:T(512)}, u32[]{:S(2)}) copy-start(f32[512]{0:T(512)} %param.33) | copy-start | bytes 6148
  0.8 6.4 %copy-start.16 = (f32[512]{0:T(512)S(1)}, f32[512]{0:T(512)}, u32[]{:S(2)}) copy-start(f32[512]{0:T(512)} %param.36) | copy-start | bytes 6148
  0.8 12.3 %slice-start = ((s8[4718592]{0:T(1024)(128)(4,1)}), s8[524288]{0:T(1024)(128)(4,1)S(1)}, s32[]{:S(2)}) async-start(s8[4718592]{0:T(1024)(128)(4,1)} %bitcast.39), calls=%async_computation | async-start | bytes 1048576
  0.8 19.7 %slice-start.2 = ((s8[4718592]{0:T(1024)(128)(4,1)}), s8[4194304]{0:T(1024)(128)(4,1)S(1)}, s32[]{:S(2)}) async-start(s8[4718592]{0:T(1024)(128)(4,1)} %bitcast.41), calls=%async_computation.2 | async-start | bytes 8388608
  4.1 6.7 %collective-permute-start.1 = (bf16[128,512]{1,0:T(8,128)(2,1)}, bf16[128,512]{1,0:T(8,128)(2,1)S(1)}, u32[]{:S(2)}, u32[]{:S(2)}) collective-permute-start(bf16[128,512]{1,0:T(8,128)(2,1)} %get-tuple-element.80), channel_id=1, source_target_pairs={{0,2},{1,3},{2,0},{3,1},{4,6},{5,7},{6,4},{7,5},{8,10},{9,11},{10,... | collective-permute-start | bytes 393224 | tf_op jit(solution)/shard_map/ppermute | solution.py:607
  7.1 6.0 %collective-permute-start = (bf16[192,512]{1,0:T(8,128)(2,1)}, bf16[192,512]{1,0:T(8,128)(2,1)S(1)}, u32[]{:S(2)}, u32[]{:S(2)}) collective-permute-start(bf16[192,512]{1,0:T(8,128)(2,1)} %get-tuple-element.79.own), channel_id=1, source_target_pairs={{0,1},{1,0},{2,3},{3,2},{4,5},{5,4},{6,7},{7,6},{8,9},{9,8},{10,11... | collective-permute-start | bytes 589832 | tf_op jit(solution)/shard_map/ppermute | solution.py:604
  7.1 6.0 %slice-start.1 = ((s8[4718592]{0:T(1024)(128)(4,1)}), s8[4194304]{0:T(1024)(128)(4,1)S(1)}, s32[]{:S(2)}) async-start(s8[4718592]{0:T(1024)(128)(4,1)} %bitcast.39), calls=%async_computation.1 | async-start | bytes 8388608
  7.2 3.6 %copy-start.5 = (bf16[192,512]{1,0:T(8,128)(2,1)S(1)}, bf16[192,512]{1,0:T(8,128)(2,1)}, u32[]{:S(2)}) copy-start(bf16[192,512]{1,0:T(8,128)(2,1)} %get-tuple-element.85.own) | copy-start | bytes 589828
  7.2 4.1 %copy-start.18 = (bf16[128,512]{1,0:T(8,128)(2,1)S(1)}, bf16[128,512]{1,0:T(8,128)(2,1)}, u32[]{:S(2)}) copy-start(bf16[128,512]{1,0:T(8,128)(2,1)} %get-tuple-element.87) | copy-start | bytes 393220
  7.2 5.9 %copy-start = (s32[2]{0:T(128)S(1)}, s32[2]{0:T(128)}, u32[]{:S(2)}) copy-start(s32[2]{0:T(128)} %get-tuple-element.78.bucket_ref) | copy-start | bytes 28
  7.2 5.9 %copy-start.6 = (bf16[192,512]{1,0:T(8,128)(2,1)S(1)}, bf16[192,512]{1,0:T(8,128)(2,1)}, u32[]{:S(2)}) copy-start(bf16[192,512]{1,0:T(8,128)(2,1)} %get-tuple-element.79.own) | copy-start | bytes 589828
  7.2 13.2 %slice-start.3 = ((s8[4718592]{0:T(1024)(128)(4,1)}), s8[524288]{0:T(1024)(128)(4,1)S(1)}, s32[]{:S(2)}) async-start(s8[4718592]{0:T(1024)(128)(4,1)} %bitcast.41), calls=%async_computation.3 | async-start | bytes 1048576
  10.8 2.3 %collective-permute-start.2 = (bf16[128,512]{1,0:T(8,128)(2,1)S(1)}, bf16[128,512]{1,0:T(8,128)(2,1)S(1)}, u32[]{:S(2)}, u32[]{:S(2)}) collective-permute-start(bf16[128,512]{1,0:T(8,128)(2,1)S(1)} %collective-permute-done.1.received), channel_id=1, source_target_pairs={{0,1},{1,0},{2,3},{3,2},{4,5},{5,4},{6,7},{7,6},{8,9},{9,8},{10,11... | collective-permute-start | bytes 393224 | tf_op jit(solution)/shard_map/ppermute | solution.py:604
  10.8 9.7 %collective-permute-start.3 = (bf16[192,512]{1,0:T(8,128)(2,1)S(1)}, bf16[192,512]{1,0:T(8,128)(2,1)S(1)}, u32[]{:S(2)}, u32[]{:S(2)}) collective-permute-start(bf16[192,512]{1,0:T(8,128)(2,1)S(1)} %copy-done.5), channel_id=1, source_target_pairs={{0,1},{1,0},{2,3},{3,2},{4,5},{5,4},{6,7},{7,6},{8,9},{9,8},{10,11... | collective-permute-start | bytes 589832 | tf_op jit(solution)/shard_map/ppermute | solution.py:604
  11.3 9.2 %collective-permute-start.4 = (bf16[128,512]{1,0:T(8,128)(2,1)S(1)}, bf16[128,512]{1,0:T(8,128)(2,1)S(1)}, u32[]{:S(2)}, u32[]{:S(2)}) collective-permute-start(bf16[128,512]{1,0:T(8,128)(2,1)S(1)} %copy-done.18), channel_id=1, source_target_pairs={{0,2},{1,3},{2,0},{3,1},{4,6},{5,7},{6,4},{7,5},{8,10},{9,11},{10,... | collective-permute-start | bytes 393224 | tf_op jit(solution)/shard_map/ppermute | solution.py:607
  13.0 7.4 %collective-permute-start.5 = (bf16[128,512]{1,0:T(8,128)(2,1)S(1)}, bf16[128,512]{1,0:T(8,128)(2,1)S(1)}, u32[]{:S(2)}, u32[]{:S(2)}) collective-permute-start(bf16[128,512]{1,0:T(8,128)(2,1)S(1)} %copy-done.18), channel_id=1, source_target_pairs={{0,3},{1,2},{2,1},{3,0},{4,7},{5,6},{6,5},{7,4},{8,11},{9,10},{10,... | collective-permute-start | bytes 393224 | tf_op jit(solution)/shard_map/ppermute | solution.py:642
  13.1 7.4 %copy-start.1 = (bf16[512,512]{1,0:T(8,128)(2,1)S(1)}, bf16[512,512]{1,0:T(8,128)(2,1)}, u32[]{:S(2)}) copy-start(bf16[512,512]{1,0:T(8,128)(2,1)} %wq.1) | copy-start | bytes 1572868
  13.1 7.4 %copy-start.2 = (bf16[512,512]{1,0:T(8,128)(2,1)S(1)}, bf16[512,512]{1,0:T(8,128)(2,1)}, u32[]{:S(2)}) copy-start(bf16[512,512]{1,0:T(8,128)(2,1)} %wk.1) | copy-start | bytes 1572868
  13.1 7.4 %copy-start.3 = (bf16[512,512]{1,0:T(8,128)(2,1)S(1)}, bf16[512,512]{1,0:T(8,128)(2,1)}, u32[]{:S(2)}) copy-start(bf16[512,512]{1,0:T(8,128)(2,1)} %wv.1) | copy-start | bytes 1572868
  13.1 7.4 %copy-start.4 = (bf16[512,512]{1,0:T(8,128)(2,1)S(1)}, bf16[512,512]{1,0:T(8,128)(2,1)}, u32[]{:S(2)}) copy-start(bf16[512,512]{1,0:T(8,128)(2,1)} %wp.1) | copy-start | bytes 1572868
  19.0 14.3 %collective-permute-start.7 = (bf16[2,256,512]{2,1,0:T(8,128)(2,1)S(1)}, bf16[2,256,512]{2,1,0:T(8,128)(2,1)S(1)}, u32[]{:S(2)}, u32[]{:S(2)}) collective-permute-start(bf16[2,256,512]{2,1,0:T(8,128)(2,1)S(1)} %get-tuple-element.95), channel_id=1, source_target_pairs={{0,2},{1,3},{2,0},{3,1},{4,6},{5,7},{6,4},{7,5},{8,10},{9,11},{10,... | collective-permute-start | bytes 1572872 | tf_op jit(solution)/shard_map/ppermute | solution.py:607
  31.0 6.8 %collective-permute-start.9 = (bf16[512,128]{1,0:T(8,128)(2,1)S(1)}, bf16[512,128]{1,0:T(8,128)(2,1)S(1)}, u32[]{:S(2)}, u32[]{:S(2)}) collective-permute-start(bf16[512,128]{1,0:T(8,128)(2,1)S(1)} %get-tuple-element.99), channel_id=1, source_target_pairs={{0,2},{1,3},{2,0},{3,1},{4,6},{5,7},{6,4},{7,5},{8,10},{9,11},{10,... | collective-permute-start | bytes 393224 | tf_op jit(solution)/shard_map/ppermute | solution.py:607
  31.7 21.5 %collective-permute-start.23 = (bf16[4,256,256]{2,1,0:T(8,128)(2,1)S(1)}, bf16[4,256,256]{2,1,0:T(8,128)(2,1)S(1)}, u32[]{:S(2)}, u32[]{:S(2)}) collective-permute-start(bf16[4,256,256]{2,1,0:T(8,128)(2,1)S(1)} %get-tuple-element.125), channel_id=1, source_target_pairs={{0,4},{4,0},{8,12},{12,8},{16,20},{20,16},{24,28},{28,24},{1,5},{5... | collective-permute-start | bytes 1572872 | tf_op jit(solution)/shard_map/ppermute | solution.py:610
  33.3 4.5 %collective-permute-start.8 = (bf16[2,256,512]{2,1,0:T(8,128)(2,1)S(1)}, bf16[2,256,512]{2,1,0:T(8,128)(2,1)S(1)}, u32[]{:S(2)}, u32[]{:S(2)}) collective-permute-start(bf16[2,256,512]{2,1,0:T(8,128)(2,1)S(1)} %collective-permute-done.7.half_t), channel_id=1, source_target_pairs={{0,1},{1,0},{2,3},{3,2},{4,5},{5,4},{6,7},{7,6},{8,9},{9,8},{10,11... | collective-permute-start | bytes 1572872 | tf_op jit(solution)/shard_map/ppermute | solution.py:604
  41.0 18.2 %collective-permute-start.16 = (bf16[4,576,128]{2,1,0:T(8,128)(2,1)S(1)}, bf16[4,576,128]{2,1,0:T(8,128)(2,1)S(1)}, u32[]{:S(2)}, u32[]{:S(2)}) collective-permute-start(bf16[4,576,128]{2,1,0:T(8,128)(2,1)S(1)} %get-tuple-element.100), channel_id=1, source_target_pairs={{0,4},{4,0},{8,12},{12,8},{16,20},{20,16},{24,28},{28,24},{1,5},{5... | collective-permute-start | bytes 1769480 | tf_op jit(solution)/shard_map/ppermute | solution.py:610
  42.8 6.7 %collective-permute-start.11 = (bf16[512,128]{1,0:T(8,128)(2,1)S(1)}, bf16[512,128]{1,0:T(8,128)(2,1)S(1)}, u32[]{:S(2)}, u32[]{:S(2)}) collective-permute-start(bf16[512,128]{1,0:T(8,128)(2,1)S(1)} %get-tuple-element.110), channel_id=1, source_target_pairs={{0,2},{1,3},{2,0},{3,1},{4,6},{5,7},{6,4},{7,5},{8,10},{9,11},{10,... | collective-permute-start | bytes 393224 | tf_op jit(solution)/shard_map/ppermute | solution.py:607
  52.6 18.9 %collective-permute-start.12 = (bf16[4,592,128]{2,1,0:T(8,128)(2,1)S(1)}, bf16[4,592,128]{2,1,0:T(8,128)(2,1)S(1)}, u32[]{:S(2)}, u32[]{:S(2)}) collective-permute-start(bf16[4,592,128]{2,1,0:T(8,128)(2,1)S(1)} %get-tuple-element.113), channel_id=1, source_target_pairs={{0,4},{4,0},{8,12},{12,8},{16,20},{20,16},{24,28},{28,24},{1,5},{5... | collective-permute-start | bytes 1818632 | tf_op jit(solution)/shard_map/ppermute | solution.py:610
  53.3 7.6 %collective-permute-start.24 = (bf16[1,256,256]{2,1,0:T(8,128)(2,1)S(1)}, bf16[1,256,256]{2,1,0:T(8,128)(2,1)S(1)}, u32[]{:S(2)}, u32[]{:S(2)}) collective-permute-start(bf16[1,256,256]{2,1,0:T(8,128)(2,1)S(1)} %get-tuple-element.127), channel_id=1, source_target_pairs={{0,8},{4,12},{8,0},{12,4},{16,24},{20,28},{24,16},{28,20},{1,9},{5... | collective-permute-start | bytes 393224 | tf_op jit(solution)/shard_map/ppermute | solution.py:610
  55.0 12.8 %collective-permute-start.25 = (bf16[1,256,256]{2,1,0:T(8,128)(2,1)S(1)}, bf16[1,256,256]{2,1,0:T(8,128)(2,1)S(1)}, u32[]{:S(2)}, u32[]{:S(2)}) collective-permute-start(bf16[1,256,256]{2,1,0:T(8,128)(2,1)S(1)} %get-tuple-element.128), channel_id=1, source_target_pairs={{0,16},{4,20},{8,24},{12,28},{16,0},{20,4},{24,8},{28,12},{1,17},{... | collective-permute-start | bytes 393224 | tf_op jit(solution)/shard_map/ppermute | solution.py:610
  57.6 13.1 %collective-permute-start.26 = (bf16[1,256,256]{2,1,0:T(8,128)(2,1)S(1)}, bf16[1,256,256]{2,1,0:T(8,128)(2,1)S(1)}, u32[]{:S(2)}, u32[]{:S(2)}) collective-permute-start(bf16[1,256,256]{2,1,0:T(8,128)(2,1)S(1)} %get-tuple-element.129), channel_id=1, source_target_pairs={{0,24},{4,28},{8,16},{12,20},{16,8},{20,12},{24,0},{28,4},{1,25},{... | collective-permute-start | bytes 393224 | tf_op jit(solution)/shard_map/ppermute | solution.py:610
  59.3 18.5 %collective-permute-start.17 = (bf16[1,576,128]{2,1,0:T(8,128)(2,1)S(1)}, bf16[1,576,128]{2,1,0:T(8,128)(2,1)S(1)}, u32[]{:S(2)}, u32[]{:S(2)}) collective-permute-start(bf16[1,576,128]{2,1,0:T(8,128)(2,1)S(1)} %get-tuple-element.120), channel_id=1, source_target_pairs={{0,8},{4,12},{8,0},{12,4},{16,24},{20,28},{24,16},{28,20},{1,9},{5... | collective-permute-start | bytes 442376 | tf_op jit(solution)/shard_map/ppermute | solution.py:610
  60.9 19.1 %collective-permute-start.18 = (bf16[1,576,128]{2,1,0:T(8,128)(2,1)S(1)}, bf16[1,576,128]{2,1,0:T(8,128)(2,1)S(1)}, u32[]{:S(2)}, u32[]{:S(2)}) collective-permute-start(bf16[1,576,128]{2,1,0:T(8,128)(2,1)S(1)} %get-tuple-element.121), channel_id=1, source_target_pairs={{0,16},{4,20},{8,24},{12,28},{16,0},{20,4},{24,8},{28,12},{1,17},{... | collective-permute-start | bytes 442376 | tf_op jit(solution)/shard_map/ppermute | solution.py:610
  67.8 12.3 %collective-permute-start.19 = (bf16[1,576,128]{2,1,0:T(8,128)(2,1)S(1)}, bf16[1,576,128]{2,1,0:T(8,128)(2,1)S(1)}, u32[]{:S(2)}, u32[]{:S(2)}) collective-permute-start(bf16[1,576,128]{2,1,0:T(8,128)(2,1)S(1)} %get-tuple-element.122), channel_id=1, source_target_pairs={{0,24},{4,28},{8,16},{12,20},{16,8},{20,12},{24,0},{28,4},{1,25},{... | collective-permute-start | bytes 442376 | tf_op jit(solution)/shard_map/ppermute | solution.py:610
  70.8 6.3 %collective-permute-start.27 = (bf16[256,256]{1,0:T(8,128)(2,1)S(1)}, bf16[256,256]{1,0:T(8,128)(2,1)S(1)}, u32[]{:S(2)}, u32[]{:S(2)}) collective-permute-start(bf16[256,256]{1,0:T(8,128)(2,1)S(1)} %fusion.2.own_ref), channel_id=1, source_target_pairs={{0,2},{1,3},{2,0},{3,1},{4,6},{5,7},{6,4},{7,5},{8,10},{9,11},{10,... | collective-permute-start | bytes 393224 | tf_op jit(solution)/shard_map/ppermute | solution.py:607
  71.5 12.1 %collective-permute-start.6 = (bf16[128,512]{1,0:T(8,128)(2,1)S(1)}, bf16[128,512]{1,0:T(8,128)(2,1)S(1)}, u32[]{:S(2)}, u32[]{:S(2)}) collective-permute-start(bf16[128,512]{1,0:T(8,128)(2,1)S(1)} %get-tuple-element.89), channel_id=1, source_target_pairs={{0,2},{1,3},{2,0},{3,1},{4,6},{5,7},{6,4},{7,5},{8,10},{9,11},{10,... | collective-permute-start | bytes 393224 | tf_op jit(solution)/shard_map/ppermute | solution.py:607
  77.1 7.8 %collective-permute-start.10 = (bf16[128,512]{1,0:T(8,128)(2,1)S(1)}, bf16[128,512]{1,0:T(8,128)(2,1)S(1)}, u32[]{:S(2)}, u32[]{:S(2)}) collective-permute-start(bf16[128,512]{1,0:T(8,128)(2,1)S(1)} %get-tuple-element.106), channel_id=1, source_target_pairs={{0,2},{1,3},{2,0},{3,1},{4,6},{5,7},{6,4},{7,5},{8,10},{9,11},{10,... | collective-permute-start | bytes 393224 | tf_op jit(solution)/shard_map/ppermute | solution.py:607
  77.8 8.6 %collective-permute-start.28 = (bf16[256,256]{1,0:T(8,128)(2,1)S(1)}, bf16[256,256]{1,0:T(8,128)(2,1)S(1)}, u32[]{:S(2)}, u32[]{:S(2)}) collective-permute-start(bf16[256,256]{1,0:T(8,128)(2,1)S(1)} %fusion.2.own_ref), channel_id=1, source_target_pairs={{0,1},{1,0},{2,3},{3,2},{4,5},{5,4},{6,7},{7,6},{8,9},{9,8},{10,11... | collective-permute-start | bytes 393224 | tf_op jit(solution)/shard_map/ppermute | solution.py:604
  80.1 9.2 %collective-permute-start.29 = (bf16[256,256]{1,0:T(8,128)(2,1)S(1)}, bf16[256,256]{1,0:T(8,128)(2,1)S(1)}, u32[]{:S(2)}, u32[]{:S(2)}) collective-permute-start(bf16[256,256]{1,0:T(8,128)(2,1)S(1)} %collective-permute-done.27.far_ref), channel_id=1, source_target_pairs={{0,1},{1,0},{2,3},{3,2},{4,5},{5,4},{6,7},{7,6},{8,9},{9,8},{10,11... | collective-permute-start | bytes 393224 | tf_op jit(solution)/shard_map/ppermute | solution.py:604
  80.1 11.4 %collective-permute-start.13 = (bf16[1,592,128]{2,1,0:T(8,128)(2,1)S(1)}, bf16[1,592,128]{2,1,0:T(8,128)(2,1)S(1)}, u32[]{:S(2)}, u32[]{:S(2)}) collective-permute-start(bf16[1,592,128]{2,1,0:T(8,128)(2,1)S(1)} %get-tuple-element.115), channel_id=1, source_target_pairs={{0,8},{4,12},{8,0},{12,4},{16,24},{20,28},{24,16},{28,20},{1,9},{5... | collective-permute-start | bytes 454664 | tf_op jit(solution)/shard_map/ppermute | solution.py:610
  83.6 14.3 %collective-permute-start.14 = (bf16[1,592,128]{2,1,0:T(8,128)(2,1)S(1)}, bf16[1,592,128]{2,1,0:T(8,128)(2,1)S(1)}, u32[]{:S(2)}, u32[]{:S(2)}) collective-permute-start(bf16[1,592,128]{2,1,0:T(8,128)(2,1)S(1)} %get-tuple-element.116), channel_id=1, source_target_pairs={{0,16},{4,20},{8,24},{12,28},{16,0},{20,4},{24,8},{28,12},{1,17},{... | collective-permute-start | bytes 454664 | tf_op jit(solution)/shard_map/ppermute | solution.py:610
  84.9 13.0 %collective-permute-start.15 = (bf16[1,592,128]{2,1,0:T(8,128)(2,1)S(1)}, bf16[1,592,128]{2,1,0:T(8,128)(2,1)S(1)}, u32[]{:S(2)}, u32[]{:S(2)}) collective-permute-start(bf16[1,592,128]{2,1,0:T(8,128)(2,1)S(1)} %get-tuple-element.117), channel_id=1, source_target_pairs={{0,24},{4,28},{8,16},{12,20},{16,8},{20,12},{24,0},{28,4},{1,25},{... | collective-permute-start | bytes 454664 | tf_op jit(solution)/shard_map/ppermute | solution.py:610
  86.4 5.1 %collective-permute-start.20 = (bf16[576,128]{1,0:T(8,128)(2,1)S(1)}, bf16[576,128]{1,0:T(8,128)(2,1)S(1)}, u32[]{:S(2)}, u32[]{:S(2)}) collective-permute-start(bf16[576,128]{1,0:T(8,128)(2,1)S(1)} %fusion.1.own_ref), channel_id=1, source_target_pairs={{0,2},{1,3},{2,0},{3,1},{4,6},{5,7},{6,4},{7,5},{8,10},{9,11},{10,... | collective-permute-start | bytes 442376 | tf_op jit(solution)/shard_map/ppermute | solution.py:607
  90.1 7.9 %collective-permute-start.21 = (bf16[576,128]{1,0:T(8,128)(2,1)S(1)}, bf16[576,128]{1,0:T(8,128)(2,1)S(1)}, u32[]{:S(2)}, u32[]{:S(2)}) collective-permute-start(bf16[576,128]{1,0:T(8,128)(2,1)S(1)} %fusion.1.own_ref), channel_id=1, source_target_pairs={{0,1},{1,0},{2,3},{3,2},{4,5},{5,4},{6,7},{7,6},{8,9},{9,8},{10,11... | collective-permute-start | bytes 442376 | tf_op jit(solution)/shard_map/ppermute | solution.py:604
  91.5 6.5 %collective-permute-start.22 = (bf16[576,128]{1,0:T(8,128)(2,1)S(1)}, bf16[576,128]{1,0:T(8,128)(2,1)S(1)}, u32[]{:S(2)}, u32[]{:S(2)}) collective-permute-start(bf16[576,128]{1,0:T(8,128)(2,1)S(1)} %collective-permute-done.20.far_ref), channel_id=1, source_target_pairs={{0,1},{1,0},{2,3},{3,2},{4,5},{5,4},{6,7},{7,6},{8,9},{9,8},{10,11... | collective-permute-start | bytes 442376 | tf_op jit(solution)/shard_map/ppermute | solution.py:604
  99.2 5.2 %collective-permute-start.30 = (bf16[592,128]{1,0:T(8,128)(2,1)S(1)}, bf16[592,128]{1,0:T(8,128)(2,1)S(1)}, u32[]{:S(2)}, u32[]{:S(2)}) collective-permute-start(bf16[592,128]{1,0:T(8,128)(2,1)S(1)} %fusion.own_ref), channel_id=1, source_target_pairs={{0,2},{1,3},{2,0},{3,1},{4,6},{5,7},{6,4},{7,5},{8,10},{9,11},{10,... | collective-permute-start | bytes 454664 | tf_op jit(solution)/shard_map/ppermute | solution.py:607
  100.8 3.5 %collective-permute-start.31 = (bf16[592,128]{1,0:T(8,128)(2,1)S(1)}, bf16[592,128]{1,0:T(8,128)(2,1)S(1)}, u32[]{:S(2)}, u32[]{:S(2)}) collective-permute-start(bf16[592,128]{1,0:T(8,128)(2,1)S(1)} %fusion.own_ref), channel_id=1, source_target_pairs={{0,1},{1,0},{2,3},{3,2},{4,5},{5,4},{6,7},{7,6},{8,9},{9,8},{10,11... | collective-permute-start | bytes 454664 | tf_op jit(solution)/shard_map/ppermute | solution.py:604
  104.4 1.4 %collective-permute-start.32 = (bf16[592,128]{1,0:T(8,128)(2,1)S(1)}, bf16[592,128]{1,0:T(8,128)(2,1)S(1)}, u32[]{:S(2)}, u32[]{:S(2)}) collective-permute-start(bf16[592,128]{1,0:T(8,128)(2,1)S(1)} %collective-permute-done.30.far_ref), channel_id=1, source_target_pairs={{0,1},{1,0},{2,3},{3,2},{4,5},{5,4},{6,7},{7,6},{8,9},{9,8},{10,11... | collective-permute-start | bytes 454664 | tf_op jit(solution)/shard_map/ppermute | solution.py:604

commit v4 on v3

--- a/solution.py
+++ b/solution.py
@@ -21,7 +21,7 @@
 HB = pl.BlockSpec(memory_space=pltpu.HBM)
 RATE = 1 << 30
 LENGTH = {
-    "pack": 10, "stack": 10, "first": 8, "second": 30, "third": 20, "fourth": 0.02, "weight2": 0.02, "weight1": 0.02,
+    "pack": 10, "stack": 10, "first": 0.02, "second": 30, "third": 20, "fourth": 0.02, "weight2": 1, "weight1": 0.02,
 }
 
 
@@ -214,47 +214,46 @@
     return vec_ref[index : index + 1, :]
 
 
-def pack_kernel(
-    bucket_hbm, x_ref, cot_ref, kinds, away_x, home_x, away_c, home_c, bucket_ref, bucket_sem, sems
-):
-    copy = pltpu.make_async_copy(bucket_hbm, bucket_ref, bucket_sem.at[0])
-    copy.start()
-    copy.wait()
+def pack(src, facts, dst, wide_rows):
+    image, tall, stride, width = facts
+
+    @pl.when(tall)
+    def _():
+        for row in range(6):
+            dst[16 * row : 16 * row + 16, :] = src[image, row, 0:16, :]
+        dst[96 : dst.shape[0], :] = jnp.zeros((dst.shape[0] - 96, dst.shape[1]), dst.dtype)
+
+    @pl.when(jnp.logical_not(tall))
+    def _():
+        for row in range(wide_rows):
+            dst[32 * row : 32 * row + 32, :] = src[image, row]
+
+
+def pack_kernel(bucket_hbm, x_hbm, kinds, away_x, home_x, bucket_ref, x_ref, sems):
+    copies = (
+        pltpu.make_async_copy(bucket_hbm, bucket_ref, sems.at[0]),
+        pltpu.make_async_copy(x_hbm, x_ref, sems.at[1]),
+    )
+    for copy in copies:
+        copy.start()
+    for copy in copies:
+        copy.wait()
     h, home, away = place(bucket_ref)
-
-    def each(act):
-        slot = 0
-        for src, away_ref, home_ref in ((x_ref, away_x, home_x), (cot_ref, away_c, home_c)):
-            for facts, dst, wide_rows in ((away, away_ref, 4), (home, home_ref, 6)):
-                image, tall, stride, width = facts
-
-                @pl.when(tall)
-                def _():
-                    for row in range(6):
-                        act(
-                            src.at[image, row, pl.ds(0, 16), :],
-                            dst.at[pl.ds(16 * row, 16), :],
-                            sems.at[slot + row],
-                        )
-
-                @pl.when(jnp.logical_not(tall))
-                def _():
-                    for row in range(wide_rows):
-                        act(src.at[image, row], dst.at[pl.ds(32 * row, 32), :], sems.at[slot + row])
-
-                slot += 6
-
-    each(lambda a, b, sem: pltpu.make_async_copy(a, b, sem).start())
     kinds[0] = bucket_ref[0]
     kinds[1] = bucket_ref[1]
-    each(lambda a, b, sem: pltpu.make_async_copy(a, b, sem).wait())
-
-
-def stack_kernel(*refs):
-    out_ref = refs[-1]
-    for index, ref in enumerate(refs[:-1]):
+    pack(x_ref, away, away_x, 4)
+    pack(x_ref, home, home_x, 6)
+
+
+def stack_kernel(kinds, cot_ref, *refs):
+    h, home, away = place(kinds)
+    out_ref, away_c, home_c = refs[-3:]
+    count = len(refs) - 3
+    for index, ref in enumerate(refs[:count]):
         out_ref[index : index + 1, :] = ref[...]
-    out_ref[len(refs) - 1 :, :] = jnp.zeros((VECS - len(refs) + 1, out_ref.shape[1]), F32)
+    out_ref[count:, :] = jnp.zeros((VECS - count, out_ref.shape[1]), F32)
+    pack(cot_ref, away, away_c, 4)
+    pack(cot_ref, home, home_c, 6)
 
 
 def first_kernel(
@@ -294,9 +293,9 @@
 def second_kernel(
     bucket_ref, image_ref, act2_ref, own, partner, received, partner_received, vecs,
     weight2, wq, wk, wv, wp,
-    out_own, out_send, grad2_ref, grad_middle_ref, attn_keep, attn_send, vec_ref,
+    middle_ref, mixed_ref, grad2_ref, grad_middle_ref, attn_keep, attn_send, vec_ref,
     block_keep, block_send,
-    shift_ref, full_ref, middle_ref, grads_ref, sum_ref,
+    shift_ref, full_ref, grads_ref, sum_ref,
 ):
     h, home, away = place(bucket_ref)
     stride = home[2]
@@ -324,9 +323,7 @@
     soft = raised * (1.0 / jnp.sum(raised, axis=1, keepdims=True))
     soft16 = soft.astype(BF16)
     mixed = mm(soft16, values).astype(BF16)
-    projected = mm(mixed, wp[...]) + vec(vecs, PB)
-    full_ref[...] = (mask * (middle_ref[...] + projected)).astype(BF16)
-    split_out(full_ref, home, h, out_own, out_send)
+    mixed_ref[...] = mixed
 
     assemble(full_ref, home, h, (own, partner, received, partner_received))
     grad_top = full_ref[...].astype(F32) * mask
@@ -412,8 +409,9 @@
 
 
 def fourth_kernel(
-    bucket_ref, grad1_ref, image_ref, stats_ref, grad_middle_ref, vecs, weight1, vec_a, vec_b,
-    grad_own, grad_send, vec_out,
+    bucket_ref, grad1_ref, image_ref, stats_ref, grad_middle_ref, middle_ref, mixed_ref, vecs,
+    weight1, wp, vec_a, vec_b,
+    out_own, grad_own, send_ref, vec_keep, vec_send,
     shift_ref, acc_ref, full_ref, vec_ref,
 ):
     h, home, away = place(bucket_ref)
@@ -421,6 +419,9 @@
     mask, pixels = pixel_mask(home)
     channels = vecs.shape[1]
     group_size = pixels * (channels // GROUPS)
+    projected = mm(mixed_ref[...], wp[...]) + vec(vecs, PB)
+    full_ref[...] = (mask * (middle_ref[...] + projected)).astype(BF16)
+    split_out(full_ref, home, h, out_own, send_ref.at[0])
     fill_shifts(shift_ref, grad1_ref[...].astype(F32), stride)
     conv_backward(shift_ref, weight1, stride, acc_ref)
     inverse = stats_ref[1:2, :]
@@ -431,28 +432,30 @@
         grad, normal, inverse, mask, group_size, vec(vecs, GAIN1)
     )
     full_ref[...] = (mask * (grad_middle_ref[...] + grad_in)).astype(BF16)
-    split_out(full_ref, home, h, grad_own, grad_send)
+    split_out(full_ref, home, h, grad_own, send_ref.at[1])
     vec_ref[0:6, :] = vec_a[0:6, :]
     vec_ref[6:9, :] = vec_b[0:3, :]
     vec_ref[9:10, :] = gain_grad
     vec_ref[10:11, :] = shift_grad
     vec_ref[11:VECS, :] = jnp.zeros((VECS - 11, channels), F32)
-    batches = vec_out.shape[0]
-    rows = channels // batches
-    for shard in range(batches):
-        start = shard * rows
-        tile = start // BLK * BLK
-        part = vec_ref[:, tile : tile + BLK]
-        if start > tile:
-            part = pltpu.roll(part, BLK - (start - tile), 1)
-        vec_out[shard] = part
+    pairs = vec_keep.shape[0]
+    rows = channels // (2 * pairs)
+    mine = (lax.axis_index("batch") & 1) == 1
+    for pair in range(pairs):
+        parts = []
+        for shard in (2 * pair, 2 * pair + 1):
+            start = shard * rows
+            tile = start // BLK * BLK
+            part = vec_ref[:, tile : tile + BLK]
+            parts.append(part if start == tile else pltpu.roll(part, BLK - (start - tile), 1))
+        vec_keep[pair] = jnp.where(mine, parts[1], parts[0]).astype(BF16)
+        vec_send[pair] = jnp.where(mine, parts[0], parts[1]).astype(BF16)
 
 
 def weight_kernel(
-    bucket_ref, act_t, half_t, partner_half_t, block_own, block_away, *rest, layer, tail
+    bucket_ref, act_t, half_t, partner_half_t, block_own, block_away,
+    keep_ref, send_ref, left_ref, right_ref, shift_ref, sum_ref, *, layer,
 ):
-    vec_in = rest[0] if tail else None
-    keep_ref, send_ref, left_ref, right_ref, shift_ref, sum_ref = rest[tail:]
     h, home, away = place(bucket_ref)
     channels = act_t.shape[0]
     half = channels // 2
@@ -479,19 +482,24 @@
     for pair in range(pairs):
         for dst, which in ((keep_ref, mine), (send_ref, 1 - mine)):
             shard = 2 * pair + which
-            dst[pair, 0:rows, :] = sum_ref[pl.ds(pl.multiple_of(shard * rows, 8), rows), :].astype(BF16)
-            if tail:
-                dst[pair, rows : rows + VECS, :] = vec_in[shard].astype(BF16)
-
-
-def route_kernel(bit, keep_ref, got_ref, own_ref, *out_refs):
-    group = (lax.axis_index("batch") >> bit) & (len(out_refs))
-    count = own_ref.shape[0]
-    for step, dst in enumerate((own_ref,) + out_refs):
-        which = group ^ step
-        for index in range(count):
-            at = index * (len(out_refs) + 1) + which
-            dst[index] = (keep_ref[at].astype(F32) + got_ref[at].astype(F32)).astype(BF16)
+            dst[pair] = sum_ref[pl.ds(pl.multiple_of(shard * rows, 8), rows), :].astype(BF16)
+
+
+def route_kernel(*refs, bit, ways):
+    group = (lax.axis_index("batch") >> bit) & (ways - 1)
+    outs = refs[len(refs) - ways :]
+    count = outs[0].shape[0]
+    first = 0
+    for keep_ref, got_ref in zip(refs[0 : len(refs) - ways : 2], refs[1 : len(refs) - ways : 2]):
+        rows = keep_ref.shape[1]
+        for step, dst in enumerate(outs):
+            which = group ^ step
+            for index in range(count):
+                at = index * ways + which
+                dst[index, first : first + rows, :] = (
+                    keep_ref[at].astype(F32) + got_ref[at].astype(F32)
+                ).astype(BF16)
+        first += rows
 
 
 def join_kernel(own_ref, far_ref, near_ref, diagonal_ref, out_ref, *tail_ref):
@@ -502,7 +510,9 @@
     if tail_ref:
         own, far = own_ref[rows:, :].astype(F32), far_ref[rows:, :].astype(F32)
         near, diagonal = near_ref[rows:, :].astype(F32), diagonal_ref[rows:, :].astype(F32)
-        tail_ref[0][...] = 0.5 * ((own + near) + (far + diagonal))
+        sums = 0.5 * ((own + near) + (far + diagonal))
+        for index, dst in enumerate(tail_ref):
+            dst[...] = sums[index : index + 1, 0 : dst.shape[1]]
 
 
 def join_attn_kernel(own_ref, far_ref, near_ref, diagonal_ref, *out_refs):
@@ -519,9 +529,12 @@
                 ) + second[at : at + rows, other : other + BLK].astype(F32)
 
 
-def unpack_kernel(bucket_ref, out_own, out_away, grad_own, grad_away, out_ref, grad_ref):
+def unpack_kernel(bucket_ref, out_own, grad_own, away_ref, out_ref, grad_ref):
     h, home, away = place(bucket_ref)
-    for own, received, dst in ((out_own, out_away, out_ref), (grad_own, grad_away, grad_ref)):
+    for own, received, dst in (
+        (out_own, away_ref.at[0], out_ref),
+        (grad_own, away_ref.at[1], grad_ref),
+    ):
         channels = dst.shape[3]
         for facts, src, wide_rows in ((away, received, 4), (home, own, 6)):
             image, tall, stride, width = facts
@@ -564,7 +577,7 @@
         ],
         compiler_params=pltpu.CompilerParams(vmem_limit_bytes=vmem << 20),
         cost_estimate=pl.CostEstimate(
-            flops=int(LENGTH.get(name, 1) * RATE), bytes_accessed=1024, transcendentals=0
+            flops=int(LENGTH.get(name, 0.02) * RATE), bytes_accessed=1024, transcendentals=0
         ),
     )(*operands)
 
@@ -619,27 +632,26 @@
     turned = ((C, PIX), BF16)
     shifts = ((3, PIX + 2 * PAD, C), BF16)
 
-    kinds, away_x, home_x, away_c, home_c = call(
+    kinds, away_x, home_x = call(
         pack_kernel, "pack",
-        [((2,), jnp.int32), ((128, C), BF16), ((192, C), BF16), ((128, C), BF16), ((192, C), BF16)],
-        [((2,), jnp.int32), ((1,), None), ((24,), None)], 54, bucket, inputs, cotangent,
+        [((2,), jnp.int32), ((128, C), BF16), ((192, C), BF16)],
+        [((2,), jnp.int32), (inputs.shape, BF16), ((2,), None)], 54, bucket, inputs,
         smem=0, any_from=0,
     )
     vectors = (
         norm1_gain, norm1_shift, conv1_bias, norm2_gain, norm2_shift, conv2_bias,
         norm3_gain, norm3_shift, query_bias, value_bias, proj_bias,
     )
-    (vecs,) = call(
-        stack_kernel, "stack", [((VECS, C), F32)], [], 8,
-        after(row(vectors[0]), away_x), *[row(v) for v in vectors[1:]], smem=0,
-    )
     recv_x = to_chip(away_x)
     core_x = to_core(home_x)
-    recv_x = after(recv_x, vecs)
-    recv_c = to_chip(after(away_c, recv_x))
+    vecs, away_c, home_c = call(
+        stack_kernel, "stack", [((VECS, C), F32), ((128, C), BF16), ((192, C), BF16)], [], 8,
+        kinds, cotangent, *[row(v) for v in vectors],
+    )
+    recv_c = to_chip(away_c)
     core_c = to_core(home_c)
-    core_recv_x = to_core(recv_x)
-    core_recv_c = lax.ppermute(after(away_c, recv_x), "height", [(i, i ^ 3) for i in range(4)])
+    core_recv_c = lax.ppermute(away_c, "height", [(i, i ^ 3) for i in range(4)])
+    core_recv_x = to_core(after(recv_x, vecs))
 
     image, conv, act2, stats, act1_t, act2_t, send_t = call(
         first_kernel, "first",
@@ -651,15 +663,14 @@
     core_half_t = to_core(half_t)
 
     attn_out = ((batches // 2, 4 * small_rows, 2 * BLK), BF16)
-    out_own, out_send, grad2, grad_middle, attn_keep, attn_send, vec_a, block2, block2_send = call(
+    middle, mixed, grad2, grad_middle, attn_keep, attn_send, vec_a, block2, block2_send = call(
         second_kernel, "second",
-        [((192, C), BF16), ((128, C), BF16), img16, img32, attn_out, attn_out, rows8, block, block],
-        [shifts, img16, img32, ((PIX, 4 * C), BF16), ((C, 8 * BLK), F32)], 32,
+        [img32, img16, img16, img32, attn_out, attn_out, rows8, block, block],
+        [shifts, img16, ((PIX, 4 * C), BF16), ((C, 8 * BLK), F32)], 32,
         kinds, image, act2, home_c, core_c, recv_c, core_recv_c, vecs,
         conv2_weight, query_weight, key_weight, value_weight, proj_weight,
     )
     block2_away = to_chip(block2_send)
-    out_away = to_chip(out_send)
     attn_got = to_batch(attn_send, 1)
 
     grad1, block1, block1_send, vec_b = call(
@@ -670,72 +681,75 @@
     )
     block1_away = to_chip(block1_send)
 
-    def weight_grad(name, act_t, index, own, away, *tail):
-        rows = shard_rows + (VECS if tail else 0)
+    def weight_grad(name, act_t, index, own, away):
         return call(
-            functools.partial(weight_kernel, layer=index, tail=len(tail)), name,
-            [((batches // 2, rows, BLK), BF16)] * 2,
+            functools.partial(weight_kernel, layer=index), name,
+            [((batches // 2, shard_rows, BLK), BF16)] * 2,
             [((C, 2 * PIX), BF16), ((2 * PIX, 9 * BLK), BF16), ((3, PIX + 2 * PAD, BLK), BF16),
              ((9 * C, BLK), F32)],
-            24, kinds, act_t, half_t, core_half_t, own, away, *tail,
+            24, kinds, act_t, half_t, core_half_t, own, away,
         )
 
     keep2, send2 = weight_grad("weight2", act2_t, 1, after(block2, block1), block2_away)
     got2 = to_batch(send2, 1)
 
-    grad_own, grad_send, vec_c = call(
-        fourth_kernel, "fourth",
-        [((192, C), BF16), ((128, C), BF16), ((batches, VECS, BLK), F32)],
-        [shifts, img32, img16, ((VECS, C), F32)], 24,
-        kinds, after(grad1, send2), image, stats, grad_middle, vecs, conv1_weight, vec_a, vec_b,
-    )
-    grad_away = to_chip(grad_send)
-    keep1, send1 = weight_grad("weight1", act1_t, 0, block1, block1_away, vec_c)
-    got1 = to_batch(send1, 1)
-
-    def scatter(name, keep, got):
+    def scatter(name, *pairs):
         bit = 1
-        while bit < bits:
+        while True:
             width = min(2, bits - bit)
             ways = 1 << width
-            shape = (keep.shape[0] // ways,) + keep.shape[1:]
+            count = pairs[0].shape[0] // ways
+            rows = sum(v.shape[1] for v in pairs[::2])
             parts = call(
-                functools.partial(route_kernel, bit), name + str(bit),
-                [(shape, BF16)] * ways, [], 16, keep, got, smem=0,
+                functools.partial(route_kernel, bit=bit, ways=ways), name + str(bit),
+                [((count, rows, pairs[0].shape[2]), BF16)] * ways, [], 16, *pairs, smem=0,
             )
             got = [to_batch(parts[j], j << bit) for j in range(1, ways)]
             bit += width
-            if bit < bits:
-                keep = parts[0]
-                got = functools.reduce(lambda a, b: a + b, [g.astype(F32) for g in got]).astype(BF16)
-            else:
-                added = parts[0].astype(F32)
-                for g in got:
-                    added = added + g.astype(F32)
-                return added.astype(BF16)[0]
+            added = functools.reduce(lambda a, b: a + b, [g.astype(F32) for g in got])
+            if bit == bits:
+                return parts, (added + parts[0].astype(F32)).astype(BF16)[0]
+            pairs = (parts[0], added.astype(BF16))
 
     def gather(shard):
         far = to_chip(shard)
         near = to_core(shard)
         return shard, far, near, to_core(far)
 
-    attn_parts = gather(scatter("routea", after(attn_keep, send1), attn_got))
-    parts2 = gather(scatter("routeb", keep2, got2))
+    routed_a, shard_a = scatter("routea", after(attn_keep, send2), attn_got)
+    keep1, send1 = weight_grad("weight1", act1_t, 0, after(block1, *routed_a), block1_away)
+    got1 = to_batch(send1, 1)
+
+    out_own, grad_own, image_send, vec_keep, vec_send = call(
+        fourth_kernel, "fourth",
+        [((192, C), BF16), ((192, C), BF16), ((2, 128, C), BF16),
+         ((batches // 2, VECS, BLK), BF16), ((batches // 2, VECS, BLK), BF16)],
+        [shifts, img32, img16, ((VECS, C), F32)], 24,
+        kinds, after(grad1, send1), image, stats, grad_middle, middle, mixed, vecs,
+        conv1_weight, proj_weight, vec_a, vec_b,
+    )
+    image_away = to_chip(image_send)
+    vec_got = to_batch(vec_send, 1)
+
+    routed_b, shard_b = scatter("routeb", after(keep2, shard_a, vec_keep), got2)
+    parts_a = gather(after(shard_a, *routed_b))
     small = call(
-        join_attn_kernel, "joina", [((small_rows, C), F32)] * 4, [], 8, *attn_parts, smem=0
-    )
-    (whole2,) = call(join_kernel, "joinb", [((shard_rows, C), F32)], [], 8, *parts2, smem=0)
+        join_attn_kernel, "joina", [((small_rows, C), F32)] * 4, [], 8, *parts_a, smem=0
+    )
     outputs, input_grad = call(
         unpack_kernel, "unpack",
         [(inputs.shape, BF16)] * 2, [], 8,
-        kinds, out_own, out_away, grad_own, grad_away,
-    )
-    shard1 = scatter("routec", keep1, got1)
-    parts1 = gather(after(shard1, whole2, small[0], outputs))
-    whole1, sums = call(
-        join_kernel, "joinc", [((shard_rows, C), F32), ((VECS, BLK), F32)], [], 8, *parts1, smem=0
-    )
-    v = [sums[i, :small_rows] for i in range(11)]
+        kinds, out_own, grad_own, after(image_away, *routed_b),
+    )
+    routed_c, shard_c = scatter(
+        "routec", after(keep1, shard_b), got1, vec_keep, vec_got
+    )
+    (whole2,) = call(join_kernel, "joinb", [((shard_rows, C), F32)], [], 8, *gather(shard_b), smem=0)
+    whole1, *sums = call(
+        join_kernel, "joinc", [((shard_rows, C), F32)] + [((1, small_rows), F32)] * 11, [], 8,
+        *gather(after(shard_c, whole2, small[0], outputs)), smem=0,
+    )
+    v = [row.reshape(small_rows) for row in sums]
 
     return (
         outputs, input_grad,

time: 108 us -> 99 us (0.917)
  waiting for transfers between devices: 28.3 us -> 23.1 us
  starting transfers between devices: 36.8 us -> 32.8 us
    ppermute x10 -> x9, waiting for transfers between devices: 12.6 us -> 7.26 us  [to_chip(): return lax.ppermute(v, 'height', [(i, i ^ 2) for i in range(4)])]
    ppermute x12 -> x13, starting transfers between devices: 21.8 us -> 18.5 us  [to_batch(): return lax.ppermute(v, 'batch', [(i, i ^ change) for i in range(batches)])]
    ppermute x10 -> x9, starting transfers between devices: 14.4 us -> 13.1 us  [to_chip(): return lax.ppermute(v, 'height', [(i, i ^ 2) for i in range(4)])]
    ppermute x12 -> x13, waiting for transfers between devices: 14.3 us -> 14.5 us  [to_batch(): return lax.ppermute(v, 'batch', [(i, i ^ change) for i in range(batches)])]
  transfers between devices with their start and end apart: 33 -> 33, of which waited for: 10 -> 8; matrix products, arithmetic and copies ran while one was open for 0% -> 0% of each run, Pallas kernels for 32% -> 36%
where the time goes in v4:
time: 99 us; the launch traced here: 98.4 us
  Pallas kernels  39.9 us (40%)
  starting transfers between devices  32.8 us (33%)
  waiting for transfers between devices  23.1 us (23%)
  between operations  1.33 us (1%)
    pallas_call x15, Pallas kernels, call(): pl.pallas_call(kernel, name=name, out_shape=[jax.ShapeDtypeStruct(shape,...  39.9 us
    ppermute x13, starting transfers between devices, to_batch(): return lax.ppermute(v, 'batch', [(i, i ^ change) for i in range(batches)])  18.5 us
    ppermute x13, waiting for transfers between devices, to_batch(): return lax.ppermute(v, 'batch', [(i, i ^ change) for i in range(batches)])  14.5 us
    ppermute x9, starting transfers between devices, to_chip(): return lax.ppermute(v, 'height', [(i, i ^ 2) for i in range(4)])  13.1 us
    ppermute x9, waiting for transfers between devices, to_chip(): return lax.ppermute(v, 'height', [(i, i ^ 2) for i in range(4)])  7.26 us
  transfers between devices with their start and end apart: 33, of which 8 were waited for; matrix products, arithmetic and copies ran while one was open for 0% of the time, Pallas kernels for 36%

profile of v4, /device:TPU:0, one launch (start us, length us, event | category | flops | bytes accessed | tf_op | source)
XLA Modules:
  0.0 98.4 jit_solution(4798855848977921646)
XLA Ops:
  0.8 0.0 slice-start
  0.8 0.0 slice-start.2
  0.8 1.9 %pack.1 = (s32[2]{0:T(128)}, bf16[128,512]{1,0:T(8,128)(2,1)}, bf16[192,512]{1,0:T(8,128)(2,1)}) custom-call(s32[2]{0:T(128)} %bucket_hbm.1, bf16[2,6,32,512]{3,2,1,0:T(8,128)(2,1)} %x_hbm.1), custom_call_target="tpu_custom_call" | custom-call | flops 10737418240 | bytes 1024 | tf_op jit(solution)/shard_map/pack/pallas_call | solution.py:566
  2.7 3.0 %collective-permute-start.1 = (bf16[128,512]{1,0:T(8,128)(2,1)}, bf16[128,512]{1,0:T(8,128)(2,1)S(1)}, u32[]{:S(2)}, u32[]{:S(2)}) collective-permute-start(bf16[128,512]{1,0:T(8,128)(2,1)} %get-tuple-element.96), channel_id=1, source_target_pairs={{0,2},{1,3},{2,0},{3,1},{4,6},{5,7},{6,4},{7,5},{8,10},{9,11},{10,... | collective-permute-start | bytes 393224 | tf_op jit(solution)/shard_map/ppermute | solution.py:620
  5.9 0.0 copy-start.2
  5.9 0.8 copy-done.2
  6.7 0.6 stack.1
  7.3 0.0 copy-start
  7.3 0.0 copy-start.4
  7.3 0.0 copy-start.5
  7.3 0.0 copy-start.6
  7.3 0.6 collective-permute-start.3
  7.9 1.6 %collective-permute-done.1.received = bf16[128,512]{1,0:T(8,128)(2,1)S(1)} collective-permute-done((bf16[128,512]{1,0:T(8,128)(2,1)}, bf16[128,512]{1,0:T(8,128)(2,1)S(1)}, u32[]{:S(2)}, u32[]{:S(2)}) %collective-permute-start.1) | collective-permute-done | bytes 131104 | tf_op jit(solution)/shard_map/ppermute | solution.py:620
  9.5 1.7 %collective-permute-start.4 = (bf16[128,512]{1,0:T(8,128)(2,1)S(1)}, bf16[128,512]{1,0:T(8,128)(2,1)S(1)}, u32[]{:S(2)}, u32[]{:S(2)}) collective-permute-start(bf16[128,512]{1,0:T(8,128)(2,1)S(1)} %get-tuple-element.102), channel_id=1, source_target_pairs={{0,2},{1,3},{2,0},{3,1},{4,6},{5,7},{6,4},{7,5},{8,10},{9,11},{10,... | collective-permute-start | bytes 393224 | tf_op jit(solution)/shard_map/ppermute | solution.py:620
  11.2 0.1 collective-permute-start.5
  11.4 5.8 %first.1 = (bf16[512,512]{1,0:T(8,128)(2,1)S(1)}, f32[512,512]{1,0:T(8,128)S(1)}, bf16[512,512]{1,0:T(8,128)(2,1)S(1)}, f32[8,512]{1,0:T(8,128)S(1)}, bf16[512,5...) custom-call(s32[2]{0:T(128)S(1)} %copy-done.3, bf16[192,512]{1,0:T(8,128)(2,1)S(1)} %copy-done.1, ...), custom_call_target="tpu_custom_call" | custom-call | flops 21474836 | bytes 1024 | tf_op jit(solution)/shard_map/first/pallas_call | solution.py:566
  17.2 1.8 %collective-permute-start.6 = (bf16[2,256,512]{2,1,0:T(8,128)(2,1)S(1)}, bf16[2,256,512]{2,1,0:T(8,128)(2,1)S(1)}, u32[]{:S(2)}, u32[]{:S(2)}) collective-permute-start(bf16[2,256,512]{2,1,0:T(8,128)(2,1)S(1)} %get-tuple-element.108), channel_id=1, source_target_pairs={{0,2},{1,3},{2,0},{3,1},{4,6},{5,7},{6,4},{7,5},{8,10},{9,11},{10,... | collective-permute-start | bytes 1572872 | tf_op jit(solution)/shard_map/ppermute | solution.py:620
  19.1 10.3 %second.1 = (f32[512,512]{1,0:T(8,128)S(1)}, bf16[512,512]{1,0:T(8,128)(2,1)S(1)}, bf16[512,512]{1,0:T(8,128)(2,1)S(1)}, f32[512,512]{1,0:T(8,128)S(1)}, bf16[4,...) custom-call(s32[2]{0:T(128)S(1)} %copy-done.3, ...), custom_call_target="tpu_custom_call" | custom-call | flops 32212254720 | bytes 1024 | tf_op jit(solution)/shard_map/second/pallas_call | solution.py:566
  29.4 0.6 collective-permute-start.8
  29.9 1.5 %collective-permute-start.9 = (bf16[4,256,256]{2,1,0:T(8,128)(2,1)S(1)}, bf16[4,256,256]{2,1,0:T(8,128)(2,1)S(1)}, u32[]{:S(2)}, u32[]{:S(2)}) collective-permute-start(bf16[4,256,256]{2,1,0:T(8,128)(2,1)S(1)} %get-tuple-element.117), channel_id=1, source_target_pairs={{0,4},{4,0},{8,12},{12,8},{16,20},{20,16},{24,28},{28,24},{1,5},{5... | collective-permute-start | bytes 1572872 | tf_op jit(solution)/shard_map/ppermute | solution.py:623
  31.4 4.5 %third.1 = (bf16[512,512]{1,0:T(8,128)(2,1)S(1)}, bf16[512,128]{1,0:T(8,128)(2,1)S(1)}, bf16[512,128]{1,0:T(8,128)(2,1)S(1)}, f32[8,512]{1,0:T(8,128)S(1)}) custom-call(s32[2]{0:T(128)S(1)} %copy-done.3, bf16[512,512]{1,0:T(8,128)(2,1)S(1)} %get-tuple-element.103.grad2_ref, f32[512,512]{1,0:T(8,128)S(1)} %get-tuple-element.104.conv_ref, ...), custom_call_target="tpu_custom_call" | custom-call | flops 21474836480 | bytes 1024 | tf_op jit(solution)/shard_map/third/pallas_call | solution.py:566
  36.0 0.0 collective-permute-done.8.block_away
  36.0 3.1 %weight2.5 = (bf16[4,576,128]{2,1,0:T(8,128)(2,1)S(1)}, bf16[4,576,128]{2,1,0:T(8,128)(2,1)S(1)}) custom-call(s32[2]{0:T(128)S(1)} %copy-done.3, bf16[512,512]{1,0:T(8,128)(2,1)S(1)} %get-tuple-element.111.act_t, bf16[2,256,512]{2,1,0:T(8,128)(2,1)S(1)} %collective-permute-done.6.half_t, bf16[2,256,512]{2,1,0:T(8,128)(2,1)S(1)} %collective-permute-done.7.partner_half_t, ...), custom_call_target="tpu_custom_call" | custom-call | flops 1073741824 | bytes 1024 | tf_op jit(solution)/shard_map/weight2/pallas_call | solution.py:566
  39.1 1.7 %collective-permute-start.15 = (bf16[4,576,128]{2,1,0:T(8,128)(2,1)S(1)}, bf16[4,576,128]{2,1,0:T(8,128)(2,1)S(1)}, u32[]{:S(2)}, u32[]{:S(2)}) collective-permute-start(bf16[4,576,128]{2,1,0:T(8,128)(2,1)S(1)} %get-tuple-element.115), channel_id=1, source_target_pairs={{0,4},{4,0},{8,12},{12,8},{16,20},{20,16},{24,28},{28,24},{1,5},{5... | collective-permute-start | bytes 1769480 | tf_op jit(solution)/shard_map/ppermute | solution.py:623
  40.8 1.9 %collective-permute-start.10 = (bf16[512,128]{1,0:T(8,128)(2,1)S(1)}, bf16[512,128]{1,0:T(8,128)(2,1)S(1)}, u32[]{:S(2)}, u32[]{:S(2)}) collective-permute-start(bf16[512,128]{1,0:T(8,128)(2,1)S(1)} %get-tuple-element.123), channel_id=1, source_target_pairs={{0,2},{1,3},{2,0},{3,1},{4,6},{5,7},{6,4},{7,5},{8,10},{9,11},{10,... | collective-permute-start | bytes 393224 | tf_op jit(solution)/shard_map/ppermute | solution.py:620
  42.7 2.1 %collective-permute-done.9.refs_1_ = bf16[4,256,256]{2,1,0:T(8,128)(2,1)S(1)} collective-permute-done((bf16[4,256,256]{2,1,0:T(8,128)(2,1)S(1)}, bf16[4,256,256]{2,1,0:T(8,128)(2,1)S(1)}, u32[]{:S(2)}, u32[]{:S(2)}) %collective-permute-start.9) | collective-permute-done | bytes 524320 | tf_op jit(solution)/shard_map/ppermute | solution.py:623
  44.7 0.1 routea1.1
  44.9 1.6 %collective-permute-start.12 = (bf16[1,256,256]{2,1,0:T(8,128)(2,1)S(1)}, bf16[1,256,256]{2,1,0:T(8,128)(2,1)S(1)}, u32[]{:S(2)}, u32[]{:S(2)}) collective-permute-start(bf16[1,256,256]{2,1,0:T(8,128)(2,1)S(1)} %get-tuple-element.119), channel_id=1, source_target_pairs={{0,8},{4,12},{8,0},{12,4},{16,24},{20,28},{24,16},{28,20},{1,9},{5... | collective-permute-start | bytes 393224 | tf_op jit(solution)/shard_map/ppermute | solution.py:623
  46.5 2.6 %collective-permute-start.13 = (bf16[1,256,256]{2,1,0:T(8,128)(2,1)S(1)}, bf16[1,256,256]{2,1,0:T(8,128)(2,1)S(1)}, u32[]{:S(2)}, u32[]{:S(2)}) collective-permute-start(bf16[1,256,256]{2,1,0:T(8,128)(2,1)S(1)} %get-tuple-element.120), channel_id=1, source_target_pairs={{0,16},{4,20},{8,24},{12,28},{16,0},{20,4},{24,8},{28,12},{1,17},{... | collective-permute-start | bytes 393224 | tf_op jit(solution)/shard_map/ppermute | solution.py:623
  49.1 0.2 collective-permute-start.14
  49.3 0.0 collective-permute-done.10.block_away
  49.3 3.1 %weight1.4 = (bf16[4,576,128]{2,1,0:T(8,128)(2,1)S(1)}, bf16[4,576,128]{2,1,0:T(8,128)(2,1)S(1)}) custom-call(s32[2]{0:T(128)S(1)} %copy-done.3, bf16[512,512]{1,0:T(8,128)(2,1)S(1)} %get-tuple-element.107.act_t, bf16[2,256,512]{2,1,0:T(8,128)(2,1)S(1)} %collective-permute-done.6.half_t, bf16[2,256,512]{2,1,0:T(8,128)(2,1)S(1)} %collective-permute-done.7.partner_half_t, ...), custom_call_target="tpu_custom_call" | custom-call | flops 21474836 | bytes 1024 | tf_op jit(solution)/shard_map/weight1/pallas_call | solution.py:566
  52.4 1.6 %collective-permute-start.19 = (bf16[4,576,128]{2,1,0:T(8,128)(2,1)S(1)}, bf16[4,576,128]{2,1,0:T(8,128)(2,1)S(1)}, u32[]{:S(2)}, u32[]{:S(2)}) collective-permute-start(bf16[4,576,128]{2,1,0:T(8,128)(2,1)S(1)} %get-tuple-element.124), channel_id=1, source_target_pairs={{0,4},{4,0},{8,12},{12,8},{16,20},{20,16},{24,28},{28,24},{1,5},{5... | collective-permute-start | bytes 1769480 | tf_op jit(solution)/shard_map/ppermute | solution.py:623
  54.0 5.4 %fourth.1 = (bf16[192,512]{1,0:T(8,128)(2,1)S(1)}, bf16[192,512]{1,0:T(8,128)(2,1)S(1)}, bf16[2,128,512]{2,1,0:T(8,128)(2,1)S(1)}, bf16[4,16,128]{2,1,0:T(8,128)(2,1)S(1)}, bf16[4,16,128]{2,1,0:T(8,128)(2,1)S(1)}) custom-call(s32[2]{0:T(128)S(1)} %copy-done.3, bf16[512,512]{1,0:T(8,128)(2,1)S(1)} %get-tuple-element.125.grad1_ref, ...), custom_call_target="tpu_custom_call" | custom-call | flops 21474836 | bytes 1024 | tf_op jit(solution)/shard_map/fourth/pallas_call | solution.py:566
  59.4 0.0 collective-permute-done.12
  59.4 0.0 collective-permute-done.13
  59.4 0.1 fusion.2.own_ref
  59.5 0.0 collective-permute-done.15.refs_1_
  59.5 0.1 routeb1.1
  59.7 0.7 collective-permute-start.16
  60.4 3.5 %collective-permute-start.17 = (bf16[1,576,128]{2,1,0:T(8,128)(2,1)S(1)}, bf16[1,576,128]{2,1,0:T(8,128)(2,1)S(1)}, u32[]{:S(2)}, u32[]{:S(2)}) collective-permute-start(bf16[1,576,128]{2,1,0:T(8,128)(2,1)S(1)} %get-tuple-element.139), channel_id=1, source_target_pairs={{0,16},{4,20},{8,24},{12,28},{16,0},{20,4},{24,8},{28,12},{1,17},{... | collective-permute-start | bytes 442376 | tf_op jit(solution)/shard_map/ppermute | solution.py:623
  63.9 0.2 collective-permute-start.18
  64.1 1.0 %collective-permute-start.11 = (bf16[2,128,512]{2,1,0:T(8,128)(2,1)S(1)}, bf16[2,128,512]{2,1,0:T(8,128)(2,1)S(1)}, u32[]{:S(2)}, u32[]{:S(2)}) collective-permute-start(bf16[2,128,512]{2,1,0:T(8,128)(2,1)S(1)} %get-tuple-element.133), channel_id=1, source_target_pairs={{0,2},{1,3},{2,0},{3,1},{4,6},{5,7},{6,4},{7,5},{8,10},{9,11},{10,... | collective-permute-start | bytes 786440 | tf_op jit(solution)/shard_map/ppermute | solution.py:620
  65.1 0.5 collective-permute-done.16
  65.6 0.3 collective-permute-start.20
  65.9 6.5 %collective-permute-done.17 = bf16[1,576,128]{2,1,0:T(8,128)(2,1)S(1)} collective-permute-done((bf16[1,576,128]{2,1,0:T(8,128)(2,1)S(1)}, bf16[1,576,128]{2,1,0:T(8,128)(2,1)S(1)}, u32[]{:S(2)}, u32[]{:S(2)}) %collective-permute-start.17) | collective-permute-done | bytes 147488 | tf_op jit(solution)/shard_map/ppermute | solution.py:623
  72.4 1.1 %collective-permute-start.27 = (bf16[256,256]{1,0:T(8,128)(2,1)S(1)}, bf16[256,256]{1,0:T(8,128)(2,1)S(1)}, u32[]{:S(2)}, u32[]{:S(2)}) collective-permute-start(bf16[256,256]{1,0:T(8,128)(2,1)S(1)} %fusion.2.own_ref), channel_id=1, source_target_pairs={{0,2},{1,3},{2,0},{3,1},{4,6},{5,7},{6,4},{7,5},{8,10},{9,11},{10,... | collective-permute-start | bytes 393224 | tf_op jit(solution)/shard_map/ppermute | solution.py:620
  73.6 0.1 fusion.1.own_ref
  73.7 0.2 routec1.1
  73.8 1.1 %collective-permute-start.21 = (bf16[1,592,128]{2,1,0:T(8,128)(2,1)S(1)}, bf16[1,592,128]{2,1,0:T(8,128)(2,1)S(1)}, u32[]{:S(2)}, u32[]{:S(2)}) collective-permute-start(bf16[1,592,128]{2,1,0:T(8,128)(2,1)S(1)} %get-tuple-element.147), channel_id=1, source_target_pairs={{0,8},{4,12},{8,0},{12,4},{16,24},{20,28},{24,16},{28,20},{1,9},{5... | collective-permute-start | bytes 454664 | tf_op jit(solution)/shard_map/ppermute | solution.py:623
  74.9 2.0 %collective-permute-start.22 = (bf16[1,592,128]{2,1,0:T(8,128)(2,1)S(1)}, bf16[1,592,128]{2,1,0:T(8,128)(2,1)S(1)}, u32[]{:S(2)}, u32[]{:S(2)}) collective-permute-start(bf16[1,592,128]{2,1,0:T(8,128)(2,1)S(1)} %get-tuple-element.148), channel_id=1, source_target_pairs={{0,16},{4,20},{8,24},{12,28},{16,0},{20,4},{24,8},{28,12},{1,17},{... | collective-permute-start | bytes 454664 | tf_op jit(solution)/shard_map/ppermute | solution.py:623
  77.0 1.3 %collective-permute-start.23 = (bf16[1,592,128]{2,1,0:T(8,128)(2,1)S(1)}, bf16[1,592,128]{2,1,0:T(8,128)(2,1)S(1)}, u32[]{:S(2)}, u32[]{:S(2)}) collective-permute-start(bf16[1,592,128]{2,1,0:T(8,128)(2,1)S(1)} %get-tuple-element.149), channel_id=1, source_target_pairs={{0,24},{4,28},{8,16},{12,20},{16,8},{20,12},{24,0},{28,4},{1,25},{... | collective-permute-start | bytes 454664 | tf_op jit(solution)/shard_map/ppermute | solution.py:623
  78.3 0.9 collective-permute-start.24
  79.2 1.5 %unpack.1 = (bf16[2,6,32,512]{3,2,1,0:T(8,128)(2,1)}, bf16[2,6,32,512]{3,2,1,0:T(8,128)(2,1)}) custom-call(s32[2]{0:T(128)S(1)} %copy-done.3, bf16[192,512]{1,0:T(8,128)(2,1)S(1)} %get-tuple-element.131.out_own, bf16[192,512]{1,0:T(8,128)(2,1)S(1)} %get-tuple-element.132.grad_own, bf16[2,128,512]{2,1,0:T(8,128)(2,1)S(1)} %collective-permute-done.11.away_ref), custom_call_target="tpu_custom_call" | custom-call | flops 21474836 | bytes 1024 | tf_op jit(solution)/shard_map/unpack/pallas_call | solution.py:566
  80.7 0.5 collective-permute-start.25
  81.2 0.9 joina.1
  82.1 1.6 %collective-permute-done.24.far_ref = bf16[576,128]{1,0:T(8,128)(2,1)S(1)} collective-permute-done((bf16[576,128]{1,0:T(8,128)(2,1)S(1)}, bf16[576,128]{1,0:T(8,128)(2,1)S(1)}, u32[]{:S(2)}, u32[]{:S(2)}) %collective-permute-start.24) | collective-permute-done | bytes 147488 | tf_op jit(solution)/shard_map/ppermute | solution.py:620
  83.7 5.4 %collective-permute-done.22 = bf16[1,592,128]{2,1,0:T(8,128)(2,1)S(1)} collective-permute-done((bf16[1,592,128]{2,1,0:T(8,128)(2,1)S(1)}, bf16[1,592,128]{2,1,0:T(8,128)(2,1)S(1)}, u32[]{:S(2)}, u32[]{:S(2)}) %collective-permute-start.22) | collective-permute-done | bytes 151584 | tf_op jit(solution)/shard_map/ppermute | solution.py:623
  89.1 0.1 fusion.own_ref
  89.2 1.2 %joinb.1 = f32[576,512]{1,0:T(8,128)} custom-call(bf16[576,128]{1,0:T(8,128)(2,1)S(1)} %fusion.1.own_ref, bf16[576,128]{1,0:T(8,128)(2,1)S(1)} %collective-permute-done.24.far_ref, bf16[576,128]{1,0:T(8,128)(2,1)S(1)} %collective-permute-done.25.near_ref, bf16[576,128]{1,0:T(8,128)(2,1)S(1)} %collective-permute-done.26.diagonal_ref), custom_call_target="tpu_custom_call" | custom-call | flops 21474836 | bytes 1024 | tf_op jit(solution)/shard_map/joinb/pallas_call | solution.py:566
  90.4 1.1 %collective-permute-start.30 = (bf16[592,128]{1,0:T(8,128)(2,1)S(1)}, bf16[592,128]{1,0:T(8,128)(2,1)S(1)}, u32[]{:S(2)}, u32[]{:S(2)}) collective-permute-start(bf16[592,128]{1,0:T(8,128)(2,1)S(1)} %fusion.own_ref), channel_id=1, source_target_pairs={{0,2},{1,3},{2,0},{3,1},{4,6},{5,7},{6,4},{7,5},{8,10},{9,11},{10,... | collective-permute-start | bytes 454664 | tf_op jit(solution)/shard_map/ppermute | solution.py:620
  91.6 4.0 %collective-permute-done.30.far_ref = bf16[592,128]{1,0:T(8,128)(2,1)S(1)} collective-permute-done((bf16[592,128]{1,0:T(8,128)(2,1)S(1)}, bf16[592,128]{1,0:T(8,128)(2,1)S(1)}, u32[]{:S(2)}, u32[]{:S(2)}) %collective-permute-start.30) | collective-permute-done | bytes 151584 | tf_op jit(solution)/shard_map/ppermute | solution.py:620
  95.6 1.4 %collective-permute-done.32.diagonal_ref = bf16[592,128]{1,0:T(8,128)(2,1)S(1)} collective-permute-done((bf16[592,128]{1,0:T(8,128)(2,1)S(1)}, bf16[592,128]{1,0:T(8,128)(2,1)S(1)}, u32[]{:S(2)}, u32[]{:S(2)}) %collective-permute-start.32) | collective-permute-done | bytes 151584 | tf_op jit(solution)/shard_map/ppermute | solution.py:617
  97.0 1.2 %joinc.1 = (f32[576,512]{1,0:T(8,128)}, f32[1,64]{1,0:T(1,128)}, f32[1,64]{1,0:T(1,128)}, f32[1,64]{1,0:T(1,128)}, f32[1,64]{1,0:T(1,128)}, /*index=5*/f32[1,64]...) custom-call(bf16[592,128]{1,0:T(8,128)(2,1)S(1)} %fusion.own_ref, ...), custom_call_target="tpu_custom_call" | custom-call | flops 21474836 | bytes 1024 | tf_op jit(solution)/shard_map/joinc/pallas_call | solution.py:566
  (68 shorter events, 0.2 us)
Async XLA Ops:
  0.7 5.1 %copy-start.8 = (f32[512]{0:T(512)S(1)}, f32[512]{0:T(512)}, u32[]{:S(2)}) copy-start(f32[512]{0:T(512)} %param.22) | copy-start | bytes 6148
  0.7 5.1 %copy-start.9 = (f32[512]{0:T(512)S(1)}, f32[512]{0:T(512)}, u32[]{:S(2)}) copy-start(f32[512]{0:T(512)} %param.23) | copy-start | bytes 6148
  0.7 5.1 %copy-start.18 = (f32[512]{0:T(512)S(1)}, f32[512]{0:T(512)}, u32[]{:S(2)}) copy-start(f32[512]{0:T(512)} %param.38) | copy-start | bytes 6148
  0.7 5.1 %copy-start.10 = (f32[512]{0:T(512)S(1)}, f32[512]{0:T(512)}, u32[]{:S(2)}) copy-start(f32[512]{0:T(512)} %param.25) | copy-start | bytes 6148
  0.7 5.1 %copy-start.11 = (f32[512]{0:T(512)S(1)}, f32[512]{0:T(512)}, u32[]{:S(2)}) copy-start(f32[512]{0:T(512)} %param.26) | copy-start | bytes 6148
  0.7 5.1 %copy-start.12 = (f32[512]{0:T(512)S(1)}, f32[512]{0:T(512)}, u32[]{:S(2)}) copy-start(f32[512]{0:T(512)} %param.27) | copy-start | bytes 6148
  0.7 5.1 %copy-start.13 = (f32[512]{0:T(512)S(1)}, f32[512]{0:T(512)}, u32[]{:S(2)}) copy-start(f32[512]{0:T(512)} %param.29) | copy-start | bytes 6148
  0.7 5.1 %copy-start.14 = (f32[512]{0:T(512)S(1)}, f32[512]{0:T(512)}, u32[]{:S(2)}) copy-start(f32[512]{0:T(512)} %param.30) | copy-start | bytes 6148
  0.7 5.1 %copy-start.15 = (f32[512]{0:T(512)S(1)}, f32[512]{0:T(512)}, u32[]{:S(2)}) copy-start(f32[512]{0:T(512)} %param.31) | copy-start | bytes 6148
  0.8 5.1 %copy-start.16 = (f32[512]{0:T(512)S(1)}, f32[512]{0:T(512)}, u32[]{:S(2)}) copy-start(f32[512]{0:T(512)} %param.33) | copy-start | bytes 6148
  0.8 5.1 %copy-start.17 = (f32[512]{0:T(512)S(1)}, f32[512]{0:T(512)}, u32[]{:S(2)}) copy-start(f32[512]{0:T(512)} %param.36) | copy-start | bytes 6148
  0.8 5.1 %copy-start.7 = (bf16[2,6,32,512]{3,2,1,0:T(8,128)(2,1)S(1)}, bf16[2,6,32,512]{3,2,1,0:T(8,128)(2,1)}, u32[]{:S(2)}) copy-start(bf16[2,6,32,512]{3,2,1,0:T(8,128)(2,1)} %cot_ref.1) | copy-start | bytes 1179652
  0.8 10.6 %slice-start = ((s8[4718592]{0:T(1024)(128)(4,1)}), s8[524288]{0:T(1024)(128)(4,1)S(1)}, s32[]{:S(2)}) async-start(s8[4718592]{0:T(1024)(128)(4,1)} %bitcast.28), calls=%async_computation | async-start | bytes 1048576
  0.8 18.2 %slice-start.2 = ((s8[4718592]{0:T(1024)(128)(4,1)}), s8[4194304]{0:T(1024)(128)(4,1)S(1)}, s32[]{:S(2)}) async-start(s8[4718592]{0:T(1024)(128)(4,1)} %bitcast.30), calls=%async_computation.2 | async-start | bytes 8388608
  2.7 6.7 %collective-permute-start.1 = (bf16[128,512]{1,0:T(8,128)(2,1)}, bf16[128,512]{1,0:T(8,128)(2,1)S(1)}, u32[]{:S(2)}, u32[]{:S(2)}) collective-permute-start(bf16[128,512]{1,0:T(8,128)(2,1)} %get-tuple-element.96), channel_id=1, source_target_pairs={{0,2},{1,3},{2,0},{3,1},{4,6},{5,7},{6,4},{7,5},{8,10},{9,11},{10,... | collective-permute-start | bytes 393224 | tf_op jit(solution)/shard_map/ppermute | solution.py:620
  5.8 5.6 %collective-permute-start = (bf16[192,512]{1,0:T(8,128)(2,1)}, bf16[192,512]{1,0:T(8,128)(2,1)S(1)}, u32[]{:S(2)}, u32[]{:S(2)}) collective-permute-start(bf16[192,512]{1,0:T(8,128)(2,1)} %get-tuple-element.95.own), channel_id=1, source_target_pairs={{0,1},{1,0},{2,3},{3,2},{4,5},{5,4},{6,7},{7,6},{8,9},{9,8},{10,11... | collective-permute-start | bytes 589832 | tf_op jit(solution)/shard_map/ppermute | solution.py:617
  5.8 5.6 %slice-start.1 = ((s8[4718592]{0:T(1024)(128)(4,1)}), s8[4194304]{0:T(1024)(128)(4,1)S(1)}, s32[]{:S(2)}) async-start(s8[4718592]{0:T(1024)(128)(4,1)} %bitcast.28), calls=%async_computation.1 | async-start | bytes 8388608
  5.9 0.8 copy-start.2
  6.7 4.7 %copy-start.1 = (bf16[192,512]{1,0:T(8,128)(2,1)S(1)}, bf16[192,512]{1,0:T(8,128)(2,1)}, u32[]{:S(2)}) copy-start(bf16[192,512]{1,0:T(8,128)(2,1)} %get-tuple-element.95.own) | copy-start | bytes 589828
  6.7 4.7 %copy-start.3 = (s32[2]{0:T(128)S(1)}, s32[2]{0:T(128)}, u32[]{:S(2)}) copy-start(s32[2]{0:T(128)} %get-tuple-element.94.kinds.bucket_ref) | copy-start | bytes 28
  6.7 12.3 %slice-start.3 = ((s8[4718592]{0:T(1024)(128)(4,1)}), s8[524288]{0:T(1024)(128)(4,1)S(1)}, s32[]{:S(2)}) async-start(s8[4718592]{0:T(1024)(128)(4,1)} %bitcast.30), calls=%async_computation.3 | async-start | bytes 1048576
  7.3 11.8 %copy-start = (bf16[512,512]{1,0:T(8,128)(2,1)S(1)}, bf16[512,512]{1,0:T(8,128)(2,1)}, u32[]{:S(2)}) copy-start(bf16[512,512]{1,0:T(8,128)(2,1)} %wp.3) | copy-start | bytes 1572868
  7.3 11.8 %copy-start.4 = (bf16[512,512]{1,0:T(8,128)(2,1)S(1)}, bf16[512,512]{1,0:T(8,128)(2,1)}, u32[]{:S(2)}) copy-start(bf16[512,512]{1,0:T(8,128)(2,1)} %wq.1) | copy-start | bytes 1572868
  7.3 11.8 %copy-start.5 = (bf16[512,512]{1,0:T(8,128)(2,1)S(1)}, bf16[512,512]{1,0:T(8,128)(2,1)}, u32[]{:S(2)}) copy-start(bf16[512,512]{1,0:T(8,128)(2,1)} %wk.1) | copy-start | bytes 1572868
  7.3 11.8 %copy-start.6 = (bf16[512,512]{1,0:T(8,128)(2,1)S(1)}, bf16[512,512]{1,0:T(8,128)(2,1)}, u32[]{:S(2)}) copy-start(bf16[512,512]{1,0:T(8,128)(2,1)} %wv.1) | copy-start | bytes 1572868
  7.3 11.7 %collective-permute-start.3 = (bf16[192,512]{1,0:T(8,128)(2,1)S(1)}, bf16[192,512]{1,0:T(8,128)(2,1)S(1)}, u32[]{:S(2)}, u32[]{:S(2)}) collective-permute-start(bf16[192,512]{1,0:T(8,128)(2,1)S(1)} %get-tuple-element.101.own), channel_id=1, source_target_pairs={{0,1},{1,0},{2,3},{3,2},{4,5},{5,4},{6,7},{7,6},{8,9},{9,8},{10,11... | collective-permute-start | bytes 589832 | tf_op jit(solution)/shard_map/ppermute | solution.py:617
  9.5 1.9 %collective-permute-start.2 = (bf16[128,512]{1,0:T(8,128)(2,1)S(1)}, bf16[128,512]{1,0:T(8,128)(2,1)S(1)}, u32[]{:S(2)}, u32[]{:S(2)}) collective-permute-start(bf16[128,512]{1,0:T(8,128)(2,1)S(1)} %collective-permute-done.1.received), channel_id=1, source_target_pairs={{0,1},{1,0},{2,3},{3,2},{4,5},{5,4},{6,7},{7,6},{8,9},{9,8},{10,11... | collective-permute-start | bytes 393224 | tf_op jit(solution)/shard_map/ppermute | solution.py:617
  9.5 9.5 %collective-permute-start.4 = (bf16[128,512]{1,0:T(8,128)(2,1)S(1)}, bf16[128,512]{1,0:T(8,128)(2,1)S(1)}, u32[]{:S(2)}, u32[]{:S(2)}) collective-permute-start(bf16[128,512]{1,0:T(8,128)(2,1)S(1)} %get-tuple-element.102), channel_id=1, source_target_pairs={{0,2},{1,3},{2,0},{3,1},{4,6},{5,7},{6,4},{7,5},{8,10},{9,11},{10,... | collective-permute-start | bytes 393224 | tf_op jit(solution)/shard_map/ppermute | solution.py:620
  11.2 7.8 %collective-permute-start.5 = (bf16[128,512]{1,0:T(8,128)(2,1)S(1)}, bf16[128,512]{1,0:T(8,128)(2,1)S(1)}, u32[]{:S(2)}, u32[]{:S(2)}) collective-permute-start(bf16[128,512]{1,0:T(8,128)(2,1)S(1)} %get-tuple-element.102), channel_id=1, source_target_pairs={{0,3},{1,2},{2,1},{3,0},{4,7},{5,6},{6,5},{7,4},{8,11},{9,10},{10,... | collective-permute-start | bytes 393224 | tf_op jit(solution)/shard_map/ppermute | solution.py:653
  17.2 14.2 %collective-permute-start.6 = (bf16[2,256,512]{2,1,0:T(8,128)(2,1)S(1)}, bf16[2,256,512]{2,1,0:T(8,128)(2,1)S(1)}, u32[]{:S(2)}, u32[]{:S(2)}) collective-permute-start(bf16[2,256,512]{2,1,0:T(8,128)(2,1)S(1)} %get-tuple-element.108), channel_id=1, source_target_pairs={{0,2},{1,3},{2,0},{3,1},{4,6},{5,7},{6,4},{7,5},{8,10},{9,11},{10,... | collective-permute-start | bytes 1572872 | tf_op jit(solution)/shard_map/ppermute | solution.py:620
  29.4 6.6 %collective-permute-start.8 = (bf16[512,128]{1,0:T(8,128)(2,1)S(1)}, bf16[512,128]{1,0:T(8,128)(2,1)S(1)}, u32[]{:S(2)}, u32[]{:S(2)}) collective-permute-start(bf16[512,128]{1,0:T(8,128)(2,1)S(1)} %get-tuple-element.114), channel_id=1, source_target_pairs={{0,2},{1,3},{2,0},{3,1},{4,6},{5,7},{6,4},{7,5},{8,10},{9,11},{10,... | collective-permute-start | bytes 393224 | tf_op jit(solution)/shard_map/ppermute | solution.py:620
  29.9 14.8 %collective-permute-start.9 = (bf16[4,256,256]{2,1,0:T(8,128)(2,1)S(1)}, bf16[4,256,256]{2,1,0:T(8,128)(2,1)S(1)}, u32[]{:S(2)}, u32[]{:S(2)}) collective-permute-start(bf16[4,256,256]{2,1,0:T(8,128)(2,1)S(1)} %get-tuple-element.117), channel_id=1, source_target_pairs={{0,4},{4,0},{8,12},{12,8},{16,20},{20,16},{24,28},{28,24},{1,5},{5... | collective-permute-start | bytes 1572872 | tf_op jit(solution)/shard_map/ppermute | solution.py:623
  31.4 4.6 %collective-permute-start.7 = (bf16[2,256,512]{2,1,0:T(8,128)(2,1)S(1)}, bf16[2,256,512]{2,1,0:T(8,128)(2,1)S(1)}, u32[]{:S(2)}, u32[]{:S(2)}) collective-permute-start(bf16[2,256,512]{2,1,0:T(8,128)(2,1)S(1)} %collective-permute-done.6.half_t), channel_id=1, source_target_pairs={{0,1},{1,0},{2,3},{3,2},{4,5},{5,4},{6,7},{7,6},{8,9},{9,8},{10,11... | collective-permute-start | bytes 1572872 | tf_op jit(solution)/shard_map/ppermute | solution.py:617
  39.1 20.4 %collective-permute-start.15 = (bf16[4,576,128]{2,1,0:T(8,128)(2,1)S(1)}, bf16[4,576,128]{2,1,0:T(8,128)(2,1)S(1)}, u32[]{:S(2)}, u32[]{:S(2)}) collective-permute-start(bf16[4,576,128]{2,1,0:T(8,128)(2,1)S(1)} %get-tuple-element.115), channel_id=1, source_target_pairs={{0,4},{4,0},{8,12},{12,8},{16,20},{20,16},{24,28},{28,24},{1,5},{5... | collective-permute-start | bytes 1769480 | tf_op jit(solution)/shard_map/ppermute | solution.py:623
  40.8 8.5 %collective-permute-start.10 = (bf16[512,128]{1,0:T(8,128)(2,1)S(1)}, bf16[512,128]{1,0:T(8,128)(2,1)S(1)}, u32[]{:S(2)}, u32[]{:S(2)}) collective-permute-start(bf16[512,128]{1,0:T(8,128)(2,1)S(1)} %get-tuple-element.123), channel_id=1, source_target_pairs={{0,2},{1,3},{2,0},{3,1},{4,6},{5,7},{6,4},{7,5},{8,10},{9,11},{10,... | collective-permute-start | bytes 393224 | tf_op jit(solution)/shard_map/ppermute | solution.py:620
  44.9 14.6 %collective-permute-start.12 = (bf16[1,256,256]{2,1,0:T(8,128)(2,1)S(1)}, bf16[1,256,256]{2,1,0:T(8,128)(2,1)S(1)}, u32[]{:S(2)}, u32[]{:S(2)}) collective-permute-start(bf16[1,256,256]{2,1,0:T(8,128)(2,1)S(1)} %get-tuple-element.119), channel_id=1, source_target_pairs={{0,8},{4,12},{8,0},{12,4},{16,24},{20,28},{24,16},{28,20},{1,9},{5... | collective-permute-start | bytes 393224 | tf_op jit(solution)/shard_map/ppermute | solution.py:623
  46.5 12.9 %collective-permute-start.13 = (bf16[1,256,256]{2,1,0:T(8,128)(2,1)S(1)}, bf16[1,256,256]{2,1,0:T(8,128)(2,1)S(1)}, u32[]{:S(2)}, u32[]{:S(2)}) collective-permute-start(bf16[1,256,256]{2,1,0:T(8,128)(2,1)S(1)} %get-tuple-element.120), channel_id=1, source_target_pairs={{0,16},{4,20},{8,24},{12,28},{16,0},{20,4},{24,8},{28,12},{1,17},{... | collective-permute-start | bytes 393224 | tf_op jit(solution)/shard_map/ppermute | solution.py:623
  49.1 10.3 %collective-permute-start.14 = (bf16[1,256,256]{2,1,0:T(8,128)(2,1)S(1)}, bf16[1,256,256]{2,1,0:T(8,128)(2,1)S(1)}, u32[]{:S(2)}, u32[]{:S(2)}) collective-permute-start(bf16[1,256,256]{2,1,0:T(8,128)(2,1)S(1)} %get-tuple-element.121), channel_id=1, source_target_pairs={{0,24},{4,28},{8,16},{12,20},{16,8},{20,12},{24,0},{28,4},{1,25},{... | collective-permute-start | bytes 393224 | tf_op jit(solution)/shard_map/ppermute | solution.py:623
  52.4 21.3 %collective-permute-start.19 = (bf16[4,576,128]{2,1,0:T(8,128)(2,1)S(1)}, bf16[4,576,128]{2,1,0:T(8,128)(2,1)S(1)}, u32[]{:S(2)}, u32[]{:S(2)}) collective-permute-start(bf16[4,576,128]{2,1,0:T(8,128)(2,1)S(1)} %get-tuple-element.124), channel_id=1, source_target_pairs={{0,4},{4,0},{8,12},{12,8},{16,20},{20,16},{24,28},{28,24},{1,5},{5... | collective-permute-start | bytes 1769480 | tf_op jit(solution)/shard_map/ppermute | solution.py:623
  59.7 5.9 %collective-permute-start.16 = (bf16[1,576,128]{2,1,0:T(8,128)(2,1)S(1)}, bf16[1,576,128]{2,1,0:T(8,128)(2,1)S(1)}, u32[]{:S(2)}, u32[]{:S(2)}) collective-permute-start(bf16[1,576,128]{2,1,0:T(8,128)(2,1)S(1)} %get-tuple-element.138), channel_id=1, source_target_pairs={{0,8},{4,12},{8,0},{12,4},{16,24},{20,28},{24,16},{28,20},{1,9},{5... | collective-permute-start | bytes 442376 | tf_op jit(solution)/shard_map/ppermute | solution.py:623
  60.4 12.0 %collective-permute-start.17 = (bf16[1,576,128]{2,1,0:T(8,128)(2,1)S(1)}, bf16[1,576,128]{2,1,0:T(8,128)(2,1)S(1)}, u32[]{:S(2)}, u32[]{:S(2)}) collective-permute-start(bf16[1,576,128]{2,1,0:T(8,128)(2,1)S(1)} %get-tuple-element.139), channel_id=1, source_target_pairs={{0,16},{4,20},{8,24},{12,28},{16,0},{20,4},{24,8},{28,12},{1,17},{... | collective-permute-start | bytes 442376 | tf_op jit(solution)/shard_map/ppermute | solution.py:623
  63.9 9.7 %collective-permute-start.18 = (bf16[1,576,128]{2,1,0:T(8,128)(2,1)S(1)}, bf16[1,576,128]{2,1,0:T(8,128)(2,1)S(1)}, u32[]{:S(2)}, u32[]{:S(2)}) collective-permute-start(bf16[1,576,128]{2,1,0:T(8,128)(2,1)S(1)} %get-tuple-element.140), channel_id=1, source_target_pairs={{0,24},{4,28},{8,16},{12,20},{16,8},{20,12},{24,0},{28,4},{1,25},{... | collective-permute-start | bytes 442376 | tf_op jit(solution)/shard_map/ppermute | solution.py:623
  64.1 12.8 %collective-permute-start.11 = (bf16[2,128,512]{2,1,0:T(8,128)(2,1)S(1)}, bf16[2,128,512]{2,1,0:T(8,128)(2,1)S(1)}, u32[]{:S(2)}, u32[]{:S(2)}) collective-permute-start(bf16[2,128,512]{2,1,0:T(8,128)(2,1)S(1)} %get-tuple-element.133), channel_id=1, source_target_pairs={{0,2},{1,3},{2,0},{3,1},{4,6},{5,7},{6,4},{7,5},{8,10},{9,11},{10,... | collective-permute-start | bytes 786440 | tf_op jit(solution)/shard_map/ppermute | solution.py:620
  65.6 8.1 %collective-permute-start.20 = (bf16[4,16,128]{2,1,0:T(8,128)(2,1)S(1)}, bf16[4,16,128]{2,1,0:T(8,128)(2,1)S(1)}, u32[]{:S(2)}, u32[]{:S(2)}) collective-permute-start(bf16[4,16,128]{2,1,0:T(8,128)(2,1)S(1)} %get-tuple-element.146), channel_id=1, source_target_pairs={{0,4},{4,0},{8,12},{12,8},{16,20},{20,16},{24,28},{28,24},{1,5},{5... | collective-permute-start | bytes 49160 | tf_op jit(solution)/shard_map/ppermute | solution.py:623
  72.4 5.9 %collective-permute-start.27 = (bf16[256,256]{1,0:T(8,128)(2,1)S(1)}, bf16[256,256]{1,0:T(8,128)(2,1)S(1)}, u32[]{:S(2)}, u32[]{:S(2)}) collective-permute-start(bf16[256,256]{1,0:T(8,128)(2,1)S(1)} %fusion.2.own_ref), channel_id=1, source_target_pairs={{0,2},{1,3},{2,0},{3,1},{4,6},{5,7},{6,4},{7,5},{8,10},{9,11},{10,... | collective-permute-start | bytes 393224 | tf_op jit(solution)/shard_map/ppermute | solution.py:620
  73.6 5.6 %collective-permute-start.28 = (bf16[256,256]{1,0:T(8,128)(2,1)S(1)}, bf16[256,256]{1,0:T(8,128)(2,1)S(1)}, u32[]{:S(2)}, u32[]{:S(2)}) collective-permute-start(bf16[256,256]{1,0:T(8,128)(2,1)S(1)} %fusion.2.own_ref), channel_id=1, source_target_pairs={{0,1},{1,0},{2,3},{3,2},{4,5},{5,4},{6,7},{7,6},{8,9},{9,8},{10,11... | collective-permute-start | bytes 393224 | tf_op jit(solution)/shard_map/ppermute | solution.py:617
  73.8 9.9 %collective-permute-start.21 = (bf16[1,592,128]{2,1,0:T(8,128)(2,1)S(1)}, bf16[1,592,128]{2,1,0:T(8,128)(2,1)S(1)}, u32[]{:S(2)}, u32[]{:S(2)}) collective-permute-start(bf16[1,592,128]{2,1,0:T(8,128)(2,1)S(1)} %get-tuple-element.147), channel_id=1, source_target_pairs={{0,8},{4,12},{8,0},{12,4},{16,24},{20,28},{24,16},{28,20},{1,9},{5... | collective-permute-start | bytes 454664 | tf_op jit(solution)/shard_map/ppermute | solution.py:623
  74.9 14.2 %collective-permute-start.22 = (bf16[1,592,128]{2,1,0:T(8,128)(2,1)S(1)}, bf16[1,592,128]{2,1,0:T(8,128)(2,1)S(1)}, u32[]{:S(2)}, u32[]{:S(2)}) collective-permute-start(bf16[1,592,128]{2,1,0:T(8,128)(2,1)S(1)} %get-tuple-element.148), channel_id=1, source_target_pairs={{0,16},{4,20},{8,24},{12,28},{16,0},{20,4},{24,8},{28,12},{1,17},{... | collective-permute-start | bytes 454664 | tf_op jit(solution)/shard_map/ppermute | solution.py:623
  77.0 12.2 %collective-permute-start.23 = (bf16[1,592,128]{2,1,0:T(8,128)(2,1)S(1)}, bf16[1,592,128]{2,1,0:T(8,128)(2,1)S(1)}, u32[]{:S(2)}, u32[]{:S(2)}) collective-permute-start(bf16[1,592,128]{2,1,0:T(8,128)(2,1)S(1)} %get-tuple-element.149), channel_id=1, source_target_pairs={{0,24},{4,28},{8,16},{12,20},{16,8},{20,12},{24,0},{28,4},{1,25},{... | collective-permute-start | bytes 454664 | tf_op jit(solution)/shard_map/ppermute | solution.py:623
  78.3 5.4 %collective-permute-start.24 = (bf16[576,128]{1,0:T(8,128)(2,1)S(1)}, bf16[576,128]{1,0:T(8,128)(2,1)S(1)}, u32[]{:S(2)}, u32[]{:S(2)}) collective-permute-start(bf16[576,128]{1,0:T(8,128)(2,1)S(1)} %fusion.1.own_ref), channel_id=1, source_target_pairs={{0,2},{1,3},{2,0},{3,1},{4,6},{5,7},{6,4},{7,5},{8,10},{9,11},{10,... | collective-permute-start | bytes 442376 | tf_op jit(solution)/shard_map/ppermute | solution.py:620
  79.2 1.5 %collective-permute-start.29 = (bf16[256,256]{1,0:T(8,128)(2,1)S(1)}, bf16[256,256]{1,0:T(8,128)(2,1)S(1)}, u32[]{:S(2)}, u32[]{:S(2)}) collective-permute-start(bf16[256,256]{1,0:T(8,128)(2,1)S(1)} %collective-permute-done.27.far_ref), channel_id=1, source_target_pairs={{0,1},{1,0},{2,3},{3,2},{4,5},{5,4},{6,7},{7,6},{8,9},{9,8},{10,11... | collective-permute-start | bytes 393224 | tf_op jit(solution)/shard_map/ppermute | solution.py:617
  80.7 8.5 %collective-permute-start.25 = (bf16[576,128]{1,0:T(8,128)(2,1)S(1)}, bf16[576,128]{1,0:T(8,128)(2,1)S(1)}, u32[]{:S(2)}, u32[]{:S(2)}) collective-permute-start(bf16[576,128]{1,0:T(8,128)(2,1)S(1)} %fusion.1.own_ref), channel_id=1, source_target_pairs={{0,1},{1,0},{2,3},{3,2},{4,5},{5,4},{6,7},{7,6},{8,9},{9,8},{10,11... | collective-permute-start | bytes 442376 | tf_op jit(solution)/shard_map/ppermute | solution.py:617
  83.7 5.5 %collective-permute-start.26 = (bf16[576,128]{1,0:T(8,128)(2,1)S(1)}, bf16[576,128]{1,0:T(8,128)(2,1)S(1)}, u32[]{:S(2)}, u32[]{:S(2)}) collective-permute-start(bf16[576,128]{1,0:T(8,128)(2,1)S(1)} %collective-permute-done.24.far_ref), channel_id=1, source_target_pairs={{0,1},{1,0},{2,3},{3,2},{4,5},{5,4},{6,7},{7,6},{8,9},{9,8},{10,11... | collective-permute-start | bytes 442376 | tf_op jit(solution)/shard_map/ppermute | solution.py:617
  90.4 5.2 %collective-permute-start.30 = (bf16[592,128]{1,0:T(8,128)(2,1)S(1)}, bf16[592,128]{1,0:T(8,128)(2,1)S(1)}, u32[]{:S(2)}, u32[]{:S(2)}) collective-permute-start(bf16[592,128]{1,0:T(8,128)(2,1)S(1)} %fusion.own_ref), channel_id=1, source_target_pairs={{0,2},{1,3},{2,0},{3,1},{4,6},{5,7},{6,4},{7,5},{8,10},{9,11},{10,... | collective-permute-start | bytes 454664 | tf_op jit(solution)/shard_map/ppermute | solution.py:620
  91.6 4.1 %collective-permute-start.31 = (bf16[592,128]{1,0:T(8,128)(2,1)S(1)}, bf16[592,128]{1,0:T(8,128)(2,1)S(1)}, u32[]{:S(2)}, u32[]{:S(2)}) collective-permute-start(bf16[592,128]{1,0:T(8,128)(2,1)S(1)} %fusion.own_ref), channel_id=1, source_target_pairs={{0,1},{1,0},{2,3},{3,2},{4,5},{5,4},{6,7},{7,6},{8,9},{9,8},{10,11... | collective-permute-start | bytes 454664 | tf_op jit(solution)/shard_map/ppermute | solution.py:617
  95.6 1.4 %collective-permute-start.32 = (bf16[592,128]{1,0:T(8,128)(2,1)S(1)}, bf16[592,128]{1,0:T(8,128)(2,1)S(1)}, u32[]{:S(2)}, u32[]{:S(2)}) collective-permute-start(bf16[592,128]{1,0:T(8,128)(2,1)S(1)} %collective-permute-done.30.far_ref), channel_id=1, source_target_pairs={{0,1},{1,0},{2,3},{3,2},{4,5},{5,4},{6,7},{7,6},{8,9},{9,8},{10,11... | collective-permute-start | bytes 454664 | tf_op jit(solution)/shard_map/ppermute | solution.py:617

commit v5 on v4

--- a/solution.py
+++ b/solution.py
@@ -21,7 +21,7 @@
 HB = pl.BlockSpec(memory_space=pltpu.HBM)
 RATE = 1 << 30
 LENGTH = {
-    "pack": 10, "stack": 10, "first": 0.02, "second": 30, "third": 20, "fourth": 0.02, "weight2": 1, "weight1": 0.02,
+    "pack": 10, "stack": 10, "first": 0.02, "second": 30, "third": 20, "fourth": 10, "weight2": 1, "weight1": 3,
 }
 
 
@@ -57,30 +57,40 @@
     return mask, size.astype(F32)
 
 
-def group_total(row):
-    channels = row.shape[-1]
-    lane = lax.broadcasted_iota(jnp.int32, row.shape, 1)
-    step = 1
-    while step < channels // GROUPS:
-        up = pltpu.roll(row, channels - step, 1)
-        down = pltpu.roll(row, step, 1)
-        row = row + jnp.where((lane & step) == 0, up, down)
-        step *= 2
-    return row
+def group_total(rows):
+    members = rows.shape[1] // GROUPS
+    lane = lax.broadcasted_iota(jnp.int32, (rows.shape[0], BLK), 1)
+    tiles = []
+    for tile in range(rows.shape[1] // BLK):
+        part = rows[:, tile * BLK : (tile + 1) * BLK]
+        step = 1
+        while step < members:
+            place_in_four = (lane // step) & 3
+            added = part
+            for d in (1, 2, 3):
+                up = pltpu.roll(part, BLK - d * step, 1)
+                down = pltpu.roll(part, (4 - d) * step, 1)
+                added = added + jnp.where(place_in_four + d < 4, up, down)
+            part = added
+            step *= 4
+        tiles.append(part)
+    return jnp.concatenate(tiles, axis=1)
 
 
 def total(values):
     return jnp.sum(values, axis=0, keepdims=True)
 
 
-def wide_total(row):
-    return group_total(jnp.broadcast_to(row, (8, row.shape[-1])))[0:1]
+def wide_total(*rows):
+    stacked = jnp.concatenate(list(rows) + [rows[0]] * (8 - len(rows)), axis=0)
+    sums = group_total(stacked)
+    return [sums[i : i + 1] for i in range(len(rows))]
 
 
 def norm_stats(values, mask, group_size):
-    mean = wide_total(total(values)) / group_size
+    mean = wide_total(total(values))[0] / group_size
     centered = (values - mean) * mask
-    variance = wide_total(total(centered * centered)) / group_size
+    variance = wide_total(total(centered * centered))[0] / group_size
     return mean, lax.rsqrt(variance + epsilon)
 
 
@@ -93,8 +103,7 @@
 def norm_back(grad, normal, inverse, mask, group_size, gain):
     plain_row = total(grad)
     cross_row = total(grad * normal)
-    plain = wide_total(plain_row * gain) / group_size
-    cross = wide_total(cross_row * gain) / group_size
+    plain, cross = [v / group_size for v in wide_total(plain_row * gain, cross_row * gain)]
     grad_in = grad * (inverse * gain) - mask * (plain * inverse + normal * (cross * inverse))
     return grad_in, cross_row, plain_row
 
@@ -182,11 +191,11 @@
 
         @pl.when(low == 0)
         def _():
-            out_ref[384:512, :] = received[...]
+            out_ref[384:512, :] = received[0:128, :]
 
         @pl.when(low == 1)
         def _():
-            out_ref[384:512, :] = partner_received[...]
+            out_ref[384:512, :] = partner_received[0:128, :]
 
 
 def split_out(full_ref, facts, h, own_ref, send_ref):
@@ -303,6 +312,7 @@
     channels = vecs.shape[1]
     group_size = pixels * (channels // GROUPS)
     scaling = channels ** (-0.5)
+    assemble(full_ref, home, h, (own, partner, received, partner_received))
     fill_shifts(shift_ref, act2_ref[...].astype(F32), stride)
     conv_forward(shift_ref, weight2, stride, middle_ref)
     middle = mask * (image_ref[...].astype(F32) + (middle_ref[...] + vec(vecs, BIAS2)))
@@ -319,17 +329,16 @@
     key_cols = lanes & (stride - 1)
     key_valid = (key_cols < home[3]) & (lanes < jnp.where(home[1], 384, 512))
     scores = jnp.where(key_valid, mm_nt(queries, keys) * scaling, -1000000000.0)
+    grad_top = full_ref[...].astype(F32) * mask
+    grad_rows = grad_top.astype(BF16)
+    grad_mixed = mm_nt(grad_rows, wp[...]).astype(BF16)
+    grad_soft = mm_nt(grad_mixed, values)
     raised = jnp.exp(scores - jnp.max(scores, axis=1, keepdims=True))
     soft = raised * (1.0 / jnp.sum(raised, axis=1, keepdims=True))
     soft16 = soft.astype(BF16)
     mixed = mm(soft16, values).astype(BF16)
     mixed_ref[...] = mixed
 
-    assemble(full_ref, home, h, (own, partner, received, partner_received))
-    grad_top = full_ref[...].astype(F32) * mask
-    grad_rows = grad_top.astype(BF16)
-    grad_mixed = mm_nt(grad_rows, wp[...]).astype(BF16)
-    grad_soft = mm_nt(grad_mixed, values)
     grad_values = mm_tn(soft16, grad_mixed).astype(BF16)
     grad_scores = soft * (grad_soft - jnp.sum(soft * grad_soft, axis=1, keepdims=True))
     grad_scores = grad_scores.astype(BF16)
@@ -369,14 +378,14 @@
 
     sum_ref[:, 0 : 6 * BLK] = mm_tn(normed, jnp.concatenate(blocks(0) + blocks(1) + blocks(2), axis=1))
     sum_ref[:, 6 * BLK : 8 * BLK] = mm_tn(mixed, jnp.concatenate(blocks(3), axis=1))
-    mine = lax.axis_index("batch") & 1
-    pairs = attn_keep.shape[0]
-    rows = channels // (2 * pairs)
-    for pair in range(pairs):
-        for dst, which in ((attn_keep, mine), (attn_send, 1 - mine)):
-            part = sum_ref[pl.ds(pl.multiple_of((2 * pair + which) * rows, 8), rows), :].astype(BF16)
-            for index in range(4):
-                dst[pair, index * rows : (index + 1) * rows, :] = part[:, index * 2 * BLK : (index + 1) * 2 * BLK]
+    shards = attn_keep.shape[0]
+    rows = channels // shards
+    for shard in range(shards):
+        part = sum_ref[shard * rows : (shard + 1) * rows, :].astype(BF16)
+        for index in range(4):
+            at = index * 2 * BLK
+            attn_keep[shard, index * rows : (index + 1) * rows, :] = part[:, at : at + BLK]
+            attn_send[shard, index * rows : (index + 1) * rows, :] = part[:, at + BLK : at + 2 * BLK]
 
 
 def third_kernel(
@@ -485,48 +494,57 @@
             dst[pair] = sum_ref[pl.ds(pl.multiple_of(shard * rows, 8), rows), :].astype(BF16)
 
 
-def route_kernel(*refs, bit, ways):
+def route_kernel(*refs, bit, ways, low):
     group = (lax.axis_index("batch") >> bit) & (ways - 1)
-    outs = refs[len(refs) - ways :]
-    count = outs[0].shape[0]
+    ins, outs = refs[: len(refs) - ways], refs[len(refs) - ways :]
     first = 0
-    for keep_ref, got_ref in zip(refs[0 : len(refs) - ways : 2], refs[1 : len(refs) - ways : 2]):
+    for keep_ref, got_ref in zip(ins[::2], ins[1::2]):
         rows = keep_ref.shape[1]
         for step, dst in enumerate(outs):
             which = group ^ step
-            for index in range(count):
-                at = index * ways + which
+            for index in range(dst.shape[0]):
+                at = (index // low * ways + which) * low + index % low
                 dst[index, first : first + rows, :] = (
                     keep_ref[at].astype(F32) + got_ref[at].astype(F32)
                 ).astype(BF16)
         first += rows
 
 
-def join_kernel(own_ref, far_ref, near_ref, diagonal_ref, out_ref, *tail_ref):
+def total_of(refs):
+    added = refs[0].astype(F32)
+    for ref in refs[1:]:
+        added = added + ref.astype(F32)
+    return added
+
+
+def half_kernel(*refs):
+    mine = lax.axis_index("batch") & 1
+    for dst, which in zip(refs[-2:], (mine, 1 - mine)):
+        dst[...] = total_of([ref[which] for ref in refs[:-2]]).astype(BF16)
+
+
+def sum_kernel(*refs, count):
+    out_ref = refs[-1]
+    rows = refs[0].shape[1]
+    out_ref[0:rows, :] = total_of([ref[0] for ref in refs[:count]]).astype(BF16)
+    if count < len(refs) - 1:
+        out_ref[rows:, :] = total_of([ref[...] for ref in refs[count:-1]]).astype(BF16)
+
+
+def join_kernel(own_ref, far_ref, near_ref, diagonal_ref, *out_refs):
     h = lax.axis_index("height")
-    rows = out_ref.shape[0]
-    for ref, index in ((own_ref, h), (far_ref, h ^ 2), (near_ref, h ^ 1), (diagonal_ref, h ^ 3)):
-        out_ref[:, pl.ds(pl.multiple_of(BLK * index, BLK), BLK)] = ref[0:rows, :].astype(F32)
-    if tail_ref:
-        own, far = own_ref[rows:, :].astype(F32), far_ref[rows:, :].astype(F32)
-        near, diagonal = near_ref[rows:, :].astype(F32), diagonal_ref[rows:, :].astype(F32)
+    first = 0
+    for dst in [ref for ref in out_refs if ref.shape[0] > 1]:
+        rows = dst.shape[0]
+        for ref, index in ((own_ref, h), (far_ref, h ^ 2), (near_ref, h ^ 1), (diagonal_ref, h ^ 3)):
+            dst[:, pl.ds(pl.multiple_of(BLK * index, BLK), BLK)] = ref[first : first + rows, :].astype(F32)
+        first += rows
+    if own_ref.shape[0] > first:
+        own, far = own_ref[first:, :].astype(F32), far_ref[first:, :].astype(F32)
+        near, diagonal = near_ref[first:, :].astype(F32), diagonal_ref[first:, :].astype(F32)
         sums = 0.5 * ((own + near) + (far + diagonal))
-        for index, dst in enumerate(tail_ref):
+        for index, dst in enumerate([ref for ref in out_refs if ref.shape[0] == 1]):
             dst[...] = sums[index : index + 1, 0 : dst.shape[1]]
-
-
-def join_attn_kernel(own_ref, far_ref, near_ref, diagonal_ref, *out_refs):
-    h = lax.axis_index("height")
-    rows = out_refs[0].shape[0]
-    for first, second, index in ((own_ref, far_ref, h), (near_ref, diagonal_ref, h ^ 1)):
-        for position in range(2):
-            lane, other = position * BLK, (1 - position) * BLK
-            column = pl.multiple_of(BLK * (index ^ (2 * position)), BLK)
-            for number, dst in enumerate(out_refs):
-                at = number * rows
-                dst[:, pl.ds(column, BLK)] = first[at : at + rows, lane : lane + BLK].astype(
-                    F32
-                ) + second[at : at + rows, other : other + BLK].astype(F32)
 
 
 def unpack_kernel(bucket_ref, out_own, grad_own, away_ref, out_ref, grad_ref):
@@ -645,7 +663,7 @@
     recv_x = to_chip(away_x)
     core_x = to_core(home_x)
     vecs, away_c, home_c = call(
-        stack_kernel, "stack", [((VECS, C), F32), ((128, C), BF16), ((192, C), BF16)], [], 8,
+        stack_kernel, "stack", [((VECS, C), F32), ((160, C), BF16), ((192, C), BF16)], [], 8,
         kinds, cotangent, *[row(v) for v in vectors],
     )
     recv_c = to_chip(away_c)
@@ -656,27 +674,27 @@
     image, conv, act2, stats, act1_t, act2_t, send_t = call(
         first_kernel, "first",
         [img16, img32, img16, rows8, turned, turned, ((2, C // 2, PIX), BF16)],
-        [shifts], 24,
+        [shifts], 14,
         kinds, home_x, core_x, recv_x, core_recv_x, vecs, conv1_weight,
     )
     half_t = to_chip(send_t)
     core_half_t = to_core(half_t)
 
-    attn_out = ((batches // 2, 4 * small_rows, 2 * BLK), BF16)
+    attn_out = ((batches, 4 * small_rows, BLK), BF16)
     middle, mixed, grad2, grad_middle, attn_keep, attn_send, vec_a, block2, block2_send = call(
         second_kernel, "second",
         [img32, img16, img16, img32, attn_out, attn_out, rows8, block, block],
-        [shifts, img16, ((PIX, 4 * C), BF16), ((C, 8 * BLK), F32)], 32,
+        [shifts, img16, ((PIX, 4 * C), BF16), ((C, 8 * BLK), F32)], 24,
         kinds, image, act2, home_c, core_c, recv_c, core_recv_c, vecs,
         conv2_weight, query_weight, key_weight, value_weight, proj_weight,
     )
     block2_away = to_chip(block2_send)
-    attn_got = to_batch(attn_send, 1)
+    attn_got = to_chip(attn_send)
 
     grad1, block1, block1_send, vec_b = call(
         third_kernel, "third",
         [img16, block, block, rows8],
-        [shifts, img32], 24,
+        [shifts, img32], 14,
         kinds, grad2, conv, stats, vecs, conv2_weight,
     )
     block1_away = to_chip(block1_send)
@@ -687,67 +705,79 @@
             [((batches // 2, shard_rows, BLK), BF16)] * 2,
             [((C, 2 * PIX), BF16), ((2 * PIX, 9 * BLK), BF16), ((3, PIX + 2 * PAD, BLK), BF16),
              ((9 * C, BLK), F32)],
-            24, kinds, act_t, half_t, core_half_t, own, away,
+            18, kinds, act_t, half_t, core_half_t, own, away,
         )
 
     keep2, send2 = weight_grad("weight2", act2_t, 1, after(block2, block1), block2_away)
     got2 = to_batch(send2, 1)
 
-    def scatter(name, *pairs):
-        bit = 1
-        while True:
-            width = min(2, bits - bit)
-            ways = 1 << width
-            count = pairs[0].shape[0] // ways
-            rows = sum(v.shape[1] for v in pairs[::2])
-            parts = call(
-                functools.partial(route_kernel, bit=bit, ways=ways), name + str(bit),
-                [((count, rows, pairs[0].shape[2]), BF16)] * ways, [], 16, *pairs, smem=0,
-            )
-            got = [to_batch(parts[j], j << bit) for j in range(1, ways)]
-            bit += width
-            added = functools.reduce(lambda a, b: a + b, [g.astype(F32) for g in got])
-            if bit == bits:
-                return parts, (added + parts[0].astype(F32)).astype(BF16)[0]
-            pairs = (parts[0], added.astype(BF16))
+    def spread(name, bit, low, *pairs):
+        ways = 1 << min(2, bits - bit)
+        count = pairs[0].shape[0] // ways
+        rows = sum(v.shape[1] for v in pairs[::2])
+        parts = call(
+            functools.partial(route_kernel, bit=bit, ways=ways, low=low), name + str(bit),
+            [((count, rows, BLK), BF16)] * ways, [], 16, *pairs, smem=0,
+        )
+        return parts, [to_batch(parts[j], j << bit) for j in range(1, ways)]
+
+    def rest(name, low, parts, got):
+        for bit in range(3, bits, 2):
+            added = total_of([parts[0]] + got).astype(BF16)
+            parts, got = spread(name, bit, low, added, jnp.zeros_like(added))
+        return [parts[0]] + got
+
+    def finish(name, arrays, *others):
+        rows = arrays[0].shape[1] + (others[0].shape[0] if others else 0)
+        return call(
+            functools.partial(sum_kernel, count=len(arrays)), name, [((rows, BLK), BF16)], [], 8,
+            *arrays, *others, smem=0,
+        )[0]
 
     def gather(shard):
         far = to_chip(shard)
         near = to_core(shard)
         return shard, far, near, to_core(far)
 
-    routed_a, shard_a = scatter("routea", after(attn_keep, send2), attn_got)
-    keep1, send1 = weight_grad("weight1", act1_t, 0, after(block1, *routed_a), block1_away)
+    parts_a, got_a = spread("routea", 1, 2, after(attn_keep, send2), attn_got)
+    keep1, send1 = weight_grad("weight1", act1_t, 0, after(block1, *parts_a), block1_away)
     got1 = to_batch(send1, 1)
+    parts_b, got_b = spread("routeb", 1, 1, after(keep2, send1), got2)
 
     out_own, grad_own, image_send, vec_keep, vec_send = call(
         fourth_kernel, "fourth",
         [((192, C), BF16), ((192, C), BF16), ((2, 128, C), BF16),
          ((batches // 2, VECS, BLK), BF16), ((batches // 2, VECS, BLK), BF16)],
-        [shifts, img32, img16, ((VECS, C), F32)], 24,
-        kinds, after(grad1, send1), image, stats, grad_middle, middle, mixed, vecs,
+        [shifts, img32, img16, ((VECS, C), F32)], 14,
+        kinds, after(grad1, *parts_b), image, stats, grad_middle, middle, mixed, vecs,
         conv1_weight, proj_weight, vec_a, vec_b,
     )
     image_away = to_chip(image_send)
     vec_got = to_batch(vec_send, 1)
 
-    routed_b, shard_b = scatter("routeb", after(keep2, shard_a, vec_keep), got2)
-    parts_a = gather(after(shard_a, *routed_b))
-    small = call(
-        join_attn_kernel, "joina", [((small_rows, C), F32)] * 4, [], 8, *parts_a, smem=0
-    )
+    attn_mine, attn_other = call(
+        half_kernel, "halfa", [((4 * small_rows, BLK), BF16)] * 2, [], 8,
+        *rest("routea", 2, parts_a, [after(g, parts_b[0]) for g in got_a]), smem=0,
+    )
+    attn_far = to_batch(attn_other, 1)
+    shard_b = finish("sumb", rest("routeb", 1, parts_b, got_b), attn_mine, attn_far)
+    parts_c, got_c = spread("routec", 1, 1, after(keep1, shard_b), got1, vec_keep, vec_got)
+    shard_b = after(shard_b, *parts_c)
+    gathered_b = gather(shard_b)
     outputs, input_grad = call(
         unpack_kernel, "unpack",
         [(inputs.shape, BF16)] * 2, [], 8,
-        kinds, out_own, grad_own, after(image_away, *routed_b),
-    )
-    routed_c, shard_c = scatter(
-        "routec", after(keep1, shard_b), got1, vec_keep, vec_got
-    )
-    (whole2,) = call(join_kernel, "joinb", [((shard_rows, C), F32)], [], 8, *gather(shard_b), smem=0)
+        kinds, out_own, grad_own, after(image_away, *parts_c),
+    )
+    shard_c = finish("sumc", rest("routec", 1, parts_c, got_c))
+    whole2, *small = call(
+        join_kernel, "joinb", [((shard_rows, C), F32)] + [((small_rows, C), F32)] * 4, [], 8,
+        after(gathered_b[0], shard_c), *gathered_b[1:], smem=0,
+    )
+    gathered_c = gather(after(shard_c, outputs))
     whole1, *sums = call(
         join_kernel, "joinc", [((shard_rows, C), F32)] + [((1, small_rows), F32)] * 11, [], 8,
-        *gather(after(shard_c, whole2, small[0], outputs)), smem=0,
+        after(gathered_c[0], whole2), *gathered_c[1:], smem=0,
     )
     v = [row.reshape(small_rows) for row in sums]
 

time: 99 us -> 98 us (0.990)
  Pallas kernels: 39.9 us -> 37.4 us
  starting transfers between devices: 32.8 us -> 33.8 us
    pallas_call x15 -> x17, Pallas kernels: 39.9 us -> 37.4 us  [call(): pl.pallas_call(kernel, name=name, out_shape=[jax.ShapeDtypeStruct(shape,...]
    ppermute x1, starting transfers between devices: 0.14 us -> 1.35 us  [on_device(): core_recv_c = lax.ppermute(away_c, 'height', [(i, i ^ 3) for i in range(4)])]
    ppermute x9, starting transfers between devices: 13.1 us -> 12 us  [to_chip(): return lax.ppermute(v, 'height', [(i, i ^ 2) for i in range(4)])]
  transfers between devices with their start and end apart: 33 -> 31, of which waited for: 8 -> 12; matrix products, arithmetic and copies ran while one was open for 0% -> 0% of each run, Pallas kernels for 36% -> 35%
where the time goes in v5:
time: 98 us; the launch traced here: 97.1 us
  Pallas kernels  37.4 us (38%)
  starting transfers between devices  33.8 us (34%)
  waiting for transfers between devices  23.7 us (24%)
  between operations  1.26 us (1%)
    pallas_call x17, Pallas kernels, call(): pl.pallas_call(kernel, name=name, out_shape=[jax.ShapeDtypeStruct(shape,...  37.4 us
    ppermute x13, starting transfers between devices, to_batch(): return lax.ppermute(v, 'batch', [(i, i ^ change) for i in range(batches)])  18.8 us
    ppermute x13, waiting for transfers between devices, to_batch(): return lax.ppermute(v, 'batch', [(i, i ^ change) for i in range(batches)])  14.4 us
    ppermute x9, starting transfers between devices, to_chip(): return lax.ppermute(v, 'height', [(i, i ^ 2) for i in range(4)])  12 us
    ppermute x9, waiting for transfers between devices, to_chip(): return lax.ppermute(v, 'height', [(i, i ^ 2) for i in range(4)])  8.25 us
  transfers between devices with their start and end apart: 31, of which 12 were waited for; matrix products, arithmetic and copies ran while one was open for 0% of the time, Pallas kernels for 35%

profile of v5, /device:TPU:0, one launch (start us, length us, event | category | flops | bytes accessed | tf_op | source)
XLA Modules:
  0.0 97.1 jit_solution(5696706207627847145)
XLA Ops:
  0.8 0.0 slice-start
  0.8 0.0 slice-start.2
  0.8 1.9 %pack.1 = (s32[2]{0:T(128)}, bf16[128,512]{1,0:T(8,128)(2,1)}, bf16[192,512]{1,0:T(8,128)(2,1)}) custom-call(s32[2]{0:T(128)} %bucket_hbm.1, bf16[2,6,32,512]{3,2,1,0:T(8,128)(2,1)} %x_hbm.1), custom_call_target="tpu_custom_call" | custom-call | flops 10737418240 | bytes 1024 | tf_op jit(solution)/shard_map/pack/pallas_call | solution.py:584
  2.7 3.0 %collective-permute-start.1 = (bf16[128,512]{1,0:T(8,128)(2,1)}, bf16[128,512]{1,0:T(8,128)(2,1)S(1)}, u32[]{:S(2)}, u32[]{:S(2)}) collective-permute-start(bf16[128,512]{1,0:T(8,128)(2,1)} %get-tuple-element.104), channel_id=1, source_target_pairs={{0,2},{1,3},{2,0},{3,1},{4,6},{5,7},{6,4},{7,5},{8,10},{9,11},{10,... | collective-permute-start | bytes 393224 | tf_op jit(solution)/shard_map/ppermute | solution.py:638
  5.8 0.0 collective-permute-start
  5.9 0.0 copy-start.1
  5.9 0.8 copy-done.1
  6.7 0.6 stack.1
  7.3 0.0 copy-start.3
  7.3 0.0 copy-start.4
  7.3 0.0 copy-start.5
  7.3 0.0 copy-start.6
  7.3 0.6 collective-permute-start.3
  7.9 0.1 collective-permute-start.4
  8.0 1.4 %collective-permute-start.5 = (bf16[160,512]{1,0:T(8,128)(2,1)S(1)}, bf16[160,512]{1,0:T(8,128)(2,1)S(1)}, u32[]{:S(2)}, u32[]{:S(2)}) collective-permute-start(bf16[160,512]{1,0:T(8,128)(2,1)S(1)} %get-tuple-element.110), channel_id=1, source_target_pairs={{0,3},{1,2},{2,1},{3,0},{4,7},{5,6},{6,5},{7,4},{8,11},{9,10},{10,... | collective-permute-start | bytes 491528 | tf_op jit(solution)/shard_map/ppermute | solution.py:671
  9.3 0.1 collective-permute-done.1.received
  9.5 0.6 collective-permute-start.2
  10.1 0.0 collective-permute-done.partner
  10.1 1.0 %collective-permute-done.2.partner_received = bf16[128,512]{1,0:T(8,128)(2,1)S(1)} collective-permute-done((bf16[128,512]{1,0:T(8,128)(2,1)S(1)}, bf16[128,512]{1,0:T(8,128)(2,1)S(1)}, u32[]{:S(2)}, u32[]{:S(2)}) %collective-permute-start.2) | collective-permute-done | bytes 131104 | tf_op jit(solution)/shard_map/ppermute | solution.py:635
  11.1 5.4 %first.1 = (bf16[512,512]{1,0:T(8,128)(2,1)S(1)}, f32[512,512]{1,0:T(8,128)S(1)}, bf16[512,512]{1,0:T(8,128)(2,1)S(1)}, f32[8,512]{1,0:T(8,128)S(1)}, bf16[512,5...) custom-call(s32[2]{0:T(128)S(1)} %copy-done.2, bf16[192,512]{1,0:T(8,128)(2,1)S(1)} %copy-done, ...), custom_call_target="tpu_custom_call" | custom-call | flops 21474836 | bytes 1024 | tf_op jit(solution)/shard_map/first/pallas_call | solution.py:584
  16.4 1.9 %collective-permute-start.6 = (bf16[2,256,512]{2,1,0:T(8,128)(2,1)S(1)}, bf16[2,256,512]{2,1,0:T(8,128)(2,1)S(1)}, u32[]{:S(2)}, u32[]{:S(2)}) collective-permute-start(bf16[2,256,512]{2,1,0:T(8,128)(2,1)S(1)} %get-tuple-element.116), channel_id=1, source_target_pairs={{0,2},{1,3},{2,0},{3,1},{4,6},{5,7},{6,4},{7,5},{8,10},{9,11},{10,... | collective-permute-start | bytes 1572872 | tf_op jit(solution)/shard_map/ppermute | solution.py:638
  18.4 9.3 %second.1 = (f32[512,512]{1,0:T(8,128)S(1)}, bf16[512,512]{1,0:T(8,128)(2,1)S(1)}, bf16[512,512]{1,0:T(8,128)(2,1)S(1)}, f32[512,512]{1,0:T(8,128)S(1)}, bf16[8,...) custom-call(s32[2]{0:T(128)S(1)} %copy-done.2, ...), custom_call_target="tpu_custom_call" | custom-call | flops 32212254720 | bytes 1024 | tf_op jit(solution)/shard_map/second/pallas_call | solution.py:584
  27.7 0.3 collective-permute-start.8
  28.0 1.8 %collective-permute-start.9 = (bf16[8,256,128]{2,1,0:T(8,128)(2,1)S(1)}, bf16[8,256,128]{2,1,0:T(8,128)(2,1)S(1)}, u32[]{:S(2)}, u32[]{:S(2)}) collective-permute-start(bf16[8,256,128]{2,1,0:T(8,128)(2,1)S(1)} %get-tuple-element.126), channel_id=1, source_target_pairs={{0,2},{1,3},{2,0},{3,1},{4,6},{5,7},{6,4},{7,5},{8,10},{9,11},{10,... | collective-permute-start | bytes 1572872 | tf_op jit(solution)/shard_map/ppermute | solution.py:638
  29.8 1.2 %collective-permute-done.6.half_t = bf16[2,256,512]{2,1,0:T(8,128)(2,1)S(1)} collective-permute-done((bf16[2,256,512]{2,1,0:T(8,128)(2,1)S(1)}, bf16[2,256,512]{2,1,0:T(8,128)(2,1)S(1)}, u32[]{:S(2)}, u32[]{:S(2)}) %collective-permute-start.6) | collective-permute-done | bytes 524320 | tf_op jit(solution)/shard_map/ppermute | solution.py:638
  31.1 4.3 %third.1 = (bf16[512,512]{1,0:T(8,128)(2,1)S(1)}, bf16[512,128]{1,0:T(8,128)(2,1)S(1)}, bf16[512,128]{1,0:T(8,128)(2,1)S(1)}, f32[8,512]{1,0:T(8,128)S(1)}) custom-call(s32[2]{0:T(128)S(1)} %copy-done.2, bf16[512,512]{1,0:T(8,128)(2,1)S(1)} %get-tuple-element.111.grad2_ref, f32[512,512]{1,0:T(8,128)S(1)} %get-tuple-element.112.conv_ref, ...), custom_call_target="tpu_custom_call" | custom-call | flops 21474836480 | bytes 1024 | tf_op jit(solution)/shard_map/third/pallas_call | solution.py:584
  35.4 3.1 %weight2.5 = (bf16[4,576,128]{2,1,0:T(8,128)(2,1)S(1)}, bf16[4,576,128]{2,1,0:T(8,128)(2,1)S(1)}) custom-call(s32[2]{0:T(128)S(1)} %copy-done.2, bf16[512,512]{1,0:T(8,128)(2,1)S(1)} %get-tuple-element.115.act_t, bf16[2,256,512]{2,1,0:T(8,128)(2,1)S(1)} %collective-permute-done.6.half_t, bf16[2,256,512]{2,1,0:T(8,128)(2,1)S(1)} %collective-permute-done.7.partner_half_t, ...), custom_call_target="tpu_custom_call" | custom-call | flops 1073741824 | bytes 1024 | tf_op jit(solution)/shard_map/weight2/pallas_call | solution.py:584
  38.5 2.0 %collective-permute-start.11 = (bf16[4,576,128]{2,1,0:T(8,128)(2,1)S(1)}, bf16[4,576,128]{2,1,0:T(8,128)(2,1)S(1)}, u32[]{:S(2)}, u32[]{:S(2)}) collective-permute-start(bf16[4,576,128]{2,1,0:T(8,128)(2,1)S(1)} %get-tuple-element.124), channel_id=1, source_target_pairs={{0,4},{4,0},{8,12},{12,8},{16,20},{20,16},{24,28},{28,24},{1,5},{5... | collective-permute-start | bytes 1769480 | tf_op jit(solution)/shard_map/ppermute | solution.py:641
  40.5 1.6 %collective-permute-start.10 = (bf16[512,128]{1,0:T(8,128)(2,1)S(1)}, bf16[512,128]{1,0:T(8,128)(2,1)S(1)}, u32[]{:S(2)}, u32[]{:S(2)}) collective-permute-start(bf16[512,128]{1,0:T(8,128)(2,1)S(1)} %get-tuple-element.132), channel_id=1, source_target_pairs={{0,2},{1,3},{2,0},{3,1},{4,6},{5,7},{6,4},{7,5},{8,10},{9,11},{10,... | collective-permute-start | bytes 393224 | tf_op jit(solution)/shard_map/ppermute | solution.py:638
  42.1 3.4 %collective-permute-done.9.refs_1_ = bf16[8,256,128]{2,1,0:T(8,128)(2,1)S(1)} collective-permute-done((bf16[8,256,128]{2,1,0:T(8,128)(2,1)S(1)}, bf16[8,256,128]{2,1,0:T(8,128)(2,1)S(1)}, u32[]{:S(2)}, u32[]{:S(2)}) %collective-permute-start.9) | collective-permute-done | bytes 524320 | tf_op jit(solution)/shard_map/ppermute | solution.py:638
  45.4 0.1 routea1.1
  45.6 3.5 %collective-permute-start.18 = (bf16[2,256,128]{2,1,0:T(8,128)(2,1)S(1)}, bf16[2,256,128]{2,1,0:T(8,128)(2,1)S(1)}, u32[]{:S(2)}, u32[]{:S(2)}) collective-permute-start(bf16[2,256,128]{2,1,0:T(8,128)(2,1)S(1)} %get-tuple-element.130), channel_id=1, source_target_pairs={{0,24},{4,28},{8,16},{12,20},{16,8},{20,12},{24,0},{28,4},{1,25},{... | collective-permute-start | bytes 393224 | tf_op jit(solution)/shard_map/ppermute | solution.py:641
  49.1 0.9 collective-permute-start.16
  50.0 3.1 %weight1.4 = (bf16[4,576,128]{2,1,0:T(8,128)(2,1)S(1)}, bf16[4,576,128]{2,1,0:T(8,128)(2,1)S(1)}) custom-call(s32[2]{0:T(128)S(1)} %copy-done.2, bf16[512,512]{1,0:T(8,128)(2,1)S(1)} %get-tuple-element.122.act_t, bf16[2,256,512]{2,1,0:T(8,128)(2,1)S(1)} %collective-permute-done.6.half_t, bf16[2,256,512]{2,1,0:T(8,128)(2,1)S(1)} %collective-permute-done.7.partner_half_t, ...), custom_call_target="tpu_custom_call" | custom-call | flops 3221225472 | bytes 1024 | tf_op jit(solution)/shard_map/weight1/pallas_call | solution.py:584
  53.1 1.4 %collective-permute-start.20 = (bf16[4,576,128]{2,1,0:T(8,128)(2,1)S(1)}, bf16[4,576,128]{2,1,0:T(8,128)(2,1)S(1)}, u32[]{:S(2)}, u32[]{:S(2)}) collective-permute-start(bf16[4,576,128]{2,1,0:T(8,128)(2,1)S(1)} %get-tuple-element.133), channel_id=1, source_target_pairs={{0,4},{4,0},{8,12},{12,8},{16,20},{20,16},{24,28},{28,24},{1,5},{5... | collective-permute-start | bytes 1769480 | tf_op jit(solution)/shard_map/ppermute | solution.py:641
  54.5 0.4 collective-permute-done.11.refs_1_
  54.9 0.1 routeb1.1
  55.1 4.3 %collective-permute-done.17.refs_2_ = bf16[2,256,128]{2,1,0:T(8,128)(2,1)S(1)} collective-permute-done((bf16[2,256,128]{2,1,0:T(8,128)(2,1)S(1)}, bf16[2,256,128]{2,1,0:T(8,128)(2,1)S(1)}, u32[]{:S(2)}, u32[]{:S(2)}) %collective-permute-start.17) | collective-permute-done | bytes 131104 | tf_op jit(solution)/shard_map/ppermute | solution.py:641
  59.3 0.1 halfa.1
  59.4 1.6 %collective-permute-start.19 = (bf16[256,128]{1,0:T(8,128)(2,1)S(1)}, bf16[256,128]{1,0:T(8,128)(2,1)S(1)}, u32[]{:S(2)}, u32[]{:S(2)}) collective-permute-start(bf16[256,128]{1,0:T(8,128)(2,1)S(1)} %get-tuple-element.153), channel_id=1, source_target_pairs={{0,4},{4,0},{8,12},{12,8},{16,20},{20,16},{24,28},{28,24},{1,5},{5... | collective-permute-start | bytes 196616 | tf_op jit(solution)/shard_map/ppermute | solution.py:641
  61.0 3.0 %collective-permute-start.14 = (bf16[1,576,128]{2,1,0:T(8,128)(2,1)S(1)}, bf16[1,576,128]{2,1,0:T(8,128)(2,1)S(1)}, u32[]{:S(2)}, u32[]{:S(2)}) collective-permute-start(bf16[1,576,128]{2,1,0:T(8,128)(2,1)S(1)} %get-tuple-element.137), channel_id=1, source_target_pairs={{0,16},{4,20},{8,24},{12,28},{16,0},{20,4},{24,8},{28,12},{1,17},{... | collective-permute-start | bytes 442376 | tf_op jit(solution)/shard_map/ppermute | solution.py:641
  64.0 1.3 %collective-permute-start.15 = (bf16[1,576,128]{2,1,0:T(8,128)(2,1)S(1)}, bf16[1,576,128]{2,1,0:T(8,128)(2,1)S(1)}, u32[]{:S(2)}, u32[]{:S(2)}) collective-permute-start(bf16[1,576,128]{2,1,0:T(8,128)(2,1)S(1)} %get-tuple-element.138), channel_id=1, source_target_pairs={{0,24},{4,28},{8,16},{12,20},{16,8},{20,12},{24,0},{28,4},{1,25},{... | collective-permute-start | bytes 442376 | tf_op jit(solution)/shard_map/ppermute | solution.py:641
  65.4 5.0 %fourth.1 = (bf16[192,512]{1,0:T(8,128)(2,1)S(1)}, bf16[192,512]{1,0:T(8,128)(2,1)S(1)}, bf16[2,128,512]{2,1,0:T(8,128)(2,1)S(1)}, bf16[4,16,128]{2,1,0:T(8,128)(2,1)S(1)}, bf16[4,16,128]{2,1,0:T(8,128)(2,1)S(1)}) custom-call(s32[2]{0:T(128)S(1)} %copy-done.2, bf16[512,512]{1,0:T(8,128)(2,1)S(1)} %get-tuple-element.139.grad1_ref, ...), custom_call_target="tpu_custom_call" | custom-call | flops 10737418240 | bytes 1024 | tf_op jit(solution)/shard_map/fourth/pallas_call | solution.py:584
  70.4 1.2 %collective-permute-start.12 = (bf16[2,128,512]{2,1,0:T(8,128)(2,1)S(1)}, bf16[2,128,512]{2,1,0:T(8,128)(2,1)S(1)}, u32[]{:S(2)}, u32[]{:S(2)}) collective-permute-start(bf16[2,128,512]{2,1,0:T(8,128)(2,1)S(1)} %get-tuple-element.147), channel_id=1, source_target_pairs={{0,2},{1,3},{2,0},{3,1},{4,6},{5,7},{6,4},{7,5},{8,10},{9,11},{10,... | collective-permute-start | bytes 786440 | tf_op jit(solution)/shard_map/ppermute | solution.py:638
  71.6 0.5 collective-permute-start.21
  72.1 2.2 %collective-permute-done.14.refs_2_ = bf16[1,576,128]{2,1,0:T(8,128)(2,1)S(1)} collective-permute-done((bf16[1,576,128]{2,1,0:T(8,128)(2,1)S(1)}, bf16[1,576,128]{2,1,0:T(8,128)(2,1)S(1)}, u32[]{:S(2)}, u32[]{:S(2)}) %collective-permute-start.14) | collective-permute-done | bytes 147488 | tf_op jit(solution)/shard_map/ppermute | solution.py:641
  74.3 0.1 sumb.1.own_ref
  74.4 0.9 collective-permute-done.21.refs_3_
  75.3 0.1 routec1.1
  75.5 1.4 %collective-permute-start.22 = (bf16[1,592,128]{2,1,0:T(8,128)(2,1)S(1)}, bf16[1,592,128]{2,1,0:T(8,128)(2,1)S(1)}, u32[]{:S(2)}, u32[]{:S(2)}) collective-permute-start(bf16[1,592,128]{2,1,0:T(8,128)(2,1)S(1)} %get-tuple-element.158), channel_id=1, source_target_pairs={{0,8},{4,12},{8,0},{12,4},{16,24},{20,28},{24,16},{28,20},{1,9},{5... | collective-permute-start | bytes 454664 | tf_op jit(solution)/shard_map/ppermute | solution.py:641
  76.9 1.7 %collective-permute-start.23 = (bf16[1,592,128]{2,1,0:T(8,128)(2,1)S(1)}, bf16[1,592,128]{2,1,0:T(8,128)(2,1)S(1)}, u32[]{:S(2)}, u32[]{:S(2)}) collective-permute-start(bf16[1,592,128]{2,1,0:T(8,128)(2,1)S(1)} %get-tuple-element.159), channel_id=1, source_target_pairs={{0,16},{4,20},{8,24},{12,28},{16,0},{20,4},{24,8},{28,12},{1,17},{... | collective-permute-start | bytes 454664 | tf_op jit(solution)/shard_map/ppermute | solution.py:641
  78.6 1.3 %collective-permute-start.24 = (bf16[1,592,128]{2,1,0:T(8,128)(2,1)S(1)}, bf16[1,592,128]{2,1,0:T(8,128)(2,1)S(1)}, u32[]{:S(2)}, u32[]{:S(2)}) collective-permute-start(bf16[1,592,128]{2,1,0:T(8,128)(2,1)S(1)} %get-tuple-element.160), channel_id=1, source_target_pairs={{0,24},{4,28},{8,16},{12,20},{16,8},{20,12},{24,0},{28,4},{1,25},{... | collective-permute-start | bytes 454664 | tf_op jit(solution)/shard_map/ppermute | solution.py:641
  79.9 0.9 collective-permute-start.25
  80.8 1.5 %unpack.1 = (bf16[2,6,32,512]{3,2,1,0:T(8,128)(2,1)}, bf16[2,6,32,512]{3,2,1,0:T(8,128)(2,1)}) custom-call(s32[2]{0:T(128)S(1)} %copy-done.2, bf16[192,512]{1,0:T(8,128)(2,1)S(1)} %get-tuple-element.145.out_own, bf16[192,512]{1,0:T(8,128)(2,1)S(1)} %get-tuple-element.146.grad_own, bf16[2,128,512]{2,1,0:T(8,128)(2,1)S(1)} %collective-permute-done.12.away_ref), custom_call_target="tpu_custom_call" | custom-call | flops 21474836 | bytes 1024 | tf_op jit(solution)/shard_map/unpack/pallas_call | solution.py:584
  82.3 1.5 %collective-permute-done.22.refs_1_ = bf16[1,592,128]{2,1,0:T(8,128)(2,1)S(1)} collective-permute-done((bf16[1,592,128]{2,1,0:T(8,128)(2,1)S(1)}, bf16[1,592,128]{2,1,0:T(8,128)(2,1)S(1)}, u32[]{:S(2)}, u32[]{:S(2)}) %collective-permute-start.22) | collective-permute-done | bytes 151584 | tf_op jit(solution)/shard_map/ppermute | solution.py:641
  83.9 5.1 %collective-permute-done.23.refs_2_ = bf16[1,592,128]{2,1,0:T(8,128)(2,1)S(1)} collective-permute-done((bf16[1,592,128]{2,1,0:T(8,128)(2,1)S(1)}, bf16[1,592,128]{2,1,0:T(8,128)(2,1)S(1)}, u32[]{:S(2)}, u32[]{:S(2)}) %collective-permute-start.23) | collective-permute-done | bytes 151584 | tf_op jit(solution)/shard_map/ppermute | solution.py:641
  89.0 0.1 sumc.1.own_ref
  89.1 1.2 %collective-permute-start.28 = (bf16[592,128]{1,0:T(8,128)(2,1)S(1)}, bf16[592,128]{1,0:T(8,128)(2,1)S(1)}, u32[]{:S(2)}, u32[]{:S(2)}) collective-permute-start(bf16[592,128]{1,0:T(8,128)(2,1)S(1)} %sumc.1.own_ref), channel_id=1, source_target_pairs={{0,2},{1,3},{2,0},{3,1},{4,6},{5,7},{6,4},{7,5},{8,10},{9,11},{10,... | collective-permute-start | bytes 454664 | tf_op jit(solution)/shard_map/ppermute | solution.py:638
  90.3 0.5 collective-permute-start.27
  90.8 0.0 collective-permute-start.29
  90.8 3.5 %collective-permute-done.28.far_ref = bf16[592,128]{1,0:T(8,128)(2,1)S(1)} collective-permute-done((bf16[592,128]{1,0:T(8,128)(2,1)S(1)}, bf16[592,128]{1,0:T(8,128)(2,1)S(1)}, u32[]{:S(2)}, u32[]{:S(2)}) %collective-permute-start.28) | collective-permute-done | bytes 151584 | tf_op jit(solution)/shard_map/ppermute | solution.py:638
  94.3 1.3 %joinb.1 = (f32[576,512]{1,0:T(8,128)}, f32[64,512]{1,0:T(8,128)}, f32[64,512]{1,0:T(8,128)}, f32[64,512]{1,0:T(8,128)}, f32[64,512]{1,0:T(8,128)}) custom-call(bf16[832,128]{1,0:T(8,128)(2,1)S(1)} %sumb.1.own_ref, bf16[832,128]{1,0:T(8,128)(2,1)S(1)} %collective-permute-done.25.far_ref, bf16[832,128]{1,0:T(8,128)(2,1)S(1)} %collective-permute-done.26.near_ref, ...), custom_call_target="tpu_custom_call" | custom-call | flops 21474836 | bytes 1024 | tf_op jit(solution)/shard_map/joinb/pallas_call | solution.py:584
  95.6 0.1 collective-permute-done.30.diagonal_ref
  95.7 1.2 %joinc.1 = (f32[576,512]{1,0:T(8,128)}, f32[1,64]{1,0:T(1,128)}, f32[1,64]{1,0:T(1,128)}, f32[1,64]{1,0:T(1,128)}, f32[1,64]{1,0:T(1,128)}, /*index=5*/f32[1,64]...) custom-call(bf16[592,128]{1,0:T(8,128)(2,1)S(1)} %sumc.1.own_ref, ...), custom_call_target="tpu_custom_call" | custom-call | flops 21474836 | bytes 1024 | tf_op jit(solution)/shard_map/joinc/pallas_call | solution.py:584
  (63 shorter events, 0.1 us)
Async XLA Ops:
  0.7 5.1 %copy-start.8 = (f32[512]{0:T(512)S(1)}, f32[512]{0:T(512)}, u32[]{:S(2)}) copy-start(f32[512]{0:T(512)} %param.22) | copy-start | bytes 6148
  0.7 5.1 %copy-start.9 = (f32[512]{0:T(512)S(1)}, f32[512]{0:T(512)}, u32[]{:S(2)}) copy-start(f32[512]{0:T(512)} %param.23) | copy-start | bytes 6148
  0.7 5.1 %copy-start.18 = (f32[512]{0:T(512)S(1)}, f32[512]{0:T(512)}, u32[]{:S(2)}) copy-start(f32[512]{0:T(512)} %param.38) | copy-start | bytes 6148
  0.7 5.1 %copy-start.10 = (f32[512]{0:T(512)S(1)}, f32[512]{0:T(512)}, u32[]{:S(2)}) copy-start(f32[512]{0:T(512)} %param.25) | copy-start | bytes 6148
  0.7 5.1 %copy-start.11 = (f32[512]{0:T(512)S(1)}, f32[512]{0:T(512)}, u32[]{:S(2)}) copy-start(f32[512]{0:T(512)} %param.26) | copy-start | bytes 6148
  0.7 5.1 %copy-start.12 = (f32[512]{0:T(512)S(1)}, f32[512]{0:T(512)}, u32[]{:S(2)}) copy-start(f32[512]{0:T(512)} %param.27) | copy-start | bytes 6148
  0.7 5.1 %copy-start.13 = (f32[512]{0:T(512)S(1)}, f32[512]{0:T(512)}, u32[]{:S(2)}) copy-start(f32[512]{0:T(512)} %param.29) | copy-start | bytes 6148
  0.7 5.1 %copy-start.14 = (f32[512]{0:T(512)S(1)}, f32[512]{0:T(512)}, u32[]{:S(2)}) copy-start(f32[512]{0:T(512)} %param.30) | copy-start | bytes 6148
  0.7 5.1 %copy-start.15 = (f32[512]{0:T(512)S(1)}, f32[512]{0:T(512)}, u32[]{:S(2)}) copy-start(f32[512]{0:T(512)} %param.31) | copy-start | bytes 6148
  0.8 5.1 %copy-start.16 = (f32[512]{0:T(512)S(1)}, f32[512]{0:T(512)}, u32[]{:S(2)}) copy-start(f32[512]{0:T(512)} %param.33) | copy-start | bytes 6148
  0.8 5.1 %copy-start.17 = (f32[512]{0:T(512)S(1)}, f32[512]{0:T(512)}, u32[]{:S(2)}) copy-start(f32[512]{0:T(512)} %param.36) | copy-start | bytes 6148
  0.8 5.1 %copy-start.7 = (bf16[2,6,32,512]{3,2,1,0:T(8,128)(2,1)S(1)}, bf16[2,6,32,512]{3,2,1,0:T(8,128)(2,1)}, u32[]{:S(2)}) copy-start(bf16[2,6,32,512]{3,2,1,0:T(8,128)(2,1)} %cot_ref.1) | copy-start | bytes 1179652
  0.8 10.3 %slice-start = ((s8[4718592]{0:T(1024)(128)(4,1)}), s8[524288]{0:T(1024)(128)(4,1)S(1)}, s32[]{:S(2)}) async-start(s8[4718592]{0:T(1024)(128)(4,1)} %bitcast.22), calls=%async_computation | async-start | bytes 1048576
  0.8 17.5 %slice-start.2 = ((s8[4718592]{0:T(1024)(128)(4,1)}), s8[4194304]{0:T(1024)(128)(4,1)S(1)}, s32[]{:S(2)}) async-start(s8[4718592]{0:T(1024)(128)(4,1)} %bitcast.24), calls=%async_computation.2 | async-start | bytes 8388608
  2.7 6.7 %collective-permute-start.1 = (bf16[128,512]{1,0:T(8,128)(2,1)}, bf16[128,512]{1,0:T(8,128)(2,1)S(1)}, u32[]{:S(2)}, u32[]{:S(2)}) collective-permute-start(bf16[128,512]{1,0:T(8,128)(2,1)} %get-tuple-element.104), channel_id=1, source_target_pairs={{0,2},{1,3},{2,0},{3,1},{4,6},{5,7},{6,4},{7,5},{8,10},{9,11},{10,... | collective-permute-start | bytes 393224 | tf_op jit(solution)/shard_map/ppermute | solution.py:638
  5.8 4.3 %collective-permute-start = (bf16[192,512]{1,0:T(8,128)(2,1)}, bf16[192,512]{1,0:T(8,128)(2,1)S(1)}, u32[]{:S(2)}, u32[]{:S(2)}) collective-permute-start(bf16[192,512]{1,0:T(8,128)(2,1)} %get-tuple-element.103.own), channel_id=1, source_target_pairs={{0,1},{1,0},{2,3},{3,2},{4,5},{5,4},{6,7},{7,6},{8,9},{9,8},{10,11... | collective-permute-start | bytes 589832 | tf_op jit(solution)/shard_map/ppermute | solution.py:635
  5.8 5.3 %slice-start.1 = ((s8[4718592]{0:T(1024)(128)(4,1)}), s8[4194304]{0:T(1024)(128)(4,1)S(1)}, s32[]{:S(2)}) async-start(s8[4718592]{0:T(1024)(128)(4,1)} %bitcast.22), calls=%async_computation.1 | async-start | bytes 8388608
  5.9 0.8 copy-start.1
  6.7 4.4 %copy-start = (bf16[192,512]{1,0:T(8,128)(2,1)S(1)}, bf16[192,512]{1,0:T(8,128)(2,1)}, u32[]{:S(2)}) copy-start(bf16[192,512]{1,0:T(8,128)(2,1)} %get-tuple-element.103.own) | copy-start | bytes 589828
  6.7 4.4 %copy-start.2 = (s32[2]{0:T(128)S(1)}, s32[2]{0:T(128)}, u32[]{:S(2)}) copy-start(s32[2]{0:T(128)} %get-tuple-element.102.kinds.bucket_ref) | copy-start | bytes 28
  6.7 11.6 %slice-start.3 = ((s8[4718592]{0:T(1024)(128)(4,1)}), s8[524288]{0:T(1024)(128)(4,1)S(1)}, s32[]{:S(2)}) async-start(s8[4718592]{0:T(1024)(128)(4,1)} %bitcast.24), calls=%async_computation.3 | async-start | bytes 1048576
  7.3 11.1 %copy-start.3 = (bf16[512,512]{1,0:T(8,128)(2,1)S(1)}, bf16[512,512]{1,0:T(8,128)(2,1)}, u32[]{:S(2)}) copy-start(bf16[512,512]{1,0:T(8,128)(2,1)} %wq.1) | copy-start | bytes 1572868
  7.3 11.0 %copy-start.4 = (bf16[512,512]{1,0:T(8,128)(2,1)S(1)}, bf16[512,512]{1,0:T(8,128)(2,1)}, u32[]{:S(2)}) copy-start(bf16[512,512]{1,0:T(8,128)(2,1)} %wk.1) | copy-start | bytes 1572868
  7.3 11.0 %copy-start.5 = (bf16[512,512]{1,0:T(8,128)(2,1)S(1)}, bf16[512,512]{1,0:T(8,128)(2,1)}, u32[]{:S(2)}) copy-start(bf16[512,512]{1,0:T(8,128)(2,1)} %wv.1) | copy-start | bytes 1572868
  7.3 11.0 %copy-start.6 = (bf16[512,512]{1,0:T(8,128)(2,1)S(1)}, bf16[512,512]{1,0:T(8,128)(2,1)}, u32[]{:S(2)}) copy-start(bf16[512,512]{1,0:T(8,128)(2,1)} %wp.3) | copy-start | bytes 1572868
  7.3 11.0 %collective-permute-start.3 = (bf16[192,512]{1,0:T(8,128)(2,1)S(1)}, bf16[192,512]{1,0:T(8,128)(2,1)S(1)}, u32[]{:S(2)}, u32[]{:S(2)}) collective-permute-start(bf16[192,512]{1,0:T(8,128)(2,1)S(1)} %get-tuple-element.109.own), channel_id=1, source_target_pairs={{0,1},{1,0},{2,3},{3,2},{4,5},{5,4},{6,7},{7,6},{8,9},{9,8},{10,11... | collective-permute-start | bytes 589832 | tf_op jit(solution)/shard_map/ppermute | solution.py:635
  7.9 10.4 %collective-permute-start.4 = (bf16[160,512]{1,0:T(8,128)(2,1)S(1)}, bf16[160,512]{1,0:T(8,128)(2,1)S(1)}, u32[]{:S(2)}, u32[]{:S(2)}) collective-permute-start(bf16[160,512]{1,0:T(8,128)(2,1)S(1)} %get-tuple-element.110), channel_id=1, source_target_pairs={{0,2},{1,3},{2,0},{3,1},{4,6},{5,7},{6,4},{7,5},{8,10},{9,11},{10,... | collective-permute-start | bytes 491528 | tf_op jit(solution)/shard_map/ppermute | solution.py:638
  8.0 10.3 %collective-permute-start.5 = (bf16[160,512]{1,0:T(8,128)(2,1)S(1)}, bf16[160,512]{1,0:T(8,128)(2,1)S(1)}, u32[]{:S(2)}, u32[]{:S(2)}) collective-permute-start(bf16[160,512]{1,0:T(8,128)(2,1)S(1)} %get-tuple-element.110), channel_id=1, source_target_pairs={{0,3},{1,2},{2,1},{3,0},{4,7},{5,6},{6,5},{7,4},{8,11},{9,10},{10,... | collective-permute-start | bytes 491528 | tf_op jit(solution)/shard_map/ppermute | solution.py:671
  9.5 1.6 %collective-permute-start.2 = (bf16[128,512]{1,0:T(8,128)(2,1)S(1)}, bf16[128,512]{1,0:T(8,128)(2,1)S(1)}, u32[]{:S(2)}, u32[]{:S(2)}) collective-permute-start(bf16[128,512]{1,0:T(8,128)(2,1)S(1)} %collective-permute-done.1.received), channel_id=1, source_target_pairs={{0,1},{1,0},{2,3},{3,2},{4,5},{5,4},{6,7},{7,6},{8,9},{9,8},{10,11... | collective-permute-start | bytes 393224 | tf_op jit(solution)/shard_map/ppermute | solution.py:635
  16.4 14.6 %collective-permute-start.6 = (bf16[2,256,512]{2,1,0:T(8,128)(2,1)S(1)}, bf16[2,256,512]{2,1,0:T(8,128)(2,1)S(1)}, u32[]{:S(2)}, u32[]{:S(2)}) collective-permute-start(bf16[2,256,512]{2,1,0:T(8,128)(2,1)S(1)} %get-tuple-element.116), channel_id=1, source_target_pairs={{0,2},{1,3},{2,0},{3,1},{4,6},{5,7},{6,4},{7,5},{8,10},{9,11},{10,... | collective-permute-start | bytes 1572872 | tf_op jit(solution)/shard_map/ppermute | solution.py:638
  27.7 7.6 %collective-permute-start.8 = (bf16[512,128]{1,0:T(8,128)(2,1)S(1)}, bf16[512,128]{1,0:T(8,128)(2,1)S(1)}, u32[]{:S(2)}, u32[]{:S(2)}) collective-permute-start(bf16[512,128]{1,0:T(8,128)(2,1)S(1)} %get-tuple-element.120), channel_id=1, source_target_pairs={{0,2},{1,3},{2,0},{3,1},{4,6},{5,7},{6,4},{7,5},{8,10},{9,11},{10,... | collective-permute-start | bytes 393224 | tf_op jit(solution)/shard_map/ppermute | solution.py:638
  28.0 17.4 %collective-permute-start.9 = (bf16[8,256,128]{2,1,0:T(8,128)(2,1)S(1)}, bf16[8,256,128]{2,1,0:T(8,128)(2,1)S(1)}, u32[]{:S(2)}, u32[]{:S(2)}) collective-permute-start(bf16[8,256,128]{2,1,0:T(8,128)(2,1)S(1)} %get-tuple-element.126), channel_id=1, source_target_pairs={{0,2},{1,3},{2,0},{3,1},{4,6},{5,7},{6,4},{7,5},{8,10},{9,11},{10,... | collective-permute-start | bytes 1572872 | tf_op jit(solution)/shard_map/ppermute | solution.py:638
  31.1 4.3 %collective-permute-start.7 = (bf16[2,256,512]{2,1,0:T(8,128)(2,1)S(1)}, bf16[2,256,512]{2,1,0:T(8,128)(2,1)S(1)}, u32[]{:S(2)}, u32[]{:S(2)}) collective-permute-start(bf16[2,256,512]{2,1,0:T(8,128)(2,1)S(1)} %collective-permute-done.6.half_t), channel_id=1, source_target_pairs={{0,1},{1,0},{2,3},{3,2},{4,5},{5,4},{6,7},{7,6},{8,9},{9,8},{10,11... | collective-permute-start | bytes 1572872 | tf_op jit(solution)/shard_map/ppermute | solution.py:635
  38.5 16.4 %collective-permute-start.11 = (bf16[4,576,128]{2,1,0:T(8,128)(2,1)S(1)}, bf16[4,576,128]{2,1,0:T(8,128)(2,1)S(1)}, u32[]{:S(2)}, u32[]{:S(2)}) collective-permute-start(bf16[4,576,128]{2,1,0:T(8,128)(2,1)S(1)} %get-tuple-element.124), channel_id=1, source_target_pairs={{0,4},{4,0},{8,12},{12,8},{16,20},{20,16},{24,28},{28,24},{1,5},{5... | collective-permute-start | bytes 1769480 | tf_op jit(solution)/shard_map/ppermute | solution.py:641
  40.5 9.5 %collective-permute-start.10 = (bf16[512,128]{1,0:T(8,128)(2,1)S(1)}, bf16[512,128]{1,0:T(8,128)(2,1)S(1)}, u32[]{:S(2)}, u32[]{:S(2)}) collective-permute-start(bf16[512,128]{1,0:T(8,128)(2,1)S(1)} %get-tuple-element.132), channel_id=1, source_target_pairs={{0,2},{1,3},{2,0},{3,1},{4,6},{5,7},{6,4},{7,5},{8,10},{9,11},{10,... | collective-permute-start | bytes 393224 | tf_op jit(solution)/shard_map/ppermute | solution.py:638
  45.6 9.5 %collective-permute-start.18 = (bf16[2,256,128]{2,1,0:T(8,128)(2,1)S(1)}, bf16[2,256,128]{2,1,0:T(8,128)(2,1)S(1)}, u32[]{:S(2)}, u32[]{:S(2)}) collective-permute-start(bf16[2,256,128]{2,1,0:T(8,128)(2,1)S(1)} %get-tuple-element.130), channel_id=1, source_target_pairs={{0,24},{4,28},{8,16},{12,20},{16,8},{20,12},{24,0},{28,4},{1,25},{... | collective-permute-start | bytes 393224 | tf_op jit(solution)/shard_map/ppermute | solution.py:641
  49.1 10.2 %collective-permute-start.17 = (bf16[2,256,128]{2,1,0:T(8,128)(2,1)S(1)}, bf16[2,256,128]{2,1,0:T(8,128)(2,1)S(1)}, u32[]{:S(2)}, u32[]{:S(2)}) collective-permute-start(bf16[2,256,128]{2,1,0:T(8,128)(2,1)S(1)} %get-tuple-element.129), channel_id=1, source_target_pairs={{0,16},{4,20},{8,24},{12,28},{16,0},{20,4},{24,8},{28,12},{1,17},{... | collective-permute-start | bytes 393224 | tf_op jit(solution)/shard_map/ppermute | solution.py:641
  49.1 10.2 %collective-permute-start.16 = (bf16[2,256,128]{2,1,0:T(8,128)(2,1)S(1)}, bf16[2,256,128]{2,1,0:T(8,128)(2,1)S(1)}, u32[]{:S(2)}, u32[]{:S(2)}) collective-permute-start(bf16[2,256,128]{2,1,0:T(8,128)(2,1)S(1)} %get-tuple-element.128), channel_id=1, source_target_pairs={{0,8},{4,12},{8,0},{12,4},{16,24},{20,28},{24,16},{28,20},{1,9},{5... | collective-permute-start | bytes 393224 | tf_op jit(solution)/shard_map/ppermute | solution.py:641
  53.1 21.3 %collective-permute-start.20 = (bf16[4,576,128]{2,1,0:T(8,128)(2,1)S(1)}, bf16[4,576,128]{2,1,0:T(8,128)(2,1)S(1)}, u32[]{:S(2)}, u32[]{:S(2)}) collective-permute-start(bf16[4,576,128]{2,1,0:T(8,128)(2,1)S(1)} %get-tuple-element.133), channel_id=1, source_target_pairs={{0,4},{4,0},{8,12},{12,8},{16,20},{20,16},{24,28},{28,24},{1,5},{5... | collective-permute-start | bytes 1769480 | tf_op jit(solution)/shard_map/ppermute | solution.py:641
  59.4 11.0 %collective-permute-start.19 = (bf16[256,128]{1,0:T(8,128)(2,1)S(1)}, bf16[256,128]{1,0:T(8,128)(2,1)S(1)}, u32[]{:S(2)}, u32[]{:S(2)}) collective-permute-start(bf16[256,128]{1,0:T(8,128)(2,1)S(1)} %get-tuple-element.153), channel_id=1, source_target_pairs={{0,4},{4,0},{8,12},{12,8},{16,20},{20,16},{24,28},{28,24},{1,5},{5... | collective-permute-start | bytes 196616 | tf_op jit(solution)/shard_map/ppermute | solution.py:641
  61.0 10.6 %collective-permute-start.13 = (bf16[1,576,128]{2,1,0:T(8,128)(2,1)S(1)}, bf16[1,576,128]{2,1,0:T(8,128)(2,1)S(1)}, u32[]{:S(2)}, u32[]{:S(2)}) collective-permute-start(bf16[1,576,128]{2,1,0:T(8,128)(2,1)S(1)} %get-tuple-element.136), channel_id=1, source_target_pairs={{0,8},{4,12},{8,0},{12,4},{16,24},{20,28},{24,16},{28,20},{1,9},{5... | collective-permute-start | bytes 442376 | tf_op jit(solution)/shard_map/ppermute | solution.py:641
  61.0 13.3 %collective-permute-start.14 = (bf16[1,576,128]{2,1,0:T(8,128)(2,1)S(1)}, bf16[1,576,128]{2,1,0:T(8,128)(2,1)S(1)}, u32[]{:S(2)}, u32[]{:S(2)}) collective-permute-start(bf16[1,576,128]{2,1,0:T(8,128)(2,1)S(1)} %get-tuple-element.137), channel_id=1, source_target_pairs={{0,16},{4,20},{8,24},{12,28},{16,0},{20,4},{24,8},{28,12},{1,17},{... | collective-permute-start | bytes 442376 | tf_op jit(solution)/shard_map/ppermute | solution.py:641
  64.0 10.3 %collective-permute-start.15 = (bf16[1,576,128]{2,1,0:T(8,128)(2,1)S(1)}, bf16[1,576,128]{2,1,0:T(8,128)(2,1)S(1)}, u32[]{:S(2)}, u32[]{:S(2)}) collective-permute-start(bf16[1,576,128]{2,1,0:T(8,128)(2,1)S(1)} %get-tuple-element.138), channel_id=1, source_target_pairs={{0,24},{4,28},{8,16},{12,20},{16,8},{20,12},{24,0},{28,4},{1,25},{... | collective-permute-start | bytes 442376 | tf_op jit(solution)/shard_map/ppermute | solution.py:641
  70.4 10.4 %collective-permute-start.12 = (bf16[2,128,512]{2,1,0:T(8,128)(2,1)S(1)}, bf16[2,128,512]{2,1,0:T(8,128)(2,1)S(1)}, u32[]{:S(2)}, u32[]{:S(2)}) collective-permute-start(bf16[2,128,512]{2,1,0:T(8,128)(2,1)S(1)} %get-tuple-element.147), channel_id=1, source_target_pairs={{0,2},{1,3},{2,0},{3,1},{4,6},{5,7},{6,4},{7,5},{8,10},{9,11},{10,... | collective-permute-start | bytes 786440 | tf_op jit(solution)/shard_map/ppermute | solution.py:638
  71.6 3.7 %collective-permute-start.21 = (bf16[4,16,128]{2,1,0:T(8,128)(2,1)S(1)}, bf16[4,16,128]{2,1,0:T(8,128)(2,1)S(1)}, u32[]{:S(2)}, u32[]{:S(2)}) collective-permute-start(bf16[4,16,128]{2,1,0:T(8,128)(2,1)S(1)} %get-tuple-element.156), channel_id=1, source_target_pairs={{0,4},{4,0},{8,12},{12,8},{16,20},{20,16},{24,28},{28,24},{1,5},{5... | collective-permute-start | bytes 49160 | tf_op jit(solution)/shard_map/ppermute | solution.py:641
  75.5 8.4 %collective-permute-start.22 = (bf16[1,592,128]{2,1,0:T(8,128)(2,1)S(1)}, bf16[1,592,128]{2,1,0:T(8,128)(2,1)S(1)}, u32[]{:S(2)}, u32[]{:S(2)}) collective-permute-start(bf16[1,592,128]{2,1,0:T(8,128)(2,1)S(1)} %get-tuple-element.158), channel_id=1, source_target_pairs={{0,8},{4,12},{8,0},{12,4},{16,24},{20,28},{24,16},{28,20},{1,9},{5... | collective-permute-start | bytes 454664 | tf_op jit(solution)/shard_map/ppermute | solution.py:641
  76.9 12.1 %collective-permute-start.23 = (bf16[1,592,128]{2,1,0:T(8,128)(2,1)S(1)}, bf16[1,592,128]{2,1,0:T(8,128)(2,1)S(1)}, u32[]{:S(2)}, u32[]{:S(2)}) collective-permute-start(bf16[1,592,128]{2,1,0:T(8,128)(2,1)S(1)} %get-tuple-element.159), channel_id=1, source_target_pairs={{0,16},{4,20},{8,24},{12,28},{16,0},{20,4},{24,8},{28,12},{1,17},{... | collective-permute-start | bytes 454664 | tf_op jit(solution)/shard_map/ppermute | solution.py:641
  78.6 10.4 %collective-permute-start.24 = (bf16[1,592,128]{2,1,0:T(8,128)(2,1)S(1)}, bf16[1,592,128]{2,1,0:T(8,128)(2,1)S(1)}, u32[]{:S(2)}, u32[]{:S(2)}) collective-permute-start(bf16[1,592,128]{2,1,0:T(8,128)(2,1)S(1)} %get-tuple-element.160), channel_id=1, source_target_pairs={{0,24},{4,28},{8,16},{12,20},{16,8},{20,12},{24,0},{28,4},{1,25},{... | collective-permute-start | bytes 454664 | tf_op jit(solution)/shard_map/ppermute | solution.py:641
  79.9 10.3 %collective-permute-start.25 = (bf16[832,128]{1,0:T(8,128)(2,1)S(1)}, bf16[832,128]{1,0:T(8,128)(2,1)S(1)}, u32[]{:S(2)}, u32[]{:S(2)}) collective-permute-start(bf16[832,128]{1,0:T(8,128)(2,1)S(1)} %sumb.1.own_ref), channel_id=1, source_target_pairs={{0,2},{1,3},{2,0},{3,1},{4,6},{5,7},{6,4},{7,5},{8,10},{9,11},{10,... | collective-permute-start | bytes 638984 | tf_op jit(solution)/shard_map/ppermute | solution.py:638
  89.1 5.3 %collective-permute-start.28 = (bf16[592,128]{1,0:T(8,128)(2,1)S(1)}, bf16[592,128]{1,0:T(8,128)(2,1)S(1)}, u32[]{:S(2)}, u32[]{:S(2)}) collective-permute-start(bf16[592,128]{1,0:T(8,128)(2,1)S(1)} %sumc.1.own_ref), channel_id=1, source_target_pairs={{0,2},{1,3},{2,0},{3,1},{4,6},{5,7},{6,4},{7,5},{8,10},{9,11},{10,... | collective-permute-start | bytes 454664 | tf_op jit(solution)/shard_map/ppermute | solution.py:638
  90.3 4.1 %collective-permute-start.26 = (bf16[832,128]{1,0:T(8,128)(2,1)S(1)}, bf16[832,128]{1,0:T(8,128)(2,1)S(1)}, u32[]{:S(2)}, u32[]{:S(2)}) collective-permute-start(bf16[832,128]{1,0:T(8,128)(2,1)S(1)} %sumb.1.own_ref), channel_id=1, source_target_pairs={{0,1},{1,0},{2,3},{3,2},{4,5},{5,4},{6,7},{7,6},{8,9},{9,8},{10,11... | collective-permute-start | bytes 638984 | tf_op jit(solution)/shard_map/ppermute | solution.py:635
  90.3 4.0 %collective-permute-start.27 = (bf16[832,128]{1,0:T(8,128)(2,1)S(1)}, bf16[832,128]{1,0:T(8,128)(2,1)S(1)}, u32[]{:S(2)}, u32[]{:S(2)}) collective-permute-start(bf16[832,128]{1,0:T(8,128)(2,1)S(1)} %collective-permute-done.25.far_ref), channel_id=1, source_target_pairs={{0,1},{1,0},{2,3},{3,2},{4,5},{5,4},{6,7},{7,6},{8,9},{9,8},{10,11... | collective-permute-start | bytes 638984 | tf_op jit(solution)/shard_map/ppermute | solution.py:635
  90.8 4.8 %collective-permute-start.29 = (bf16[592,128]{1,0:T(8,128)(2,1)S(1)}, bf16[592,128]{1,0:T(8,128)(2,1)S(1)}, u32[]{:S(2)}, u32[]{:S(2)}) collective-permute-start(bf16[592,128]{1,0:T(8,128)(2,1)S(1)} %sumc.1.own_ref), channel_id=1, source_target_pairs={{0,1},{1,0},{2,3},{3,2},{4,5},{5,4},{6,7},{7,6},{8,9},{9,8},{10,11... | collective-permute-start | bytes 454664 | tf_op jit(solution)/shard_map/ppermute | solution.py:635
  94.3 1.4 %collective-permute-start.30 = (bf16[592,128]{1,0:T(8,128)(2,1)S(1)}, bf16[592,128]{1,0:T(8,128)(2,1)S(1)}, u32[]{:S(2)}, u32[]{:S(2)}) collective-permute-start(bf16[592,128]{1,0:T(8,128)(2,1)S(1)} %collective-permute-done.28.far_ref), channel_id=1, source_target_pairs={{0,1},{1,0},{2,3},{3,2},{4,5},{5,4},{6,7},{7,6},{8,9},{9,8},{10,11... | collective-permute-start | bytes 454664 | tf_op jit(solution)/shard_map/ppermute | solution.py:635

commit v6 on v5

--- a/solution.py
+++ b/solution.py
@@ -21,7 +21,7 @@
 HB = pl.BlockSpec(memory_space=pltpu.HBM)
 RATE = 1 << 30
 LENGTH = {
-    "pack": 10, "stack": 10, "first": 0.02, "second": 30, "third": 20, "fourth": 10, "weight2": 1, "weight1": 3,
+    "pack": 10, "stack": 10, "first": 0.02, "second": 30, "third": 20, "fourth": 10, "weight2": 1, "weight1": 0.02, "routeb1": 20, "unpack": 5,
 }
 
 
@@ -378,14 +378,15 @@
 
     sum_ref[:, 0 : 6 * BLK] = mm_tn(normed, jnp.concatenate(blocks(0) + blocks(1) + blocks(2), axis=1))
     sum_ref[:, 6 * BLK : 8 * BLK] = mm_tn(mixed, jnp.concatenate(blocks(3), axis=1))
-    shards = attn_keep.shape[0]
-    rows = channels // shards
-    for shard in range(shards):
-        part = sum_ref[shard * rows : (shard + 1) * rows, :].astype(BF16)
-        for index in range(4):
-            at = index * 2 * BLK
-            attn_keep[shard, index * rows : (index + 1) * rows, :] = part[:, at : at + BLK]
-            attn_send[shard, index * rows : (index + 1) * rows, :] = part[:, at + BLK : at + 2 * BLK]
+    mine = lax.axis_index("batch") & 1
+    pairs = attn_keep.shape[0]
+    rows = channels // (2 * pairs)
+    for pair in range(pairs):
+        for dst, which in ((attn_keep, mine), (attn_send, 1 - mine)):
+            part = sum_ref[pl.ds(pl.multiple_of((2 * pair + which) * rows, 8), rows), :].astype(BF16)
+            for index in range(4):
+                at = index * 2 * BLK
+                dst[pair, index * rows : (index + 1) * rows, :] = part[:, at : at + 2 * BLK]
 
 
 def third_kernel(
@@ -420,7 +421,7 @@
 def fourth_kernel(
     bucket_ref, grad1_ref, image_ref, stats_ref, grad_middle_ref, middle_ref, mixed_ref, vecs,
     weight1, wp, vec_a, vec_b,
-    out_own, grad_own, send_ref, vec_keep, vec_send,
+    out_own, grad_own, send_ref, vec_out,
     shift_ref, acc_ref, full_ref, vec_ref,
 ):
     h, home, away = place(bucket_ref)
@@ -447,24 +448,21 @@
     vec_ref[9:10, :] = gain_grad
     vec_ref[10:11, :] = shift_grad
     vec_ref[11:VECS, :] = jnp.zeros((VECS - 11, channels), F32)
-    pairs = vec_keep.shape[0]
-    rows = channels // (2 * pairs)
-    mine = (lax.axis_index("batch") & 1) == 1
-    for pair in range(pairs):
-        parts = []
-        for shard in (2 * pair, 2 * pair + 1):
-            start = shard * rows
-            tile = start // BLK * BLK
-            part = vec_ref[:, tile : tile + BLK]
-            parts.append(part if start == tile else pltpu.roll(part, BLK - (start - tile), 1))
-        vec_keep[pair] = jnp.where(mine, parts[1], parts[0]).astype(BF16)
-        vec_send[pair] = jnp.where(mine, parts[0], parts[1]).astype(BF16)
+    shards = vec_out.shape[0]
+    rows = channels // shards
+    for shard in range(shards):
+        start = shard * rows
+        tile = start // BLK * BLK
+        part = vec_ref[:, tile : tile + BLK]
+        vec_out[shard] = part if start == tile else pltpu.roll(part, BLK - (start - tile), 1)
 
 
 def weight_kernel(
     bucket_ref, act_t, half_t, partner_half_t, block_own, block_away,
-    keep_ref, send_ref, left_ref, right_ref, shift_ref, sum_ref, *, layer,
+    *rest, layer,
 ):
+    vec_ref = rest[0] if len(rest) == 7 else None
+    keep_ref, send_ref, left_ref, right_ref, shift_ref, sum_ref = rest[-6:]
     h, home, away = place(bucket_ref)
     channels = act_t.shape[0]
     half = channels // 2
@@ -491,10 +489,12 @@
     for pair in range(pairs):
         for dst, which in ((keep_ref, mine), (send_ref, 1 - mine)):
             shard = 2 * pair + which
-            dst[pair] = sum_ref[pl.ds(pl.multiple_of(shard * rows, 8), rows), :].astype(BF16)
-
-
-def route_kernel(*refs, bit, ways, low):
+            dst[pair, 0:rows, :] = sum_ref[pl.ds(pl.multiple_of(shard * rows, 8), rows), :].astype(BF16)
+            if vec_ref is not None:
+                dst[pair, rows : rows + VECS, :] = vec_ref[shard].astype(BF16)
+
+
+def route_kernel(*refs, bit, ways):
     group = (lax.axis_index("batch") >> bit) & (ways - 1)
     ins, outs = refs[: len(refs) - ways], refs[len(refs) - ways :]
     first = 0
@@ -503,7 +503,7 @@
         for step, dst in enumerate(outs):
             which = group ^ step
             for index in range(dst.shape[0]):
-                at = (index // low * ways + which) * low + index % low
+                at = index * ways + which
                 dst[index, first : first + rows, :] = (
                     keep_ref[at].astype(F32) + got_ref[at].astype(F32)
                 ).astype(BF16)
@@ -517,18 +517,8 @@
     return added
 
 
-def half_kernel(*refs):
-    mine = lax.axis_index("batch") & 1
-    for dst, which in zip(refs[-2:], (mine, 1 - mine)):
-        dst[...] = total_of([ref[which] for ref in refs[:-2]]).astype(BF16)
-
-
-def sum_kernel(*refs, count):
-    out_ref = refs[-1]
-    rows = refs[0].shape[1]
-    out_ref[0:rows, :] = total_of([ref[0] for ref in refs[:count]]).astype(BF16)
-    if count < len(refs) - 1:
-        out_ref[rows:, :] = total_of([ref[...] for ref in refs[count:-1]]).astype(BF16)
+def sum_kernel(*refs):
+    refs[-1][...] = total_of([ref[0] for ref in refs[:-1]]).astype(BF16)
 
 
 def join_kernel(own_ref, far_ref, near_ref, diagonal_ref, *out_refs):
@@ -545,6 +535,20 @@
         sums = 0.5 * ((own + near) + (far + diagonal))
         for index, dst in enumerate([ref for ref in out_refs if ref.shape[0] == 1]):
             dst[...] = sums[index : index + 1, 0 : dst.shape[1]]
+
+
+def join_attn_kernel(own_ref, far_ref, near_ref, diagonal_ref, *out_refs):
+    h = lax.axis_index("height")
+    rows = out_refs[0].shape[0]
+    for first, second, index in ((own_ref, far_ref, h), (near_ref, diagonal_ref, h ^ 1)):
+        for position in range(2):
+            lane, other = position * BLK, (1 - position) * BLK
+            column = pl.multiple_of(BLK * (index ^ (2 * position)), BLK)
+            for number, dst in enumerate(out_refs):
+                at = number * rows
+                dst[:, pl.ds(column, BLK)] = first[at : at + rows, lane : lane + BLK].astype(
+                    F32
+                ) + second[at : at + rows, other : other + BLK].astype(F32)
 
 
 def unpack_kernel(bucket_ref, out_own, grad_own, away_ref, out_ref, grad_ref):
@@ -680,7 +684,7 @@
     half_t = to_chip(send_t)
     core_half_t = to_core(half_t)
 
-    attn_out = ((batches, 4 * small_rows, BLK), BF16)
+    attn_out = ((batches // 2, 4 * small_rows, 2 * BLK), BF16)
     middle, mixed, grad2, grad_middle, attn_keep, attn_send, vec_a, block2, block2_send = call(
         second_kernel, "second",
         [img32, img16, img16, img32, attn_out, attn_out, rows8, block, block],
@@ -689,7 +693,7 @@
         conv2_weight, query_weight, key_weight, value_weight, proj_weight,
     )
     block2_away = to_chip(block2_send)
-    attn_got = to_chip(attn_send)
+    attn_got = to_batch(attn_send, 1)
 
     grad1, block1, block1_send, vec_b = call(
         third_kernel, "third",
@@ -699,85 +703,78 @@
     )
     block1_away = to_chip(block1_send)
 
-    def weight_grad(name, act_t, index, own, away):
+    def weight_grad(name, act_t, index, own, away, *vec):
+        rows = shard_rows + (VECS if vec else 0)
         return call(
             functools.partial(weight_kernel, layer=index), name,
-            [((batches // 2, shard_rows, BLK), BF16)] * 2,
+            [((batches // 2, rows, BLK), BF16)] * 2,
             [((C, 2 * PIX), BF16), ((2 * PIX, 9 * BLK), BF16), ((3, PIX + 2 * PAD, BLK), BF16),
              ((9 * C, BLK), F32)],
-            18, kinds, act_t, half_t, core_half_t, own, away,
+            18, kinds, act_t, half_t, core_half_t, own, away, *vec,
         )
 
     keep2, send2 = weight_grad("weight2", act2_t, 1, after(block2, block1), block2_away)
     got2 = to_batch(send2, 1)
 
-    def spread(name, bit, low, *pairs):
+    def spread(name, bit, *pairs, behind=()):
         ways = 1 << min(2, bits - bit)
-        count = pairs[0].shape[0] // ways
-        rows = sum(v.shape[1] for v in pairs[::2])
+        shape = (pairs[0].shape[0] // ways, sum(v.shape[1] for v in pairs[::2]), pairs[0].shape[2])
         parts = call(
-            functools.partial(route_kernel, bit=bit, ways=ways, low=low), name + str(bit),
-            [((count, rows, BLK), BF16)] * ways, [], 16, *pairs, smem=0,
+            functools.partial(route_kernel, bit=bit, ways=ways), name + str(bit),
+            [(shape, BF16)] * ways, [], 16, *pairs, smem=0,
         )
-        return parts, [to_batch(parts[j], j << bit) for j in range(1, ways)]
-
-    def rest(name, low, parts, got):
+        return parts, [to_batch(after(parts[j], *behind), j << bit) for j in range(1, ways)]
+
+    def finish(name, parts, got):
         for bit in range(3, bits, 2):
             added = total_of([parts[0]] + got).astype(BF16)
-            parts, got = spread(name, bit, low, added, jnp.zeros_like(added))
-        return [parts[0]] + got
-
-    def finish(name, arrays, *others):
-        rows = arrays[0].shape[1] + (others[0].shape[0] if others else 0)
+            parts, got = spread(name, bit, added, jnp.zeros_like(added))
         return call(
-            functools.partial(sum_kernel, count=len(arrays)), name, [((rows, BLK), BF16)], [], 8,
-            *arrays, *others, smem=0,
+            sum_kernel, "sum" + name, [(parts[0].shape[1:], BF16)], [], 8, parts[0], *got, smem=0
         )[0]
 
-    def gather(shard):
+    def gather(shard, *between):
         far = to_chip(shard)
         near = to_core(shard)
-        return shard, far, near, to_core(far)
-
-    parts_a, got_a = spread("routea", 1, 2, after(attn_keep, send2), attn_got)
-    keep1, send1 = weight_grad("weight1", act1_t, 0, after(block1, *parts_a), block1_away)
+        return shard, far, near, to_core(after(far, *between))
+
+    parts_a, got_a = spread("routea", 1, after(attn_keep, send2), attn_got)
+    out_own, grad_own, image_send, vec_c = call(
+        fourth_kernel, "fourth",
+        [((192, C), BF16), ((192, C), BF16), ((2, 128, C), BF16), ((batches, VECS, BLK), F32)],
+        [shifts, img32, img16, ((VECS, C), F32)], 14,
+        kinds, after(grad1, *parts_a), image, stats, grad_middle, middle, mixed, vecs,
+        conv1_weight, proj_weight, vec_a, vec_b,
+    )
+    image_away = to_chip(image_send)
+    keep1, send1 = weight_grad("weight1", act1_t, 0, block1, block1_away, vec_c)
     got1 = to_batch(send1, 1)
-    parts_b, got_b = spread("routeb", 1, 1, after(keep2, send1), got2)
-
-    out_own, grad_own, image_send, vec_keep, vec_send = call(
-        fourth_kernel, "fourth",
-        [((192, C), BF16), ((192, C), BF16), ((2, 128, C), BF16),
-         ((batches // 2, VECS, BLK), BF16), ((batches // 2, VECS, BLK), BF16)],
-        [shifts, img32, img16, ((VECS, C), F32)], 14,
-        kinds, after(grad1, *parts_b), image, stats, grad_middle, middle, mixed, vecs,
-        conv1_weight, proj_weight, vec_a, vec_b,
-    )
-    image_away = to_chip(image_send)
-    vec_got = to_batch(vec_send, 1)
-
-    attn_mine, attn_other = call(
-        half_kernel, "halfa", [((4 * small_rows, BLK), BF16)] * 2, [], 8,
-        *rest("routea", 2, parts_a, [after(g, parts_b[0]) for g in got_a]), smem=0,
-    )
-    attn_far = to_batch(attn_other, 1)
-    shard_b = finish("sumb", rest("routeb", 1, parts_b, got_b), attn_mine, attn_far)
-    parts_c, got_c = spread("routec", 1, 1, after(keep1, shard_b), got1, vec_keep, vec_got)
-    shard_b = after(shard_b, *parts_c)
-    gathered_b = gather(shard_b)
+    shard_a = finish("routea", parts_a, [after(g, vec_c) for g in got_a])
+    parts_b, got_b = spread("routeb", 1, after(keep2, send1, shard_a), got2)
+    gathered_a = gather(shard_a)
     outputs, input_grad = call(
         unpack_kernel, "unpack",
         [(inputs.shape, BF16)] * 2, [], 8,
-        kinds, out_own, grad_own, after(image_away, *parts_c),
-    )
-    shard_c = finish("sumc", rest("routec", 1, parts_c, got_c))
-    whole2, *small = call(
-        join_kernel, "joinb", [((shard_rows, C), F32)] + [((small_rows, C), F32)] * 4, [], 8,
+        kinds, out_own, grad_own, after(image_away, parts_b[0]),
+    )
+    parts_c, got_c = spread("routec", 1, after(keep1, outputs), got1, behind=got_b)
+    shard_b = finish("routeb", parts_b, [after(g, parts_c[0]) for g in got_b])
+    gathered_b = gather(shard_b)
+    shard_c = finish(
+        "routec", parts_c, [after(g, gathered_b[1], gathered_a[1]) for g in got_c]
+    )
+    small = call(
+        join_attn_kernel, "joina", [((small_rows, C), F32)] * 4, [], 8,
+        after(gathered_a[0], shard_c), *gathered_a[1:], smem=0,
+    )
+    (whole2,) = call(
+        join_kernel, "joinb", [((shard_rows, C), F32)], [], 8,
         after(gathered_b[0], shard_c), *gathered_b[1:], smem=0,
     )
-    gathered_c = gather(after(shard_c, outputs))
+    gathered_c = gather(shard_c, whole2, *small)
     whole1, *sums = call(
         join_kernel, "joinc", [((shard_rows, C), F32)] + [((1, small_rows), F32)] * 11, [], 8,
-        after(gathered_c[0], whole2), *gathered_c[1:], smem=0,
+        *gathered_c, smem=0,
     )
     v = [row.reshape(small_rows) for row in sums]
 

time: 98 us -> 97 us (0.990)
  starting transfers between devices: 33.8 us -> 32.4 us
  Pallas kernels: 37.4 us -> 38.6 us
    ppermute x8 -> x10, waiting for transfers between devices: 1.07 us -> 3.21 us  [to_core(): return lax.ppermute(v, 'height', [(i, i ^ 1) for i in range(4)])]
    ppermute x13 -> x12, waiting for transfers between devices: 14.4 us -> 12.3 us  [to_batch(): return lax.ppermute(v, 'batch', [(i, i ^ change) for i in range(batches)])]
    ppermute x13 -> x12, starting transfers between devices: 18.8 us -> 17.4 us  [to_batch(): return lax.ppermute(v, 'batch', [(i, i ^ change) for i in range(batches)])]
    pallas_call x17 -> x18, Pallas kernels: 37.4 us -> 38.6 us  [call(): pl.pallas_call(kernel, name=name, out_shape=[jax.ShapeDtypeStruct(shape,...]
    ppermute x8 -> x10, starting transfers between devices: 1.67 us -> 2.44 us  [to_core(): return lax.ppermute(v, 'height', [(i, i ^ 1) for i in range(4)])]
  transfers between devices with their start and end apart: 31 -> 32, of which waited for: 12 -> 11; matrix products, arithmetic and copies ran while one was open for 0% -> 0% of each run, Pallas kernels for 35% -> 37%
where the time goes in v6:
time: 97 us; the launch traced here: 96.8 us
  Pallas kernels  38.6 us (40%)
  starting transfers between devices  32.4 us (33%)
  waiting for transfers between devices  23.7 us (24%)
  between operations  1.28 us (1%)
    pallas_call x18, Pallas kernels, call(): pl.pallas_call(kernel, name=name, out_shape=[jax.ShapeDtypeStruct(shape,...  38.6 us
    ppermute x12, starting transfers between devices, to_batch(): return lax.ppermute(v, 'batch', [(i, i ^ change) for i in range(batches)])  17.4 us
    ppermute x12, waiting for transfers between devices, to_batch(): return lax.ppermute(v, 'batch', [(i, i ^ change) for i in range(batches)])  12.3 us
    ppermute x9, starting transfers between devices, to_chip(): return lax.ppermute(v, 'height', [(i, i ^ 2) for i in range(4)])  11.2 us
    ppermute x9, waiting for transfers between devices, to_chip(): return lax.ppermute(v, 'height', [(i, i ^ 2) for i in range(4)])  8.14 us
    ppermute x10, waiting for transfers between devices, to_core(): return lax.ppermute(v, 'height', [(i, i ^ 1) for i in range(4)])  3.21 us
    ppermute x10, starting transfers between devices, to_core(): return lax.ppermute(v, 'height', [(i, i ^ 1) for i in range(4)])  2.44 us
  transfers between devices with their start and end apart: 32, of which 11 were waited for; matrix products, arithmetic and copies ran while one was open for 0% of the time, Pallas kernels for 37%

profile of v6, /device:TPU:0, one launch (start us, length us, event | category | flops | bytes accessed | tf_op | source)
XLA Modules:
  0.0 96.8 jit_solution(15249770978697032222)
XLA Ops:
  0.8 0.0 slice-start
  0.8 0.0 slice-start.2
  0.8 1.9 %pack.1 = (s32[2]{0:T(128)}, bf16[128,512]{1,0:T(8,128)(2,1)}, bf16[192,512]{1,0:T(8,128)(2,1)}) custom-call(s32[2]{0:T(128)} %bucket_hbm.1, bf16[2,6,32,512]{3,2,1,0:T(8,128)(2,1)} %x_hbm.1), custom_call_target="tpu_custom_call" | custom-call | flops 10737418240 | bytes 1024 | tf_op jit(solution)/shard_map/pack/pallas_call | solution.py:588
  2.7 3.0 %collective-permute-start.1 = (bf16[128,512]{1,0:T(8,128)(2,1)}, bf16[128,512]{1,0:T(8,128)(2,1)S(1)}, u32[]{:S(2)}, u32[]{:S(2)}) collective-permute-start(bf16[128,512]{1,0:T(8,128)(2,1)} %get-tuple-element.107), channel_id=1, source_target_pairs={{0,2},{1,3},{2,0},{3,1},{4,6},{5,7},{6,4},{7,5},{8,10},{9,11},{10,... | collective-permute-start | bytes 393224 | tf_op jit(solution)/shard_map/ppermute | solution.py:642
  5.9 0.0 copy-start.1
  5.9 0.8 copy-done.1
  6.7 0.6 stack.1
  7.3 0.0 copy-start.3
  7.3 0.0 copy-start.5
  7.3 0.0 copy-start.6
  7.3 0.6 collective-permute-start.3
  7.9 0.1 collective-permute-start.4
  8.0 1.4 %collective-permute-start.5 = (bf16[160,512]{1,0:T(8,128)(2,1)S(1)}, bf16[160,512]{1,0:T(8,128)(2,1)S(1)}, u32[]{:S(2)}, u32[]{:S(2)}) collective-permute-start(bf16[160,512]{1,0:T(8,128)(2,1)S(1)} %get-tuple-element.113), channel_id=1, source_target_pairs={{0,3},{1,2},{2,1},{3,0},{4,7},{5,6},{6,5},{7,4},{8,11},{9,10},{10,... | collective-permute-start | bytes 491528 | tf_op jit(solution)/shard_map/ppermute | solution.py:675
  9.3 0.1 collective-permute-done.1.received
  9.5 0.6 collective-permute-start.2
  10.1 1.0 %collective-permute-done.2.partner_received = bf16[128,512]{1,0:T(8,128)(2,1)S(1)} collective-permute-done((bf16[128,512]{1,0:T(8,128)(2,1)S(1)}, bf16[128,512]{1,0:T(8,128)(2,1)S(1)}, u32[]{:S(2)}, u32[]{:S(2)}) %collective-permute-start.2) | collective-permute-done | bytes 131104 | tf_op jit(solution)/shard_map/ppermute | solution.py:639
  11.1 5.4 %first.1 = (bf16[512,512]{1,0:T(8,128)(2,1)S(1)}, f32[512,512]{1,0:T(8,128)S(1)}, bf16[512,512]{1,0:T(8,128)(2,1)S(1)}, f32[8,512]{1,0:T(8,128)S(1)}, bf16[512,5...) custom-call(s32[2]{0:T(128)S(1)} %copy-done.2, bf16[192,512]{1,0:T(8,128)(2,1)S(1)} %copy-done, ...), custom_call_target="tpu_custom_call" | custom-call | flops 21474836 | bytes 1024 | tf_op jit(solution)/shard_map/first/pallas_call | solution.py:588
  16.4 1.9 %collective-permute-start.6 = (bf16[2,256,512]{2,1,0:T(8,128)(2,1)S(1)}, bf16[2,256,512]{2,1,0:T(8,128)(2,1)S(1)}, u32[]{:S(2)}, u32[]{:S(2)}) collective-permute-start(bf16[2,256,512]{2,1,0:T(8,128)(2,1)S(1)} %get-tuple-element.120), channel_id=1, source_target_pairs={{0,2},{1,3},{2,0},{3,1},{4,6},{5,7},{6,4},{7,5},{8,10},{9,11},{10,... | collective-permute-start | bytes 1572872 | tf_op jit(solution)/shard_map/ppermute | solution.py:642
  18.4 9.6 %second.1 = (f32[512,512]{1,0:T(8,128)S(1)}, bf16[512,512]{1,0:T(8,128)(2,1)S(1)}, bf16[512,512]{1,0:T(8,128)(2,1)S(1)}, f32[512,512]{1,0:T(8,128)S(1)}, bf16[4,...) custom-call(s32[2]{0:T(128)S(1)} %copy-done.2, ...), custom_call_target="tpu_custom_call" | custom-call | flops 32212254720 | bytes 1024 | tf_op jit(solution)/shard_map/second/pallas_call | solution.py:588
  28.0 0.3 collective-permute-start.8
  28.3 1.5 %collective-permute-start.9 = (bf16[4,256,256]{2,1,0:T(8,128)(2,1)S(1)}, bf16[4,256,256]{2,1,0:T(8,128)(2,1)S(1)}, u32[]{:S(2)}, u32[]{:S(2)}) collective-permute-start(bf16[4,256,256]{2,1,0:T(8,128)(2,1)S(1)} %get-tuple-element.127), channel_id=1, source_target_pairs={{0,4},{4,0},{8,12},{12,8},{16,20},{20,16},{24,28},{28,24},{1,5},{5... | collective-permute-start | bytes 1572872 | tf_op jit(solution)/shard_map/ppermute | solution.py:645
  29.8 1.1 %collective-permute-done.6.half_t = bf16[2,256,512]{2,1,0:T(8,128)(2,1)S(1)} collective-permute-done((bf16[2,256,512]{2,1,0:T(8,128)(2,1)S(1)}, bf16[2,256,512]{2,1,0:T(8,128)(2,1)S(1)}, u32[]{:S(2)}, u32[]{:S(2)}) %collective-permute-start.6) | collective-permute-done | bytes 524320 | tf_op jit(solution)/shard_map/ppermute | solution.py:642
  30.8 4.3 %third.1 = (bf16[512,512]{1,0:T(8,128)(2,1)S(1)}, bf16[512,128]{1,0:T(8,128)(2,1)S(1)}, bf16[512,128]{1,0:T(8,128)(2,1)S(1)}, f32[8,512]{1,0:T(8,128)S(1)}) custom-call(s32[2]{0:T(128)S(1)} %copy-done.2, bf16[512,512]{1,0:T(8,128)(2,1)S(1)} %get-tuple-element.114.grad2_ref, f32[512,512]{1,0:T(8,128)S(1)} %get-tuple-element.115.conv_ref, ...), custom_call_target="tpu_custom_call" | custom-call | flops 21474836480 | bytes 1024 | tf_op jit(solution)/shard_map/third/pallas_call | solution.py:588
  35.2 2.3 %collective-permute-start.11 = (bf16[512,128]{1,0:T(8,128)(2,1)S(1)}, bf16[512,128]{1,0:T(8,128)(2,1)S(1)}, u32[]{:S(2)}, u32[]{:S(2)}) collective-permute-start(bf16[512,128]{1,0:T(8,128)(2,1)S(1)} %get-tuple-element.143), channel_id=1, source_target_pairs={{0,2},{1,3},{2,0},{3,1},{4,6},{5,7},{6,4},{7,5},{8,10},{9,11},{10,... | collective-permute-start | bytes 393224 | tf_op jit(solution)/shard_map/ppermute | solution.py:642
  37.5 3.3 %weight2.5 = (bf16[4,576,128]{2,1,0:T(8,128)(2,1)S(1)}, bf16[4,576,128]{2,1,0:T(8,128)(2,1)S(1)}) custom-call(s32[2]{0:T(128)S(1)} %copy-done.2, bf16[512,512]{1,0:T(8,128)(2,1)S(1)} %get-tuple-element.119.act_t, bf16[2,256,512]{2,1,0:T(8,128)(2,1)S(1)} %collective-permute-done.6.half_t, bf16[2,256,512]{2,1,0:T(8,128)(2,1)S(1)} %collective-permute-done.7.partner_half_t, ...), custom_call_target="tpu_custom_call" | custom-call | flops 1073741824 | bytes 1024 | tf_op jit(solution)/shard_map/weight2/pallas_call | solution.py:588
  40.8 1.3 %collective-permute-start.15 = (bf16[4,576,128]{2,1,0:T(8,128)(2,1)S(1)}, bf16[4,576,128]{2,1,0:T(8,128)(2,1)S(1)}, u32[]{:S(2)}, u32[]{:S(2)}) collective-permute-start(bf16[4,576,128]{2,1,0:T(8,128)(2,1)S(1)} %get-tuple-element.125), channel_id=1, source_target_pairs={{0,4},{4,0},{8,12},{12,8},{16,20},{20,16},{24,28},{28,24},{1,5},{5... | collective-permute-start | bytes 1769480 | tf_op jit(solution)/shard_map/ppermute | solution.py:645
  42.1 0.1 routea1.1
  42.3 3.7 %collective-permute-start.14 = (bf16[1,256,256]{2,1,0:T(8,128)(2,1)S(1)}, bf16[1,256,256]{2,1,0:T(8,128)(2,1)S(1)}, u32[]{:S(2)}, u32[]{:S(2)}) collective-permute-start(bf16[1,256,256]{2,1,0:T(8,128)(2,1)S(1)} %get-tuple-element.131), channel_id=1, source_target_pairs={{0,24},{4,28},{8,16},{12,20},{16,8},{20,12},{24,0},{28,4},{1,25},{... | collective-permute-start | bytes 393224 | tf_op jit(solution)/shard_map/ppermute | solution.py:645
  45.9 0.8 collective-permute-start.12
  46.7 5.0 %fourth.1 = (bf16[192,512]{1,0:T(8,128)(2,1)S(1)}, bf16[192,512]{1,0:T(8,128)(2,1)S(1)}, bf16[2,128,512]{2,1,0:T(8,128)(2,1)S(1)}, f32[8,16,128]{2,1,0:T(8,128)S(1)}) custom-call(s32[2]{0:T(128)S(1)} %copy-done.2, bf16[512,512]{1,0:T(8,128)(2,1)S(1)} %get-tuple-element.132.grad1_ref, bf16[512,512]{1,0:T(8,128)(2,1)S(1)} %get-tuple-element.110.image_ref, ...), custom_call_target="tpu_custom_call" | custom-call | flops 10737418240 | bytes 1024 | tf_op jit(solution)/shard_map/fourth/pallas_call | solution.py:588
  51.7 1.4 %collective-permute-start.10 = (bf16[2,128,512]{2,1,0:T(8,128)(2,1)S(1)}, bf16[2,128,512]{2,1,0:T(8,128)(2,1)S(1)}, u32[]{:S(2)}, u32[]{:S(2)}) collective-permute-start(bf16[2,128,512]{2,1,0:T(8,128)(2,1)S(1)} %get-tuple-element.140), channel_id=1, source_target_pairs={{0,2},{1,3},{2,0},{3,1},{4,6},{5,7},{6,4},{7,5},{8,10},{9,11},{10,... | collective-permute-start | bytes 786440 | tf_op jit(solution)/shard_map/ppermute | solution.py:642
  53.2 3.1 %weight1.5 = (bf16[4,592,128]{2,1,0:T(8,128)(2,1)S(1)}, bf16[4,592,128]{2,1,0:T(8,128)(2,1)S(1)}) custom-call(s32[2]{0:T(128)S(1)} %copy-done.2, bf16[512,512]{1,0:T(8,128)(2,1)S(1)} %get-tuple-element.142.act_t, bf16[2,256,512]{2,1,0:T(8,128)(2,1)S(1)} %collective-permute-done.6.half_t, bf16[2,256,512]{2,1,0:T(8,128)(2,1)S(1)} %collective-permute-done.7.partner_half_t, ...), custom_call_target="tpu_custom_call" | custom-call | flops 21474836 | bytes 1024 | tf_op jit(solution)/shard_map/weight1/pallas_call | solution.py:588
  56.3 1.3 %collective-permute-start.16 = (bf16[4,592,128]{2,1,0:T(8,128)(2,1)S(1)}, bf16[4,592,128]{2,1,0:T(8,128)(2,1)S(1)}, u32[]{:S(2)}, u32[]{:S(2)}) collective-permute-start(bf16[4,592,128]{2,1,0:T(8,128)(2,1)S(1)} %get-tuple-element.145), channel_id=1, source_target_pairs={{0,4},{4,0},{8,12},{12,8},{16,20},{20,16},{24,28},{28,24},{1,5},{5... | collective-permute-start | bytes 1818632 | tf_op jit(solution)/shard_map/ppermute | solution.py:645
  57.6 0.1 sumroutea.1.own_ref
  57.7 0.1 routeb1.1
  57.9 1.4 %collective-permute-done.10.away_ref = bf16[2,128,512]{2,1,0:T(8,128)(2,1)S(1)} collective-permute-done((bf16[2,128,512]{2,1,0:T(8,128)(2,1)S(1)}, bf16[2,128,512]{2,1,0:T(8,128)(2,1)S(1)}, u32[]{:S(2)}, u32[]{:S(2)}) %collective-permute-start.10) | collective-permute-done | bytes 262176 | tf_op jit(solution)/shard_map/ppermute | solution.py:642
  59.3 1.4 %collective-permute-start.17 = (bf16[1,576,128]{2,1,0:T(8,128)(2,1)S(1)}, bf16[1,576,128]{2,1,0:T(8,128)(2,1)S(1)}, u32[]{:S(2)}, u32[]{:S(2)}) collective-permute-start(bf16[1,576,128]{2,1,0:T(8,128)(2,1)S(1)} %get-tuple-element.158), channel_id=1, source_target_pairs={{0,8},{4,12},{8,0},{12,4},{16,24},{20,28},{24,16},{28,20},{1,9},{5... | collective-permute-start | bytes 442376 | tf_op jit(solution)/shard_map/ppermute | solution.py:645
  60.6 2.6 %collective-permute-start.18 = (bf16[1,576,128]{2,1,0:T(8,128)(2,1)S(1)}, bf16[1,576,128]{2,1,0:T(8,128)(2,1)S(1)}, u32[]{:S(2)}, u32[]{:S(2)}) collective-permute-start(bf16[1,576,128]{2,1,0:T(8,128)(2,1)S(1)} %get-tuple-element.159), channel_id=1, source_target_pairs={{0,16},{4,20},{8,24},{12,28},{16,0},{20,4},{24,8},{28,12},{1,17},{... | collective-permute-start | bytes 442376 | tf_op jit(solution)/shard_map/ppermute | solution.py:645
  63.3 0.4 collective-permute-start.19
  63.7 1.5 %unpack.1 = (bf16[2,6,32,512]{3,2,1,0:T(8,128)(2,1)}, bf16[2,6,32,512]{3,2,1,0:T(8,128)(2,1)}) custom-call(s32[2]{0:T(128)S(1)} %copy-done.2, bf16[192,512]{1,0:T(8,128)(2,1)S(1)} %get-tuple-element.138.out_own, bf16[192,512]{1,0:T(8,128)(2,1)S(1)} %get-tuple-element.139.grad_own, bf16[2,128,512]{2,1,0:T(8,128)(2,1)S(1)} %collective-permute-done.10.away_ref), custom_call_target="tpu_custom_call" | custom-call | flops 5368709120 | bytes 1024 | tf_op jit(solution)/shard_map/unpack/pallas_call | solution.py:588
  65.2 4.7 %collective-permute-done.16.refs_1_ = bf16[4,592,128]{2,1,0:T(8,128)(2,1)S(1)} collective-permute-done((bf16[4,592,128]{2,1,0:T(8,128)(2,1)S(1)}, bf16[4,592,128]{2,1,0:T(8,128)(2,1)S(1)}, u32[]{:S(2)}, u32[]{:S(2)}) %collective-permute-start.16) | collective-permute-done | bytes 606240 | tf_op jit(solution)/shard_map/ppermute | solution.py:645
  69.8 0.1 routec1.1
  70.0 5.0 %collective-permute-done.18.refs_2_ = bf16[1,576,128]{2,1,0:T(8,128)(2,1)S(1)} collective-permute-done((bf16[1,576,128]{2,1,0:T(8,128)(2,1)S(1)}, bf16[1,576,128]{2,1,0:T(8,128)(2,1)S(1)}, u32[]{:S(2)}, u32[]{:S(2)}) %collective-permute-start.18) | collective-permute-done | bytes 147488 | tf_op jit(solution)/shard_map/ppermute | solution.py:645
  75.0 0.7 collective-permute-start.24
  75.8 2.9 %collective-permute-start.23 = (bf16[1,592,128]{2,1,0:T(8,128)(2,1)S(1)}, bf16[1,592,128]{2,1,0:T(8,128)(2,1)S(1)}, u32[]{:S(2)}, u32[]{:S(2)}) collective-permute-start(bf16[1,592,128]{2,1,0:T(8,128)(2,1)S(1)} %get-tuple-element.167), channel_id=1, source_target_pairs={{0,16},{4,20},{8,24},{12,28},{16,0},{20,4},{24,8},{28,12},{1,17},{... | collective-permute-start | bytes 454664 | tf_op jit(solution)/shard_map/ppermute | solution.py:645
  78.6 0.8 collective-permute-start.20
  79.4 0.1 sumrouteb.1.own_ref
  79.5 0.1 collective-permute-start.21
  79.6 2.0 %collective-permute-start.22 = (bf16[256,256]{1,0:T(8,128)(2,1)S(1)}, bf16[256,256]{1,0:T(8,128)(2,1)S(1)}, u32[]{:S(2)}, u32[]{:S(2)}) collective-permute-start(bf16[256,256]{1,0:T(8,128)(2,1)S(1)} %sumroutea.1.own_ref), channel_id=1, source_target_pairs={{0,2},{1,3},{2,0},{3,1},{4,6},{5,7},{6,4},{7,5},{8,10},{9,11},{10,... | collective-permute-start | bytes 393224 | tf_op jit(solution)/shard_map/ppermute | solution.py:642
  81.6 4.5 %collective-permute-done.22.far_ref = bf16[256,256]{1,0:T(8,128)(2,1)S(1)} collective-permute-done((bf16[256,256]{1,0:T(8,128)(2,1)S(1)}, bf16[256,256]{1,0:T(8,128)(2,1)S(1)}, u32[]{:S(2)}, u32[]{:S(2)}) %collective-permute-start.22) | collective-permute-done | bytes 131104 | tf_op jit(solution)/shard_map/ppermute | solution.py:642
  86.1 2.6 %collective-permute-done.23.refs_2_ = bf16[1,592,128]{2,1,0:T(8,128)(2,1)S(1)} collective-permute-done((bf16[1,592,128]{2,1,0:T(8,128)(2,1)S(1)}, bf16[1,592,128]{2,1,0:T(8,128)(2,1)S(1)}, u32[]{:S(2)}, u32[]{:S(2)}) %collective-permute-start.23) | collective-permute-done | bytes 151584 | tf_op jit(solution)/shard_map/ppermute | solution.py:645
  88.7 0.1 sumroutec.1.own_ref
  88.8 0.1 collective-permute-start.25
  88.9 0.1 collective-permute-start.27
  89.0 0.5 collective-permute-start.28
  89.5 0.1 collective-permute-start.29
  89.6 0.4 collective-permute-start.30
  90.0 0.8 collective-permute-done.29.near_ref
  90.8 0.2 collective-permute-start.26
  91.0 0.9 joina.1
  91.9 1.2 %joinb.1 = f32[576,512]{1,0:T(8,128)} custom-call(bf16[576,128]{1,0:T(8,128)(2,1)S(1)} %sumrouteb.1.own_ref, bf16[576,128]{1,0:T(8,128)(2,1)S(1)} %collective-permute-done.21.far_ref, bf16[576,128]{1,0:T(8,128)(2,1)S(1)} %collective-permute-done.27.near_ref, bf16[576,128]{1,0:T(8,128)(2,1)S(1)} %collective-permute-done.28.diagonal_ref), custom_call_target="tpu_custom_call" | custom-call | flops 21474836 | bytes 1024 | tf_op jit(solution)/shard_map/joinb/pallas_call | solution.py:588
  93.1 1.0 %collective-permute-done.25.far_ref = bf16[592,128]{1,0:T(8,128)(2,1)S(1)} collective-permute-done((bf16[592,128]{1,0:T(8,128)(2,1)S(1)}, bf16[592,128]{1,0:T(8,128)(2,1)S(1)}, u32[]{:S(2)}, u32[]{:S(2)}) %collective-permute-start.25) | collective-permute-done | bytes 151584 | tf_op jit(solution)/shard_map/ppermute | solution.py:642
  94.1 1.4 %collective-permute-done.31.diagonal_ref = bf16[592,128]{1,0:T(8,128)(2,1)S(1)} collective-permute-done((bf16[592,128]{1,0:T(8,128)(2,1)S(1)}, bf16[592,128]{1,0:T(8,128)(2,1)S(1)}, u32[]{:S(2)}, u32[]{:S(2)}) %collective-permute-start.31) | collective-permute-done | bytes 151584 | tf_op jit(solution)/shard_map/ppermute | solution.py:639
  95.5 1.2 %joinc.1 = (f32[576,512]{1,0:T(8,128)}, f32[1,64]{1,0:T(1,128)}, f32[1,64]{1,0:T(1,128)}, f32[1,64]{1,0:T(1,128)}, f32[1,64]{1,0:T(1,128)}, /*index=5*/f32[1,64]...) custom-call(bf16[592,128]{1,0:T(8,128)(2,1)S(1)} %sumroutec.1.own_re, ...), custom_call_target="tpu_custom_call" | custom-call | flops 21474836 | bytes 1024 | tf_op jit(solution)/shard_map/joinc/pallas_call | solution.py:588
  (66 shorter events, 0.1 us)
Async XLA Ops:
  0.7 5.1 %copy-start.8 = (f32[512]{0:T(512)S(1)}, f32[512]{0:T(512)}, u32[]{:S(2)}) copy-start(f32[512]{0:T(512)} %param.22) | copy-start | bytes 6148
  0.7 5.1 %copy-start.9 = (f32[512]{0:T(512)S(1)}, f32[512]{0:T(512)}, u32[]{:S(2)}) copy-start(f32[512]{0:T(512)} %param.23) | copy-start | bytes 6148
  0.7 5.1 %copy-start.18 = (f32[512]{0:T(512)S(1)}, f32[512]{0:T(512)}, u32[]{:S(2)}) copy-start(f32[512]{0:T(512)} %param.38) | copy-start | bytes 6148
  0.7 5.1 %copy-start.10 = (f32[512]{0:T(512)S(1)}, f32[512]{0:T(512)}, u32[]{:S(2)}) copy-start(f32[512]{0:T(512)} %param.25) | copy-start | bytes 6148
  0.7 5.1 %copy-start.11 = (f32[512]{0:T(512)S(1)}, f32[512]{0:T(512)}, u32[]{:S(2)}) copy-start(f32[512]{0:T(512)} %param.26) | copy-start | bytes 6148
  0.7 5.1 %copy-start.12 = (f32[512]{0:T(512)S(1)}, f32[512]{0:T(512)}, u32[]{:S(2)}) copy-start(f32[512]{0:T(512)} %param.27) | copy-start | bytes 6148
  0.7 5.1 %copy-start.13 = (f32[512]{0:T(512)S(1)}, f32[512]{0:T(512)}, u32[]{:S(2)}) copy-start(f32[512]{0:T(512)} %param.29) | copy-start | bytes 6148
  0.7 5.1 %copy-start.14 = (f32[512]{0:T(512)S(1)}, f32[512]{0:T(512)}, u32[]{:S(2)}) copy-start(f32[512]{0:T(512)} %param.30) | copy-start | bytes 6148
  0.7 5.1 %copy-start.15 = (f32[512]{0:T(512)S(1)}, f32[512]{0:T(512)}, u32[]{:S(2)}) copy-start(f32[512]{0:T(512)} %param.31) | copy-start | bytes 6148
  0.8 5.1 %copy-start.16 = (f32[512]{0:T(512)S(1)}, f32[512]{0:T(512)}, u32[]{:S(2)}) copy-start(f32[512]{0:T(512)} %param.33) | copy-start | bytes 6148
  0.8 5.1 %copy-start.17 = (f32[512]{0:T(512)S(1)}, f32[512]{0:T(512)}, u32[]{:S(2)}) copy-start(f32[512]{0:T(512)} %param.36) | copy-start | bytes 6148
  0.8 5.1 %copy-start.7 = (bf16[2,6,32,512]{3,2,1,0:T(8,128)(2,1)S(1)}, bf16[2,6,32,512]{3,2,1,0:T(8,128)(2,1)}, u32[]{:S(2)}) copy-start(bf16[2,6,32,512]{3,2,1,0:T(8,128)(2,1)} %cot_ref.1) | copy-start | bytes 1179652
  0.8 10.3 %slice-start = ((s8[4718592]{0:T(1024)(128)(4,1)}), s8[524288]{0:T(1024)(128)(4,1)S(1)}, s32[]{:S(2)}) async-start(s8[4718592]{0:T(1024)(128)(4,1)} %bitcast.22), calls=%async_computation | async-start | bytes 1048576
  0.8 17.5 %slice-start.2 = ((s8[4718592]{0:T(1024)(128)(4,1)}), s8[4194304]{0:T(1024)(128)(4,1)S(1)}, s32[]{:S(2)}) async-start(s8[4718592]{0:T(1024)(128)(4,1)} %bitcast.24), calls=%async_computation.2 | async-start | bytes 8388608
  2.7 6.7 %collective-permute-start.1 = (bf16[128,512]{1,0:T(8,128)(2,1)}, bf16[128,512]{1,0:T(8,128)(2,1)S(1)}, u32[]{:S(2)}, u32[]{:S(2)}) collective-permute-start(bf16[128,512]{1,0:T(8,128)(2,1)} %get-tuple-element.107), channel_id=1, source_target_pairs={{0,2},{1,3},{2,0},{3,1},{4,6},{5,7},{6,4},{7,5},{8,10},{9,11},{10,... | collective-permute-start | bytes 393224 | tf_op jit(solution)/shard_map/ppermute | solution.py:642
  5.8 4.3 %collective-permute-start = (bf16[192,512]{1,0:T(8,128)(2,1)}, bf16[192,512]{1,0:T(8,128)(2,1)S(1)}, u32[]{:S(2)}, u32[]{:S(2)}) collective-permute-start(bf16[192,512]{1,0:T(8,128)(2,1)} %get-tuple-element.106.own), channel_id=1, source_target_pairs={{0,1},{1,0},{2,3},{3,2},{4,5},{5,4},{6,7},{7,6},{8,9},{9,8},{10,11... | collective-permute-start | bytes 589832 | tf_op jit(solution)/shard_map/ppermute | solution.py:639
  5.8 5.3 %slice-start.1 = ((s8[4718592]{0:T(1024)(128)(4,1)}), s8[4194304]{0:T(1024)(128)(4,1)S(1)}, s32[]{:S(2)}) async-start(s8[4718592]{0:T(1024)(128)(4,1)} %bitcast.22), calls=%async_computation.1 | async-start | bytes 8388608
  5.9 0.8 copy-start.1
  6.7 4.4 %copy-start = (bf16[192,512]{1,0:T(8,128)(2,1)S(1)}, bf16[192,512]{1,0:T(8,128)(2,1)}, u32[]{:S(2)}) copy-start(bf16[192,512]{1,0:T(8,128)(2,1)} %get-tuple-element.106.own) | copy-start | bytes 589828
  6.7 4.4 %copy-start.2 = (s32[2]{0:T(128)S(1)}, s32[2]{0:T(128)}, u32[]{:S(2)}) copy-start(s32[2]{0:T(128)} %get-tuple-element.105.kinds.bucket_ref) | copy-start | bytes 28
  6.7 11.6 %slice-start.3 = ((s8[4718592]{0:T(1024)(128)(4,1)}), s8[524288]{0:T(1024)(128)(4,1)S(1)}, s32[]{:S(2)}) async-start(s8[4718592]{0:T(1024)(128)(4,1)} %bitcast.24), calls=%async_computation.3 | async-start | bytes 1048576
  7.3 11.1 %copy-start.3 = (bf16[512,512]{1,0:T(8,128)(2,1)S(1)}, bf16[512,512]{1,0:T(8,128)(2,1)}, u32[]{:S(2)}) copy-start(bf16[512,512]{1,0:T(8,128)(2,1)} %wq.1) | copy-start | bytes 1572868
  7.3 11.1 %copy-start.4 = (bf16[512,512]{1,0:T(8,128)(2,1)S(1)}, bf16[512,512]{1,0:T(8,128)(2,1)}, u32[]{:S(2)}) copy-start(bf16[512,512]{1,0:T(8,128)(2,1)} %wk.1) | copy-start | bytes 1572868
  7.3 11.0 %copy-start.5 = (bf16[512,512]{1,0:T(8,128)(2,1)S(1)}, bf16[512,512]{1,0:T(8,128)(2,1)}, u32[]{:S(2)}) copy-start(bf16[512,512]{1,0:T(8,128)(2,1)} %wv.1) | copy-start | bytes 1572868
  7.3 11.0 %copy-start.6 = (bf16[512,512]{1,0:T(8,128)(2,1)S(1)}, bf16[512,512]{1,0:T(8,128)(2,1)}, u32[]{:S(2)}) copy-start(bf16[512,512]{1,0:T(8,128)(2,1)} %wp.3) | copy-start | bytes 1572868
  7.3 11.0 %collective-permute-start.3 = (bf16[192,512]{1,0:T(8,128)(2,1)S(1)}, bf16[192,512]{1,0:T(8,128)(2,1)S(1)}, u32[]{:S(2)}, u32[]{:S(2)}) collective-permute-start(bf16[192,512]{1,0:T(8,128)(2,1)S(1)} %get-tuple-element.112.own), channel_id=1, source_target_pairs={{0,1},{1,0},{2,3},{3,2},{4,5},{5,4},{6,7},{7,6},{8,9},{9,8},{10,11... | collective-permute-start | bytes 589832 | tf_op jit(solution)/shard_map/ppermute | solution.py:639
  7.9 10.4 %collective-permute-start.4 = (bf16[160,512]{1,0:T(8,128)(2,1)S(1)}, bf16[160,512]{1,0:T(8,128)(2,1)S(1)}, u32[]{:S(2)}, u32[]{:S(2)}) collective-permute-start(bf16[160,512]{1,0:T(8,128)(2,1)S(1)} %get-tuple-element.113), channel_id=1, source_target_pairs={{0,2},{1,3},{2,0},{3,1},{4,6},{5,7},{6,4},{7,5},{8,10},{9,11},{10,... | collective-permute-start | bytes 491528 | tf_op jit(solution)/shard_map/ppermute | solution.py:642
  8.0 10.3 %collective-permute-start.5 = (bf16[160,512]{1,0:T(8,128)(2,1)S(1)}, bf16[160,512]{1,0:T(8,128)(2,1)S(1)}, u32[]{:S(2)}, u32[]{:S(2)}) collective-permute-start(bf16[160,512]{1,0:T(8,128)(2,1)S(1)} %get-tuple-element.113), channel_id=1, source_target_pairs={{0,3},{1,2},{2,1},{3,0},{4,7},{5,6},{6,5},{7,4},{8,11},{9,10},{10,... | collective-permute-start | bytes 491528 | tf_op jit(solution)/shard_map/ppermute | solution.py:675
  9.5 1.6 %collective-permute-start.2 = (bf16[128,512]{1,0:T(8,128)(2,1)S(1)}, bf16[128,512]{1,0:T(8,128)(2,1)S(1)}, u32[]{:S(2)}, u32[]{:S(2)}) collective-permute-start(bf16[128,512]{1,0:T(8,128)(2,1)S(1)} %collective-permute-done.1.received), channel_id=1, source_target_pairs={{0,1},{1,0},{2,3},{3,2},{4,5},{5,4},{6,7},{7,6},{8,9},{9,8},{10,11... | collective-permute-start | bytes 393224 | tf_op jit(solution)/shard_map/ppermute | solution.py:639
  16.4 14.4 %collective-permute-start.6 = (bf16[2,256,512]{2,1,0:T(8,128)(2,1)S(1)}, bf16[2,256,512]{2,1,0:T(8,128)(2,1)S(1)}, u32[]{:S(2)}, u32[]{:S(2)}) collective-permute-start(bf16[2,256,512]{2,1,0:T(8,128)(2,1)S(1)} %get-tuple-element.120), channel_id=1, source_target_pairs={{0,2},{1,3},{2,0},{3,1},{4,6},{5,7},{6,4},{7,5},{8,10},{9,11},{10,... | collective-permute-start | bytes 1572872 | tf_op jit(solution)/shard_map/ppermute | solution.py:642
  28.0 9.5 %collective-permute-start.8 = (bf16[512,128]{1,0:T(8,128)(2,1)S(1)}, bf16[512,128]{1,0:T(8,128)(2,1)S(1)}, u32[]{:S(2)}, u32[]{:S(2)}) collective-permute-start(bf16[512,128]{1,0:T(8,128)(2,1)S(1)} %get-tuple-element.124), channel_id=1, source_target_pairs={{0,2},{1,3},{2,0},{3,1},{4,6},{5,7},{6,4},{7,5},{8,10},{9,11},{10,... | collective-permute-start | bytes 393224 | tf_op jit(solution)/shard_map/ppermute | solution.py:642
  28.3 13.9 %collective-permute-start.9 = (bf16[4,256,256]{2,1,0:T(8,128)(2,1)S(1)}, bf16[4,256,256]{2,1,0:T(8,128)(2,1)S(1)}, u32[]{:S(2)}, u32[]{:S(2)}) collective-permute-start(bf16[4,256,256]{2,1,0:T(8,128)(2,1)S(1)} %get-tuple-element.127), channel_id=1, source_target_pairs={{0,4},{4,0},{8,12},{12,8},{16,20},{20,16},{24,28},{28,24},{1,5},{5... | collective-permute-start | bytes 1572872 | tf_op jit(solution)/shard_map/ppermute | solution.py:645
  30.8 6.7 %collective-permute-start.7 = (bf16[2,256,512]{2,1,0:T(8,128)(2,1)S(1)}, bf16[2,256,512]{2,1,0:T(8,128)(2,1)S(1)}, u32[]{:S(2)}, u32[]{:S(2)}) collective-permute-start(bf16[2,256,512]{2,1,0:T(8,128)(2,1)S(1)} %collective-permute-done.6.half_t), channel_id=1, source_target_pairs={{0,1},{1,0},{2,3},{3,2},{4,5},{5,4},{6,7},{7,6},{8,9},{9,8},{10,11... | collective-permute-start | bytes 1572872 | tf_op jit(solution)/shard_map/ppermute | solution.py:639
  35.2 16.6 %collective-permute-start.11 = (bf16[512,128]{1,0:T(8,128)(2,1)S(1)}, bf16[512,128]{1,0:T(8,128)(2,1)S(1)}, u32[]{:S(2)}, u32[]{:S(2)}) collective-permute-start(bf16[512,128]{1,0:T(8,128)(2,1)S(1)} %get-tuple-element.143), channel_id=1, source_target_pairs={{0,2},{1,3},{2,0},{3,1},{4,6},{5,7},{6,4},{7,5},{8,10},{9,11},{10,... | collective-permute-start | bytes 393224 | tf_op jit(solution)/shard_map/ppermute | solution.py:642
  40.8 16.9 %collective-permute-start.15 = (bf16[4,576,128]{2,1,0:T(8,128)(2,1)S(1)}, bf16[4,576,128]{2,1,0:T(8,128)(2,1)S(1)}, u32[]{:S(2)}, u32[]{:S(2)}) collective-permute-start(bf16[4,576,128]{2,1,0:T(8,128)(2,1)S(1)} %get-tuple-element.125), channel_id=1, source_target_pairs={{0,4},{4,0},{8,12},{12,8},{16,20},{20,16},{24,28},{28,24},{1,5},{5... | collective-permute-start | bytes 1769480 | tf_op jit(solution)/shard_map/ppermute | solution.py:645
  42.3 14.0 %collective-permute-start.14 = (bf16[1,256,256]{2,1,0:T(8,128)(2,1)S(1)}, bf16[1,256,256]{2,1,0:T(8,128)(2,1)S(1)}, u32[]{:S(2)}, u32[]{:S(2)}) collective-permute-start(bf16[1,256,256]{2,1,0:T(8,128)(2,1)S(1)} %get-tuple-element.131), channel_id=1, source_target_pairs={{0,24},{4,28},{8,16},{12,20},{16,8},{20,12},{24,0},{28,4},{1,25},{... | collective-permute-start | bytes 393224 | tf_op jit(solution)/shard_map/ppermute | solution.py:645
  45.9 11.7 %collective-permute-start.13 = (bf16[1,256,256]{2,1,0:T(8,128)(2,1)S(1)}, bf16[1,256,256]{2,1,0:T(8,128)(2,1)S(1)}, u32[]{:S(2)}, u32[]{:S(2)}) collective-permute-start(bf16[1,256,256]{2,1,0:T(8,128)(2,1)S(1)} %get-tuple-element.130), channel_id=1, source_target_pairs={{0,16},{4,20},{8,24},{12,28},{16,0},{20,4},{24,8},{28,12},{1,17},{... | collective-permute-start | bytes 393224 | tf_op jit(solution)/shard_map/ppermute | solution.py:645
  45.9 11.7 %collective-permute-start.12 = (bf16[1,256,256]{2,1,0:T(8,128)(2,1)S(1)}, bf16[1,256,256]{2,1,0:T(8,128)(2,1)S(1)}, u32[]{:S(2)}, u32[]{:S(2)}) collective-permute-start(bf16[1,256,256]{2,1,0:T(8,128)(2,1)S(1)} %get-tuple-element.129), channel_id=1, source_target_pairs={{0,8},{4,12},{8,0},{12,4},{16,24},{20,28},{24,16},{28,20},{1,9},{5... | collective-permute-start | bytes 393224 | tf_op jit(solution)/shard_map/ppermute | solution.py:645
  51.7 7.5 %collective-permute-start.10 = (bf16[2,128,512]{2,1,0:T(8,128)(2,1)S(1)}, bf16[2,128,512]{2,1,0:T(8,128)(2,1)S(1)}, u32[]{:S(2)}, u32[]{:S(2)}) collective-permute-start(bf16[2,128,512]{2,1,0:T(8,128)(2,1)S(1)} %get-tuple-element.140), channel_id=1, source_target_pairs={{0,2},{1,3},{2,0},{3,1},{4,6},{5,7},{6,4},{7,5},{8,10},{9,11},{10,... | collective-permute-start | bytes 786440 | tf_op jit(solution)/shard_map/ppermute | solution.py:642
  56.3 13.6 %collective-permute-start.16 = (bf16[4,592,128]{2,1,0:T(8,128)(2,1)S(1)}, bf16[4,592,128]{2,1,0:T(8,128)(2,1)S(1)}, u32[]{:S(2)}, u32[]{:S(2)}) collective-permute-start(bf16[4,592,128]{2,1,0:T(8,128)(2,1)S(1)} %get-tuple-element.145), channel_id=1, source_target_pairs={{0,4},{4,0},{8,12},{12,8},{16,20},{20,16},{24,28},{28,24},{1,5},{5... | collective-permute-start | bytes 1818632 | tf_op jit(solution)/shard_map/ppermute | solution.py:645
  59.3 10.7 %collective-permute-start.17 = (bf16[1,576,128]{2,1,0:T(8,128)(2,1)S(1)}, bf16[1,576,128]{2,1,0:T(8,128)(2,1)S(1)}, u32[]{:S(2)}, u32[]{:S(2)}) collective-permute-start(bf16[1,576,128]{2,1,0:T(8,128)(2,1)S(1)} %get-tuple-element.158), channel_id=1, source_target_pairs={{0,8},{4,12},{8,0},{12,4},{16,24},{20,28},{24,16},{28,20},{1,9},{5... | collective-permute-start | bytes 442376 | tf_op jit(solution)/shard_map/ppermute | solution.py:645
  60.6 14.4 %collective-permute-start.18 = (bf16[1,576,128]{2,1,0:T(8,128)(2,1)S(1)}, bf16[1,576,128]{2,1,0:T(8,128)(2,1)S(1)}, u32[]{:S(2)}, u32[]{:S(2)}) collective-permute-start(bf16[1,576,128]{2,1,0:T(8,128)(2,1)S(1)} %get-tuple-element.159), channel_id=1, source_target_pairs={{0,16},{4,20},{8,24},{12,28},{16,0},{20,4},{24,8},{28,12},{1,17},{... | collective-permute-start | bytes 442376 | tf_op jit(solution)/shard_map/ppermute | solution.py:645
  63.3 11.7 %collective-permute-start.19 = (bf16[1,576,128]{2,1,0:T(8,128)(2,1)S(1)}, bf16[1,576,128]{2,1,0:T(8,128)(2,1)S(1)}, u32[]{:S(2)}, u32[]{:S(2)}) collective-permute-start(bf16[1,576,128]{2,1,0:T(8,128)(2,1)S(1)} %get-tuple-element.160), channel_id=1, source_target_pairs={{0,24},{4,28},{8,16},{12,20},{16,8},{20,12},{24,0},{28,4},{1,25},{... | collective-permute-start | bytes 442376 | tf_op jit(solution)/shard_map/ppermute | solution.py:645
  75.0 11.1 %collective-permute-start.24 = (bf16[1,592,128]{2,1,0:T(8,128)(2,1)S(1)}, bf16[1,592,128]{2,1,0:T(8,128)(2,1)S(1)}, u32[]{:S(2)}, u32[]{:S(2)}) collective-permute-start(bf16[1,592,128]{2,1,0:T(8,128)(2,1)S(1)} %get-tuple-element.170), channel_id=1, source_target_pairs={{0,24},{4,28},{8,16},{12,20},{16,8},{20,12},{24,0},{28,4},{1,25},{... | collective-permute-start | bytes 454664 | tf_op jit(solution)/shard_map/ppermute | solution.py:645
  75.8 13.0 %collective-permute-start.23 = (bf16[1,592,128]{2,1,0:T(8,128)(2,1)S(1)}, bf16[1,592,128]{2,1,0:T(8,128)(2,1)S(1)}, u32[]{:S(2)}, u32[]{:S(2)}) collective-permute-start(bf16[1,592,128]{2,1,0:T(8,128)(2,1)S(1)} %get-tuple-element.167), channel_id=1, source_target_pairs={{0,16},{4,20},{8,24},{12,28},{16,0},{20,4},{24,8},{28,12},{1,17},{... | collective-permute-start | bytes 454664 | tf_op jit(solution)/shard_map/ppermute | solution.py:645
  78.6 10.1 %collective-permute-start.20 = (bf16[1,592,128]{2,1,0:T(8,128)(2,1)S(1)}, bf16[1,592,128]{2,1,0:T(8,128)(2,1)S(1)}, u32[]{:S(2)}, u32[]{:S(2)}) collective-permute-start(bf16[1,592,128]{2,1,0:T(8,128)(2,1)S(1)} %get-tuple-element.161), channel_id=1, source_target_pairs={{0,8},{4,12},{8,0},{12,4},{16,24},{20,28},{24,16},{28,20},{1,9},{5... | collective-permute-start | bytes 454664 | tf_op jit(solution)/shard_map/ppermute | solution.py:645
  79.5 6.6 %collective-permute-start.21 = (bf16[576,128]{1,0:T(8,128)(2,1)S(1)}, bf16[576,128]{1,0:T(8,128)(2,1)S(1)}, u32[]{:S(2)}, u32[]{:S(2)}) collective-permute-start(bf16[576,128]{1,0:T(8,128)(2,1)S(1)} %sumrouteb.1.own_ref), channel_id=1, source_target_pairs={{0,2},{1,3},{2,0},{3,1},{4,6},{5,7},{6,4},{7,5},{8,10},{9,11},{10,... | collective-permute-start | bytes 442376 | tf_op jit(solution)/shard_map/ppermute | solution.py:642
  79.6 6.5 %collective-permute-start.22 = (bf16[256,256]{1,0:T(8,128)(2,1)S(1)}, bf16[256,256]{1,0:T(8,128)(2,1)S(1)}, u32[]{:S(2)}, u32[]{:S(2)}) collective-permute-start(bf16[256,256]{1,0:T(8,128)(2,1)S(1)} %sumroutea.1.own_ref), channel_id=1, source_target_pairs={{0,2},{1,3},{2,0},{3,1},{4,6},{5,7},{6,4},{7,5},{8,10},{9,11},{10,... | collective-permute-start | bytes 393224 | tf_op jit(solution)/shard_map/ppermute | solution.py:642
  88.8 5.3 %collective-permute-start.25 = (bf16[592,128]{1,0:T(8,128)(2,1)S(1)}, bf16[592,128]{1,0:T(8,128)(2,1)S(1)}, u32[]{:S(2)}, u32[]{:S(2)}) collective-permute-start(bf16[592,128]{1,0:T(8,128)(2,1)S(1)} %sumroutec.1.own_ref), channel_id=1, source_target_pairs={{0,2},{1,3},{2,0},{3,1},{4,6},{5,7},{6,4},{7,5},{8,10},{9,11},{10,... | collective-permute-start | bytes 454664 | tf_op jit(solution)/shard_map/ppermute | solution.py:642
  88.9 3.0 %collective-permute-start.27 = (bf16[576,128]{1,0:T(8,128)(2,1)S(1)}, bf16[576,128]{1,0:T(8,128)(2,1)S(1)}, u32[]{:S(2)}, u32[]{:S(2)}) collective-permute-start(bf16[576,128]{1,0:T(8,128)(2,1)S(1)} %sumrouteb.1.own_ref), channel_id=1, source_target_pairs={{0,1},{1,0},{2,3},{3,2},{4,5},{5,4},{6,7},{7,6},{8,9},{9,8},{10,11... | collective-permute-start | bytes 442376 | tf_op jit(solution)/shard_map/ppermute | solution.py:639
  89.0 2.9 %collective-permute-start.28 = (bf16[576,128]{1,0:T(8,128)(2,1)S(1)}, bf16[576,128]{1,0:T(8,128)(2,1)S(1)}, u32[]{:S(2)}, u32[]{:S(2)}) collective-permute-start(bf16[576,128]{1,0:T(8,128)(2,1)S(1)} %collective-permute-done.21.far_ref), channel_id=1, source_target_pairs={{0,1},{1,0},{2,3},{3,2},{4,5},{5,4},{6,7},{7,6},{8,9},{9,8},{10,11... | collective-permute-start | bytes 442376 | tf_op jit(solution)/shard_map/ppermute | solution.py:639
  89.5 1.3 %collective-permute-start.29 = (bf16[256,256]{1,0:T(8,128)(2,1)S(1)}, bf16[256,256]{1,0:T(8,128)(2,1)S(1)}, u32[]{:S(2)}, u32[]{:S(2)}) collective-permute-start(bf16[256,256]{1,0:T(8,128)(2,1)S(1)} %sumroutea.1.own_ref), channel_id=1, source_target_pairs={{0,1},{1,0},{2,3},{3,2},{4,5},{5,4},{6,7},{7,6},{8,9},{9,8},{10,11... | collective-permute-start | bytes 393224 | tf_op jit(solution)/shard_map/ppermute | solution.py:639
  89.6 1.5 %collective-permute-start.30 = (bf16[256,256]{1,0:T(8,128)(2,1)S(1)}, bf16[256,256]{1,0:T(8,128)(2,1)S(1)}, u32[]{:S(2)}, u32[]{:S(2)}) collective-permute-start(bf16[256,256]{1,0:T(8,128)(2,1)S(1)} %collective-permute-done.22.far_ref), channel_id=1, source_target_pairs={{0,1},{1,0},{2,3},{3,2},{4,5},{5,4},{6,7},{7,6},{8,9},{9,8},{10,11... | collective-permute-start | bytes 393224 | tf_op jit(solution)/shard_map/ppermute | solution.py:639
  90.8 3.3 %collective-permute-start.26 = (bf16[592,128]{1,0:T(8,128)(2,1)S(1)}, bf16[592,128]{1,0:T(8,128)(2,1)S(1)}, u32[]{:S(2)}, u32[]{:S(2)}) collective-permute-start(bf16[592,128]{1,0:T(8,128)(2,1)S(1)} %sumroutec.1.own_ref), channel_id=1, source_target_pairs={{0,1},{1,0},{2,3},{3,2},{4,5},{5,4},{6,7},{7,6},{8,9},{9,8},{10,11... | collective-permute-start | bytes 454664 | tf_op jit(solution)/shard_map/ppermute | solution.py:639
  94.1 1.4 %collective-permute-start.31 = (bf16[592,128]{1,0:T(8,128)(2,1)S(1)}, bf16[592,128]{1,0:T(8,128)(2,1)S(1)}, u32[]{:S(2)}, u32[]{:S(2)}) collective-permute-start(bf16[592,128]{1,0:T(8,128)(2,1)S(1)} %collective-permute-done.25.far_ref), channel_id=1, source_target_pairs={{0,1},{1,0},{2,3},{3,2},{4,5},{5,4},{6,7},{7,6},{8,9},{9,8},{10,11... | collective-permute-start | bytes 454664 | tf_op jit(solution)/shard_map/ppermute | solution.py:639

commit v7 on v6

--- a/solution.py
+++ b/solution.py
@@ -21,7 +21,7 @@
 HB = pl.BlockSpec(memory_space=pltpu.HBM)
 RATE = 1 << 30
 LENGTH = {
-    "pack": 10, "stack": 10, "first": 0.02, "second": 30, "third": 20, "fourth": 10, "weight2": 1, "weight1": 0.02, "routeb1": 20, "unpack": 5,
+    "pack": 10, "stack": 10, "first": 0.02, "second": 30, "third": 20, "fourth": 10, "weight2": 1, "weight1": 3, "routeb1": 20,
 }
 
 
@@ -421,7 +421,7 @@
 def fourth_kernel(
     bucket_ref, grad1_ref, image_ref, stats_ref, grad_middle_ref, middle_ref, mixed_ref, vecs,
     weight1, wp, vec_a, vec_b,
-    out_own, grad_own, send_ref, vec_out,
+    out_own, grad_own, send_ref, vec_keep, vec_send,
     shift_ref, acc_ref, full_ref, vec_ref,
 ):
     h, home, away = place(bucket_ref)
@@ -448,21 +448,24 @@
     vec_ref[9:10, :] = gain_grad
     vec_ref[10:11, :] = shift_grad
     vec_ref[11:VECS, :] = jnp.zeros((VECS - 11, channels), F32)
-    shards = vec_out.shape[0]
-    rows = channels // shards
-    for shard in range(shards):
-        start = shard * rows
-        tile = start // BLK * BLK
-        part = vec_ref[:, tile : tile + BLK]
-        vec_out[shard] = part if start == tile else pltpu.roll(part, BLK - (start - tile), 1)
+    pairs = vec_keep.shape[0]
+    rows = channels // (2 * pairs)
+    mine = (lax.axis_index("batch") & 1) == 1
+    for pair in range(pairs):
+        parts = []
+        for shard in (2 * pair, 2 * pair + 1):
+            start = shard * rows
+            tile = start // BLK * BLK
+            part = vec_ref[:, tile : tile + BLK]
+            parts.append(part if start == tile else pltpu.roll(part, BLK - (start - tile), 1))
+        vec_keep[pair] = jnp.where(mine, parts[1], parts[0]).astype(BF16)
+        vec_send[pair] = jnp.where(mine, parts[0], parts[1]).astype(BF16)
 
 
 def weight_kernel(
     bucket_ref, act_t, half_t, partner_half_t, block_own, block_away,
-    *rest, layer,
+    keep_ref, send_ref, left_ref, right_ref, shift_ref, sum_ref, *, layer,
 ):
-    vec_ref = rest[0] if len(rest) == 7 else None
-    keep_ref, send_ref, left_ref, right_ref, shift_ref, sum_ref = rest[-6:]
     h, home, away = place(bucket_ref)
     channels = act_t.shape[0]
     half = channels // 2
@@ -489,25 +492,20 @@
     for pair in range(pairs):
         for dst, which in ((keep_ref, mine), (send_ref, 1 - mine)):
             shard = 2 * pair + which
-            dst[pair, 0:rows, :] = sum_ref[pl.ds(pl.multiple_of(shard * rows, 8), rows), :].astype(BF16)
-            if vec_ref is not None:
-                dst[pair, rows : rows + VECS, :] = vec_ref[shard].astype(BF16)
-
-
-def route_kernel(*refs, bit, ways):
+            dst[pair] = sum_ref[pl.ds(pl.multiple_of(shard * rows, 8), rows), :].astype(BF16)
+
+
+def route_kernel(keep_ref, got_ref, *outs, bit, first):
+    ways = len(outs) if first == 0 else len(outs) // 2
     group = (lax.axis_index("batch") >> bit) & (ways - 1)
-    ins, outs = refs[: len(refs) - ways], refs[len(refs) - ways :]
-    first = 0
-    for keep_ref, got_ref in zip(ins[::2], ins[1::2]):
-        rows = keep_ref.shape[1]
-        for step, dst in enumerate(outs):
-            which = group ^ step
-            for index in range(dst.shape[0]):
-                at = index * ways + which
-                dst[index, first : first + rows, :] = (
-                    keep_ref[at].astype(F32) + got_ref[at].astype(F32)
-                ).astype(BF16)
-        first += rows
+    rows = keep_ref.shape[1]
+    for step, dst in enumerate(outs[-ways:]):
+        which = group ^ step
+        for index in range(dst.shape[0]):
+            at = index * ways + which
+            dst[index, first : first + rows, :] = (
+                keep_ref[at].astype(F32) + got_ref[at].astype(F32)
+            ).astype(BF16)
 
 
 def total_of(refs):
@@ -582,7 +580,7 @@
                         dst[image, row] = jnp.zeros((32, channels), dst.dtype)
 
 
-def call(kernel, name, outs, scratch, vmem, *operands, smem=1, any_from=99):
+def call(kernel, name, outs, scratch, vmem, *operands, smem=1, any_from=99, aliases={}):
     specs = [SM] * smem + [VM] * (len(operands) - smem)
     specs = [HB if i >= any_from else spec for i, spec in enumerate(specs)]
     return pl.pallas_call(
@@ -597,6 +595,7 @@
             else (pltpu.SMEM if dtype == jnp.int32 else pltpu.VMEM)(shape, dtype)
             for shape, dtype in scratch
         ],
+        input_output_aliases=aliases,
         compiler_params=pltpu.CompilerParams(vmem_limit_bytes=vmem << 20),
         cost_estimate=pl.CostEstimate(
             flops=int(LENGTH.get(name, 0.02) * RATE), bytes_accessed=1024, transcendentals=0
@@ -703,26 +702,32 @@
     )
     block1_away = to_chip(block1_send)
 
-    def weight_grad(name, act_t, index, own, away, *vec):
-        rows = shard_rows + (VECS if vec else 0)
+    def weight_grad(name, act_t, index, own, away):
         return call(
             functools.partial(weight_kernel, layer=index), name,
-            [((batches // 2, rows, BLK), BF16)] * 2,
+            [((batches // 2, shard_rows, BLK), BF16)] * 2,
             [((C, 2 * PIX), BF16), ((2 * PIX, 9 * BLK), BF16), ((3, PIX + 2 * PAD, BLK), BF16),
              ((9 * C, BLK), F32)],
-            18, kinds, act_t, half_t, core_half_t, own, away, *vec,
+            18, kinds, act_t, half_t, core_half_t, own, away,
         )
 
     keep2, send2 = weight_grad("weight2", act2_t, 1, after(block2, block1), block2_away)
     got2 = to_batch(send2, 1)
 
-    def spread(name, bit, *pairs, behind=()):
+    def spread(name, bit, keep, got, tail=None, behind=()):
         ways = 1 << min(2, bits - bit)
-        shape = (pairs[0].shape[0] // ways, sum(v.shape[1] for v in pairs[::2]), pairs[0].shape[2])
+        rows = keep.shape[1]
+        shape = (keep.shape[0] // ways, rows + (VECS if tail else 0), keep.shape[2])
         parts = call(
-            functools.partial(route_kernel, bit=bit, ways=ways), name + str(bit),
-            [(shape, BF16)] * ways, [], 16, *pairs, smem=0,
+            functools.partial(route_kernel, bit=bit, first=0), name + str(bit),
+            [(shape, BF16)] * ways, [], 16, keep, got, smem=0,
         )
+        if tail:
+            parts = call(
+                functools.partial(route_kernel, bit=bit, first=rows), name + "tail",
+                [(shape, BF16)] * ways, [], 16, *tail, *parts, smem=0,
+                aliases={2 + j: j for j in range(ways)},
+            )
         return parts, [to_batch(after(parts[j], *behind), j << bit) for j in range(1, ways)]
 
     def finish(name, parts, got):
@@ -739,39 +744,41 @@
         return shard, far, near, to_core(after(far, *between))
 
     parts_a, got_a = spread("routea", 1, after(attn_keep, send2), attn_got)
-    out_own, grad_own, image_send, vec_c = call(
+    keep1, send1 = weight_grad("weight1", act1_t, 0, after(block1, *parts_a), block1_away)
+    got1 = to_batch(send1, 1)
+    shard_a = finish("routea", parts_a, [after(g, send1) for g in got_a])
+    out_own, grad_own, image_send, vec_keep, vec_send = call(
         fourth_kernel, "fourth",
-        [((192, C), BF16), ((192, C), BF16), ((2, 128, C), BF16), ((batches, VECS, BLK), F32)],
+        [((192, C), BF16), ((192, C), BF16), ((2, 128, C), BF16),
+         ((batches // 2, VECS, BLK), BF16), ((batches // 2, VECS, BLK), BF16)],
         [shifts, img32, img16, ((VECS, C), F32)], 14,
-        kinds, after(grad1, *parts_a), image, stats, grad_middle, middle, mixed, vecs,
+        kinds, after(grad1, send1), image, stats, grad_middle, middle, mixed, vecs,
         conv1_weight, proj_weight, vec_a, vec_b,
     )
     image_away = to_chip(image_send)
-    keep1, send1 = weight_grad("weight1", act1_t, 0, block1, block1_away, vec_c)
-    got1 = to_batch(send1, 1)
-    shard_a = finish("routea", parts_a, [after(g, vec_c) for g in got_a])
-    parts_b, got_b = spread("routeb", 1, after(keep2, send1, shard_a), got2)
+    vec_got = to_batch(vec_send, 1)
+    parts_b, got_b = spread("routeb", 1, after(keep2, vec_keep, shard_a), got2)
+    parts_c, got_c = spread("routec", 1, keep1, got1, (vec_keep, vec_got), behind=got_b)
+    shard_b = finish("routeb", parts_b, [after(g, parts_c[0]) for g in got_b])
     gathered_a = gather(shard_a)
+    gathered_b = gather(shard_b)
+    shard_c = finish(
+        "routec", parts_c, [after(g, gathered_b[1], gathered_a[1]) for g in got_c]
+    )
+    small = call(
+        join_attn_kernel, "joina", [((small_rows, C), F32)] * 4, [], 8,
+        after(gathered_a[0], shard_c), *gathered_a[1:], smem=0,
+    )
+    (whole2,) = call(
+        join_kernel, "joinb", [((shard_rows, C), F32)], [], 8,
+        after(gathered_b[0], shard_c), *gathered_b[1:], smem=0,
+    )
     outputs, input_grad = call(
         unpack_kernel, "unpack",
         [(inputs.shape, BF16)] * 2, [], 8,
-        kinds, out_own, grad_own, after(image_away, parts_b[0]),
-    )
-    parts_c, got_c = spread("routec", 1, after(keep1, outputs), got1, behind=got_b)
-    shard_b = finish("routeb", parts_b, [after(g, parts_c[0]) for g in got_b])
-    gathered_b = gather(shard_b)
-    shard_c = finish(
-        "routec", parts_c, [after(g, gathered_b[1], gathered_a[1]) for g in got_c]
-    )
-    small = call(
-        join_attn_kernel, "joina", [((small_rows, C), F32)] * 4, [], 8,
-        after(gathered_a[0], shard_c), *gathered_a[1:], smem=0,
-    )
-    (whole2,) = call(
-        join_kernel, "joinb", [((shard_rows, C), F32)], [], 8,
-        after(gathered_b[0], shard_c), *gathered_b[1:], smem=0,
-    )
-    gathered_c = gather(shard_c, whole2, *small)
+        kinds, out_own, grad_own, after(image_away, shard_c),
+    )
+    gathered_c = gather(shard_c, whole2, outputs, *small)
     whole1, *sums = call(
         join_kernel, "joinc", [((shard_rows, C), F32)] + [((1, small_rows), F32)] * 11, [], 8,
         *gathered_c, smem=0,

time: 97 us -> 95.2 us (0.981)
  waiting for transfers between devices: 23.7 us -> 21.2 us
    ppermute x12 -> x13, starting transfers between devices: 17.4 us -> 18.6 us  [to_batch(): return lax.ppermute(v, 'batch', [(i, i ^ change) for i in range(batches)])]
    ppermute x10, waiting for transfers between devices: 3.21 us -> 2.05 us  [to_core(): return lax.ppermute(v, 'height', [(i, i ^ 1) for i in range(4)])]
    ppermute x12 -> x13, waiting for transfers between devices: 12.3 us -> 11.4 us  [to_batch(): return lax.ppermute(v, 'batch', [(i, i ^ change) for i in range(batches)])]
    pallas_call x18 -> x19, Pallas kernels: 38.6 us -> 38.6 us  [call(): pl.pallas_call(kernel, name=name, out_shape=[jax.ShapeDtypeStruct(shape,...]
  transfers between devices with their start and end apart: 32 -> 33, of which waited for: 11 -> 10; matrix products, arithmetic and copies ran while one was open for 0% -> 0% of each run, Pallas kernels for 37% -> 37%
where the time goes in v7:
time: 95.2 us; the launch traced here: 95 us
  Pallas kernels  38.6 us (41%)
  starting transfers between devices  33 us (35%)
  waiting for transfers between devices  21.2 us (22%)
  between operations  1.27 us (1%)
    pallas_call x19, Pallas kernels, call(): pl.pallas_call(kernel, name=name, out_shape=[jax.ShapeDtypeStruct(shape,...  38.6 us
    ppermute x13, starting transfers between devices, to_batch(): return lax.ppermute(v, 'batch', [(i, i ^ change) for i in range(batches)])  18.6 us
    ppermute x13, waiting for transfers between devices, to_batch(): return lax.ppermute(v, 'batch', [(i, i ^ change) for i in range(batches)])  11.4 us
    ppermute x9, starting transfers between devices, to_chip(): return lax.ppermute(v, 'height', [(i, i ^ 2) for i in range(4)])  10.6 us
    ppermute x9, waiting for transfers between devices, to_chip(): return lax.ppermute(v, 'height', [(i, i ^ 2) for i in range(4)])  7.74 us
    ppermute x10, starting transfers between devices, to_core(): return lax.ppermute(v, 'height', [(i, i ^ 1) for i in range(4)])  2.51 us
    ppermute x10, waiting for transfers between devices, to_core(): return lax.ppermute(v, 'height', [(i, i ^ 1) for i in range(4)])  2.05 us
  transfers between devices with their start and end apart: 33, of which 10 were waited for; matrix products, arithmetic and copies ran while one was open for 0% of the time, Pallas kernels for 37%

profile of v7, /device:TPU:0, one launch (start us, length us, event | category | flops | bytes accessed | tf_op | source)
XLA Modules:
  0.0 95.0 jit_solution(12000193623468874182)
XLA Ops:
  0.8 0.0 slice-start
  0.8 0.0 slice-start.2
  0.8 1.9 %pack.1 = (s32[2]{0:T(128)}, bf16[128,512]{1,0:T(8,128)(2,1)}, bf16[192,512]{1,0:T(8,128)(2,1)}) custom-call(s32[2]{0:T(128)} %bucket_hbm.1, bf16[2,6,32,512]{3,2,1,0:T(8,128)(2,1)} %x_hbm.1), custom_call_target="tpu_custom_call" | custom-call | flops 10737418240 | bytes 1024 | tf_op jit(solution)/shard_map/pack/pallas_call | solution.py:586
  2.7 3.0 %collective-permute-start.1 = (bf16[128,512]{1,0:T(8,128)(2,1)}, bf16[128,512]{1,0:T(8,128)(2,1)S(1)}, u32[]{:S(2)}, u32[]{:S(2)}) collective-permute-start(bf16[128,512]{1,0:T(8,128)(2,1)} %get-tuple-element.112), channel_id=1, source_target_pairs={{0,2},{1,3},{2,0},{3,1},{4,6},{5,7},{6,4},{7,5},{8,10},{9,11},{10,... | collective-permute-start | bytes 393224 | tf_op jit(solution)/shard_map/ppermute | solution.py:641
  5.9 0.0 copy-start.1
  5.9 0.8 copy-done.1
  6.7 0.6 stack.1
  7.3 0.0 copy-start.3
  7.3 0.0 copy-start.4
  7.3 0.0 copy-start.5
  7.3 0.0 copy-start.6
  7.3 0.6 collective-permute-start.3
  7.9 0.1 collective-permute-start.4
  8.0 1.4 %collective-permute-start.5 = (bf16[160,512]{1,0:T(8,128)(2,1)S(1)}, bf16[160,512]{1,0:T(8,128)(2,1)S(1)}, u32[]{:S(2)}, u32[]{:S(2)}) collective-permute-start(bf16[160,512]{1,0:T(8,128)(2,1)S(1)} %get-tuple-element.118), channel_id=1, source_target_pairs={{0,3},{1,2},{2,1},{3,0},{4,7},{5,6},{6,5},{7,4},{8,11},{9,10},{10,... | collective-permute-start | bytes 491528 | tf_op jit(solution)/shard_map/ppermute | solution.py:674
  9.3 0.1 collective-permute-done.1.received
  9.5 0.6 collective-permute-start.2
  10.1 1.0 %collective-permute-done.2.partner_received = bf16[128,512]{1,0:T(8,128)(2,1)S(1)} collective-permute-done((bf16[128,512]{1,0:T(8,128)(2,1)S(1)}, bf16[128,512]{1,0:T(8,128)(2,1)S(1)}, u32[]{:S(2)}, u32[]{:S(2)}) %collective-permute-start.2) | collective-permute-done | bytes 131104 | tf_op jit(solution)/shard_map/ppermute | solution.py:638
  11.1 5.4 %first.1 = (bf16[512,512]{1,0:T(8,128)(2,1)S(1)}, f32[512,512]{1,0:T(8,128)S(1)}, bf16[512,512]{1,0:T(8,128)(2,1)S(1)}, f32[8,512]{1,0:T(8,128)S(1)}, bf16[512,5...) custom-call(s32[2]{0:T(128)S(1)} %copy-done.2, bf16[192,512]{1,0:T(8,128)(2,1)S(1)} %copy-done, ...), custom_call_target="tpu_custom_call" | custom-call | flops 21474836 | bytes 1024 | tf_op jit(solution)/shard_map/first/pallas_call | solution.py:586
  16.4 1.9 %collective-permute-start.6 = (bf16[2,256,512]{2,1,0:T(8,128)(2,1)S(1)}, bf16[2,256,512]{2,1,0:T(8,128)(2,1)S(1)}, u32[]{:S(2)}, u32[]{:S(2)}) collective-permute-start(bf16[2,256,512]{2,1,0:T(8,128)(2,1)S(1)} %get-tuple-element.124), channel_id=1, source_target_pairs={{0,2},{1,3},{2,0},{3,1},{4,6},{5,7},{6,4},{7,5},{8,10},{9,11},{10,... | collective-permute-start | bytes 1572872 | tf_op jit(solution)/shard_map/ppermute | solution.py:641
  18.4 9.6 %second.1 = (f32[512,512]{1,0:T(8,128)S(1)}, bf16[512,512]{1,0:T(8,128)(2,1)S(1)}, bf16[512,512]{1,0:T(8,128)(2,1)S(1)}, f32[512,512]{1,0:T(8,128)S(1)}, bf16[4,...) custom-call(s32[2]{0:T(128)S(1)} %copy-done.2, ...), custom_call_target="tpu_custom_call" | custom-call | flops 32212254720 | bytes 1024 | tf_op jit(solution)/shard_map/second/pallas_call | solution.py:586
  28.0 0.3 collective-permute-start.8
  28.3 1.5 %collective-permute-start.9 = (bf16[4,256,256]{2,1,0:T(8,128)(2,1)S(1)}, bf16[4,256,256]{2,1,0:T(8,128)(2,1)S(1)}, u32[]{:S(2)}, u32[]{:S(2)}) collective-permute-start(bf16[4,256,256]{2,1,0:T(8,128)(2,1)S(1)} %get-tuple-element.133), channel_id=1, source_target_pairs={{0,4},{4,0},{8,12},{12,8},{16,20},{20,16},{24,28},{28,24},{1,5},{5... | collective-permute-start | bytes 1572872 | tf_op jit(solution)/shard_map/ppermute | solution.py:644
  29.8 1.1 %collective-permute-done.6.half_t = bf16[2,256,512]{2,1,0:T(8,128)(2,1)S(1)} collective-permute-done((bf16[2,256,512]{2,1,0:T(8,128)(2,1)S(1)}, bf16[2,256,512]{2,1,0:T(8,128)(2,1)S(1)}, u32[]{:S(2)}, u32[]{:S(2)}) %collective-permute-start.6) | collective-permute-done | bytes 524320 | tf_op jit(solution)/shard_map/ppermute | solution.py:641
  30.8 4.3 %third.1 = (bf16[512,512]{1,0:T(8,128)(2,1)S(1)}, bf16[512,128]{1,0:T(8,128)(2,1)S(1)}, bf16[512,128]{1,0:T(8,128)(2,1)S(1)}, f32[8,512]{1,0:T(8,128)S(1)}) custom-call(s32[2]{0:T(128)S(1)} %copy-done.2, bf16[512,512]{1,0:T(8,128)(2,1)S(1)} %get-tuple-element.119.grad2_ref, f32[512,512]{1,0:T(8,128)S(1)} %get-tuple-element.120.conv_ref, ...), custom_call_target="tpu_custom_call" | custom-call | flops 21474836480 | bytes 1024 | tf_op jit(solution)/shard_map/third/pallas_call | solution.py:586
  35.1 2.3 %collective-permute-start.10 = (bf16[512,128]{1,0:T(8,128)(2,1)S(1)}, bf16[512,128]{1,0:T(8,128)(2,1)S(1)}, u32[]{:S(2)}, u32[]{:S(2)}) collective-permute-start(bf16[512,128]{1,0:T(8,128)(2,1)S(1)} %get-tuple-element.139), channel_id=1, source_target_pairs={{0,2},{1,3},{2,0},{3,1},{4,6},{5,7},{6,4},{7,5},{8,10},{9,11},{10,... | collective-permute-start | bytes 393224 | tf_op jit(solution)/shard_map/ppermute | solution.py:641
  37.5 3.3 %weight2.5 = (bf16[4,576,128]{2,1,0:T(8,128)(2,1)S(1)}, bf16[4,576,128]{2,1,0:T(8,128)(2,1)S(1)}) custom-call(s32[2]{0:T(128)S(1)} %copy-done.2, bf16[512,512]{1,0:T(8,128)(2,1)S(1)} %get-tuple-element.127.act_t, bf16[2,256,512]{2,1,0:T(8,128)(2,1)S(1)} %collective-permute-done.6.half_t, bf16[2,256,512]{2,1,0:T(8,128)(2,1)S(1)} %collective-permute-done.7.partner_half_t, ...), custom_call_target="tpu_custom_call" | custom-call | flops 1073741824 | bytes 1024 | tf_op jit(solution)/shard_map/weight2/pallas_call | solution.py:586
  40.8 1.3 %collective-permute-start.17 = (bf16[4,576,128]{2,1,0:T(8,128)(2,1)S(1)}, bf16[4,576,128]{2,1,0:T(8,128)(2,1)S(1)}, u32[]{:S(2)}, u32[]{:S(2)}) collective-permute-start(bf16[4,576,128]{2,1,0:T(8,128)(2,1)S(1)} %get-tuple-element.131), channel_id=1, source_target_pairs={{0,4},{4,0},{8,12},{12,8},{16,20},{20,16},{24,28},{28,24},{1,5},{5... | collective-permute-start | bytes 1769480 | tf_op jit(solution)/shard_map/ppermute | solution.py:644
  42.1 0.1 routea1.1
  42.3 3.7 %collective-permute-start.16 = (bf16[1,256,256]{2,1,0:T(8,128)(2,1)S(1)}, bf16[1,256,256]{2,1,0:T(8,128)(2,1)S(1)}, u32[]{:S(2)}, u32[]{:S(2)}) collective-permute-start(bf16[1,256,256]{2,1,0:T(8,128)(2,1)S(1)} %get-tuple-element.137), channel_id=1, source_target_pairs={{0,24},{4,28},{8,16},{12,20},{16,8},{20,12},{24,0},{28,4},{1,25},{... | collective-permute-start | bytes 393224 | tf_op jit(solution)/shard_map/ppermute | solution.py:644
  45.9 0.8 collective-permute-start.14
  46.7 3.1 %weight1.4 = (bf16[4,576,128]{2,1,0:T(8,128)(2,1)S(1)}, bf16[4,576,128]{2,1,0:T(8,128)(2,1)S(1)}) custom-call(s32[2]{0:T(128)S(1)} %copy-done.2, bf16[512,512]{1,0:T(8,128)(2,1)S(1)} %get-tuple-element.123.act_t, bf16[2,256,512]{2,1,0:T(8,128)(2,1)S(1)} %collective-permute-done.6.half_t, bf16[2,256,512]{2,1,0:T(8,128)(2,1)S(1)} %collective-permute-done.7.partner_half_t, ...), custom_call_target="tpu_custom_call" | custom-call | flops 3221225472 | bytes 1024 | tf_op jit(solution)/shard_map/weight1/pallas_call | solution.py:586
  49.8 1.4 %collective-permute-start.13 = (bf16[4,576,128]{2,1,0:T(8,128)(2,1)S(1)}, bf16[4,576,128]{2,1,0:T(8,128)(2,1)S(1)}, u32[]{:S(2)}, u32[]{:S(2)}) collective-permute-start(bf16[4,576,128]{2,1,0:T(8,128)(2,1)S(1)} %get-tuple-element.140), channel_id=1, source_target_pairs={{0,4},{4,0},{8,12},{12,8},{16,20},{20,16},{24,28},{28,24},{1,5},{5... | collective-permute-start | bytes 1769480 | tf_op jit(solution)/shard_map/ppermute | solution.py:644
  51.2 5.0 %fourth.1 = (bf16[192,512]{1,0:T(8,128)(2,1)S(1)}, bf16[192,512]{1,0:T(8,128)(2,1)S(1)}, bf16[2,128,512]{2,1,0:T(8,128)(2,1)S(1)}, bf16[4,16,128]{2,1,0:T(8,128)(2,1)S(1)}, bf16[4,16,128]{2,1,0:T(8,128)(2,1)S(1)}) custom-call(s32[2]{0:T(128)S(1)} %copy-done.2, bf16[512,512]{1,0:T(8,128)(2,1)S(1)} %get-tuple-element.141.grad1_ref, ...), custom_call_target="tpu_custom_call" | custom-call | flops 10737418240 | bytes 1024 | tf_op jit(solution)/shard_map/fourth/pallas_call | solution.py:586
  56.2 0.9 collective-permute-done.15.refs_2_
  57.1 0.1 sumroutea.1.own_ref
  57.2 0.1 routeb1.1
  57.4 1.2 %collective-permute-start.18 = (bf16[1,576,128]{2,1,0:T(8,128)(2,1)S(1)}, bf16[1,576,128]{2,1,0:T(8,128)(2,1)S(1)}, u32[]{:S(2)}, u32[]{:S(2)}) collective-permute-start(bf16[1,576,128]{2,1,0:T(8,128)(2,1)S(1)} %get-tuple-element.164), channel_id=1, source_target_pairs={{0,8},{4,12},{8,0},{12,4},{16,24},{20,28},{24,16},{28,20},{1,9},{5... | collective-permute-start | bytes 442376 | tf_op jit(solution)/shard_map/ppermute | solution.py:644
  58.6 2.6 %collective-permute-start.19 = (bf16[1,576,128]{2,1,0:T(8,128)(2,1)S(1)}, bf16[1,576,128]{2,1,0:T(8,128)(2,1)S(1)}, u32[]{:S(2)}, u32[]{:S(2)}) collective-permute-start(bf16[1,576,128]{2,1,0:T(8,128)(2,1)S(1)} %get-tuple-element.165), channel_id=1, source_target_pairs={{0,16},{4,20},{8,24},{12,28},{16,0},{20,4},{24,8},{28,12},{1,17},{... | collective-permute-start | bytes 442376 | tf_op jit(solution)/shard_map/ppermute | solution.py:644
  61.2 0.7 collective-permute-start.20
  61.8 1.1 %collective-permute-start.12 = (bf16[4,16,128]{2,1,0:T(8,128)(2,1)S(1)}, bf16[4,16,128]{2,1,0:T(8,128)(2,1)S(1)}, u32[]{:S(2)}, u32[]{:S(2)}) collective-permute-start(bf16[4,16,128]{2,1,0:T(8,128)(2,1)S(1)} %get-tuple-element.151), channel_id=1, source_target_pairs={{0,4},{4,0},{8,12},{12,8},{16,20},{20,16},{24,28},{28,24},{1,5},{5... | collective-permute-start | bytes 49160 | tf_op jit(solution)/shard_map/ppermute | solution.py:644
  62.9 6.4 %collective-permute-done.12.got_ref = bf16[4,16,128]{2,1,0:T(8,128)(2,1)S(1)} collective-permute-done((bf16[4,16,128]{2,1,0:T(8,128)(2,1)S(1)}, bf16[4,16,128]{2,1,0:T(8,128)(2,1)S(1)}, u32[]{:S(2)}, u32[]{:S(2)}) %collective-permute-start.12) | collective-permute-done | bytes 16416 | tf_op jit(solution)/shard_map/ppermute | solution.py:644
  69.3 0.3 collective-permute-start.23
  69.6 1.7 %collective-permute-start.11 = (bf16[2,128,512]{2,1,0:T(8,128)(2,1)S(1)}, bf16[2,128,512]{2,1,0:T(8,128)(2,1)S(1)}, u32[]{:S(2)}, u32[]{:S(2)}) collective-permute-start(bf16[2,128,512]{2,1,0:T(8,128)(2,1)S(1)} %get-tuple-element.149), channel_id=1, source_target_pairs={{0,2},{1,3},{2,0},{3,1},{4,6},{5,7},{6,4},{7,5},{8,10},{9,11},{10,... | collective-permute-start | bytes 786440 | tf_op jit(solution)/shard_map/ppermute | solution.py:641
  71.3 0.1 routec1.1
  71.5 0.1 collective-permute-done.19.refs_2_
  71.6 3.4 %collective-permute-start.25 = (bf16[1,592,128]{2,1,0:T(8,128)(2,1)S(1)}, bf16[1,592,128]{2,1,0:T(8,128)(2,1)S(1)}, u32[]{:S(2)}, u32[]{:S(2)}) collective-permute-start(bf16[1,592,128]{2,1,0:T(8,128)(2,1)S(1)} %get-tuple-element.177), channel_id=1, source_target_pairs={{0,24},{4,28},{8,16},{12,20},{16,8},{20,12},{24,0},{28,4},{1,25},{... | collective-permute-start | bytes 454664 | tf_op jit(solution)/shard_map/ppermute | solution.py:644
  75.0 0.2 collective-permute-start.24
  75.2 0.8 collective-permute-start.21
  76.0 0.1 sumrouteb.1.own_ref
  76.1 0.4 collective-permute-start.22
  76.5 6.4 %collective-permute-done.22.far_ref = bf16[576,128]{1,0:T(8,128)(2,1)S(1)} collective-permute-done((bf16[576,128]{1,0:T(8,128)(2,1)S(1)}, bf16[576,128]{1,0:T(8,128)(2,1)S(1)}, u32[]{:S(2)}, u32[]{:S(2)}) %collective-permute-start.22) | collective-permute-done | bytes 147488 | tf_op jit(solution)/shard_map/ppermute | solution.py:641
  82.9 4.0 %collective-permute-done.24.refs_2_ = bf16[1,592,128]{2,1,0:T(8,128)(2,1)S(1)} collective-permute-done((bf16[1,592,128]{2,1,0:T(8,128)(2,1)S(1)}, bf16[1,592,128]{2,1,0:T(8,128)(2,1)S(1)}, u32[]{:S(2)}, u32[]{:S(2)}) %collective-permute-start.24) | collective-permute-done | bytes 151584 | tf_op jit(solution)/shard_map/ppermute | solution.py:644
  86.9 0.1 sumroutec.1.own_ref
  87.0 0.5 collective-permute-start.26
  87.5 0.5 collective-permute-start.29
  88.0 0.5 collective-permute-start.31
  88.5 1.5 %unpack.1 = (bf16[2,6,32,512]{3,2,1,0:T(8,128)(2,1)}, bf16[2,6,32,512]{3,2,1,0:T(8,128)(2,1)}) custom-call(s32[2]{0:T(128)S(1)} %copy-done.2, bf16[192,512]{1,0:T(8,128)(2,1)S(1)} %get-tuple-element.147.out_own, bf16[192,512]{1,0:T(8,128)(2,1)S(1)} %get-tuple-element.148.grad_own, bf16[2,128,512]{2,1,0:T(8,128)(2,1)S(1)} %collective-permute-done.11.away_ref), custom_call_target="tpu_custom_call" | custom-call | flops 21474836 | bytes 1024 | tf_op jit(solution)/shard_map/unpack/pallas_call | solution.py:586
  90.0 0.0 collective-permute-start.27
  90.0 0.9 joina.1
  90.9 1.2 %joinb.1 = f32[576,512]{1,0:T(8,128)} custom-call(bf16[576,128]{1,0:T(8,128)(2,1)S(1)} %sumrouteb.1.own_ref, bf16[576,128]{1,0:T(8,128)(2,1)S(1)} %collective-permute-done.22.far_ref, bf16[576,128]{1,0:T(8,128)(2,1)S(1)} %collective-permute-done.28.near_ref, bf16[576,128]{1,0:T(8,128)(2,1)S(1)} %collective-permute-done.29.diagonal_ref), custom_call_target="tpu_custom_call" | custom-call | flops 21474836 | bytes 1024 | tf_op jit(solution)/shard_map/joinb/pallas_call | solution.py:586
  92.1 0.2 collective-permute-done.26.far_ref
  92.2 0.3 collective-permute-start.32
  92.6 1.0 %collective-permute-done.32.diagonal_ref = bf16[592,128]{1,0:T(8,128)(2,1)S(1)} collective-permute-done((bf16[592,128]{1,0:T(8,128)(2,1)S(1)}, bf16[592,128]{1,0:T(8,128)(2,1)S(1)}, u32[]{:S(2)}, u32[]{:S(2)}) %collective-permute-start.32) | collective-permute-done | bytes 151584 | tf_op jit(solution)/shard_map/ppermute | solution.py:638
  93.6 1.2 %joinc.1 = (f32[576,512]{1,0:T(8,128)}, f32[1,64]{1,0:T(1,128)}, f32[1,64]{1,0:T(1,128)}, f32[1,64]{1,0:T(1,128)}, f32[1,64]{1,0:T(1,128)}, /*index=5*/f32[1,64]...) custom-call(bf16[592,128]{1,0:T(8,128)(2,1)S(1)} %sumroutec.1.own_re, ...), custom_call_target="tpu_custom_call" | custom-call | flops 21474836 | bytes 1024 | tf_op jit(solution)/shard_map/joinc/pallas_call | solution.py:586
  (69 shorter events, 0.2 us)
Async XLA Ops:
  0.7 5.1 %copy-start.8 = (f32[512]{0:T(512)S(1)}, f32[512]{0:T(512)}, u32[]{:S(2)}) copy-start(f32[512]{0:T(512)} %param.22) | copy-start | bytes 6148
  0.7 5.1 %copy-start.9 = (f32[512]{0:T(512)S(1)}, f32[512]{0:T(512)}, u32[]{:S(2)}) copy-start(f32[512]{0:T(512)} %param.23) | copy-start | bytes 6148
  0.7 5.1 %copy-start.18 = (f32[512]{0:T(512)S(1)}, f32[512]{0:T(512)}, u32[]{:S(2)}) copy-start(f32[512]{0:T(512)} %param.38) | copy-start | bytes 6148
  0.7 5.1 %copy-start.10 = (f32[512]{0:T(512)S(1)}, f32[512]{0:T(512)}, u32[]{:S(2)}) copy-start(f32[512]{0:T(512)} %param.25) | copy-start | bytes 6148
  0.7 5.1 %copy-start.11 = (f32[512]{0:T(512)S(1)}, f32[512]{0:T(512)}, u32[]{:S(2)}) copy-start(f32[512]{0:T(512)} %param.26) | copy-start | bytes 6148
  0.7 5.1 %copy-start.12 = (f32[512]{0:T(512)S(1)}, f32[512]{0:T(512)}, u32[]{:S(2)}) copy-start(f32[512]{0:T(512)} %param.27) | copy-start | bytes 6148
  0.7 5.1 %copy-start.13 = (f32[512]{0:T(512)S(1)}, f32[512]{0:T(512)}, u32[]{:S(2)}) copy-start(f32[512]{0:T(512)} %param.29) | copy-start | bytes 6148
  0.7 5.1 %copy-start.14 = (f32[512]{0:T(512)S(1)}, f32[512]{0:T(512)}, u32[]{:S(2)}) copy-start(f32[512]{0:T(512)} %param.30) | copy-start | bytes 6148
  0.7 5.1 %copy-start.15 = (f32[512]{0:T(512)S(1)}, f32[512]{0:T(512)}, u32[]{:S(2)}) copy-start(f32[512]{0:T(512)} %param.31) | copy-start | bytes 6148
  0.8 5.1 %copy-start.16 = (f32[512]{0:T(512)S(1)}, f32[512]{0:T(512)}, u32[]{:S(2)}) copy-start(f32[512]{0:T(512)} %param.33) | copy-start | bytes 6148
  0.8 5.1 %copy-start.17 = (f32[512]{0:T(512)S(1)}, f32[512]{0:T(512)}, u32[]{:S(2)}) copy-start(f32[512]{0:T(512)} %param.36) | copy-start | bytes 6148
  0.8 5.1 %copy-start.7 = (bf16[2,6,32,512]{3,2,1,0:T(8,128)(2,1)S(1)}, bf16[2,6,32,512]{3,2,1,0:T(8,128)(2,1)}, u32[]{:S(2)}) copy-start(bf16[2,6,32,512]{3,2,1,0:T(8,128)(2,1)} %cot_ref.1) | copy-start | bytes 1179652
  0.8 10.3 %slice-start = ((s8[4718592]{0:T(1024)(128)(4,1)}), s8[524288]{0:T(1024)(128)(4,1)S(1)}, s32[]{:S(2)}) async-start(s8[4718592]{0:T(1024)(128)(4,1)} %bitcast.22), calls=%async_computation | async-start | bytes 1048576
  0.8 17.5 %slice-start.2 = ((s8[4718592]{0:T(1024)(128)(4,1)}), s8[4194304]{0:T(1024)(128)(4,1)S(1)}, s32[]{:S(2)}) async-start(s8[4718592]{0:T(1024)(128)(4,1)} %bitcast.24), calls=%async_computation.2 | async-start | bytes 8388608
  2.7 6.7 %collective-permute-start.1 = (bf16[128,512]{1,0:T(8,128)(2,1)}, bf16[128,512]{1,0:T(8,128)(2,1)S(1)}, u32[]{:S(2)}, u32[]{:S(2)}) collective-permute-start(bf16[128,512]{1,0:T(8,128)(2,1)} %get-tuple-element.112), channel_id=1, source_target_pairs={{0,2},{1,3},{2,0},{3,1},{4,6},{5,7},{6,4},{7,5},{8,10},{9,11},{10,... | collective-permute-start | bytes 393224 | tf_op jit(solution)/shard_map/ppermute | solution.py:641
  5.8 4.3 %collective-permute-start = (bf16[192,512]{1,0:T(8,128)(2,1)}, bf16[192,512]{1,0:T(8,128)(2,1)S(1)}, u32[]{:S(2)}, u32[]{:S(2)}) collective-permute-start(bf16[192,512]{1,0:T(8,128)(2,1)} %get-tuple-element.111.own), channel_id=1, source_target_pairs={{0,1},{1,0},{2,3},{3,2},{4,5},{5,4},{6,7},{7,6},{8,9},{9,8},{10,11... | collective-permute-start | bytes 589832 | tf_op jit(solution)/shard_map/ppermute | solution.py:638
  5.8 5.3 %slice-start.1 = ((s8[4718592]{0:T(1024)(128)(4,1)}), s8[4194304]{0:T(1024)(128)(4,1)S(1)}, s32[]{:S(2)}) async-start(s8[4718592]{0:T(1024)(128)(4,1)} %bitcast.22), calls=%async_computation.1 | async-start | bytes 8388608
  5.9 0.8 copy-start.1
  6.7 4.4 %copy-start = (bf16[192,512]{1,0:T(8,128)(2,1)S(1)}, bf16[192,512]{1,0:T(8,128)(2,1)}, u32[]{:S(2)}) copy-start(bf16[192,512]{1,0:T(8,128)(2,1)} %get-tuple-element.111.own) | copy-start | bytes 589828
  6.7 4.4 %copy-start.2 = (s32[2]{0:T(128)S(1)}, s32[2]{0:T(128)}, u32[]{:S(2)}) copy-start(s32[2]{0:T(128)} %get-tuple-element.110.kinds.bucket_ref) | copy-start | bytes 28
  6.7 11.6 %slice-start.3 = ((s8[4718592]{0:T(1024)(128)(4,1)}), s8[524288]{0:T(1024)(128)(4,1)S(1)}, s32[]{:S(2)}) async-start(s8[4718592]{0:T(1024)(128)(4,1)} %bitcast.24), calls=%async_computation.3 | async-start | bytes 1048576
  7.3 11.1 %copy-start.3 = (bf16[512,512]{1,0:T(8,128)(2,1)S(1)}, bf16[512,512]{1,0:T(8,128)(2,1)}, u32[]{:S(2)}) copy-start(bf16[512,512]{1,0:T(8,128)(2,1)} %wq.1) | copy-start | bytes 1572868
  7.3 11.0 %copy-start.4 = (bf16[512,512]{1,0:T(8,128)(2,1)S(1)}, bf16[512,512]{1,0:T(8,128)(2,1)}, u32[]{:S(2)}) copy-start(bf16[512,512]{1,0:T(8,128)(2,1)} %wk.1) | copy-start | bytes 1572868
  7.3 11.0 %copy-start.5 = (bf16[512,512]{1,0:T(8,128)(2,1)S(1)}, bf16[512,512]{1,0:T(8,128)(2,1)}, u32[]{:S(2)}) copy-start(bf16[512,512]{1,0:T(8,128)(2,1)} %wv.1) | copy-start | bytes 1572868
  7.3 11.0 %copy-start.6 = (bf16[512,512]{1,0:T(8,128)(2,1)S(1)}, bf16[512,512]{1,0:T(8,128)(2,1)}, u32[]{:S(2)}) copy-start(bf16[512,512]{1,0:T(8,128)(2,1)} %wp.3) | copy-start | bytes 1572868
  7.3 11.0 %collective-permute-start.3 = (bf16[192,512]{1,0:T(8,128)(2,1)S(1)}, bf16[192,512]{1,0:T(8,128)(2,1)S(1)}, u32[]{:S(2)}, u32[]{:S(2)}) collective-permute-start(bf16[192,512]{1,0:T(8,128)(2,1)S(1)} %get-tuple-element.117.own), channel_id=1, source_target_pairs={{0,1},{1,0},{2,3},{3,2},{4,5},{5,4},{6,7},{7,6},{8,9},{9,8},{10,11... | collective-permute-start | bytes 589832 | tf_op jit(solution)/shard_map/ppermute | solution.py:638
  7.9 10.4 %collective-permute-start.4 = (bf16[160,512]{1,0:T(8,128)(2,1)S(1)}, bf16[160,512]{1,0:T(8,128)(2,1)S(1)}, u32[]{:S(2)}, u32[]{:S(2)}) collective-permute-start(bf16[160,512]{1,0:T(8,128)(2,1)S(1)} %get-tuple-element.118), channel_id=1, source_target_pairs={{0,2},{1,3},{2,0},{3,1},{4,6},{5,7},{6,4},{7,5},{8,10},{9,11},{10,... | collective-permute-start | bytes 491528 | tf_op jit(solution)/shard_map/ppermute | solution.py:641
  8.0 10.3 %collective-permute-start.5 = (bf16[160,512]{1,0:T(8,128)(2,1)S(1)}, bf16[160,512]{1,0:T(8,128)(2,1)S(1)}, u32[]{:S(2)}, u32[]{:S(2)}) collective-permute-start(bf16[160,512]{1,0:T(8,128)(2,1)S(1)} %get-tuple-element.118), channel_id=1, source_target_pairs={{0,3},{1,2},{2,1},{3,0},{4,7},{5,6},{6,5},{7,4},{8,11},{9,10},{10,... | collective-permute-start | bytes 491528 | tf_op jit(solution)/shard_map/ppermute | solution.py:674
  9.5 1.6 %collective-permute-start.2 = (bf16[128,512]{1,0:T(8,128)(2,1)S(1)}, bf16[128,512]{1,0:T(8,128)(2,1)S(1)}, u32[]{:S(2)}, u32[]{:S(2)}) collective-permute-start(bf16[128,512]{1,0:T(8,128)(2,1)S(1)} %collective-permute-done.1.received), channel_id=1, source_target_pairs={{0,1},{1,0},{2,3},{3,2},{4,5},{5,4},{6,7},{7,6},{8,9},{9,8},{10,11... | collective-permute-start | bytes 393224 | tf_op jit(solution)/shard_map/ppermute | solution.py:638
  16.4 14.4 %collective-permute-start.6 = (bf16[2,256,512]{2,1,0:T(8,128)(2,1)S(1)}, bf16[2,256,512]{2,1,0:T(8,128)(2,1)S(1)}, u32[]{:S(2)}, u32[]{:S(2)}) collective-permute-start(bf16[2,256,512]{2,1,0:T(8,128)(2,1)S(1)} %get-tuple-element.124), channel_id=1, source_target_pairs={{0,2},{1,3},{2,0},{3,1},{4,6},{5,7},{6,4},{7,5},{8,10},{9,11},{10,... | collective-permute-start | bytes 1572872 | tf_op jit(solution)/shard_map/ppermute | solution.py:641
  28.0 9.5 %collective-permute-start.8 = (bf16[512,128]{1,0:T(8,128)(2,1)S(1)}, bf16[512,128]{1,0:T(8,128)(2,1)S(1)}, u32[]{:S(2)}, u32[]{:S(2)}) collective-permute-start(bf16[512,128]{1,0:T(8,128)(2,1)S(1)} %get-tuple-element.130), channel_id=1, source_target_pairs={{0,2},{1,3},{2,0},{3,1},{4,6},{5,7},{6,4},{7,5},{8,10},{9,11},{10,... | collective-permute-start | bytes 393224 | tf_op jit(solution)/shard_map/ppermute | solution.py:641
  28.3 13.9 %collective-permute-start.9 = (bf16[4,256,256]{2,1,0:T(8,128)(2,1)S(1)}, bf16[4,256,256]{2,1,0:T(8,128)(2,1)S(1)}, u32[]{:S(2)}, u32[]{:S(2)}) collective-permute-start(bf16[4,256,256]{2,1,0:T(8,128)(2,1)S(1)} %get-tuple-element.133), channel_id=1, source_target_pairs={{0,4},{4,0},{8,12},{12,8},{16,20},{20,16},{24,28},{28,24},{1,5},{5... | collective-permute-start | bytes 1572872 | tf_op jit(solution)/shard_map/ppermute | solution.py:644
  30.8 6.7 %collective-permute-start.7 = (bf16[2,256,512]{2,1,0:T(8,128)(2,1)S(1)}, bf16[2,256,512]{2,1,0:T(8,128)(2,1)S(1)}, u32[]{:S(2)}, u32[]{:S(2)}) collective-permute-start(bf16[2,256,512]{2,1,0:T(8,128)(2,1)S(1)} %collective-permute-done.6.half_t), channel_id=1, source_target_pairs={{0,1},{1,0},{2,3},{3,2},{4,5},{5,4},{6,7},{7,6},{8,9},{9,8},{10,11... | collective-permute-start | bytes 1572872 | tf_op jit(solution)/shard_map/ppermute | solution.py:638
  35.1 11.6 %collective-permute-start.10 = (bf16[512,128]{1,0:T(8,128)(2,1)S(1)}, bf16[512,128]{1,0:T(8,128)(2,1)S(1)}, u32[]{:S(2)}, u32[]{:S(2)}) collective-permute-start(bf16[512,128]{1,0:T(8,128)(2,1)S(1)} %get-tuple-element.139), channel_id=1, source_target_pairs={{0,2},{1,3},{2,0},{3,1},{4,6},{5,7},{6,4},{7,5},{8,10},{9,11},{10,... | collective-permute-start | bytes 393224 | tf_op jit(solution)/shard_map/ppermute | solution.py:641
  40.8 16.4 %collective-permute-start.17 = (bf16[4,576,128]{2,1,0:T(8,128)(2,1)S(1)}, bf16[4,576,128]{2,1,0:T(8,128)(2,1)S(1)}, u32[]{:S(2)}, u32[]{:S(2)}) collective-permute-start(bf16[4,576,128]{2,1,0:T(8,128)(2,1)S(1)} %get-tuple-element.131), channel_id=1, source_target_pairs={{0,4},{4,0},{8,12},{12,8},{16,20},{20,16},{24,28},{28,24},{1,5},{5... | collective-permute-start | bytes 1769480 | tf_op jit(solution)/shard_map/ppermute | solution.py:644
  42.3 13.9 %collective-permute-start.16 = (bf16[1,256,256]{2,1,0:T(8,128)(2,1)S(1)}, bf16[1,256,256]{2,1,0:T(8,128)(2,1)S(1)}, u32[]{:S(2)}, u32[]{:S(2)}) collective-permute-start(bf16[1,256,256]{2,1,0:T(8,128)(2,1)S(1)} %get-tuple-element.137), channel_id=1, source_target_pairs={{0,24},{4,28},{8,16},{12,20},{16,8},{20,12},{24,0},{28,4},{1,25},{... | collective-permute-start | bytes 393224 | tf_op jit(solution)/shard_map/ppermute | solution.py:644
  45.9 11.2 %collective-permute-start.15 = (bf16[1,256,256]{2,1,0:T(8,128)(2,1)S(1)}, bf16[1,256,256]{2,1,0:T(8,128)(2,1)S(1)}, u32[]{:S(2)}, u32[]{:S(2)}) collective-permute-start(bf16[1,256,256]{2,1,0:T(8,128)(2,1)S(1)} %get-tuple-element.136), channel_id=1, source_target_pairs={{0,16},{4,20},{8,24},{12,28},{16,0},{20,4},{24,8},{28,12},{1,17},{... | collective-permute-start | bytes 393224 | tf_op jit(solution)/shard_map/ppermute | solution.py:644
  45.9 11.2 %collective-permute-start.14 = (bf16[1,256,256]{2,1,0:T(8,128)(2,1)S(1)}, bf16[1,256,256]{2,1,0:T(8,128)(2,1)S(1)}, u32[]{:S(2)}, u32[]{:S(2)}) collective-permute-start(bf16[1,256,256]{2,1,0:T(8,128)(2,1)S(1)} %get-tuple-element.135), channel_id=1, source_target_pairs={{0,8},{4,12},{8,0},{12,4},{16,24},{20,28},{24,16},{28,20},{1,9},{5... | collective-permute-start | bytes 393224 | tf_op jit(solution)/shard_map/ppermute | solution.py:644
  49.8 19.8 %collective-permute-start.13 = (bf16[4,576,128]{2,1,0:T(8,128)(2,1)S(1)}, bf16[4,576,128]{2,1,0:T(8,128)(2,1)S(1)}, u32[]{:S(2)}, u32[]{:S(2)}) collective-permute-start(bf16[4,576,128]{2,1,0:T(8,128)(2,1)S(1)} %get-tuple-element.140), channel_id=1, source_target_pairs={{0,4},{4,0},{8,12},{12,8},{16,20},{20,16},{24,28},{28,24},{1,5},{5... | collective-permute-start | bytes 1769480 | tf_op jit(solution)/shard_map/ppermute | solution.py:644
  57.4 14.2 %collective-permute-start.18 = (bf16[1,576,128]{2,1,0:T(8,128)(2,1)S(1)}, bf16[1,576,128]{2,1,0:T(8,128)(2,1)S(1)}, u32[]{:S(2)}, u32[]{:S(2)}) collective-permute-start(bf16[1,576,128]{2,1,0:T(8,128)(2,1)S(1)} %get-tuple-element.164), channel_id=1, source_target_pairs={{0,8},{4,12},{8,0},{12,4},{16,24},{20,28},{24,16},{28,20},{1,9},{5... | collective-permute-start | bytes 442376 | tf_op jit(solution)/shard_map/ppermute | solution.py:644
  58.6 13.0 %collective-permute-start.19 = (bf16[1,576,128]{2,1,0:T(8,128)(2,1)S(1)}, bf16[1,576,128]{2,1,0:T(8,128)(2,1)S(1)}, u32[]{:S(2)}, u32[]{:S(2)}) collective-permute-start(bf16[1,576,128]{2,1,0:T(8,128)(2,1)S(1)} %get-tuple-element.165), channel_id=1, source_target_pairs={{0,16},{4,20},{8,24},{12,28},{16,0},{20,4},{24,8},{28,12},{1,17},{... | collective-permute-start | bytes 442376 | tf_op jit(solution)/shard_map/ppermute | solution.py:644
  61.2 10.4 %collective-permute-start.20 = (bf16[1,576,128]{2,1,0:T(8,128)(2,1)S(1)}, bf16[1,576,128]{2,1,0:T(8,128)(2,1)S(1)}, u32[]{:S(2)}, u32[]{:S(2)}) collective-permute-start(bf16[1,576,128]{2,1,0:T(8,128)(2,1)S(1)} %get-tuple-element.166), channel_id=1, source_target_pairs={{0,24},{4,28},{8,16},{12,20},{16,8},{20,12},{24,0},{28,4},{1,25},{... | collective-permute-start | bytes 442376 | tf_op jit(solution)/shard_map/ppermute | solution.py:644
  61.8 7.5 %collective-permute-start.12 = (bf16[4,16,128]{2,1,0:T(8,128)(2,1)S(1)}, bf16[4,16,128]{2,1,0:T(8,128)(2,1)S(1)}, u32[]{:S(2)}, u32[]{:S(2)}) collective-permute-start(bf16[4,16,128]{2,1,0:T(8,128)(2,1)S(1)} %get-tuple-element.151), channel_id=1, source_target_pairs={{0,4},{4,0},{8,12},{12,8},{16,20},{20,16},{24,28},{28,24},{1,5},{5... | collective-permute-start | bytes 49160 | tf_op jit(solution)/shard_map/ppermute | solution.py:644
  69.3 6.8 %collective-permute-start.23 = (bf16[256,256]{1,0:T(8,128)(2,1)S(1)}, bf16[256,256]{1,0:T(8,128)(2,1)S(1)}, u32[]{:S(2)}, u32[]{:S(2)}) collective-permute-start(bf16[256,256]{1,0:T(8,128)(2,1)S(1)} %sumroutea.1.own_ref), channel_id=1, source_target_pairs={{0,2},{1,3},{2,0},{3,1},{4,6},{5,7},{6,4},{7,5},{8,10},{9,11},{10,... | collective-permute-start | bytes 393224 | tf_op jit(solution)/shard_map/ppermute | solution.py:641
  69.6 18.4 %collective-permute-start.11 = (bf16[2,128,512]{2,1,0:T(8,128)(2,1)S(1)}, bf16[2,128,512]{2,1,0:T(8,128)(2,1)S(1)}, u32[]{:S(2)}, u32[]{:S(2)}) collective-permute-start(bf16[2,128,512]{2,1,0:T(8,128)(2,1)S(1)} %get-tuple-element.149), channel_id=1, source_target_pairs={{0,2},{1,3},{2,0},{3,1},{4,6},{5,7},{6,4},{7,5},{8,10},{9,11},{10,... | collective-permute-start | bytes 786440 | tf_op jit(solution)/shard_map/ppermute | solution.py:641
  71.6 11.3 %collective-permute-start.25 = (bf16[1,592,128]{2,1,0:T(8,128)(2,1)S(1)}, bf16[1,592,128]{2,1,0:T(8,128)(2,1)S(1)}, u32[]{:S(2)}, u32[]{:S(2)}) collective-permute-start(bf16[1,592,128]{2,1,0:T(8,128)(2,1)S(1)} %get-tuple-element.177), channel_id=1, source_target_pairs={{0,24},{4,28},{8,16},{12,20},{16,8},{20,12},{24,0},{28,4},{1,25},{... | collective-permute-start | bytes 454664 | tf_op jit(solution)/shard_map/ppermute | solution.py:644
  75.0 11.9 %collective-permute-start.24 = (bf16[1,592,128]{2,1,0:T(8,128)(2,1)S(1)}, bf16[1,592,128]{2,1,0:T(8,128)(2,1)S(1)}, u32[]{:S(2)}, u32[]{:S(2)}) collective-permute-start(bf16[1,592,128]{2,1,0:T(8,128)(2,1)S(1)} %get-tuple-element.174), channel_id=1, source_target_pairs={{0,16},{4,20},{8,24},{12,28},{16,0},{20,4},{24,8},{28,12},{1,17},{... | collective-permute-start | bytes 454664 | tf_op jit(solution)/shard_map/ppermute | solution.py:644
  75.2 11.7 %collective-permute-start.21 = (bf16[1,592,128]{2,1,0:T(8,128)(2,1)S(1)}, bf16[1,592,128]{2,1,0:T(8,128)(2,1)S(1)}, u32[]{:S(2)}, u32[]{:S(2)}) collective-permute-start(bf16[1,592,128]{2,1,0:T(8,128)(2,1)S(1)} %get-tuple-element.167), channel_id=1, source_target_pairs={{0,8},{4,12},{8,0},{12,4},{16,24},{20,28},{24,16},{28,20},{1,9},{5... | collective-permute-start | bytes 454664 | tf_op jit(solution)/shard_map/ppermute | solution.py:644
  76.1 6.8 %collective-permute-start.22 = (bf16[576,128]{1,0:T(8,128)(2,1)S(1)}, bf16[576,128]{1,0:T(8,128)(2,1)S(1)}, u32[]{:S(2)}, u32[]{:S(2)}) collective-permute-start(bf16[576,128]{1,0:T(8,128)(2,1)S(1)} %sumrouteb.1.own_ref), channel_id=1, source_target_pairs={{0,2},{1,3},{2,0},{3,1},{4,6},{5,7},{6,4},{7,5},{8,10},{9,11},{10,... | collective-permute-start | bytes 442376 | tf_op jit(solution)/shard_map/ppermute | solution.py:641
  87.0 5.3 %collective-permute-start.26 = (bf16[592,128]{1,0:T(8,128)(2,1)S(1)}, bf16[592,128]{1,0:T(8,128)(2,1)S(1)}, u32[]{:S(2)}, u32[]{:S(2)}) collective-permute-start(bf16[592,128]{1,0:T(8,128)(2,1)S(1)} %sumroutec.1.own_ref), channel_id=1, source_target_pairs={{0,2},{1,3},{2,0},{3,1},{4,6},{5,7},{6,4},{7,5},{8,10},{9,11},{10,... | collective-permute-start | bytes 454664 | tf_op jit(solution)/shard_map/ppermute | solution.py:641
  87.4 3.4 %collective-permute-start.28 = (bf16[576,128]{1,0:T(8,128)(2,1)S(1)}, bf16[576,128]{1,0:T(8,128)(2,1)S(1)}, u32[]{:S(2)}, u32[]{:S(2)}) collective-permute-start(bf16[576,128]{1,0:T(8,128)(2,1)S(1)} %sumrouteb.1.own_ref), channel_id=1, source_target_pairs={{0,1},{1,0},{2,3},{3,2},{4,5},{5,4},{6,7},{7,6},{8,9},{9,8},{10,11... | collective-permute-start | bytes 442376 | tf_op jit(solution)/shard_map/ppermute | solution.py:638
  87.5 3.4 %collective-permute-start.29 = (bf16[576,128]{1,0:T(8,128)(2,1)S(1)}, bf16[576,128]{1,0:T(8,128)(2,1)S(1)}, u32[]{:S(2)}, u32[]{:S(2)}) collective-permute-start(bf16[576,128]{1,0:T(8,128)(2,1)S(1)} %collective-permute-done.22.far_ref), channel_id=1, source_target_pairs={{0,1},{1,0},{2,3},{3,2},{4,5},{5,4},{6,7},{7,6},{8,9},{9,8},{10,11... | collective-permute-start | bytes 442376 | tf_op jit(solution)/shard_map/ppermute | solution.py:638
  88.0 2.0 %collective-permute-start.30 = (bf16[256,256]{1,0:T(8,128)(2,1)S(1)}, bf16[256,256]{1,0:T(8,128)(2,1)S(1)}, u32[]{:S(2)}, u32[]{:S(2)}) collective-permute-start(bf16[256,256]{1,0:T(8,128)(2,1)S(1)} %sumroutea.1.own_ref), channel_id=1, source_target_pairs={{0,1},{1,0},{2,3},{3,2},{4,5},{5,4},{6,7},{7,6},{8,9},{9,8},{10,11... | collective-permute-start | bytes 393224 | tf_op jit(solution)/shard_map/ppermute | solution.py:638
  88.0 2.0 %collective-permute-start.31 = (bf16[256,256]{1,0:T(8,128)(2,1)S(1)}, bf16[256,256]{1,0:T(8,128)(2,1)S(1)}, u32[]{:S(2)}, u32[]{:S(2)}) collective-permute-start(bf16[256,256]{1,0:T(8,128)(2,1)S(1)} %collective-permute-done.23.far_ref), channel_id=1, source_target_pairs={{0,1},{1,0},{2,3},{3,2},{4,5},{5,4},{6,7},{7,6},{8,9},{9,8},{10,11... | collective-permute-start | bytes 393224 | tf_op jit(solution)/shard_map/ppermute | solution.py:638
  90.0 2.6 %collective-permute-start.27 = (bf16[592,128]{1,0:T(8,128)(2,1)S(1)}, bf16[592,128]{1,0:T(8,128)(2,1)S(1)}, u32[]{:S(2)}, u32[]{:S(2)}) collective-permute-start(bf16[592,128]{1,0:T(8,128)(2,1)S(1)} %sumroutec.1.own_ref), channel_id=1, source_target_pairs={{0,1},{1,0},{2,3},{3,2},{4,5},{5,4},{6,7},{7,6},{8,9},{9,8},{10,11... | collective-permute-start | bytes 454664 | tf_op jit(solution)/shard_map/ppermute | solution.py:638
  92.2 1.4 %collective-permute-start.32 = (bf16[592,128]{1,0:T(8,128)(2,1)S(1)}, bf16[592,128]{1,0:T(8,128)(2,1)S(1)}, u32[]{:S(2)}, u32[]{:S(2)}) collective-permute-start(bf16[592,128]{1,0:T(8,128)(2,1)S(1)} %collective-permute-done.26.far_ref), channel_id=1, source_target_pairs={{0,1},{1,0},{2,3},{3,2},{4,5},{5,4},{6,7},{7,6},{8,9},{9,8},{10,11... | collective-permute-start | bytes 454664 | tf_op jit(solution)/shard_map/ppermute | solution.py:638

commit v8 on v7

--- a/solution.py
+++ b/solution.py
@@ -21,7 +21,7 @@
 HB = pl.BlockSpec(memory_space=pltpu.HBM)
 RATE = 1 << 30
 LENGTH = {
-    "pack": 10, "stack": 10, "first": 0.02, "second": 30, "third": 20, "fourth": 10, "weight2": 1, "weight1": 3, "routeb1": 20,
+    "pack": 10, "stack": 10, "first": 0.02, "second": 30, "third": 20, "fourth": 0.5, "weight2": 1, "weight1": 3, "routeb1": 20,
 }
 
 
@@ -419,9 +419,8 @@
 
 
 def fourth_kernel(
-    bucket_ref, grad1_ref, image_ref, stats_ref, grad_middle_ref, middle_ref, mixed_ref, vecs,
-    weight1, wp, vec_a, vec_b,
-    out_own, grad_own, send_ref, vec_keep, vec_send,
+    bucket_ref, grad1_ref, image_ref, stats_ref, grad_middle_ref, vecs, weight1, vec_a, vec_b,
+    grad_own, send_ref, vec_keep, vec_send,
     shift_ref, acc_ref, full_ref, vec_ref,
 ):
     h, home, away = place(bucket_ref)
@@ -429,9 +428,6 @@
     mask, pixels = pixel_mask(home)
     channels = vecs.shape[1]
     group_size = pixels * (channels // GROUPS)
-    projected = mm(mixed_ref[...], wp[...]) + vec(vecs, PB)
-    full_ref[...] = (mask * (middle_ref[...] + projected)).astype(BF16)
-    split_out(full_ref, home, h, out_own, send_ref.at[0])
     fill_shifts(shift_ref, grad1_ref[...].astype(F32), stride)
     conv_backward(shift_ref, weight1, stride, acc_ref)
     inverse = stats_ref[1:2, :]
@@ -442,7 +438,7 @@
         grad, normal, inverse, mask, group_size, vec(vecs, GAIN1)
     )
     full_ref[...] = (mask * (grad_middle_ref[...] + grad_in)).astype(BF16)
-    split_out(full_ref, home, h, grad_own, send_ref.at[1])
+    split_out(full_ref, home, h, grad_own, send_ref)
     vec_ref[0:6, :] = vec_a[0:6, :]
     vec_ref[6:9, :] = vec_b[0:3, :]
     vec_ref[9:10, :] = gain_grad
@@ -460,6 +456,17 @@
             parts.append(part if start == tile else pltpu.roll(part, BLK - (start - tile), 1))
         vec_keep[pair] = jnp.where(mine, parts[1], parts[0]).astype(BF16)
         vec_send[pair] = jnp.where(mine, parts[0], parts[1]).astype(BF16)
+
+
+def output_kernel(
+    bucket_ref, middle_ref, mixed_ref, vecs, wp, grad_send, out_own, send_ref, full_ref
+):
+    h, home, away = place(bucket_ref)
+    mask, pixels = pixel_mask(home)
+    projected = mm(mixed_ref[...], wp[...]) + vec(vecs, PB)
+    full_ref[...] = (mask * (middle_ref[...] + projected)).astype(BF16)
+    split_out(full_ref, home, h, out_own, send_ref.at[0])
+    send_ref[1] = grad_send[...]
 
 
 def weight_kernel(
@@ -646,6 +653,9 @@
     def after(v, *others):
         return lax.optimization_barrier((v,) + others)[0]
 
+    def together(got, *others):
+        return list(lax.optimization_barrier((*got, *others))[: len(got)])
+
     img16 = ((PIX, C), BF16)
     img32 = ((PIX, C), F32)
     rows8 = ((8, C), F32)
@@ -746,24 +756,27 @@
     parts_a, got_a = spread("routea", 1, after(attn_keep, send2), attn_got)
     keep1, send1 = weight_grad("weight1", act1_t, 0, after(block1, *parts_a), block1_away)
     got1 = to_batch(send1, 1)
-    shard_a = finish("routea", parts_a, [after(g, send1) for g in got_a])
-    out_own, grad_own, image_send, vec_keep, vec_send = call(
+    shard_a = finish("routea", parts_a, together(got_a, send1))
+    grad_own, grad_send, vec_keep, vec_send = call(
         fourth_kernel, "fourth",
-        [((192, C), BF16), ((192, C), BF16), ((2, 128, C), BF16),
+        [((192, C), BF16), ((128, C), BF16),
          ((batches // 2, VECS, BLK), BF16), ((batches // 2, VECS, BLK), BF16)],
         [shifts, img32, img16, ((VECS, C), F32)], 14,
-        kinds, after(grad1, send1), image, stats, grad_middle, middle, mixed, vecs,
-        conv1_weight, proj_weight, vec_a, vec_b,
-    )
-    image_away = to_chip(image_send)
+        kinds, after(grad1, send1), image, stats, grad_middle, vecs, conv1_weight, vec_a, vec_b,
+    )
     vec_got = to_batch(vec_send, 1)
     parts_b, got_b = spread("routeb", 1, after(keep2, vec_keep, shard_a), got2)
+    out_own, image_send = call(
+        output_kernel, "output", [((192, C), BF16), ((2, 128, C), BF16)], [img16], 10,
+        kinds, after(middle, *parts_b), mixed, vecs, proj_weight, grad_send,
+    )
+    image_away = to_chip(image_send)
     parts_c, got_c = spread("routec", 1, keep1, got1, (vec_keep, vec_got), behind=got_b)
-    shard_b = finish("routeb", parts_b, [after(g, parts_c[0]) for g in got_b])
+    shard_b = finish("routeb", parts_b, together(got_b, parts_c[0]))
     gathered_a = gather(shard_a)
     gathered_b = gather(shard_b)
     shard_c = finish(
-        "routec", parts_c, [after(g, gathered_b[1], gathered_a[1]) for g in got_c]
+        "routec", parts_c, together(got_c[::-1], gathered_b[1], gathered_a[1])
     )
     small = call(
         join_attn_kernel, "joina", [((small_rows, C), F32)] * 4, [], 8,

time: 95.2 us -> 96.1 us (level)
    ppermute x13, waiting for transfers between devices: 11.4 us -> 13.4 us  [to_batch(): return lax.ppermute(v, 'batch', [(i, i ^ change) for i in range(batches)])]
    ppermute x9, waiting for transfers between devices: 7.74 us -> 6.38 us  [to_chip(): return lax.ppermute(v, 'height', [(i, i ^ 2) for i in range(4)])]
    pallas_call x19 -> x20, Pallas kernels: 38.6 us -> 39.2 us  [call(): pl.pallas_call(kernel, name=name, out_shape=[jax.ShapeDtypeStruct(shape,...]
  transfers between devices with their start and end apart: 33 -> 33, of which waited for: 10 -> 10; matrix products, arithmetic and copies ran while one was open for 0% -> 0% of each run, Pallas kernels for 37% -> 38%
where the time goes in v8:
time: 96.1 us; the launch traced here: 95.9 us
  Pallas kernels  39.2 us (41%)
  starting transfers between devices  32.5 us (34%)
  waiting for transfers between devices  22 us (23%)
  between operations  1.3 us (1%)
    pallas_call x20, Pallas kernels, call(): pl.pallas_call(kernel, name=name, out_shape=[jax.ShapeDtypeStruct(shape,...  39.2 us
    ppermute x13, starting transfers between devices, to_batch(): return lax.ppermute(v, 'batch', [(i, i ^ change) for i in range(batches)])  19 us
    ppermute x13, waiting for transfers between devices, to_batch(): return lax.ppermute(v, 'batch', [(i, i ^ change) for i in range(batches)])  13.4 us
    ppermute x9, starting transfers between devices, to_chip(): return lax.ppermute(v, 'height', [(i, i ^ 2) for i in range(4)])  9.81 us
    ppermute x9, waiting for transfers between devices, to_chip(): return lax.ppermute(v, 'height', [(i, i ^ 2) for i in range(4)])  6.38 us
    ppermute x10, starting transfers between devices, to_core(): return lax.ppermute(v, 'height', [(i, i ^ 1) for i in range(4)])  2.3 us
    ppermute x10, waiting for transfers between devices, to_core(): return lax.ppermute(v, 'height', [(i, i ^ 1) for i in range(4)])  2.26 us
  transfers between devices with their start and end apart: 33, of which 10 were waited for; matrix products, arithmetic and copies ran while one was open for 0% of the time, Pallas kernels for 38%

profile of v8, /device:TPU:0, one launch (start us, length us, event | category | flops | bytes accessed | tf_op | source)
XLA Modules:
  0.0 95.9 jit_solution(1862802322035441765)
XLA Ops:
  0.8 0.0 slice-start
  0.8 0.0 slice-start.2
  0.8 1.9 %pack.1 = (s32[2]{0:T(128)}, bf16[128,512]{1,0:T(8,128)(2,1)}, bf16[192,512]{1,0:T(8,128)(2,1)}) custom-call(s32[2]{0:T(128)} %bucket_hbm.1, bf16[2,6,32,512]{3,2,1,0:T(8,128)(2,1)} %x_hbm.1), custom_call_target="tpu_custom_call" | custom-call | flops 10737418240 | bytes 1024 | tf_op jit(solution)/shard_map/pack/pallas_call | solution.py:593
  2.7 3.0 %collective-permute-start.1 = (bf16[128,512]{1,0:T(8,128)(2,1)}, bf16[128,512]{1,0:T(8,128)(2,1)S(1)}, u32[]{:S(2)}, u32[]{:S(2)}) collective-permute-start(bf16[128,512]{1,0:T(8,128)(2,1)} %get-tuple-element.114), channel_id=1, source_target_pairs={{0,2},{1,3},{2,0},{3,1},{4,6},{5,7},{6,4},{7,5},{8,10},{9,11},{10,... | collective-permute-start | bytes 393224 | tf_op jit(solution)/shard_map/ppermute | solution.py:648
  5.9 0.0 copy-start.2
  5.9 0.8 copy-done.2
  6.7 0.6 stack.1
  7.3 0.0 copy-start
  7.3 0.0 copy-start.5
  7.3 0.0 copy-start.6
  7.3 0.6 collective-permute-start.3
  7.9 0.1 collective-permute-start.4
  8.0 1.4 %collective-permute-start.5 = (bf16[160,512]{1,0:T(8,128)(2,1)S(1)}, bf16[160,512]{1,0:T(8,128)(2,1)S(1)}, u32[]{:S(2)}, u32[]{:S(2)}) collective-permute-start(bf16[160,512]{1,0:T(8,128)(2,1)S(1)} %get-tuple-element.120), channel_id=1, source_target_pairs={{0,3},{1,2},{2,1},{3,0},{4,7},{5,6},{6,5},{7,4},{8,11},{9,10},{10,... | collective-permute-start | bytes 491528 | tf_op jit(solution)/shard_map/ppermute | solution.py:684
  9.3 0.1 collective-permute-done.1.received
  9.5 0.6 collective-permute-start.2
  10.1 1.0 %collective-permute-done.2.partner_received = bf16[128,512]{1,0:T(8,128)(2,1)S(1)} collective-permute-done((bf16[128,512]{1,0:T(8,128)(2,1)S(1)}, bf16[128,512]{1,0:T(8,128)(2,1)S(1)}, u32[]{:S(2)}, u32[]{:S(2)}) %collective-permute-start.2) | collective-permute-done | bytes 131104 | tf_op jit(solution)/shard_map/ppermute | solution.py:645
  11.1 5.4 %first.1 = (bf16[512,512]{1,0:T(8,128)(2,1)S(1)}, f32[512,512]{1,0:T(8,128)S(1)}, bf16[512,512]{1,0:T(8,128)(2,1)S(1)}, f32[8,512]{1,0:T(8,128)S(1)}, bf16[512,5...) custom-call(s32[2]{0:T(128)S(1)} %copy-done.3, bf16[192,512]{1,0:T(8,128)(2,1)S(1)} %copy-done.1, ...), custom_call_target="tpu_custom_call" | custom-call | flops 21474836 | bytes 1024 | tf_op jit(solution)/shard_map/first/pallas_call | solution.py:593
  16.4 1.9 %collective-permute-start.6 = (bf16[2,256,512]{2,1,0:T(8,128)(2,1)S(1)}, bf16[2,256,512]{2,1,0:T(8,128)(2,1)S(1)}, u32[]{:S(2)}, u32[]{:S(2)}) collective-permute-start(bf16[2,256,512]{2,1,0:T(8,128)(2,1)S(1)} %get-tuple-element.123), channel_id=1, source_target_pairs={{0,2},{1,3},{2,0},{3,1},{4,6},{5,7},{6,4},{7,5},{8,10},{9,11},{10,... | collective-permute-start | bytes 1572872 | tf_op jit(solution)/shard_map/ppermute | solution.py:648
  18.4 9.6 %second.1 = (f32[512,512]{1,0:T(8,128)S(1)}, bf16[512,512]{1,0:T(8,128)(2,1)S(1)}, bf16[512,512]{1,0:T(8,128)(2,1)S(1)}, f32[512,512]{1,0:T(8,128)S(1)}, bf16[4,...) custom-call(s32[2]{0:T(128)S(1)} %copy-done.3, ...), custom_call_target="tpu_custom_call" | custom-call | flops 32212254720 | bytes 1024 | tf_op jit(solution)/shard_map/second/pallas_call | solution.py:593
  28.0 0.3 collective-permute-start.8
  28.3 1.5 %collective-permute-start.9 = (bf16[4,256,256]{2,1,0:T(8,128)(2,1)S(1)}, bf16[4,256,256]{2,1,0:T(8,128)(2,1)S(1)}, u32[]{:S(2)}, u32[]{:S(2)}) collective-permute-start(bf16[4,256,256]{2,1,0:T(8,128)(2,1)S(1)} %get-tuple-element.137), channel_id=1, source_target_pairs={{0,4},{4,0},{8,12},{12,8},{16,20},{20,16},{24,28},{28,24},{1,5},{5... | collective-permute-start | bytes 1572872 | tf_op jit(solution)/shard_map/ppermute | solution.py:651
  29.8 1.1 %collective-permute-done.6.half_t = bf16[2,256,512]{2,1,0:T(8,128)(2,1)S(1)} collective-permute-done((bf16[2,256,512]{2,1,0:T(8,128)(2,1)S(1)}, bf16[2,256,512]{2,1,0:T(8,128)(2,1)S(1)}, u32[]{:S(2)}, u32[]{:S(2)}) %collective-permute-start.6) | collective-permute-done | bytes 524320 | tf_op jit(solution)/shard_map/ppermute | solution.py:648
  30.8 4.3 %third.1 = (bf16[512,512]{1,0:T(8,128)(2,1)S(1)}, bf16[512,128]{1,0:T(8,128)(2,1)S(1)}, bf16[512,128]{1,0:T(8,128)(2,1)S(1)}, f32[8,512]{1,0:T(8,128)S(1)}) custom-call(s32[2]{0:T(128)S(1)} %copy-done.3, bf16[512,512]{1,0:T(8,128)(2,1)S(1)} %get-tuple-element.125.grad2_ref, f32[512,512]{1,0:T(8,128)S(1)} %get-tuple-element.126.conv_ref, ...), custom_call_target="tpu_custom_call" | custom-call | flops 21474836480 | bytes 1024 | tf_op jit(solution)/shard_map/third/pallas_call | solution.py:593
  35.2 3.3 %weight2.5 = (bf16[4,576,128]{2,1,0:T(8,128)(2,1)S(1)}, bf16[4,576,128]{2,1,0:T(8,128)(2,1)S(1)}) custom-call(s32[2]{0:T(128)S(1)} %copy-done.3, bf16[512,512]{1,0:T(8,128)(2,1)S(1)} %get-tuple-element.122.act_t, bf16[2,256,512]{2,1,0:T(8,128)(2,1)S(1)} %collective-permute-done.6.half_t, bf16[2,256,512]{2,1,0:T(8,128)(2,1)S(1)} %collective-permute-done.7.partner_half_t, ...), custom_call_target="tpu_custom_call" | custom-call | flops 1073741824 | bytes 1024 | tf_op jit(solution)/shard_map/weight2/pallas_call | solution.py:593
  38.5 1.8 %collective-permute-start.14 = (bf16[4,576,128]{2,1,0:T(8,128)(2,1)S(1)}, bf16[4,576,128]{2,1,0:T(8,128)(2,1)S(1)}, u32[]{:S(2)}, u32[]{:S(2)}) collective-permute-start(bf16[4,576,128]{2,1,0:T(8,128)(2,1)S(1)} %get-tuple-element.135), channel_id=1, source_target_pairs={{0,4},{4,0},{8,12},{12,8},{16,20},{20,16},{24,28},{28,24},{1,5},{5... | collective-permute-start | bytes 1769480 | tf_op jit(solution)/shard_map/ppermute | solution.py:651
  40.3 1.8 %collective-permute-start.10 = (bf16[512,128]{1,0:T(8,128)(2,1)S(1)}, bf16[512,128]{1,0:T(8,128)(2,1)S(1)}, u32[]{:S(2)}, u32[]{:S(2)}) collective-permute-start(bf16[512,128]{1,0:T(8,128)(2,1)S(1)} %get-tuple-element.143), channel_id=1, source_target_pairs={{0,2},{1,3},{2,0},{3,1},{4,6},{5,7},{6,4},{7,5},{8,10},{9,11},{10,... | collective-permute-start | bytes 393224 | tf_op jit(solution)/shard_map/ppermute | solution.py:648
  42.1 0.1 routea1.1
  42.2 1.6 %collective-permute-start.11 = (bf16[1,256,256]{2,1,0:T(8,128)(2,1)S(1)}, bf16[1,256,256]{2,1,0:T(8,128)(2,1)S(1)}, u32[]{:S(2)}, u32[]{:S(2)}) collective-permute-start(bf16[1,256,256]{2,1,0:T(8,128)(2,1)S(1)} %get-tuple-element.139), channel_id=1, source_target_pairs={{0,8},{4,12},{8,0},{12,4},{16,24},{20,28},{24,16},{28,20},{1,9},{5... | collective-permute-start | bytes 393224 | tf_op jit(solution)/shard_map/ppermute | solution.py:651
  43.8 2.6 %collective-permute-start.12 = (bf16[1,256,256]{2,1,0:T(8,128)(2,1)S(1)}, bf16[1,256,256]{2,1,0:T(8,128)(2,1)S(1)}, u32[]{:S(2)}, u32[]{:S(2)}) collective-permute-start(bf16[1,256,256]{2,1,0:T(8,128)(2,1)S(1)} %get-tuple-element.140), channel_id=1, source_target_pairs={{0,16},{4,20},{8,24},{12,28},{16,0},{20,4},{24,8},{28,12},{1,17},{... | collective-permute-start | bytes 393224 | tf_op jit(solution)/shard_map/ppermute | solution.py:651
  46.4 0.2 collective-permute-start.13
  46.7 3.1 %weight1.4 = (bf16[4,576,128]{2,1,0:T(8,128)(2,1)S(1)}, bf16[4,576,128]{2,1,0:T(8,128)(2,1)S(1)}) custom-call(s32[2]{0:T(128)S(1)} %copy-done.3, bf16[512,512]{1,0:T(8,128)(2,1)S(1)} %get-tuple-element.133.act_t, bf16[2,256,512]{2,1,0:T(8,128)(2,1)S(1)} %collective-permute-done.6.half_t, bf16[2,256,512]{2,1,0:T(8,128)(2,1)S(1)} %collective-permute-done.7.partner_half_t, ...), custom_call_target="tpu_custom_call" | custom-call | flops 3221225472 | bytes 1024 | tf_op jit(solution)/shard_map/weight1/pallas_call | solution.py:593
  49.7 1.4 %collective-permute-start.17 = (bf16[4,576,128]{2,1,0:T(8,128)(2,1)S(1)}, bf16[4,576,128]{2,1,0:T(8,128)(2,1)S(1)}, u32[]{:S(2)}, u32[]{:S(2)}) collective-permute-start(bf16[4,576,128]{2,1,0:T(8,128)(2,1)S(1)} %get-tuple-element.144), channel_id=1, source_target_pairs={{0,4},{4,0},{8,12},{12,8},{16,20},{20,16},{24,28},{28,24},{1,5},{5... | collective-permute-start | bytes 1769480 | tf_op jit(solution)/shard_map/ppermute | solution.py:651
  51.2 4.6 %fourth.1 = (bf16[192,512]{1,0:T(8,128)(2,1)S(1)}, bf16[128,512]{1,0:T(8,128)(2,1)S(1)}, bf16[4,16,128]{2,1,0:T(8,128)(2,1)S(1)}, bf16[4,16,128]{2,1,0:T(8,128)(2,1)S(1)}) custom-call(s32[2]{0:T(128)S(1)} %copy-done.3, bf16[512,512]{1,0:T(8,128)(2,1)S(1)} %get-tuple-element.145.grad1_ref, bf16[512,512]{1,0:T(8,128)(2,1)S(1)} %get-tuple-element.117.image_ref, ...), custom_call_target="tpu_custom_call" | custom-call | flops 536870912 | bytes 1024 | tf_op jit(solution)/shard_map/fourth/pallas_call | solution.py:593
  55.8 1.0 %collective-permute-done.12.refs_2_ = bf16[1,256,256]{2,1,0:T(8,128)(2,1)S(1)} collective-permute-done((bf16[1,256,256]{2,1,0:T(8,128)(2,1)S(1)}, bf16[1,256,256]{2,1,0:T(8,128)(2,1)S(1)}, u32[]{:S(2)}, u32[]{:S(2)}) %collective-permute-start.12) | collective-permute-done | bytes 131104 | tf_op jit(solution)/shard_map/ppermute | solution.py:651
  56.8 0.1 sumroutea.1.own_ref
  56.9 0.1 routeb1.1
  57.0 2.1 %collective-permute-start.18 = (bf16[1,576,128]{2,1,0:T(8,128)(2,1)S(1)}, bf16[1,576,128]{2,1,0:T(8,128)(2,1)S(1)}, u32[]{:S(2)}, u32[]{:S(2)}) collective-permute-start(bf16[1,576,128]{2,1,0:T(8,128)(2,1)S(1)} %get-tuple-element.155), channel_id=1, source_target_pairs={{0,8},{4,12},{8,0},{12,4},{16,24},{20,28},{24,16},{28,20},{1,9},{5... | collective-permute-start | bytes 442376 | tf_op jit(solution)/shard_map/ppermute | solution.py:651
  59.2 1.1 %collective-permute-start.19 = (bf16[1,576,128]{2,1,0:T(8,128)(2,1)S(1)}, bf16[1,576,128]{2,1,0:T(8,128)(2,1)S(1)}, u32[]{:S(2)}, u32[]{:S(2)}) collective-permute-start(bf16[1,576,128]{2,1,0:T(8,128)(2,1)S(1)} %get-tuple-element.156), channel_id=1, source_target_pairs={{0,16},{4,20},{8,24},{12,28},{16,0},{20,4},{24,8},{28,12},{1,17},{... | collective-permute-start | bytes 442376 | tf_op jit(solution)/shard_map/ppermute | solution.py:651
  60.3 1.3 %collective-permute-start.20 = (bf16[1,576,128]{2,1,0:T(8,128)(2,1)S(1)}, bf16[1,576,128]{2,1,0:T(8,128)(2,1)S(1)}, u32[]{:S(2)}, u32[]{:S(2)}) collective-permute-start(bf16[1,576,128]{2,1,0:T(8,128)(2,1)S(1)} %get-tuple-element.157), channel_id=1, source_target_pairs={{0,24},{4,28},{8,16},{12,20},{16,8},{20,12},{24,0},{28,4},{1,25},{... | collective-permute-start | bytes 442376 | tf_op jit(solution)/shard_map/ppermute | solution.py:651
  61.6 0.5 collective-permute-start.16
  62.1 5.4 %collective-permute-done.16.got_ref = bf16[4,16,128]{2,1,0:T(8,128)(2,1)S(1)} collective-permute-done((bf16[4,16,128]{2,1,0:T(8,128)(2,1)S(1)}, bf16[4,16,128]{2,1,0:T(8,128)(2,1)S(1)}, u32[]{:S(2)}, u32[]{:S(2)}) %collective-permute-start.16) | collective-permute-done | bytes 16416 | tf_op jit(solution)/shard_map/ppermute | solution.py:651
  67.5 2.0 %collective-permute-start.25 = (bf16[256,256]{1,0:T(8,128)(2,1)S(1)}, bf16[256,256]{1,0:T(8,128)(2,1)S(1)}, u32[]{:S(2)}, u32[]{:S(2)}) collective-permute-start(bf16[256,256]{1,0:T(8,128)(2,1)S(1)} %sumroutea.1.own_ref), channel_id=1, source_target_pairs={{0,2},{1,3},{2,0},{3,1},{4,6},{5,7},{6,4},{7,5},{8,10},{9,11},{10,... | collective-permute-start | bytes 393224 | tf_op jit(solution)/shard_map/ppermute | solution.py:648
  69.5 1.0 %output.1 = (bf16[192,512]{1,0:T(8,128)(2,1)S(1)}, bf16[2,128,512]{2,1,0:T(8,128)(2,1)S(1)}) custom-call(s32[2]{0:T(128)S(1)} %copy-done.3, f32[512,512]{1,0:T(8,128)S(1)} %get-tuple-element.158.middle_ref, bf16[512,512]{1,0:T(8,128)(2,1)S(1)} %get-tuple-element.159.mixed_ref, f32[16,512]{1,0:T(8,128)S(1)} %get-tuple-element.115.vecs, ...), custom_call_target="tpu_custom_call" | custom-call | flops 21474836 | bytes 1024 | tf_op jit(solution)/shard_map/output/pallas_call | solution.py:593
  70.6 0.1 collective-permute-start.15
  70.7 0.1 routec1.1
  70.8 1.5 %collective-permute-done.19.refs_2_ = bf16[1,576,128]{2,1,0:T(8,128)(2,1)S(1)} collective-permute-done((bf16[1,576,128]{2,1,0:T(8,128)(2,1)S(1)}, bf16[1,576,128]{2,1,0:T(8,128)(2,1)S(1)}, u32[]{:S(2)}, u32[]{:S(2)}) %collective-permute-start.19) | collective-permute-done | bytes 147488 | tf_op jit(solution)/shard_map/ppermute | solution.py:651
  72.3 2.1 %collective-permute-start.23 = (bf16[1,592,128]{2,1,0:T(8,128)(2,1)S(1)}, bf16[1,592,128]{2,1,0:T(8,128)(2,1)S(1)}, u32[]{:S(2)}, u32[]{:S(2)}) collective-permute-start(bf16[1,592,128]{2,1,0:T(8,128)(2,1)S(1)} %get-tuple-element.176), channel_id=1, source_target_pairs={{0,8},{4,12},{8,0},{12,4},{16,24},{20,28},{24,16},{28,20},{1,9},{5... | collective-permute-start | bytes 454664 | tf_op jit(solution)/shard_map/ppermute | solution.py:651
  74.4 1.1 %collective-permute-start.22 = (bf16[1,592,128]{2,1,0:T(8,128)(2,1)S(1)}, bf16[1,592,128]{2,1,0:T(8,128)(2,1)S(1)}, u32[]{:S(2)}, u32[]{:S(2)}) collective-permute-start(bf16[1,592,128]{2,1,0:T(8,128)(2,1)S(1)} %get-tuple-element.174), channel_id=1, source_target_pairs={{0,16},{4,20},{8,24},{12,28},{16,0},{20,4},{24,8},{28,12},{1,17},{... | collective-permute-start | bytes 454664 | tf_op jit(solution)/shard_map/ppermute | solution.py:651
  75.5 1.5 %collective-permute-start.21 = (bf16[1,592,128]{2,1,0:T(8,128)(2,1)S(1)}, bf16[1,592,128]{2,1,0:T(8,128)(2,1)S(1)}, u32[]{:S(2)}, u32[]{:S(2)}) collective-permute-start(bf16[1,592,128]{2,1,0:T(8,128)(2,1)S(1)} %get-tuple-element.172), channel_id=1, source_target_pairs={{0,24},{4,28},{8,16},{12,20},{16,8},{20,12},{24,0},{28,4},{1,25},{... | collective-permute-start | bytes 454664 | tf_op jit(solution)/shard_map/ppermute | solution.py:651
  77.0 0.1 sumrouteb.1.own_ref
  77.1 0.4 collective-permute-start.24
  77.5 4.8 %collective-permute-done.24.far_ref = bf16[576,128]{1,0:T(8,128)(2,1)S(1)} collective-permute-done((bf16[576,128]{1,0:T(8,128)(2,1)S(1)}, bf16[576,128]{1,0:T(8,128)(2,1)S(1)}, u32[]{:S(2)}, u32[]{:S(2)}) %collective-permute-start.24) | collective-permute-done | bytes 147488 | tf_op jit(solution)/shard_map/ppermute | solution.py:648
  82.3 5.6 %collective-permute-done.22.refs_2_ = bf16[1,592,128]{2,1,0:T(8,128)(2,1)S(1)} collective-permute-done((bf16[1,592,128]{2,1,0:T(8,128)(2,1)S(1)}, bf16[1,592,128]{2,1,0:T(8,128)(2,1)S(1)}, u32[]{:S(2)}, u32[]{:S(2)}) %collective-permute-start.22) | collective-permute-done | bytes 151584 | tf_op jit(solution)/shard_map/ppermute | solution.py:651
  87.8 0.1 sumroutec.1.own_ref
  87.9 0.3 collective-permute-start.26
  88.2 0.5 collective-permute-start.29
  88.7 0.5 collective-permute-start.31
  89.2 1.5 %unpack.1 = (bf16[2,6,32,512]{3,2,1,0:T(8,128)(2,1)}, bf16[2,6,32,512]{3,2,1,0:T(8,128)(2,1)}) custom-call(s32[2]{0:T(128)S(1)} %copy-done.3, bf16[192,512]{1,0:T(8,128)(2,1)S(1)} %get-tuple-element.161.out_own, bf16[192,512]{1,0:T(8,128)(2,1)S(1)} %get-tuple-element.162.grad_own, bf16[2,128,512]{2,1,0:T(8,128)(2,1)S(1)} %collective-permute-done.15.away_ref), custom_call_target="tpu_custom_call" | custom-call | flops 21474836 | bytes 1024 | tf_op jit(solution)/shard_map/unpack/pallas_call | solution.py:593
  90.8 0.9 joina.1
  91.6 1.2 %joinb.1 = f32[576,512]{1,0:T(8,128)} custom-call(bf16[576,128]{1,0:T(8,128)(2,1)S(1)} %sumrouteb.1.own_ref, bf16[576,128]{1,0:T(8,128)(2,1)S(1)} %collective-permute-done.24.far_ref, bf16[576,128]{1,0:T(8,128)(2,1)S(1)} %collective-permute-done.28.near_ref, bf16[576,128]{1,0:T(8,128)(2,1)S(1)} %collective-permute-done.29.diagonal_ref), custom_call_target="tpu_custom_call" | custom-call | flops 21474836 | bytes 1024 | tf_op jit(solution)/shard_map/joinb/pallas_call | solution.py:593
  92.8 0.4 collective-permute-done.26.far_ref
  93.2 0.1 collective-permute-start.32
  93.3 1.3 %collective-permute-done.32.diagonal_ref = bf16[592,128]{1,0:T(8,128)(2,1)S(1)} collective-permute-done((bf16[592,128]{1,0:T(8,128)(2,1)S(1)}, bf16[592,128]{1,0:T(8,128)(2,1)S(1)}, u32[]{:S(2)}, u32[]{:S(2)}) %collective-permute-start.32) | collective-permute-done | bytes 151584 | tf_op jit(solution)/shard_map/ppermute | solution.py:645
  94.6 1.2 %joinc.1 = (f32[576,512]{1,0:T(8,128)}, f32[1,64]{1,0:T(1,128)}, f32[1,64]{1,0:T(1,128)}, f32[1,64]{1,0:T(1,128)}, f32[1,64]{1,0:T(1,128)}, /*index=5*/f32[1,64]...) custom-call(bf16[592,128]{1,0:T(8,128)(2,1)S(1)} %sumroutec.1.own_re, ...), custom_call_target="tpu_custom_call" | custom-call | flops 21474836 | bytes 1024 | tf_op jit(solution)/shard_map/joinc/pallas_call | solution.py:593
  (70 shorter events, 0.2 us)
Async XLA Ops:
  0.7 5.1 %copy-start.8 = (f32[512]{0:T(512)S(1)}, f32[512]{0:T(512)}, u32[]{:S(2)}) copy-start(f32[512]{0:T(512)} %param.22) | copy-start | bytes 6148
  0.7 5.1 %copy-start.9 = (f32[512]{0:T(512)S(1)}, f32[512]{0:T(512)}, u32[]{:S(2)}) copy-start(f32[512]{0:T(512)} %param.23) | copy-start | bytes 6148
  0.7 5.1 %copy-start.18 = (f32[512]{0:T(512)S(1)}, f32[512]{0:T(512)}, u32[]{:S(2)}) copy-start(f32[512]{0:T(512)} %param.38) | copy-start | bytes 6148
  0.7 5.1 %copy-start.10 = (f32[512]{0:T(512)S(1)}, f32[512]{0:T(512)}, u32[]{:S(2)}) copy-start(f32[512]{0:T(512)} %param.25) | copy-start | bytes 6148
  0.7 5.1 %copy-start.11 = (f32[512]{0:T(512)S(1)}, f32[512]{0:T(512)}, u32[]{:S(2)}) copy-start(f32[512]{0:T(512)} %param.26) | copy-start | bytes 6148
  0.7 5.1 %copy-start.12 = (f32[512]{0:T(512)S(1)}, f32[512]{0:T(512)}, u32[]{:S(2)}) copy-start(f32[512]{0:T(512)} %param.27) | copy-start | bytes 6148
  0.7 5.1 %copy-start.13 = (f32[512]{0:T(512)S(1)}, f32[512]{0:T(512)}, u32[]{:S(2)}) copy-start(f32[512]{0:T(512)} %param.29) | copy-start | bytes 6148
  0.7 5.1 %copy-start.14 = (f32[512]{0:T(512)S(1)}, f32[512]{0:T(512)}, u32[]{:S(2)}) copy-start(f32[512]{0:T(512)} %param.30) | copy-start | bytes 6148
  0.7 5.1 %copy-start.15 = (f32[512]{0:T(512)S(1)}, f32[512]{0:T(512)}, u32[]{:S(2)}) copy-start(f32[512]{0:T(512)} %param.31) | copy-start | bytes 6148
  0.8 5.1 %copy-start.16 = (f32[512]{0:T(512)S(1)}, f32[512]{0:T(512)}, u32[]{:S(2)}) copy-start(f32[512]{0:T(512)} %param.33) | copy-start | bytes 6148
  0.8 5.1 %copy-start.17 = (f32[512]{0:T(512)S(1)}, f32[512]{0:T(512)}, u32[]{:S(2)}) copy-start(f32[512]{0:T(512)} %param.36) | copy-start | bytes 6148
  0.8 5.1 %copy-start.7 = (bf16[2,6,32,512]{3,2,1,0:T(8,128)(2,1)S(1)}, bf16[2,6,32,512]{3,2,1,0:T(8,128)(2,1)}, u32[]{:S(2)}) copy-start(bf16[2,6,32,512]{3,2,1,0:T(8,128)(2,1)} %cot_ref.1) | copy-start | bytes 1179652
  0.8 10.3 %slice-start = ((s8[4718592]{0:T(1024)(128)(4,1)}), s8[524288]{0:T(1024)(128)(4,1)S(1)}, s32[]{:S(2)}) async-start(s8[4718592]{0:T(1024)(128)(4,1)} %bitcast.22), calls=%async_computation | async-start | bytes 1048576
  0.8 17.5 %slice-start.2 = ((s8[4718592]{0:T(1024)(128)(4,1)}), s8[4194304]{0:T(1024)(128)(4,1)S(1)}, s32[]{:S(2)}) async-start(s8[4718592]{0:T(1024)(128)(4,1)} %bitcast.24), calls=%async_computation.2 | async-start | bytes 8388608
  2.7 6.7 %collective-permute-start.1 = (bf16[128,512]{1,0:T(8,128)(2,1)}, bf16[128,512]{1,0:T(8,128)(2,1)S(1)}, u32[]{:S(2)}, u32[]{:S(2)}) collective-permute-start(bf16[128,512]{1,0:T(8,128)(2,1)} %get-tuple-element.114), channel_id=1, source_target_pairs={{0,2},{1,3},{2,0},{3,1},{4,6},{5,7},{6,4},{7,5},{8,10},{9,11},{10,... | collective-permute-start | bytes 393224 | tf_op jit(solution)/shard_map/ppermute | solution.py:648
  5.8 4.3 %collective-permute-start = (bf16[192,512]{1,0:T(8,128)(2,1)}, bf16[192,512]{1,0:T(8,128)(2,1)S(1)}, u32[]{:S(2)}, u32[]{:S(2)}) collective-permute-start(bf16[192,512]{1,0:T(8,128)(2,1)} %get-tuple-element.113.own), channel_id=1, source_target_pairs={{0,1},{1,0},{2,3},{3,2},{4,5},{5,4},{6,7},{7,6},{8,9},{9,8},{10,11... | collective-permute-start | bytes 589832 | tf_op jit(solution)/shard_map/ppermute | solution.py:645
  5.8 5.3 %slice-start.1 = ((s8[4718592]{0:T(1024)(128)(4,1)}), s8[4194304]{0:T(1024)(128)(4,1)S(1)}, s32[]{:S(2)}) async-start(s8[4718592]{0:T(1024)(128)(4,1)} %bitcast.22), calls=%async_computation.1 | async-start | bytes 8388608
  5.9 0.8 copy-start.2
  6.7 4.4 %copy-start.1 = (bf16[192,512]{1,0:T(8,128)(2,1)S(1)}, bf16[192,512]{1,0:T(8,128)(2,1)}, u32[]{:S(2)}) copy-start(bf16[192,512]{1,0:T(8,128)(2,1)} %get-tuple-element.113.own) | copy-start | bytes 589828
  6.7 4.4 %copy-start.3 = (s32[2]{0:T(128)S(1)}, s32[2]{0:T(128)}, u32[]{:S(2)}) copy-start(s32[2]{0:T(128)} %get-tuple-element.112.kinds.bucket_ref) | copy-start | bytes 28
  6.7 11.6 %slice-start.3 = ((s8[4718592]{0:T(1024)(128)(4,1)}), s8[524288]{0:T(1024)(128)(4,1)S(1)}, s32[]{:S(2)}) async-start(s8[4718592]{0:T(1024)(128)(4,1)} %bitcast.24), calls=%async_computation.3 | async-start | bytes 1048576
  7.3 11.1 %copy-start = (bf16[512,512]{1,0:T(8,128)(2,1)S(1)}, bf16[512,512]{1,0:T(8,128)(2,1)}, u32[]{:S(2)}) copy-start(bf16[512,512]{1,0:T(8,128)(2,1)} %wp.3) | copy-start | bytes 1572868
  7.3 11.0 %copy-start.4 = (bf16[512,512]{1,0:T(8,128)(2,1)S(1)}, bf16[512,512]{1,0:T(8,128)(2,1)}, u32[]{:S(2)}) copy-start(bf16[512,512]{1,0:T(8,128)(2,1)} %wq.1) | copy-start | bytes 1572868
  7.3 11.0 %copy-start.5 = (bf16[512,512]{1,0:T(8,128)(2,1)S(1)}, bf16[512,512]{1,0:T(8,128)(2,1)}, u32[]{:S(2)}) copy-start(bf16[512,512]{1,0:T(8,128)(2,1)} %wk.1) | copy-start | bytes 1572868
  7.3 11.0 %copy-start.6 = (bf16[512,512]{1,0:T(8,128)(2,1)S(1)}, bf16[512,512]{1,0:T(8,128)(2,1)}, u32[]{:S(2)}) copy-start(bf16[512,512]{1,0:T(8,128)(2,1)} %wv.1) | copy-start | bytes 1572868
  7.3 11.0 %collective-permute-start.3 = (bf16[192,512]{1,0:T(8,128)(2,1)S(1)}, bf16[192,512]{1,0:T(8,128)(2,1)S(1)}, u32[]{:S(2)}, u32[]{:S(2)}) collective-permute-start(bf16[192,512]{1,0:T(8,128)(2,1)S(1)} %get-tuple-element.119.own), channel_id=1, source_target_pairs={{0,1},{1,0},{2,3},{3,2},{4,5},{5,4},{6,7},{7,6},{8,9},{9,8},{10,11... | collective-permute-start | bytes 589832 | tf_op jit(solution)/shard_map/ppermute | solution.py:645
  7.9 10.4 %collective-permute-start.4 = (bf16[160,512]{1,0:T(8,128)(2,1)S(1)}, bf16[160,512]{1,0:T(8,128)(2,1)S(1)}, u32[]{:S(2)}, u32[]{:S(2)}) collective-permute-start(bf16[160,512]{1,0:T(8,128)(2,1)S(1)} %get-tuple-element.120), channel_id=1, source_target_pairs={{0,2},{1,3},{2,0},{3,1},{4,6},{5,7},{6,4},{7,5},{8,10},{9,11},{10,... | collective-permute-start | bytes 491528 | tf_op jit(solution)/shard_map/ppermute | solution.py:648
  8.0 10.3 %collective-permute-start.5 = (bf16[160,512]{1,0:T(8,128)(2,1)S(1)}, bf16[160,512]{1,0:T(8,128)(2,1)S(1)}, u32[]{:S(2)}, u32[]{:S(2)}) collective-permute-start(bf16[160,512]{1,0:T(8,128)(2,1)S(1)} %get-tuple-element.120), channel_id=1, source_target_pairs={{0,3},{1,2},{2,1},{3,0},{4,7},{5,6},{6,5},{7,4},{8,11},{9,10},{10,... | collective-permute-start | bytes 491528 | tf_op jit(solution)/shard_map/ppermute | solution.py:684
  9.5 1.6 %collective-permute-start.2 = (bf16[128,512]{1,0:T(8,128)(2,1)S(1)}, bf16[128,512]{1,0:T(8,128)(2,1)S(1)}, u32[]{:S(2)}, u32[]{:S(2)}) collective-permute-start(bf16[128,512]{1,0:T(8,128)(2,1)S(1)} %collective-permute-done.1.received), channel_id=1, source_target_pairs={{0,1},{1,0},{2,3},{3,2},{4,5},{5,4},{6,7},{7,6},{8,9},{9,8},{10,11... | collective-permute-start | bytes 393224 | tf_op jit(solution)/shard_map/ppermute | solution.py:645
  16.4 14.4 %collective-permute-start.6 = (bf16[2,256,512]{2,1,0:T(8,128)(2,1)S(1)}, bf16[2,256,512]{2,1,0:T(8,128)(2,1)S(1)}, u32[]{:S(2)}, u32[]{:S(2)}) collective-permute-start(bf16[2,256,512]{2,1,0:T(8,128)(2,1)S(1)} %get-tuple-element.123), channel_id=1, source_target_pairs={{0,2},{1,3},{2,0},{3,1},{4,6},{5,7},{6,4},{7,5},{8,10},{9,11},{10,... | collective-permute-start | bytes 1572872 | tf_op jit(solution)/shard_map/ppermute | solution.py:648
  28.0 7.2 %collective-permute-start.8 = (bf16[512,128]{1,0:T(8,128)(2,1)S(1)}, bf16[512,128]{1,0:T(8,128)(2,1)S(1)}, u32[]{:S(2)}, u32[]{:S(2)}) collective-permute-start(bf16[512,128]{1,0:T(8,128)(2,1)S(1)} %get-tuple-element.130), channel_id=1, source_target_pairs={{0,2},{1,3},{2,0},{3,1},{4,6},{5,7},{6,4},{7,5},{8,10},{9,11},{10,... | collective-permute-start | bytes 393224 | tf_op jit(solution)/shard_map/ppermute | solution.py:648
  28.3 13.8 %collective-permute-start.9 = (bf16[4,256,256]{2,1,0:T(8,128)(2,1)S(1)}, bf16[4,256,256]{2,1,0:T(8,128)(2,1)S(1)}, u32[]{:S(2)}, u32[]{:S(2)}) collective-permute-start(bf16[4,256,256]{2,1,0:T(8,128)(2,1)S(1)} %get-tuple-element.137), channel_id=1, source_target_pairs={{0,4},{4,0},{8,12},{12,8},{16,20},{20,16},{24,28},{28,24},{1,5},{5... | collective-permute-start | bytes 1572872 | tf_op jit(solution)/shard_map/ppermute | solution.py:651
  30.8 4.3 %collective-permute-start.7 = (bf16[2,256,512]{2,1,0:T(8,128)(2,1)S(1)}, bf16[2,256,512]{2,1,0:T(8,128)(2,1)S(1)}, u32[]{:S(2)}, u32[]{:S(2)}) collective-permute-start(bf16[2,256,512]{2,1,0:T(8,128)(2,1)S(1)} %collective-permute-done.6.half_t), channel_id=1, source_target_pairs={{0,1},{1,0},{2,3},{3,2},{4,5},{5,4},{6,7},{7,6},{8,9},{9,8},{10,11... | collective-permute-start | bytes 1572872 | tf_op jit(solution)/shard_map/ppermute | solution.py:645
  38.5 18.4 %collective-permute-start.14 = (bf16[4,576,128]{2,1,0:T(8,128)(2,1)S(1)}, bf16[4,576,128]{2,1,0:T(8,128)(2,1)S(1)}, u32[]{:S(2)}, u32[]{:S(2)}) collective-permute-start(bf16[4,576,128]{2,1,0:T(8,128)(2,1)S(1)} %get-tuple-element.135), channel_id=1, source_target_pairs={{0,4},{4,0},{8,12},{12,8},{16,20},{20,16},{24,28},{28,24},{1,5},{5... | collective-permute-start | bytes 1769480 | tf_op jit(solution)/shard_map/ppermute | solution.py:651
  40.3 6.4 %collective-permute-start.10 = (bf16[512,128]{1,0:T(8,128)(2,1)S(1)}, bf16[512,128]{1,0:T(8,128)(2,1)S(1)}, u32[]{:S(2)}, u32[]{:S(2)}) collective-permute-start(bf16[512,128]{1,0:T(8,128)(2,1)S(1)} %get-tuple-element.143), channel_id=1, source_target_pairs={{0,2},{1,3},{2,0},{3,1},{4,6},{5,7},{6,4},{7,5},{8,10},{9,11},{10,... | collective-permute-start | bytes 393224 | tf_op jit(solution)/shard_map/ppermute | solution.py:648
  42.2 13.6 %collective-permute-start.11 = (bf16[1,256,256]{2,1,0:T(8,128)(2,1)S(1)}, bf16[1,256,256]{2,1,0:T(8,128)(2,1)S(1)}, u32[]{:S(2)}, u32[]{:S(2)}) collective-permute-start(bf16[1,256,256]{2,1,0:T(8,128)(2,1)S(1)} %get-tuple-element.139), channel_id=1, source_target_pairs={{0,8},{4,12},{8,0},{12,4},{16,24},{20,28},{24,16},{28,20},{1,9},{5... | collective-permute-start | bytes 393224 | tf_op jit(solution)/shard_map/ppermute | solution.py:651
  43.8 12.9 %collective-permute-start.12 = (bf16[1,256,256]{2,1,0:T(8,128)(2,1)S(1)}, bf16[1,256,256]{2,1,0:T(8,128)(2,1)S(1)}, u32[]{:S(2)}, u32[]{:S(2)}) collective-permute-start(bf16[1,256,256]{2,1,0:T(8,128)(2,1)S(1)} %get-tuple-element.140), channel_id=1, source_target_pairs={{0,16},{4,20},{8,24},{12,28},{16,0},{20,4},{24,8},{28,12},{1,17},{... | collective-permute-start | bytes 393224 | tf_op jit(solution)/shard_map/ppermute | solution.py:651
  46.4 10.3 %collective-permute-start.13 = (bf16[1,256,256]{2,1,0:T(8,128)(2,1)S(1)}, bf16[1,256,256]{2,1,0:T(8,128)(2,1)S(1)}, u32[]{:S(2)}, u32[]{:S(2)}) collective-permute-start(bf16[1,256,256]{2,1,0:T(8,128)(2,1)S(1)} %get-tuple-element.141), channel_id=1, source_target_pairs={{0,24},{4,28},{8,16},{12,20},{16,8},{20,12},{24,0},{28,4},{1,25},{... | collective-permute-start | bytes 393224 | tf_op jit(solution)/shard_map/ppermute | solution.py:651
  49.7 20.8 %collective-permute-start.17 = (bf16[4,576,128]{2,1,0:T(8,128)(2,1)S(1)}, bf16[4,576,128]{2,1,0:T(8,128)(2,1)S(1)}, u32[]{:S(2)}, u32[]{:S(2)}) collective-permute-start(bf16[4,576,128]{2,1,0:T(8,128)(2,1)S(1)} %get-tuple-element.144), channel_id=1, source_target_pairs={{0,4},{4,0},{8,12},{12,8},{16,20},{20,16},{24,28},{28,24},{1,5},{5... | collective-permute-start | bytes 1769480 | tf_op jit(solution)/shard_map/ppermute | solution.py:651
  57.0 13.8 %collective-permute-start.18 = (bf16[1,576,128]{2,1,0:T(8,128)(2,1)S(1)}, bf16[1,576,128]{2,1,0:T(8,128)(2,1)S(1)}, u32[]{:S(2)}, u32[]{:S(2)}) collective-permute-start(bf16[1,576,128]{2,1,0:T(8,128)(2,1)S(1)} %get-tuple-element.155), channel_id=1, source_target_pairs={{0,8},{4,12},{8,0},{12,4},{16,24},{20,28},{24,16},{28,20},{1,9},{5... | collective-permute-start | bytes 442376 | tf_op jit(solution)/shard_map/ppermute | solution.py:651
  59.2 13.1 %collective-permute-start.19 = (bf16[1,576,128]{2,1,0:T(8,128)(2,1)S(1)}, bf16[1,576,128]{2,1,0:T(8,128)(2,1)S(1)}, u32[]{:S(2)}, u32[]{:S(2)}) collective-permute-start(bf16[1,576,128]{2,1,0:T(8,128)(2,1)S(1)} %get-tuple-element.156), channel_id=1, source_target_pairs={{0,16},{4,20},{8,24},{12,28},{16,0},{20,4},{24,8},{28,12},{1,17},{... | collective-permute-start | bytes 442376 | tf_op jit(solution)/shard_map/ppermute | solution.py:651
  60.3 12.0 %collective-permute-start.20 = (bf16[1,576,128]{2,1,0:T(8,128)(2,1)S(1)}, bf16[1,576,128]{2,1,0:T(8,128)(2,1)S(1)}, u32[]{:S(2)}, u32[]{:S(2)}) collective-permute-start(bf16[1,576,128]{2,1,0:T(8,128)(2,1)S(1)} %get-tuple-element.157), channel_id=1, source_target_pairs={{0,24},{4,28},{8,16},{12,20},{16,8},{20,12},{24,0},{28,4},{1,25},{... | collective-permute-start | bytes 442376 | tf_op jit(solution)/shard_map/ppermute | solution.py:651
  61.6 5.9 %collective-permute-start.16 = (bf16[4,16,128]{2,1,0:T(8,128)(2,1)S(1)}, bf16[4,16,128]{2,1,0:T(8,128)(2,1)S(1)}, u32[]{:S(2)}, u32[]{:S(2)}) collective-permute-start(bf16[4,16,128]{2,1,0:T(8,128)(2,1)S(1)} %get-tuple-element.164), channel_id=1, source_target_pairs={{0,4},{4,0},{8,12},{12,8},{16,20},{20,16},{24,28},{28,24},{1,5},{5... | collective-permute-start | bytes 49160 | tf_op jit(solution)/shard_map/ppermute | solution.py:651
  67.5 9.5 %collective-permute-start.25 = (bf16[256,256]{1,0:T(8,128)(2,1)S(1)}, bf16[256,256]{1,0:T(8,128)(2,1)S(1)}, u32[]{:S(2)}, u32[]{:S(2)}) collective-permute-start(bf16[256,256]{1,0:T(8,128)(2,1)S(1)} %sumroutea.1.own_ref), channel_id=1, source_target_pairs={{0,2},{1,3},{2,0},{3,1},{4,6},{5,7},{6,4},{7,5},{8,10},{9,11},{10,... | collective-permute-start | bytes 393224 | tf_op jit(solution)/shard_map/ppermute | solution.py:648
  70.6 18.1 %collective-permute-start.15 = (bf16[2,128,512]{2,1,0:T(8,128)(2,1)S(1)}, bf16[2,128,512]{2,1,0:T(8,128)(2,1)S(1)}, u32[]{:S(2)}, u32[]{:S(2)}) collective-permute-start(bf16[2,128,512]{2,1,0:T(8,128)(2,1)S(1)} %get-tuple-element.163), channel_id=1, source_target_pairs={{0,2},{1,3},{2,0},{3,1},{4,6},{5,7},{6,4},{7,5},{8,10},{9,11},{10,... | collective-permute-start | bytes 786440 | tf_op jit(solution)/shard_map/ppermute | solution.py:648
  72.3 10.0 %collective-permute-start.23 = (bf16[1,592,128]{2,1,0:T(8,128)(2,1)S(1)}, bf16[1,592,128]{2,1,0:T(8,128)(2,1)S(1)}, u32[]{:S(2)}, u32[]{:S(2)}) collective-permute-start(bf16[1,592,128]{2,1,0:T(8,128)(2,1)S(1)} %get-tuple-element.176), channel_id=1, source_target_pairs={{0,8},{4,12},{8,0},{12,4},{16,24},{20,28},{24,16},{28,20},{1,9},{5... | collective-permute-start | bytes 454664 | tf_op jit(solution)/shard_map/ppermute | solution.py:651
  74.4 13.4 %collective-permute-start.22 = (bf16[1,592,128]{2,1,0:T(8,128)(2,1)S(1)}, bf16[1,592,128]{2,1,0:T(8,128)(2,1)S(1)}, u32[]{:S(2)}, u32[]{:S(2)}) collective-permute-start(bf16[1,592,128]{2,1,0:T(8,128)(2,1)S(1)} %get-tuple-element.174), channel_id=1, source_target_pairs={{0,16},{4,20},{8,24},{12,28},{16,0},{20,4},{24,8},{28,12},{1,17},{... | collective-permute-start | bytes 454664 | tf_op jit(solution)/shard_map/ppermute | solution.py:651
  75.5 12.3 %collective-permute-start.21 = (bf16[1,592,128]{2,1,0:T(8,128)(2,1)S(1)}, bf16[1,592,128]{2,1,0:T(8,128)(2,1)S(1)}, u32[]{:S(2)}, u32[]{:S(2)}) collective-permute-start(bf16[1,592,128]{2,1,0:T(8,128)(2,1)S(1)} %get-tuple-element.172), channel_id=1, source_target_pairs={{0,24},{4,28},{8,16},{12,20},{16,8},{20,12},{24,0},{28,4},{1,25},{... | collective-permute-start | bytes 454664 | tf_op jit(solution)/shard_map/ppermute | solution.py:651
  77.1 5.2 %collective-permute-start.24 = (bf16[576,128]{1,0:T(8,128)(2,1)S(1)}, bf16[576,128]{1,0:T(8,128)(2,1)S(1)}, u32[]{:S(2)}, u32[]{:S(2)}) collective-permute-start(bf16[576,128]{1,0:T(8,128)(2,1)S(1)} %sumrouteb.1.own_ref), channel_id=1, source_target_pairs={{0,2},{1,3},{2,0},{3,1},{4,6},{5,7},{6,4},{7,5},{8,10},{9,11},{10,... | collective-permute-start | bytes 442376 | tf_op jit(solution)/shard_map/ppermute | solution.py:648
  87.9 5.3 %collective-permute-start.26 = (bf16[592,128]{1,0:T(8,128)(2,1)S(1)}, bf16[592,128]{1,0:T(8,128)(2,1)S(1)}, u32[]{:S(2)}, u32[]{:S(2)}) collective-permute-start(bf16[592,128]{1,0:T(8,128)(2,1)S(1)} %sumroutec.1.own_ref), channel_id=1, source_target_pairs={{0,2},{1,3},{2,0},{3,1},{4,6},{5,7},{6,4},{7,5},{8,10},{9,11},{10,... | collective-permute-start | bytes 454664 | tf_op jit(solution)/shard_map/ppermute | solution.py:648
  88.2 3.4 %collective-permute-start.28 = (bf16[576,128]{1,0:T(8,128)(2,1)S(1)}, bf16[576,128]{1,0:T(8,128)(2,1)S(1)}, u32[]{:S(2)}, u32[]{:S(2)}) collective-permute-start(bf16[576,128]{1,0:T(8,128)(2,1)S(1)} %sumrouteb.1.own_ref), channel_id=1, source_target_pairs={{0,1},{1,0},{2,3},{3,2},{4,5},{5,4},{6,7},{7,6},{8,9},{9,8},{10,11... | collective-permute-start | bytes 442376 | tf_op jit(solution)/shard_map/ppermute | solution.py:645
  88.2 3.4 %collective-permute-start.29 = (bf16[576,128]{1,0:T(8,128)(2,1)S(1)}, bf16[576,128]{1,0:T(8,128)(2,1)S(1)}, u32[]{:S(2)}, u32[]{:S(2)}) collective-permute-start(bf16[576,128]{1,0:T(8,128)(2,1)S(1)} %collective-permute-done.24.far_ref), channel_id=1, source_target_pairs={{0,1},{1,0},{2,3},{3,2},{4,5},{5,4},{6,7},{7,6},{8,9},{9,8},{10,11... | collective-permute-start | bytes 442376 | tf_op jit(solution)/shard_map/ppermute | solution.py:645
  88.7 2.0 %collective-permute-start.30 = (bf16[256,256]{1,0:T(8,128)(2,1)S(1)}, bf16[256,256]{1,0:T(8,128)(2,1)S(1)}, u32[]{:S(2)}, u32[]{:S(2)}) collective-permute-start(bf16[256,256]{1,0:T(8,128)(2,1)S(1)} %sumroutea.1.own_ref), channel_id=1, source_target_pairs={{0,1},{1,0},{2,3},{3,2},{4,5},{5,4},{6,7},{7,6},{8,9},{9,8},{10,11... | collective-permute-start | bytes 393224 | tf_op jit(solution)/shard_map/ppermute | solution.py:645
  88.7 2.0 %collective-permute-start.31 = (bf16[256,256]{1,0:T(8,128)(2,1)S(1)}, bf16[256,256]{1,0:T(8,128)(2,1)S(1)}, u32[]{:S(2)}, u32[]{:S(2)}) collective-permute-start(bf16[256,256]{1,0:T(8,128)(2,1)S(1)} %collective-permute-done.25.far_ref), channel_id=1, source_target_pairs={{0,1},{1,0},{2,3},{3,2},{4,5},{5,4},{6,7},{7,6},{8,9},{9,8},{10,11... | collective-permute-start | bytes 393224 | tf_op jit(solution)/shard_map/ppermute | solution.py:645
  90.7 2.6 %collective-permute-start.27 = (bf16[592,128]{1,0:T(8,128)(2,1)S(1)}, bf16[592,128]{1,0:T(8,128)(2,1)S(1)}, u32[]{:S(2)}, u32[]{:S(2)}) collective-permute-start(bf16[592,128]{1,0:T(8,128)(2,1)S(1)} %sumroutec.1.own_ref), channel_id=1, source_target_pairs={{0,1},{1,0},{2,3},{3,2},{4,5},{5,4},{6,7},{7,6},{8,9},{9,8},{10,11... | collective-permute-start | bytes 454664 | tf_op jit(solution)/shard_map/ppermute | solution.py:645
  93.2 1.4 %collective-permute-start.32 = (bf16[592,128]{1,0:T(8,128)(2,1)S(1)}, bf16[592,128]{1,0:T(8,128)(2,1)S(1)}, u32[]{:S(2)}, u32[]{:S(2)}) collective-permute-start(bf16[592,128]{1,0:T(8,128)(2,1)S(1)} %collective-permute-done.26.far_ref), channel_id=1, source_target_pairs={{0,1},{1,0},{2,3},{3,2},{4,5},{5,4},{6,7},{7,6},{8,9},{9,8},{10,11... | collective-permute-start | bytes 454664 | tf_op jit(solution)/shard_map/ppermute | solution.py:645

commit v9 on v8

--- a/solution.py
+++ b/solution.py
@@ -766,14 +766,14 @@
     )
     vec_got = to_batch(vec_send, 1)
     parts_b, got_b = spread("routeb", 1, after(keep2, vec_keep, shard_a), got2)
+    parts_c, got_c = spread("routec", 1, keep1, got1, (vec_keep, vec_got))
     out_own, image_send = call(
         output_kernel, "output", [((192, C), BF16), ((2, 128, C), BF16)], [img16], 10,
-        kinds, after(middle, *parts_b), mixed, vecs, proj_weight, grad_send,
+        kinds, after(middle, *got_b), mixed, vecs, proj_weight, grad_send,
     )
     image_away = to_chip(image_send)
-    parts_c, got_c = spread("routec", 1, keep1, got1, (vec_keep, vec_got), behind=got_b)
     shard_b = finish("routeb", parts_b, together(got_b, parts_c[0]))
-    gathered_a = gather(shard_a)
+    gathered_a = gather(after(shard_a, *got_b))
     gathered_b = gather(shard_b)
     shard_c = finish(
         "routec", parts_c, together(got_c[::-1], gathered_b[1], gathered_a[1])

time: 96.1 us -> 101 us (1.051)
  starting transfers between devices: 32.5 us -> 39 us
  waiting for transfers between devices: 22 us -> 20.1 us
    ppermute x13, starting transfers between devices: 19 us -> 23.7 us  [to_batch(): return lax.ppermute(v, 'batch', [(i, i ^ change) for i in range(batches)])]
    ppermute x9, waiting for transfers between devices: 6.38 us -> 3.2 us  [to_chip(): return lax.ppermute(v, 'height', [(i, i ^ 2) for i in range(4)])]
    ppermute x9, starting transfers between devices: 9.81 us -> 11.3 us  [to_chip(): return lax.ppermute(v, 'height', [(i, i ^ 2) for i in range(4)])]
    ppermute x13, waiting for transfers between devices: 13.4 us -> 14.8 us  [to_batch(): return lax.ppermute(v, 'batch', [(i, i ^ change) for i in range(batches)])]
  transfers between devices with their start and end apart: 33 -> 33, of which waited for: 10 -> 10; matrix products, arithmetic and copies ran while one was open for 0% -> 0% of each run, Pallas kernels for 38% -> 36%
where the time goes in v9:
time: 101 us; the launch traced here: 100 us
  Pallas kernels  39.2 us (39%)
  starting transfers between devices  39 us (39%)
  waiting for transfers between devices  20.1 us (20%)
  between operations  1.28 us (1%)
    pallas_call x20, Pallas kernels, call(): pl.pallas_call(kernel, name=name, out_shape=[jax.ShapeDtypeStruct(shape,...  39.2 us
    ppermute x13, starting transfers between devices, to_batch(): return lax.ppermute(v, 'batch', [(i, i ^ change) for i in range(batches)])  23.7 us
    ppermute x13, waiting for transfers between devices, to_batch(): return lax.ppermute(v, 'batch', [(i, i ^ change) for i in range(batches)])  14.8 us
    ppermute x9, starting transfers between devices, to_chip(): return lax.ppermute(v, 'height', [(i, i ^ 2) for i in range(4)])  11.3 us
    ppermute x9, waiting for transfers between devices, to_chip(): return lax.ppermute(v, 'height', [(i, i ^ 2) for i in range(4)])  3.2 us
    ppermute x10, starting transfers between devices, to_core(): return lax.ppermute(v, 'height', [(i, i ^ 1) for i in range(4)])  2.68 us
  transfers between devices with their start and end apart: 33, of which 10 were waited for; matrix products, arithmetic and copies ran while one was open for 0% of the time, Pallas kernels for 36%

profile of v9, /device:TPU:0, one launch (start us, length us, event | category | flops | bytes accessed | tf_op | source)
XLA Modules:
  0.0 100.5 jit_solution(13967820780141416440)
XLA Ops:
  0.8 0.0 slice-start
  0.8 0.0 slice-start.2
  0.8 1.9 %pack.1 = (s32[2]{0:T(128)}, bf16[128,512]{1,0:T(8,128)(2,1)}, bf16[192,512]{1,0:T(8,128)(2,1)}) custom-call(s32[2]{0:T(128)} %bucket_hbm.1, bf16[2,6,32,512]{3,2,1,0:T(8,128)(2,1)} %x_hbm.1), custom_call_target="tpu_custom_call" | custom-call | flops 10737418240 | bytes 1024 | tf_op jit(solution)/shard_map/pack/pallas_call | solution.py:593
  2.7 3.0 %collective-permute-start.1 = (bf16[128,512]{1,0:T(8,128)(2,1)}, bf16[128,512]{1,0:T(8,128)(2,1)S(1)}, u32[]{:S(2)}, u32[]{:S(2)}) collective-permute-start(bf16[128,512]{1,0:T(8,128)(2,1)} %get-tuple-element.112), channel_id=1, source_target_pairs={{0,2},{1,3},{2,0},{3,1},{4,6},{5,7},{6,4},{7,5},{8,10},{9,11},{10,... | collective-permute-start | bytes 393224 | tf_op jit(solution)/shard_map/ppermute | solution.py:648
  5.9 0.0 copy-start.2
  5.9 0.8 copy-done.2
  6.7 0.6 stack.1
  7.3 0.0 copy-start
  7.3 0.0 copy-start.4
  7.3 0.0 copy-start.5
  7.3 0.6 collective-permute-start.3
  7.9 0.1 collective-permute-start.4
  8.0 1.4 %collective-permute-start.5 = (bf16[160,512]{1,0:T(8,128)(2,1)S(1)}, bf16[160,512]{1,0:T(8,128)(2,1)S(1)}, u32[]{:S(2)}, u32[]{:S(2)}) collective-permute-start(bf16[160,512]{1,0:T(8,128)(2,1)S(1)} %get-tuple-element.118), channel_id=1, source_target_pairs={{0,3},{1,2},{2,1},{3,0},{4,7},{5,6},{6,5},{7,4},{8,11},{9,10},{10,... | collective-permute-start | bytes 491528 | tf_op jit(solution)/shard_map/ppermute | solution.py:684
  9.3 0.1 collective-permute-done.1.received
  9.5 0.6 collective-permute-start.2
  10.1 1.0 collective-permute-done.2.partner_received
  11.1 5.4 %first.1 = (bf16[512,512]{1,0:T(8,128)(2,1)S(1)}, f32[512,512]{1,0:T(8,128)S(1)}, bf16[512,512]{1,0:T(8,128)(2,1)S(1)}, f32[8,512]{1,0:T(8,128)S(1)}, bf16[512,5...) custom-call(s32[2]{0:T(128)S(1)} %copy-done.3, bf16[192,512]{1,0:T(8,128)(2,1)S(1)} %copy-done.1, ...), custom_call_target="tpu_custom_call" | custom-call | flops 21474836 | bytes 1024 | tf_op jit(solution)/shard_map/first/pallas_call | solution.py:593
  16.4 1.9 %collective-permute-start.6 = (bf16[2,256,512]{2,1,0:T(8,128)(2,1)S(1)}, bf16[2,256,512]{2,1,0:T(8,128)(2,1)S(1)}, u32[]{:S(2)}, u32[]{:S(2)}) collective-permute-start(bf16[2,256,512]{2,1,0:T(8,128)(2,1)S(1)} %get-tuple-element.121), channel_id=1, source_target_pairs={{0,2},{1,3},{2,0},{3,1},{4,6},{5,7},{6,4},{7,5},{8,10},{9,11},{10,... | collective-permute-start | bytes 1572872 | tf_op jit(solution)/shard_map/ppermute | solution.py:648
  18.4 9.6 %second.1 = (f32[512,512]{1,0:T(8,128)S(1)}, bf16[512,512]{1,0:T(8,128)(2,1)S(1)}, bf16[512,512]{1,0:T(8,128)(2,1)S(1)}, f32[512,512]{1,0:T(8,128)S(1)}, bf16[4,...) custom-call(s32[2]{0:T(128)S(1)} %copy-done.3, ...), custom_call_target="tpu_custom_call" | custom-call | flops 32212254720 | bytes 1024 | tf_op jit(solution)/shard_map/second/pallas_call | solution.py:593
  28.0 0.3 collective-permute-start.8
  28.3 1.5 %collective-permute-start.9 = (bf16[4,256,256]{2,1,0:T(8,128)(2,1)S(1)}, bf16[4,256,256]{2,1,0:T(8,128)(2,1)S(1)}, u32[]{:S(2)}, u32[]{:S(2)}) collective-permute-start(bf16[4,256,256]{2,1,0:T(8,128)(2,1)S(1)} %get-tuple-element.135), channel_id=1, source_target_pairs={{0,4},{4,0},{8,12},{12,8},{16,20},{20,16},{24,28},{28,24},{1,5},{5... | collective-permute-start | bytes 1572872 | tf_op jit(solution)/shard_map/ppermute | solution.py:651
  29.8 1.1 %collective-permute-done.6.half_t = bf16[2,256,512]{2,1,0:T(8,128)(2,1)S(1)} collective-permute-done((bf16[2,256,512]{2,1,0:T(8,128)(2,1)S(1)}, bf16[2,256,512]{2,1,0:T(8,128)(2,1)S(1)}, u32[]{:S(2)}, u32[]{:S(2)}) %collective-permute-start.6) | collective-permute-done | bytes 524320 | tf_op jit(solution)/shard_map/ppermute | solution.py:648
  30.8 4.3 %third.1 = (bf16[512,512]{1,0:T(8,128)(2,1)S(1)}, bf16[512,128]{1,0:T(8,128)(2,1)S(1)}, bf16[512,128]{1,0:T(8,128)(2,1)S(1)}, f32[8,512]{1,0:T(8,128)S(1)}) custom-call(s32[2]{0:T(128)S(1)} %copy-done.3, bf16[512,512]{1,0:T(8,128)(2,1)S(1)} %get-tuple-element.123.grad2_ref, f32[512,512]{1,0:T(8,128)S(1)} %get-tuple-element.124.conv_ref, ...), custom_call_target="tpu_custom_call" | custom-call | flops 21474836480 | bytes 1024 | tf_op jit(solution)/shard_map/third/pallas_call | solution.py:593
  35.2 3.3 %weight2.5 = (bf16[4,576,128]{2,1,0:T(8,128)(2,1)S(1)}, bf16[4,576,128]{2,1,0:T(8,128)(2,1)S(1)}) custom-call(s32[2]{0:T(128)S(1)} %copy-done.3, bf16[512,512]{1,0:T(8,128)(2,1)S(1)} %get-tuple-element.120.act_t, bf16[2,256,512]{2,1,0:T(8,128)(2,1)S(1)} %collective-permute-done.6.half_t, bf16[2,256,512]{2,1,0:T(8,128)(2,1)S(1)} %collective-permute-done.7.partner_half_t, ...), custom_call_target="tpu_custom_call" | custom-call | flops 1073741824 | bytes 1024 | tf_op jit(solution)/shard_map/weight2/pallas_call | solution.py:593
  38.5 1.8 %collective-permute-start.14 = (bf16[4,576,128]{2,1,0:T(8,128)(2,1)S(1)}, bf16[4,576,128]{2,1,0:T(8,128)(2,1)S(1)}, u32[]{:S(2)}, u32[]{:S(2)}) collective-permute-start(bf16[4,576,128]{2,1,0:T(8,128)(2,1)S(1)} %get-tuple-element.133), channel_id=1, source_target_pairs={{0,4},{4,0},{8,12},{12,8},{16,20},{20,16},{24,28},{28,24},{1,5},{5... | collective-permute-start | bytes 1769480 | tf_op jit(solution)/shard_map/ppermute | solution.py:651
  40.3 1.8 %collective-permute-start.10 = (bf16[512,128]{1,0:T(8,128)(2,1)S(1)}, bf16[512,128]{1,0:T(8,128)(2,1)S(1)}, u32[]{:S(2)}, u32[]{:S(2)}) collective-permute-start(bf16[512,128]{1,0:T(8,128)(2,1)S(1)} %get-tuple-element.141), channel_id=1, source_target_pairs={{0,2},{1,3},{2,0},{3,1},{4,6},{5,7},{6,4},{7,5},{8,10},{9,11},{10,... | collective-permute-start | bytes 393224 | tf_op jit(solution)/shard_map/ppermute | solution.py:648
  42.1 0.1 routea1.1
  42.2 1.6 %collective-permute-start.11 = (bf16[1,256,256]{2,1,0:T(8,128)(2,1)S(1)}, bf16[1,256,256]{2,1,0:T(8,128)(2,1)S(1)}, u32[]{:S(2)}, u32[]{:S(2)}) collective-permute-start(bf16[1,256,256]{2,1,0:T(8,128)(2,1)S(1)} %get-tuple-element.137), channel_id=1, source_target_pairs={{0,8},{4,12},{8,0},{12,4},{16,24},{20,28},{24,16},{28,20},{1,9},{5... | collective-permute-start | bytes 393224 | tf_op jit(solution)/shard_map/ppermute | solution.py:651
  43.8 2.6 %collective-permute-start.12 = (bf16[1,256,256]{2,1,0:T(8,128)(2,1)S(1)}, bf16[1,256,256]{2,1,0:T(8,128)(2,1)S(1)}, u32[]{:S(2)}, u32[]{:S(2)}) collective-permute-start(bf16[1,256,256]{2,1,0:T(8,128)(2,1)S(1)} %get-tuple-element.138), channel_id=1, source_target_pairs={{0,16},{4,20},{8,24},{12,28},{16,0},{20,4},{24,8},{28,12},{1,17},{... | collective-permute-start | bytes 393224 | tf_op jit(solution)/shard_map/ppermute | solution.py:651
  46.4 0.2 collective-permute-start.13
  46.7 3.1 %weight1.4 = (bf16[4,576,128]{2,1,0:T(8,128)(2,1)S(1)}, bf16[4,576,128]{2,1,0:T(8,128)(2,1)S(1)}) custom-call(s32[2]{0:T(128)S(1)} %copy-done.3, bf16[512,512]{1,0:T(8,128)(2,1)S(1)} %get-tuple-element.131.act_t, bf16[2,256,512]{2,1,0:T(8,128)(2,1)S(1)} %collective-permute-done.6.half_t, bf16[2,256,512]{2,1,0:T(8,128)(2,1)S(1)} %collective-permute-done.7.partner_half_t, ...), custom_call_target="tpu_custom_call" | custom-call | flops 3221225472 | bytes 1024 | tf_op jit(solution)/shard_map/weight1/pallas_call | solution.py:593
  49.7 1.4 %collective-permute-start.20 = (bf16[4,576,128]{2,1,0:T(8,128)(2,1)S(1)}, bf16[4,576,128]{2,1,0:T(8,128)(2,1)S(1)}, u32[]{:S(2)}, u32[]{:S(2)}) collective-permute-start(bf16[4,576,128]{2,1,0:T(8,128)(2,1)S(1)} %get-tuple-element.142), channel_id=1, source_target_pairs={{0,4},{4,0},{8,12},{12,8},{16,20},{20,16},{24,28},{28,24},{1,5},{5... | collective-permute-start | bytes 1769480 | tf_op jit(solution)/shard_map/ppermute | solution.py:651
  51.2 4.6 %fourth.1 = (bf16[192,512]{1,0:T(8,128)(2,1)S(1)}, bf16[128,512]{1,0:T(8,128)(2,1)S(1)}, bf16[4,16,128]{2,1,0:T(8,128)(2,1)S(1)}, bf16[4,16,128]{2,1,0:T(8,128)(2,1)S(1)}) custom-call(s32[2]{0:T(128)S(1)} %copy-done.3, bf16[512,512]{1,0:T(8,128)(2,1)S(1)} %get-tuple-element.143.grad1_ref, bf16[512,512]{1,0:T(8,128)(2,1)S(1)} %get-tuple-element.115.image_ref, ...), custom_call_target="tpu_custom_call" | custom-call | flops 536870912 | bytes 1024 | tf_op jit(solution)/shard_map/fourth/pallas_call | solution.py:593
  55.8 1.0 collective-permute-done.12.refs_2_
  56.8 0.1 sumroutea.1.own_ref
  56.8 0.1 routeb1.1
  57.0 2.1 %collective-permute-start.15 = (bf16[1,576,128]{2,1,0:T(8,128)(2,1)S(1)}, bf16[1,576,128]{2,1,0:T(8,128)(2,1)S(1)}, u32[]{:S(2)}, u32[]{:S(2)}) collective-permute-start(bf16[1,576,128]{2,1,0:T(8,128)(2,1)S(1)} %get-tuple-element.152), channel_id=1, source_target_pairs={{0,8},{4,12},{8,0},{12,4},{16,24},{20,28},{24,16},{28,20},{1,9},{5... | collective-permute-start | bytes 442376 | tf_op jit(solution)/shard_map/ppermute | solution.py:651
  59.2 1.1 %collective-permute-start.16 = (bf16[1,576,128]{2,1,0:T(8,128)(2,1)S(1)}, bf16[1,576,128]{2,1,0:T(8,128)(2,1)S(1)}, u32[]{:S(2)}, u32[]{:S(2)}) collective-permute-start(bf16[1,576,128]{2,1,0:T(8,128)(2,1)S(1)} %get-tuple-element.153), channel_id=1, source_target_pairs={{0,16},{4,20},{8,24},{12,28},{16,0},{20,4},{24,8},{28,12},{1,17},{... | collective-permute-start | bytes 442376 | tf_op jit(solution)/shard_map/ppermute | solution.py:651
  60.3 1.3 %collective-permute-start.17 = (bf16[1,576,128]{2,1,0:T(8,128)(2,1)S(1)}, bf16[1,576,128]{2,1,0:T(8,128)(2,1)S(1)}, u32[]{:S(2)}, u32[]{:S(2)}) collective-permute-start(bf16[1,576,128]{2,1,0:T(8,128)(2,1)S(1)} %get-tuple-element.154), channel_id=1, source_target_pairs={{0,24},{4,28},{8,16},{12,20},{16,8},{20,12},{24,0},{28,4},{1,25},{... | collective-permute-start | bytes 442376 | tf_op jit(solution)/shard_map/ppermute | solution.py:651
  61.6 0.5 collective-permute-start.19
  62.1 5.2 %collective-permute-done.20.got_ref = bf16[4,576,128]{2,1,0:T(8,128)(2,1)S(1)} collective-permute-done((bf16[4,576,128]{2,1,0:T(8,128)(2,1)S(1)}, bf16[4,576,128]{2,1,0:T(8,128)(2,1)S(1)}, u32[]{:S(2)}, u32[]{:S(2)}) %collective-permute-start.20) | collective-permute-done | bytes 589856 | tf_op jit(solution)/shard_map/ppermute | solution.py:651
  67.4 0.1 routec1.1
  67.5 0.0 collective-permute-done.19.got_ref
  67.5 3.7 %collective-permute-start.21 = (bf16[1,592,128]{2,1,0:T(8,128)(2,1)S(1)}, bf16[1,592,128]{2,1,0:T(8,128)(2,1)S(1)}, u32[]{:S(2)}, u32[]{:S(2)}) collective-permute-start(bf16[1,592,128]{2,1,0:T(8,128)(2,1)S(1)} %get-tuple-element.168), channel_id=1, source_target_pairs={{0,24},{4,28},{8,16},{12,20},{16,8},{20,12},{24,0},{28,4},{1,25},{... | collective-permute-start | bytes 454664 | tf_op jit(solution)/shard_map/ppermute | solution.py:651
  71.2 4.5 %collective-permute-done.16.refs_2_ = bf16[1,576,128]{2,1,0:T(8,128)(2,1)S(1)} collective-permute-done((bf16[1,576,128]{2,1,0:T(8,128)(2,1)S(1)}, bf16[1,576,128]{2,1,0:T(8,128)(2,1)S(1)}, u32[]{:S(2)}, u32[]{:S(2)}) %collective-permute-start.16) | collective-permute-done | bytes 147488 | tf_op jit(solution)/shard_map/ppermute | solution.py:651
  75.7 1.0 %output.1 = (bf16[192,512]{1,0:T(8,128)(2,1)S(1)}, bf16[2,128,512]{2,1,0:T(8,128)(2,1)S(1)}) custom-call(s32[2]{0:T(128)S(1)} %copy-done.3, f32[512,512]{1,0:T(8,128)S(1)} %get-tuple-element.155.middle_ref, bf16[512,512]{1,0:T(8,128)(2,1)S(1)} %get-tuple-element.156.mixed_ref, f32[16,512]{1,0:T(8,128)S(1)} %get-tuple-element.113.vecs, ...), custom_call_target="tpu_custom_call" | custom-call | flops 21474836 | bytes 1024 | tf_op jit(solution)/shard_map/output/pallas_call | solution.py:593
  76.7 0.1 collective-permute-start.18
  76.8 5.8 %collective-permute-start.22 = (bf16[1,592,128]{2,1,0:T(8,128)(2,1)S(1)}, bf16[1,592,128]{2,1,0:T(8,128)(2,1)S(1)}, u32[]{:S(2)}, u32[]{:S(2)}) collective-permute-start(bf16[1,592,128]{2,1,0:T(8,128)(2,1)S(1)} %get-tuple-element.169), channel_id=1, source_target_pairs={{0,16},{4,20},{8,24},{12,28},{16,0},{20,4},{24,8},{28,12},{1,17},{... | collective-permute-start | bytes 454664 | tf_op jit(solution)/shard_map/ppermute | solution.py:651
  82.6 0.1 sumrouteb.1.own_ref
  82.6 2.0 %collective-permute-start.24 = (bf16[576,128]{1,0:T(8,128)(2,1)S(1)}, bf16[576,128]{1,0:T(8,128)(2,1)S(1)}, u32[]{:S(2)}, u32[]{:S(2)}) collective-permute-start(bf16[576,128]{1,0:T(8,128)(2,1)S(1)} %sumrouteb.1.own_ref), channel_id=1, source_target_pairs={{0,2},{1,3},{2,0},{3,1},{4,6},{5,7},{6,4},{7,5},{8,10},{9,11},{10,... | collective-permute-start | bytes 442376 | tf_op jit(solution)/shard_map/ppermute | solution.py:648
  84.6 0.1 collective-permute-start.25
  84.7 2.7 %collective-permute-done.22.refs_2_ = bf16[1,592,128]{2,1,0:T(8,128)(2,1)S(1)} collective-permute-done((bf16[1,592,128]{2,1,0:T(8,128)(2,1)S(1)}, bf16[1,592,128]{2,1,0:T(8,128)(2,1)S(1)}, u32[]{:S(2)}, u32[]{:S(2)}) %collective-permute-start.22) | collective-permute-done | bytes 151584 | tf_op jit(solution)/shard_map/ppermute | solution.py:651
  87.4 1.4 %collective-permute-done.23.refs_3_ = bf16[1,592,128]{2,1,0:T(8,128)(2,1)S(1)} collective-permute-done((bf16[1,592,128]{2,1,0:T(8,128)(2,1)S(1)}, bf16[1,592,128]{2,1,0:T(8,128)(2,1)S(1)}, u32[]{:S(2)}, u32[]{:S(2)}) %collective-permute-start.23) | collective-permute-done | bytes 151584 | tf_op jit(solution)/shard_map/ppermute | solution.py:651
  88.9 2.0 %collective-permute-done.25.far_ref = bf16[256,256]{1,0:T(8,128)(2,1)S(1)} collective-permute-done((bf16[256,256]{1,0:T(8,128)(2,1)S(1)}, bf16[256,256]{1,0:T(8,128)(2,1)S(1)}, u32[]{:S(2)}, u32[]{:S(2)}) %collective-permute-start.25) | collective-permute-done | bytes 131104 | tf_op jit(solution)/shard_map/ppermute | solution.py:648
  90.9 0.1 sumroutec.1.own_ref
  91.0 2.0 %collective-permute-start.26 = (bf16[592,128]{1,0:T(8,128)(2,1)S(1)}, bf16[592,128]{1,0:T(8,128)(2,1)S(1)}, u32[]{:S(2)}, u32[]{:S(2)}) collective-permute-start(bf16[592,128]{1,0:T(8,128)(2,1)S(1)} %sumroutec.1.own_ref), channel_id=1, source_target_pairs={{0,2},{1,3},{2,0},{3,1},{4,6},{5,7},{6,4},{7,5},{8,10},{9,11},{10,... | collective-permute-start | bytes 454664 | tf_op jit(solution)/shard_map/ppermute | solution.py:648
  93.0 0.5 collective-permute-start.29
  93.5 0.5 collective-permute-start.31
  94.0 1.5 %unpack.1 = (bf16[2,6,32,512]{3,2,1,0:T(8,128)(2,1)}, bf16[2,6,32,512]{3,2,1,0:T(8,128)(2,1)}) custom-call(s32[2]{0:T(128)S(1)} %copy-done.3, bf16[192,512]{1,0:T(8,128)(2,1)S(1)} %get-tuple-element.158.out_own, bf16[192,512]{1,0:T(8,128)(2,1)S(1)} %get-tuple-element.159.grad_own, bf16[2,128,512]{2,1,0:T(8,128)(2,1)S(1)} %collective-permute-done.18.away_ref), custom_call_target="tpu_custom_call" | custom-call | flops 21474836 | bytes 1024 | tf_op jit(solution)/shard_map/unpack/pallas_call | solution.py:593
  95.5 0.9 joina.1
  96.4 1.2 %joinb.1 = f32[576,512]{1,0:T(8,128)} custom-call(bf16[576,128]{1,0:T(8,128)(2,1)S(1)} %sumrouteb.1.own_ref, bf16[576,128]{1,0:T(8,128)(2,1)S(1)} %collective-permute-done.24.far_ref, bf16[576,128]{1,0:T(8,128)(2,1)S(1)} %collective-permute-done.28.near_ref, bf16[576,128]{1,0:T(8,128)(2,1)S(1)} %collective-permute-done.29.diagonal_ref), custom_call_target="tpu_custom_call" | custom-call | flops 21474836 | bytes 1024 | tf_op jit(solution)/shard_map/joinb/pallas_call | solution.py:593
  97.6 0.5 collective-permute-start.32
  98.1 1.0 %collective-permute-done.32.diagonal_ref = bf16[592,128]{1,0:T(8,128)(2,1)S(1)} collective-permute-done((bf16[592,128]{1,0:T(8,128)(2,1)S(1)}, bf16[592,128]{1,0:T(8,128)(2,1)S(1)}, u32[]{:S(2)}, u32[]{:S(2)}) %collective-permute-start.32) | collective-permute-done | bytes 151584 | tf_op jit(solution)/shard_map/ppermute | solution.py:645
  99.1 1.2 %joinc.1 = (f32[576,512]{1,0:T(8,128)}, f32[1,64]{1,0:T(1,128)}, f32[1,64]{1,0:T(1,128)}, f32[1,64]{1,0:T(1,128)}, f32[1,64]{1,0:T(1,128)}, /*index=5*/f32[1,64]...) custom-call(bf16[592,128]{1,0:T(8,128)(2,1)S(1)} %sumroutec.1.own_re, ...), custom_call_target="tpu_custom_call" | custom-call | flops 21474836 | bytes 1024 | tf_op jit(solution)/shard_map/joinc/pallas_call | solution.py:593
  (70 shorter events, 0.2 us)
Async XLA Ops:
  0.7 5.1 %copy-start.8 = (f32[512]{0:T(512)S(1)}, f32[512]{0:T(512)}, u32[]{:S(2)}) copy-start(f32[512]{0:T(512)} %param.22) | copy-start | bytes 6148
  0.7 5.1 %copy-start.9 = (f32[512]{0:T(512)S(1)}, f32[512]{0:T(512)}, u32[]{:S(2)}) copy-start(f32[512]{0:T(512)} %param.23) | copy-start | bytes 6148
  0.7 5.1 %copy-start.18 = (f32[512]{0:T(512)S(1)}, f32[512]{0:T(512)}, u32[]{:S(2)}) copy-start(f32[512]{0:T(512)} %param.38) | copy-start | bytes 6148
  0.7 5.1 %copy-start.10 = (f32[512]{0:T(512)S(1)}, f32[512]{0:T(512)}, u32[]{:S(2)}) copy-start(f32[512]{0:T(512)} %param.25) | copy-start | bytes 6148
  0.7 5.1 %copy-start.11 = (f32[512]{0:T(512)S(1)}, f32[512]{0:T(512)}, u32[]{:S(2)}) copy-start(f32[512]{0:T(512)} %param.26) | copy-start | bytes 6148
  0.7 5.1 %copy-start.12 = (f32[512]{0:T(512)S(1)}, f32[512]{0:T(512)}, u32[]{:S(2)}) copy-start(f32[512]{0:T(512)} %param.27) | copy-start | bytes 6148
  0.7 5.1 %copy-start.13 = (f32[512]{0:T(512)S(1)}, f32[512]{0:T(512)}, u32[]{:S(2)}) copy-start(f32[512]{0:T(512)} %param.29) | copy-start | bytes 6148
  0.7 5.1 %copy-start.14 = (f32[512]{0:T(512)S(1)}, f32[512]{0:T(512)}, u32[]{:S(2)}) copy-start(f32[512]{0:T(512)} %param.30) | copy-start | bytes 6148
  0.7 5.1 %copy-start.15 = (f32[512]{0:T(512)S(1)}, f32[512]{0:T(512)}, u32[]{:S(2)}) copy-start(f32[512]{0:T(512)} %param.31) | copy-start | bytes 6148
  0.8 5.1 %copy-start.16 = (f32[512]{0:T(512)S(1)}, f32[512]{0:T(512)}, u32[]{:S(2)}) copy-start(f32[512]{0:T(512)} %param.33) | copy-start | bytes 6148
  0.8 5.1 %copy-start.17 = (f32[512]{0:T(512)S(1)}, f32[512]{0:T(512)}, u32[]{:S(2)}) copy-start(f32[512]{0:T(512)} %param.36) | copy-start | bytes 6148
  0.8 5.1 %copy-start.7 = (bf16[2,6,32,512]{3,2,1,0:T(8,128)(2,1)S(1)}, bf16[2,6,32,512]{3,2,1,0:T(8,128)(2,1)}, u32[]{:S(2)}) copy-start(bf16[2,6,32,512]{3,2,1,0:T(8,128)(2,1)} %cot_ref.1) | copy-start | bytes 1179652
  0.8 10.3 %slice-start = ((s8[4718592]{0:T(1024)(128)(4,1)}), s8[524288]{0:T(1024)(128)(4,1)S(1)}, s32[]{:S(2)}) async-start(s8[4718592]{0:T(1024)(128)(4,1)} %bitcast.22), calls=%async_computation | async-start | bytes 1048576
  0.8 17.5 %slice-start.2 = ((s8[4718592]{0:T(1024)(128)(4,1)}), s8[4194304]{0:T(1024)(128)(4,1)S(1)}, s32[]{:S(2)}) async-start(s8[4718592]{0:T(1024)(128)(4,1)} %bitcast.24), calls=%async_computation.2 | async-start | bytes 8388608
  2.7 6.7 %collective-permute-start.1 = (bf16[128,512]{1,0:T(8,128)(2,1)}, bf16[128,512]{1,0:T(8,128)(2,1)S(1)}, u32[]{:S(2)}, u32[]{:S(2)}) collective-permute-start(bf16[128,512]{1,0:T(8,128)(2,1)} %get-tuple-element.112), channel_id=1, source_target_pairs={{0,2},{1,3},{2,0},{3,1},{4,6},{5,7},{6,4},{7,5},{8,10},{9,11},{10,... | collective-permute-start | bytes 393224 | tf_op jit(solution)/shard_map/ppermute | solution.py:648
  5.8 4.3 %collective-permute-start = (bf16[192,512]{1,0:T(8,128)(2,1)}, bf16[192,512]{1,0:T(8,128)(2,1)S(1)}, u32[]{:S(2)}, u32[]{:S(2)}) collective-permute-start(bf16[192,512]{1,0:T(8,128)(2,1)} %get-tuple-element.111.own), channel_id=1, source_target_pairs={{0,1},{1,0},{2,3},{3,2},{4,5},{5,4},{6,7},{7,6},{8,9},{9,8},{10,11... | collective-permute-start | bytes 589832 | tf_op jit(solution)/shard_map/ppermute | solution.py:645
  5.8 5.3 %slice-start.1 = ((s8[4718592]{0:T(1024)(128)(4,1)}), s8[4194304]{0:T(1024)(128)(4,1)S(1)}, s32[]{:S(2)}) async-start(s8[4718592]{0:T(1024)(128)(4,1)} %bitcast.22), calls=%async_computation.1 | async-start | bytes 8388608
  5.9 0.8 copy-start.2
  6.7 4.4 %copy-start.1 = (bf16[192,512]{1,0:T(8,128)(2,1)S(1)}, bf16[192,512]{1,0:T(8,128)(2,1)}, u32[]{:S(2)}) copy-start(bf16[192,512]{1,0:T(8,128)(2,1)} %get-tuple-element.111.own) | copy-start | bytes 589828
  6.7 4.4 %copy-start.3 = (s32[2]{0:T(128)S(1)}, s32[2]{0:T(128)}, u32[]{:S(2)}) copy-start(s32[2]{0:T(128)} %get-tuple-element.110.kinds.bucket_ref) | copy-start | bytes 28
  6.7 11.6 %slice-start.3 = ((s8[4718592]{0:T(1024)(128)(4,1)}), s8[524288]{0:T(1024)(128)(4,1)S(1)}, s32[]{:S(2)}) async-start(s8[4718592]{0:T(1024)(128)(4,1)} %bitcast.24), calls=%async_computation.3 | async-start | bytes 1048576
  7.3 11.1 %copy-start = (bf16[512,512]{1,0:T(8,128)(2,1)S(1)}, bf16[512,512]{1,0:T(8,128)(2,1)}, u32[]{:S(2)}) copy-start(bf16[512,512]{1,0:T(8,128)(2,1)} %wp.3) | copy-start | bytes 1572868
  7.3 11.1 %copy-start.4 = (bf16[512,512]{1,0:T(8,128)(2,1)S(1)}, bf16[512,512]{1,0:T(8,128)(2,1)}, u32[]{:S(2)}) copy-start(bf16[512,512]{1,0:T(8,128)(2,1)} %wq.1) | copy-start | bytes 1572868
  7.3 11.0 %copy-start.5 = (bf16[512,512]{1,0:T(8,128)(2,1)S(1)}, bf16[512,512]{1,0:T(8,128)(2,1)}, u32[]{:S(2)}) copy-start(bf16[512,512]{1,0:T(8,128)(2,1)} %wk.1) | copy-start | bytes 1572868
  7.3 11.0 %copy-start.6 = (bf16[512,512]{1,0:T(8,128)(2,1)S(1)}, bf16[512,512]{1,0:T(8,128)(2,1)}, u32[]{:S(2)}) copy-start(bf16[512,512]{1,0:T(8,128)(2,1)} %wv.1) | copy-start | bytes 1572868
  7.3 11.0 %collective-permute-start.3 = (bf16[192,512]{1,0:T(8,128)(2,1)S(1)}, bf16[192,512]{1,0:T(8,128)(2,1)S(1)}, u32[]{:S(2)}, u32[]{:S(2)}) collective-permute-start(bf16[192,512]{1,0:T(8,128)(2,1)S(1)} %get-tuple-element.117.own), channel_id=1, source_target_pairs={{0,1},{1,0},{2,3},{3,2},{4,5},{5,4},{6,7},{7,6},{8,9},{9,8},{10,11... | collective-permute-start | bytes 589832 | tf_op jit(solution)/shard_map/ppermute | solution.py:645
  7.9 10.4 %collective-permute-start.4 = (bf16[160,512]{1,0:T(8,128)(2,1)S(1)}, bf16[160,512]{1,0:T(8,128)(2,1)S(1)}, u32[]{:S(2)}, u32[]{:S(2)}) collective-permute-start(bf16[160,512]{1,0:T(8,128)(2,1)S(1)} %get-tuple-element.118), channel_id=1, source_target_pairs={{0,2},{1,3},{2,0},{3,1},{4,6},{5,7},{6,4},{7,5},{8,10},{9,11},{10,... | collective-permute-start | bytes 491528 | tf_op jit(solution)/shard_map/ppermute | solution.py:648
  8.0 10.3 %collective-permute-start.5 = (bf16[160,512]{1,0:T(8,128)(2,1)S(1)}, bf16[160,512]{1,0:T(8,128)(2,1)S(1)}, u32[]{:S(2)}, u32[]{:S(2)}) collective-permute-start(bf16[160,512]{1,0:T(8,128)(2,1)S(1)} %get-tuple-element.118), channel_id=1, source_target_pairs={{0,3},{1,2},{2,1},{3,0},{4,7},{5,6},{6,5},{7,4},{8,11},{9,10},{10,... | collective-permute-start | bytes 491528 | tf_op jit(solution)/shard_map/ppermute | solution.py:684
  9.5 1.6 %collective-permute-start.2 = (bf16[128,512]{1,0:T(8,128)(2,1)S(1)}, bf16[128,512]{1,0:T(8,128)(2,1)S(1)}, u32[]{:S(2)}, u32[]{:S(2)}) collective-permute-start(bf16[128,512]{1,0:T(8,128)(2,1)S(1)} %collective-permute-done.1.received), channel_id=1, source_target_pairs={{0,1},{1,0},{2,3},{3,2},{4,5},{5,4},{6,7},{7,6},{8,9},{9,8},{10,11... | collective-permute-start | bytes 393224 | tf_op jit(solution)/shard_map/ppermute | solution.py:645
  16.4 14.4 %collective-permute-start.6 = (bf16[2,256,512]{2,1,0:T(8,128)(2,1)S(1)}, bf16[2,256,512]{2,1,0:T(8,128)(2,1)S(1)}, u32[]{:S(2)}, u32[]{:S(2)}) collective-permute-start(bf16[2,256,512]{2,1,0:T(8,128)(2,1)S(1)} %get-tuple-element.121), channel_id=1, source_target_pairs={{0,2},{1,3},{2,0},{3,1},{4,6},{5,7},{6,4},{7,5},{8,10},{9,11},{10,... | collective-permute-start | bytes 1572872 | tf_op jit(solution)/shard_map/ppermute | solution.py:648
  28.0 7.2 %collective-permute-start.8 = (bf16[512,128]{1,0:T(8,128)(2,1)S(1)}, bf16[512,128]{1,0:T(8,128)(2,1)S(1)}, u32[]{:S(2)}, u32[]{:S(2)}) collective-permute-start(bf16[512,128]{1,0:T(8,128)(2,1)S(1)} %get-tuple-element.128), channel_id=1, source_target_pairs={{0,2},{1,3},{2,0},{3,1},{4,6},{5,7},{6,4},{7,5},{8,10},{9,11},{10,... | collective-permute-start | bytes 393224 | tf_op jit(solution)/shard_map/ppermute | solution.py:648
  28.3 13.8 %collective-permute-start.9 = (bf16[4,256,256]{2,1,0:T(8,128)(2,1)S(1)}, bf16[4,256,256]{2,1,0:T(8,128)(2,1)S(1)}, u32[]{:S(2)}, u32[]{:S(2)}) collective-permute-start(bf16[4,256,256]{2,1,0:T(8,128)(2,1)S(1)} %get-tuple-element.135), channel_id=1, source_target_pairs={{0,4},{4,0},{8,12},{12,8},{16,20},{20,16},{24,28},{28,24},{1,5},{5... | collective-permute-start | bytes 1572872 | tf_op jit(solution)/shard_map/ppermute | solution.py:651
  30.8 4.3 %collective-permute-start.7 = (bf16[2,256,512]{2,1,0:T(8,128)(2,1)S(1)}, bf16[2,256,512]{2,1,0:T(8,128)(2,1)S(1)}, u32[]{:S(2)}, u32[]{:S(2)}) collective-permute-start(bf16[2,256,512]{2,1,0:T(8,128)(2,1)S(1)} %collective-permute-done.6.half_t), channel_id=1, source_target_pairs={{0,1},{1,0},{2,3},{3,2},{4,5},{5,4},{6,7},{7,6},{8,9},{9,8},{10,11... | collective-permute-start | bytes 1572872 | tf_op jit(solution)/shard_map/ppermute | solution.py:645
  38.5 18.3 %collective-permute-start.14 = (bf16[4,576,128]{2,1,0:T(8,128)(2,1)S(1)}, bf16[4,576,128]{2,1,0:T(8,128)(2,1)S(1)}, u32[]{:S(2)}, u32[]{:S(2)}) collective-permute-start(bf16[4,576,128]{2,1,0:T(8,128)(2,1)S(1)} %get-tuple-element.133), channel_id=1, source_target_pairs={{0,4},{4,0},{8,12},{12,8},{16,20},{20,16},{24,28},{28,24},{1,5},{5... | collective-permute-start | bytes 1769480 | tf_op jit(solution)/shard_map/ppermute | solution.py:651
  40.3 6.4 %collective-permute-start.10 = (bf16[512,128]{1,0:T(8,128)(2,1)S(1)}, bf16[512,128]{1,0:T(8,128)(2,1)S(1)}, u32[]{:S(2)}, u32[]{:S(2)}) collective-permute-start(bf16[512,128]{1,0:T(8,128)(2,1)S(1)} %get-tuple-element.141), channel_id=1, source_target_pairs={{0,2},{1,3},{2,0},{3,1},{4,6},{5,7},{6,4},{7,5},{8,10},{9,11},{10,... | collective-permute-start | bytes 393224 | tf_op jit(solution)/shard_map/ppermute | solution.py:648
  42.2 13.6 %collective-permute-start.11 = (bf16[1,256,256]{2,1,0:T(8,128)(2,1)S(1)}, bf16[1,256,256]{2,1,0:T(8,128)(2,1)S(1)}, u32[]{:S(2)}, u32[]{:S(2)}) collective-permute-start(bf16[1,256,256]{2,1,0:T(8,128)(2,1)S(1)} %get-tuple-element.137), channel_id=1, source_target_pairs={{0,8},{4,12},{8,0},{12,4},{16,24},{20,28},{24,16},{28,20},{1,9},{5... | collective-permute-start | bytes 393224 | tf_op jit(solution)/shard_map/ppermute | solution.py:651
  43.8 12.9 %collective-permute-start.12 = (bf16[1,256,256]{2,1,0:T(8,128)(2,1)S(1)}, bf16[1,256,256]{2,1,0:T(8,128)(2,1)S(1)}, u32[]{:S(2)}, u32[]{:S(2)}) collective-permute-start(bf16[1,256,256]{2,1,0:T(8,128)(2,1)S(1)} %get-tuple-element.138), channel_id=1, source_target_pairs={{0,16},{4,20},{8,24},{12,28},{16,0},{20,4},{24,8},{28,12},{1,17},{... | collective-permute-start | bytes 393224 | tf_op jit(solution)/shard_map/ppermute | solution.py:651
  46.4 10.3 %collective-permute-start.13 = (bf16[1,256,256]{2,1,0:T(8,128)(2,1)S(1)}, bf16[1,256,256]{2,1,0:T(8,128)(2,1)S(1)}, u32[]{:S(2)}, u32[]{:S(2)}) collective-permute-start(bf16[1,256,256]{2,1,0:T(8,128)(2,1)S(1)} %get-tuple-element.139), channel_id=1, source_target_pairs={{0,24},{4,28},{8,16},{12,20},{16,8},{20,12},{24,0},{28,4},{1,25},{... | collective-permute-start | bytes 393224 | tf_op jit(solution)/shard_map/ppermute | solution.py:651
  49.7 17.6 %collective-permute-start.20 = (bf16[4,576,128]{2,1,0:T(8,128)(2,1)S(1)}, bf16[4,576,128]{2,1,0:T(8,128)(2,1)S(1)}, u32[]{:S(2)}, u32[]{:S(2)}) collective-permute-start(bf16[4,576,128]{2,1,0:T(8,128)(2,1)S(1)} %get-tuple-element.142), channel_id=1, source_target_pairs={{0,4},{4,0},{8,12},{12,8},{16,20},{20,16},{24,28},{28,24},{1,5},{5... | collective-permute-start | bytes 1769480 | tf_op jit(solution)/shard_map/ppermute | solution.py:651
  57.0 14.2 %collective-permute-start.15 = (bf16[1,576,128]{2,1,0:T(8,128)(2,1)S(1)}, bf16[1,576,128]{2,1,0:T(8,128)(2,1)S(1)}, u32[]{:S(2)}, u32[]{:S(2)}) collective-permute-start(bf16[1,576,128]{2,1,0:T(8,128)(2,1)S(1)} %get-tuple-element.152), channel_id=1, source_target_pairs={{0,8},{4,12},{8,0},{12,4},{16,24},{20,28},{24,16},{28,20},{1,9},{5... | collective-permute-start | bytes 442376 | tf_op jit(solution)/shard_map/ppermute | solution.py:651
  59.2 16.5 %collective-permute-start.16 = (bf16[1,576,128]{2,1,0:T(8,128)(2,1)S(1)}, bf16[1,576,128]{2,1,0:T(8,128)(2,1)S(1)}, u32[]{:S(2)}, u32[]{:S(2)}) collective-permute-start(bf16[1,576,128]{2,1,0:T(8,128)(2,1)S(1)} %get-tuple-element.153), channel_id=1, source_target_pairs={{0,16},{4,20},{8,24},{12,28},{16,0},{20,4},{24,8},{28,12},{1,17},{... | collective-permute-start | bytes 442376 | tf_op jit(solution)/shard_map/ppermute | solution.py:651
  60.3 15.4 %collective-permute-start.17 = (bf16[1,576,128]{2,1,0:T(8,128)(2,1)S(1)}, bf16[1,576,128]{2,1,0:T(8,128)(2,1)S(1)}, u32[]{:S(2)}, u32[]{:S(2)}) collective-permute-start(bf16[1,576,128]{2,1,0:T(8,128)(2,1)S(1)} %get-tuple-element.154), channel_id=1, source_target_pairs={{0,24},{4,28},{8,16},{12,20},{16,8},{20,12},{24,0},{28,4},{1,25},{... | collective-permute-start | bytes 442376 | tf_op jit(solution)/shard_map/ppermute | solution.py:651
  61.6 5.9 %collective-permute-start.19 = (bf16[4,16,128]{2,1,0:T(8,128)(2,1)S(1)}, bf16[4,16,128]{2,1,0:T(8,128)(2,1)S(1)}, u32[]{:S(2)}, u32[]{:S(2)}) collective-permute-start(bf16[4,16,128]{2,1,0:T(8,128)(2,1)S(1)} %get-tuple-element.161), channel_id=1, source_target_pairs={{0,4},{4,0},{8,12},{12,8},{16,20},{20,16},{24,28},{28,24},{1,5},{5... | collective-permute-start | bytes 49160 | tf_op jit(solution)/shard_map/ppermute | solution.py:651
  67.5 17.1 %collective-permute-start.21 = (bf16[1,592,128]{2,1,0:T(8,128)(2,1)S(1)}, bf16[1,592,128]{2,1,0:T(8,128)(2,1)S(1)}, u32[]{:S(2)}, u32[]{:S(2)}) collective-permute-start(bf16[1,592,128]{2,1,0:T(8,128)(2,1)S(1)} %get-tuple-element.168), channel_id=1, source_target_pairs={{0,24},{4,28},{8,16},{12,20},{16,8},{20,12},{24,0},{28,4},{1,25},{... | collective-permute-start | bytes 454664 | tf_op jit(solution)/shard_map/ppermute | solution.py:651
  76.7 16.8 %collective-permute-start.18 = (bf16[2,128,512]{2,1,0:T(8,128)(2,1)S(1)}, bf16[2,128,512]{2,1,0:T(8,128)(2,1)S(1)}, u32[]{:S(2)}, u32[]{:S(2)}) collective-permute-start(bf16[2,128,512]{2,1,0:T(8,128)(2,1)S(1)} %get-tuple-element.160), channel_id=1, source_target_pairs={{0,2},{1,3},{2,0},{3,1},{4,6},{5,7},{6,4},{7,5},{8,10},{9,11},{10,... | collective-permute-start | bytes 786440 | tf_op jit(solution)/shard_map/ppermute | solution.py:648
  76.8 10.6 %collective-permute-start.22 = (bf16[1,592,128]{2,1,0:T(8,128)(2,1)S(1)}, bf16[1,592,128]{2,1,0:T(8,128)(2,1)S(1)}, u32[]{:S(2)}, u32[]{:S(2)}) collective-permute-start(bf16[1,592,128]{2,1,0:T(8,128)(2,1)S(1)} %get-tuple-element.169), channel_id=1, source_target_pairs={{0,16},{4,20},{8,24},{12,28},{16,0},{20,4},{24,8},{28,12},{1,17},{... | collective-permute-start | bytes 454664 | tf_op jit(solution)/shard_map/ppermute | solution.py:651
  82.5 6.3 %collective-permute-start.23 = (bf16[1,592,128]{2,1,0:T(8,128)(2,1)S(1)}, bf16[1,592,128]{2,1,0:T(8,128)(2,1)S(1)}, u32[]{:S(2)}, u32[]{:S(2)}) collective-permute-start(bf16[1,592,128]{2,1,0:T(8,128)(2,1)S(1)} %get-tuple-element.170), channel_id=1, source_target_pairs={{0,8},{4,12},{8,0},{12,4},{16,24},{20,28},{24,16},{28,20},{1,9},{5... | collective-permute-start | bytes 454664 | tf_op jit(solution)/shard_map/ppermute | solution.py:651
  82.6 8.2 %collective-permute-start.24 = (bf16[576,128]{1,0:T(8,128)(2,1)S(1)}, bf16[576,128]{1,0:T(8,128)(2,1)S(1)}, u32[]{:S(2)}, u32[]{:S(2)}) collective-permute-start(bf16[576,128]{1,0:T(8,128)(2,1)S(1)} %sumrouteb.1.own_ref), channel_id=1, source_target_pairs={{0,2},{1,3},{2,0},{3,1},{4,6},{5,7},{6,4},{7,5},{8,10},{9,11},{10,... | collective-permute-start | bytes 442376 | tf_op jit(solution)/shard_map/ppermute | solution.py:648
  84.6 6.2 %collective-permute-start.25 = (bf16[256,256]{1,0:T(8,128)(2,1)S(1)}, bf16[256,256]{1,0:T(8,128)(2,1)S(1)}, u32[]{:S(2)}, u32[]{:S(2)}) collective-permute-start(bf16[256,256]{1,0:T(8,128)(2,1)S(1)} %sumroutea.1.own_ref), channel_id=1, source_target_pairs={{0,2},{1,3},{2,0},{3,1},{4,6},{5,7},{6,4},{7,5},{8,10},{9,11},{10,... | collective-permute-start | bytes 393224 | tf_op jit(solution)/shard_map/ppermute | solution.py:648
  91.0 6.6 %collective-permute-start.26 = (bf16[592,128]{1,0:T(8,128)(2,1)S(1)}, bf16[592,128]{1,0:T(8,128)(2,1)S(1)}, u32[]{:S(2)}, u32[]{:S(2)}) collective-permute-start(bf16[592,128]{1,0:T(8,128)(2,1)S(1)} %sumroutec.1.own_ref), channel_id=1, source_target_pairs={{0,2},{1,3},{2,0},{3,1},{4,6},{5,7},{6,4},{7,5},{8,10},{9,11},{10,... | collective-permute-start | bytes 454664 | tf_op jit(solution)/shard_map/ppermute | solution.py:648
  93.0 3.4 %collective-permute-start.28 = (bf16[576,128]{1,0:T(8,128)(2,1)S(1)}, bf16[576,128]{1,0:T(8,128)(2,1)S(1)}, u32[]{:S(2)}, u32[]{:S(2)}) collective-permute-start(bf16[576,128]{1,0:T(8,128)(2,1)S(1)} %sumrouteb.1.own_ref), channel_id=1, source_target_pairs={{0,1},{1,0},{2,3},{3,2},{4,5},{5,4},{6,7},{7,6},{8,9},{9,8},{10,11... | collective-permute-start | bytes 442376 | tf_op jit(solution)/shard_map/ppermute | solution.py:645
  93.0 3.4 %collective-permute-start.29 = (bf16[576,128]{1,0:T(8,128)(2,1)S(1)}, bf16[576,128]{1,0:T(8,128)(2,1)S(1)}, u32[]{:S(2)}, u32[]{:S(2)}) collective-permute-start(bf16[576,128]{1,0:T(8,128)(2,1)S(1)} %collective-permute-done.24.far_ref), channel_id=1, source_target_pairs={{0,1},{1,0},{2,3},{3,2},{4,5},{5,4},{6,7},{7,6},{8,9},{9,8},{10,11... | collective-permute-start | bytes 442376 | tf_op jit(solution)/shard_map/ppermute | solution.py:645
  93.5 2.0 %collective-permute-start.30 = (bf16[256,256]{1,0:T(8,128)(2,1)S(1)}, bf16[256,256]{1,0:T(8,128)(2,1)S(1)}, u32[]{:S(2)}, u32[]{:S(2)}) collective-permute-start(bf16[256,256]{1,0:T(8,128)(2,1)S(1)} %sumroutea.1.own_ref), channel_id=1, source_target_pairs={{0,1},{1,0},{2,3},{3,2},{4,5},{5,4},{6,7},{7,6},{8,9},{9,8},{10,11... | collective-permute-start | bytes 393224 | tf_op jit(solution)/shard_map/ppermute | solution.py:645
  93.5 2.0 %collective-permute-start.31 = (bf16[256,256]{1,0:T(8,128)(2,1)S(1)}, bf16[256,256]{1,0:T(8,128)(2,1)S(1)}, u32[]{:S(2)}, u32[]{:S(2)}) collective-permute-start(bf16[256,256]{1,0:T(8,128)(2,1)S(1)} %collective-permute-done.25.far_ref), channel_id=1, source_target_pairs={{0,1},{1,0},{2,3},{3,2},{4,5},{5,4},{6,7},{7,6},{8,9},{9,8},{10,11... | collective-permute-start | bytes 393224 | tf_op jit(solution)/shard_map/ppermute | solution.py:645
  95.5 2.6 %collective-permute-start.27 = (bf16[592,128]{1,0:T(8,128)(2,1)S(1)}, bf16[592,128]{1,0:T(8,128)(2,1)S(1)}, u32[]{:S(2)}, u32[]{:S(2)}) collective-permute-start(bf16[592,128]{1,0:T(8,128)(2,1)S(1)} %sumroutec.1.own_ref), channel_id=1, source_target_pairs={{0,1},{1,0},{2,3},{3,2},{4,5},{5,4},{6,7},{7,6},{8,9},{9,8},{10,11... | collective-permute-start | bytes 454664 | tf_op jit(solution)/shard_map/ppermute | solution.py:645
  97.6 1.5 %collective-permute-start.32 = (bf16[592,128]{1,0:T(8,128)(2,1)S(1)}, bf16[592,128]{1,0:T(8,128)(2,1)S(1)}, u32[]{:S(2)}, u32[]{:S(2)}) collective-permute-start(bf16[592,128]{1,0:T(8,128)(2,1)S(1)} %collective-permute-done.26.far_ref), channel_id=1, source_target_pairs={{0,1},{1,0},{2,3},{3,2},{4,5},{5,4},{6,7},{7,6},{8,9},{9,8},{10,11... | collective-permute-start | bytes 454664 | tf_op jit(solution)/shard_map/ppermute | solution.py:645

commit v10 on v8

--- a/solution.py
+++ b/solution.py
@@ -21,7 +21,7 @@
 HB = pl.BlockSpec(memory_space=pltpu.HBM)
 RATE = 1 << 30
 LENGTH = {
-    "pack": 10, "stack": 10, "first": 0.02, "second": 30, "third": 20, "fourth": 0.5, "weight2": 1, "weight1": 3, "routeb1": 20,
+    "pack": 10, "stack": 10, "first": 0.02, "second": 30, "third": 20, "fourth": 0.02, "weight2": 1, "weight1": 3, "routeb1": 20,
 }
 
 
@@ -267,7 +267,7 @@
 
 def first_kernel(
     bucket_ref, own, partner, received, partner_received, vecs, weight1,
-    image_ref, conv_ref, act2_ref, stats_ref, act1_t, act2_t, send_t,
+    image_ref, conv_ref, act2_ref, stats_ref, act1_ref, send_ref,
     shift_ref,
 ):
     h, home, away = place(bucket_ref)
@@ -280,7 +280,7 @@
     mean1, inverse1 = norm_stats(values, mask, group_size)
     act = silu_norm(values, mean1, inverse1, vec(vecs, GAIN1), vec(vecs, SHIFT1), mask)
     fill_shifts(shift_ref, act, stride)
-    act1_t[...] = act.astype(BF16).T
+    act1_ref[...] = act.astype(BF16)
     conv_forward(shift_ref, weight1, stride, conv_ref)
     values = (conv_ref[...] + vec(vecs, BIAS1)) * mask
     conv_ref[...] = values
@@ -288,10 +288,9 @@
     act = silu_norm(values, mean2, inverse2, vec(vecs, GAIN2), vec(vecs, SHIFT2), mask)
     act = act.astype(BF16)
     act2_ref[...] = act
-    act2_t[...] = act.T
-    half = pl.multiple_of((h & 1) * (channels // 2), 16)
-    send_t[0] = act1_t[pl.ds(half, channels // 2), :]
-    send_t[1] = act2_t[pl.ds(half, channels // 2), :]
+    half = pl.multiple_of((h & 1) * (channels // 2), BLK)
+    send_ref[0] = act1_ref[:, pl.ds(half, channels // 2)]
+    send_ref[1] = act2_ref[:, pl.ds(half, channels // 2)]
     stats_ref[0:1, :] = mean1
     stats_ref[1:2, :] = inverse1
     stats_ref[2:3, :] = mean2
@@ -470,16 +469,16 @@
 
 
 def weight_kernel(
-    bucket_ref, act_t, half_t, partner_half_t, block_own, block_away,
+    bucket_ref, act_ref, half_ref, partner_half_ref, block_own, block_away,
     keep_ref, send_ref, left_ref, right_ref, shift_ref, sum_ref, *, layer,
 ):
     h, home, away = place(bucket_ref)
-    channels = act_t.shape[0]
+    channels = act_ref.shape[1]
     half = channels // 2
-    left_ref[:, 0:PIX] = act_t[...]
-    left_ref[pl.ds(pl.multiple_of((h & 1) * half, 16), half), PIX : 2 * PIX] = half_t[layer]
+    left_ref[:, 0:PIX] = act_ref[...].T
+    left_ref[pl.ds(pl.multiple_of((h & 1) * half, 16), half), PIX : 2 * PIX] = half_ref[layer].T
     left_ref[pl.ds(pl.multiple_of((1 - (h & 1)) * half, 16), half), PIX : 2 * PIX] = (
-        partner_half_t[layer]
+        partner_half_ref[layer].T
     )
     for index, (facts, block) in enumerate(((home, block_own), (away, block_away))):
         stride = facts[2]
@@ -660,7 +659,6 @@
     img32 = ((PIX, C), F32)
     rows8 = ((8, C), F32)
     block = ((PIX, BLK), BF16)
-    turned = ((C, PIX), BF16)
     shifts = ((3, PIX + 2 * PAD, C), BF16)
 
     kinds, away_x, home_x = call(
@@ -684,14 +682,14 @@
     core_recv_c = lax.ppermute(away_c, "height", [(i, i ^ 3) for i in range(4)])
     core_recv_x = to_core(after(recv_x, vecs))
 
-    image, conv, act2, stats, act1_t, act2_t, send_t = call(
+    image, conv, act2, stats, act1, act_send = call(
         first_kernel, "first",
-        [img16, img32, img16, rows8, turned, turned, ((2, C // 2, PIX), BF16)],
+        [img16, img32, img16, rows8, img16, ((2, PIX, C // 2), BF16)],
         [shifts], 14,
         kinds, home_x, core_x, recv_x, core_recv_x, vecs, conv1_weight,
     )
-    half_t = to_chip(send_t)
-    core_half_t = to_core(half_t)
+    half = to_chip(act_send)
+    core_half = to_core(half)
 
     attn_out = ((batches // 2, 4 * small_rows, 2 * BLK), BF16)
     middle, mixed, grad2, grad_middle, attn_keep, attn_send, vec_a, block2, block2_send = call(
@@ -712,16 +710,16 @@
     )
     block1_away = to_chip(block1_send)
 
-    def weight_grad(name, act_t, index, own, away):
+    def weight_grad(name, act, index, own, away):
         return call(
             functools.partial(weight_kernel, layer=index), name,
             [((batches // 2, shard_rows, BLK), BF16)] * 2,
             [((C, 2 * PIX), BF16), ((2 * PIX, 9 * BLK), BF16), ((3, PIX + 2 * PAD, BLK), BF16),
              ((9 * C, BLK), F32)],
-            18, kinds, act_t, half_t, core_half_t, own, away,
+            18, kinds, act, half, core_half, own, away,
         )
 
-    keep2, send2 = weight_grad("weight2", act2_t, 1, after(block2, block1), block2_away)
+    keep2, send2 = weight_grad("weight2", act2, 1, after(block2, block1), block2_away)
     got2 = to_batch(send2, 1)
 
     def spread(name, bit, keep, got, tail=None, behind=()):
@@ -754,24 +752,24 @@
         return shard, far, near, to_core(after(far, *between))
 
     parts_a, got_a = spread("routea", 1, after(attn_keep, send2), attn_got)
-    keep1, send1 = weight_grad("weight1", act1_t, 0, after(block1, *parts_a), block1_away)
+    keep1, send1 = weight_grad("weight1", act1, 0, after(block1, *parts_a), block1_away)
     got1 = to_batch(send1, 1)
     shard_a = finish("routea", parts_a, together(got_a, send1))
+    parts_b, got_b = spread("routeb", 1, after(keep2, send1, shard_a), got2)
     grad_own, grad_send, vec_keep, vec_send = call(
         fourth_kernel, "fourth",
         [((192, C), BF16), ((128, C), BF16),
          ((batches // 2, VECS, BLK), BF16), ((batches // 2, VECS, BLK), BF16)],
         [shifts, img32, img16, ((VECS, C), F32)], 14,
-        kinds, after(grad1, send1), image, stats, grad_middle, vecs, conv1_weight, vec_a, vec_b,
+        kinds, after(grad1, *parts_b), image, stats, grad_middle, vecs, conv1_weight, vec_a, vec_b,
     )
     vec_got = to_batch(vec_send, 1)
-    parts_b, got_b = spread("routeb", 1, after(keep2, vec_keep, shard_a), got2)
+    parts_c, got_c = spread("routec", 1, keep1, got1, (vec_keep, vec_got), behind=got_b)
     out_own, image_send = call(
         output_kernel, "output", [((192, C), BF16), ((2, 128, C), BF16)], [img16], 10,
-        kinds, after(middle, *parts_b), mixed, vecs, proj_weight, grad_send,
+        kinds, after(middle, parts_c[0]), mixed, vecs, proj_weight, grad_send,
     )
     image_away = to_chip(image_send)
-    parts_c, got_c = spread("routec", 1, keep1, got1, (vec_keep, vec_got), behind=got_b)
     shard_b = finish("routeb", parts_b, together(got_b, parts_c[0]))
     gathered_a = gather(shard_a)
     gathered_b = gather(shard_b)

time: 96.1 us -> 96.9 us (level)
  starting transfers between devices: 32.5 us -> 33.5 us
  transfers between devices with their start and end apart: 33 -> 33, of which waited for: 10 -> 10; matrix products, arithmetic and copies ran while one was open for 0% -> 0% of each run, Pallas kernels for 38% -> 37%
where the time goes in v10:
time: 96.9 us; the launch traced here: 96.8 us
  Pallas kernels  39.3 us (41%)
  starting transfers between devices  33.5 us (35%)
  waiting for transfers between devices  21.7 us (22%)
  between operations  1.28 us (1%)
    pallas_call x20, Pallas kernels, call(): pl.pallas_call(kernel, name=name, out_shape=[jax.ShapeDtypeStruct(shape,...  39.3 us
    ppermute x13, starting transfers between devices, to_batch(): return lax.ppermute(v, 'batch', [(i, i ^ change) for i in range(batches)])  19.8 us
    ppermute x13, waiting for transfers between devices, to_batch(): return lax.ppermute(v, 'batch', [(i, i ^ change) for i in range(batches)])  13 us
    ppermute x9, starting transfers between devices, to_chip(): return lax.ppermute(v, 'height', [(i, i ^ 2) for i in range(4)])  9.99 us
    ppermute x9, waiting for transfers between devices, to_chip(): return lax.ppermute(v, 'height', [(i, i ^ 2) for i in range(4)])  6.57 us
    ppermute x10, starting transfers between devices, to_core(): return lax.ppermute(v, 'height', [(i, i ^ 1) for i in range(4)])  2.42 us
    ppermute x10, waiting for transfers between devices, to_core(): return lax.ppermute(v, 'height', [(i, i ^ 1) for i in range(4)])  2.14 us
  transfers between devices with their start and end apart: 33, of which 10 were waited for; matrix products, arithmetic and copies ran while one was open for 0% of the time, Pallas kernels for 37%

profile of v10, /device:TPU:0, one launch (start us, length us, event | category | flops | bytes accessed | tf_op | source)
XLA Modules:
  0.0 96.8 jit_solution(9369535724810219504)
XLA Ops:
  0.8 0.0 slice-start
  0.8 0.0 slice-start.2
  0.8 1.9 %pack.1 = (s32[2]{0:T(128)}, bf16[128,512]{1,0:T(8,128)(2,1)}, bf16[192,512]{1,0:T(8,128)(2,1)}) custom-call(s32[2]{0:T(128)} %bucket_hbm.1, bf16[2,6,32,512]{3,2,1,0:T(8,128)(2,1)} %x_hbm.1), custom_call_target="tpu_custom_call" | custom-call | flops 10737418240 | bytes 1024 | tf_op jit(solution)/shard_map/pack/pallas_call | solution.py:592
  2.7 3.0 %collective-permute-start.1 = (bf16[128,512]{1,0:T(8,128)(2,1)}, bf16[128,512]{1,0:T(8,128)(2,1)S(1)}, u32[]{:S(2)}, u32[]{:S(2)}) collective-permute-start(bf16[128,512]{1,0:T(8,128)(2,1)} %get-tuple-element.113), channel_id=1, source_target_pairs={{0,2},{1,3},{2,0},{3,1},{4,6},{5,7},{6,4},{7,5},{8,10},{9,11},{10,... | collective-permute-start | bytes 393224 | tf_op jit(solution)/shard_map/ppermute | solution.py:647
  5.9 0.0 copy-start.2
  5.9 0.8 copy-done.2
  6.7 0.6 stack.1
  7.3 0.0 copy-start
  7.3 0.0 copy-start.4
  7.3 0.6 collective-permute-start.3
  7.9 0.1 collective-permute-start.4
  8.0 1.4 %collective-permute-start.5 = (bf16[160,512]{1,0:T(8,128)(2,1)S(1)}, bf16[160,512]{1,0:T(8,128)(2,1)S(1)}, u32[]{:S(2)}, u32[]{:S(2)}) collective-permute-start(bf16[160,512]{1,0:T(8,128)(2,1)S(1)} %get-tuple-element.119), channel_id=1, source_target_pairs={{0,3},{1,2},{2,1},{3,0},{4,7},{5,6},{6,5},{7,4},{8,11},{9,10},{10,... | collective-permute-start | bytes 491528 | tf_op jit(solution)/shard_map/ppermute | solution.py:682
  9.3 0.1 collective-permute-done.1.received
  9.5 0.6 collective-permute-start.2
  10.1 1.0 %collective-permute-done.2.partner_received = bf16[128,512]{1,0:T(8,128)(2,1)S(1)} collective-permute-done((bf16[128,512]{1,0:T(8,128)(2,1)S(1)}, bf16[128,512]{1,0:T(8,128)(2,1)S(1)}, u32[]{:S(2)}, u32[]{:S(2)}) %collective-permute-start.2) | collective-permute-done | bytes 131104 | tf_op jit(solution)/shard_map/ppermute | solution.py:644
  11.1 5.3 %first.1 = (bf16[512,512]{1,0:T(8,128)(2,1)S(1)}, f32[512,512]{1,0:T(8,128)S(1)}, bf16[512,512]{1,0:T(8,128)(2,1)S(1)}, f32[8,512]{1,0:T(8,128)S(1)}, bf16[512,5...) custom-call(s32[2]{0:T(128)S(1)} %copy-done.3, bf16[192,512]{1,0:T(8,128)(2,1)S(1)} %copy-done.1, ...), custom_call_target="tpu_custom_call" | custom-call | flops 21474836 | bytes 1024 | tf_op jit(solution)/shard_map/first/pallas_call | solution.py:592
  16.4 1.9 %collective-permute-start.6 = (bf16[2,512,256]{2,1,0:T(8,128)(2,1)S(1)}, bf16[2,512,256]{2,1,0:T(8,128)(2,1)S(1)}, u32[]{:S(2)}, u32[]{:S(2)}) collective-permute-start(bf16[2,512,256]{2,1,0:T(8,128)(2,1)S(1)} %get-tuple-element.125), channel_id=1, source_target_pairs={{0,2},{1,3},{2,0},{3,1},{4,6},{5,7},{6,4},{7,5},{8,10},{9,11},{10,... | collective-permute-start | bytes 1572872 | tf_op jit(solution)/shard_map/ppermute | solution.py:647
  18.4 9.6 %second.1 = (f32[512,512]{1,0:T(8,128)S(1)}, bf16[512,512]{1,0:T(8,128)(2,1)S(1)}, bf16[512,512]{1,0:T(8,128)(2,1)S(1)}, f32[512,512]{1,0:T(8,128)S(1)}, bf16[4,...) custom-call(s32[2]{0:T(128)S(1)} %copy-done.3, ...), custom_call_target="tpu_custom_call" | custom-call | flops 32212254720 | bytes 1024 | tf_op jit(solution)/shard_map/second/pallas_call | solution.py:592
  28.0 0.3 collective-permute-start.8
  28.2 1.5 %collective-permute-start.9 = (bf16[4,256,256]{2,1,0:T(8,128)(2,1)S(1)}, bf16[4,256,256]{2,1,0:T(8,128)(2,1)S(1)}, u32[]{:S(2)}, u32[]{:S(2)}) collective-permute-start(bf16[4,256,256]{2,1,0:T(8,128)(2,1)S(1)} %get-tuple-element.135), channel_id=1, source_target_pairs={{0,4},{4,0},{8,12},{12,8},{16,20},{20,16},{24,28},{28,24},{1,5},{5... | collective-permute-start | bytes 1572872 | tf_op jit(solution)/shard_map/ppermute | solution.py:650
  29.8 1.1 %collective-permute-done.6.half_ref = bf16[2,512,256]{2,1,0:T(8,128)(2,1)S(1)} collective-permute-done((bf16[2,512,256]{2,1,0:T(8,128)(2,1)S(1)}, bf16[2,512,256]{2,1,0:T(8,128)(2,1)S(1)}, u32[]{:S(2)}, u32[]{:S(2)}) %collective-permute-start.6) | collective-permute-done | bytes 524320 | tf_op jit(solution)/shard_map/ppermute | solution.py:647
  30.8 4.3 %third.1 = (bf16[512,512]{1,0:T(8,128)(2,1)S(1)}, bf16[512,128]{1,0:T(8,128)(2,1)S(1)}, bf16[512,128]{1,0:T(8,128)(2,1)S(1)}, f32[8,512]{1,0:T(8,128)S(1)}) custom-call(s32[2]{0:T(128)S(1)} %copy-done.3, bf16[512,512]{1,0:T(8,128)(2,1)S(1)} %get-tuple-element.121.grad2_ref, f32[512,512]{1,0:T(8,128)S(1)} %get-tuple-element.122.conv_ref, ...), custom_call_target="tpu_custom_call" | custom-call | flops 21474836480 | bytes 1024 | tf_op jit(solution)/shard_map/third/pallas_call | solution.py:592
  35.2 3.4 %weight2.5 = (bf16[4,576,128]{2,1,0:T(8,128)(2,1)S(1)}, bf16[4,576,128]{2,1,0:T(8,128)(2,1)S(1)}) custom-call(s32[2]{0:T(128)S(1)} %copy-done.3, bf16[512,512]{1,0:T(8,128)(2,1)S(1)} %get-tuple-element.117.act2_ref.act_ref, bf16[2,512,256]{2,1,0:T(8,128)(2,1)S(1)} %collective-permute-done.6.half_ref, ...), custom_call_target="tpu_custom_call" | custom-call | flops 1073741824 | bytes 1024 | tf_op jit(solution)/shard_map/weight2/pallas_call | solution.py:592
  38.5 1.8 %collective-permute-start.14 = (bf16[4,576,128]{2,1,0:T(8,128)(2,1)S(1)}, bf16[4,576,128]{2,1,0:T(8,128)(2,1)S(1)}, u32[]{:S(2)}, u32[]{:S(2)}) collective-permute-start(bf16[4,576,128]{2,1,0:T(8,128)(2,1)S(1)} %get-tuple-element.133), channel_id=1, source_target_pairs={{0,4},{4,0},{8,12},{12,8},{16,20},{20,16},{24,28},{28,24},{1,5},{5... | collective-permute-start | bytes 1769480 | tf_op jit(solution)/shard_map/ppermute | solution.py:650
  40.3 1.8 %collective-permute-start.10 = (bf16[512,128]{1,0:T(8,128)(2,1)S(1)}, bf16[512,128]{1,0:T(8,128)(2,1)S(1)}, u32[]{:S(2)}, u32[]{:S(2)}) collective-permute-start(bf16[512,128]{1,0:T(8,128)(2,1)S(1)} %get-tuple-element.141), channel_id=1, source_target_pairs={{0,2},{1,3},{2,0},{3,1},{4,6},{5,7},{6,4},{7,5},{8,10},{9,11},{10,... | collective-permute-start | bytes 393224 | tf_op jit(solution)/shard_map/ppermute | solution.py:647
  42.1 0.1 routea1.1
  42.3 1.6 %collective-permute-start.11 = (bf16[1,256,256]{2,1,0:T(8,128)(2,1)S(1)}, bf16[1,256,256]{2,1,0:T(8,128)(2,1)S(1)}, u32[]{:S(2)}, u32[]{:S(2)}) collective-permute-start(bf16[1,256,256]{2,1,0:T(8,128)(2,1)S(1)} %get-tuple-element.137), channel_id=1, source_target_pairs={{0,8},{4,12},{8,0},{12,4},{16,24},{20,28},{24,16},{28,20},{1,9},{5... | collective-permute-start | bytes 393224 | tf_op jit(solution)/shard_map/ppermute | solution.py:650
  43.9 2.6 %collective-permute-start.12 = (bf16[1,256,256]{2,1,0:T(8,128)(2,1)S(1)}, bf16[1,256,256]{2,1,0:T(8,128)(2,1)S(1)}, u32[]{:S(2)}, u32[]{:S(2)}) collective-permute-start(bf16[1,256,256]{2,1,0:T(8,128)(2,1)S(1)} %get-tuple-element.138), channel_id=1, source_target_pairs={{0,16},{4,20},{8,24},{12,28},{16,0},{20,4},{24,8},{28,12},{1,17},{... | collective-permute-start | bytes 393224 | tf_op jit(solution)/shard_map/ppermute | solution.py:650
  46.5 0.2 collective-permute-start.13
  46.7 3.2 %weight1.4 = (bf16[4,576,128]{2,1,0:T(8,128)(2,1)S(1)}, bf16[4,576,128]{2,1,0:T(8,128)(2,1)S(1)}) custom-call(s32[2]{0:T(128)S(1)} %copy-done.3, bf16[512,512]{1,0:T(8,128)(2,1)S(1)} %get-tuple-element.131.act_ref, bf16[2,512,256]{2,1,0:T(8,128)(2,1)S(1)} %collective-permute-done.6.half_ref, ...), custom_call_target="tpu_custom_call" | custom-call | flops 3221225472 | bytes 1024 | tf_op jit(solution)/shard_map/weight1/pallas_call | solution.py:592
  49.9 1.3 %collective-permute-start.16 = (bf16[4,576,128]{2,1,0:T(8,128)(2,1)S(1)}, bf16[4,576,128]{2,1,0:T(8,128)(2,1)S(1)}, u32[]{:S(2)}, u32[]{:S(2)}) collective-permute-start(bf16[4,576,128]{2,1,0:T(8,128)(2,1)S(1)} %get-tuple-element.142), channel_id=1, source_target_pairs={{0,4},{4,0},{8,12},{12,8},{16,20},{20,16},{24,28},{28,24},{1,5},{5... | collective-permute-start | bytes 1769480 | tf_op jit(solution)/shard_map/ppermute | solution.py:650
  51.2 5.6 %collective-permute-done.12.refs_2_ = bf16[1,256,256]{2,1,0:T(8,128)(2,1)S(1)} collective-permute-done((bf16[1,256,256]{2,1,0:T(8,128)(2,1)S(1)}, bf16[1,256,256]{2,1,0:T(8,128)(2,1)S(1)}, u32[]{:S(2)}, u32[]{:S(2)}) %collective-permute-start.12) | collective-permute-done | bytes 131104 | tf_op jit(solution)/shard_map/ppermute | solution.py:650
  56.8 0.1 sumroutea.1.own_ref
  56.9 0.1 routeb1.1
  57.1 2.1 %collective-permute-start.18 = (bf16[1,576,128]{2,1,0:T(8,128)(2,1)S(1)}, bf16[1,576,128]{2,1,0:T(8,128)(2,1)S(1)}, u32[]{:S(2)}, u32[]{:S(2)}) collective-permute-start(bf16[1,576,128]{2,1,0:T(8,128)(2,1)S(1)} %get-tuple-element.148), channel_id=1, source_target_pairs={{0,8},{4,12},{8,0},{12,4},{16,24},{20,28},{24,16},{28,20},{1,9},{5... | collective-permute-start | bytes 442376 | tf_op jit(solution)/shard_map/ppermute | solution.py:650
  59.2 1.1 %collective-permute-start.19 = (bf16[1,576,128]{2,1,0:T(8,128)(2,1)S(1)}, bf16[1,576,128]{2,1,0:T(8,128)(2,1)S(1)}, u32[]{:S(2)}, u32[]{:S(2)}) collective-permute-start(bf16[1,576,128]{2,1,0:T(8,128)(2,1)S(1)} %get-tuple-element.149), channel_id=1, source_target_pairs={{0,16},{4,20},{8,24},{12,28},{16,0},{20,4},{24,8},{28,12},{1,17},{... | collective-permute-start | bytes 442376 | tf_op jit(solution)/shard_map/ppermute | solution.py:650
  60.3 1.4 %collective-permute-start.20 = (bf16[1,576,128]{2,1,0:T(8,128)(2,1)S(1)}, bf16[1,576,128]{2,1,0:T(8,128)(2,1)S(1)}, u32[]{:S(2)}, u32[]{:S(2)}) collective-permute-start(bf16[1,576,128]{2,1,0:T(8,128)(2,1)S(1)} %get-tuple-element.150), channel_id=1, source_target_pairs={{0,24},{4,28},{8,16},{12,20},{16,8},{20,12},{24,0},{28,4},{1,25},{... | collective-permute-start | bytes 442376 | tf_op jit(solution)/shard_map/ppermute | solution.py:650
  61.7 0.3 collective-permute-start.25
  62.0 4.6 %fourth.1 = (bf16[192,512]{1,0:T(8,128)(2,1)S(1)}, bf16[128,512]{1,0:T(8,128)(2,1)S(1)}, bf16[4,16,128]{2,1,0:T(8,128)(2,1)S(1)}, bf16[4,16,128]{2,1,0:T(8,128)(2,1)S(1)}) custom-call(s32[2]{0:T(128)S(1)} %copy-done.3, bf16[512,512]{1,0:T(8,128)(2,1)S(1)} %get-tuple-element.151.grad1_ref, bf16[512,512]{1,0:T(8,128)(2,1)S(1)} %get-tuple-element.116.image_ref, ...), custom_call_target="tpu_custom_call" | custom-call | flops 21474836 | bytes 1024 | tf_op jit(solution)/shard_map/fourth/pallas_call | solution.py:592
  66.6 0.6 collective-permute-done.16.got_ref
  67.1 1.6 %collective-permute-start.15 = (bf16[4,16,128]{2,1,0:T(8,128)(2,1)S(1)}, bf16[4,16,128]{2,1,0:T(8,128)(2,1)S(1)}, u32[]{:S(2)}, u32[]{:S(2)}) collective-permute-start(bf16[4,16,128]{2,1,0:T(8,128)(2,1)S(1)} %get-tuple-element.156), channel_id=1, source_target_pairs={{0,4},{4,0},{8,12},{12,8},{16,20},{20,16},{24,28},{28,24},{1,5},{5... | collective-permute-start | bytes 49160 | tf_op jit(solution)/shard_map/ppermute | solution.py:650
  68.7 0.1 routec1.1
  68.9 2.0 %collective-permute-done.15.got_ref = bf16[4,16,128]{2,1,0:T(8,128)(2,1)S(1)} collective-permute-done((bf16[4,16,128]{2,1,0:T(8,128)(2,1)S(1)}, bf16[4,16,128]{2,1,0:T(8,128)(2,1)S(1)}, u32[]{:S(2)}, u32[]{:S(2)}) %collective-permute-start.15) | collective-permute-done | bytes 16416 | tf_op jit(solution)/shard_map/ppermute | solution.py:650
  70.9 1.0 %output.1 = (bf16[192,512]{1,0:T(8,128)(2,1)S(1)}, bf16[2,128,512]{2,1,0:T(8,128)(2,1)S(1)}) custom-call(s32[2]{0:T(128)S(1)} %copy-done.3, f32[512,512]{1,0:T(8,128)S(1)} %get-tuple-element.163.middle_ref, bf16[512,512]{1,0:T(8,128)(2,1)S(1)} %get-tuple-element.164.mixed_ref, f32[16,512]{1,0:T(8,128)S(1)} %get-tuple-element.114.vecs, ...), custom_call_target="tpu_custom_call" | custom-call | flops 21474836 | bytes 1024 | tf_op jit(solution)/shard_map/output/pallas_call | solution.py:592
  71.9 2.2 %collective-permute-start.17 = (bf16[2,128,512]{2,1,0:T(8,128)(2,1)S(1)}, bf16[2,128,512]{2,1,0:T(8,128)(2,1)S(1)}, u32[]{:S(2)}, u32[]{:S(2)}) collective-permute-start(bf16[2,128,512]{2,1,0:T(8,128)(2,1)S(1)} %get-tuple-element.168), channel_id=1, source_target_pairs={{0,2},{1,3},{2,0},{3,1},{4,6},{5,7},{6,4},{7,5},{8,10},{9,11},{10,... | collective-permute-start | bytes 786440 | tf_op jit(solution)/shard_map/ppermute | solution.py:647
  74.1 1.4 %collective-permute-start.23 = (bf16[1,592,128]{2,1,0:T(8,128)(2,1)S(1)}, bf16[1,592,128]{2,1,0:T(8,128)(2,1)S(1)}, u32[]{:S(2)}, u32[]{:S(2)}) collective-permute-start(bf16[1,592,128]{2,1,0:T(8,128)(2,1)S(1)} %get-tuple-element.174), channel_id=1, source_target_pairs={{0,8},{4,12},{8,0},{12,4},{16,24},{20,28},{24,16},{28,20},{1,9},{5... | collective-permute-start | bytes 454664 | tf_op jit(solution)/shard_map/ppermute | solution.py:650
  75.5 2.6 %collective-permute-start.22 = (bf16[1,592,128]{2,1,0:T(8,128)(2,1)S(1)}, bf16[1,592,128]{2,1,0:T(8,128)(2,1)S(1)}, u32[]{:S(2)}, u32[]{:S(2)}) collective-permute-start(bf16[1,592,128]{2,1,0:T(8,128)(2,1)S(1)} %get-tuple-element.172), channel_id=1, source_target_pairs={{0,16},{4,20},{8,24},{12,28},{16,0},{20,4},{24,8},{28,12},{1,17},{... | collective-permute-start | bytes 454664 | tf_op jit(solution)/shard_map/ppermute | solution.py:650
  78.1 0.5 collective-permute-start.21
  78.6 0.1 sumrouteb.1.own_ref
  78.7 0.1 collective-permute-start.24
  78.7 5.1 %collective-permute-done.24.far_ref = bf16[576,128]{1,0:T(8,128)(2,1)S(1)} collective-permute-done((bf16[576,128]{1,0:T(8,128)(2,1)S(1)}, bf16[576,128]{1,0:T(8,128)(2,1)S(1)}, u32[]{:S(2)}, u32[]{:S(2)}) %collective-permute-start.24) | collective-permute-done | bytes 147488 | tf_op jit(solution)/shard_map/ppermute | solution.py:647
  83.9 4.8 %collective-permute-done.22.refs_2_ = bf16[1,592,128]{2,1,0:T(8,128)(2,1)S(1)} collective-permute-done((bf16[1,592,128]{2,1,0:T(8,128)(2,1)S(1)}, bf16[1,592,128]{2,1,0:T(8,128)(2,1)S(1)}, u32[]{:S(2)}, u32[]{:S(2)}) %collective-permute-start.22) | collective-permute-done | bytes 151584 | tf_op jit(solution)/shard_map/ppermute | solution.py:650
  88.7 0.1 sumroutec.1.own_ref
  88.7 0.4 collective-permute-start.26
  89.1 0.5 collective-permute-start.29
  89.6 0.5 collective-permute-start.31
  90.2 1.5 %unpack.1 = (bf16[2,6,32,512]{3,2,1,0:T(8,128)(2,1)}, bf16[2,6,32,512]{3,2,1,0:T(8,128)(2,1)}) custom-call(s32[2]{0:T(128)S(1)} %copy-done.3, bf16[192,512]{1,0:T(8,128)(2,1)S(1)} %get-tuple-element.166.out_own, bf16[192,512]{1,0:T(8,128)(2,1)S(1)} %get-tuple-element.167.grad_own, bf16[2,128,512]{2,1,0:T(8,128)(2,1)S(1)} %collective-permute-done.17.away_ref), custom_call_target="tpu_custom_call" | custom-call | flops 21474836 | bytes 1024 | tf_op jit(solution)/shard_map/unpack/pallas_call | solution.py:592
  91.7 0.0 collective-permute-start.27
  91.7 0.9 joina.1
  92.5 1.2 %joinb.1 = f32[576,512]{1,0:T(8,128)} custom-call(bf16[576,128]{1,0:T(8,128)(2,1)S(1)} %sumrouteb.1.own_ref, bf16[576,128]{1,0:T(8,128)(2,1)S(1)} %collective-permute-done.24.far_ref, bf16[576,128]{1,0:T(8,128)(2,1)S(1)} %collective-permute-done.28.near_ref, bf16[576,128]{1,0:T(8,128)(2,1)S(1)} %collective-permute-done.29.diagonal_ref), custom_call_target="tpu_custom_call" | custom-call | flops 21474836 | bytes 1024 | tf_op jit(solution)/shard_map/joinb/pallas_call | solution.py:592
  93.7 0.3 collective-permute-done.26.far_ref
  94.0 0.2 collective-permute-start.32
  94.2 1.1 %collective-permute-done.32.diagonal_ref = bf16[592,128]{1,0:T(8,128)(2,1)S(1)} collective-permute-done((bf16[592,128]{1,0:T(8,128)(2,1)S(1)}, bf16[592,128]{1,0:T(8,128)(2,1)S(1)}, u32[]{:S(2)}, u32[]{:S(2)}) %collective-permute-start.32) | collective-permute-done | bytes 151584 | tf_op jit(solution)/shard_map/ppermute | solution.py:644
  95.4 1.2 %joinc.1 = (f32[576,512]{1,0:T(8,128)}, f32[1,64]{1,0:T(1,128)}, f32[1,64]{1,0:T(1,128)}, f32[1,64]{1,0:T(1,128)}, f32[1,64]{1,0:T(1,128)}, /*index=5*/f32[1,64]...) custom-call(bf16[592,128]{1,0:T(8,128)(2,1)S(1)} %sumroutec.1.own_re, ...), custom_call_target="tpu_custom_call" | custom-call | flops 21474836 | bytes 1024 | tf_op jit(solution)/shard_map/joinc/pallas_call | solution.py:592
  (70 shorter events, 0.2 us)
Async XLA Ops:
  0.7 5.1 %copy-start.8 = (f32[512]{0:T(512)S(1)}, f32[512]{0:T(512)}, u32[]{:S(2)}) copy-start(f32[512]{0:T(512)} %param.22) | copy-start | bytes 6148
  0.7 5.1 %copy-start.9 = (f32[512]{0:T(512)S(1)}, f32[512]{0:T(512)}, u32[]{:S(2)}) copy-start(f32[512]{0:T(512)} %param.23) | copy-start | bytes 6148
  0.7 5.1 %copy-start.18 = (f32[512]{0:T(512)S(1)}, f32[512]{0:T(512)}, u32[]{:S(2)}) copy-start(f32[512]{0:T(512)} %param.38) | copy-start | bytes 6148
  0.7 5.1 %copy-start.10 = (f32[512]{0:T(512)S(1)}, f32[512]{0:T(512)}, u32[]{:S(2)}) copy-start(f32[512]{0:T(512)} %param.25) | copy-start | bytes 6148
  0.7 5.1 %copy-start.11 = (f32[512]{0:T(512)S(1)}, f32[512]{0:T(512)}, u32[]{:S(2)}) copy-start(f32[512]{0:T(512)} %param.26) | copy-start | bytes 6148
  0.7 5.1 %copy-start.12 = (f32[512]{0:T(512)S(1)}, f32[512]{0:T(512)}, u32[]{:S(2)}) copy-start(f32[512]{0:T(512)} %param.27) | copy-start | bytes 6148
  0.7 5.1 %copy-start.13 = (f32[512]{0:T(512)S(1)}, f32[512]{0:T(512)}, u32[]{:S(2)}) copy-start(f32[512]{0:T(512)} %param.29) | copy-start | bytes 6148
  0.7 5.1 %copy-start.14 = (f32[512]{0:T(512)S(1)}, f32[512]{0:T(512)}, u32[]{:S(2)}) copy-start(f32[512]{0:T(512)} %param.30) | copy-start | bytes 6148
  0.7 5.1 %copy-start.15 = (f32[512]{0:T(512)S(1)}, f32[512]{0:T(512)}, u32[]{:S(2)}) copy-start(f32[512]{0:T(512)} %param.31) | copy-start | bytes 6148
  0.8 5.1 %copy-start.16 = (f32[512]{0:T(512)S(1)}, f32[512]{0:T(512)}, u32[]{:S(2)}) copy-start(f32[512]{0:T(512)} %param.33) | copy-start | bytes 6148
  0.8 5.1 %copy-start.17 = (f32[512]{0:T(512)S(1)}, f32[512]{0:T(512)}, u32[]{:S(2)}) copy-start(f32[512]{0:T(512)} %param.36) | copy-start | bytes 6148
  0.8 5.1 %copy-start.7 = (bf16[2,6,32,512]{3,2,1,0:T(8,128)(2,1)S(1)}, bf16[2,6,32,512]{3,2,1,0:T(8,128)(2,1)}, u32[]{:S(2)}) copy-start(bf16[2,6,32,512]{3,2,1,0:T(8,128)(2,1)} %cot_ref.1) | copy-start | bytes 1179652
  0.8 10.3 %slice-start = ((s8[4718592]{0:T(1024)(128)(4,1)}), s8[524288]{0:T(1024)(128)(4,1)S(1)}, s32[]{:S(2)}) async-start(s8[4718592]{0:T(1024)(128)(4,1)} %bitcast.22), calls=%async_computation | async-start | bytes 1048576
  0.8 17.5 %slice-start.2 = ((s8[4718592]{0:T(1024)(128)(4,1)}), s8[4194304]{0:T(1024)(128)(4,1)S(1)}, s32[]{:S(2)}) async-start(s8[4718592]{0:T(1024)(128)(4,1)} %bitcast.24), calls=%async_computation.2 | async-start | bytes 8388608
  2.7 6.7 %collective-permute-start.1 = (bf16[128,512]{1,0:T(8,128)(2,1)}, bf16[128,512]{1,0:T(8,128)(2,1)S(1)}, u32[]{:S(2)}, u32[]{:S(2)}) collective-permute-start(bf16[128,512]{1,0:T(8,128)(2,1)} %get-tuple-element.113), channel_id=1, source_target_pairs={{0,2},{1,3},{2,0},{3,1},{4,6},{5,7},{6,4},{7,5},{8,10},{9,11},{10,... | collective-permute-start | bytes 393224 | tf_op jit(solution)/shard_map/ppermute | solution.py:647
  5.8 4.3 %collective-permute-start = (bf16[192,512]{1,0:T(8,128)(2,1)}, bf16[192,512]{1,0:T(8,128)(2,1)S(1)}, u32[]{:S(2)}, u32[]{:S(2)}) collective-permute-start(bf16[192,512]{1,0:T(8,128)(2,1)} %get-tuple-element.112.own), channel_id=1, source_target_pairs={{0,1},{1,0},{2,3},{3,2},{4,5},{5,4},{6,7},{7,6},{8,9},{9,8},{10,11... | collective-permute-start | bytes 589832 | tf_op jit(solution)/shard_map/ppermute | solution.py:644
  5.8 5.3 %slice-start.1 = ((s8[4718592]{0:T(1024)(128)(4,1)}), s8[4194304]{0:T(1024)(128)(4,1)S(1)}, s32[]{:S(2)}) async-start(s8[4718592]{0:T(1024)(128)(4,1)} %bitcast.22), calls=%async_computation.1 | async-start | bytes 8388608
  5.9 0.8 copy-start.2
  6.7 4.4 %copy-start.1 = (bf16[192,512]{1,0:T(8,128)(2,1)S(1)}, bf16[192,512]{1,0:T(8,128)(2,1)}, u32[]{:S(2)}) copy-start(bf16[192,512]{1,0:T(8,128)(2,1)} %get-tuple-element.112.own) | copy-start | bytes 589828
  6.7 4.4 %copy-start.3 = (s32[2]{0:T(128)S(1)}, s32[2]{0:T(128)}, u32[]{:S(2)}) copy-start(s32[2]{0:T(128)} %get-tuple-element.111.kinds.bucket_ref) | copy-start | bytes 28
  6.7 11.6 %slice-start.3 = ((s8[4718592]{0:T(1024)(128)(4,1)}), s8[524288]{0:T(1024)(128)(4,1)S(1)}, s32[]{:S(2)}) async-start(s8[4718592]{0:T(1024)(128)(4,1)} %bitcast.24), calls=%async_computation.3 | async-start | bytes 1048576
  7.3 11.0 %copy-start = (bf16[512,512]{1,0:T(8,128)(2,1)S(1)}, bf16[512,512]{1,0:T(8,128)(2,1)}, u32[]{:S(2)}) copy-start(bf16[512,512]{1,0:T(8,128)(2,1)} %wp.3) | copy-start | bytes 1572868
  7.3 11.0 %copy-start.4 = (bf16[512,512]{1,0:T(8,128)(2,1)S(1)}, bf16[512,512]{1,0:T(8,128)(2,1)}, u32[]{:S(2)}) copy-start(bf16[512,512]{1,0:T(8,128)(2,1)} %wq.1) | copy-start | bytes 1572868
  7.3 11.0 %copy-start.5 = (bf16[512,512]{1,0:T(8,128)(2,1)S(1)}, bf16[512,512]{1,0:T(8,128)(2,1)}, u32[]{:S(2)}) copy-start(bf16[512,512]{1,0:T(8,128)(2,1)} %wk.1) | copy-start | bytes 1572868
  7.3 11.0 %copy-start.6 = (bf16[512,512]{1,0:T(8,128)(2,1)S(1)}, bf16[512,512]{1,0:T(8,128)(2,1)}, u32[]{:S(2)}) copy-start(bf16[512,512]{1,0:T(8,128)(2,1)} %wv.1) | copy-start | bytes 1572868
  7.3 11.0 %collective-permute-start.3 = (bf16[192,512]{1,0:T(8,128)(2,1)S(1)}, bf16[192,512]{1,0:T(8,128)(2,1)S(1)}, u32[]{:S(2)}, u32[]{:S(2)}) collective-permute-start(bf16[192,512]{1,0:T(8,128)(2,1)S(1)} %get-tuple-element.118.own), channel_id=1, source_target_pairs={{0,1},{1,0},{2,3},{3,2},{4,5},{5,4},{6,7},{7,6},{8,9},{9,8},{10,11... | collective-permute-start | bytes 589832 | tf_op jit(solution)/shard_map/ppermute | solution.py:644
  7.9 10.4 %collective-permute-start.4 = (bf16[160,512]{1,0:T(8,128)(2,1)S(1)}, bf16[160,512]{1,0:T(8,128)(2,1)S(1)}, u32[]{:S(2)}, u32[]{:S(2)}) collective-permute-start(bf16[160,512]{1,0:T(8,128)(2,1)S(1)} %get-tuple-element.119), channel_id=1, source_target_pairs={{0,2},{1,3},{2,0},{3,1},{4,6},{5,7},{6,4},{7,5},{8,10},{9,11},{10,... | collective-permute-start | bytes 491528 | tf_op jit(solution)/shard_map/ppermute | solution.py:647
  8.0 10.3 %collective-permute-start.5 = (bf16[160,512]{1,0:T(8,128)(2,1)S(1)}, bf16[160,512]{1,0:T(8,128)(2,1)S(1)}, u32[]{:S(2)}, u32[]{:S(2)}) collective-permute-start(bf16[160,512]{1,0:T(8,128)(2,1)S(1)} %get-tuple-element.119), channel_id=1, source_target_pairs={{0,3},{1,2},{2,1},{3,0},{4,7},{5,6},{6,5},{7,4},{8,11},{9,10},{10,... | collective-permute-start | bytes 491528 | tf_op jit(solution)/shard_map/ppermute | solution.py:682
  9.5 1.6 %collective-permute-start.2 = (bf16[128,512]{1,0:T(8,128)(2,1)S(1)}, bf16[128,512]{1,0:T(8,128)(2,1)S(1)}, u32[]{:S(2)}, u32[]{:S(2)}) collective-permute-start(bf16[128,512]{1,0:T(8,128)(2,1)S(1)} %collective-permute-done.1.received), channel_id=1, source_target_pairs={{0,1},{1,0},{2,3},{3,2},{4,5},{5,4},{6,7},{7,6},{8,9},{9,8},{10,11... | collective-permute-start | bytes 393224 | tf_op jit(solution)/shard_map/ppermute | solution.py:644
  16.4 14.4 %collective-permute-start.6 = (bf16[2,512,256]{2,1,0:T(8,128)(2,1)S(1)}, bf16[2,512,256]{2,1,0:T(8,128)(2,1)S(1)}, u32[]{:S(2)}, u32[]{:S(2)}) collective-permute-start(bf16[2,512,256]{2,1,0:T(8,128)(2,1)S(1)} %get-tuple-element.125), channel_id=1, source_target_pairs={{0,2},{1,3},{2,0},{3,1},{4,6},{5,7},{6,4},{7,5},{8,10},{9,11},{10,... | collective-permute-start | bytes 1572872 | tf_op jit(solution)/shard_map/ppermute | solution.py:647
  28.0 7.2 %collective-permute-start.8 = (bf16[512,128]{1,0:T(8,128)(2,1)S(1)}, bf16[512,128]{1,0:T(8,128)(2,1)S(1)}, u32[]{:S(2)}, u32[]{:S(2)}) collective-permute-start(bf16[512,128]{1,0:T(8,128)(2,1)S(1)} %get-tuple-element.129), channel_id=1, source_target_pairs={{0,2},{1,3},{2,0},{3,1},{4,6},{5,7},{6,4},{7,5},{8,10},{9,11},{10,... | collective-permute-start | bytes 393224 | tf_op jit(solution)/shard_map/ppermute | solution.py:647
  28.2 13.9 %collective-permute-start.9 = (bf16[4,256,256]{2,1,0:T(8,128)(2,1)S(1)}, bf16[4,256,256]{2,1,0:T(8,128)(2,1)S(1)}, u32[]{:S(2)}, u32[]{:S(2)}) collective-permute-start(bf16[4,256,256]{2,1,0:T(8,128)(2,1)S(1)} %get-tuple-element.135), channel_id=1, source_target_pairs={{0,4},{4,0},{8,12},{12,8},{16,20},{20,16},{24,28},{28,24},{1,5},{5... | collective-permute-start | bytes 1572872 | tf_op jit(solution)/shard_map/ppermute | solution.py:650
  30.8 4.3 %collective-permute-start.7 = (bf16[2,512,256]{2,1,0:T(8,128)(2,1)S(1)}, bf16[2,512,256]{2,1,0:T(8,128)(2,1)S(1)}, u32[]{:S(2)}, u32[]{:S(2)}) collective-permute-start(bf16[2,512,256]{2,1,0:T(8,128)(2,1)S(1)} %collective-permute-done.6.half_ref), channel_id=1, source_target_pairs={{0,1},{1,0},{2,3},{3,2},{4,5},{5,4},{6,7},{7,6},{8,9},{9,8},{10,11... | collective-permute-start | bytes 1572872 | tf_op jit(solution)/shard_map/ppermute | solution.py:644
  38.5 18.4 %collective-permute-start.14 = (bf16[4,576,128]{2,1,0:T(8,128)(2,1)S(1)}, bf16[4,576,128]{2,1,0:T(8,128)(2,1)S(1)}, u32[]{:S(2)}, u32[]{:S(2)}) collective-permute-start(bf16[4,576,128]{2,1,0:T(8,128)(2,1)S(1)} %get-tuple-element.133), channel_id=1, source_target_pairs={{0,4},{4,0},{8,12},{12,8},{16,20},{20,16},{24,28},{28,24},{1,5},{5... | collective-permute-start | bytes 1769480 | tf_op jit(solution)/shard_map/ppermute | solution.py:650
  40.3 6.4 %collective-permute-start.10 = (bf16[512,128]{1,0:T(8,128)(2,1)S(1)}, bf16[512,128]{1,0:T(8,128)(2,1)S(1)}, u32[]{:S(2)}, u32[]{:S(2)}) collective-permute-start(bf16[512,128]{1,0:T(8,128)(2,1)S(1)} %get-tuple-element.141), channel_id=1, source_target_pairs={{0,2},{1,3},{2,0},{3,1},{4,6},{5,7},{6,4},{7,5},{8,10},{9,11},{10,... | collective-permute-start | bytes 393224 | tf_op jit(solution)/shard_map/ppermute | solution.py:647
  42.3 8.9 %collective-permute-start.11 = (bf16[1,256,256]{2,1,0:T(8,128)(2,1)S(1)}, bf16[1,256,256]{2,1,0:T(8,128)(2,1)S(1)}, u32[]{:S(2)}, u32[]{:S(2)}) collective-permute-start(bf16[1,256,256]{2,1,0:T(8,128)(2,1)S(1)} %get-tuple-element.137), channel_id=1, source_target_pairs={{0,8},{4,12},{8,0},{12,4},{16,24},{20,28},{24,16},{28,20},{1,9},{5... | collective-permute-start | bytes 393224 | tf_op jit(solution)/shard_map/ppermute | solution.py:650
  43.9 12.9 %collective-permute-start.12 = (bf16[1,256,256]{2,1,0:T(8,128)(2,1)S(1)}, bf16[1,256,256]{2,1,0:T(8,128)(2,1)S(1)}, u32[]{:S(2)}, u32[]{:S(2)}) collective-permute-start(bf16[1,256,256]{2,1,0:T(8,128)(2,1)S(1)} %get-tuple-element.138), channel_id=1, source_target_pairs={{0,16},{4,20},{8,24},{12,28},{16,0},{20,4},{24,8},{28,12},{1,17},{... | collective-permute-start | bytes 393224 | tf_op jit(solution)/shard_map/ppermute | solution.py:650
  46.5 10.3 %collective-permute-start.13 = (bf16[1,256,256]{2,1,0:T(8,128)(2,1)S(1)}, bf16[1,256,256]{2,1,0:T(8,128)(2,1)S(1)}, u32[]{:S(2)}, u32[]{:S(2)}) collective-permute-start(bf16[1,256,256]{2,1,0:T(8,128)(2,1)S(1)} %get-tuple-element.139), channel_id=1, source_target_pairs={{0,24},{4,28},{8,16},{12,20},{16,8},{20,12},{24,0},{28,4},{1,25},{... | collective-permute-start | bytes 393224 | tf_op jit(solution)/shard_map/ppermute | solution.py:650
  49.9 17.2 %collective-permute-start.16 = (bf16[4,576,128]{2,1,0:T(8,128)(2,1)S(1)}, bf16[4,576,128]{2,1,0:T(8,128)(2,1)S(1)}, u32[]{:S(2)}, u32[]{:S(2)}) collective-permute-start(bf16[4,576,128]{2,1,0:T(8,128)(2,1)S(1)} %get-tuple-element.142), channel_id=1, source_target_pairs={{0,4},{4,0},{8,12},{12,8},{16,20},{20,16},{24,28},{28,24},{1,5},{5... | collective-permute-start | bytes 1769480 | tf_op jit(solution)/shard_map/ppermute | solution.py:650
  57.1 17.0 %collective-permute-start.18 = (bf16[1,576,128]{2,1,0:T(8,128)(2,1)S(1)}, bf16[1,576,128]{2,1,0:T(8,128)(2,1)S(1)}, u32[]{:S(2)}, u32[]{:S(2)}) collective-permute-start(bf16[1,576,128]{2,1,0:T(8,128)(2,1)S(1)} %get-tuple-element.148), channel_id=1, source_target_pairs={{0,8},{4,12},{8,0},{12,4},{16,24},{20,28},{24,16},{28,20},{1,9},{5... | collective-permute-start | bytes 442376 | tf_op jit(solution)/shard_map/ppermute | solution.py:650
  59.2 14.9 %collective-permute-start.19 = (bf16[1,576,128]{2,1,0:T(8,128)(2,1)S(1)}, bf16[1,576,128]{2,1,0:T(8,128)(2,1)S(1)}, u32[]{:S(2)}, u32[]{:S(2)}) collective-permute-start(bf16[1,576,128]{2,1,0:T(8,128)(2,1)S(1)} %get-tuple-element.149), channel_id=1, source_target_pairs={{0,16},{4,20},{8,24},{12,28},{16,0},{20,4},{24,8},{28,12},{1,17},{... | collective-permute-start | bytes 442376 | tf_op jit(solution)/shard_map/ppermute | solution.py:650
  60.3 13.8 %collective-permute-start.20 = (bf16[1,576,128]{2,1,0:T(8,128)(2,1)S(1)}, bf16[1,576,128]{2,1,0:T(8,128)(2,1)S(1)}, u32[]{:S(2)}, u32[]{:S(2)}) collective-permute-start(bf16[1,576,128]{2,1,0:T(8,128)(2,1)S(1)} %get-tuple-element.150), channel_id=1, source_target_pairs={{0,24},{4,28},{8,16},{12,20},{16,8},{20,12},{24,0},{28,4},{1,25},{... | collective-permute-start | bytes 442376 | tf_op jit(solution)/shard_map/ppermute | solution.py:650
  61.7 16.9 %collective-permute-start.25 = (bf16[256,256]{1,0:T(8,128)(2,1)S(1)}, bf16[256,256]{1,0:T(8,128)(2,1)S(1)}, u32[]{:S(2)}, u32[]{:S(2)}) collective-permute-start(bf16[256,256]{1,0:T(8,128)(2,1)S(1)} %sumroutea.1.own_ref), channel_id=1, source_target_pairs={{0,2},{1,3},{2,0},{3,1},{4,6},{5,7},{6,4},{7,5},{8,10},{9,11},{10,... | collective-permute-start | bytes 393224 | tf_op jit(solution)/shard_map/ppermute | solution.py:647
  67.1 3.7 %collective-permute-start.15 = (bf16[4,16,128]{2,1,0:T(8,128)(2,1)S(1)}, bf16[4,16,128]{2,1,0:T(8,128)(2,1)S(1)}, u32[]{:S(2)}, u32[]{:S(2)}) collective-permute-start(bf16[4,16,128]{2,1,0:T(8,128)(2,1)S(1)} %get-tuple-element.156), channel_id=1, source_target_pairs={{0,4},{4,0},{8,12},{12,8},{16,20},{20,16},{24,28},{28,24},{1,5},{5... | collective-permute-start | bytes 49160 | tf_op jit(solution)/shard_map/ppermute | solution.py:650
  71.9 17.7 %collective-permute-start.17 = (bf16[2,128,512]{2,1,0:T(8,128)(2,1)S(1)}, bf16[2,128,512]{2,1,0:T(8,128)(2,1)S(1)}, u32[]{:S(2)}, u32[]{:S(2)}) collective-permute-start(bf16[2,128,512]{2,1,0:T(8,128)(2,1)S(1)} %get-tuple-element.168), channel_id=1, source_target_pairs={{0,2},{1,3},{2,0},{3,1},{4,6},{5,7},{6,4},{7,5},{8,10},{9,11},{10,... | collective-permute-start | bytes 786440 | tf_op jit(solution)/shard_map/ppermute | solution.py:647
  74.1 9.8 %collective-permute-start.23 = (bf16[1,592,128]{2,1,0:T(8,128)(2,1)S(1)}, bf16[1,592,128]{2,1,0:T(8,128)(2,1)S(1)}, u32[]{:S(2)}, u32[]{:S(2)}) collective-permute-start(bf16[1,592,128]{2,1,0:T(8,128)(2,1)S(1)} %get-tuple-element.174), channel_id=1, source_target_pairs={{0,8},{4,12},{8,0},{12,4},{16,24},{20,28},{24,16},{28,20},{1,9},{5... | collective-permute-start | bytes 454664 | tf_op jit(solution)/shard_map/ppermute | solution.py:650
  75.5 13.2 %collective-permute-start.22 = (bf16[1,592,128]{2,1,0:T(8,128)(2,1)S(1)}, bf16[1,592,128]{2,1,0:T(8,128)(2,1)S(1)}, u32[]{:S(2)}, u32[]{:S(2)}) collective-permute-start(bf16[1,592,128]{2,1,0:T(8,128)(2,1)S(1)} %get-tuple-element.172), channel_id=1, source_target_pairs={{0,16},{4,20},{8,24},{12,28},{16,0},{20,4},{24,8},{28,12},{1,17},{... | collective-permute-start | bytes 454664 | tf_op jit(solution)/shard_map/ppermute | solution.py:650
  78.1 10.6 %collective-permute-start.21 = (bf16[1,592,128]{2,1,0:T(8,128)(2,1)S(1)}, bf16[1,592,128]{2,1,0:T(8,128)(2,1)S(1)}, u32[]{:S(2)}, u32[]{:S(2)}) collective-permute-start(bf16[1,592,128]{2,1,0:T(8,128)(2,1)S(1)} %get-tuple-element.170), channel_id=1, source_target_pairs={{0,24},{4,28},{8,16},{12,20},{16,8},{20,12},{24,0},{28,4},{1,25},{... | collective-permute-start | bytes 454664 | tf_op jit(solution)/shard_map/ppermute | solution.py:650
  78.7 5.2 %collective-permute-start.24 = (bf16[576,128]{1,0:T(8,128)(2,1)S(1)}, bf16[576,128]{1,0:T(8,128)(2,1)S(1)}, u32[]{:S(2)}, u32[]{:S(2)}) collective-permute-start(bf16[576,128]{1,0:T(8,128)(2,1)S(1)} %sumrouteb.1.own_ref), channel_id=1, source_target_pairs={{0,2},{1,3},{2,0},{3,1},{4,6},{5,7},{6,4},{7,5},{8,10},{9,11},{10,... | collective-permute-start | bytes 442376 | tf_op jit(solution)/shard_map/ppermute | solution.py:647
  88.7 5.3 %collective-permute-start.26 = (bf16[592,128]{1,0:T(8,128)(2,1)S(1)}, bf16[592,128]{1,0:T(8,128)(2,1)S(1)}, u32[]{:S(2)}, u32[]{:S(2)}) collective-permute-start(bf16[592,128]{1,0:T(8,128)(2,1)S(1)} %sumroutec.1.own_ref), channel_id=1, source_target_pairs={{0,2},{1,3},{2,0},{3,1},{4,6},{5,7},{6,4},{7,5},{8,10},{9,11},{10,... | collective-permute-start | bytes 454664 | tf_op jit(solution)/shard_map/ppermute | solution.py:647
  89.1 3.4 %collective-permute-start.28 = (bf16[576,128]{1,0:T(8,128)(2,1)S(1)}, bf16[576,128]{1,0:T(8,128)(2,1)S(1)}, u32[]{:S(2)}, u32[]{:S(2)}) collective-permute-start(bf16[576,128]{1,0:T(8,128)(2,1)S(1)} %sumrouteb.1.own_ref), channel_id=1, source_target_pairs={{0,1},{1,0},{2,3},{3,2},{4,5},{5,4},{6,7},{7,6},{8,9},{9,8},{10,11... | collective-permute-start | bytes 442376 | tf_op jit(solution)/shard_map/ppermute | solution.py:644
  89.1 3.4 %collective-permute-start.29 = (bf16[576,128]{1,0:T(8,128)(2,1)S(1)}, bf16[576,128]{1,0:T(8,128)(2,1)S(1)}, u32[]{:S(2)}, u32[]{:S(2)}) collective-permute-start(bf16[576,128]{1,0:T(8,128)(2,1)S(1)} %collective-permute-done.24.far_ref), channel_id=1, source_target_pairs={{0,1},{1,0},{2,3},{3,2},{4,5},{5,4},{6,7},{7,6},{8,9},{9,8},{10,11... | collective-permute-start | bytes 442376 | tf_op jit(solution)/shard_map/ppermute | solution.py:644
  89.6 2.0 %collective-permute-start.30 = (bf16[256,256]{1,0:T(8,128)(2,1)S(1)}, bf16[256,256]{1,0:T(8,128)(2,1)S(1)}, u32[]{:S(2)}, u32[]{:S(2)}) collective-permute-start(bf16[256,256]{1,0:T(8,128)(2,1)S(1)} %sumroutea.1.own_ref), channel_id=1, source_target_pairs={{0,1},{1,0},{2,3},{3,2},{4,5},{5,4},{6,7},{7,6},{8,9},{9,8},{10,11... | collective-permute-start | bytes 393224 | tf_op jit(solution)/shard_map/ppermute | solution.py:644
  89.6 2.0 %collective-permute-start.31 = (bf16[256,256]{1,0:T(8,128)(2,1)S(1)}, bf16[256,256]{1,0:T(8,128)(2,1)S(1)}, u32[]{:S(2)}, u32[]{:S(2)}) collective-permute-start(bf16[256,256]{1,0:T(8,128)(2,1)S(1)} %collective-permute-done.25.far_ref), channel_id=1, source_target_pairs={{0,1},{1,0},{2,3},{3,2},{4,5},{5,4},{6,7},{7,6},{8,9},{9,8},{10,11... | collective-permute-start | bytes 393224 | tf_op jit(solution)/shard_map/ppermute | solution.py:644
  91.7 2.6 %collective-permute-start.27 = (bf16[592,128]{1,0:T(8,128)(2,1)S(1)}, bf16[592,128]{1,0:T(8,128)(2,1)S(1)}, u32[]{:S(2)}, u32[]{:S(2)}) collective-permute-start(bf16[592,128]{1,0:T(8,128)(2,1)S(1)} %sumroutec.1.own_ref), channel_id=1, source_target_pairs={{0,1},{1,0},{2,3},{3,2},{4,5},{5,4},{6,7},{7,6},{8,9},{9,8},{10,11... | collective-permute-start | bytes 454664 | tf_op jit(solution)/shard_map/ppermute | solution.py:644
  94.0 1.4 %collective-permute-start.32 = (bf16[592,128]{1,0:T(8,128)(2,1)S(1)}, bf16[592,128]{1,0:T(8,128)(2,1)S(1)}, u32[]{:S(2)}, u32[]{:S(2)}) collective-permute-start(bf16[592,128]{1,0:T(8,128)(2,1)S(1)} %collective-permute-done.26.far_ref), channel_id=1, source_target_pairs={{0,1},{1,0},{2,3},{3,2},{4,5},{5,4},{6,7},{7,6},{8,9},{9,8},{10,11... | collective-permute-start | bytes 454664 | tf_op jit(solution)/shard_map/ppermute | solution.py:644

commit v11 on v8

--- a/solution.py
+++ b/solution.py
@@ -766,13 +766,13 @@
     )
     vec_got = to_batch(vec_send, 1)
     parts_b, got_b = spread("routeb", 1, after(keep2, vec_keep, shard_a), got2)
+    parts_c, got_c = spread("routec", 1, keep1, got1, (vec_keep, vec_got), behind=got_b)
+    shard_b = finish("routeb", parts_b, together(got_b, parts_c[0]))
     out_own, image_send = call(
         output_kernel, "output", [((192, C), BF16), ((2, 128, C), BF16)], [img16], 10,
-        kinds, after(middle, *parts_b), mixed, vecs, proj_weight, grad_send,
+        kinds, after(middle, shard_b), mixed, vecs, proj_weight, grad_send,
     )
     image_away = to_chip(image_send)
-    parts_c, got_c = spread("routec", 1, keep1, got1, (vec_keep, vec_got), behind=got_b)
-    shard_b = finish("routeb", parts_b, together(got_b, parts_c[0]))
     gathered_a = gather(shard_a)
     gathered_b = gather(shard_b)
     shard_c = finish(

time: 96.1 us -> 98.5 us (1.025)
  waiting for transfers between devices: 22 us -> 24.5 us
    ppermute x13, waiting for transfers between devices: 13.4 us -> 19.9 us  [to_batch(): return lax.ppermute(v, 'batch', [(i, i ^ change) for i in range(batches)])]
    ppermute x9, waiting for transfers between devices: 6.38 us -> 1.21 us  [to_chip(): return lax.ppermute(v, 'height', [(i, i ^ 2) for i in range(4)])]
    ppermute x10, waiting for transfers between devices: 2.26 us -> 3.42 us  [to_core(): return lax.ppermute(v, 'height', [(i, i ^ 1) for i in range(4)])]
  transfers between devices with their start and end apart: 33 -> 33, of which waited for: 10 -> 10; matrix products, arithmetic and copies ran while one was open for 0% -> 0% of each run, Pallas kernels for 38% -> 37%
where the time goes in v11:
time: 98.5 us; the launch traced here: 98.4 us
  Pallas kernels  39.2 us (40%)
  starting transfers between devices  32.5 us (33%)
  waiting for transfers between devices  24.5 us (25%)
  between operations  1.29 us (1%)
    pallas_call x20, Pallas kernels, call(): pl.pallas_call(kernel, name=name, out_shape=[jax.ShapeDtypeStruct(shape,...  39.2 us
    ppermute x13, waiting for transfers between devices, to_batch(): return lax.ppermute(v, 'batch', [(i, i ^ change) for i in range(batches)])  19.9 us
    ppermute x13, starting transfers between devices, to_batch(): return lax.ppermute(v, 'batch', [(i, i ^ change) for i in range(batches)])  19 us
    ppermute x9, starting transfers between devices, to_chip(): return lax.ppermute(v, 'height', [(i, i ^ 2) for i in range(4)])  9.93 us
    ppermute x10, waiting for transfers between devices, to_core(): return lax.ppermute(v, 'height', [(i, i ^ 1) for i in range(4)])  3.42 us
    ppermute x10, starting transfers between devices, to_core(): return lax.ppermute(v, 'height', [(i, i ^ 1) for i in range(4)])  2.18 us
  transfers between devices with their start and end apart: 33, of which 10 were waited for; matrix products, arithmetic and copies ran while one was open for 0% of the time, Pallas kernels for 37%

profile of v11, /device:TPU:0, one launch (start us, length us, event | category | flops | bytes accessed | tf_op | source)
XLA Modules:
  0.0 98.4 jit_solution(12630735851682119984)
XLA Ops:
  0.8 0.0 slice-start
  0.8 0.0 slice-start.2
  0.8 1.9 %pack.1 = (s32[2]{0:T(128)}, bf16[128,512]{1,0:T(8,128)(2,1)}, bf16[192,512]{1,0:T(8,128)(2,1)}) custom-call(s32[2]{0:T(128)} %bucket_hbm.1, bf16[2,6,32,512]{3,2,1,0:T(8,128)(2,1)} %x_hbm.1), custom_call_target="tpu_custom_call" | custom-call | flops 10737418240 | bytes 1024 | tf_op jit(solution)/shard_map/pack/pallas_call | solution.py:593
  2.7 3.0 %collective-permute-start.1 = (bf16[128,512]{1,0:T(8,128)(2,1)}, bf16[128,512]{1,0:T(8,128)(2,1)S(1)}, u32[]{:S(2)}, u32[]{:S(2)}) collective-permute-start(bf16[128,512]{1,0:T(8,128)(2,1)} %get-tuple-element.114), channel_id=1, source_target_pairs={{0,2},{1,3},{2,0},{3,1},{4,6},{5,7},{6,4},{7,5},{8,10},{9,11},{10,... | collective-permute-start | bytes 393224 | tf_op jit(solution)/shard_map/ppermute | solution.py:648
  5.9 0.0 copy-start.2
  5.9 0.8 copy-done.2
  6.7 0.6 stack.1
  7.3 0.0 copy-start.5
  7.3 0.0 copy-start.6
  7.3 0.6 collective-permute-start.3
  7.9 0.1 collective-permute-start.4
  8.0 1.4 %collective-permute-start.5 = (bf16[160,512]{1,0:T(8,128)(2,1)S(1)}, bf16[160,512]{1,0:T(8,128)(2,1)S(1)}, u32[]{:S(2)}, u32[]{:S(2)}) collective-permute-start(bf16[160,512]{1,0:T(8,128)(2,1)S(1)} %get-tuple-element.120), channel_id=1, source_target_pairs={{0,3},{1,2},{2,1},{3,0},{4,7},{5,6},{6,5},{7,4},{8,11},{9,10},{10,... | collective-permute-start | bytes 491528 | tf_op jit(solution)/shard_map/ppermute | solution.py:684
  9.3 0.1 collective-permute-done.1.received
  9.5 0.6 collective-permute-start.2
  10.1 1.0 collective-permute-done.2.partner_received
  11.1 5.4 %first.1 = (bf16[512,512]{1,0:T(8,128)(2,1)S(1)}, f32[512,512]{1,0:T(8,128)S(1)}, bf16[512,512]{1,0:T(8,128)(2,1)S(1)}, f32[8,512]{1,0:T(8,128)S(1)}, bf16[512,5...) custom-call(s32[2]{0:T(128)S(1)} %copy-done.3, bf16[192,512]{1,0:T(8,128)(2,1)S(1)} %copy-done.1, ...), custom_call_target="tpu_custom_call" | custom-call | flops 21474836 | bytes 1024 | tf_op jit(solution)/shard_map/first/pallas_call | solution.py:593
  16.4 1.9 %collective-permute-start.6 = (bf16[2,256,512]{2,1,0:T(8,128)(2,1)S(1)}, bf16[2,256,512]{2,1,0:T(8,128)(2,1)S(1)}, u32[]{:S(2)}, u32[]{:S(2)}) collective-permute-start(bf16[2,256,512]{2,1,0:T(8,128)(2,1)S(1)} %get-tuple-element.123), channel_id=1, source_target_pairs={{0,2},{1,3},{2,0},{3,1},{4,6},{5,7},{6,4},{7,5},{8,10},{9,11},{10,... | collective-permute-start | bytes 1572872 | tf_op jit(solution)/shard_map/ppermute | solution.py:648
  18.4 9.6 %second.1 = (f32[512,512]{1,0:T(8,128)S(1)}, bf16[512,512]{1,0:T(8,128)(2,1)S(1)}, bf16[512,512]{1,0:T(8,128)(2,1)S(1)}, f32[512,512]{1,0:T(8,128)S(1)}, bf16[4,...) custom-call(s32[2]{0:T(128)S(1)} %copy-done.3, ...), custom_call_target="tpu_custom_call" | custom-call | flops 32212254720 | bytes 1024 | tf_op jit(solution)/shard_map/second/pallas_call | solution.py:593
  28.0 0.3 collective-permute-start.8
  28.3 1.5 %collective-permute-start.9 = (bf16[4,256,256]{2,1,0:T(8,128)(2,1)S(1)}, bf16[4,256,256]{2,1,0:T(8,128)(2,1)S(1)}, u32[]{:S(2)}, u32[]{:S(2)}) collective-permute-start(bf16[4,256,256]{2,1,0:T(8,128)(2,1)S(1)} %get-tuple-element.137), channel_id=1, source_target_pairs={{0,4},{4,0},{8,12},{12,8},{16,20},{20,16},{24,28},{28,24},{1,5},{5... | collective-permute-start | bytes 1572872 | tf_op jit(solution)/shard_map/ppermute | solution.py:651
  29.8 1.1 %collective-permute-done.6.half_t = bf16[2,256,512]{2,1,0:T(8,128)(2,1)S(1)} collective-permute-done((bf16[2,256,512]{2,1,0:T(8,128)(2,1)S(1)}, bf16[2,256,512]{2,1,0:T(8,128)(2,1)S(1)}, u32[]{:S(2)}, u32[]{:S(2)}) %collective-permute-start.6) | collective-permute-done | bytes 524320 | tf_op jit(solution)/shard_map/ppermute | solution.py:648
  30.8 4.3 %third.1 = (bf16[512,512]{1,0:T(8,128)(2,1)S(1)}, bf16[512,128]{1,0:T(8,128)(2,1)S(1)}, bf16[512,128]{1,0:T(8,128)(2,1)S(1)}, f32[8,512]{1,0:T(8,128)S(1)}) custom-call(s32[2]{0:T(128)S(1)} %copy-done.3, bf16[512,512]{1,0:T(8,128)(2,1)S(1)} %get-tuple-element.125.grad2_ref, f32[512,512]{1,0:T(8,128)S(1)} %get-tuple-element.126.conv_ref, ...), custom_call_target="tpu_custom_call" | custom-call | flops 21474836480 | bytes 1024 | tf_op jit(solution)/shard_map/third/pallas_call | solution.py:593
  35.2 3.3 %weight2.5 = (bf16[4,576,128]{2,1,0:T(8,128)(2,1)S(1)}, bf16[4,576,128]{2,1,0:T(8,128)(2,1)S(1)}) custom-call(s32[2]{0:T(128)S(1)} %copy-done.3, bf16[512,512]{1,0:T(8,128)(2,1)S(1)} %get-tuple-element.122.act_t, bf16[2,256,512]{2,1,0:T(8,128)(2,1)S(1)} %collective-permute-done.6.half_t, bf16[2,256,512]{2,1,0:T(8,128)(2,1)S(1)} %collective-permute-done.7.partner_half_t, ...), custom_call_target="tpu_custom_call" | custom-call | flops 1073741824 | bytes 1024 | tf_op jit(solution)/shard_map/weight2/pallas_call | solution.py:593
  38.5 1.8 %collective-permute-start.14 = (bf16[4,576,128]{2,1,0:T(8,128)(2,1)S(1)}, bf16[4,576,128]{2,1,0:T(8,128)(2,1)S(1)}, u32[]{:S(2)}, u32[]{:S(2)}) collective-permute-start(bf16[4,576,128]{2,1,0:T(8,128)(2,1)S(1)} %get-tuple-element.135), channel_id=1, source_target_pairs={{0,4},{4,0},{8,12},{12,8},{16,20},{20,16},{24,28},{28,24},{1,5},{5... | collective-permute-start | bytes 1769480 | tf_op jit(solution)/shard_map/ppermute | solution.py:651
  40.3 1.8 %collective-permute-start.10 = (bf16[512,128]{1,0:T(8,128)(2,1)S(1)}, bf16[512,128]{1,0:T(8,128)(2,1)S(1)}, u32[]{:S(2)}, u32[]{:S(2)}) collective-permute-start(bf16[512,128]{1,0:T(8,128)(2,1)S(1)} %get-tuple-element.143), channel_id=1, source_target_pairs={{0,2},{1,3},{2,0},{3,1},{4,6},{5,7},{6,4},{7,5},{8,10},{9,11},{10,... | collective-permute-start | bytes 393224 | tf_op jit(solution)/shard_map/ppermute | solution.py:648
  42.1 0.1 routea1.1
  42.2 1.6 %collective-permute-start.11 = (bf16[1,256,256]{2,1,0:T(8,128)(2,1)S(1)}, bf16[1,256,256]{2,1,0:T(8,128)(2,1)S(1)}, u32[]{:S(2)}, u32[]{:S(2)}) collective-permute-start(bf16[1,256,256]{2,1,0:T(8,128)(2,1)S(1)} %get-tuple-element.139), channel_id=1, source_target_pairs={{0,8},{4,12},{8,0},{12,4},{16,24},{20,28},{24,16},{28,20},{1,9},{5... | collective-permute-start | bytes 393224 | tf_op jit(solution)/shard_map/ppermute | solution.py:651
  43.8 2.6 %collective-permute-start.12 = (bf16[1,256,256]{2,1,0:T(8,128)(2,1)S(1)}, bf16[1,256,256]{2,1,0:T(8,128)(2,1)S(1)}, u32[]{:S(2)}, u32[]{:S(2)}) collective-permute-start(bf16[1,256,256]{2,1,0:T(8,128)(2,1)S(1)} %get-tuple-element.140), channel_id=1, source_target_pairs={{0,16},{4,20},{8,24},{12,28},{16,0},{20,4},{24,8},{28,12},{1,17},{... | collective-permute-start | bytes 393224 | tf_op jit(solution)/shard_map/ppermute | solution.py:651
  46.4 0.2 collective-permute-start.13
  46.7 3.1 %weight1.4 = (bf16[4,576,128]{2,1,0:T(8,128)(2,1)S(1)}, bf16[4,576,128]{2,1,0:T(8,128)(2,1)S(1)}) custom-call(s32[2]{0:T(128)S(1)} %copy-done.3, bf16[512,512]{1,0:T(8,128)(2,1)S(1)} %get-tuple-element.133.act_t, bf16[2,256,512]{2,1,0:T(8,128)(2,1)S(1)} %collective-permute-done.6.half_t, bf16[2,256,512]{2,1,0:T(8,128)(2,1)S(1)} %collective-permute-done.7.partner_half_t, ...), custom_call_target="tpu_custom_call" | custom-call | flops 3221225472 | bytes 1024 | tf_op jit(solution)/shard_map/weight1/pallas_call | solution.py:593
  49.7 1.4 %collective-permute-start.19 = (bf16[4,576,128]{2,1,0:T(8,128)(2,1)S(1)}, bf16[4,576,128]{2,1,0:T(8,128)(2,1)S(1)}, u32[]{:S(2)}, u32[]{:S(2)}) collective-permute-start(bf16[4,576,128]{2,1,0:T(8,128)(2,1)S(1)} %get-tuple-element.144), channel_id=1, source_target_pairs={{0,4},{4,0},{8,12},{12,8},{16,20},{20,16},{24,28},{28,24},{1,5},{5... | collective-permute-start | bytes 1769480 | tf_op jit(solution)/shard_map/ppermute | solution.py:651
  51.2 4.6 %fourth.1 = (bf16[192,512]{1,0:T(8,128)(2,1)S(1)}, bf16[128,512]{1,0:T(8,128)(2,1)S(1)}, bf16[4,16,128]{2,1,0:T(8,128)(2,1)S(1)}, bf16[4,16,128]{2,1,0:T(8,128)(2,1)S(1)}) custom-call(s32[2]{0:T(128)S(1)} %copy-done.3, bf16[512,512]{1,0:T(8,128)(2,1)S(1)} %get-tuple-element.145.grad1_ref, bf16[512,512]{1,0:T(8,128)(2,1)S(1)} %get-tuple-element.117.image_ref, ...), custom_call_target="tpu_custom_call" | custom-call | flops 536870912 | bytes 1024 | tf_op jit(solution)/shard_map/fourth/pallas_call | solution.py:593
  55.8 1.0 collective-permute-done.12.refs_2_
  56.8 0.1 sumroutea.1.own_ref
  56.9 0.1 routeb1.1
  57.0 2.1 %collective-permute-start.15 = (bf16[1,576,128]{2,1,0:T(8,128)(2,1)S(1)}, bf16[1,576,128]{2,1,0:T(8,128)(2,1)S(1)}, u32[]{:S(2)}, u32[]{:S(2)}) collective-permute-start(bf16[1,576,128]{2,1,0:T(8,128)(2,1)S(1)} %get-tuple-element.155), channel_id=1, source_target_pairs={{0,8},{4,12},{8,0},{12,4},{16,24},{20,28},{24,16},{28,20},{1,9},{5... | collective-permute-start | bytes 442376 | tf_op jit(solution)/shard_map/ppermute | solution.py:651
  59.2 1.1 %collective-permute-start.16 = (bf16[1,576,128]{2,1,0:T(8,128)(2,1)S(1)}, bf16[1,576,128]{2,1,0:T(8,128)(2,1)S(1)}, u32[]{:S(2)}, u32[]{:S(2)}) collective-permute-start(bf16[1,576,128]{2,1,0:T(8,128)(2,1)S(1)} %get-tuple-element.156), channel_id=1, source_target_pairs={{0,16},{4,20},{8,24},{12,28},{16,0},{20,4},{24,8},{28,12},{1,17},{... | collective-permute-start | bytes 442376 | tf_op jit(solution)/shard_map/ppermute | solution.py:651
  60.3 1.3 %collective-permute-start.17 = (bf16[1,576,128]{2,1,0:T(8,128)(2,1)S(1)}, bf16[1,576,128]{2,1,0:T(8,128)(2,1)S(1)}, u32[]{:S(2)}, u32[]{:S(2)}) collective-permute-start(bf16[1,576,128]{2,1,0:T(8,128)(2,1)S(1)} %get-tuple-element.157), channel_id=1, source_target_pairs={{0,24},{4,28},{8,16},{12,20},{16,8},{20,12},{24,0},{28,4},{1,25},{... | collective-permute-start | bytes 442376 | tf_op jit(solution)/shard_map/ppermute | solution.py:651
  61.6 0.5 collective-permute-start.18
  62.1 5.2 %collective-permute-done.19.got_ref = bf16[4,576,128]{2,1,0:T(8,128)(2,1)S(1)} collective-permute-done((bf16[4,576,128]{2,1,0:T(8,128)(2,1)S(1)}, bf16[4,576,128]{2,1,0:T(8,128)(2,1)S(1)}, u32[]{:S(2)}, u32[]{:S(2)}) %collective-permute-start.19) | collective-permute-done | bytes 589856 | tf_op jit(solution)/shard_map/ppermute | solution.py:651
  67.3 0.1 routec1.1
  67.5 0.0 collective-permute-done.18.got_ref
  67.5 4.8 %collective-permute-done.16.refs_2_ = bf16[1,576,128]{2,1,0:T(8,128)(2,1)S(1)} collective-permute-done((bf16[1,576,128]{2,1,0:T(8,128)(2,1)S(1)}, bf16[1,576,128]{2,1,0:T(8,128)(2,1)S(1)}, u32[]{:S(2)}, u32[]{:S(2)}) %collective-permute-start.16) | collective-permute-done | bytes 147488 | tf_op jit(solution)/shard_map/ppermute | solution.py:651
  72.3 0.1 sumrouteb.1.own_ref
  72.4 0.1 collective-permute-start.24
  72.5 2.0 %collective-permute-start.25 = (bf16[256,256]{1,0:T(8,128)(2,1)S(1)}, bf16[256,256]{1,0:T(8,128)(2,1)S(1)}, u32[]{:S(2)}, u32[]{:S(2)}) collective-permute-start(bf16[256,256]{1,0:T(8,128)(2,1)S(1)} %sumroutea.1.own_ref), channel_id=1, source_target_pairs={{0,2},{1,3},{2,0},{3,1},{4,6},{5,7},{6,4},{7,5},{8,10},{9,11},{10,... | collective-permute-start | bytes 393224 | tf_op jit(solution)/shard_map/ppermute | solution.py:648
  74.5 2.1 %collective-permute-start.23 = (bf16[1,592,128]{2,1,0:T(8,128)(2,1)S(1)}, bf16[1,592,128]{2,1,0:T(8,128)(2,1)S(1)}, u32[]{:S(2)}, u32[]{:S(2)}) collective-permute-start(bf16[1,592,128]{2,1,0:T(8,128)(2,1)S(1)} %get-tuple-element.179), channel_id=1, source_target_pairs={{0,8},{4,12},{8,0},{12,4},{16,24},{20,28},{24,16},{28,20},{1,9},{5... | collective-permute-start | bytes 454664 | tf_op jit(solution)/shard_map/ppermute | solution.py:651
  76.6 1.1 %collective-permute-start.22 = (bf16[1,592,128]{2,1,0:T(8,128)(2,1)S(1)}, bf16[1,592,128]{2,1,0:T(8,128)(2,1)S(1)}, u32[]{:S(2)}, u32[]{:S(2)}) collective-permute-start(bf16[1,592,128]{2,1,0:T(8,128)(2,1)S(1)} %get-tuple-element.177), channel_id=1, source_target_pairs={{0,16},{4,20},{8,24},{12,28},{16,0},{20,4},{24,8},{28,12},{1,17},{... | collective-permute-start | bytes 454664 | tf_op jit(solution)/shard_map/ppermute | solution.py:651
  77.7 1.5 %collective-permute-start.21 = (bf16[1,592,128]{2,1,0:T(8,128)(2,1)S(1)}, bf16[1,592,128]{2,1,0:T(8,128)(2,1)S(1)}, u32[]{:S(2)}, u32[]{:S(2)}) collective-permute-start(bf16[1,592,128]{2,1,0:T(8,128)(2,1)S(1)} %get-tuple-element.175), channel_id=1, source_target_pairs={{0,24},{4,28},{8,16},{12,20},{16,8},{20,12},{24,0},{28,4},{1,25},{... | collective-permute-start | bytes 454664 | tf_op jit(solution)/shard_map/ppermute | solution.py:651
  79.1 1.0 %output.1 = (bf16[192,512]{1,0:T(8,128)(2,1)S(1)}, bf16[2,128,512]{2,1,0:T(8,128)(2,1)S(1)}) custom-call(s32[2]{0:T(128)S(1)} %copy-done.3, f32[512,512]{1,0:T(8,128)S(1)} %get-tuple-element.168.middle_ref, bf16[512,512]{1,0:T(8,128)(2,1)S(1)} %get-tuple-element.169.mixed_ref, f32[16,512]{1,0:T(8,128)S(1)} %get-tuple-element.115.vecs, ...), custom_call_target="tpu_custom_call" | custom-call | flops 21474836 | bytes 1024 | tf_op jit(solution)/shard_map/output/pallas_call | solution.py:593
  80.2 0.4 collective-permute-start.20
  80.6 0.4 collective-permute-done.23.refs_3_
  81.0 8.5 %collective-permute-done.22.refs_2_ = bf16[1,592,128]{2,1,0:T(8,128)(2,1)S(1)} collective-permute-done((bf16[1,592,128]{2,1,0:T(8,128)(2,1)S(1)}, bf16[1,592,128]{2,1,0:T(8,128)(2,1)S(1)}, u32[]{:S(2)}, u32[]{:S(2)}) %collective-permute-start.22) | collective-permute-done | bytes 151584 | tf_op jit(solution)/shard_map/ppermute | solution.py:651
  89.5 0.1 sumroutec.1.own_ref
  89.5 0.4 collective-permute-start.26
  90.0 0.5 collective-permute-start.29
  90.5 1.3 %collective-permute-done.31.diagonal_ref = bf16[256,256]{1,0:T(8,128)(2,1)S(1)} collective-permute-done((bf16[256,256]{1,0:T(8,128)(2,1)S(1)}, bf16[256,256]{1,0:T(8,128)(2,1)S(1)}, u32[]{:S(2)}, u32[]{:S(2)}) %collective-permute-start.31) | collective-permute-done | bytes 131104 | tf_op jit(solution)/shard_map/ppermute | solution.py:645
  91.8 0.2 collective-permute-start.27
  92.0 0.9 joina.1
  92.9 1.5 %unpack.1 = (bf16[2,6,32,512]{3,2,1,0:T(8,128)(2,1)}, bf16[2,6,32,512]{3,2,1,0:T(8,128)(2,1)}) custom-call(s32[2]{0:T(128)S(1)} %copy-done.3, bf16[192,512]{1,0:T(8,128)(2,1)S(1)} %get-tuple-element.171.out_own, bf16[192,512]{1,0:T(8,128)(2,1)S(1)} %get-tuple-element.172.grad_own, bf16[2,128,512]{2,1,0:T(8,128)(2,1)S(1)} %collective-permute-done.20.away_ref), custom_call_target="tpu_custom_call" | custom-call | flops 21474836 | bytes 1024 | tf_op jit(solution)/shard_map/unpack/pallas_call | solution.py:593
  94.4 1.2 %joinb.1 = f32[576,512]{1,0:T(8,128)} custom-call(bf16[576,128]{1,0:T(8,128)(2,1)S(1)} %sumrouteb.1.own_ref, bf16[576,128]{1,0:T(8,128)(2,1)S(1)} %collective-permute-done.24.far_ref, bf16[576,128]{1,0:T(8,128)(2,1)S(1)} %collective-permute-done.28.near_ref, bf16[576,128]{1,0:T(8,128)(2,1)S(1)} %collective-permute-done.29.diagonal_ref), custom_call_target="tpu_custom_call" | custom-call | flops 21474836 | bytes 1024 | tf_op jit(solution)/shard_map/joinb/pallas_call | solution.py:593
  95.6 0.3 collective-permute-start.32
  95.9 1.1 %collective-permute-done.32.diagonal_ref = bf16[592,128]{1,0:T(8,128)(2,1)S(1)} collective-permute-done((bf16[592,128]{1,0:T(8,128)(2,1)S(1)}, bf16[592,128]{1,0:T(8,128)(2,1)S(1)}, u32[]{:S(2)}, u32[]{:S(2)}) %collective-permute-start.32) | collective-permute-done | bytes 151584 | tf_op jit(solution)/shard_map/ppermute | solution.py:645
  97.0 1.2 %joinc.1 = (f32[576,512]{1,0:T(8,128)}, f32[1,64]{1,0:T(1,128)}, f32[1,64]{1,0:T(1,128)}, f32[1,64]{1,0:T(1,128)}, f32[1,64]{1,0:T(1,128)}, /*index=5*/f32[1,64]...) custom-call(bf16[592,128]{1,0:T(8,128)(2,1)S(1)} %sumroutec.1.own_re, ...), custom_call_target="tpu_custom_call" | custom-call | flops 21474836 | bytes 1024 | tf_op jit(solution)/shard_map/joinc/pallas_call | solution.py:593
  (70 shorter events, 0.2 us)
Async XLA Ops:
  0.7 5.1 %copy-start.8 = (f32[512]{0:T(512)S(1)}, f32[512]{0:T(512)}, u32[]{:S(2)}) copy-start(f32[512]{0:T(512)} %param.22) | copy-start | bytes 6148
  0.7 5.1 %copy-start.9 = (f32[512]{0:T(512)S(1)}, f32[512]{0:T(512)}, u32[]{:S(2)}) copy-start(f32[512]{0:T(512)} %param.23) | copy-start | bytes 6148
  0.7 5.1 %copy-start.18 = (f32[512]{0:T(512)S(1)}, f32[512]{0:T(512)}, u32[]{:S(2)}) copy-start(f32[512]{0:T(512)} %param.38) | copy-start | bytes 6148
  0.7 5.1 %copy-start.10 = (f32[512]{0:T(512)S(1)}, f32[512]{0:T(512)}, u32[]{:S(2)}) copy-start(f32[512]{0:T(512)} %param.25) | copy-start | bytes 6148
  0.7 5.1 %copy-start.11 = (f32[512]{0:T(512)S(1)}, f32[512]{0:T(512)}, u32[]{:S(2)}) copy-start(f32[512]{0:T(512)} %param.26) | copy-start | bytes 6148
  0.7 5.1 %copy-start.12 = (f32[512]{0:T(512)S(1)}, f32[512]{0:T(512)}, u32[]{:S(2)}) copy-start(f32[512]{0:T(512)} %param.27) | copy-start | bytes 6148
  0.7 5.1 %copy-start.13 = (f32[512]{0:T(512)S(1)}, f32[512]{0:T(512)}, u32[]{:S(2)}) copy-start(f32[512]{0:T(512)} %param.29) | copy-start | bytes 6148
  0.7 5.1 %copy-start.14 = (f32[512]{0:T(512)S(1)}, f32[512]{0:T(512)}, u32[]{:S(2)}) copy-start(f32[512]{0:T(512)} %param.30) | copy-start | bytes 6148
  0.7 5.1 %copy-start.15 = (f32[512]{0:T(512)S(1)}, f32[512]{0:T(512)}, u32[]{:S(2)}) copy-start(f32[512]{0:T(512)} %param.31) | copy-start | bytes 6148
  0.8 5.1 %copy-start.16 = (f32[512]{0:T(512)S(1)}, f32[512]{0:T(512)}, u32[]{:S(2)}) copy-start(f32[512]{0:T(512)} %param.33) | copy-start | bytes 6148
  0.8 5.1 %copy-start.17 = (f32[512]{0:T(512)S(1)}, f32[512]{0:T(512)}, u32[]{:S(2)}) copy-start(f32[512]{0:T(512)} %param.36) | copy-start | bytes 6148
  0.8 5.1 %copy-start.7 = (bf16[2,6,32,512]{3,2,1,0:T(8,128)(2,1)S(1)}, bf16[2,6,32,512]{3,2,1,0:T(8,128)(2,1)}, u32[]{:S(2)}) copy-start(bf16[2,6,32,512]{3,2,1,0:T(8,128)(2,1)} %cot_ref.1) | copy-start | bytes 1179652
  0.8 10.3 %slice-start = ((s8[4718592]{0:T(1024)(128)(4,1)}), s8[524288]{0:T(1024)(128)(4,1)S(1)}, s32[]{:S(2)}) async-start(s8[4718592]{0:T(1024)(128)(4,1)} %bitcast.22), calls=%async_computation | async-start | bytes 1048576
  0.8 17.5 %slice-start.2 = ((s8[4718592]{0:T(1024)(128)(4,1)}), s8[4194304]{0:T(1024)(128)(4,1)S(1)}, s32[]{:S(2)}) async-start(s8[4718592]{0:T(1024)(128)(4,1)} %bitcast.24), calls=%async_computation.2 | async-start | bytes 8388608
  2.7 6.7 %collective-permute-start.1 = (bf16[128,512]{1,0:T(8,128)(2,1)}, bf16[128,512]{1,0:T(8,128)(2,1)S(1)}, u32[]{:S(2)}, u32[]{:S(2)}) collective-permute-start(bf16[128,512]{1,0:T(8,128)(2,1)} %get-tuple-element.114), channel_id=1, source_target_pairs={{0,2},{1,3},{2,0},{3,1},{4,6},{5,7},{6,4},{7,5},{8,10},{9,11},{10,... | collective-permute-start | bytes 393224 | tf_op jit(solution)/shard_map/ppermute | solution.py:648
  5.8 4.3 %collective-permute-start = (bf16[192,512]{1,0:T(8,128)(2,1)}, bf16[192,512]{1,0:T(8,128)(2,1)S(1)}, u32[]{:S(2)}, u32[]{:S(2)}) collective-permute-start(bf16[192,512]{1,0:T(8,128)(2,1)} %get-tuple-element.113.own), channel_id=1, source_target_pairs={{0,1},{1,0},{2,3},{3,2},{4,5},{5,4},{6,7},{7,6},{8,9},{9,8},{10,11... | collective-permute-start | bytes 589832 | tf_op jit(solution)/shard_map/ppermute | solution.py:645
  5.8 5.3 %slice-start.1 = ((s8[4718592]{0:T(1024)(128)(4,1)}), s8[4194304]{0:T(1024)(128)(4,1)S(1)}, s32[]{:S(2)}) async-start(s8[4718592]{0:T(1024)(128)(4,1)} %bitcast.22), calls=%async_computation.1 | async-start | bytes 8388608
  5.9 0.8 copy-start.2
  6.7 4.4 %copy-start.1 = (bf16[192,512]{1,0:T(8,128)(2,1)S(1)}, bf16[192,512]{1,0:T(8,128)(2,1)}, u32[]{:S(2)}) copy-start(bf16[192,512]{1,0:T(8,128)(2,1)} %get-tuple-element.113.own) | copy-start | bytes 589828
  6.7 4.4 %copy-start.3 = (s32[2]{0:T(128)S(1)}, s32[2]{0:T(128)}, u32[]{:S(2)}) copy-start(s32[2]{0:T(128)} %get-tuple-element.112.kinds.bucket_ref) | copy-start | bytes 28
  6.7 11.6 %slice-start.3 = ((s8[4718592]{0:T(1024)(128)(4,1)}), s8[524288]{0:T(1024)(128)(4,1)S(1)}, s32[]{:S(2)}) async-start(s8[4718592]{0:T(1024)(128)(4,1)} %bitcast.24), calls=%async_computation.3 | async-start | bytes 1048576
  7.3 11.1 %copy-start = (bf16[512,512]{1,0:T(8,128)(2,1)S(1)}, bf16[512,512]{1,0:T(8,128)(2,1)}, u32[]{:S(2)}) copy-start(bf16[512,512]{1,0:T(8,128)(2,1)} %wp.3) | copy-start | bytes 1572868
  7.3 11.0 %copy-start.4 = (bf16[512,512]{1,0:T(8,128)(2,1)S(1)}, bf16[512,512]{1,0:T(8,128)(2,1)}, u32[]{:S(2)}) copy-start(bf16[512,512]{1,0:T(8,128)(2,1)} %wq.1) | copy-start | bytes 1572868
  7.3 11.0 %copy-start.5 = (bf16[512,512]{1,0:T(8,128)(2,1)S(1)}, bf16[512,512]{1,0:T(8,128)(2,1)}, u32[]{:S(2)}) copy-start(bf16[512,512]{1,0:T(8,128)(2,1)} %wk.1) | copy-start | bytes 1572868
  7.3 11.0 %copy-start.6 = (bf16[512,512]{1,0:T(8,128)(2,1)S(1)}, bf16[512,512]{1,0:T(8,128)(2,1)}, u32[]{:S(2)}) copy-start(bf16[512,512]{1,0:T(8,128)(2,1)} %wv.1) | copy-start | bytes 1572868
  7.3 11.0 %collective-permute-start.3 = (bf16[192,512]{1,0:T(8,128)(2,1)S(1)}, bf16[192,512]{1,0:T(8,128)(2,1)S(1)}, u32[]{:S(2)}, u32[]{:S(2)}) collective-permute-start(bf16[192,512]{1,0:T(8,128)(2,1)S(1)} %get-tuple-element.119.own), channel_id=1, source_target_pairs={{0,1},{1,0},{2,3},{3,2},{4,5},{5,4},{6,7},{7,6},{8,9},{9,8},{10,11... | collective-permute-start | bytes 589832 | tf_op jit(solution)/shard_map/ppermute | solution.py:645
  7.9 10.4 %collective-permute-start.4 = (bf16[160,512]{1,0:T(8,128)(2,1)S(1)}, bf16[160,512]{1,0:T(8,128)(2,1)S(1)}, u32[]{:S(2)}, u32[]{:S(2)}) collective-permute-start(bf16[160,512]{1,0:T(8,128)(2,1)S(1)} %get-tuple-element.120), channel_id=1, source_target_pairs={{0,2},{1,3},{2,0},{3,1},{4,6},{5,7},{6,4},{7,5},{8,10},{9,11},{10,... | collective-permute-start | bytes 491528 | tf_op jit(solution)/shard_map/ppermute | solution.py:648
  8.0 10.3 %collective-permute-start.5 = (bf16[160,512]{1,0:T(8,128)(2,1)S(1)}, bf16[160,512]{1,0:T(8,128)(2,1)S(1)}, u32[]{:S(2)}, u32[]{:S(2)}) collective-permute-start(bf16[160,512]{1,0:T(8,128)(2,1)S(1)} %get-tuple-element.120), channel_id=1, source_target_pairs={{0,3},{1,2},{2,1},{3,0},{4,7},{5,6},{6,5},{7,4},{8,11},{9,10},{10,... | collective-permute-start | bytes 491528 | tf_op jit(solution)/shard_map/ppermute | solution.py:684
  9.5 1.6 %collective-permute-start.2 = (bf16[128,512]{1,0:T(8,128)(2,1)S(1)}, bf16[128,512]{1,0:T(8,128)(2,1)S(1)}, u32[]{:S(2)}, u32[]{:S(2)}) collective-permute-start(bf16[128,512]{1,0:T(8,128)(2,1)S(1)} %collective-permute-done.1.received), channel_id=1, source_target_pairs={{0,1},{1,0},{2,3},{3,2},{4,5},{5,4},{6,7},{7,6},{8,9},{9,8},{10,11... | collective-permute-start | bytes 393224 | tf_op jit(solution)/shard_map/ppermute | solution.py:645
  16.4 14.4 %collective-permute-start.6 = (bf16[2,256,512]{2,1,0:T(8,128)(2,1)S(1)}, bf16[2,256,512]{2,1,0:T(8,128)(2,1)S(1)}, u32[]{:S(2)}, u32[]{:S(2)}) collective-permute-start(bf16[2,256,512]{2,1,0:T(8,128)(2,1)S(1)} %get-tuple-element.123), channel_id=1, source_target_pairs={{0,2},{1,3},{2,0},{3,1},{4,6},{5,7},{6,4},{7,5},{8,10},{9,11},{10,... | collective-permute-start | bytes 1572872 | tf_op jit(solution)/shard_map/ppermute | solution.py:648
  28.0 7.2 %collective-permute-start.8 = (bf16[512,128]{1,0:T(8,128)(2,1)S(1)}, bf16[512,128]{1,0:T(8,128)(2,1)S(1)}, u32[]{:S(2)}, u32[]{:S(2)}) collective-permute-start(bf16[512,128]{1,0:T(8,128)(2,1)S(1)} %get-tuple-element.130), channel_id=1, source_target_pairs={{0,2},{1,3},{2,0},{3,1},{4,6},{5,7},{6,4},{7,5},{8,10},{9,11},{10,... | collective-permute-start | bytes 393224 | tf_op jit(solution)/shard_map/ppermute | solution.py:648
  28.3 13.8 %collective-permute-start.9 = (bf16[4,256,256]{2,1,0:T(8,128)(2,1)S(1)}, bf16[4,256,256]{2,1,0:T(8,128)(2,1)S(1)}, u32[]{:S(2)}, u32[]{:S(2)}) collective-permute-start(bf16[4,256,256]{2,1,0:T(8,128)(2,1)S(1)} %get-tuple-element.137), channel_id=1, source_target_pairs={{0,4},{4,0},{8,12},{12,8},{16,20},{20,16},{24,28},{28,24},{1,5},{5... | collective-permute-start | bytes 1572872 | tf_op jit(solution)/shard_map/ppermute | solution.py:651
  30.8 4.3 %collective-permute-start.7 = (bf16[2,256,512]{2,1,0:T(8,128)(2,1)S(1)}, bf16[2,256,512]{2,1,0:T(8,128)(2,1)S(1)}, u32[]{:S(2)}, u32[]{:S(2)}) collective-permute-start(bf16[2,256,512]{2,1,0:T(8,128)(2,1)S(1)} %collective-permute-done.6.half_t), channel_id=1, source_target_pairs={{0,1},{1,0},{2,3},{3,2},{4,5},{5,4},{6,7},{7,6},{8,9},{9,8},{10,11... | collective-permute-start | bytes 1572872 | tf_op jit(solution)/shard_map/ppermute | solution.py:645
  38.5 18.4 %collective-permute-start.14 = (bf16[4,576,128]{2,1,0:T(8,128)(2,1)S(1)}, bf16[4,576,128]{2,1,0:T(8,128)(2,1)S(1)}, u32[]{:S(2)}, u32[]{:S(2)}) collective-permute-start(bf16[4,576,128]{2,1,0:T(8,128)(2,1)S(1)} %get-tuple-element.135), channel_id=1, source_target_pairs={{0,4},{4,0},{8,12},{12,8},{16,20},{20,16},{24,28},{28,24},{1,5},{5... | collective-permute-start | bytes 1769480 | tf_op jit(solution)/shard_map/ppermute | solution.py:651
  40.3 6.4 %collective-permute-start.10 = (bf16[512,128]{1,0:T(8,128)(2,1)S(1)}, bf16[512,128]{1,0:T(8,128)(2,1)S(1)}, u32[]{:S(2)}, u32[]{:S(2)}) collective-permute-start(bf16[512,128]{1,0:T(8,128)(2,1)S(1)} %get-tuple-element.143), channel_id=1, source_target_pairs={{0,2},{1,3},{2,0},{3,1},{4,6},{5,7},{6,4},{7,5},{8,10},{9,11},{10,... | collective-permute-start | bytes 393224 | tf_op jit(solution)/shard_map/ppermute | solution.py:648
  42.2 13.6 %collective-permute-start.11 = (bf16[1,256,256]{2,1,0:T(8,128)(2,1)S(1)}, bf16[1,256,256]{2,1,0:T(8,128)(2,1)S(1)}, u32[]{:S(2)}, u32[]{:S(2)}) collective-permute-start(bf16[1,256,256]{2,1,0:T(8,128)(2,1)S(1)} %get-tuple-element.139), channel_id=1, source_target_pairs={{0,8},{4,12},{8,0},{12,4},{16,24},{20,28},{24,16},{28,20},{1,9},{5... | collective-permute-start | bytes 393224 | tf_op jit(solution)/shard_map/ppermute | solution.py:651
  43.8 12.9 %collective-permute-start.12 = (bf16[1,256,256]{2,1,0:T(8,128)(2,1)S(1)}, bf16[1,256,256]{2,1,0:T(8,128)(2,1)S(1)}, u32[]{:S(2)}, u32[]{:S(2)}) collective-permute-start(bf16[1,256,256]{2,1,0:T(8,128)(2,1)S(1)} %get-tuple-element.140), channel_id=1, source_target_pairs={{0,16},{4,20},{8,24},{12,28},{16,0},{20,4},{24,8},{28,12},{1,17},{... | collective-permute-start | bytes 393224 | tf_op jit(solution)/shard_map/ppermute | solution.py:651
  46.4 10.3 %collective-permute-start.13 = (bf16[1,256,256]{2,1,0:T(8,128)(2,1)S(1)}, bf16[1,256,256]{2,1,0:T(8,128)(2,1)S(1)}, u32[]{:S(2)}, u32[]{:S(2)}) collective-permute-start(bf16[1,256,256]{2,1,0:T(8,128)(2,1)S(1)} %get-tuple-element.141), channel_id=1, source_target_pairs={{0,24},{4,28},{8,16},{12,20},{16,8},{20,12},{24,0},{28,4},{1,25},{... | collective-permute-start | bytes 393224 | tf_op jit(solution)/shard_map/ppermute | solution.py:651
  49.7 17.6 %collective-permute-start.19 = (bf16[4,576,128]{2,1,0:T(8,128)(2,1)S(1)}, bf16[4,576,128]{2,1,0:T(8,128)(2,1)S(1)}, u32[]{:S(2)}, u32[]{:S(2)}) collective-permute-start(bf16[4,576,128]{2,1,0:T(8,128)(2,1)S(1)} %get-tuple-element.144), channel_id=1, source_target_pairs={{0,4},{4,0},{8,12},{12,8},{16,20},{20,16},{24,28},{28,24},{1,5},{5... | collective-permute-start | bytes 1769480 | tf_op jit(solution)/shard_map/ppermute | solution.py:651
  57.0 10.5 %collective-permute-start.15 = (bf16[1,576,128]{2,1,0:T(8,128)(2,1)S(1)}, bf16[1,576,128]{2,1,0:T(8,128)(2,1)S(1)}, u32[]{:S(2)}, u32[]{:S(2)}) collective-permute-start(bf16[1,576,128]{2,1,0:T(8,128)(2,1)S(1)} %get-tuple-element.155), channel_id=1, source_target_pairs={{0,8},{4,12},{8,0},{12,4},{16,24},{20,28},{24,16},{28,20},{1,9},{5... | collective-permute-start | bytes 442376 | tf_op jit(solution)/shard_map/ppermute | solution.py:651
  59.2 13.1 %collective-permute-start.16 = (bf16[1,576,128]{2,1,0:T(8,128)(2,1)S(1)}, bf16[1,576,128]{2,1,0:T(8,128)(2,1)S(1)}, u32[]{:S(2)}, u32[]{:S(2)}) collective-permute-start(bf16[1,576,128]{2,1,0:T(8,128)(2,1)S(1)} %get-tuple-element.156), channel_id=1, source_target_pairs={{0,16},{4,20},{8,24},{12,28},{16,0},{20,4},{24,8},{28,12},{1,17},{... | collective-permute-start | bytes 442376 | tf_op jit(solution)/shard_map/ppermute | solution.py:651
  60.3 12.0 %collective-permute-start.17 = (bf16[1,576,128]{2,1,0:T(8,128)(2,1)S(1)}, bf16[1,576,128]{2,1,0:T(8,128)(2,1)S(1)}, u32[]{:S(2)}, u32[]{:S(2)}) collective-permute-start(bf16[1,576,128]{2,1,0:T(8,128)(2,1)S(1)} %get-tuple-element.157), channel_id=1, source_target_pairs={{0,24},{4,28},{8,16},{12,20},{16,8},{20,12},{24,0},{28,4},{1,25},{... | collective-permute-start | bytes 442376 | tf_op jit(solution)/shard_map/ppermute | solution.py:651
  61.6 5.9 %collective-permute-start.18 = (bf16[4,16,128]{2,1,0:T(8,128)(2,1)S(1)}, bf16[4,16,128]{2,1,0:T(8,128)(2,1)S(1)}, u32[]{:S(2)}, u32[]{:S(2)}) collective-permute-start(bf16[4,16,128]{2,1,0:T(8,128)(2,1)S(1)} %get-tuple-element.158), channel_id=1, source_target_pairs={{0,4},{4,0},{8,12},{12,8},{16,20},{20,16},{24,28},{28,24},{1,5},{5... | collective-permute-start | bytes 49160 | tf_op jit(solution)/shard_map/ppermute | solution.py:651
  72.4 7.8 %collective-permute-start.24 = (bf16[576,128]{1,0:T(8,128)(2,1)S(1)}, bf16[576,128]{1,0:T(8,128)(2,1)S(1)}, u32[]{:S(2)}, u32[]{:S(2)}) collective-permute-start(bf16[576,128]{1,0:T(8,128)(2,1)S(1)} %sumrouteb.1.own_ref), channel_id=1, source_target_pairs={{0,2},{1,3},{2,0},{3,1},{4,6},{5,7},{6,4},{7,5},{8,10},{9,11},{10,... | collective-permute-start | bytes 442376 | tf_op jit(solution)/shard_map/ppermute | solution.py:648
  72.5 6.7 %collective-permute-start.25 = (bf16[256,256]{1,0:T(8,128)(2,1)S(1)}, bf16[256,256]{1,0:T(8,128)(2,1)S(1)}, u32[]{:S(2)}, u32[]{:S(2)}) collective-permute-start(bf16[256,256]{1,0:T(8,128)(2,1)S(1)} %sumroutea.1.own_ref), channel_id=1, source_target_pairs={{0,2},{1,3},{2,0},{3,1},{4,6},{5,7},{6,4},{7,5},{8,10},{9,11},{10,... | collective-permute-start | bytes 393224 | tf_op jit(solution)/shard_map/ppermute | solution.py:648
  74.5 6.5 %collective-permute-start.23 = (bf16[1,592,128]{2,1,0:T(8,128)(2,1)S(1)}, bf16[1,592,128]{2,1,0:T(8,128)(2,1)S(1)}, u32[]{:S(2)}, u32[]{:S(2)}) collective-permute-start(bf16[1,592,128]{2,1,0:T(8,128)(2,1)S(1)} %get-tuple-element.179), channel_id=1, source_target_pairs={{0,8},{4,12},{8,0},{12,4},{16,24},{20,28},{24,16},{28,20},{1,9},{5... | collective-permute-start | bytes 454664 | tf_op jit(solution)/shard_map/ppermute | solution.py:651
  76.6 12.8 %collective-permute-start.22 = (bf16[1,592,128]{2,1,0:T(8,128)(2,1)S(1)}, bf16[1,592,128]{2,1,0:T(8,128)(2,1)S(1)}, u32[]{:S(2)}, u32[]{:S(2)}) collective-permute-start(bf16[1,592,128]{2,1,0:T(8,128)(2,1)S(1)} %get-tuple-element.177), channel_id=1, source_target_pairs={{0,16},{4,20},{8,24},{12,28},{16,0},{20,4},{24,8},{28,12},{1,17},{... | collective-permute-start | bytes 454664 | tf_op jit(solution)/shard_map/ppermute | solution.py:651
  77.7 11.8 %collective-permute-start.21 = (bf16[1,592,128]{2,1,0:T(8,128)(2,1)S(1)}, bf16[1,592,128]{2,1,0:T(8,128)(2,1)S(1)}, u32[]{:S(2)}, u32[]{:S(2)}) collective-permute-start(bf16[1,592,128]{2,1,0:T(8,128)(2,1)S(1)} %get-tuple-element.175), channel_id=1, source_target_pairs={{0,24},{4,28},{8,16},{12,20},{16,8},{20,12},{24,0},{28,4},{1,25},{... | collective-permute-start | bytes 454664 | tf_op jit(solution)/shard_map/ppermute | solution.py:651
  79.1 11.3 %collective-permute-start.30 = (bf16[256,256]{1,0:T(8,128)(2,1)S(1)}, bf16[256,256]{1,0:T(8,128)(2,1)S(1)}, u32[]{:S(2)}, u32[]{:S(2)}) collective-permute-start(bf16[256,256]{1,0:T(8,128)(2,1)S(1)} %sumroutea.1.own_ref), channel_id=1, source_target_pairs={{0,1},{1,0},{2,3},{3,2},{4,5},{5,4},{6,7},{7,6},{8,9},{9,8},{10,11... | collective-permute-start | bytes 393224 | tf_op jit(solution)/shard_map/ppermute | solution.py:645
  80.2 12.7 %collective-permute-start.20 = (bf16[2,128,512]{2,1,0:T(8,128)(2,1)S(1)}, bf16[2,128,512]{2,1,0:T(8,128)(2,1)S(1)}, u32[]{:S(2)}, u32[]{:S(2)}) collective-permute-start(bf16[2,128,512]{2,1,0:T(8,128)(2,1)S(1)} %get-tuple-element.173), channel_id=1, source_target_pairs={{0,2},{1,3},{2,0},{3,1},{4,6},{5,7},{6,4},{7,5},{8,10},{9,11},{10,... | collective-permute-start | bytes 786440 | tf_op jit(solution)/shard_map/ppermute | solution.py:648
  89.5 6.1 %collective-permute-start.26 = (bf16[592,128]{1,0:T(8,128)(2,1)S(1)}, bf16[592,128]{1,0:T(8,128)(2,1)S(1)}, u32[]{:S(2)}, u32[]{:S(2)}) collective-permute-start(bf16[592,128]{1,0:T(8,128)(2,1)S(1)} %sumroutec.1.own_ref), channel_id=1, source_target_pairs={{0,2},{1,3},{2,0},{3,1},{4,6},{5,7},{6,4},{7,5},{8,10},{9,11},{10,... | collective-permute-start | bytes 454664 | tf_op jit(solution)/shard_map/ppermute | solution.py:648
  90.0 4.4 %collective-permute-start.28 = (bf16[576,128]{1,0:T(8,128)(2,1)S(1)}, bf16[576,128]{1,0:T(8,128)(2,1)S(1)}, u32[]{:S(2)}, u32[]{:S(2)}) collective-permute-start(bf16[576,128]{1,0:T(8,128)(2,1)S(1)} %sumrouteb.1.own_ref), channel_id=1, source_target_pairs={{0,1},{1,0},{2,3},{3,2},{4,5},{5,4},{6,7},{7,6},{8,9},{9,8},{10,11... | collective-permute-start | bytes 442376 | tf_op jit(solution)/shard_map/ppermute | solution.py:645
  90.0 4.4 %collective-permute-start.29 = (bf16[576,128]{1,0:T(8,128)(2,1)S(1)}, bf16[576,128]{1,0:T(8,128)(2,1)S(1)}, u32[]{:S(2)}, u32[]{:S(2)}) collective-permute-start(bf16[576,128]{1,0:T(8,128)(2,1)S(1)} %collective-permute-done.24.far_ref), channel_id=1, source_target_pairs={{0,1},{1,0},{2,3},{3,2},{4,5},{5,4},{6,7},{7,6},{8,9},{9,8},{10,11... | collective-permute-start | bytes 442376 | tf_op jit(solution)/shard_map/ppermute | solution.py:645
  90.5 1.3 %collective-permute-start.31 = (bf16[256,256]{1,0:T(8,128)(2,1)S(1)}, bf16[256,256]{1,0:T(8,128)(2,1)S(1)}, u32[]{:S(2)}, u32[]{:S(2)}) collective-permute-start(bf16[256,256]{1,0:T(8,128)(2,1)S(1)} %collective-permute-done.25.far_ref), channel_id=1, source_target_pairs={{0,1},{1,0},{2,3},{3,2},{4,5},{5,4},{6,7},{7,6},{8,9},{9,8},{10,11... | collective-permute-start | bytes 393224 | tf_op jit(solution)/shard_map/ppermute | solution.py:645
  91.8 4.1 %collective-permute-start.27 = (bf16[592,128]{1,0:T(8,128)(2,1)S(1)}, bf16[592,128]{1,0:T(8,128)(2,1)S(1)}, u32[]{:S(2)}, u32[]{:S(2)}) collective-permute-start(bf16[592,128]{1,0:T(8,128)(2,1)S(1)} %sumroutec.1.own_ref), channel_id=1, source_target_pairs={{0,1},{1,0},{2,3},{3,2},{4,5},{5,4},{6,7},{7,6},{8,9},{9,8},{10,11... | collective-permute-start | bytes 454664 | tf_op jit(solution)/shard_map/ppermute | solution.py:645
  95.6 1.4 %collective-permute-start.32 = (bf16[592,128]{1,0:T(8,128)(2,1)S(1)}, bf16[592,128]{1,0:T(8,128)(2,1)S(1)}, u32[]{:S(2)}, u32[]{:S(2)}) collective-permute-start(bf16[592,128]{1,0:T(8,128)(2,1)S(1)} %collective-permute-done.26.far_ref), channel_id=1, source_target_pairs={{0,1},{1,0},{2,3},{3,2},{4,5},{5,4},{6,7},{7,6},{8,9},{9,8},{10,11... | collective-permute-start | bytes 454664 | tf_op jit(solution)/shard_map/ppermute | solution.py:645

commit v12 on v7

--- a/solution.py
+++ b/solution.py
@@ -21,7 +21,7 @@
 HB = pl.BlockSpec(memory_space=pltpu.HBM)
 RATE = 1 << 30
 LENGTH = {
-    "pack": 10, "stack": 10, "first": 0.02, "second": 30, "third": 20, "fourth": 10, "weight2": 1, "weight1": 3, "routeb1": 20,
+    "pack": 10, "stack": 10, "first": 0.02, "second": 30, "third": 20, "fourth": 0.5, "weight2": 1, "weight1": 3, "routeb1": 20,
 }
 
 
@@ -646,6 +646,9 @@
     def after(v, *others):
         return lax.optimization_barrier((v,) + others)[0]
 
+    def together(got, *others):
+        return list(lax.optimization_barrier((*others, *got))[len(others) :])
+
     img16 = ((PIX, C), BF16)
     img32 = ((PIX, C), F32)
     rows8 = ((8, C), F32)
@@ -746,7 +749,7 @@
     parts_a, got_a = spread("routea", 1, after(attn_keep, send2), attn_got)
     keep1, send1 = weight_grad("weight1", act1_t, 0, after(block1, *parts_a), block1_away)
     got1 = to_batch(send1, 1)
-    shard_a = finish("routea", parts_a, [after(g, send1) for g in got_a])
+    shard_a = finish("routea", parts_a, together(got_a, send1))
     out_own, grad_own, image_send, vec_keep, vec_send = call(
         fourth_kernel, "fourth",
         [((192, C), BF16), ((192, C), BF16), ((2, 128, C), BF16),
@@ -759,11 +762,11 @@
     vec_got = to_batch(vec_send, 1)
     parts_b, got_b = spread("routeb", 1, after(keep2, vec_keep, shard_a), got2)
     parts_c, got_c = spread("routec", 1, keep1, got1, (vec_keep, vec_got), behind=got_b)
-    shard_b = finish("routeb", parts_b, [after(g, parts_c[0]) for g in got_b])
+    shard_b = finish("routeb", parts_b, together(got_b, parts_c[0]))
     gathered_a = gather(shard_a)
     gathered_b = gather(shard_b)
     shard_c = finish(
-        "routec", parts_c, [after(g, gathered_b[1], gathered_a[1]) for g in got_c]
+        "routec", parts_c, together(got_c, gathered_b[1], gathered_a[1])
     )
     small = call(
         join_attn_kernel, "joina", [((small_rows, C), F32)] * 4, [], 8,

time: 95.2 us -> 96 us (level)
  starting transfers between devices: 33 us -> 34.1 us
    ppermute x9, waiting for transfers between devices: 7.74 us -> 6.35 us  [to_chip(): return lax.ppermute(v, 'height', [(i, i ^ 2) for i in range(4)])]
    ppermute x13, waiting for transfers between devices: 11.4 us -> 12.6 us  [to_batch(): return lax.ppermute(v, 'batch', [(i, i ^ change) for i in range(batches)])]
  transfers between devices with their start and end apart: 33 -> 33, of which waited for: 10 -> 9; matrix products, arithmetic and copies ran while one was open for 0% -> 0% of each run, Pallas kernels for 37% -> 37%
where the time goes in v12:
time: 96 us; the launch traced here: 95.8 us
  Pallas kernels  38.6 us (40%)
  starting transfers between devices  34.1 us (36%)
  waiting for transfers between devices  20.9 us (22%)
  between operations  1.29 us (1%)
    pallas_call x19, Pallas kernels, call(): pl.pallas_call(kernel, name=name, out_shape=[jax.ShapeDtypeStruct(shape,...  38.6 us
    ppermute x13, starting transfers between devices, to_batch(): return lax.ppermute(v, 'batch', [(i, i ^ change) for i in range(batches)])  19.5 us
    ppermute x13, waiting for transfers between devices, to_batch(): return lax.ppermute(v, 'batch', [(i, i ^ change) for i in range(batches)])  12.6 us
    ppermute x9, starting transfers between devices, to_chip(): return lax.ppermute(v, 'height', [(i, i ^ 2) for i in range(4)])  10.5 us
    ppermute x9, waiting for transfers between devices, to_chip(): return lax.ppermute(v, 'height', [(i, i ^ 2) for i in range(4)])  6.35 us
    ppermute x10, starting transfers between devices, to_core(): return lax.ppermute(v, 'height', [(i, i ^ 1) for i in range(4)])  2.68 us
    ppermute x10, waiting for transfers between devices, to_core(): return lax.ppermute(v, 'height', [(i, i ^ 1) for i in range(4)])  2.01 us
  transfers between devices with their start and end apart: 33, of which 9 were waited for; matrix products, arithmetic and copies ran while one was open for 0% of the time, Pallas kernels for 37%

profile of v12, /device:TPU:0, one launch (start us, length us, event | category | flops | bytes accessed | tf_op | source)
XLA Modules:
  0.0 95.8 jit_solution(16803767792308848911)
XLA Ops:
  0.8 0.0 slice-start
  0.8 0.0 slice-start.2
  0.8 1.9 %pack.1 = (s32[2]{0:T(128)}, bf16[128,512]{1,0:T(8,128)(2,1)}, bf16[192,512]{1,0:T(8,128)(2,1)}) custom-call(s32[2]{0:T(128)} %bucket_hbm.1, bf16[2,6,32,512]{3,2,1,0:T(8,128)(2,1)} %x_hbm.1), custom_call_target="tpu_custom_call" | custom-call | flops 10737418240 | bytes 1024 | tf_op jit(solution)/shard_map/pack/pallas_call | solution.py:586
  2.7 3.0 %collective-permute-start.1 = (bf16[128,512]{1,0:T(8,128)(2,1)}, bf16[128,512]{1,0:T(8,128)(2,1)S(1)}, u32[]{:S(2)}, u32[]{:S(2)}) collective-permute-start(bf16[128,512]{1,0:T(8,128)(2,1)} %get-tuple-element.112), channel_id=1, source_target_pairs={{0,2},{1,3},{2,0},{3,1},{4,6},{5,7},{6,4},{7,5},{8,10},{9,11},{10,... | collective-permute-start | bytes 393224 | tf_op jit(solution)/shard_map/ppermute | solution.py:641
  5.8 0.0 collective-permute-start
  5.9 0.0 copy-start.2
  5.9 0.8 copy-done.2
  6.7 0.6 stack.1
  7.3 0.0 copy-start
  7.3 0.0 copy-start.4
  7.3 0.0 copy-start.5
  7.3 0.0 copy-start.6
  7.3 0.6 collective-permute-start.3
  7.9 0.1 collective-permute-start.4
  8.0 1.4 %collective-permute-start.5 = (bf16[160,512]{1,0:T(8,128)(2,1)S(1)}, bf16[160,512]{1,0:T(8,128)(2,1)S(1)}, u32[]{:S(2)}, u32[]{:S(2)}) collective-permute-start(bf16[160,512]{1,0:T(8,128)(2,1)S(1)} %get-tuple-element.118), channel_id=1, source_target_pairs={{0,3},{1,2},{2,1},{3,0},{4,7},{5,6},{6,5},{7,4},{8,11},{9,10},{10,... | collective-permute-start | bytes 491528 | tf_op jit(solution)/shard_map/ppermute | solution.py:677
  9.3 0.1 collective-permute-done.1.received
  9.5 0.6 collective-permute-start.2
  10.1 1.0 %collective-permute-done.2.partner_received = bf16[128,512]{1,0:T(8,128)(2,1)S(1)} collective-permute-done((bf16[128,512]{1,0:T(8,128)(2,1)S(1)}, bf16[128,512]{1,0:T(8,128)(2,1)S(1)}, u32[]{:S(2)}, u32[]{:S(2)}) %collective-permute-start.2) | collective-permute-done | bytes 131104 | tf_op jit(solution)/shard_map/ppermute | solution.py:638
  11.1 5.4 %first.1 = (bf16[512,512]{1,0:T(8,128)(2,1)S(1)}, f32[512,512]{1,0:T(8,128)S(1)}, bf16[512,512]{1,0:T(8,128)(2,1)S(1)}, f32[8,512]{1,0:T(8,128)S(1)}, bf16[512,5...) custom-call(s32[2]{0:T(128)S(1)} %copy-done.3, bf16[192,512]{1,0:T(8,128)(2,1)S(1)} %copy-done.1, ...), custom_call_target="tpu_custom_call" | custom-call | flops 21474836 | bytes 1024 | tf_op jit(solution)/shard_map/first/pallas_call | solution.py:586
  16.4 1.9 %collective-permute-start.6 = (bf16[2,256,512]{2,1,0:T(8,128)(2,1)S(1)}, bf16[2,256,512]{2,1,0:T(8,128)(2,1)S(1)}, u32[]{:S(2)}, u32[]{:S(2)}) collective-permute-start(bf16[2,256,512]{2,1,0:T(8,128)(2,1)S(1)} %get-tuple-element.124), channel_id=1, source_target_pairs={{0,2},{1,3},{2,0},{3,1},{4,6},{5,7},{6,4},{7,5},{8,10},{9,11},{10,... | collective-permute-start | bytes 1572872 | tf_op jit(solution)/shard_map/ppermute | solution.py:641
  18.4 9.6 %second.1 = (f32[512,512]{1,0:T(8,128)S(1)}, bf16[512,512]{1,0:T(8,128)(2,1)S(1)}, bf16[512,512]{1,0:T(8,128)(2,1)S(1)}, f32[512,512]{1,0:T(8,128)S(1)}, bf16[4,...) custom-call(s32[2]{0:T(128)S(1)} %copy-done.3, ...), custom_call_target="tpu_custom_call" | custom-call | flops 32212254720 | bytes 1024 | tf_op jit(solution)/shard_map/second/pallas_call | solution.py:586
  28.0 0.3 collective-permute-start.8
  28.3 1.5 %collective-permute-start.9 = (bf16[4,256,256]{2,1,0:T(8,128)(2,1)S(1)}, bf16[4,256,256]{2,1,0:T(8,128)(2,1)S(1)}, u32[]{:S(2)}, u32[]{:S(2)}) collective-permute-start(bf16[4,256,256]{2,1,0:T(8,128)(2,1)S(1)} %get-tuple-element.133), channel_id=1, source_target_pairs={{0,4},{4,0},{8,12},{12,8},{16,20},{20,16},{24,28},{28,24},{1,5},{5... | collective-permute-start | bytes 1572872 | tf_op jit(solution)/shard_map/ppermute | solution.py:644
  29.8 1.1 %collective-permute-done.6.half_t = bf16[2,256,512]{2,1,0:T(8,128)(2,1)S(1)} collective-permute-done((bf16[2,256,512]{2,1,0:T(8,128)(2,1)S(1)}, bf16[2,256,512]{2,1,0:T(8,128)(2,1)S(1)}, u32[]{:S(2)}, u32[]{:S(2)}) %collective-permute-start.6) | collective-permute-done | bytes 524320 | tf_op jit(solution)/shard_map/ppermute | solution.py:641
  30.8 4.3 %third.1 = (bf16[512,512]{1,0:T(8,128)(2,1)S(1)}, bf16[512,128]{1,0:T(8,128)(2,1)S(1)}, bf16[512,128]{1,0:T(8,128)(2,1)S(1)}, f32[8,512]{1,0:T(8,128)S(1)}) custom-call(s32[2]{0:T(128)S(1)} %copy-done.3, bf16[512,512]{1,0:T(8,128)(2,1)S(1)} %get-tuple-element.119.grad2_ref, f32[512,512]{1,0:T(8,128)S(1)} %get-tuple-element.120.conv_ref, ...), custom_call_target="tpu_custom_call" | custom-call | flops 21474836480 | bytes 1024 | tf_op jit(solution)/shard_map/third/pallas_call | solution.py:586
  35.2 3.3 %weight2.5 = (bf16[4,576,128]{2,1,0:T(8,128)(2,1)S(1)}, bf16[4,576,128]{2,1,0:T(8,128)(2,1)S(1)}) custom-call(s32[2]{0:T(128)S(1)} %copy-done.3, bf16[512,512]{1,0:T(8,128)(2,1)S(1)} %get-tuple-element.127.act_t, bf16[2,256,512]{2,1,0:T(8,128)(2,1)S(1)} %collective-permute-done.6.half_t, bf16[2,256,512]{2,1,0:T(8,128)(2,1)S(1)} %collective-permute-done.7.partner_half_t, ...), custom_call_target="tpu_custom_call" | custom-call | flops 1073741824 | bytes 1024 | tf_op jit(solution)/shard_map/weight2/pallas_call | solution.py:586
  38.5 1.8 %collective-permute-start.17 = (bf16[4,576,128]{2,1,0:T(8,128)(2,1)S(1)}, bf16[4,576,128]{2,1,0:T(8,128)(2,1)S(1)}, u32[]{:S(2)}, u32[]{:S(2)}) collective-permute-start(bf16[4,576,128]{2,1,0:T(8,128)(2,1)S(1)} %get-tuple-element.131), channel_id=1, source_target_pairs={{0,4},{4,0},{8,12},{12,8},{16,20},{20,16},{24,28},{28,24},{1,5},{5... | collective-permute-start | bytes 1769480 | tf_op jit(solution)/shard_map/ppermute | solution.py:644
  40.3 1.8 %collective-permute-start.10 = (bf16[512,128]{1,0:T(8,128)(2,1)S(1)}, bf16[512,128]{1,0:T(8,128)(2,1)S(1)}, u32[]{:S(2)}, u32[]{:S(2)}) collective-permute-start(bf16[512,128]{1,0:T(8,128)(2,1)S(1)} %get-tuple-element.139), channel_id=1, source_target_pairs={{0,2},{1,3},{2,0},{3,1},{4,6},{5,7},{6,4},{7,5},{8,10},{9,11},{10,... | collective-permute-start | bytes 393224 | tf_op jit(solution)/shard_map/ppermute | solution.py:641
  42.1 0.1 routea1.1
  42.2 1.6 %collective-permute-start.14 = (bf16[1,256,256]{2,1,0:T(8,128)(2,1)S(1)}, bf16[1,256,256]{2,1,0:T(8,128)(2,1)S(1)}, u32[]{:S(2)}, u32[]{:S(2)}) collective-permute-start(bf16[1,256,256]{2,1,0:T(8,128)(2,1)S(1)} %get-tuple-element.135), channel_id=1, source_target_pairs={{0,8},{4,12},{8,0},{12,4},{16,24},{20,28},{24,16},{28,20},{1,9},{5... | collective-permute-start | bytes 393224 | tf_op jit(solution)/shard_map/ppermute | solution.py:644
  43.8 2.6 %collective-permute-start.15 = (bf16[1,256,256]{2,1,0:T(8,128)(2,1)S(1)}, bf16[1,256,256]{2,1,0:T(8,128)(2,1)S(1)}, u32[]{:S(2)}, u32[]{:S(2)}) collective-permute-start(bf16[1,256,256]{2,1,0:T(8,128)(2,1)S(1)} %get-tuple-element.136), channel_id=1, source_target_pairs={{0,16},{4,20},{8,24},{12,28},{16,0},{20,4},{24,8},{28,12},{1,17},{... | collective-permute-start | bytes 393224 | tf_op jit(solution)/shard_map/ppermute | solution.py:644
  46.4 0.2 collective-permute-start.16
  46.7 3.1 %weight1.4 = (bf16[4,576,128]{2,1,0:T(8,128)(2,1)S(1)}, bf16[4,576,128]{2,1,0:T(8,128)(2,1)S(1)}) custom-call(s32[2]{0:T(128)S(1)} %copy-done.3, bf16[512,512]{1,0:T(8,128)(2,1)S(1)} %get-tuple-element.123.act_t, bf16[2,256,512]{2,1,0:T(8,128)(2,1)S(1)} %collective-permute-done.6.half_t, bf16[2,256,512]{2,1,0:T(8,128)(2,1)S(1)} %collective-permute-done.7.partner_half_t, ...), custom_call_target="tpu_custom_call" | custom-call | flops 3221225472 | bytes 1024 | tf_op jit(solution)/shard_map/weight1/pallas_call | solution.py:586
  49.7 1.4 %collective-permute-start.13 = (bf16[4,576,128]{2,1,0:T(8,128)(2,1)S(1)}, bf16[4,576,128]{2,1,0:T(8,128)(2,1)S(1)}, u32[]{:S(2)}, u32[]{:S(2)}) collective-permute-start(bf16[4,576,128]{2,1,0:T(8,128)(2,1)S(1)} %get-tuple-element.140), channel_id=1, source_target_pairs={{0,4},{4,0},{8,12},{12,8},{16,20},{20,16},{24,28},{28,24},{1,5},{5... | collective-permute-start | bytes 1769480 | tf_op jit(solution)/shard_map/ppermute | solution.py:644
  51.2 5.0 %fourth.1 = (bf16[192,512]{1,0:T(8,128)(2,1)S(1)}, bf16[192,512]{1,0:T(8,128)(2,1)S(1)}, bf16[2,128,512]{2,1,0:T(8,128)(2,1)S(1)}, bf16[4,16,128]{2,1,0:T(8,128)(2,1)S(1)}, bf16[4,16,128]{2,1,0:T(8,128)(2,1)S(1)}) custom-call(s32[2]{0:T(128)S(1)} %copy-done.3, bf16[512,512]{1,0:T(8,128)(2,1)S(1)} %get-tuple-element.141.grad1_ref, ...), custom_call_target="tpu_custom_call" | custom-call | flops 536870912 | bytes 1024 | tf_op jit(solution)/shard_map/fourth/pallas_call | solution.py:586
  56.2 0.6 collective-permute-done.15.refs_2_
  56.8 0.1 sumroutea.1.own_ref
  56.9 0.1 routeb1.1
  57.0 2.1 %collective-permute-start.18 = (bf16[1,576,128]{2,1,0:T(8,128)(2,1)S(1)}, bf16[1,576,128]{2,1,0:T(8,128)(2,1)S(1)}, u32[]{:S(2)}, u32[]{:S(2)}) collective-permute-start(bf16[1,576,128]{2,1,0:T(8,128)(2,1)S(1)} %get-tuple-element.164), channel_id=1, source_target_pairs={{0,8},{4,12},{8,0},{12,4},{16,24},{20,28},{24,16},{28,20},{1,9},{5... | collective-permute-start | bytes 442376 | tf_op jit(solution)/shard_map/ppermute | solution.py:644
  59.2 1.5 %collective-permute-start.19 = (bf16[1,576,128]{2,1,0:T(8,128)(2,1)S(1)}, bf16[1,576,128]{2,1,0:T(8,128)(2,1)S(1)}, u32[]{:S(2)}, u32[]{:S(2)}) collective-permute-start(bf16[1,576,128]{2,1,0:T(8,128)(2,1)S(1)} %get-tuple-element.165), channel_id=1, source_target_pairs={{0,16},{4,20},{8,24},{12,28},{16,0},{20,4},{24,8},{28,12},{1,17},{... | collective-permute-start | bytes 442376 | tf_op jit(solution)/shard_map/ppermute | solution.py:644
  60.7 0.9 collective-permute-start.20
  61.6 0.5 collective-permute-start.12
  62.1 5.4 %collective-permute-done.12.got_ref = bf16[4,16,128]{2,1,0:T(8,128)(2,1)S(1)} collective-permute-done((bf16[4,16,128]{2,1,0:T(8,128)(2,1)S(1)}, bf16[4,16,128]{2,1,0:T(8,128)(2,1)S(1)}, u32[]{:S(2)}, u32[]{:S(2)}) %collective-permute-start.12) | collective-permute-done | bytes 16416 | tf_op jit(solution)/shard_map/ppermute | solution.py:644
  67.5 2.0 %collective-permute-start.22 = (bf16[256,256]{1,0:T(8,128)(2,1)S(1)}, bf16[256,256]{1,0:T(8,128)(2,1)S(1)}, u32[]{:S(2)}, u32[]{:S(2)}) collective-permute-start(bf16[256,256]{1,0:T(8,128)(2,1)S(1)} %sumroutea.1.own_ref), channel_id=1, source_target_pairs={{0,2},{1,3},{2,0},{3,1},{4,6},{5,7},{6,4},{7,5},{8,10},{9,11},{10,... | collective-permute-start | bytes 393224 | tf_op jit(solution)/shard_map/ppermute | solution.py:641
  69.5 0.0 collective-permute-start.11
  69.6 0.1 routec1.1
  69.8 2.5 %collective-permute-done.19.refs_2_ = bf16[1,576,128]{2,1,0:T(8,128)(2,1)S(1)} collective-permute-done((bf16[1,576,128]{2,1,0:T(8,128)(2,1)S(1)}, bf16[1,576,128]{2,1,0:T(8,128)(2,1)S(1)}, u32[]{:S(2)}, u32[]{:S(2)}) %collective-permute-start.19) | collective-permute-done | bytes 147488 | tf_op jit(solution)/shard_map/ppermute | solution.py:644
  72.3 1.9 %collective-permute-start.25 = (bf16[1,592,128]{2,1,0:T(8,128)(2,1)S(1)}, bf16[1,592,128]{2,1,0:T(8,128)(2,1)S(1)}, u32[]{:S(2)}, u32[]{:S(2)}) collective-permute-start(bf16[1,592,128]{2,1,0:T(8,128)(2,1)S(1)} %get-tuple-element.175), channel_id=1, source_target_pairs={{0,24},{4,28},{8,16},{12,20},{16,8},{20,12},{24,0},{28,4},{1,25},{... | collective-permute-start | bytes 454664 | tf_op jit(solution)/shard_map/ppermute | solution.py:644
  74.3 3.3 %collective-permute-start.24 = (bf16[1,592,128]{2,1,0:T(8,128)(2,1)S(1)}, bf16[1,592,128]{2,1,0:T(8,128)(2,1)S(1)}, u32[]{:S(2)}, u32[]{:S(2)}) collective-permute-start(bf16[1,592,128]{2,1,0:T(8,128)(2,1)S(1)} %get-tuple-element.173), channel_id=1, source_target_pairs={{0,16},{4,20},{8,24},{12,28},{16,0},{20,4},{24,8},{28,12},{1,17},{... | collective-permute-start | bytes 454664 | tf_op jit(solution)/shard_map/ppermute | solution.py:644
  77.5 0.1 sumrouteb.1.own_ref
  77.6 0.1 collective-permute-start.21
  77.7 5.1 %collective-permute-done.21.far_ref = bf16[576,128]{1,0:T(8,128)(2,1)S(1)} collective-permute-done((bf16[576,128]{1,0:T(8,128)(2,1)S(1)}, bf16[576,128]{1,0:T(8,128)(2,1)S(1)}, u32[]{:S(2)}, u32[]{:S(2)}) %collective-permute-start.21) | collective-permute-done | bytes 147488 | tf_op jit(solution)/shard_map/ppermute | solution.py:641
  82.8 4.0 %collective-permute-done.24.refs_2_ = bf16[1,592,128]{2,1,0:T(8,128)(2,1)S(1)} collective-permute-done((bf16[1,592,128]{2,1,0:T(8,128)(2,1)S(1)}, bf16[1,592,128]{2,1,0:T(8,128)(2,1)S(1)}, u32[]{:S(2)}, u32[]{:S(2)}) %collective-permute-start.24) | collective-permute-done | bytes 151584 | tf_op jit(solution)/shard_map/ppermute | solution.py:644
  86.9 0.1 sumroutec.1.own_ref
  87.0 1.3 %collective-permute-start.26 = (bf16[592,128]{1,0:T(8,128)(2,1)S(1)}, bf16[592,128]{1,0:T(8,128)(2,1)S(1)}, u32[]{:S(2)}, u32[]{:S(2)}) collective-permute-start(bf16[592,128]{1,0:T(8,128)(2,1)S(1)} %sumroutec.1.own_ref), channel_id=1, source_target_pairs={{0,2},{1,3},{2,0},{3,1},{4,6},{5,7},{6,4},{7,5},{8,10},{9,11},{10,... | collective-permute-start | bytes 454664 | tf_op jit(solution)/shard_map/ppermute | solution.py:641
  88.3 0.5 collective-permute-start.29
  88.8 0.5 collective-permute-start.31
  89.3 1.5 %unpack.1 = (bf16[2,6,32,512]{3,2,1,0:T(8,128)(2,1)}, bf16[2,6,32,512]{3,2,1,0:T(8,128)(2,1)}) custom-call(s32[2]{0:T(128)S(1)} %copy-done.3, bf16[192,512]{1,0:T(8,128)(2,1)S(1)} %get-tuple-element.147.out_own, bf16[192,512]{1,0:T(8,128)(2,1)S(1)} %get-tuple-element.148.grad_own, bf16[2,128,512]{2,1,0:T(8,128)(2,1)S(1)} %collective-permute-done.11.away_ref), custom_call_target="tpu_custom_call" | custom-call | flops 21474836 | bytes 1024 | tf_op jit(solution)/shard_map/unpack/pallas_call | solution.py:586
  90.8 0.0 collective-permute-start.27
  90.8 0.9 joina.1
  91.7 1.2 %joinb.1 = f32[576,512]{1,0:T(8,128)} custom-call(bf16[576,128]{1,0:T(8,128)(2,1)S(1)} %sumrouteb.1.own_ref, bf16[576,128]{1,0:T(8,128)(2,1)S(1)} %collective-permute-done.21.far_ref, bf16[576,128]{1,0:T(8,128)(2,1)S(1)} %collective-permute-done.28.near_ref, bf16[576,128]{1,0:T(8,128)(2,1)S(1)} %collective-permute-done.29.diagonal_ref), custom_call_target="tpu_custom_call" | custom-call | flops 21474836 | bytes 1024 | tf_op jit(solution)/shard_map/joinb/pallas_call | solution.py:586
  92.9 0.5 collective-permute-start.32
  93.4 1.0 %collective-permute-done.32.diagonal_ref = bf16[592,128]{1,0:T(8,128)(2,1)S(1)} collective-permute-done((bf16[592,128]{1,0:T(8,128)(2,1)S(1)}, bf16[592,128]{1,0:T(8,128)(2,1)S(1)}, u32[]{:S(2)}, u32[]{:S(2)}) %collective-permute-start.32) | collective-permute-done | bytes 151584 | tf_op jit(solution)/shard_map/ppermute | solution.py:638
  94.4 1.2 %joinc.1 = (f32[576,512]{1,0:T(8,128)}, f32[1,64]{1,0:T(1,128)}, f32[1,64]{1,0:T(1,128)}, f32[1,64]{1,0:T(1,128)}, f32[1,64]{1,0:T(1,128)}, /*index=5*/f32[1,64]...) custom-call(bf16[592,128]{1,0:T(8,128)(2,1)S(1)} %sumroutec.1.own_re, ...), custom_call_target="tpu_custom_call" | custom-call | flops 21474836 | bytes 1024 | tf_op jit(solution)/shard_map/joinc/pallas_call | solution.py:586
  (69 shorter events, 0.2 us)
Async XLA Ops:
  0.7 5.1 %copy-start.8 = (f32[512]{0:T(512)S(1)}, f32[512]{0:T(512)}, u32[]{:S(2)}) copy-start(f32[512]{0:T(512)} %param.22) | copy-start | bytes 6148
  0.7 5.1 %copy-start.9 = (f32[512]{0:T(512)S(1)}, f32[512]{0:T(512)}, u32[]{:S(2)}) copy-start(f32[512]{0:T(512)} %param.23) | copy-start | bytes 6148
  0.7 5.1 %copy-start.18 = (f32[512]{0:T(512)S(1)}, f32[512]{0:T(512)}, u32[]{:S(2)}) copy-start(f32[512]{0:T(512)} %param.38) | copy-start | bytes 6148
  0.7 5.1 %copy-start.10 = (f32[512]{0:T(512)S(1)}, f32[512]{0:T(512)}, u32[]{:S(2)}) copy-start(f32[512]{0:T(512)} %param.25) | copy-start | bytes 6148
  0.7 5.1 %copy-start.11 = (f32[512]{0:T(512)S(1)}, f32[512]{0:T(512)}, u32[]{:S(2)}) copy-start(f32[512]{0:T(512)} %param.26) | copy-start | bytes 6148
  0.7 5.1 %copy-start.12 = (f32[512]{0:T(512)S(1)}, f32[512]{0:T(512)}, u32[]{:S(2)}) copy-start(f32[512]{0:T(512)} %param.27) | copy-start | bytes 6148
  0.7 5.1 %copy-start.13 = (f32[512]{0:T(512)S(1)}, f32[512]{0:T(512)}, u32[]{:S(2)}) copy-start(f32[512]{0:T(512)} %param.29) | copy-start | bytes 6148
  0.7 5.1 %copy-start.14 = (f32[512]{0:T(512)S(1)}, f32[512]{0:T(512)}, u32[]{:S(2)}) copy-start(f32[512]{0:T(512)} %param.30) | copy-start | bytes 6148
  0.7 5.1 %copy-start.15 = (f32[512]{0:T(512)S(1)}, f32[512]{0:T(512)}, u32[]{:S(2)}) copy-start(f32[512]{0:T(512)} %param.31) | copy-start | bytes 6148
  0.8 5.1 %copy-start.16 = (f32[512]{0:T(512)S(1)}, f32[512]{0:T(512)}, u32[]{:S(2)}) copy-start(f32[512]{0:T(512)} %param.33) | copy-start | bytes 6148
  0.8 5.1 %copy-start.17 = (f32[512]{0:T(512)S(1)}, f32[512]{0:T(512)}, u32[]{:S(2)}) copy-start(f32[512]{0:T(512)} %param.36) | copy-start | bytes 6148
  0.8 5.1 %copy-start.7 = (bf16[2,6,32,512]{3,2,1,0:T(8,128)(2,1)S(1)}, bf16[2,6,32,512]{3,2,1,0:T(8,128)(2,1)}, u32[]{:S(2)}) copy-start(bf16[2,6,32,512]{3,2,1,0:T(8,128)(2,1)} %cot_ref.1) | copy-start | bytes 1179652
  0.8 10.3 %slice-start = ((s8[4718592]{0:T(1024)(128)(4,1)}), s8[524288]{0:T(1024)(128)(4,1)S(1)}, s32[]{:S(2)}) async-start(s8[4718592]{0:T(1024)(128)(4,1)} %bitcast.22), calls=%async_computation | async-start | bytes 1048576
  0.8 17.5 %slice-start.2 = ((s8[4718592]{0:T(1024)(128)(4,1)}), s8[4194304]{0:T(1024)(128)(4,1)S(1)}, s32[]{:S(2)}) async-start(s8[4718592]{0:T(1024)(128)(4,1)} %bitcast.24), calls=%async_computation.2 | async-start | bytes 8388608
  2.7 6.7 %collective-permute-start.1 = (bf16[128,512]{1,0:T(8,128)(2,1)}, bf16[128,512]{1,0:T(8,128)(2,1)S(1)}, u32[]{:S(2)}, u32[]{:S(2)}) collective-permute-start(bf16[128,512]{1,0:T(8,128)(2,1)} %get-tuple-element.112), channel_id=1, source_target_pairs={{0,2},{1,3},{2,0},{3,1},{4,6},{5,7},{6,4},{7,5},{8,10},{9,11},{10,... | collective-permute-start | bytes 393224 | tf_op jit(solution)/shard_map/ppermute | solution.py:641
  5.8 4.3 %collective-permute-start = (bf16[192,512]{1,0:T(8,128)(2,1)}, bf16[192,512]{1,0:T(8,128)(2,1)S(1)}, u32[]{:S(2)}, u32[]{:S(2)}) collective-permute-start(bf16[192,512]{1,0:T(8,128)(2,1)} %get-tuple-element.111.own), channel_id=1, source_target_pairs={{0,1},{1,0},{2,3},{3,2},{4,5},{5,4},{6,7},{7,6},{8,9},{9,8},{10,11... | collective-permute-start | bytes 589832 | tf_op jit(solution)/shard_map/ppermute | solution.py:638
  5.8 5.3 %slice-start.1 = ((s8[4718592]{0:T(1024)(128)(4,1)}), s8[4194304]{0:T(1024)(128)(4,1)S(1)}, s32[]{:S(2)}) async-start(s8[4718592]{0:T(1024)(128)(4,1)} %bitcast.22), calls=%async_computation.1 | async-start | bytes 8388608
  5.9 0.8 copy-start.2
  6.7 4.4 %copy-start.1 = (bf16[192,512]{1,0:T(8,128)(2,1)S(1)}, bf16[192,512]{1,0:T(8,128)(2,1)}, u32[]{:S(2)}) copy-start(bf16[192,512]{1,0:T(8,128)(2,1)} %get-tuple-element.111.own) | copy-start | bytes 589828
  6.7 4.4 %copy-start.3 = (s32[2]{0:T(128)S(1)}, s32[2]{0:T(128)}, u32[]{:S(2)}) copy-start(s32[2]{0:T(128)} %get-tuple-element.110.kinds.bucket_ref) | copy-start | bytes 28
  6.7 11.6 %slice-start.3 = ((s8[4718592]{0:T(1024)(128)(4,1)}), s8[524288]{0:T(1024)(128)(4,1)S(1)}, s32[]{:S(2)}) async-start(s8[4718592]{0:T(1024)(128)(4,1)} %bitcast.24), calls=%async_computation.3 | async-start | bytes 1048576
  7.3 11.1 %copy-start = (bf16[512,512]{1,0:T(8,128)(2,1)S(1)}, bf16[512,512]{1,0:T(8,128)(2,1)}, u32[]{:S(2)}) copy-start(bf16[512,512]{1,0:T(8,128)(2,1)} %wp.3) | copy-start | bytes 1572868
  7.3 11.1 %copy-start.4 = (bf16[512,512]{1,0:T(8,128)(2,1)S(1)}, bf16[512,512]{1,0:T(8,128)(2,1)}, u32[]{:S(2)}) copy-start(bf16[512,512]{1,0:T(8,128)(2,1)} %wq.1) | copy-start | bytes 1572868
  7.3 11.0 %copy-start.5 = (bf16[512,512]{1,0:T(8,128)(2,1)S(1)}, bf16[512,512]{1,0:T(8,128)(2,1)}, u32[]{:S(2)}) copy-start(bf16[512,512]{1,0:T(8,128)(2,1)} %wk.1) | copy-start | bytes 1572868
  7.3 11.0 %copy-start.6 = (bf16[512,512]{1,0:T(8,128)(2,1)S(1)}, bf16[512,512]{1,0:T(8,128)(2,1)}, u32[]{:S(2)}) copy-start(bf16[512,512]{1,0:T(8,128)(2,1)} %wv.1) | copy-start | bytes 1572868
  7.3 11.0 %collective-permute-start.3 = (bf16[192,512]{1,0:T(8,128)(2,1)S(1)}, bf16[192,512]{1,0:T(8,128)(2,1)S(1)}, u32[]{:S(2)}, u32[]{:S(2)}) collective-permute-start(bf16[192,512]{1,0:T(8,128)(2,1)S(1)} %get-tuple-element.117.own), channel_id=1, source_target_pairs={{0,1},{1,0},{2,3},{3,2},{4,5},{5,4},{6,7},{7,6},{8,9},{9,8},{10,11... | collective-permute-start | bytes 589832 | tf_op jit(solution)/shard_map/ppermute | solution.py:638
  7.9 10.4 %collective-permute-start.4 = (bf16[160,512]{1,0:T(8,128)(2,1)S(1)}, bf16[160,512]{1,0:T(8,128)(2,1)S(1)}, u32[]{:S(2)}, u32[]{:S(2)}) collective-permute-start(bf16[160,512]{1,0:T(8,128)(2,1)S(1)} %get-tuple-element.118), channel_id=1, source_target_pairs={{0,2},{1,3},{2,0},{3,1},{4,6},{5,7},{6,4},{7,5},{8,10},{9,11},{10,... | collective-permute-start | bytes 491528 | tf_op jit(solution)/shard_map/ppermute | solution.py:641
  8.0 10.3 %collective-permute-start.5 = (bf16[160,512]{1,0:T(8,128)(2,1)S(1)}, bf16[160,512]{1,0:T(8,128)(2,1)S(1)}, u32[]{:S(2)}, u32[]{:S(2)}) collective-permute-start(bf16[160,512]{1,0:T(8,128)(2,1)S(1)} %get-tuple-element.118), channel_id=1, source_target_pairs={{0,3},{1,2},{2,1},{3,0},{4,7},{5,6},{6,5},{7,4},{8,11},{9,10},{10,... | collective-permute-start | bytes 491528 | tf_op jit(solution)/shard_map/ppermute | solution.py:677
  9.5 1.6 %collective-permute-start.2 = (bf16[128,512]{1,0:T(8,128)(2,1)S(1)}, bf16[128,512]{1,0:T(8,128)(2,1)S(1)}, u32[]{:S(2)}, u32[]{:S(2)}) collective-permute-start(bf16[128,512]{1,0:T(8,128)(2,1)S(1)} %collective-permute-done.1.received), channel_id=1, source_target_pairs={{0,1},{1,0},{2,3},{3,2},{4,5},{5,4},{6,7},{7,6},{8,9},{9,8},{10,11... | collective-permute-start | bytes 393224 | tf_op jit(solution)/shard_map/ppermute | solution.py:638
  16.4 14.4 %collective-permute-start.6 = (bf16[2,256,512]{2,1,0:T(8,128)(2,1)S(1)}, bf16[2,256,512]{2,1,0:T(8,128)(2,1)S(1)}, u32[]{:S(2)}, u32[]{:S(2)}) collective-permute-start(bf16[2,256,512]{2,1,0:T(8,128)(2,1)S(1)} %get-tuple-element.124), channel_id=1, source_target_pairs={{0,2},{1,3},{2,0},{3,1},{4,6},{5,7},{6,4},{7,5},{8,10},{9,11},{10,... | collective-permute-start | bytes 1572872 | tf_op jit(solution)/shard_map/ppermute | solution.py:641
  28.0 7.2 %collective-permute-start.8 = (bf16[512,128]{1,0:T(8,128)(2,1)S(1)}, bf16[512,128]{1,0:T(8,128)(2,1)S(1)}, u32[]{:S(2)}, u32[]{:S(2)}) collective-permute-start(bf16[512,128]{1,0:T(8,128)(2,1)S(1)} %get-tuple-element.130), channel_id=1, source_target_pairs={{0,2},{1,3},{2,0},{3,1},{4,6},{5,7},{6,4},{7,5},{8,10},{9,11},{10,... | collective-permute-start | bytes 393224 | tf_op jit(solution)/shard_map/ppermute | solution.py:641
  28.3 13.8 %collective-permute-start.9 = (bf16[4,256,256]{2,1,0:T(8,128)(2,1)S(1)}, bf16[4,256,256]{2,1,0:T(8,128)(2,1)S(1)}, u32[]{:S(2)}, u32[]{:S(2)}) collective-permute-start(bf16[4,256,256]{2,1,0:T(8,128)(2,1)S(1)} %get-tuple-element.133), channel_id=1, source_target_pairs={{0,4},{4,0},{8,12},{12,8},{16,20},{20,16},{24,28},{28,24},{1,5},{5... | collective-permute-start | bytes 1572872 | tf_op jit(solution)/shard_map/ppermute | solution.py:644
  30.8 4.3 %collective-permute-start.7 = (bf16[2,256,512]{2,1,0:T(8,128)(2,1)S(1)}, bf16[2,256,512]{2,1,0:T(8,128)(2,1)S(1)}, u32[]{:S(2)}, u32[]{:S(2)}) collective-permute-start(bf16[2,256,512]{2,1,0:T(8,128)(2,1)S(1)} %collective-permute-done.6.half_t), channel_id=1, source_target_pairs={{0,1},{1,0},{2,3},{3,2},{4,5},{5,4},{6,7},{7,6},{8,9},{9,8},{10,11... | collective-permute-start | bytes 1572872 | tf_op jit(solution)/shard_map/ppermute | solution.py:638
  38.5 18.3 %collective-permute-start.17 = (bf16[4,576,128]{2,1,0:T(8,128)(2,1)S(1)}, bf16[4,576,128]{2,1,0:T(8,128)(2,1)S(1)}, u32[]{:S(2)}, u32[]{:S(2)}) collective-permute-start(bf16[4,576,128]{2,1,0:T(8,128)(2,1)S(1)} %get-tuple-element.131), channel_id=1, source_target_pairs={{0,4},{4,0},{8,12},{12,8},{16,20},{20,16},{24,28},{28,24},{1,5},{5... | collective-permute-start | bytes 1769480 | tf_op jit(solution)/shard_map/ppermute | solution.py:644
  40.3 6.4 %collective-permute-start.10 = (bf16[512,128]{1,0:T(8,128)(2,1)S(1)}, bf16[512,128]{1,0:T(8,128)(2,1)S(1)}, u32[]{:S(2)}, u32[]{:S(2)}) collective-permute-start(bf16[512,128]{1,0:T(8,128)(2,1)S(1)} %get-tuple-element.139), channel_id=1, source_target_pairs={{0,2},{1,3},{2,0},{3,1},{4,6},{5,7},{6,4},{7,5},{8,10},{9,11},{10,... | collective-permute-start | bytes 393224 | tf_op jit(solution)/shard_map/ppermute | solution.py:641
  42.2 14.0 %collective-permute-start.14 = (bf16[1,256,256]{2,1,0:T(8,128)(2,1)S(1)}, bf16[1,256,256]{2,1,0:T(8,128)(2,1)S(1)}, u32[]{:S(2)}, u32[]{:S(2)}) collective-permute-start(bf16[1,256,256]{2,1,0:T(8,128)(2,1)S(1)} %get-tuple-element.135), channel_id=1, source_target_pairs={{0,8},{4,12},{8,0},{12,4},{16,24},{20,28},{24,16},{28,20},{1,9},{5... | collective-permute-start | bytes 393224 | tf_op jit(solution)/shard_map/ppermute | solution.py:644
  43.8 12.9 %collective-permute-start.15 = (bf16[1,256,256]{2,1,0:T(8,128)(2,1)S(1)}, bf16[1,256,256]{2,1,0:T(8,128)(2,1)S(1)}, u32[]{:S(2)}, u32[]{:S(2)}) collective-permute-start(bf16[1,256,256]{2,1,0:T(8,128)(2,1)S(1)} %get-tuple-element.136), channel_id=1, source_target_pairs={{0,16},{4,20},{8,24},{12,28},{16,0},{20,4},{24,8},{28,12},{1,17},{... | collective-permute-start | bytes 393224 | tf_op jit(solution)/shard_map/ppermute | solution.py:644
  46.4 10.3 %collective-permute-start.16 = (bf16[1,256,256]{2,1,0:T(8,128)(2,1)S(1)}, bf16[1,256,256]{2,1,0:T(8,128)(2,1)S(1)}, u32[]{:S(2)}, u32[]{:S(2)}) collective-permute-start(bf16[1,256,256]{2,1,0:T(8,128)(2,1)S(1)} %get-tuple-element.137), channel_id=1, source_target_pairs={{0,24},{4,28},{8,16},{12,20},{16,8},{20,12},{24,0},{28,4},{1,25},{... | collective-permute-start | bytes 393224 | tf_op jit(solution)/shard_map/ppermute | solution.py:644
  49.7 19.8 %collective-permute-start.13 = (bf16[4,576,128]{2,1,0:T(8,128)(2,1)S(1)}, bf16[4,576,128]{2,1,0:T(8,128)(2,1)S(1)}, u32[]{:S(2)}, u32[]{:S(2)}) collective-permute-start(bf16[4,576,128]{2,1,0:T(8,128)(2,1)S(1)} %get-tuple-element.140), channel_id=1, source_target_pairs={{0,4},{4,0},{8,12},{12,8},{16,20},{20,16},{24,28},{28,24},{1,5},{5... | collective-permute-start | bytes 1769480 | tf_op jit(solution)/shard_map/ppermute | solution.py:644
  57.0 12.7 %collective-permute-start.18 = (bf16[1,576,128]{2,1,0:T(8,128)(2,1)S(1)}, bf16[1,576,128]{2,1,0:T(8,128)(2,1)S(1)}, u32[]{:S(2)}, u32[]{:S(2)}) collective-permute-start(bf16[1,576,128]{2,1,0:T(8,128)(2,1)S(1)} %get-tuple-element.164), channel_id=1, source_target_pairs={{0,8},{4,12},{8,0},{12,4},{16,24},{20,28},{24,16},{28,20},{1,9},{5... | collective-permute-start | bytes 442376 | tf_op jit(solution)/shard_map/ppermute | solution.py:644
  59.2 13.1 %collective-permute-start.19 = (bf16[1,576,128]{2,1,0:T(8,128)(2,1)S(1)}, bf16[1,576,128]{2,1,0:T(8,128)(2,1)S(1)}, u32[]{:S(2)}, u32[]{:S(2)}) collective-permute-start(bf16[1,576,128]{2,1,0:T(8,128)(2,1)S(1)} %get-tuple-element.165), channel_id=1, source_target_pairs={{0,16},{4,20},{8,24},{12,28},{16,0},{20,4},{24,8},{28,12},{1,17},{... | collective-permute-start | bytes 442376 | tf_op jit(solution)/shard_map/ppermute | solution.py:644
  60.7 11.6 %collective-permute-start.20 = (bf16[1,576,128]{2,1,0:T(8,128)(2,1)S(1)}, bf16[1,576,128]{2,1,0:T(8,128)(2,1)S(1)}, u32[]{:S(2)}, u32[]{:S(2)}) collective-permute-start(bf16[1,576,128]{2,1,0:T(8,128)(2,1)S(1)} %get-tuple-element.166), channel_id=1, source_target_pairs={{0,24},{4,28},{8,16},{12,20},{16,8},{20,12},{24,0},{28,4},{1,25},{... | collective-permute-start | bytes 442376 | tf_op jit(solution)/shard_map/ppermute | solution.py:644
  61.6 5.9 %collective-permute-start.12 = (bf16[4,16,128]{2,1,0:T(8,128)(2,1)S(1)}, bf16[4,16,128]{2,1,0:T(8,128)(2,1)S(1)}, u32[]{:S(2)}, u32[]{:S(2)}) collective-permute-start(bf16[4,16,128]{2,1,0:T(8,128)(2,1)S(1)} %get-tuple-element.151), channel_id=1, source_target_pairs={{0,4},{4,0},{8,12},{12,8},{16,20},{20,16},{24,28},{28,24},{1,5},{5... | collective-permute-start | bytes 49160 | tf_op jit(solution)/shard_map/ppermute | solution.py:644
  67.5 10.1 %collective-permute-start.22 = (bf16[256,256]{1,0:T(8,128)(2,1)S(1)}, bf16[256,256]{1,0:T(8,128)(2,1)S(1)}, u32[]{:S(2)}, u32[]{:S(2)}) collective-permute-start(bf16[256,256]{1,0:T(8,128)(2,1)S(1)} %sumroutea.1.own_ref), channel_id=1, source_target_pairs={{0,2},{1,3},{2,0},{3,1},{4,6},{5,7},{6,4},{7,5},{8,10},{9,11},{10,... | collective-permute-start | bytes 393224 | tf_op jit(solution)/shard_map/ppermute | solution.py:641
  69.5 19.3 %collective-permute-start.11 = (bf16[2,128,512]{2,1,0:T(8,128)(2,1)S(1)}, bf16[2,128,512]{2,1,0:T(8,128)(2,1)S(1)}, u32[]{:S(2)}, u32[]{:S(2)}) collective-permute-start(bf16[2,128,512]{2,1,0:T(8,128)(2,1)S(1)} %get-tuple-element.149), channel_id=1, source_target_pairs={{0,2},{1,3},{2,0},{3,1},{4,6},{5,7},{6,4},{7,5},{8,10},{9,11},{10,... | collective-permute-start | bytes 786440 | tf_op jit(solution)/shard_map/ppermute | solution.py:641
  72.3 10.5 %collective-permute-start.25 = (bf16[1,592,128]{2,1,0:T(8,128)(2,1)S(1)}, bf16[1,592,128]{2,1,0:T(8,128)(2,1)S(1)}, u32[]{:S(2)}, u32[]{:S(2)}) collective-permute-start(bf16[1,592,128]{2,1,0:T(8,128)(2,1)S(1)} %get-tuple-element.175), channel_id=1, source_target_pairs={{0,24},{4,28},{8,16},{12,20},{16,8},{20,12},{24,0},{28,4},{1,25},{... | collective-permute-start | bytes 454664 | tf_op jit(solution)/shard_map/ppermute | solution.py:644
  74.3 12.6 %collective-permute-start.24 = (bf16[1,592,128]{2,1,0:T(8,128)(2,1)S(1)}, bf16[1,592,128]{2,1,0:T(8,128)(2,1)S(1)}, u32[]{:S(2)}, u32[]{:S(2)}) collective-permute-start(bf16[1,592,128]{2,1,0:T(8,128)(2,1)S(1)} %get-tuple-element.173), channel_id=1, source_target_pairs={{0,16},{4,20},{8,24},{12,28},{16,0},{20,4},{24,8},{28,12},{1,17},{... | collective-permute-start | bytes 454664 | tf_op jit(solution)/shard_map/ppermute | solution.py:644
  77.5 9.3 %collective-permute-start.23 = (bf16[1,592,128]{2,1,0:T(8,128)(2,1)S(1)}, bf16[1,592,128]{2,1,0:T(8,128)(2,1)S(1)}, u32[]{:S(2)}, u32[]{:S(2)}) collective-permute-start(bf16[1,592,128]{2,1,0:T(8,128)(2,1)S(1)} %get-tuple-element.171), channel_id=1, source_target_pairs={{0,8},{4,12},{8,0},{12,4},{16,24},{20,28},{24,16},{28,20},{1,9},{5... | collective-permute-start | bytes 454664 | tf_op jit(solution)/shard_map/ppermute | solution.py:644
  77.6 5.2 %collective-permute-start.21 = (bf16[576,128]{1,0:T(8,128)(2,1)S(1)}, bf16[576,128]{1,0:T(8,128)(2,1)S(1)}, u32[]{:S(2)}, u32[]{:S(2)}) collective-permute-start(bf16[576,128]{1,0:T(8,128)(2,1)S(1)} %sumrouteb.1.own_ref), channel_id=1, source_target_pairs={{0,2},{1,3},{2,0},{3,1},{4,6},{5,7},{6,4},{7,5},{8,10},{9,11},{10,... | collective-permute-start | bytes 442376 | tf_op jit(solution)/shard_map/ppermute | solution.py:641
  87.0 5.9 %collective-permute-start.26 = (bf16[592,128]{1,0:T(8,128)(2,1)S(1)}, bf16[592,128]{1,0:T(8,128)(2,1)S(1)}, u32[]{:S(2)}, u32[]{:S(2)}) collective-permute-start(bf16[592,128]{1,0:T(8,128)(2,1)S(1)} %sumroutec.1.own_ref), channel_id=1, source_target_pairs={{0,2},{1,3},{2,0},{3,1},{4,6},{5,7},{6,4},{7,5},{8,10},{9,11},{10,... | collective-permute-start | bytes 454664 | tf_op jit(solution)/shard_map/ppermute | solution.py:641
  88.3 3.4 %collective-permute-start.28 = (bf16[576,128]{1,0:T(8,128)(2,1)S(1)}, bf16[576,128]{1,0:T(8,128)(2,1)S(1)}, u32[]{:S(2)}, u32[]{:S(2)}) collective-permute-start(bf16[576,128]{1,0:T(8,128)(2,1)S(1)} %sumrouteb.1.own_ref), channel_id=1, source_target_pairs={{0,1},{1,0},{2,3},{3,2},{4,5},{5,4},{6,7},{7,6},{8,9},{9,8},{10,11... | collective-permute-start | bytes 442376 | tf_op jit(solution)/shard_map/ppermute | solution.py:638
  88.3 3.4 %collective-permute-start.29 = (bf16[576,128]{1,0:T(8,128)(2,1)S(1)}, bf16[576,128]{1,0:T(8,128)(2,1)S(1)}, u32[]{:S(2)}, u32[]{:S(2)}) collective-permute-start(bf16[576,128]{1,0:T(8,128)(2,1)S(1)} %collective-permute-done.21.far_ref), channel_id=1, source_target_pairs={{0,1},{1,0},{2,3},{3,2},{4,5},{5,4},{6,7},{7,6},{8,9},{9,8},{10,11... | collective-permute-start | bytes 442376 | tf_op jit(solution)/shard_map/ppermute | solution.py:638
  88.8 2.0 %collective-permute-start.30 = (bf16[256,256]{1,0:T(8,128)(2,1)S(1)}, bf16[256,256]{1,0:T(8,128)(2,1)S(1)}, u32[]{:S(2)}, u32[]{:S(2)}) collective-permute-start(bf16[256,256]{1,0:T(8,128)(2,1)S(1)} %sumroutea.1.own_ref), channel_id=1, source_target_pairs={{0,1},{1,0},{2,3},{3,2},{4,5},{5,4},{6,7},{7,6},{8,9},{9,8},{10,11... | collective-permute-start | bytes 393224 | tf_op jit(solution)/shard_map/ppermute | solution.py:638
  88.8 2.0 %collective-permute-start.31 = (bf16[256,256]{1,0:T(8,128)(2,1)S(1)}, bf16[256,256]{1,0:T(8,128)(2,1)S(1)}, u32[]{:S(2)}, u32[]{:S(2)}) collective-permute-start(bf16[256,256]{1,0:T(8,128)(2,1)S(1)} %collective-permute-done.22.far_ref), channel_id=1, source_target_pairs={{0,1},{1,0},{2,3},{3,2},{4,5},{5,4},{6,7},{7,6},{8,9},{9,8},{10,11... | collective-permute-start | bytes 393224 | tf_op jit(solution)/shard_map/ppermute | solution.py:638
  90.8 2.6 %collective-permute-start.27 = (bf16[592,128]{1,0:T(8,128)(2,1)S(1)}, bf16[592,128]{1,0:T(8,128)(2,1)S(1)}, u32[]{:S(2)}, u32[]{:S(2)}) collective-permute-start(bf16[592,128]{1,0:T(8,128)(2,1)S(1)} %sumroutec.1.own_ref), channel_id=1, source_target_pairs={{0,1},{1,0},{2,3},{3,2},{4,5},{5,4},{6,7},{7,6},{8,9},{9,8},{10,11... | collective-permute-start | bytes 454664 | tf_op jit(solution)/shard_map/ppermute | solution.py:638
  92.9 1.5 %collective-permute-start.32 = (bf16[592,128]{1,0:T(8,128)(2,1)S(1)}, bf16[592,128]{1,0:T(8,128)(2,1)S(1)}, u32[]{:S(2)}, u32[]{:S(2)}) collective-permute-start(bf16[592,128]{1,0:T(8,128)(2,1)S(1)} %collective-permute-done.26.far_ref), channel_id=1, source_target_pairs={{0,1},{1,0},{2,3},{3,2},{4,5},{5,4},{6,7},{7,6},{8,9},{9,8},{10,11... | collective-permute-start | bytes 454664 | tf_op jit(solution)/shard_map/ppermute | solution.py:638

commit v13 on v7

--- a/solution.py
+++ b/solution.py
@@ -21,7 +21,7 @@
 HB = pl.BlockSpec(memory_space=pltpu.HBM)
 RATE = 1 << 30
 LENGTH = {
-    "pack": 10, "stack": 10, "first": 0.02, "second": 30, "third": 20, "fourth": 10, "weight2": 1, "weight1": 3, "routeb1": 20,
+    "pack": 10, "stack": 10, "first": 0.02, "second": 30, "third": 20, "fourth": 0.5, "weight2": 1, "weight1": 3, "routeb1": 20,
 }
 
 
@@ -519,20 +519,26 @@
     refs[-1][...] = total_of([ref[0] for ref in refs[:-1]]).astype(BF16)
 
 
-def join_kernel(own_ref, far_ref, near_ref, diagonal_ref, *out_refs):
+def join_kernel(own_ref, far_ref, near_ref, diagonal_ref, out_ref, *refs):
     h = lax.axis_index("height")
-    first = 0
-    for dst in [ref for ref in out_refs if ref.shape[0] > 1]:
-        rows = dst.shape[0]
-        for ref, index in ((own_ref, h), (far_ref, h ^ 2), (near_ref, h ^ 1), (diagonal_ref, h ^ 3)):
-            dst[:, pl.ds(pl.multiple_of(BLK * index, BLK), BLK)] = ref[first : first + rows, :].astype(F32)
-        first += rows
-    if own_ref.shape[0] > first:
-        own, far = own_ref[first:, :].astype(F32), far_ref[first:, :].astype(F32)
-        near, diagonal = near_ref[first:, :].astype(F32), diagonal_ref[first:, :].astype(F32)
+    rows = out_ref.shape[0]
+    tail_refs, wide_ref, sems = refs[:-2], refs[-2], refs[-1]
+    copies = []
+    for slot, (ref, index) in enumerate(
+        ((own_ref, h), (near_ref, h ^ 1), (far_ref, h ^ 2), (diagonal_ref, h ^ 3))
+    ):
+        wide_ref[slot] = ref[0:rows, :].astype(F32)
+        column = pl.ds(pl.multiple_of(BLK * index, BLK), BLK)
+        copies.append(pltpu.make_async_copy(wide_ref.at[slot], out_ref.at[:, column], sems.at[slot]))
+        copies[-1].start()
+    if tail_refs:
+        own, far = own_ref[rows:, :].astype(F32), far_ref[rows:, :].astype(F32)
+        near, diagonal = near_ref[rows:, :].astype(F32), diagonal_ref[rows:, :].astype(F32)
         sums = 0.5 * ((own + near) + (far + diagonal))
-        for index, dst in enumerate([ref for ref in out_refs if ref.shape[0] == 1]):
+        for index, dst in enumerate(tail_refs):
             dst[...] = sums[index : index + 1, 0 : dst.shape[1]]
+    for copy in copies:
+        copy.wait()
 
 
 def join_attn_kernel(own_ref, far_ref, near_ref, diagonal_ref, *out_refs):
@@ -580,7 +586,7 @@
                         dst[image, row] = jnp.zeros((32, channels), dst.dtype)
 
 
-def call(kernel, name, outs, scratch, vmem, *operands, smem=1, any_from=99, aliases={}):
+def call(kernel, name, outs, scratch, vmem, *operands, smem=1, any_from=99, aliases={}, far_outs=0):
     specs = [SM] * smem + [VM] * (len(operands) - smem)
     specs = [HB if i >= any_from else spec for i, spec in enumerate(specs)]
     return pl.pallas_call(
@@ -588,7 +594,8 @@
         name=name,
         out_shape=[jax.ShapeDtypeStruct(shape, dtype) for shape, dtype in outs],
         in_specs=specs,
-        out_specs=[SM if dtype == jnp.int32 else VM for shape, dtype in outs],
+        out_specs=[HB] * far_outs
+        + [SM if dtype == jnp.int32 else VM for shape, dtype in outs[far_outs:]],
         scratch_shapes=[
             pltpu.SemaphoreType.DMA(shape)
             if dtype is None
@@ -769,9 +776,10 @@
         join_attn_kernel, "joina", [((small_rows, C), F32)] * 4, [], 8,
         after(gathered_a[0], shard_c), *gathered_a[1:], smem=0,
     )
+    joined = [((4, shard_rows, BLK), F32), ((4,), None)]
     (whole2,) = call(
-        join_kernel, "joinb", [((shard_rows, C), F32)], [], 8,
-        after(gathered_b[0], shard_c), *gathered_b[1:], smem=0,
+        join_kernel, "joinb", [((shard_rows, C), F32)], joined, 8,
+        after(gathered_b[0], shard_c), *gathered_b[1:], smem=0, far_outs=1,
     )
     outputs, input_grad = call(
         unpack_kernel, "unpack",
@@ -780,8 +788,8 @@
     )
     gathered_c = gather(shard_c, whole2, outputs, *small)
     whole1, *sums = call(
-        join_kernel, "joinc", [((shard_rows, C), F32)] + [((1, small_rows), F32)] * 11, [], 8,
-        *gathered_c, smem=0,
+        join_kernel, "joinc", [((shard_rows, C), F32)] + [((1, small_rows), F32)] * 11, joined, 8,
+        *gathered_c, smem=0, far_outs=1,
     )
     v = [row.reshape(small_rows) for row in sums]
 

time: 95.2 us -> 95.6 us (level)
    ppermute x9, waiting for transfers between devices: 7.74 us -> 6.55 us  [to_chip(): return lax.ppermute(v, 'height', [(i, i ^ 2) for i in range(4)])]
    ppermute x13, waiting for transfers between devices: 11.4 us -> 12.5 us  [to_batch(): return lax.ppermute(v, 'batch', [(i, i ^ change) for i in range(batches)])]
where the time goes in v13:
time: 95.6 us; the launch traced here: 95.4 us
  Pallas kernels  38.9 us (41%)
  starting transfers between devices  33.2 us (35%)
  waiting for transfers between devices  21.1 us (22%)
  between operations  1.29 us (1%)
    pallas_call x19, Pallas kernels, call(): pl.pallas_call(kernel, name=name, out_shape=[jax.ShapeDtypeStruct(shape,...  38.9 us
    ppermute x13, starting transfers between devices, to_batch(): return lax.ppermute(v, 'batch', [(i, i ^ change) for i in range(batches)])  18.5 us
    ppermute x13, waiting for transfers between devices, to_batch(): return lax.ppermute(v, 'batch', [(i, i ^ change) for i in range(batches)])  12.5 us
    ppermute x9, starting transfers between devices, to_chip(): return lax.ppermute(v, 'height', [(i, i ^ 2) for i in range(4)])  10.8 us
    ppermute x9, waiting for transfers between devices, to_chip(): return lax.ppermute(v, 'height', [(i, i ^ 2) for i in range(4)])  6.55 us
    ppermute x10, starting transfers between devices, to_core(): return lax.ppermute(v, 'height', [(i, i ^ 1) for i in range(4)])  2.49 us
    ppermute x10, waiting for transfers between devices, to_core(): return lax.ppermute(v, 'height', [(i, i ^ 1) for i in range(4)])  2.06 us
  transfers between devices with their start and end apart: 33, of which 10 were waited for; matrix products, arithmetic and copies ran while one was open for 0% of the time, Pallas kernels for 37%

profile of v13, /device:TPU:0, one launch (start us, length us, event | category | flops | bytes accessed | tf_op | source)
XLA Modules:
  0.0 95.4 jit_solution(16362358119287478542)
XLA Ops:
  0.8 0.0 slice-start
  0.8 0.0 slice-start.2
  0.8 1.9 %pack.1 = (s32[2]{0:T(128)}, bf16[128,512]{1,0:T(8,128)(2,1)}, bf16[192,512]{1,0:T(8,128)(2,1)}) custom-call(s32[2]{0:T(128)} %bucket_hbm.1, bf16[2,6,32,512]{3,2,1,0:T(8,128)(2,1)} %x_hbm.1), custom_call_target="tpu_custom_call" | custom-call | flops 10737418240 | bytes 1024 | tf_op jit(solution)/shard_map/pack/pallas_call | solution.py:592
  2.7 3.0 %collective-permute-start.1 = (bf16[128,512]{1,0:T(8,128)(2,1)}, bf16[128,512]{1,0:T(8,128)(2,1)S(1)}, u32[]{:S(2)}, u32[]{:S(2)}) collective-permute-start(bf16[128,512]{1,0:T(8,128)(2,1)} %get-tuple-element.112), channel_id=1, source_target_pairs={{0,2},{1,3},{2,0},{3,1},{4,6},{5,7},{6,4},{7,5},{8,10},{9,11},{10,... | collective-permute-start | bytes 393224 | tf_op jit(solution)/shard_map/ppermute | solution.py:648
  5.9 0.0 copy-start.2
  5.9 0.8 copy-done.2
  6.7 0.6 stack.1
  7.3 0.0 copy-start
  7.3 0.0 copy-start.4
  7.3 0.0 copy-start.5
  7.3 0.0 copy-start.6
  7.3 0.6 collective-permute-start.3
  7.9 0.1 collective-permute-start.4
  8.0 1.4 %collective-permute-start.5 = (bf16[160,512]{1,0:T(8,128)(2,1)S(1)}, bf16[160,512]{1,0:T(8,128)(2,1)S(1)}, u32[]{:S(2)}, u32[]{:S(2)}) collective-permute-start(bf16[160,512]{1,0:T(8,128)(2,1)S(1)} %get-tuple-element.118), channel_id=1, source_target_pairs={{0,3},{1,2},{2,1},{3,0},{4,7},{5,6},{6,5},{7,4},{8,11},{9,10},{10,... | collective-permute-start | bytes 491528 | tf_op jit(solution)/shard_map/ppermute | solution.py:681
  9.3 0.1 collective-permute-done.1.received
  9.5 0.6 collective-permute-start.2
  10.1 1.0 %collective-permute-done.2.partner_received = bf16[128,512]{1,0:T(8,128)(2,1)S(1)} collective-permute-done((bf16[128,512]{1,0:T(8,128)(2,1)S(1)}, bf16[128,512]{1,0:T(8,128)(2,1)S(1)}, u32[]{:S(2)}, u32[]{:S(2)}) %collective-permute-start.2) | collective-permute-done | bytes 131104 | tf_op jit(solution)/shard_map/ppermute | solution.py:645
  11.1 5.4 %first.1 = (bf16[512,512]{1,0:T(8,128)(2,1)S(1)}, f32[512,512]{1,0:T(8,128)S(1)}, bf16[512,512]{1,0:T(8,128)(2,1)S(1)}, f32[8,512]{1,0:T(8,128)S(1)}, bf16[512,5...) custom-call(s32[2]{0:T(128)S(1)} %copy-done.3, bf16[192,512]{1,0:T(8,128)(2,1)S(1)} %copy-done.1, ...), custom_call_target="tpu_custom_call" | custom-call | flops 21474836 | bytes 1024 | tf_op jit(solution)/shard_map/first/pallas_call | solution.py:592
  16.4 1.9 %collective-permute-start.6 = (bf16[2,256,512]{2,1,0:T(8,128)(2,1)S(1)}, bf16[2,256,512]{2,1,0:T(8,128)(2,1)S(1)}, u32[]{:S(2)}, u32[]{:S(2)}) collective-permute-start(bf16[2,256,512]{2,1,0:T(8,128)(2,1)S(1)} %get-tuple-element.124), channel_id=1, source_target_pairs={{0,2},{1,3},{2,0},{3,1},{4,6},{5,7},{6,4},{7,5},{8,10},{9,11},{10,... | collective-permute-start | bytes 1572872 | tf_op jit(solution)/shard_map/ppermute | solution.py:648
  18.4 9.6 %second.1 = (f32[512,512]{1,0:T(8,128)S(1)}, bf16[512,512]{1,0:T(8,128)(2,1)S(1)}, bf16[512,512]{1,0:T(8,128)(2,1)S(1)}, f32[512,512]{1,0:T(8,128)S(1)}, bf16[4,...) custom-call(s32[2]{0:T(128)S(1)} %copy-done.3, ...), custom_call_target="tpu_custom_call" | custom-call | flops 32212254720 | bytes 1024 | tf_op jit(solution)/shard_map/second/pallas_call | solution.py:592
  28.0 0.3 collective-permute-start.8
  28.3 1.5 %collective-permute-start.9 = (bf16[4,256,256]{2,1,0:T(8,128)(2,1)S(1)}, bf16[4,256,256]{2,1,0:T(8,128)(2,1)S(1)}, u32[]{:S(2)}, u32[]{:S(2)}) collective-permute-start(bf16[4,256,256]{2,1,0:T(8,128)(2,1)S(1)} %get-tuple-element.133), channel_id=1, source_target_pairs={{0,4},{4,0},{8,12},{12,8},{16,20},{20,16},{24,28},{28,24},{1,5},{5... | collective-permute-start | bytes 1572872 | tf_op jit(solution)/shard_map/ppermute | solution.py:651
  29.8 1.1 %collective-permute-done.6.half_t = bf16[2,256,512]{2,1,0:T(8,128)(2,1)S(1)} collective-permute-done((bf16[2,256,512]{2,1,0:T(8,128)(2,1)S(1)}, bf16[2,256,512]{2,1,0:T(8,128)(2,1)S(1)}, u32[]{:S(2)}, u32[]{:S(2)}) %collective-permute-start.6) | collective-permute-done | bytes 524320 | tf_op jit(solution)/shard_map/ppermute | solution.py:648
  30.8 4.3 %third.1 = (bf16[512,512]{1,0:T(8,128)(2,1)S(1)}, bf16[512,128]{1,0:T(8,128)(2,1)S(1)}, bf16[512,128]{1,0:T(8,128)(2,1)S(1)}, f32[8,512]{1,0:T(8,128)S(1)}) custom-call(s32[2]{0:T(128)S(1)} %copy-done.3, bf16[512,512]{1,0:T(8,128)(2,1)S(1)} %get-tuple-element.119.grad2_ref, f32[512,512]{1,0:T(8,128)S(1)} %get-tuple-element.120.conv_ref, ...), custom_call_target="tpu_custom_call" | custom-call | flops 21474836480 | bytes 1024 | tf_op jit(solution)/shard_map/third/pallas_call | solution.py:592
  35.2 3.3 %weight2.5 = (bf16[4,576,128]{2,1,0:T(8,128)(2,1)S(1)}, bf16[4,576,128]{2,1,0:T(8,128)(2,1)S(1)}) custom-call(s32[2]{0:T(128)S(1)} %copy-done.3, bf16[512,512]{1,0:T(8,128)(2,1)S(1)} %get-tuple-element.127.act_t, bf16[2,256,512]{2,1,0:T(8,128)(2,1)S(1)} %collective-permute-done.6.half_t, bf16[2,256,512]{2,1,0:T(8,128)(2,1)S(1)} %collective-permute-done.7.partner_half_t, ...), custom_call_target="tpu_custom_call" | custom-call | flops 1073741824 | bytes 1024 | tf_op jit(solution)/shard_map/weight2/pallas_call | solution.py:592
  38.5 1.8 %collective-permute-start.17 = (bf16[4,576,128]{2,1,0:T(8,128)(2,1)S(1)}, bf16[4,576,128]{2,1,0:T(8,128)(2,1)S(1)}, u32[]{:S(2)}, u32[]{:S(2)}) collective-permute-start(bf16[4,576,128]{2,1,0:T(8,128)(2,1)S(1)} %get-tuple-element.131), channel_id=1, source_target_pairs={{0,4},{4,0},{8,12},{12,8},{16,20},{20,16},{24,28},{28,24},{1,5},{5... | collective-permute-start | bytes 1769480 | tf_op jit(solution)/shard_map/ppermute | solution.py:651
  40.3 1.8 %collective-permute-start.10 = (bf16[512,128]{1,0:T(8,128)(2,1)S(1)}, bf16[512,128]{1,0:T(8,128)(2,1)S(1)}, u32[]{:S(2)}, u32[]{:S(2)}) collective-permute-start(bf16[512,128]{1,0:T(8,128)(2,1)S(1)} %get-tuple-element.139), channel_id=1, source_target_pairs={{0,2},{1,3},{2,0},{3,1},{4,6},{5,7},{6,4},{7,5},{8,10},{9,11},{10,... | collective-permute-start | bytes 393224 | tf_op jit(solution)/shard_map/ppermute | solution.py:648
  42.1 0.1 routea1.1
  42.2 3.7 %collective-permute-start.16 = (bf16[1,256,256]{2,1,0:T(8,128)(2,1)S(1)}, bf16[1,256,256]{2,1,0:T(8,128)(2,1)S(1)}, u32[]{:S(2)}, u32[]{:S(2)}) collective-permute-start(bf16[1,256,256]{2,1,0:T(8,128)(2,1)S(1)} %get-tuple-element.137), channel_id=1, source_target_pairs={{0,24},{4,28},{8,16},{12,20},{16,8},{20,12},{24,0},{28,4},{1,25},{... | collective-permute-start | bytes 393224 | tf_op jit(solution)/shard_map/ppermute | solution.py:651
  45.9 0.8 collective-permute-start.14
  46.7 3.1 %weight1.4 = (bf16[4,576,128]{2,1,0:T(8,128)(2,1)S(1)}, bf16[4,576,128]{2,1,0:T(8,128)(2,1)S(1)}) custom-call(s32[2]{0:T(128)S(1)} %copy-done.3, bf16[512,512]{1,0:T(8,128)(2,1)S(1)} %get-tuple-element.123.act_t, bf16[2,256,512]{2,1,0:T(8,128)(2,1)S(1)} %collective-permute-done.6.half_t, bf16[2,256,512]{2,1,0:T(8,128)(2,1)S(1)} %collective-permute-done.7.partner_half_t, ...), custom_call_target="tpu_custom_call" | custom-call | flops 3221225472 | bytes 1024 | tf_op jit(solution)/shard_map/weight1/pallas_call | solution.py:592
  49.7 1.4 %collective-permute-start.13 = (bf16[4,576,128]{2,1,0:T(8,128)(2,1)S(1)}, bf16[4,576,128]{2,1,0:T(8,128)(2,1)S(1)}, u32[]{:S(2)}, u32[]{:S(2)}) collective-permute-start(bf16[4,576,128]{2,1,0:T(8,128)(2,1)S(1)} %get-tuple-element.140), channel_id=1, source_target_pairs={{0,4},{4,0},{8,12},{12,8},{16,20},{20,16},{24,28},{28,24},{1,5},{5... | collective-permute-start | bytes 1769480 | tf_op jit(solution)/shard_map/ppermute | solution.py:651
  51.2 5.0 %fourth.1 = (bf16[192,512]{1,0:T(8,128)(2,1)S(1)}, bf16[192,512]{1,0:T(8,128)(2,1)S(1)}, bf16[2,128,512]{2,1,0:T(8,128)(2,1)S(1)}, bf16[4,16,128]{2,1,0:T(8,128)(2,1)S(1)}, bf16[4,16,128]{2,1,0:T(8,128)(2,1)S(1)}) custom-call(s32[2]{0:T(128)S(1)} %copy-done.3, bf16[512,512]{1,0:T(8,128)(2,1)S(1)} %get-tuple-element.141.grad1_ref, ...), custom_call_target="tpu_custom_call" | custom-call | flops 536870912 | bytes 1024 | tf_op jit(solution)/shard_map/fourth/pallas_call | solution.py:592
  56.2 0.9 collective-permute-done.15.refs_2_
  57.1 0.1 sumroutea.1.own_ref
  57.1 0.1 routeb1.1
  57.3 0.4 collective-permute-start.18
  57.7 2.9 %collective-permute-start.19 = (bf16[1,576,128]{2,1,0:T(8,128)(2,1)S(1)}, bf16[1,576,128]{2,1,0:T(8,128)(2,1)S(1)}, u32[]{:S(2)}, u32[]{:S(2)}) collective-permute-start(bf16[1,576,128]{2,1,0:T(8,128)(2,1)S(1)} %get-tuple-element.165), channel_id=1, source_target_pairs={{0,16},{4,20},{8,24},{12,28},{16,0},{20,4},{24,8},{28,12},{1,17},{... | collective-permute-start | bytes 442376 | tf_op jit(solution)/shard_map/ppermute | solution.py:651
  60.7 1.1 %collective-permute-start.20 = (bf16[1,576,128]{2,1,0:T(8,128)(2,1)S(1)}, bf16[1,576,128]{2,1,0:T(8,128)(2,1)S(1)}, u32[]{:S(2)}, u32[]{:S(2)}) collective-permute-start(bf16[1,576,128]{2,1,0:T(8,128)(2,1)S(1)} %get-tuple-element.166), channel_id=1, source_target_pairs={{0,24},{4,28},{8,16},{12,20},{16,8},{20,12},{24,0},{28,4},{1,25},{... | collective-permute-start | bytes 442376 | tf_op jit(solution)/shard_map/ppermute | solution.py:651
  61.8 0.5 collective-permute-start.12
  62.3 5.3 %collective-permute-done.12.got_ref = bf16[4,16,128]{2,1,0:T(8,128)(2,1)S(1)} collective-permute-done((bf16[4,16,128]{2,1,0:T(8,128)(2,1)S(1)}, bf16[4,16,128]{2,1,0:T(8,128)(2,1)S(1)}, u32[]{:S(2)}, u32[]{:S(2)}) %collective-permute-start.12) | collective-permute-done | bytes 16416 | tf_op jit(solution)/shard_map/ppermute | solution.py:651
  67.5 2.0 %collective-permute-start.23 = (bf16[256,256]{1,0:T(8,128)(2,1)S(1)}, bf16[256,256]{1,0:T(8,128)(2,1)S(1)}, u32[]{:S(2)}, u32[]{:S(2)}) collective-permute-start(bf16[256,256]{1,0:T(8,128)(2,1)S(1)} %sumroutea.1.own_ref), channel_id=1, source_target_pairs={{0,2},{1,3},{2,0},{3,1},{4,6},{5,7},{6,4},{7,5},{8,10},{9,11},{10,... | collective-permute-start | bytes 393224 | tf_op jit(solution)/shard_map/ppermute | solution.py:648
  69.5 0.0 collective-permute-start.11
  69.6 0.1 routec1.1
  69.8 1.4 %collective-permute-done.19.refs_2_ = bf16[1,576,128]{2,1,0:T(8,128)(2,1)S(1)} collective-permute-done((bf16[1,576,128]{2,1,0:T(8,128)(2,1)S(1)}, bf16[1,576,128]{2,1,0:T(8,128)(2,1)S(1)}, u32[]{:S(2)}, u32[]{:S(2)}) %collective-permute-start.19) | collective-permute-done | bytes 147488 | tf_op jit(solution)/shard_map/ppermute | solution.py:651
  71.1 2.5 %collective-permute-start.25 = (bf16[1,592,128]{2,1,0:T(8,128)(2,1)S(1)}, bf16[1,592,128]{2,1,0:T(8,128)(2,1)S(1)}, u32[]{:S(2)}, u32[]{:S(2)}) collective-permute-start(bf16[1,592,128]{2,1,0:T(8,128)(2,1)S(1)} %get-tuple-element.177), channel_id=1, source_target_pairs={{0,24},{4,28},{8,16},{12,20},{16,8},{20,12},{24,0},{28,4},{1,25},{... | collective-permute-start | bytes 454664 | tf_op jit(solution)/shard_map/ppermute | solution.py:651
  73.6 1.2 %collective-permute-start.24 = (bf16[1,592,128]{2,1,0:T(8,128)(2,1)S(1)}, bf16[1,592,128]{2,1,0:T(8,128)(2,1)S(1)}, u32[]{:S(2)}, u32[]{:S(2)}) collective-permute-start(bf16[1,592,128]{2,1,0:T(8,128)(2,1)S(1)} %get-tuple-element.174), channel_id=1, source_target_pairs={{0,16},{4,20},{8,24},{12,28},{16,0},{20,4},{24,8},{28,12},{1,17},{... | collective-permute-start | bytes 454664 | tf_op jit(solution)/shard_map/ppermute | solution.py:651
  74.8 0.7 collective-permute-start.21
  75.5 0.1 sumrouteb.1.own_ref
  75.6 1.0 %collective-permute-start.22 = (bf16[576,128]{1,0:T(8,128)(2,1)S(1)}, bf16[576,128]{1,0:T(8,128)(2,1)S(1)}, u32[]{:S(2)}, u32[]{:S(2)}) collective-permute-start(bf16[576,128]{1,0:T(8,128)(2,1)S(1)} %sumrouteb.1.own_ref), channel_id=1, source_target_pairs={{0,2},{1,3},{2,0},{3,1},{4,6},{5,7},{6,4},{7,5},{8,10},{9,11},{10,... | collective-permute-start | bytes 442376 | tf_op jit(solution)/shard_map/ppermute | solution.py:648
  76.6 5.1 %collective-permute-done.22.far_ref = bf16[576,128]{1,0:T(8,128)(2,1)S(1)} collective-permute-done((bf16[576,128]{1,0:T(8,128)(2,1)S(1)}, bf16[576,128]{1,0:T(8,128)(2,1)S(1)}, u32[]{:S(2)}, u32[]{:S(2)}) %collective-permute-start.22) | collective-permute-done | bytes 147488 | tf_op jit(solution)/shard_map/ppermute | solution.py:648
  81.7 5.0 %collective-permute-done.24.refs_2_ = bf16[1,592,128]{2,1,0:T(8,128)(2,1)S(1)} collective-permute-done((bf16[1,592,128]{2,1,0:T(8,128)(2,1)S(1)}, bf16[1,592,128]{2,1,0:T(8,128)(2,1)S(1)}, u32[]{:S(2)}, u32[]{:S(2)}) %collective-permute-start.24) | collective-permute-done | bytes 151584 | tf_op jit(solution)/shard_map/ppermute | solution.py:651
  86.7 0.1 sumroutec.1.own_ref
  86.7 0.7 collective-permute-start.26
  87.5 0.5 collective-permute-start.29
  88.0 0.5 collective-permute-start.31
  88.5 1.5 %unpack.1 = (bf16[2,6,32,512]{3,2,1,0:T(8,128)(2,1)}, bf16[2,6,32,512]{3,2,1,0:T(8,128)(2,1)}) custom-call(s32[2]{0:T(128)S(1)} %copy-done.3, bf16[192,512]{1,0:T(8,128)(2,1)S(1)} %get-tuple-element.147.out_own, bf16[192,512]{1,0:T(8,128)(2,1)S(1)} %get-tuple-element.148.grad_own, bf16[2,128,512]{2,1,0:T(8,128)(2,1)S(1)} %collective-permute-done.11.away_ref), custom_call_target="tpu_custom_call" | custom-call | flops 21474836 | bytes 1024 | tf_op jit(solution)/shard_map/unpack/pallas_call | solution.py:592
  90.0 0.0 collective-permute-start.27
  90.0 0.9 joina.1
  90.9 1.1 %joinb.1 = f32[576,512]{1,0:T(8,128)} custom-call(bf16[576,128]{1,0:T(8,128)(2,1)S(1)} %sumrouteb.1.own_ref, bf16[576,128]{1,0:T(8,128)(2,1)S(1)} %collective-permute-done.22.far_ref, bf16[576,128]{1,0:T(8,128)(2,1)S(1)} %collective-permute-done.28.near_ref, bf16[576,128]{1,0:T(8,128)(2,1)S(1)} %collective-permute-done.29.diagonal_ref), custom_call_target="tpu_custom_call" | custom-call | flops 21474836 | bytes 1024 | tf_op jit(solution)/shard_map/joinb/pallas_call | solution.py:592
  92.0 0.3 collective-permute-done.26.far_ref
  92.2 0.3 collective-permute-start.32
  92.6 1.1 %collective-permute-done.32.diagonal_ref = bf16[592,128]{1,0:T(8,128)(2,1)S(1)} collective-permute-done((bf16[592,128]{1,0:T(8,128)(2,1)S(1)}, bf16[592,128]{1,0:T(8,128)(2,1)S(1)}, u32[]{:S(2)}, u32[]{:S(2)}) %collective-permute-start.32) | collective-permute-done | bytes 151584 | tf_op jit(solution)/shard_map/ppermute | solution.py:645
  93.6 1.6 %joinc.1 = (f32[576,512]{1,0:T(8,128)}, f32[1,64]{1,0:T(1,128)}, f32[1,64]{1,0:T(1,128)}, f32[1,64]{1,0:T(1,128)}, f32[1,64]{1,0:T(1,128)}, /*index=5*/f32[1,64]...) custom-call(bf16[592,128]{1,0:T(8,128)(2,1)S(1)} %sumroutec.1.own_re, ...), custom_call_target="tpu_custom_call" | custom-call | flops 21474836 | bytes 1024 | tf_op jit(solution)/shard_map/joinc/pallas_call | solution.py:592
  (69 shorter events, 0.2 us)
Async XLA Ops:
  0.7 5.1 %copy-start.8 = (f32[512]{0:T(512)S(1)}, f32[512]{0:T(512)}, u32[]{:S(2)}) copy-start(f32[512]{0:T(512)} %param.22) | copy-start | bytes 6148
  0.7 5.1 %copy-start.9 = (f32[512]{0:T(512)S(1)}, f32[512]{0:T(512)}, u32[]{:S(2)}) copy-start(f32[512]{0:T(512)} %param.23) | copy-start | bytes 6148
  0.7 5.1 %copy-start.18 = (f32[512]{0:T(512)S(1)}, f32[512]{0:T(512)}, u32[]{:S(2)}) copy-start(f32[512]{0:T(512)} %param.38) | copy-start | bytes 6148
  0.7 5.1 %copy-start.10 = (f32[512]{0:T(512)S(1)}, f32[512]{0:T(512)}, u32[]{:S(2)}) copy-start(f32[512]{0:T(512)} %param.25) | copy-start | bytes 6148
  0.7 5.1 %copy-start.11 = (f32[512]{0:T(512)S(1)}, f32[512]{0:T(512)}, u32[]{:S(2)}) copy-start(f32[512]{0:T(512)} %param.26) | copy-start | bytes 6148
  0.7 5.1 %copy-start.12 = (f32[512]{0:T(512)S(1)}, f32[512]{0:T(512)}, u32[]{:S(2)}) copy-start(f32[512]{0:T(512)} %param.27) | copy-start | bytes 6148
  0.7 5.1 %copy-start.13 = (f32[512]{0:T(512)S(1)}, f32[512]{0:T(512)}, u32[]{:S(2)}) copy-start(f32[512]{0:T(512)} %param.29) | copy-start | bytes 6148
  0.7 5.1 %copy-start.14 = (f32[512]{0:T(512)S(1)}, f32[512]{0:T(512)}, u32[]{:S(2)}) copy-start(f32[512]{0:T(512)} %param.30) | copy-start | bytes 6148
  0.7 5.1 %copy-start.15 = (f32[512]{0:T(512)S(1)}, f32[512]{0:T(512)}, u32[]{:S(2)}) copy-start(f32[512]{0:T(512)} %param.31) | copy-start | bytes 6148
  0.8 5.1 %copy-start.16 = (f32[512]{0:T(512)S(1)}, f32[512]{0:T(512)}, u32[]{:S(2)}) copy-start(f32[512]{0:T(512)} %param.33) | copy-start | bytes 6148
  0.8 5.1 %copy-start.17 = (f32[512]{0:T(512)S(1)}, f32[512]{0:T(512)}, u32[]{:S(2)}) copy-start(f32[512]{0:T(512)} %param.36) | copy-start | bytes 6148
  0.8 5.1 %copy-start.7 = (bf16[2,6,32,512]{3,2,1,0:T(8,128)(2,1)S(1)}, bf16[2,6,32,512]{3,2,1,0:T(8,128)(2,1)}, u32[]{:S(2)}) copy-start(bf16[2,6,32,512]{3,2,1,0:T(8,128)(2,1)} %cot_ref.1) | copy-start | bytes 1179652
  0.8 10.3 %slice-start = ((s8[4718592]{0:T(1024)(128)(4,1)}), s8[524288]{0:T(1024)(128)(4,1)S(1)}, s32[]{:S(2)}) async-start(s8[4718592]{0:T(1024)(128)(4,1)} %bitcast.22), calls=%async_computation | async-start | bytes 1048576
  0.8 17.5 %slice-start.2 = ((s8[4718592]{0:T(1024)(128)(4,1)}), s8[4194304]{0:T(1024)(128)(4,1)S(1)}, s32[]{:S(2)}) async-start(s8[4718592]{0:T(1024)(128)(4,1)} %bitcast.24), calls=%async_computation.2 | async-start | bytes 8388608
  2.7 6.7 %collective-permute-start.1 = (bf16[128,512]{1,0:T(8,128)(2,1)}, bf16[128,512]{1,0:T(8,128)(2,1)S(1)}, u32[]{:S(2)}, u32[]{:S(2)}) collective-permute-start(bf16[128,512]{1,0:T(8,128)(2,1)} %get-tuple-element.112), channel_id=1, source_target_pairs={{0,2},{1,3},{2,0},{3,1},{4,6},{5,7},{6,4},{7,5},{8,10},{9,11},{10,... | collective-permute-start | bytes 393224 | tf_op jit(solution)/shard_map/ppermute | solution.py:648
  5.8 4.3 %collective-permute-start = (bf16[192,512]{1,0:T(8,128)(2,1)}, bf16[192,512]{1,0:T(8,128)(2,1)S(1)}, u32[]{:S(2)}, u32[]{:S(2)}) collective-permute-start(bf16[192,512]{1,0:T(8,128)(2,1)} %get-tuple-element.111.own), channel_id=1, source_target_pairs={{0,1},{1,0},{2,3},{3,2},{4,5},{5,4},{6,7},{7,6},{8,9},{9,8},{10,11... | collective-permute-start | bytes 589832 | tf_op jit(solution)/shard_map/ppermute | solution.py:645
  5.8 5.3 %slice-start.1 = ((s8[4718592]{0:T(1024)(128)(4,1)}), s8[4194304]{0:T(1024)(128)(4,1)S(1)}, s32[]{:S(2)}) async-start(s8[4718592]{0:T(1024)(128)(4,1)} %bitcast.22), calls=%async_computation.1 | async-start | bytes 8388608
  5.9 0.8 copy-start.2
  6.7 4.4 %copy-start.1 = (bf16[192,512]{1,0:T(8,128)(2,1)S(1)}, bf16[192,512]{1,0:T(8,128)(2,1)}, u32[]{:S(2)}) copy-start(bf16[192,512]{1,0:T(8,128)(2,1)} %get-tuple-element.111.own) | copy-start | bytes 589828
  6.7 4.4 %copy-start.3 = (s32[2]{0:T(128)S(1)}, s32[2]{0:T(128)}, u32[]{:S(2)}) copy-start(s32[2]{0:T(128)} %get-tuple-element.110.kinds.bucket_ref) | copy-start | bytes 28
  6.7 11.6 %slice-start.3 = ((s8[4718592]{0:T(1024)(128)(4,1)}), s8[524288]{0:T(1024)(128)(4,1)S(1)}, s32[]{:S(2)}) async-start(s8[4718592]{0:T(1024)(128)(4,1)} %bitcast.24), calls=%async_computation.3 | async-start | bytes 1048576
  7.3 11.1 %copy-start = (bf16[512,512]{1,0:T(8,128)(2,1)S(1)}, bf16[512,512]{1,0:T(8,128)(2,1)}, u32[]{:S(2)}) copy-start(bf16[512,512]{1,0:T(8,128)(2,1)} %wp.3) | copy-start | bytes 1572868
  7.3 11.1 %copy-start.4 = (bf16[512,512]{1,0:T(8,128)(2,1)S(1)}, bf16[512,512]{1,0:T(8,128)(2,1)}, u32[]{:S(2)}) copy-start(bf16[512,512]{1,0:T(8,128)(2,1)} %wq.1) | copy-start | bytes 1572868
  7.3 11.0 %copy-start.5 = (bf16[512,512]{1,0:T(8,128)(2,1)S(1)}, bf16[512,512]{1,0:T(8,128)(2,1)}, u32[]{:S(2)}) copy-start(bf16[512,512]{1,0:T(8,128)(2,1)} %wk.1) | copy-start | bytes 1572868
  7.3 11.0 %copy-start.6 = (bf16[512,512]{1,0:T(8,128)(2,1)S(1)}, bf16[512,512]{1,0:T(8,128)(2,1)}, u32[]{:S(2)}) copy-start(bf16[512,512]{1,0:T(8,128)(2,1)} %wv.1) | copy-start | bytes 1572868
  7.3 11.0 %collective-permute-start.3 = (bf16[192,512]{1,0:T(8,128)(2,1)S(1)}, bf16[192,512]{1,0:T(8,128)(2,1)S(1)}, u32[]{:S(2)}, u32[]{:S(2)}) collective-permute-start(bf16[192,512]{1,0:T(8,128)(2,1)S(1)} %get-tuple-element.117.own), channel_id=1, source_target_pairs={{0,1},{1,0},{2,3},{3,2},{4,5},{5,4},{6,7},{7,6},{8,9},{9,8},{10,11... | collective-permute-start | bytes 589832 | tf_op jit(solution)/shard_map/ppermute | solution.py:645
  7.9 10.4 %collective-permute-start.4 = (bf16[160,512]{1,0:T(8,128)(2,1)S(1)}, bf16[160,512]{1,0:T(8,128)(2,1)S(1)}, u32[]{:S(2)}, u32[]{:S(2)}) collective-permute-start(bf16[160,512]{1,0:T(8,128)(2,1)S(1)} %get-tuple-element.118), channel_id=1, source_target_pairs={{0,2},{1,3},{2,0},{3,1},{4,6},{5,7},{6,4},{7,5},{8,10},{9,11},{10,... | collective-permute-start | bytes 491528 | tf_op jit(solution)/shard_map/ppermute | solution.py:648
  8.0 10.3 %collective-permute-start.5 = (bf16[160,512]{1,0:T(8,128)(2,1)S(1)}, bf16[160,512]{1,0:T(8,128)(2,1)S(1)}, u32[]{:S(2)}, u32[]{:S(2)}) collective-permute-start(bf16[160,512]{1,0:T(8,128)(2,1)S(1)} %get-tuple-element.118), channel_id=1, source_target_pairs={{0,3},{1,2},{2,1},{3,0},{4,7},{5,6},{6,5},{7,4},{8,11},{9,10},{10,... | collective-permute-start | bytes 491528 | tf_op jit(solution)/shard_map/ppermute | solution.py:681
  9.5 1.6 %collective-permute-start.2 = (bf16[128,512]{1,0:T(8,128)(2,1)S(1)}, bf16[128,512]{1,0:T(8,128)(2,1)S(1)}, u32[]{:S(2)}, u32[]{:S(2)}) collective-permute-start(bf16[128,512]{1,0:T(8,128)(2,1)S(1)} %collective-permute-done.1.received), channel_id=1, source_target_pairs={{0,1},{1,0},{2,3},{3,2},{4,5},{5,4},{6,7},{7,6},{8,9},{9,8},{10,11... | collective-permute-start | bytes 393224 | tf_op jit(solution)/shard_map/ppermute | solution.py:645
  16.4 14.4 %collective-permute-start.6 = (bf16[2,256,512]{2,1,0:T(8,128)(2,1)S(1)}, bf16[2,256,512]{2,1,0:T(8,128)(2,1)S(1)}, u32[]{:S(2)}, u32[]{:S(2)}) collective-permute-start(bf16[2,256,512]{2,1,0:T(8,128)(2,1)S(1)} %get-tuple-element.124), channel_id=1, source_target_pairs={{0,2},{1,3},{2,0},{3,1},{4,6},{5,7},{6,4},{7,5},{8,10},{9,11},{10,... | collective-permute-start | bytes 1572872 | tf_op jit(solution)/shard_map/ppermute | solution.py:648
  28.0 7.2 %collective-permute-start.8 = (bf16[512,128]{1,0:T(8,128)(2,1)S(1)}, bf16[512,128]{1,0:T(8,128)(2,1)S(1)}, u32[]{:S(2)}, u32[]{:S(2)}) collective-permute-start(bf16[512,128]{1,0:T(8,128)(2,1)S(1)} %get-tuple-element.130), channel_id=1, source_target_pairs={{0,2},{1,3},{2,0},{3,1},{4,6},{5,7},{6,4},{7,5},{8,10},{9,11},{10,... | collective-permute-start | bytes 393224 | tf_op jit(solution)/shard_map/ppermute | solution.py:648
  28.3 13.8 %collective-permute-start.9 = (bf16[4,256,256]{2,1,0:T(8,128)(2,1)S(1)}, bf16[4,256,256]{2,1,0:T(8,128)(2,1)S(1)}, u32[]{:S(2)}, u32[]{:S(2)}) collective-permute-start(bf16[4,256,256]{2,1,0:T(8,128)(2,1)S(1)} %get-tuple-element.133), channel_id=1, source_target_pairs={{0,4},{4,0},{8,12},{12,8},{16,20},{20,16},{24,28},{28,24},{1,5},{5... | collective-permute-start | bytes 1572872 | tf_op jit(solution)/shard_map/ppermute | solution.py:651
  30.8 4.3 %collective-permute-start.7 = (bf16[2,256,512]{2,1,0:T(8,128)(2,1)S(1)}, bf16[2,256,512]{2,1,0:T(8,128)(2,1)S(1)}, u32[]{:S(2)}, u32[]{:S(2)}) collective-permute-start(bf16[2,256,512]{2,1,0:T(8,128)(2,1)S(1)} %collective-permute-done.6.half_t), channel_id=1, source_target_pairs={{0,1},{1,0},{2,3},{3,2},{4,5},{5,4},{6,7},{7,6},{8,9},{9,8},{10,11... | collective-permute-start | bytes 1572872 | tf_op jit(solution)/shard_map/ppermute | solution.py:645
  38.5 18.6 %collective-permute-start.17 = (bf16[4,576,128]{2,1,0:T(8,128)(2,1)S(1)}, bf16[4,576,128]{2,1,0:T(8,128)(2,1)S(1)}, u32[]{:S(2)}, u32[]{:S(2)}) collective-permute-start(bf16[4,576,128]{2,1,0:T(8,128)(2,1)S(1)} %get-tuple-element.131), channel_id=1, source_target_pairs={{0,4},{4,0},{8,12},{12,8},{16,20},{20,16},{24,28},{28,24},{1,5},{5... | collective-permute-start | bytes 1769480 | tf_op jit(solution)/shard_map/ppermute | solution.py:651
  40.3 6.4 %collective-permute-start.10 = (bf16[512,128]{1,0:T(8,128)(2,1)S(1)}, bf16[512,128]{1,0:T(8,128)(2,1)S(1)}, u32[]{:S(2)}, u32[]{:S(2)}) collective-permute-start(bf16[512,128]{1,0:T(8,128)(2,1)S(1)} %get-tuple-element.139), channel_id=1, source_target_pairs={{0,2},{1,3},{2,0},{3,1},{4,6},{5,7},{6,4},{7,5},{8,10},{9,11},{10,... | collective-permute-start | bytes 393224 | tf_op jit(solution)/shard_map/ppermute | solution.py:648
  42.2 14.0 %collective-permute-start.16 = (bf16[1,256,256]{2,1,0:T(8,128)(2,1)S(1)}, bf16[1,256,256]{2,1,0:T(8,128)(2,1)S(1)}, u32[]{:S(2)}, u32[]{:S(2)}) collective-permute-start(bf16[1,256,256]{2,1,0:T(8,128)(2,1)S(1)} %get-tuple-element.137), channel_id=1, source_target_pairs={{0,24},{4,28},{8,16},{12,20},{16,8},{20,12},{24,0},{28,4},{1,25},{... | collective-permute-start | bytes 393224 | tf_op jit(solution)/shard_map/ppermute | solution.py:651
  45.9 11.2 %collective-permute-start.15 = (bf16[1,256,256]{2,1,0:T(8,128)(2,1)S(1)}, bf16[1,256,256]{2,1,0:T(8,128)(2,1)S(1)}, u32[]{:S(2)}, u32[]{:S(2)}) collective-permute-start(bf16[1,256,256]{2,1,0:T(8,128)(2,1)S(1)} %get-tuple-element.136), channel_id=1, source_target_pairs={{0,16},{4,20},{8,24},{12,28},{16,0},{20,4},{24,8},{28,12},{1,17},{... | collective-permute-start | bytes 393224 | tf_op jit(solution)/shard_map/ppermute | solution.py:651
  45.9 11.2 %collective-permute-start.14 = (bf16[1,256,256]{2,1,0:T(8,128)(2,1)S(1)}, bf16[1,256,256]{2,1,0:T(8,128)(2,1)S(1)}, u32[]{:S(2)}, u32[]{:S(2)}) collective-permute-start(bf16[1,256,256]{2,1,0:T(8,128)(2,1)S(1)} %get-tuple-element.135), channel_id=1, source_target_pairs={{0,8},{4,12},{8,0},{12,4},{16,24},{20,28},{24,16},{28,20},{1,9},{5... | collective-permute-start | bytes 393224 | tf_op jit(solution)/shard_map/ppermute | solution.py:651
  49.7 19.8 %collective-permute-start.13 = (bf16[4,576,128]{2,1,0:T(8,128)(2,1)S(1)}, bf16[4,576,128]{2,1,0:T(8,128)(2,1)S(1)}, u32[]{:S(2)}, u32[]{:S(2)}) collective-permute-start(bf16[4,576,128]{2,1,0:T(8,128)(2,1)S(1)} %get-tuple-element.140), channel_id=1, source_target_pairs={{0,4},{4,0},{8,12},{12,8},{16,20},{20,16},{24,28},{28,24},{1,5},{5... | collective-permute-start | bytes 1769480 | tf_op jit(solution)/shard_map/ppermute | solution.py:651
  57.3 12.4 %collective-permute-start.18 = (bf16[1,576,128]{2,1,0:T(8,128)(2,1)S(1)}, bf16[1,576,128]{2,1,0:T(8,128)(2,1)S(1)}, u32[]{:S(2)}, u32[]{:S(2)}) collective-permute-start(bf16[1,576,128]{2,1,0:T(8,128)(2,1)S(1)} %get-tuple-element.164), channel_id=1, source_target_pairs={{0,8},{4,12},{8,0},{12,4},{16,24},{20,28},{24,16},{28,20},{1,9},{5... | collective-permute-start | bytes 442376 | tf_op jit(solution)/shard_map/ppermute | solution.py:651
  57.7 13.4 %collective-permute-start.19 = (bf16[1,576,128]{2,1,0:T(8,128)(2,1)S(1)}, bf16[1,576,128]{2,1,0:T(8,128)(2,1)S(1)}, u32[]{:S(2)}, u32[]{:S(2)}) collective-permute-start(bf16[1,576,128]{2,1,0:T(8,128)(2,1)S(1)} %get-tuple-element.165), channel_id=1, source_target_pairs={{0,16},{4,20},{8,24},{12,28},{16,0},{20,4},{24,8},{28,12},{1,17},{... | collective-permute-start | bytes 442376 | tf_op jit(solution)/shard_map/ppermute | solution.py:651
  60.7 10.5 %collective-permute-start.20 = (bf16[1,576,128]{2,1,0:T(8,128)(2,1)S(1)}, bf16[1,576,128]{2,1,0:T(8,128)(2,1)S(1)}, u32[]{:S(2)}, u32[]{:S(2)}) collective-permute-start(bf16[1,576,128]{2,1,0:T(8,128)(2,1)S(1)} %get-tuple-element.166), channel_id=1, source_target_pairs={{0,24},{4,28},{8,16},{12,20},{16,8},{20,12},{24,0},{28,4},{1,25},{... | collective-permute-start | bytes 442376 | tf_op jit(solution)/shard_map/ppermute | solution.py:651
  61.8 5.8 %collective-permute-start.12 = (bf16[4,16,128]{2,1,0:T(8,128)(2,1)S(1)}, bf16[4,16,128]{2,1,0:T(8,128)(2,1)S(1)}, u32[]{:S(2)}, u32[]{:S(2)}) collective-permute-start(bf16[4,16,128]{2,1,0:T(8,128)(2,1)S(1)} %get-tuple-element.151), channel_id=1, source_target_pairs={{0,4},{4,0},{8,12},{12,8},{16,20},{20,16},{24,28},{28,24},{1,5},{5... | collective-permute-start | bytes 49160 | tf_op jit(solution)/shard_map/ppermute | solution.py:651
  67.5 8.1 %collective-permute-start.23 = (bf16[256,256]{1,0:T(8,128)(2,1)S(1)}, bf16[256,256]{1,0:T(8,128)(2,1)S(1)}, u32[]{:S(2)}, u32[]{:S(2)}) collective-permute-start(bf16[256,256]{1,0:T(8,128)(2,1)S(1)} %sumroutea.1.own_ref), channel_id=1, source_target_pairs={{0,2},{1,3},{2,0},{3,1},{4,6},{5,7},{6,4},{7,5},{8,10},{9,11},{10,... | collective-permute-start | bytes 393224 | tf_op jit(solution)/shard_map/ppermute | solution.py:648
  69.5 18.5 %collective-permute-start.11 = (bf16[2,128,512]{2,1,0:T(8,128)(2,1)S(1)}, bf16[2,128,512]{2,1,0:T(8,128)(2,1)S(1)}, u32[]{:S(2)}, u32[]{:S(2)}) collective-permute-start(bf16[2,128,512]{2,1,0:T(8,128)(2,1)S(1)} %get-tuple-element.149), channel_id=1, source_target_pairs={{0,2},{1,3},{2,0},{3,1},{4,6},{5,7},{6,4},{7,5},{8,10},{9,11},{10,... | collective-permute-start | bytes 786440 | tf_op jit(solution)/shard_map/ppermute | solution.py:648
  71.1 10.5 %collective-permute-start.25 = (bf16[1,592,128]{2,1,0:T(8,128)(2,1)S(1)}, bf16[1,592,128]{2,1,0:T(8,128)(2,1)S(1)}, u32[]{:S(2)}, u32[]{:S(2)}) collective-permute-start(bf16[1,592,128]{2,1,0:T(8,128)(2,1)S(1)} %get-tuple-element.177), channel_id=1, source_target_pairs={{0,24},{4,28},{8,16},{12,20},{16,8},{20,12},{24,0},{28,4},{1,25},{... | collective-permute-start | bytes 454664 | tf_op jit(solution)/shard_map/ppermute | solution.py:651
  73.6 13.1 %collective-permute-start.24 = (bf16[1,592,128]{2,1,0:T(8,128)(2,1)S(1)}, bf16[1,592,128]{2,1,0:T(8,128)(2,1)S(1)}, u32[]{:S(2)}, u32[]{:S(2)}) collective-permute-start(bf16[1,592,128]{2,1,0:T(8,128)(2,1)S(1)} %get-tuple-element.174), channel_id=1, source_target_pairs={{0,16},{4,20},{8,24},{12,28},{16,0},{20,4},{24,8},{28,12},{1,17},{... | collective-permute-start | bytes 454664 | tf_op jit(solution)/shard_map/ppermute | solution.py:651
  74.8 11.8 %collective-permute-start.21 = (bf16[1,592,128]{2,1,0:T(8,128)(2,1)S(1)}, bf16[1,592,128]{2,1,0:T(8,128)(2,1)S(1)}, u32[]{:S(2)}, u32[]{:S(2)}) collective-permute-start(bf16[1,592,128]{2,1,0:T(8,128)(2,1)S(1)} %get-tuple-element.167), channel_id=1, source_target_pairs={{0,8},{4,12},{8,0},{12,4},{16,24},{20,28},{24,16},{28,20},{1,9},{5... | collective-permute-start | bytes 454664 | tf_op jit(solution)/shard_map/ppermute | solution.py:651
  75.6 6.1 %collective-permute-start.22 = (bf16[576,128]{1,0:T(8,128)(2,1)S(1)}, bf16[576,128]{1,0:T(8,128)(2,1)S(1)}, u32[]{:S(2)}, u32[]{:S(2)}) collective-permute-start(bf16[576,128]{1,0:T(8,128)(2,1)S(1)} %sumrouteb.1.own_ref), channel_id=1, source_target_pairs={{0,2},{1,3},{2,0},{3,1},{4,6},{5,7},{6,4},{7,5},{8,10},{9,11},{10,... | collective-permute-start | bytes 442376 | tf_op jit(solution)/shard_map/ppermute | solution.py:648
  86.7 5.5 %collective-permute-start.26 = (bf16[592,128]{1,0:T(8,128)(2,1)S(1)}, bf16[592,128]{1,0:T(8,128)(2,1)S(1)}, u32[]{:S(2)}, u32[]{:S(2)}) collective-permute-start(bf16[592,128]{1,0:T(8,128)(2,1)S(1)} %sumroutec.1.own_ref), channel_id=1, source_target_pairs={{0,2},{1,3},{2,0},{3,1},{4,6},{5,7},{6,4},{7,5},{8,10},{9,11},{10,... | collective-permute-start | bytes 454664 | tf_op jit(solution)/shard_map/ppermute | solution.py:648
  87.5 3.4 %collective-permute-start.28 = (bf16[576,128]{1,0:T(8,128)(2,1)S(1)}, bf16[576,128]{1,0:T(8,128)(2,1)S(1)}, u32[]{:S(2)}, u32[]{:S(2)}) collective-permute-start(bf16[576,128]{1,0:T(8,128)(2,1)S(1)} %sumrouteb.1.own_ref), channel_id=1, source_target_pairs={{0,1},{1,0},{2,3},{3,2},{4,5},{5,4},{6,7},{7,6},{8,9},{9,8},{10,11... | collective-permute-start | bytes 442376 | tf_op jit(solution)/shard_map/ppermute | solution.py:645
  87.5 3.4 %collective-permute-start.29 = (bf16[576,128]{1,0:T(8,128)(2,1)S(1)}, bf16[576,128]{1,0:T(8,128)(2,1)S(1)}, u32[]{:S(2)}, u32[]{:S(2)}) collective-permute-start(bf16[576,128]{1,0:T(8,128)(2,1)S(1)} %collective-permute-done.22.far_ref), channel_id=1, source_target_pairs={{0,1},{1,0},{2,3},{3,2},{4,5},{5,4},{6,7},{7,6},{8,9},{9,8},{10,11... | collective-permute-start | bytes 442376 | tf_op jit(solution)/shard_map/ppermute | solution.py:645
  88.0 2.0 %collective-permute-start.30 = (bf16[256,256]{1,0:T(8,128)(2,1)S(1)}, bf16[256,256]{1,0:T(8,128)(2,1)S(1)}, u32[]{:S(2)}, u32[]{:S(2)}) collective-permute-start(bf16[256,256]{1,0:T(8,128)(2,1)S(1)} %sumroutea.1.own_ref), channel_id=1, source_target_pairs={{0,1},{1,0},{2,3},{3,2},{4,5},{5,4},{6,7},{7,6},{8,9},{9,8},{10,11... | collective-permute-start | bytes 393224 | tf_op jit(solution)/shard_map/ppermute | solution.py:645
  88.0 2.0 %collective-permute-start.31 = (bf16[256,256]{1,0:T(8,128)(2,1)S(1)}, bf16[256,256]{1,0:T(8,128)(2,1)S(1)}, u32[]{:S(2)}, u32[]{:S(2)}) collective-permute-start(bf16[256,256]{1,0:T(8,128)(2,1)S(1)} %collective-permute-done.23.far_ref), channel_id=1, source_target_pairs={{0,1},{1,0},{2,3},{3,2},{4,5},{5,4},{6,7},{7,6},{8,9},{9,8},{10,11... | collective-permute-start | bytes 393224 | tf_op jit(solution)/shard_map/ppermute | solution.py:645
  90.0 2.5 %collective-permute-start.27 = (bf16[592,128]{1,0:T(8,128)(2,1)S(1)}, bf16[592,128]{1,0:T(8,128)(2,1)S(1)}, u32[]{:S(2)}, u32[]{:S(2)}) collective-permute-start(bf16[592,128]{1,0:T(8,128)(2,1)S(1)} %sumroutec.1.own_ref), channel_id=1, source_target_pairs={{0,1},{1,0},{2,3},{3,2},{4,5},{5,4},{6,7},{7,6},{8,9},{9,8},{10,11... | collective-permute-start | bytes 454664 | tf_op jit(solution)/shard_map/ppermute | solution.py:645
  92.2 1.4 %collective-permute-start.32 = (bf16[592,128]{1,0:T(8,128)(2,1)S(1)}, bf16[592,128]{1,0:T(8,128)(2,1)S(1)}, u32[]{:S(2)}, u32[]{:S(2)}) collective-permute-start(bf16[592,128]{1,0:T(8,128)(2,1)S(1)} %collective-permute-done.26.far_ref), channel_id=1, source_target_pairs={{0,1},{1,0},{2,3},{3,2},{4,5},{5,4},{6,7},{7,6},{8,9},{9,8},{10,11... | collective-permute-start | bytes 454664 | tf_op jit(solution)/shard_map/ppermute | solution.py:645

commit v14 on v7

--- a/solution.py
+++ b/solution.py
@@ -21,7 +21,7 @@
 HB = pl.BlockSpec(memory_space=pltpu.HBM)
 RATE = 1 << 30
 LENGTH = {
-    "pack": 10, "stack": 10, "first": 0.02, "second": 30, "third": 20, "fourth": 10, "weight2": 1, "weight1": 3, "routeb1": 20,
+    "pack": 10, "stack": 10, "first": 0.02, "second": 30, "third": 20, "fourth": 0.02, "weight2": 1, "weight1": 3, "routeb1": 20,
 }
 
 
@@ -700,7 +700,6 @@
         [shifts, img32], 14,
         kinds, grad2, conv, stats, vecs, conv2_weight,
     )
-    block1_away = to_chip(block1_send)
 
     def weight_grad(name, act_t, index, own, away):
         return call(
@@ -744,20 +743,21 @@
         return shard, far, near, to_core(after(far, *between))
 
     parts_a, got_a = spread("routea", 1, after(attn_keep, send2), attn_got)
+    block1_away = to_chip(after(block1_send, *parts_a))
     keep1, send1 = weight_grad("weight1", act1_t, 0, after(block1, *parts_a), block1_away)
     got1 = to_batch(send1, 1)
     shard_a = finish("routea", parts_a, [after(g, send1) for g in got_a])
+    parts_b, got_b = spread("routeb", 1, after(keep2, send1, shard_a), got2)
     out_own, grad_own, image_send, vec_keep, vec_send = call(
         fourth_kernel, "fourth",
         [((192, C), BF16), ((192, C), BF16), ((2, 128, C), BF16),
          ((batches // 2, VECS, BLK), BF16), ((batches // 2, VECS, BLK), BF16)],
         [shifts, img32, img16, ((VECS, C), F32)], 14,
-        kinds, after(grad1, send1), image, stats, grad_middle, middle, mixed, vecs,
+        kinds, after(grad1, *parts_b), image, stats, grad_middle, middle, mixed, vecs,
         conv1_weight, proj_weight, vec_a, vec_b,
     )
     image_away = to_chip(image_send)
     vec_got = to_batch(vec_send, 1)
-    parts_b, got_b = spread("routeb", 1, after(keep2, vec_keep, shard_a), got2)
     parts_c, got_c = spread("routec", 1, keep1, got1, (vec_keep, vec_got), behind=got_b)
     shard_b = finish("routeb", parts_b, [after(g, parts_c[0]) for g in got_b])
     gathered_a = gather(shard_a)

time: 95.2 us -> 95.9 us (level)
    ppermute x13, waiting for transfers between devices: 11.4 us -> 13.5 us  [to_batch(): return lax.ppermute(v, 'batch', [(i, i ^ change) for i in range(batches)])]
    ppermute x9, waiting for transfers between devices: 7.74 us -> 6.29 us  [to_chip(): return lax.ppermute(v, 'height', [(i, i ^ 2) for i in range(4)])]
where the time goes in v14:
time: 95.9 us; the launch traced here: 95.8 us
  Pallas kernels  38.6 us (40%)
  starting transfers between devices  32.8 us (34%)
  waiting for transfers between devices  22.1 us (23%)
  between operations  1.3 us (1%)
    pallas_call x19, Pallas kernels, call(): pl.pallas_call(kernel, name=name, out_shape=[jax.ShapeDtypeStruct(shape,...  38.6 us
    ppermute x13, starting transfers between devices, to_batch(): return lax.ppermute(v, 'batch', [(i, i ^ change) for i in range(batches)])  19.1 us
    ppermute x13, waiting for transfers between devices, to_batch(): return lax.ppermute(v, 'batch', [(i, i ^ change) for i in range(batches)])  13.5 us
    ppermute x9, starting transfers between devices, to_chip(): return lax.ppermute(v, 'height', [(i, i ^ 2) for i in range(4)])  10.2 us
    ppermute x9, waiting for transfers between devices, to_chip(): return lax.ppermute(v, 'height', [(i, i ^ 2) for i in range(4)])  6.29 us
    ppermute x10, waiting for transfers between devices, to_core(): return lax.ppermute(v, 'height', [(i, i ^ 1) for i in range(4)])  2.35 us
    ppermute x10, starting transfers between devices, to_core(): return lax.ppermute(v, 'height', [(i, i ^ 1) for i in range(4)])  2.21 us
  transfers between devices with their start and end apart: 33, of which 10 were waited for; matrix products, arithmetic and copies ran while one was open for 0% of the time, Pallas kernels for 37%

profile of v14, /device:TPU:0, one launch (start us, length us, event | category | flops | bytes accessed | tf_op | source)
XLA Modules:
  0.0 95.8 jit_solution(10371895129072873332)
XLA Ops:
  0.8 0.0 slice-start
  0.8 0.0 slice-start.2
  0.8 1.9 %pack.1 = (s32[2]{0:T(128)}, bf16[128,512]{1,0:T(8,128)(2,1)}, bf16[192,512]{1,0:T(8,128)(2,1)}) custom-call(s32[2]{0:T(128)} %bucket_hbm.1, bf16[2,6,32,512]{3,2,1,0:T(8,128)(2,1)} %x_hbm.1), custom_call_target="tpu_custom_call" | custom-call | flops 10737418240 | bytes 1024 | tf_op jit(solution)/shard_map/pack/pallas_call | solution.py:586
  2.7 3.0 %collective-permute-start.1 = (bf16[128,512]{1,0:T(8,128)(2,1)}, bf16[128,512]{1,0:T(8,128)(2,1)S(1)}, u32[]{:S(2)}, u32[]{:S(2)}) collective-permute-start(bf16[128,512]{1,0:T(8,128)(2,1)} %get-tuple-element.113), channel_id=1, source_target_pairs={{0,2},{1,3},{2,0},{3,1},{4,6},{5,7},{6,4},{7,5},{8,10},{9,11},{10,... | collective-permute-start | bytes 393224 | tf_op jit(solution)/shard_map/ppermute | solution.py:641
  5.8 0.0 collective-permute-start
  5.9 0.0 copy-start.2
  5.9 0.8 copy-done.2
  6.7 0.6 stack.1
  7.3 0.0 copy-start
  7.3 0.0 copy-start.4
  7.3 0.0 copy-start.5
  7.3 0.0 copy-start.6
  7.3 0.6 collective-permute-start.3
  7.9 0.1 collective-permute-start.4
  8.0 1.4 %collective-permute-start.5 = (bf16[160,512]{1,0:T(8,128)(2,1)S(1)}, bf16[160,512]{1,0:T(8,128)(2,1)S(1)}, u32[]{:S(2)}, u32[]{:S(2)}) collective-permute-start(bf16[160,512]{1,0:T(8,128)(2,1)S(1)} %get-tuple-element.119), channel_id=1, source_target_pairs={{0,3},{1,2},{2,1},{3,0},{4,7},{5,6},{6,5},{7,4},{8,11},{9,10},{10,... | collective-permute-start | bytes 491528 | tf_op jit(solution)/shard_map/ppermute | solution.py:674
  9.3 0.1 collective-permute-done.1.received
  9.5 0.6 collective-permute-start.2
  10.1 1.0 %collective-permute-done.2.partner_received = bf16[128,512]{1,0:T(8,128)(2,1)S(1)} collective-permute-done((bf16[128,512]{1,0:T(8,128)(2,1)S(1)}, bf16[128,512]{1,0:T(8,128)(2,1)S(1)}, u32[]{:S(2)}, u32[]{:S(2)}) %collective-permute-start.2) | collective-permute-done | bytes 131104 | tf_op jit(solution)/shard_map/ppermute | solution.py:638
  11.1 5.4 %first.1 = (bf16[512,512]{1,0:T(8,128)(2,1)S(1)}, f32[512,512]{1,0:T(8,128)S(1)}, bf16[512,512]{1,0:T(8,128)(2,1)S(1)}, f32[8,512]{1,0:T(8,128)S(1)}, bf16[512,5...) custom-call(s32[2]{0:T(128)S(1)} %copy-done.3, bf16[192,512]{1,0:T(8,128)(2,1)S(1)} %copy-done.1, ...), custom_call_target="tpu_custom_call" | custom-call | flops 21474836 | bytes 1024 | tf_op jit(solution)/shard_map/first/pallas_call | solution.py:586
  16.4 1.9 %collective-permute-start.6 = (bf16[2,256,512]{2,1,0:T(8,128)(2,1)S(1)}, bf16[2,256,512]{2,1,0:T(8,128)(2,1)S(1)}, u32[]{:S(2)}, u32[]{:S(2)}) collective-permute-start(bf16[2,256,512]{2,1,0:T(8,128)(2,1)S(1)} %get-tuple-element.125), channel_id=1, source_target_pairs={{0,2},{1,3},{2,0},{3,1},{4,6},{5,7},{6,4},{7,5},{8,10},{9,11},{10,... | collective-permute-start | bytes 1572872 | tf_op jit(solution)/shard_map/ppermute | solution.py:641
  18.4 9.6 %second.1 = (f32[512,512]{1,0:T(8,128)S(1)}, bf16[512,512]{1,0:T(8,128)(2,1)S(1)}, bf16[512,512]{1,0:T(8,128)(2,1)S(1)}, f32[512,512]{1,0:T(8,128)S(1)}, bf16[4,...) custom-call(s32[2]{0:T(128)S(1)} %copy-done.3, ...), custom_call_target="tpu_custom_call" | custom-call | flops 32212254720 | bytes 1024 | tf_op jit(solution)/shard_map/second/pallas_call | solution.py:586
  28.0 0.3 collective-permute-start.8
  28.3 1.5 %collective-permute-start.9 = (bf16[4,256,256]{2,1,0:T(8,128)(2,1)S(1)}, bf16[4,256,256]{2,1,0:T(8,128)(2,1)S(1)}, u32[]{:S(2)}, u32[]{:S(2)}) collective-permute-start(bf16[4,256,256]{2,1,0:T(8,128)(2,1)S(1)} %get-tuple-element.135), channel_id=1, source_target_pairs={{0,4},{4,0},{8,12},{12,8},{16,20},{20,16},{24,28},{28,24},{1,5},{5... | collective-permute-start | bytes 1572872 | tf_op jit(solution)/shard_map/ppermute | solution.py:644
  29.8 1.1 %collective-permute-done.6.half_t = bf16[2,256,512]{2,1,0:T(8,128)(2,1)S(1)} collective-permute-done((bf16[2,256,512]{2,1,0:T(8,128)(2,1)S(1)}, bf16[2,256,512]{2,1,0:T(8,128)(2,1)S(1)}, u32[]{:S(2)}, u32[]{:S(2)}) %collective-permute-start.6) | collective-permute-done | bytes 524320 | tf_op jit(solution)/shard_map/ppermute | solution.py:641
  30.8 4.3 %third.1 = (bf16[512,512]{1,0:T(8,128)(2,1)S(1)}, bf16[512,128]{1,0:T(8,128)(2,1)S(1)}, bf16[512,128]{1,0:T(8,128)(2,1)S(1)}, f32[8,512]{1,0:T(8,128)S(1)}) custom-call(s32[2]{0:T(128)S(1)} %copy-done.3, bf16[512,512]{1,0:T(8,128)(2,1)S(1)} %get-tuple-element.120.grad2_ref, f32[512,512]{1,0:T(8,128)S(1)} %get-tuple-element.121.conv_ref, ...), custom_call_target="tpu_custom_call" | custom-call | flops 21474836480 | bytes 1024 | tf_op jit(solution)/shard_map/third/pallas_call | solution.py:586
  35.2 3.3 %weight2.5 = (bf16[4,576,128]{2,1,0:T(8,128)(2,1)S(1)}, bf16[4,576,128]{2,1,0:T(8,128)(2,1)S(1)}) custom-call(s32[2]{0:T(128)S(1)} %copy-done.3, bf16[512,512]{1,0:T(8,128)(2,1)S(1)} %get-tuple-element.124.act_t, bf16[2,256,512]{2,1,0:T(8,128)(2,1)S(1)} %collective-permute-done.6.half_t, bf16[2,256,512]{2,1,0:T(8,128)(2,1)S(1)} %collective-permute-done.7.partner_half_t, ...), custom_call_target="tpu_custom_call" | custom-call | flops 1073741824 | bytes 1024 | tf_op jit(solution)/shard_map/weight2/pallas_call | solution.py:586
  38.5 1.8 %collective-permute-start.14 = (bf16[4,576,128]{2,1,0:T(8,128)(2,1)S(1)}, bf16[4,576,128]{2,1,0:T(8,128)(2,1)S(1)}, u32[]{:S(2)}, u32[]{:S(2)}) collective-permute-start(bf16[4,576,128]{2,1,0:T(8,128)(2,1)S(1)} %get-tuple-element.133), channel_id=1, source_target_pairs={{0,4},{4,0},{8,12},{12,8},{16,20},{20,16},{24,28},{28,24},{1,5},{5... | collective-permute-start | bytes 1769480 | tf_op jit(solution)/shard_map/ppermute | solution.py:644
  40.3 1.8 %collective-permute-done.9.got_ref = bf16[4,256,256]{2,1,0:T(8,128)(2,1)S(1)} collective-permute-done((bf16[4,256,256]{2,1,0:T(8,128)(2,1)S(1)}, bf16[4,256,256]{2,1,0:T(8,128)(2,1)S(1)}, u32[]{:S(2)}, u32[]{:S(2)}) %collective-permute-start.9) | collective-permute-done | bytes 524320 | tf_op jit(solution)/shard_map/ppermute | solution.py:644
  42.1 0.1 routea1.1
  42.2 1.5 %collective-permute-start.10 = (bf16[512,128]{1,0:T(8,128)(2,1)S(1)}, bf16[512,128]{1,0:T(8,128)(2,1)S(1)}, u32[]{:S(2)}, u32[]{:S(2)}) collective-permute-start(bf16[512,128]{1,0:T(8,128)(2,1)S(1)} %get-tuple-element.142), channel_id=1, source_target_pairs={{0,2},{1,3},{2,0},{3,1},{4,6},{5,7},{6,4},{7,5},{8,10},{9,11},{10,... | collective-permute-start | bytes 393224 | tf_op jit(solution)/shard_map/ppermute | solution.py:641
  43.7 3.4 %collective-permute-start.13 = (bf16[1,256,256]{2,1,0:T(8,128)(2,1)S(1)}, bf16[1,256,256]{2,1,0:T(8,128)(2,1)S(1)}, u32[]{:S(2)}, u32[]{:S(2)}) collective-permute-start(bf16[1,256,256]{2,1,0:T(8,128)(2,1)S(1)} %get-tuple-element.139), channel_id=1, source_target_pairs={{0,24},{4,28},{8,16},{12,20},{16,8},{20,12},{24,0},{28,4},{1,25},{... | collective-permute-start | bytes 393224 | tf_op jit(solution)/shard_map/ppermute | solution.py:644
  47.1 1.0 %collective-permute-start.11 = (bf16[1,256,256]{2,1,0:T(8,128)(2,1)S(1)}, bf16[1,256,256]{2,1,0:T(8,128)(2,1)S(1)}, u32[]{:S(2)}, u32[]{:S(2)}) collective-permute-start(bf16[1,256,256]{2,1,0:T(8,128)(2,1)S(1)} %get-tuple-element.137), channel_id=1, source_target_pairs={{0,8},{4,12},{8,0},{12,4},{16,24},{20,28},{24,16},{28,20},{1,9},{5... | collective-permute-start | bytes 393224 | tf_op jit(solution)/shard_map/ppermute | solution.py:644
  48.1 3.1 %weight1.4 = (bf16[4,576,128]{2,1,0:T(8,128)(2,1)S(1)}, bf16[4,576,128]{2,1,0:T(8,128)(2,1)S(1)}) custom-call(s32[2]{0:T(128)S(1)} %copy-done.3, bf16[512,512]{1,0:T(8,128)(2,1)S(1)} %get-tuple-element.131.act_t, bf16[2,256,512]{2,1,0:T(8,128)(2,1)S(1)} %collective-permute-done.6.half_t, bf16[2,256,512]{2,1,0:T(8,128)(2,1)S(1)} %collective-permute-done.7.partner_half_t, ...), custom_call_target="tpu_custom_call" | custom-call | flops 3221225472 | bytes 1024 | tf_op jit(solution)/shard_map/weight1/pallas_call | solution.py:586
  51.2 1.3 %collective-permute-start.17 = (bf16[4,576,128]{2,1,0:T(8,128)(2,1)S(1)}, bf16[4,576,128]{2,1,0:T(8,128)(2,1)S(1)}, u32[]{:S(2)}, u32[]{:S(2)}) collective-permute-start(bf16[4,576,128]{2,1,0:T(8,128)(2,1)S(1)} %get-tuple-element.143), channel_id=1, source_target_pairs={{0,4},{4,0},{8,12},{12,8},{16,20},{20,16},{24,28},{28,24},{1,5},{5... | collective-permute-start | bytes 1769480 | tf_op jit(solution)/shard_map/ppermute | solution.py:644
  52.5 4.6 %collective-permute-done.12.refs_2_ = bf16[1,256,256]{2,1,0:T(8,128)(2,1)S(1)} collective-permute-done((bf16[1,256,256]{2,1,0:T(8,128)(2,1)S(1)}, bf16[1,256,256]{2,1,0:T(8,128)(2,1)S(1)}, u32[]{:S(2)}, u32[]{:S(2)}) %collective-permute-start.12) | collective-permute-done | bytes 131104 | tf_op jit(solution)/shard_map/ppermute | solution.py:644
  57.1 0.1 sumroutea.1.own_ref
  57.1 0.1 routeb1.1
  57.3 0.1 collective-permute-start.18
  57.4 3.0 %collective-permute-start.19 = (bf16[1,576,128]{2,1,0:T(8,128)(2,1)S(1)}, bf16[1,576,128]{2,1,0:T(8,128)(2,1)S(1)}, u32[]{:S(2)}, u32[]{:S(2)}) collective-permute-start(bf16[1,576,128]{2,1,0:T(8,128)(2,1)S(1)} %get-tuple-element.150), channel_id=1, source_target_pairs={{0,16},{4,20},{8,24},{12,28},{16,0},{20,4},{24,8},{28,12},{1,17},{... | collective-permute-start | bytes 442376 | tf_op jit(solution)/shard_map/ppermute | solution.py:644
  60.4 1.4 %collective-permute-start.20 = (bf16[1,576,128]{2,1,0:T(8,128)(2,1)S(1)}, bf16[1,576,128]{2,1,0:T(8,128)(2,1)S(1)}, u32[]{:S(2)}, u32[]{:S(2)}) collective-permute-start(bf16[1,576,128]{2,1,0:T(8,128)(2,1)S(1)} %get-tuple-element.151), channel_id=1, source_target_pairs={{0,24},{4,28},{8,16},{12,20},{16,8},{20,12},{24,0},{28,4},{1,25},{... | collective-permute-start | bytes 442376 | tf_op jit(solution)/shard_map/ppermute | solution.py:644
  61.8 5.0 %fourth.1 = (bf16[192,512]{1,0:T(8,128)(2,1)S(1)}, bf16[192,512]{1,0:T(8,128)(2,1)S(1)}, bf16[2,128,512]{2,1,0:T(8,128)(2,1)S(1)}, bf16[4,16,128]{2,1,0:T(8,128)(2,1)S(1)}, bf16[4,16,128]{2,1,0:T(8,128)(2,1)S(1)}) custom-call(s32[2]{0:T(128)S(1)} %copy-done.3, bf16[512,512]{1,0:T(8,128)(2,1)S(1)} %get-tuple-element.152.grad1_ref, ...), custom_call_target="tpu_custom_call" | custom-call | flops 21474836 | bytes 1024 | tf_op jit(solution)/shard_map/fourth/pallas_call | solution.py:586
  66.8 1.1 %collective-permute-start.16 = (bf16[4,16,128]{2,1,0:T(8,128)(2,1)S(1)}, bf16[4,16,128]{2,1,0:T(8,128)(2,1)S(1)}, u32[]{:S(2)}, u32[]{:S(2)}) collective-permute-start(bf16[4,16,128]{2,1,0:T(8,128)(2,1)S(1)} %get-tuple-element.162), channel_id=1, source_target_pairs={{0,4},{4,0},{8,12},{12,8},{16,20},{20,16},{24,28},{28,24},{1,5},{5... | collective-permute-start | bytes 49160 | tf_op jit(solution)/shard_map/ppermute | solution.py:644
  67.9 2.6 %collective-permute-done.16.got_ref = bf16[4,16,128]{2,1,0:T(8,128)(2,1)S(1)} collective-permute-done((bf16[4,16,128]{2,1,0:T(8,128)(2,1)S(1)}, bf16[4,16,128]{2,1,0:T(8,128)(2,1)S(1)}, u32[]{:S(2)}, u32[]{:S(2)}) %collective-permute-start.16) | collective-permute-done | bytes 16416 | tf_op jit(solution)/shard_map/ppermute | solution.py:644
  70.5 0.6 collective-permute-start.23
  71.1 1.5 %collective-permute-start.15 = (bf16[2,128,512]{2,1,0:T(8,128)(2,1)S(1)}, bf16[2,128,512]{2,1,0:T(8,128)(2,1)S(1)}, u32[]{:S(2)}, u32[]{:S(2)}) collective-permute-start(bf16[2,128,512]{2,1,0:T(8,128)(2,1)S(1)} %get-tuple-element.160), channel_id=1, source_target_pairs={{0,2},{1,3},{2,0},{3,1},{4,6},{5,7},{6,4},{7,5},{8,10},{9,11},{10,... | collective-permute-start | bytes 786440 | tf_op jit(solution)/shard_map/ppermute | solution.py:641
  72.5 0.1 routec1.1
  72.8 2.6 %collective-permute-start.25 = (bf16[1,592,128]{2,1,0:T(8,128)(2,1)S(1)}, bf16[1,592,128]{2,1,0:T(8,128)(2,1)S(1)}, u32[]{:S(2)}, u32[]{:S(2)}) collective-permute-start(bf16[1,592,128]{2,1,0:T(8,128)(2,1)S(1)} %get-tuple-element.179), channel_id=1, source_target_pairs={{0,24},{4,28},{8,16},{12,20},{16,8},{20,12},{24,0},{28,4},{1,25},{... | collective-permute-start | bytes 454664 | tf_op jit(solution)/shard_map/ppermute | solution.py:644
  75.3 1.9 %collective-permute-start.21 = (bf16[1,592,128]{2,1,0:T(8,128)(2,1)S(1)}, bf16[1,592,128]{2,1,0:T(8,128)(2,1)S(1)}, u32[]{:S(2)}, u32[]{:S(2)}) collective-permute-start(bf16[1,592,128]{2,1,0:T(8,128)(2,1)S(1)} %get-tuple-element.170), channel_id=1, source_target_pairs={{0,8},{4,12},{8,0},{12,4},{16,24},{20,28},{24,16},{28,20},{1,9},{5... | collective-permute-start | bytes 454664 | tf_op jit(solution)/shard_map/ppermute | solution.py:644
  77.2 0.1 sumrouteb.1.own_ref
  77.3 0.6 collective-permute-start.22
  77.9 4.6 %collective-permute-done.22.far_ref = bf16[576,128]{1,0:T(8,128)(2,1)S(1)} collective-permute-done((bf16[576,128]{1,0:T(8,128)(2,1)S(1)}, bf16[576,128]{1,0:T(8,128)(2,1)S(1)}, u32[]{:S(2)}, u32[]{:S(2)}) %collective-permute-start.22) | collective-permute-done | bytes 147488 | tf_op jit(solution)/shard_map/ppermute | solution.py:641
  82.5 4.5 %collective-permute-done.24.refs_2_ = bf16[1,592,128]{2,1,0:T(8,128)(2,1)S(1)} collective-permute-done((bf16[1,592,128]{2,1,0:T(8,128)(2,1)S(1)}, bf16[1,592,128]{2,1,0:T(8,128)(2,1)S(1)}, u32[]{:S(2)}, u32[]{:S(2)}) %collective-permute-start.24) | collective-permute-done | bytes 151584 | tf_op jit(solution)/shard_map/ppermute | solution.py:644
  87.0 0.1 sumroutec.1.own_ref
  87.1 0.8 collective-permute-start.26
  87.9 0.5 collective-permute-start.29
  88.4 0.5 collective-permute-start.31
  89.0 1.5 %unpack.1 = (bf16[2,6,32,512]{3,2,1,0:T(8,128)(2,1)}, bf16[2,6,32,512]{3,2,1,0:T(8,128)(2,1)}) custom-call(s32[2]{0:T(128)S(1)} %copy-done.3, bf16[192,512]{1,0:T(8,128)(2,1)S(1)} %get-tuple-element.158.out_own, bf16[192,512]{1,0:T(8,128)(2,1)S(1)} %get-tuple-element.159.grad_own, bf16[2,128,512]{2,1,0:T(8,128)(2,1)S(1)} %collective-permute-done.15.away_ref), custom_call_target="tpu_custom_call" | custom-call | flops 21474836 | bytes 1024 | tf_op jit(solution)/shard_map/unpack/pallas_call | solution.py:586
  90.5 0.0 collective-permute-start.27
  90.5 0.9 joina.1
  91.3 1.2 %joinb.1 = f32[576,512]{1,0:T(8,128)} custom-call(bf16[576,128]{1,0:T(8,128)(2,1)S(1)} %sumrouteb.1.own_ref, bf16[576,128]{1,0:T(8,128)(2,1)S(1)} %collective-permute-done.22.far_ref, bf16[576,128]{1,0:T(8,128)(2,1)S(1)} %collective-permute-done.28.near_ref, bf16[576,128]{1,0:T(8,128)(2,1)S(1)} %collective-permute-done.29.diagonal_ref), custom_call_target="tpu_custom_call" | custom-call | flops 21474836 | bytes 1024 | tf_op jit(solution)/shard_map/joinb/pallas_call | solution.py:586
  92.5 0.5 collective-permute-done.26.far_ref
  93.0 0.0 collective-permute-start.32
  93.0 1.3 %collective-permute-done.32.diagonal_ref = bf16[592,128]{1,0:T(8,128)(2,1)S(1)} collective-permute-done((bf16[592,128]{1,0:T(8,128)(2,1)S(1)}, bf16[592,128]{1,0:T(8,128)(2,1)S(1)}, u32[]{:S(2)}, u32[]{:S(2)}) %collective-permute-start.32) | collective-permute-done | bytes 151584 | tf_op jit(solution)/shard_map/ppermute | solution.py:638
  94.4 1.2 %joinc.1 = (f32[576,512]{1,0:T(8,128)}, f32[1,64]{1,0:T(1,128)}, f32[1,64]{1,0:T(1,128)}, f32[1,64]{1,0:T(1,128)}, f32[1,64]{1,0:T(1,128)}, /*index=5*/f32[1,64]...) custom-call(bf16[592,128]{1,0:T(8,128)(2,1)S(1)} %sumroutec.1.own_re, ...), custom_call_target="tpu_custom_call" | custom-call | flops 21474836 | bytes 1024 | tf_op jit(solution)/shard_map/joinc/pallas_call | solution.py:586
  (69 shorter events, 0.2 us)
Async XLA Ops:
  0.7 5.1 %copy-start.8 = (f32[512]{0:T(512)S(1)}, f32[512]{0:T(512)}, u32[]{:S(2)}) copy-start(f32[512]{0:T(512)} %param.22) | copy-start | bytes 6148
  0.7 5.1 %copy-start.9 = (f32[512]{0:T(512)S(1)}, f32[512]{0:T(512)}, u32[]{:S(2)}) copy-start(f32[512]{0:T(512)} %param.23) | copy-start | bytes 6148
  0.7 5.1 %copy-start.18 = (f32[512]{0:T(512)S(1)}, f32[512]{0:T(512)}, u32[]{:S(2)}) copy-start(f32[512]{0:T(512)} %param.38) | copy-start | bytes 6148
  0.7 5.1 %copy-start.10 = (f32[512]{0:T(512)S(1)}, f32[512]{0:T(512)}, u32[]{:S(2)}) copy-start(f32[512]{0:T(512)} %param.25) | copy-start | bytes 6148
  0.7 5.1 %copy-start.11 = (f32[512]{0:T(512)S(1)}, f32[512]{0:T(512)}, u32[]{:S(2)}) copy-start(f32[512]{0:T(512)} %param.26) | copy-start | bytes 6148
  0.7 5.1 %copy-start.12 = (f32[512]{0:T(512)S(1)}, f32[512]{0:T(512)}, u32[]{:S(2)}) copy-start(f32[512]{0:T(512)} %param.27) | copy-start | bytes 6148
  0.7 5.1 %copy-start.13 = (f32[512]{0:T(512)S(1)}, f32[512]{0:T(512)}, u32[]{:S(2)}) copy-start(f32[512]{0:T(512)} %param.29) | copy-start | bytes 6148
  0.7 5.1 %copy-start.14 = (f32[512]{0:T(512)S(1)}, f32[512]{0:T(512)}, u32[]{:S(2)}) copy-start(f32[512]{0:T(512)} %param.30) | copy-start | bytes 6148
  0.7 5.1 %copy-start.15 = (f32[512]{0:T(512)S(1)}, f32[512]{0:T(512)}, u32[]{:S(2)}) copy-start(f32[512]{0:T(512)} %param.31) | copy-start | bytes 6148
  0.8 5.1 %copy-start.16 = (f32[512]{0:T(512)S(1)}, f32[512]{0:T(512)}, u32[]{:S(2)}) copy-start(f32[512]{0:T(512)} %param.33) | copy-start | bytes 6148
  0.8 5.1 %copy-start.17 = (f32[512]{0:T(512)S(1)}, f32[512]{0:T(512)}, u32[]{:S(2)}) copy-start(f32[512]{0:T(512)} %param.36) | copy-start | bytes 6148
  0.8 5.1 %copy-start.7 = (bf16[2,6,32,512]{3,2,1,0:T(8,128)(2,1)S(1)}, bf16[2,6,32,512]{3,2,1,0:T(8,128)(2,1)}, u32[]{:S(2)}) copy-start(bf16[2,6,32,512]{3,2,1,0:T(8,128)(2,1)} %cot_ref.1) | copy-start | bytes 1179652
  0.8 10.3 %slice-start = ((s8[4718592]{0:T(1024)(128)(4,1)}), s8[524288]{0:T(1024)(128)(4,1)S(1)}, s32[]{:S(2)}) async-start(s8[4718592]{0:T(1024)(128)(4,1)} %bitcast.22), calls=%async_computation | async-start | bytes 1048576
  0.8 17.5 %slice-start.2 = ((s8[4718592]{0:T(1024)(128)(4,1)}), s8[4194304]{0:T(1024)(128)(4,1)S(1)}, s32[]{:S(2)}) async-start(s8[4718592]{0:T(1024)(128)(4,1)} %bitcast.24), calls=%async_computation.2 | async-start | bytes 8388608
  2.7 6.7 %collective-permute-start.1 = (bf16[128,512]{1,0:T(8,128)(2,1)}, bf16[128,512]{1,0:T(8,128)(2,1)S(1)}, u32[]{:S(2)}, u32[]{:S(2)}) collective-permute-start(bf16[128,512]{1,0:T(8,128)(2,1)} %get-tuple-element.113), channel_id=1, source_target_pairs={{0,2},{1,3},{2,0},{3,1},{4,6},{5,7},{6,4},{7,5},{8,10},{9,11},{10,... | collective-permute-start | bytes 393224 | tf_op jit(solution)/shard_map/ppermute | solution.py:641
  5.8 4.3 %collective-permute-start = (bf16[192,512]{1,0:T(8,128)(2,1)}, bf16[192,512]{1,0:T(8,128)(2,1)S(1)}, u32[]{:S(2)}, u32[]{:S(2)}) collective-permute-start(bf16[192,512]{1,0:T(8,128)(2,1)} %get-tuple-element.112.own), channel_id=1, source_target_pairs={{0,1},{1,0},{2,3},{3,2},{4,5},{5,4},{6,7},{7,6},{8,9},{9,8},{10,11... | collective-permute-start | bytes 589832 | tf_op jit(solution)/shard_map/ppermute | solution.py:638
  5.8 5.3 %slice-start.1 = ((s8[4718592]{0:T(1024)(128)(4,1)}), s8[4194304]{0:T(1024)(128)(4,1)S(1)}, s32[]{:S(2)}) async-start(s8[4718592]{0:T(1024)(128)(4,1)} %bitcast.22), calls=%async_computation.1 | async-start | bytes 8388608
  5.9 0.8 copy-start.2
  6.7 4.4 %copy-start.1 = (bf16[192,512]{1,0:T(8,128)(2,1)S(1)}, bf16[192,512]{1,0:T(8,128)(2,1)}, u32[]{:S(2)}) copy-start(bf16[192,512]{1,0:T(8,128)(2,1)} %get-tuple-element.112.own) | copy-start | bytes 589828
  6.7 4.4 %copy-start.3 = (s32[2]{0:T(128)S(1)}, s32[2]{0:T(128)}, u32[]{:S(2)}) copy-start(s32[2]{0:T(128)} %get-tuple-element.111.kinds.bucket_ref) | copy-start | bytes 28
  6.7 11.6 %slice-start.3 = ((s8[4718592]{0:T(1024)(128)(4,1)}), s8[524288]{0:T(1024)(128)(4,1)S(1)}, s32[]{:S(2)}) async-start(s8[4718592]{0:T(1024)(128)(4,1)} %bitcast.24), calls=%async_computation.3 | async-start | bytes 1048576
  7.3 11.1 %copy-start = (bf16[512,512]{1,0:T(8,128)(2,1)S(1)}, bf16[512,512]{1,0:T(8,128)(2,1)}, u32[]{:S(2)}) copy-start(bf16[512,512]{1,0:T(8,128)(2,1)} %wp.3) | copy-start | bytes 1572868
  7.3 11.0 %copy-start.4 = (bf16[512,512]{1,0:T(8,128)(2,1)S(1)}, bf16[512,512]{1,0:T(8,128)(2,1)}, u32[]{:S(2)}) copy-start(bf16[512,512]{1,0:T(8,128)(2,1)} %wq.1) | copy-start | bytes 1572868
  7.3 11.0 %copy-start.5 = (bf16[512,512]{1,0:T(8,128)(2,1)S(1)}, bf16[512,512]{1,0:T(8,128)(2,1)}, u32[]{:S(2)}) copy-start(bf16[512,512]{1,0:T(8,128)(2,1)} %wk.1) | copy-start | bytes 1572868
  7.3 11.0 %copy-start.6 = (bf16[512,512]{1,0:T(8,128)(2,1)S(1)}, bf16[512,512]{1,0:T(8,128)(2,1)}, u32[]{:S(2)}) copy-start(bf16[512,512]{1,0:T(8,128)(2,1)} %wv.1) | copy-start | bytes 1572868
  7.3 11.0 %collective-permute-start.3 = (bf16[192,512]{1,0:T(8,128)(2,1)S(1)}, bf16[192,512]{1,0:T(8,128)(2,1)S(1)}, u32[]{:S(2)}, u32[]{:S(2)}) collective-permute-start(bf16[192,512]{1,0:T(8,128)(2,1)S(1)} %get-tuple-element.118.own), channel_id=1, source_target_pairs={{0,1},{1,0},{2,3},{3,2},{4,5},{5,4},{6,7},{7,6},{8,9},{9,8},{10,11... | collective-permute-start | bytes 589832 | tf_op jit(solution)/shard_map/ppermute | solution.py:638
  7.9 10.4 %collective-permute-start.4 = (bf16[160,512]{1,0:T(8,128)(2,1)S(1)}, bf16[160,512]{1,0:T(8,128)(2,1)S(1)}, u32[]{:S(2)}, u32[]{:S(2)}) collective-permute-start(bf16[160,512]{1,0:T(8,128)(2,1)S(1)} %get-tuple-element.119), channel_id=1, source_target_pairs={{0,2},{1,3},{2,0},{3,1},{4,6},{5,7},{6,4},{7,5},{8,10},{9,11},{10,... | collective-permute-start | bytes 491528 | tf_op jit(solution)/shard_map/ppermute | solution.py:641
  8.0 10.3 %collective-permute-start.5 = (bf16[160,512]{1,0:T(8,128)(2,1)S(1)}, bf16[160,512]{1,0:T(8,128)(2,1)S(1)}, u32[]{:S(2)}, u32[]{:S(2)}) collective-permute-start(bf16[160,512]{1,0:T(8,128)(2,1)S(1)} %get-tuple-element.119), channel_id=1, source_target_pairs={{0,3},{1,2},{2,1},{3,0},{4,7},{5,6},{6,5},{7,4},{8,11},{9,10},{10,... | collective-permute-start | bytes 491528 | tf_op jit(solution)/shard_map/ppermute | solution.py:674
  9.5 1.6 %collective-permute-start.2 = (bf16[128,512]{1,0:T(8,128)(2,1)S(1)}, bf16[128,512]{1,0:T(8,128)(2,1)S(1)}, u32[]{:S(2)}, u32[]{:S(2)}) collective-permute-start(bf16[128,512]{1,0:T(8,128)(2,1)S(1)} %collective-permute-done.1.received), channel_id=1, source_target_pairs={{0,1},{1,0},{2,3},{3,2},{4,5},{5,4},{6,7},{7,6},{8,9},{9,8},{10,11... | collective-permute-start | bytes 393224 | tf_op jit(solution)/shard_map/ppermute | solution.py:638
  16.4 14.4 %collective-permute-start.6 = (bf16[2,256,512]{2,1,0:T(8,128)(2,1)S(1)}, bf16[2,256,512]{2,1,0:T(8,128)(2,1)S(1)}, u32[]{:S(2)}, u32[]{:S(2)}) collective-permute-start(bf16[2,256,512]{2,1,0:T(8,128)(2,1)S(1)} %get-tuple-element.125), channel_id=1, source_target_pairs={{0,2},{1,3},{2,0},{3,1},{4,6},{5,7},{6,4},{7,5},{8,10},{9,11},{10,... | collective-permute-start | bytes 1572872 | tf_op jit(solution)/shard_map/ppermute | solution.py:641
  28.0 7.2 %collective-permute-start.8 = (bf16[512,128]{1,0:T(8,128)(2,1)S(1)}, bf16[512,128]{1,0:T(8,128)(2,1)S(1)}, u32[]{:S(2)}, u32[]{:S(2)}) collective-permute-start(bf16[512,128]{1,0:T(8,128)(2,1)S(1)} %get-tuple-element.129), channel_id=1, source_target_pairs={{0,2},{1,3},{2,0},{3,1},{4,6},{5,7},{6,4},{7,5},{8,10},{9,11},{10,... | collective-permute-start | bytes 393224 | tf_op jit(solution)/shard_map/ppermute | solution.py:641
  28.3 13.8 %collective-permute-start.9 = (bf16[4,256,256]{2,1,0:T(8,128)(2,1)S(1)}, bf16[4,256,256]{2,1,0:T(8,128)(2,1)S(1)}, u32[]{:S(2)}, u32[]{:S(2)}) collective-permute-start(bf16[4,256,256]{2,1,0:T(8,128)(2,1)S(1)} %get-tuple-element.135), channel_id=1, source_target_pairs={{0,4},{4,0},{8,12},{12,8},{16,20},{20,16},{24,28},{28,24},{1,5},{5... | collective-permute-start | bytes 1572872 | tf_op jit(solution)/shard_map/ppermute | solution.py:644
  30.8 4.3 %collective-permute-start.7 = (bf16[2,256,512]{2,1,0:T(8,128)(2,1)S(1)}, bf16[2,256,512]{2,1,0:T(8,128)(2,1)S(1)}, u32[]{:S(2)}, u32[]{:S(2)}) collective-permute-start(bf16[2,256,512]{2,1,0:T(8,128)(2,1)S(1)} %collective-permute-done.6.half_t), channel_id=1, source_target_pairs={{0,1},{1,0},{2,3},{3,2},{4,5},{5,4},{6,7},{7,6},{8,9},{9,8},{10,11... | collective-permute-start | bytes 1572872 | tf_op jit(solution)/shard_map/ppermute | solution.py:638
  38.5 18.6 %collective-permute-start.14 = (bf16[4,576,128]{2,1,0:T(8,128)(2,1)S(1)}, bf16[4,576,128]{2,1,0:T(8,128)(2,1)S(1)}, u32[]{:S(2)}, u32[]{:S(2)}) collective-permute-start(bf16[4,576,128]{2,1,0:T(8,128)(2,1)S(1)} %get-tuple-element.133), channel_id=1, source_target_pairs={{0,4},{4,0},{8,12},{12,8},{16,20},{20,16},{24,28},{28,24},{1,5},{5... | collective-permute-start | bytes 1769480 | tf_op jit(solution)/shard_map/ppermute | solution.py:644
  42.2 5.9 %collective-permute-start.10 = (bf16[512,128]{1,0:T(8,128)(2,1)S(1)}, bf16[512,128]{1,0:T(8,128)(2,1)S(1)}, u32[]{:S(2)}, u32[]{:S(2)}) collective-permute-start(bf16[512,128]{1,0:T(8,128)(2,1)S(1)} %get-tuple-element.142), channel_id=1, source_target_pairs={{0,2},{1,3},{2,0},{3,1},{4,6},{5,7},{6,4},{7,5},{8,10},{9,11},{10,... | collective-permute-start | bytes 393224 | tf_op jit(solution)/shard_map/ppermute | solution.py:641
  43.7 8.8 %collective-permute-start.13 = (bf16[1,256,256]{2,1,0:T(8,128)(2,1)S(1)}, bf16[1,256,256]{2,1,0:T(8,128)(2,1)S(1)}, u32[]{:S(2)}, u32[]{:S(2)}) collective-permute-start(bf16[1,256,256]{2,1,0:T(8,128)(2,1)S(1)} %get-tuple-element.139), channel_id=1, source_target_pairs={{0,24},{4,28},{8,16},{12,20},{16,8},{20,12},{24,0},{28,4},{1,25},{... | collective-permute-start | bytes 393224 | tf_op jit(solution)/shard_map/ppermute | solution.py:644
  47.0 10.0 %collective-permute-start.12 = (bf16[1,256,256]{2,1,0:T(8,128)(2,1)S(1)}, bf16[1,256,256]{2,1,0:T(8,128)(2,1)S(1)}, u32[]{:S(2)}, u32[]{:S(2)}) collective-permute-start(bf16[1,256,256]{2,1,0:T(8,128)(2,1)S(1)} %get-tuple-element.138), channel_id=1, source_target_pairs={{0,16},{4,20},{8,24},{12,28},{16,0},{20,4},{24,8},{28,12},{1,17},{... | collective-permute-start | bytes 393224 | tf_op jit(solution)/shard_map/ppermute | solution.py:644
  47.1 10.0 %collective-permute-start.11 = (bf16[1,256,256]{2,1,0:T(8,128)(2,1)S(1)}, bf16[1,256,256]{2,1,0:T(8,128)(2,1)S(1)}, u32[]{:S(2)}, u32[]{:S(2)}) collective-permute-start(bf16[1,256,256]{2,1,0:T(8,128)(2,1)S(1)} %get-tuple-element.137), channel_id=1, source_target_pairs={{0,8},{4,12},{8,0},{12,4},{16,24},{20,28},{24,16},{28,20},{1,9},{5... | collective-permute-start | bytes 393224 | tf_op jit(solution)/shard_map/ppermute | solution.py:644
  51.2 19.9 %collective-permute-start.17 = (bf16[4,576,128]{2,1,0:T(8,128)(2,1)S(1)}, bf16[4,576,128]{2,1,0:T(8,128)(2,1)S(1)}, u32[]{:S(2)}, u32[]{:S(2)}) collective-permute-start(bf16[4,576,128]{2,1,0:T(8,128)(2,1)S(1)} %get-tuple-element.143), channel_id=1, source_target_pairs={{0,4},{4,0},{8,12},{12,8},{16,20},{20,16},{24,28},{28,24},{1,5},{5... | collective-permute-start | bytes 1769480 | tf_op jit(solution)/shard_map/ppermute | solution.py:644
  57.3 15.4 %collective-permute-start.18 = (bf16[1,576,128]{2,1,0:T(8,128)(2,1)S(1)}, bf16[1,576,128]{2,1,0:T(8,128)(2,1)S(1)}, u32[]{:S(2)}, u32[]{:S(2)}) collective-permute-start(bf16[1,576,128]{2,1,0:T(8,128)(2,1)S(1)} %get-tuple-element.149), channel_id=1, source_target_pairs={{0,8},{4,12},{8,0},{12,4},{16,24},{20,28},{24,16},{28,20},{1,9},{5... | collective-permute-start | bytes 442376 | tf_op jit(solution)/shard_map/ppermute | solution.py:644
  57.4 15.3 %collective-permute-start.19 = (bf16[1,576,128]{2,1,0:T(8,128)(2,1)S(1)}, bf16[1,576,128]{2,1,0:T(8,128)(2,1)S(1)}, u32[]{:S(2)}, u32[]{:S(2)}) collective-permute-start(bf16[1,576,128]{2,1,0:T(8,128)(2,1)S(1)} %get-tuple-element.150), channel_id=1, source_target_pairs={{0,16},{4,20},{8,24},{12,28},{16,0},{20,4},{24,8},{28,12},{1,17},{... | collective-permute-start | bytes 442376 | tf_op jit(solution)/shard_map/ppermute | solution.py:644
  60.4 12.3 %collective-permute-start.20 = (bf16[1,576,128]{2,1,0:T(8,128)(2,1)S(1)}, bf16[1,576,128]{2,1,0:T(8,128)(2,1)S(1)}, u32[]{:S(2)}, u32[]{:S(2)}) collective-permute-start(bf16[1,576,128]{2,1,0:T(8,128)(2,1)S(1)} %get-tuple-element.151), channel_id=1, source_target_pairs={{0,24},{4,28},{8,16},{12,20},{16,8},{20,12},{24,0},{28,4},{1,25},{... | collective-permute-start | bytes 442376 | tf_op jit(solution)/shard_map/ppermute | solution.py:644
  66.8 3.7 %collective-permute-start.16 = (bf16[4,16,128]{2,1,0:T(8,128)(2,1)S(1)}, bf16[4,16,128]{2,1,0:T(8,128)(2,1)S(1)}, u32[]{:S(2)}, u32[]{:S(2)}) collective-permute-start(bf16[4,16,128]{2,1,0:T(8,128)(2,1)S(1)} %get-tuple-element.162), channel_id=1, source_target_pairs={{0,4},{4,0},{8,12},{12,8},{16,20},{20,16},{24,28},{28,24},{1,5},{5... | collective-permute-start | bytes 49160 | tf_op jit(solution)/shard_map/ppermute | solution.py:644
  70.5 6.8 %collective-permute-start.23 = (bf16[256,256]{1,0:T(8,128)(2,1)S(1)}, bf16[256,256]{1,0:T(8,128)(2,1)S(1)}, u32[]{:S(2)}, u32[]{:S(2)}) collective-permute-start(bf16[256,256]{1,0:T(8,128)(2,1)S(1)} %sumroutea.1.own_ref), channel_id=1, source_target_pairs={{0,2},{1,3},{2,0},{3,1},{4,6},{5,7},{6,4},{7,5},{8,10},{9,11},{10,... | collective-permute-start | bytes 393224 | tf_op jit(solution)/shard_map/ppermute | solution.py:641
  71.1 17.4 %collective-permute-start.15 = (bf16[2,128,512]{2,1,0:T(8,128)(2,1)S(1)}, bf16[2,128,512]{2,1,0:T(8,128)(2,1)S(1)}, u32[]{:S(2)}, u32[]{:S(2)}) collective-permute-start(bf16[2,128,512]{2,1,0:T(8,128)(2,1)S(1)} %get-tuple-element.160), channel_id=1, source_target_pairs={{0,2},{1,3},{2,0},{3,1},{4,6},{5,7},{6,4},{7,5},{8,10},{9,11},{10,... | collective-permute-start | bytes 786440 | tf_op jit(solution)/shard_map/ppermute | solution.py:641
  72.8 9.8 %collective-permute-start.25 = (bf16[1,592,128]{2,1,0:T(8,128)(2,1)S(1)}, bf16[1,592,128]{2,1,0:T(8,128)(2,1)S(1)}, u32[]{:S(2)}, u32[]{:S(2)}) collective-permute-start(bf16[1,592,128]{2,1,0:T(8,128)(2,1)S(1)} %get-tuple-element.179), channel_id=1, source_target_pairs={{0,24},{4,28},{8,16},{12,20},{16,8},{20,12},{24,0},{28,4},{1,25},{... | collective-permute-start | bytes 454664 | tf_op jit(solution)/shard_map/ppermute | solution.py:644
  75.3 11.7 %collective-permute-start.24 = (bf16[1,592,128]{2,1,0:T(8,128)(2,1)S(1)}, bf16[1,592,128]{2,1,0:T(8,128)(2,1)S(1)}, u32[]{:S(2)}, u32[]{:S(2)}) collective-permute-start(bf16[1,592,128]{2,1,0:T(8,128)(2,1)S(1)} %get-tuple-element.176), channel_id=1, source_target_pairs={{0,16},{4,20},{8,24},{12,28},{16,0},{20,4},{24,8},{28,12},{1,17},{... | collective-permute-start | bytes 454664 | tf_op jit(solution)/shard_map/ppermute | solution.py:644
  75.3 11.7 %collective-permute-start.21 = (bf16[1,592,128]{2,1,0:T(8,128)(2,1)S(1)}, bf16[1,592,128]{2,1,0:T(8,128)(2,1)S(1)}, u32[]{:S(2)}, u32[]{:S(2)}) collective-permute-start(bf16[1,592,128]{2,1,0:T(8,128)(2,1)S(1)} %get-tuple-element.170), channel_id=1, source_target_pairs={{0,8},{4,12},{8,0},{12,4},{16,24},{20,28},{24,16},{28,20},{1,9},{5... | collective-permute-start | bytes 454664 | tf_op jit(solution)/shard_map/ppermute | solution.py:644
  77.3 5.2 %collective-permute-start.22 = (bf16[576,128]{1,0:T(8,128)(2,1)S(1)}, bf16[576,128]{1,0:T(8,128)(2,1)S(1)}, u32[]{:S(2)}, u32[]{:S(2)}) collective-permute-start(bf16[576,128]{1,0:T(8,128)(2,1)S(1)} %sumrouteb.1.own_ref), channel_id=1, source_target_pairs={{0,2},{1,3},{2,0},{3,1},{4,6},{5,7},{6,4},{7,5},{8,10},{9,11},{10,... | collective-permute-start | bytes 442376 | tf_op jit(solution)/shard_map/ppermute | solution.py:641
  87.1 5.9 %collective-permute-start.26 = (bf16[592,128]{1,0:T(8,128)(2,1)S(1)}, bf16[592,128]{1,0:T(8,128)(2,1)S(1)}, u32[]{:S(2)}, u32[]{:S(2)}) collective-permute-start(bf16[592,128]{1,0:T(8,128)(2,1)S(1)} %sumroutec.1.own_ref), channel_id=1, source_target_pairs={{0,2},{1,3},{2,0},{3,1},{4,6},{5,7},{6,4},{7,5},{8,10},{9,11},{10,... | collective-permute-start | bytes 454664 | tf_op jit(solution)/shard_map/ppermute | solution.py:641
  87.9 3.4 %collective-permute-start.28 = (bf16[576,128]{1,0:T(8,128)(2,1)S(1)}, bf16[576,128]{1,0:T(8,128)(2,1)S(1)}, u32[]{:S(2)}, u32[]{:S(2)}) collective-permute-start(bf16[576,128]{1,0:T(8,128)(2,1)S(1)} %sumrouteb.1.own_ref), channel_id=1, source_target_pairs={{0,1},{1,0},{2,3},{3,2},{4,5},{5,4},{6,7},{7,6},{8,9},{9,8},{10,11... | collective-permute-start | bytes 442376 | tf_op jit(solution)/shard_map/ppermute | solution.py:638
  87.9 3.4 %collective-permute-start.29 = (bf16[576,128]{1,0:T(8,128)(2,1)S(1)}, bf16[576,128]{1,0:T(8,128)(2,1)S(1)}, u32[]{:S(2)}, u32[]{:S(2)}) collective-permute-start(bf16[576,128]{1,0:T(8,128)(2,1)S(1)} %collective-permute-done.22.far_ref), channel_id=1, source_target_pairs={{0,1},{1,0},{2,3},{3,2},{4,5},{5,4},{6,7},{7,6},{8,9},{9,8},{10,11... | collective-permute-start | bytes 442376 | tf_op jit(solution)/shard_map/ppermute | solution.py:638
  88.4 2.0 %collective-permute-start.30 = (bf16[256,256]{1,0:T(8,128)(2,1)S(1)}, bf16[256,256]{1,0:T(8,128)(2,1)S(1)}, u32[]{:S(2)}, u32[]{:S(2)}) collective-permute-start(bf16[256,256]{1,0:T(8,128)(2,1)S(1)} %sumroutea.1.own_ref), channel_id=1, source_target_pairs={{0,1},{1,0},{2,3},{3,2},{4,5},{5,4},{6,7},{7,6},{8,9},{9,8},{10,11... | collective-permute-start | bytes 393224 | tf_op jit(solution)/shard_map/ppermute | solution.py:638
  88.4 2.0 %collective-permute-start.31 = (bf16[256,256]{1,0:T(8,128)(2,1)S(1)}, bf16[256,256]{1,0:T(8,128)(2,1)S(1)}, u32[]{:S(2)}, u32[]{:S(2)}) collective-permute-start(bf16[256,256]{1,0:T(8,128)(2,1)S(1)} %collective-permute-done.23.far_ref), channel_id=1, source_target_pairs={{0,1},{1,0},{2,3},{3,2},{4,5},{5,4},{6,7},{7,6},{8,9},{9,8},{10,11... | collective-permute-start | bytes 393224 | tf_op jit(solution)/shard_map/ppermute | solution.py:638
  90.5 2.6 %collective-permute-start.27 = (bf16[592,128]{1,0:T(8,128)(2,1)S(1)}, bf16[592,128]{1,0:T(8,128)(2,1)S(1)}, u32[]{:S(2)}, u32[]{:S(2)}) collective-permute-start(bf16[592,128]{1,0:T(8,128)(2,1)S(1)} %sumroutec.1.own_ref), channel_id=1, source_target_pairs={{0,1},{1,0},{2,3},{3,2},{4,5},{5,4},{6,7},{7,6},{8,9},{9,8},{10,11... | collective-permute-start | bytes 454664 | tf_op jit(solution)/shard_map/ppermute | solution.py:638
  93.0 1.4 %collective-permute-start.32 = (bf16[592,128]{1,0:T(8,128)(2,1)S(1)}, bf16[592,128]{1,0:T(8,128)(2,1)S(1)}, u32[]{:S(2)}, u32[]{:S(2)}) collective-permute-start(bf16[592,128]{1,0:T(8,128)(2,1)S(1)} %collective-permute-done.26.far_ref), channel_id=1, source_target_pairs={{0,1},{1,0},{2,3},{3,2},{4,5},{5,4},{6,7},{7,6},{8,9},{9,8},{10,11... | collective-permute-start | bytes 454664 | tf_op jit(solution)/shard_map/ppermute | solution.py:638

commit v15 on v7

--- a/solution.py
+++ b/solution.py
@@ -254,15 +254,18 @@
     pack(x_ref, home, home_x, 6)
 
 
-def stack_kernel(kinds, cot_ref, *refs):
+def stack_kernel(kinds, cot_ref, wq, wk, wv, *refs):
     h, home, away = place(kinds)
-    out_ref, away_c, home_c = refs[-3:]
-    count = len(refs) - 3
+    out_ref, away_c, home_c, wide_ref = refs[-4:]
+    count = len(refs) - 4
     for index, ref in enumerate(refs[:count]):
         out_ref[index : index + 1, :] = ref[...]
     out_ref[count:, :] = jnp.zeros((VECS - count, out_ref.shape[1]), F32)
     pack(cot_ref, away, away_c, 4)
     pack(cot_ref, home, home_c, 6)
+    channels = wq.shape[1]
+    for index, ref in enumerate((wq, wk, wv)):
+        wide_ref[:, index * channels : (index + 1) * channels] = ref[...]
 
 
 def first_kernel(
@@ -301,7 +304,7 @@
 
 def second_kernel(
     bucket_ref, image_ref, act2_ref, own, partner, received, partner_received, vecs,
-    weight2, wq, wk, wv, wp,
+    weight2, wide_ref, wp,
     middle_ref, mixed_ref, grad2_ref, grad_middle_ref, attn_keep, attn_send, vec_ref,
     block_keep, block_send,
     shift_ref, full_ref, grads_ref, sum_ref,
@@ -320,8 +323,7 @@
     mean3, inverse3 = norm_stats(middle, mask, group_size)
     normal = (middle - mean3) * inverse3
     normed = (normal * vec(vecs, GAIN3) + vec(vecs, SHIFT3)).astype(BF16)
-    wide = jnp.concatenate([wq[...], wk[...], wv[...]], axis=1)
-    joint = mm(normed, wide)
+    joint = mm(normed, wide_ref[...])
     queries = (joint[:, 0:channels] + vec(vecs, QB)).astype(BF16)
     keys = joint[:, channels : 2 * channels].astype(BF16)
     values = (joint[:, 2 * channels :] + vec(vecs, VB)).astype(BF16)
@@ -348,7 +350,7 @@
     grads_ref[:, channels : 2 * channels] = grad_keys
     grads_ref[:, 2 * channels : 3 * channels] = grad_values
     grads_ref[:, 3 * channels : 4 * channels] = grad_rows
-    grad_normed = mm_nt(grads_ref[:, 0 : 3 * channels], wide)
+    grad_normed = mm_nt(grads_ref[:, 0 : 3 * channels], wide_ref[...])
     grad_in, gain_grad, shift_grad = norm_back(
         grad_normed, normal, inverse3, mask, group_size, vec(vecs, GAIN3)
     )
@@ -665,9 +667,10 @@
     )
     recv_x = to_chip(away_x)
     core_x = to_core(home_x)
-    vecs, away_c, home_c = call(
-        stack_kernel, "stack", [((VECS, C), F32), ((160, C), BF16), ((192, C), BF16)], [], 8,
-        kinds, cotangent, *[row(v) for v in vectors],
+    vecs, away_c, home_c, wide = call(
+        stack_kernel, "stack",
+        [((VECS, C), F32), ((160, C), BF16), ((192, C), BF16), ((C, 3 * C), BF16)], [], 8,
+        kinds, cotangent, query_weight, key_weight, value_weight, *[row(v) for v in vectors],
     )
     recv_c = to_chip(away_c)
     core_c = to_core(home_c)
@@ -689,7 +692,7 @@
         [img32, img16, img16, img32, attn_out, attn_out, rows8, block, block],
         [shifts, img16, ((PIX, 4 * C), BF16), ((C, 8 * BLK), F32)], 24,
         kinds, image, act2, home_c, core_c, recv_c, core_recv_c, vecs,
-        conv2_weight, query_weight, key_weight, value_weight, proj_weight,
+        conv2_weight, wide, proj_weight,
     )
     block2_away = to_chip(block2_send)
     attn_got = to_batch(attn_send, 1)

time: 95.2 us -> 95.4 us (level)
  transfers between devices with their start and end apart: 33 -> 33, of which waited for: 10 -> 9; matrix products, arithmetic and copies ran while one was open for 0% -> 0% of each run, Pallas kernels for 37% -> 37%
where the time goes in v15:
time: 95.4 us; the launch traced here: 95.2 us
  Pallas kernels  38.8 us (41%)
  starting transfers between devices  33.1 us (35%)
  waiting for transfers between devices  21.1 us (22%)
  between operations  1.26 us (1%)
    pallas_call x19, Pallas kernels, call(): pl.pallas_call(kernel, name=name, out_shape=[jax.ShapeDtypeStruct(shape,...  38.8 us
    ppermute x13, starting transfers between devices, to_batch(): return lax.ppermute(v, 'batch', [(i, i ^ change) for i in range(batches)])  18.7 us
    ppermute x13, waiting for transfers between devices, to_batch(): return lax.ppermute(v, 'batch', [(i, i ^ change) for i in range(batches)])  11.5 us
    ppermute x9, starting transfers between devices, to_chip(): return lax.ppermute(v, 'height', [(i, i ^ 2) for i in range(4)])  10.3 us
    ppermute x9, waiting for transfers between devices, to_chip(): return lax.ppermute(v, 'height', [(i, i ^ 2) for i in range(4)])  7.64 us
    ppermute x10, starting transfers between devices, to_core(): return lax.ppermute(v, 'height', [(i, i ^ 1) for i in range(4)])  2.73 us
    ppermute x10, waiting for transfers between devices, to_core(): return lax.ppermute(v, 'height', [(i, i ^ 1) for i in range(4)])  2.01 us
  transfers between devices with their start and end apart: 33, of which 9 were waited for; matrix products, arithmetic and copies ran while one was open for 0% of the time, Pallas kernels for 37%

profile of v15, /device:TPU:0, one launch (start us, length us, event | category | flops | bytes accessed | tf_op | source)
XLA Modules:
  0.0 95.2 jit_solution(472772925616547735)
XLA Ops:
  0.8 0.0 slice-start.2
  0.8 1.9 %pack.1 = (s32[2]{0:T(128)}, bf16[128,512]{1,0:T(8,128)(2,1)}, bf16[192,512]{1,0:T(8,128)(2,1)}) custom-call(s32[2]{0:T(128)} %bucket_hbm.1, bf16[2,6,32,512]{3,2,1,0:T(8,128)(2,1)} %x_hbm.1), custom_call_target="tpu_custom_call" | custom-call | flops 10737418240 | bytes 1024 | tf_op jit(solution)/shard_map/pack/pallas_call | solution.py:588
  2.7 3.0 %collective-permute-start.1 = (bf16[128,512]{1,0:T(8,128)(2,1)}, bf16[128,512]{1,0:T(8,128)(2,1)S(1)}, u32[]{:S(2)}, u32[]{:S(2)}) collective-permute-start(bf16[128,512]{1,0:T(8,128)(2,1)} %get-tuple-element.113), channel_id=1, source_target_pairs={{0,2},{1,3},{2,0},{3,1},{4,6},{5,7},{6,4},{7,5},{8,10},{9,11},{10,... | collective-permute-start | bytes 393224 | tf_op jit(solution)/shard_map/ppermute | solution.py:643
  5.9 0.0 copy-start.1
  5.9 0.8 copy-done.1
  6.7 0.7 stack.1
  7.5 0.6 collective-permute-start.3
  8.0 0.1 collective-permute-start.4
  8.1 1.4 %collective-permute-start.5 = (bf16[160,512]{1,0:T(8,128)(2,1)S(1)}, bf16[160,512]{1,0:T(8,128)(2,1)S(1)}, u32[]{:S(2)}, u32[]{:S(2)}) collective-permute-start(bf16[160,512]{1,0:T(8,128)(2,1)S(1)} %get-tuple-element.119), channel_id=1, source_target_pairs={{0,3},{1,2},{2,1},{3,0},{4,7},{5,6},{6,5},{7,4},{8,11},{9,10},{10,... | collective-permute-start | bytes 491528 | tf_op jit(solution)/shard_map/ppermute | solution.py:677
  9.5 0.0 collective-permute-done.1.received
  9.5 0.7 collective-permute-start.2
  10.2 0.0 collective-permute-done.partner
  10.2 1.0 %collective-permute-done.2.partner_received = bf16[128,512]{1,0:T(8,128)(2,1)S(1)} collective-permute-done((bf16[128,512]{1,0:T(8,128)(2,1)S(1)}, bf16[128,512]{1,0:T(8,128)(2,1)S(1)}, u32[]{:S(2)}, u32[]{:S(2)}) %collective-permute-start.2) | collective-permute-done | bytes 131104 | tf_op jit(solution)/shard_map/ppermute | solution.py:640
  11.2 5.4 %first.1 = (bf16[512,512]{1,0:T(8,128)(2,1)S(1)}, f32[512,512]{1,0:T(8,128)S(1)}, bf16[512,512]{1,0:T(8,128)(2,1)S(1)}, f32[8,512]{1,0:T(8,128)S(1)}, bf16[512,5...) custom-call(s32[2]{0:T(128)S(1)} %copy-done.2, bf16[192,512]{1,0:T(8,128)(2,1)S(1)} %copy-done, ...), custom_call_target="tpu_custom_call" | custom-call | flops 21474836 | bytes 1024 | tf_op jit(solution)/shard_map/first/pallas_call | solution.py:588
  16.6 1.7 %collective-permute-start.6 = (bf16[2,256,512]{2,1,0:T(8,128)(2,1)S(1)}, bf16[2,256,512]{2,1,0:T(8,128)(2,1)S(1)}, u32[]{:S(2)}, u32[]{:S(2)}) collective-permute-start(bf16[2,256,512]{2,1,0:T(8,128)(2,1)S(1)} %get-tuple-element.126), channel_id=1, source_target_pairs={{0,2},{1,3},{2,0},{3,1},{4,6},{5,7},{6,4},{7,5},{8,10},{9,11},{10,... | collective-permute-start | bytes 1572872 | tf_op jit(solution)/shard_map/ppermute | solution.py:643
  18.3 0.0 collective-permute-done.4.received
  18.3 0.0 collective-permute-done.5.partner_received
  18.4 9.5 %second.1 = (f32[512,512]{1,0:T(8,128)S(1)}, bf16[512,512]{1,0:T(8,128)(2,1)S(1)}, bf16[512,512]{1,0:T(8,128)(2,1)S(1)}, f32[512,512]{1,0:T(8,128)S(1)}, bf16[4,...) custom-call(s32[2]{0:T(128)S(1)} %copy-done.2, ...), custom_call_target="tpu_custom_call" | custom-call | flops 32212254720 | bytes 1024 | tf_op jit(solution)/shard_map/second/pallas_call | solution.py:588
  27.9 0.5 collective-permute-start.8
  28.4 1.5 %collective-permute-start.9 = (bf16[4,256,256]{2,1,0:T(8,128)(2,1)S(1)}, bf16[4,256,256]{2,1,0:T(8,128)(2,1)S(1)}, u32[]{:S(2)}, u32[]{:S(2)}) collective-permute-start(bf16[4,256,256]{2,1,0:T(8,128)(2,1)S(1)} %get-tuple-element.135), channel_id=1, source_target_pairs={{0,4},{4,0},{8,12},{12,8},{16,20},{20,16},{24,28},{28,24},{1,5},{5... | collective-permute-start | bytes 1572872 | tf_op jit(solution)/shard_map/ppermute | solution.py:646
  29.9 1.4 %collective-permute-done.6.half_t = bf16[2,256,512]{2,1,0:T(8,128)(2,1)S(1)} collective-permute-done((bf16[2,256,512]{2,1,0:T(8,128)(2,1)S(1)}, bf16[2,256,512]{2,1,0:T(8,128)(2,1)S(1)}, u32[]{:S(2)}, u32[]{:S(2)}) %collective-permute-start.6) | collective-permute-done | bytes 524320 | tf_op jit(solution)/shard_map/ppermute | solution.py:643
  31.3 4.3 %third.1 = (bf16[512,512]{1,0:T(8,128)(2,1)S(1)}, bf16[512,128]{1,0:T(8,128)(2,1)S(1)}, bf16[512,128]{1,0:T(8,128)(2,1)S(1)}, f32[8,512]{1,0:T(8,128)S(1)}) custom-call(s32[2]{0:T(128)S(1)} %copy-done.2, bf16[512,512]{1,0:T(8,128)(2,1)S(1)} %get-tuple-element.121.grad2_ref, f32[512,512]{1,0:T(8,128)S(1)} %get-tuple-element.122.conv_ref, ...), custom_call_target="tpu_custom_call" | custom-call | flops 21474836480 | bytes 1024 | tf_op jit(solution)/shard_map/third/pallas_call | solution.py:588
  35.7 1.8 %collective-permute-start.10 = (bf16[512,128]{1,0:T(8,128)(2,1)S(1)}, bf16[512,128]{1,0:T(8,128)(2,1)S(1)}, u32[]{:S(2)}, u32[]{:S(2)}) collective-permute-start(bf16[512,128]{1,0:T(8,128)(2,1)S(1)} %get-tuple-element.141), channel_id=1, source_target_pairs={{0,2},{1,3},{2,0},{3,1},{4,6},{5,7},{6,4},{7,5},{8,10},{9,11},{10,... | collective-permute-start | bytes 393224 | tf_op jit(solution)/shard_map/ppermute | solution.py:643
  37.5 0.0 collective-permute-done.8.block_away
  37.5 0.0 collective-permute-done.7.partner_half_t
  37.5 3.3 %weight2.5 = (bf16[4,576,128]{2,1,0:T(8,128)(2,1)S(1)}, bf16[4,576,128]{2,1,0:T(8,128)(2,1)S(1)}) custom-call(s32[2]{0:T(128)S(1)} %copy-done.2, bf16[512,512]{1,0:T(8,128)(2,1)S(1)} %get-tuple-element.129.act_t, bf16[2,256,512]{2,1,0:T(8,128)(2,1)S(1)} %collective-permute-done.6.half_t, bf16[2,256,512]{2,1,0:T(8,128)(2,1)S(1)} %collective-permute-done.7.partner_half_t, ...), custom_call_target="tpu_custom_call" | custom-call | flops 1073741824 | bytes 1024 | tf_op jit(solution)/shard_map/weight2/pallas_call | solution.py:588
  40.8 1.4 %collective-permute-start.17 = (bf16[4,576,128]{2,1,0:T(8,128)(2,1)S(1)}, bf16[4,576,128]{2,1,0:T(8,128)(2,1)S(1)}, u32[]{:S(2)}, u32[]{:S(2)}) collective-permute-start(bf16[4,576,128]{2,1,0:T(8,128)(2,1)S(1)} %get-tuple-element.133), channel_id=1, source_target_pairs={{0,4},{4,0},{8,12},{12,8},{16,20},{20,16},{24,28},{28,24},{1,5},{5... | collective-permute-start | bytes 1769480 | tf_op jit(solution)/shard_map/ppermute | solution.py:646
  42.2 0.1 routea1.1
  42.3 3.7 %collective-permute-start.16 = (bf16[1,256,256]{2,1,0:T(8,128)(2,1)S(1)}, bf16[1,256,256]{2,1,0:T(8,128)(2,1)S(1)}, u32[]{:S(2)}, u32[]{:S(2)}) collective-permute-start(bf16[1,256,256]{2,1,0:T(8,128)(2,1)S(1)} %get-tuple-element.139), channel_id=1, source_target_pairs={{0,24},{4,28},{8,16},{12,20},{16,8},{20,12},{24,0},{28,4},{1,25},{... | collective-permute-start | bytes 393224 | tf_op jit(solution)/shard_map/ppermute | solution.py:646
  46.0 0.8 collective-permute-start.14
  46.8 3.1 %weight1.4 = (bf16[4,576,128]{2,1,0:T(8,128)(2,1)S(1)}, bf16[4,576,128]{2,1,0:T(8,128)(2,1)S(1)}) custom-call(s32[2]{0:T(128)S(1)} %copy-done.2, bf16[512,512]{1,0:T(8,128)(2,1)S(1)} %get-tuple-element.125.act_t, bf16[2,256,512]{2,1,0:T(8,128)(2,1)S(1)} %collective-permute-done.6.half_t, bf16[2,256,512]{2,1,0:T(8,128)(2,1)S(1)} %collective-permute-done.7.partner_half_t, ...), custom_call_target="tpu_custom_call" | custom-call | flops 3221225472 | bytes 1024 | tf_op jit(solution)/shard_map/weight1/pallas_call | solution.py:588
  49.9 1.5 %collective-permute-start.13 = (bf16[4,576,128]{2,1,0:T(8,128)(2,1)S(1)}, bf16[4,576,128]{2,1,0:T(8,128)(2,1)S(1)}, u32[]{:S(2)}, u32[]{:S(2)}) collective-permute-start(bf16[4,576,128]{2,1,0:T(8,128)(2,1)S(1)} %get-tuple-element.142), channel_id=1, source_target_pairs={{0,4},{4,0},{8,12},{12,8},{16,20},{20,16},{24,28},{28,24},{1,5},{5... | collective-permute-start | bytes 1769480 | tf_op jit(solution)/shard_map/ppermute | solution.py:646
  51.3 5.1 %fourth.1 = (bf16[192,512]{1,0:T(8,128)(2,1)S(1)}, bf16[192,512]{1,0:T(8,128)(2,1)S(1)}, bf16[2,128,512]{2,1,0:T(8,128)(2,1)S(1)}, bf16[4,16,128]{2,1,0:T(8,128)(2,1)S(1)}, bf16[4,16,128]{2,1,0:T(8,128)(2,1)S(1)}) custom-call(s32[2]{0:T(128)S(1)} %copy-done.2, bf16[512,512]{1,0:T(8,128)(2,1)S(1)} %get-tuple-element.143.grad1_ref, ...), custom_call_target="tpu_custom_call" | custom-call | flops 10737418240 | bytes 1024 | tf_op jit(solution)/shard_map/fourth/pallas_call | solution.py:588
  56.4 0.8 collective-permute-done.15.refs_2_
  57.2 0.1 sumroutea.1.own_ref
  57.2 0.1 routeb1.1
  57.4 1.2 %collective-permute-start.18 = (bf16[1,576,128]{2,1,0:T(8,128)(2,1)S(1)}, bf16[1,576,128]{2,1,0:T(8,128)(2,1)S(1)}, u32[]{:S(2)}, u32[]{:S(2)}) collective-permute-start(bf16[1,576,128]{2,1,0:T(8,128)(2,1)S(1)} %get-tuple-element.166), channel_id=1, source_target_pairs={{0,8},{4,12},{8,0},{12,4},{16,24},{20,28},{24,16},{28,20},{1,9},{5... | collective-permute-start | bytes 442376 | tf_op jit(solution)/shard_map/ppermute | solution.py:646
  58.6 2.6 %collective-permute-start.19 = (bf16[1,576,128]{2,1,0:T(8,128)(2,1)S(1)}, bf16[1,576,128]{2,1,0:T(8,128)(2,1)S(1)}, u32[]{:S(2)}, u32[]{:S(2)}) collective-permute-start(bf16[1,576,128]{2,1,0:T(8,128)(2,1)S(1)} %get-tuple-element.167), channel_id=1, source_target_pairs={{0,16},{4,20},{8,24},{12,28},{16,0},{20,4},{24,8},{28,12},{1,17},{... | collective-permute-start | bytes 442376 | tf_op jit(solution)/shard_map/ppermute | solution.py:646
  61.2 0.6 collective-permute-start.20
  61.9 1.1 %collective-permute-start.12 = (bf16[4,16,128]{2,1,0:T(8,128)(2,1)S(1)}, bf16[4,16,128]{2,1,0:T(8,128)(2,1)S(1)}, u32[]{:S(2)}, u32[]{:S(2)}) collective-permute-start(bf16[4,16,128]{2,1,0:T(8,128)(2,1)S(1)} %get-tuple-element.153), channel_id=1, source_target_pairs={{0,4},{4,0},{8,12},{12,8},{16,20},{20,16},{24,28},{28,24},{1,5},{5... | collective-permute-start | bytes 49160 | tf_op jit(solution)/shard_map/ppermute | solution.py:646
  62.9 6.4 %collective-permute-done.12.got_ref = bf16[4,16,128]{2,1,0:T(8,128)(2,1)S(1)} collective-permute-done((bf16[4,16,128]{2,1,0:T(8,128)(2,1)S(1)}, bf16[4,16,128]{2,1,0:T(8,128)(2,1)S(1)}, u32[]{:S(2)}, u32[]{:S(2)}) %collective-permute-start.12) | collective-permute-done | bytes 16416 | tf_op jit(solution)/shard_map/ppermute | solution.py:646
  69.3 0.3 collective-permute-start.23
  69.6 1.7 %collective-permute-start.11 = (bf16[2,128,512]{2,1,0:T(8,128)(2,1)S(1)}, bf16[2,128,512]{2,1,0:T(8,128)(2,1)S(1)}, u32[]{:S(2)}, u32[]{:S(2)}) collective-permute-start(bf16[2,128,512]{2,1,0:T(8,128)(2,1)S(1)} %get-tuple-element.151), channel_id=1, source_target_pairs={{0,2},{1,3},{2,0},{3,1},{4,6},{5,7},{6,4},{7,5},{8,10},{9,11},{10,... | collective-permute-start | bytes 786440 | tf_op jit(solution)/shard_map/ppermute | solution.py:643
  71.3 0.1 routec1.1
  71.5 0.2 collective-permute-done.19.refs_2_
  71.7 3.4 %collective-permute-start.25 = (bf16[1,592,128]{2,1,0:T(8,128)(2,1)S(1)}, bf16[1,592,128]{2,1,0:T(8,128)(2,1)S(1)}, u32[]{:S(2)}, u32[]{:S(2)}) collective-permute-start(bf16[1,592,128]{2,1,0:T(8,128)(2,1)S(1)} %get-tuple-element.179), channel_id=1, source_target_pairs={{0,24},{4,28},{8,16},{12,20},{16,8},{20,12},{24,0},{28,4},{1,25},{... | collective-permute-start | bytes 454664 | tf_op jit(solution)/shard_map/ppermute | solution.py:646
  75.0 0.3 collective-permute-start.24
  75.3 0.8 collective-permute-start.21
  76.1 0.1 sumrouteb.1.own_ref
  76.1 0.6 collective-permute-start.22
  76.7 6.1 %collective-permute-done.22.far_ref = bf16[576,128]{1,0:T(8,128)(2,1)S(1)} collective-permute-done((bf16[576,128]{1,0:T(8,128)(2,1)S(1)}, bf16[576,128]{1,0:T(8,128)(2,1)S(1)}, u32[]{:S(2)}, u32[]{:S(2)}) %collective-permute-start.22) | collective-permute-done | bytes 147488 | tf_op jit(solution)/shard_map/ppermute | solution.py:643
  82.9 4.2 %collective-permute-done.24.refs_2_ = bf16[1,592,128]{2,1,0:T(8,128)(2,1)S(1)} collective-permute-done((bf16[1,592,128]{2,1,0:T(8,128)(2,1)S(1)}, bf16[1,592,128]{2,1,0:T(8,128)(2,1)S(1)}, u32[]{:S(2)}, u32[]{:S(2)}) %collective-permute-start.24) | collective-permute-done | bytes 151584 | tf_op jit(solution)/shard_map/ppermute | solution.py:646
  87.0 0.1 sumroutec.1.own_ref
  87.1 0.6 collective-permute-start.26
  87.7 0.5 collective-permute-start.29
  88.2 0.5 collective-permute-start.31
  88.7 1.5 %unpack.1 = (bf16[2,6,32,512]{3,2,1,0:T(8,128)(2,1)}, bf16[2,6,32,512]{3,2,1,0:T(8,128)(2,1)}) custom-call(s32[2]{0:T(128)S(1)} %copy-done.2, bf16[192,512]{1,0:T(8,128)(2,1)S(1)} %get-tuple-element.149.out_own, bf16[192,512]{1,0:T(8,128)(2,1)S(1)} %get-tuple-element.150.grad_own, bf16[2,128,512]{2,1,0:T(8,128)(2,1)S(1)} %collective-permute-done.11.away_ref), custom_call_target="tpu_custom_call" | custom-call | flops 21474836 | bytes 1024 | tf_op jit(solution)/shard_map/unpack/pallas_call | solution.py:588
  90.3 0.0 collective-permute-start.27
  90.3 0.9 joina.1
  91.1 1.2 %joinb.1 = f32[576,512]{1,0:T(8,128)} custom-call(bf16[576,128]{1,0:T(8,128)(2,1)S(1)} %sumrouteb.1.own_ref, bf16[576,128]{1,0:T(8,128)(2,1)S(1)} %collective-permute-done.22.far_ref, bf16[576,128]{1,0:T(8,128)(2,1)S(1)} %collective-permute-done.28.near_ref, bf16[576,128]{1,0:T(8,128)(2,1)S(1)} %collective-permute-done.29.diagonal_ref), custom_call_target="tpu_custom_call" | custom-call | flops 21474836 | bytes 1024 | tf_op jit(solution)/shard_map/joinb/pallas_call | solution.py:588
  92.3 0.1 collective-permute-done.26.far_ref
  92.4 0.5 collective-permute-start.32
  92.8 1.0 %collective-permute-done.32.diagonal_ref = bf16[592,128]{1,0:T(8,128)(2,1)S(1)} collective-permute-done((bf16[592,128]{1,0:T(8,128)(2,1)S(1)}, bf16[592,128]{1,0:T(8,128)(2,1)S(1)}, u32[]{:S(2)}, u32[]{:S(2)}) %collective-permute-start.32) | collective-permute-done | bytes 151584 | tf_op jit(solution)/shard_map/ppermute | solution.py:640
  93.8 1.2 %joinc.1 = (f32[576,512]{1,0:T(8,128)}, f32[1,64]{1,0:T(1,128)}, f32[1,64]{1,0:T(1,128)}, f32[1,64]{1,0:T(1,128)}, f32[1,64]{1,0:T(1,128)}, /*index=5*/f32[1,64]...) custom-call(bf16[592,128]{1,0:T(8,128)(2,1)S(1)} %sumroutec.1.own_re, ...), custom_call_target="tpu_custom_call" | custom-call | flops 21474836 | bytes 1024 | tf_op jit(solution)/shard_map/joinc/pallas_call | solution.py:588
  (69 shorter events, 0.2 us)
Async XLA Ops:
  0.7 5.1 %copy-start.8 = (f32[512]{0:T(512)S(1)}, f32[512]{0:T(512)}, u32[]{:S(2)}) copy-start(f32[512]{0:T(512)} %param.22) | copy-start | bytes 6148
  0.7 5.1 %copy-start.9 = (f32[512]{0:T(512)S(1)}, f32[512]{0:T(512)}, u32[]{:S(2)}) copy-start(f32[512]{0:T(512)} %param.23) | copy-start | bytes 6148
  0.7 5.1 %copy-start.18 = (f32[512]{0:T(512)S(1)}, f32[512]{0:T(512)}, u32[]{:S(2)}) copy-start(f32[512]{0:T(512)} %param.38) | copy-start | bytes 6148
  0.7 5.1 %copy-start.10 = (f32[512]{0:T(512)S(1)}, f32[512]{0:T(512)}, u32[]{:S(2)}) copy-start(f32[512]{0:T(512)} %param.25) | copy-start | bytes 6148
  0.7 5.1 %copy-start.11 = (f32[512]{0:T(512)S(1)}, f32[512]{0:T(512)}, u32[]{:S(2)}) copy-start(f32[512]{0:T(512)} %param.26) | copy-start | bytes 6148
  0.7 5.1 %copy-start.12 = (f32[512]{0:T(512)S(1)}, f32[512]{0:T(512)}, u32[]{:S(2)}) copy-start(f32[512]{0:T(512)} %param.27) | copy-start | bytes 6148
  0.7 5.1 %copy-start.13 = (f32[512]{0:T(512)S(1)}, f32[512]{0:T(512)}, u32[]{:S(2)}) copy-start(f32[512]{0:T(512)} %param.29) | copy-start | bytes 6148
  0.7 5.1 %copy-start.14 = (f32[512]{0:T(512)S(1)}, f32[512]{0:T(512)}, u32[]{:S(2)}) copy-start(f32[512]{0:T(512)} %param.30) | copy-start | bytes 6148
  0.7 5.1 %copy-start.15 = (f32[512]{0:T(512)S(1)}, f32[512]{0:T(512)}, u32[]{:S(2)}) copy-start(f32[512]{0:T(512)} %param.31) | copy-start | bytes 6148
  0.8 5.1 %copy-start.16 = (f32[512]{0:T(512)S(1)}, f32[512]{0:T(512)}, u32[]{:S(2)}) copy-start(f32[512]{0:T(512)} %param.33) | copy-start | bytes 6148
  0.8 5.1 %copy-start.17 = (f32[512]{0:T(512)S(1)}, f32[512]{0:T(512)}, u32[]{:S(2)}) copy-start(f32[512]{0:T(512)} %param.36) | copy-start | bytes 6148
  0.8 5.1 %copy-start.3 = (bf16[512,512]{1,0:T(8,128)(2,1)S(1)}, bf16[512,512]{1,0:T(8,128)(2,1)}, u32[]{:S(2)}) copy-start(bf16[512,512]{1,0:T(8,128)(2,1)} %wq.1) | copy-start | bytes 1572868
  0.8 5.1 %copy-start.4 = (bf16[512,512]{1,0:T(8,128)(2,1)S(1)}, bf16[512,512]{1,0:T(8,128)(2,1)}, u32[]{:S(2)}) copy-start(bf16[512,512]{1,0:T(8,128)(2,1)} %wk.1) | copy-start | bytes 1572868
  0.8 5.1 %copy-start.5 = (bf16[512,512]{1,0:T(8,128)(2,1)S(1)}, bf16[512,512]{1,0:T(8,128)(2,1)}, u32[]{:S(2)}) copy-start(bf16[512,512]{1,0:T(8,128)(2,1)} %wv.1) | copy-start | bytes 1572868
  0.8 5.1 %copy-start.7 = (bf16[2,6,32,512]{3,2,1,0:T(8,128)(2,1)S(1)}, bf16[2,6,32,512]{3,2,1,0:T(8,128)(2,1)}, u32[]{:S(2)}) copy-start(bf16[2,6,32,512]{3,2,1,0:T(8,128)(2,1)} %cot_ref.1) | copy-start | bytes 1179652
  0.8 17.5 %slice-start.2 = ((s8[4718592]{0:T(1024)(128)(4,1)}), s8[524288]{0:T(1024)(128)(4,1)S(1)}, s32[]{:S(2)}) async-start(s8[4718592]{0:T(1024)(128)(4,1)} %bitcast.24), calls=%async_computation.2 | async-start | bytes 1048576
  2.7 6.7 %collective-permute-start.1 = (bf16[128,512]{1,0:T(8,128)(2,1)}, bf16[128,512]{1,0:T(8,128)(2,1)S(1)}, u32[]{:S(2)}, u32[]{:S(2)}) collective-permute-start(bf16[128,512]{1,0:T(8,128)(2,1)} %get-tuple-element.113), channel_id=1, source_target_pairs={{0,2},{1,3},{2,0},{3,1},{4,6},{5,7},{6,4},{7,5},{8,10},{9,11},{10,... | collective-permute-start | bytes 393224 | tf_op jit(solution)/shard_map/ppermute | solution.py:643
  5.8 4.4 %collective-permute-start = (bf16[192,512]{1,0:T(8,128)(2,1)}, bf16[192,512]{1,0:T(8,128)(2,1)S(1)}, u32[]{:S(2)}, u32[]{:S(2)}) collective-permute-start(bf16[192,512]{1,0:T(8,128)(2,1)} %get-tuple-element.112.own), channel_id=1, source_target_pairs={{0,1},{1,0},{2,3},{3,2},{4,5},{5,4},{6,7},{7,6},{8,9},{9,8},{10,11... | collective-permute-start | bytes 589832 | tf_op jit(solution)/shard_map/ppermute | solution.py:640
  5.8 5.4 %slice-start = ((s8[4718592]{0:T(1024)(128)(4,1)}), s8[4194304]{0:T(1024)(128)(4,1)S(1)}, s32[]{:S(2)}) async-start(s8[4718592]{0:T(1024)(128)(4,1)} %bitcast.22), calls=%async_computation | async-start | bytes 8388608
  5.9 0.8 copy-start.1
  6.7 4.4 %slice-start.1 = ((s8[4718592]{0:T(1024)(128)(4,1)}), s8[524288]{0:T(1024)(128)(4,1)S(1)}, s32[]{:S(2)}) async-start(s8[4718592]{0:T(1024)(128)(4,1)} %bitcast.22), calls=%async_computation.1 | async-start | bytes 1048576
  6.7 4.4 %copy-start = (bf16[192,512]{1,0:T(8,128)(2,1)S(1)}, bf16[192,512]{1,0:T(8,128)(2,1)}, u32[]{:S(2)}) copy-start(bf16[192,512]{1,0:T(8,128)(2,1)} %get-tuple-element.112.own) | copy-start | bytes 589828
  6.7 4.4 %copy-start.2 = (s32[2]{0:T(128)S(1)}, s32[2]{0:T(128)}, u32[]{:S(2)}) copy-start(s32[2]{0:T(128)} %get-tuple-element.111.kinds.bucket_ref) | copy-start | bytes 28
  6.7 11.6 %slice-start.3 = ((s8[4718592]{0:T(1024)(128)(4,1)}), s8[4194304]{0:T(1024)(128)(4,1)S(1)}, s32[]{:S(2)}) async-start(s8[4718592]{0:T(1024)(128)(4,1)} %bitcast.24), calls=%async_computation.3 | async-start | bytes 8388608
  7.5 10.9 %collective-permute-start.3 = (bf16[192,512]{1,0:T(8,128)(2,1)S(1)}, bf16[192,512]{1,0:T(8,128)(2,1)S(1)}, u32[]{:S(2)}, u32[]{:S(2)}) collective-permute-start(bf16[192,512]{1,0:T(8,128)(2,1)S(1)} %get-tuple-element.118.own), channel_id=1, source_target_pairs={{0,1},{1,0},{2,3},{3,2},{4,5},{5,4},{6,7},{7,6},{8,9},{9,8},{10,11... | collective-permute-start | bytes 589832 | tf_op jit(solution)/shard_map/ppermute | solution.py:640
  8.0 10.3 %collective-permute-start.4 = (bf16[160,512]{1,0:T(8,128)(2,1)S(1)}, bf16[160,512]{1,0:T(8,128)(2,1)S(1)}, u32[]{:S(2)}, u32[]{:S(2)}) collective-permute-start(bf16[160,512]{1,0:T(8,128)(2,1)S(1)} %get-tuple-element.119), channel_id=1, source_target_pairs={{0,2},{1,3},{2,0},{3,1},{4,6},{5,7},{6,4},{7,5},{8,10},{9,11},{10,... | collective-permute-start | bytes 491528 | tf_op jit(solution)/shard_map/ppermute | solution.py:643
  8.1 10.2 %collective-permute-start.5 = (bf16[160,512]{1,0:T(8,128)(2,1)S(1)}, bf16[160,512]{1,0:T(8,128)(2,1)S(1)}, u32[]{:S(2)}, u32[]{:S(2)}) collective-permute-start(bf16[160,512]{1,0:T(8,128)(2,1)S(1)} %get-tuple-element.119), channel_id=1, source_target_pairs={{0,3},{1,2},{2,1},{3,0},{4,7},{5,6},{6,5},{7,4},{8,11},{9,10},{10,... | collective-permute-start | bytes 491528 | tf_op jit(solution)/shard_map/ppermute | solution.py:677
  9.5 8.9 %copy-start.6 = (bf16[512,512]{1,0:T(8,128)(2,1)S(1)}, bf16[512,512]{1,0:T(8,128)(2,1)}, u32[]{:S(2)}) copy-start(bf16[512,512]{1,0:T(8,128)(2,1)} %wp.3) | copy-start | bytes 1572868
  9.5 1.7 %collective-permute-start.2 = (bf16[128,512]{1,0:T(8,128)(2,1)S(1)}, bf16[128,512]{1,0:T(8,128)(2,1)S(1)}, u32[]{:S(2)}, u32[]{:S(2)}) collective-permute-start(bf16[128,512]{1,0:T(8,128)(2,1)S(1)} %collective-permute-done.1.received), channel_id=1, source_target_pairs={{0,1},{1,0},{2,3},{3,2},{4,5},{5,4},{6,7},{7,6},{8,9},{9,8},{10,11... | collective-permute-start | bytes 393224 | tf_op jit(solution)/shard_map/ppermute | solution.py:640
  16.6 14.7 %collective-permute-start.6 = (bf16[2,256,512]{2,1,0:T(8,128)(2,1)S(1)}, bf16[2,256,512]{2,1,0:T(8,128)(2,1)S(1)}, u32[]{:S(2)}, u32[]{:S(2)}) collective-permute-start(bf16[2,256,512]{2,1,0:T(8,128)(2,1)S(1)} %get-tuple-element.126), channel_id=1, source_target_pairs={{0,2},{1,3},{2,0},{3,1},{4,6},{5,7},{6,4},{7,5},{8,10},{9,11},{10,... | collective-permute-start | bytes 1572872 | tf_op jit(solution)/shard_map/ppermute | solution.py:643
  27.9 9.6 %collective-permute-start.8 = (bf16[512,128]{1,0:T(8,128)(2,1)S(1)}, bf16[512,128]{1,0:T(8,128)(2,1)S(1)}, u32[]{:S(2)}, u32[]{:S(2)}) collective-permute-start(bf16[512,128]{1,0:T(8,128)(2,1)S(1)} %get-tuple-element.132), channel_id=1, source_target_pairs={{0,2},{1,3},{2,0},{3,1},{4,6},{5,7},{6,4},{7,5},{8,10},{9,11},{10,... | collective-permute-start | bytes 393224 | tf_op jit(solution)/shard_map/ppermute | solution.py:643
  28.4 13.8 %collective-permute-start.9 = (bf16[4,256,256]{2,1,0:T(8,128)(2,1)S(1)}, bf16[4,256,256]{2,1,0:T(8,128)(2,1)S(1)}, u32[]{:S(2)}, u32[]{:S(2)}) collective-permute-start(bf16[4,256,256]{2,1,0:T(8,128)(2,1)S(1)} %get-tuple-element.135), channel_id=1, source_target_pairs={{0,4},{4,0},{8,12},{12,8},{16,20},{20,16},{24,28},{28,24},{1,5},{5... | collective-permute-start | bytes 1572872 | tf_op jit(solution)/shard_map/ppermute | solution.py:646
  31.3 6.2 %collective-permute-start.7 = (bf16[2,256,512]{2,1,0:T(8,128)(2,1)S(1)}, bf16[2,256,512]{2,1,0:T(8,128)(2,1)S(1)}, u32[]{:S(2)}, u32[]{:S(2)}) collective-permute-start(bf16[2,256,512]{2,1,0:T(8,128)(2,1)S(1)} %collective-permute-done.6.half_t), channel_id=1, source_target_pairs={{0,1},{1,0},{2,3},{3,2},{4,5},{5,4},{6,7},{7,6},{8,9},{9,8},{10,11... | collective-permute-start | bytes 1572872 | tf_op jit(solution)/shard_map/ppermute | solution.py:640
  35.7 11.1 %collective-permute-start.10 = (bf16[512,128]{1,0:T(8,128)(2,1)S(1)}, bf16[512,128]{1,0:T(8,128)(2,1)S(1)}, u32[]{:S(2)}, u32[]{:S(2)}) collective-permute-start(bf16[512,128]{1,0:T(8,128)(2,1)S(1)} %get-tuple-element.141), channel_id=1, source_target_pairs={{0,2},{1,3},{2,0},{3,1},{4,6},{5,7},{6,4},{7,5},{8,10},{9,11},{10,... | collective-permute-start | bytes 393224 | tf_op jit(solution)/shard_map/ppermute | solution.py:643
  40.8 16.4 %collective-permute-start.17 = (bf16[4,576,128]{2,1,0:T(8,128)(2,1)S(1)}, bf16[4,576,128]{2,1,0:T(8,128)(2,1)S(1)}, u32[]{:S(2)}, u32[]{:S(2)}) collective-permute-start(bf16[4,576,128]{2,1,0:T(8,128)(2,1)S(1)} %get-tuple-element.133), channel_id=1, source_target_pairs={{0,4},{4,0},{8,12},{12,8},{16,20},{20,16},{24,28},{28,24},{1,5},{5... | collective-permute-start | bytes 1769480 | tf_op jit(solution)/shard_map/ppermute | solution.py:646
  42.3 14.1 %collective-permute-start.16 = (bf16[1,256,256]{2,1,0:T(8,128)(2,1)S(1)}, bf16[1,256,256]{2,1,0:T(8,128)(2,1)S(1)}, u32[]{:S(2)}, u32[]{:S(2)}) collective-permute-start(bf16[1,256,256]{2,1,0:T(8,128)(2,1)S(1)} %get-tuple-element.139), channel_id=1, source_target_pairs={{0,24},{4,28},{8,16},{12,20},{16,8},{20,12},{24,0},{28,4},{1,25},{... | collective-permute-start | bytes 393224 | tf_op jit(solution)/shard_map/ppermute | solution.py:646
  46.0 11.2 %collective-permute-start.15 = (bf16[1,256,256]{2,1,0:T(8,128)(2,1)S(1)}, bf16[1,256,256]{2,1,0:T(8,128)(2,1)S(1)}, u32[]{:S(2)}, u32[]{:S(2)}) collective-permute-start(bf16[1,256,256]{2,1,0:T(8,128)(2,1)S(1)} %get-tuple-element.138), channel_id=1, source_target_pairs={{0,16},{4,20},{8,24},{12,28},{16,0},{20,4},{24,8},{28,12},{1,17},{... | collective-permute-start | bytes 393224 | tf_op jit(solution)/shard_map/ppermute | solution.py:646
  46.0 11.2 %collective-permute-start.14 = (bf16[1,256,256]{2,1,0:T(8,128)(2,1)S(1)}, bf16[1,256,256]{2,1,0:T(8,128)(2,1)S(1)}, u32[]{:S(2)}, u32[]{:S(2)}) collective-permute-start(bf16[1,256,256]{2,1,0:T(8,128)(2,1)S(1)} %get-tuple-element.137), channel_id=1, source_target_pairs={{0,8},{4,12},{8,0},{12,4},{16,24},{20,28},{24,16},{28,20},{1,9},{5... | collective-permute-start | bytes 393224 | tf_op jit(solution)/shard_map/ppermute | solution.py:646
  49.9 19.7 %collective-permute-start.13 = (bf16[4,576,128]{2,1,0:T(8,128)(2,1)S(1)}, bf16[4,576,128]{2,1,0:T(8,128)(2,1)S(1)}, u32[]{:S(2)}, u32[]{:S(2)}) collective-permute-start(bf16[4,576,128]{2,1,0:T(8,128)(2,1)S(1)} %get-tuple-element.142), channel_id=1, source_target_pairs={{0,4},{4,0},{8,12},{12,8},{16,20},{20,16},{24,28},{28,24},{1,5},{5... | collective-permute-start | bytes 1769480 | tf_op jit(solution)/shard_map/ppermute | solution.py:646
  57.4 14.1 %collective-permute-start.18 = (bf16[1,576,128]{2,1,0:T(8,128)(2,1)S(1)}, bf16[1,576,128]{2,1,0:T(8,128)(2,1)S(1)}, u32[]{:S(2)}, u32[]{:S(2)}) collective-permute-start(bf16[1,576,128]{2,1,0:T(8,128)(2,1)S(1)} %get-tuple-element.166), channel_id=1, source_target_pairs={{0,8},{4,12},{8,0},{12,4},{16,24},{20,28},{24,16},{28,20},{1,9},{5... | collective-permute-start | bytes 442376 | tf_op jit(solution)/shard_map/ppermute | solution.py:646
  58.6 13.0 %collective-permute-start.19 = (bf16[1,576,128]{2,1,0:T(8,128)(2,1)S(1)}, bf16[1,576,128]{2,1,0:T(8,128)(2,1)S(1)}, u32[]{:S(2)}, u32[]{:S(2)}) collective-permute-start(bf16[1,576,128]{2,1,0:T(8,128)(2,1)S(1)} %get-tuple-element.167), channel_id=1, source_target_pairs={{0,16},{4,20},{8,24},{12,28},{16,0},{20,4},{24,8},{28,12},{1,17},{... | collective-permute-start | bytes 442376 | tf_op jit(solution)/shard_map/ppermute | solution.py:646
  61.2 10.5 %collective-permute-start.20 = (bf16[1,576,128]{2,1,0:T(8,128)(2,1)S(1)}, bf16[1,576,128]{2,1,0:T(8,128)(2,1)S(1)}, u32[]{:S(2)}, u32[]{:S(2)}) collective-permute-start(bf16[1,576,128]{2,1,0:T(8,128)(2,1)S(1)} %get-tuple-element.168), channel_id=1, source_target_pairs={{0,24},{4,28},{8,16},{12,20},{16,8},{20,12},{24,0},{28,4},{1,25},{... | collective-permute-start | bytes 442376 | tf_op jit(solution)/shard_map/ppermute | solution.py:646
  61.9 7.4 %collective-permute-start.12 = (bf16[4,16,128]{2,1,0:T(8,128)(2,1)S(1)}, bf16[4,16,128]{2,1,0:T(8,128)(2,1)S(1)}, u32[]{:S(2)}, u32[]{:S(2)}) collective-permute-start(bf16[4,16,128]{2,1,0:T(8,128)(2,1)S(1)} %get-tuple-element.153), channel_id=1, source_target_pairs={{0,4},{4,0},{8,12},{12,8},{16,20},{20,16},{24,28},{28,24},{1,5},{5... | collective-permute-start | bytes 49160 | tf_op jit(solution)/shard_map/ppermute | solution.py:646
  69.3 6.8 %collective-permute-start.23 = (bf16[256,256]{1,0:T(8,128)(2,1)S(1)}, bf16[256,256]{1,0:T(8,128)(2,1)S(1)}, u32[]{:S(2)}, u32[]{:S(2)}) collective-permute-start(bf16[256,256]{1,0:T(8,128)(2,1)S(1)} %sumroutea.1.own_ref), channel_id=1, source_target_pairs={{0,2},{1,3},{2,0},{3,1},{4,6},{5,7},{6,4},{7,5},{8,10},{9,11},{10,... | collective-permute-start | bytes 393224 | tf_op jit(solution)/shard_map/ppermute | solution.py:643
  69.6 18.6 %collective-permute-start.11 = (bf16[2,128,512]{2,1,0:T(8,128)(2,1)S(1)}, bf16[2,128,512]{2,1,0:T(8,128)(2,1)S(1)}, u32[]{:S(2)}, u32[]{:S(2)}) collective-permute-start(bf16[2,128,512]{2,1,0:T(8,128)(2,1)S(1)} %get-tuple-element.151), channel_id=1, source_target_pairs={{0,2},{1,3},{2,0},{3,1},{4,6},{5,7},{6,4},{7,5},{8,10},{9,11},{10,... | collective-permute-start | bytes 786440 | tf_op jit(solution)/shard_map/ppermute | solution.py:643
  71.7 11.2 %collective-permute-start.25 = (bf16[1,592,128]{2,1,0:T(8,128)(2,1)S(1)}, bf16[1,592,128]{2,1,0:T(8,128)(2,1)S(1)}, u32[]{:S(2)}, u32[]{:S(2)}) collective-permute-start(bf16[1,592,128]{2,1,0:T(8,128)(2,1)S(1)} %get-tuple-element.179), channel_id=1, source_target_pairs={{0,24},{4,28},{8,16},{12,20},{16,8},{20,12},{24,0},{28,4},{1,25},{... | collective-permute-start | bytes 454664 | tf_op jit(solution)/shard_map/ppermute | solution.py:646
  75.0 12.0 %collective-permute-start.24 = (bf16[1,592,128]{2,1,0:T(8,128)(2,1)S(1)}, bf16[1,592,128]{2,1,0:T(8,128)(2,1)S(1)}, u32[]{:S(2)}, u32[]{:S(2)}) collective-permute-start(bf16[1,592,128]{2,1,0:T(8,128)(2,1)S(1)} %get-tuple-element.176), channel_id=1, source_target_pairs={{0,16},{4,20},{8,24},{12,28},{16,0},{20,4},{24,8},{28,12},{1,17},{... | collective-permute-start | bytes 454664 | tf_op jit(solution)/shard_map/ppermute | solution.py:646
  75.3 11.8 %collective-permute-start.21 = (bf16[1,592,128]{2,1,0:T(8,128)(2,1)S(1)}, bf16[1,592,128]{2,1,0:T(8,128)(2,1)S(1)}, u32[]{:S(2)}, u32[]{:S(2)}) collective-permute-start(bf16[1,592,128]{2,1,0:T(8,128)(2,1)S(1)} %get-tuple-element.169), channel_id=1, source_target_pairs={{0,8},{4,12},{8,0},{12,4},{16,24},{20,28},{24,16},{28,20},{1,9},{5... | collective-permute-start | bytes 454664 | tf_op jit(solution)/shard_map/ppermute | solution.py:646
  76.1 6.7 %collective-permute-start.22 = (bf16[576,128]{1,0:T(8,128)(2,1)S(1)}, bf16[576,128]{1,0:T(8,128)(2,1)S(1)}, u32[]{:S(2)}, u32[]{:S(2)}) collective-permute-start(bf16[576,128]{1,0:T(8,128)(2,1)S(1)} %sumrouteb.1.own_ref), channel_id=1, source_target_pairs={{0,2},{1,3},{2,0},{3,1},{4,6},{5,7},{6,4},{7,5},{8,10},{9,11},{10,... | collective-permute-start | bytes 442376 | tf_op jit(solution)/shard_map/ppermute | solution.py:643
  87.1 5.3 %collective-permute-start.26 = (bf16[592,128]{1,0:T(8,128)(2,1)S(1)}, bf16[592,128]{1,0:T(8,128)(2,1)S(1)}, u32[]{:S(2)}, u32[]{:S(2)}) collective-permute-start(bf16[592,128]{1,0:T(8,128)(2,1)S(1)} %sumroutec.1.own_ref), channel_id=1, source_target_pairs={{0,2},{1,3},{2,0},{3,1},{4,6},{5,7},{6,4},{7,5},{8,10},{9,11},{10,... | collective-permute-start | bytes 454664 | tf_op jit(solution)/shard_map/ppermute | solution.py:643
  87.7 3.4 %collective-permute-start.28 = (bf16[576,128]{1,0:T(8,128)(2,1)S(1)}, bf16[576,128]{1,0:T(8,128)(2,1)S(1)}, u32[]{:S(2)}, u32[]{:S(2)}) collective-permute-start(bf16[576,128]{1,0:T(8,128)(2,1)S(1)} %sumrouteb.1.own_ref), channel_id=1, source_target_pairs={{0,1},{1,0},{2,3},{3,2},{4,5},{5,4},{6,7},{7,6},{8,9},{9,8},{10,11... | collective-permute-start | bytes 442376 | tf_op jit(solution)/shard_map/ppermute | solution.py:640
  87.7 3.4 %collective-permute-start.29 = (bf16[576,128]{1,0:T(8,128)(2,1)S(1)}, bf16[576,128]{1,0:T(8,128)(2,1)S(1)}, u32[]{:S(2)}, u32[]{:S(2)}) collective-permute-start(bf16[576,128]{1,0:T(8,128)(2,1)S(1)} %collective-permute-done.22.far_ref), channel_id=1, source_target_pairs={{0,1},{1,0},{2,3},{3,2},{4,5},{5,4},{6,7},{7,6},{8,9},{9,8},{10,11... | collective-permute-start | bytes 442376 | tf_op jit(solution)/shard_map/ppermute | solution.py:640
  88.2 2.0 %collective-permute-start.30 = (bf16[256,256]{1,0:T(8,128)(2,1)S(1)}, bf16[256,256]{1,0:T(8,128)(2,1)S(1)}, u32[]{:S(2)}, u32[]{:S(2)}) collective-permute-start(bf16[256,256]{1,0:T(8,128)(2,1)S(1)} %sumroutea.1.own_ref), channel_id=1, source_target_pairs={{0,1},{1,0},{2,3},{3,2},{4,5},{5,4},{6,7},{7,6},{8,9},{9,8},{10,11... | collective-permute-start | bytes 393224 | tf_op jit(solution)/shard_map/ppermute | solution.py:640
  88.2 2.0 %collective-permute-start.31 = (bf16[256,256]{1,0:T(8,128)(2,1)S(1)}, bf16[256,256]{1,0:T(8,128)(2,1)S(1)}, u32[]{:S(2)}, u32[]{:S(2)}) collective-permute-start(bf16[256,256]{1,0:T(8,128)(2,1)S(1)} %collective-permute-done.23.far_ref), channel_id=1, source_target_pairs={{0,1},{1,0},{2,3},{3,2},{4,5},{5,4},{6,7},{7,6},{8,9},{9,8},{10,11... | collective-permute-start | bytes 393224 | tf_op jit(solution)/shard_map/ppermute | solution.py:640
  90.3 2.6 %collective-permute-start.27 = (bf16[592,128]{1,0:T(8,128)(2,1)S(1)}, bf16[592,128]{1,0:T(8,128)(2,1)S(1)}, u32[]{:S(2)}, u32[]{:S(2)}) collective-permute-start(bf16[592,128]{1,0:T(8,128)(2,1)S(1)} %sumroutec.1.own_ref), channel_id=1, source_target_pairs={{0,1},{1,0},{2,3},{3,2},{4,5},{5,4},{6,7},{7,6},{8,9},{9,8},{10,11... | collective-permute-start | bytes 454664 | tf_op jit(solution)/shard_map/ppermute | solution.py:640
  92.4 1.5 %collective-permute-start.32 = (bf16[592,128]{1,0:T(8,128)(2,1)S(1)}, bf16[592,128]{1,0:T(8,128)(2,1)S(1)}, u32[]{:S(2)}, u32[]{:S(2)}) collective-permute-start(bf16[592,128]{1,0:T(8,128)(2,1)S(1)} %collective-permute-done.26.far_ref), channel_id=1, source_target_pairs={{0,1},{1,0},{2,3},{3,2},{4,5},{5,4},{6,7},{7,6},{8,9},{9,8},{10,11... | collective-permute-start | bytes 454664 | tf_op jit(solution)/shard_map/ppermute | solution.py:640

commit v16 on v14

--- a/solution.py
+++ b/solution.py
@@ -700,6 +700,7 @@
         [shifts, img32], 14,
         kinds, grad2, conv, stats, vecs, conv2_weight,
     )
+    block1_away = to_chip(block1_send)
 
     def weight_grad(name, act_t, index, own, away):
         return call(
@@ -743,7 +744,6 @@
         return shard, far, near, to_core(after(far, *between))
 
     parts_a, got_a = spread("routea", 1, after(attn_keep, send2), attn_got)
-    block1_away = to_chip(after(block1_send, *parts_a))
     keep1, send1 = weight_grad("weight1", act1_t, 0, after(block1, *parts_a), block1_away)
     got1 = to_batch(send1, 1)
     shard_a = finish("routea", parts_a, [after(g, send1) for g in got_a])

time: 95.9 us -> 96.4 us (level)
  no operation moved by 1% of the time
where the time goes in v16:
time: 96.4 us; the launch traced here: 96.2 us
  Pallas kernels  38.6 us (40%)
  starting transfers between devices  33.1 us (34%)
  waiting for transfers between devices  22.3 us (23%)
  between operations  1.3 us (1%)
    pallas_call x19, Pallas kernels, call(): pl.pallas_call(kernel, name=name, out_shape=[jax.ShapeDtypeStruct(shape,...  38.6 us
    ppermute x13, starting transfers between devices, to_batch(): return lax.ppermute(v, 'batch', [(i, i ^ change) for i in range(batches)])  19.6 us
    ppermute x13, waiting for transfers between devices, to_batch(): return lax.ppermute(v, 'batch', [(i, i ^ change) for i in range(batches)])  13.5 us
    ppermute x9, starting transfers between devices, to_chip(): return lax.ppermute(v, 'height', [(i, i ^ 2) for i in range(4)])  9.78 us
    ppermute x9, waiting for transfers between devices, to_chip(): return lax.ppermute(v, 'height', [(i, i ^ 2) for i in range(4)])  6.64 us
    ppermute x10, starting transfers between devices, to_core(): return lax.ppermute(v, 'height', [(i, i ^ 1) for i in range(4)])  2.39 us
    ppermute x10, waiting for transfers between devices, to_core(): return lax.ppermute(v, 'height', [(i, i ^ 1) for i in range(4)])  2.17 us
  transfers between devices with their start and end apart: 33, of which 10 were waited for; matrix products, arithmetic and copies ran while one was open for 0% of the time, Pallas kernels for 37%

profile of v16, /device:TPU:0, one launch (start us, length us, event | category | flops | bytes accessed | tf_op | source)
XLA Modules:
  0.0 96.2 jit_solution(17732374442632033254)
XLA Ops:
  0.8 0.0 slice-start
  0.8 0.0 slice-start.2
  0.8 1.9 %pack.1 = (s32[2]{0:T(128)}, bf16[128,512]{1,0:T(8,128)(2,1)}, bf16[192,512]{1,0:T(8,128)(2,1)}) custom-call(s32[2]{0:T(128)} %bucket_hbm.1, bf16[2,6,32,512]{3,2,1,0:T(8,128)(2,1)} %x_hbm.1), custom_call_target="tpu_custom_call" | custom-call | flops 10737418240 | bytes 1024 | tf_op jit(solution)/shard_map/pack/pallas_call | solution.py:586
  2.7 3.0 %collective-permute-start.1 = (bf16[128,512]{1,0:T(8,128)(2,1)}, bf16[128,512]{1,0:T(8,128)(2,1)S(1)}, u32[]{:S(2)}, u32[]{:S(2)}) collective-permute-start(bf16[128,512]{1,0:T(8,128)(2,1)} %get-tuple-element.112), channel_id=1, source_target_pairs={{0,2},{1,3},{2,0},{3,1},{4,6},{5,7},{6,4},{7,5},{8,10},{9,11},{10,... | collective-permute-start | bytes 393224 | tf_op jit(solution)/shard_map/ppermute | solution.py:641
  5.9 0.0 copy-start.2
  5.9 0.8 copy-done.2
  6.7 0.6 stack.1
  7.3 0.0 copy-start
  7.3 0.0 copy-start.4
  7.3 0.0 copy-start.5
  7.3 0.0 copy-start.6
  7.3 0.6 collective-permute-start.3
  7.9 0.1 collective-permute-start.4
  8.0 1.4 %collective-permute-start.5 = (bf16[160,512]{1,0:T(8,128)(2,1)S(1)}, bf16[160,512]{1,0:T(8,128)(2,1)S(1)}, u32[]{:S(2)}, u32[]{:S(2)}) collective-permute-start(bf16[160,512]{1,0:T(8,128)(2,1)S(1)} %get-tuple-element.118), channel_id=1, source_target_pairs={{0,3},{1,2},{2,1},{3,0},{4,7},{5,6},{6,5},{7,4},{8,11},{9,10},{10,... | collective-permute-start | bytes 491528 | tf_op jit(solution)/shard_map/ppermute | solution.py:674
  9.3 0.1 collective-permute-done.1.received
  9.5 0.6 collective-permute-start.2
  10.1 0.0 collective-permute-done.partner
  10.1 1.0 %collective-permute-done.2.partner_received = bf16[128,512]{1,0:T(8,128)(2,1)S(1)} collective-permute-done((bf16[128,512]{1,0:T(8,128)(2,1)S(1)}, bf16[128,512]{1,0:T(8,128)(2,1)S(1)}, u32[]{:S(2)}, u32[]{:S(2)}) %collective-permute-start.2) | collective-permute-done | bytes 131104 | tf_op jit(solution)/shard_map/ppermute | solution.py:638
  11.1 5.4 %first.1 = (bf16[512,512]{1,0:T(8,128)(2,1)S(1)}, f32[512,512]{1,0:T(8,128)S(1)}, bf16[512,512]{1,0:T(8,128)(2,1)S(1)}, f32[8,512]{1,0:T(8,128)S(1)}, bf16[512,5...) custom-call(s32[2]{0:T(128)S(1)} %copy-done.3, bf16[192,512]{1,0:T(8,128)(2,1)S(1)} %copy-done.1, ...), custom_call_target="tpu_custom_call" | custom-call | flops 21474836 | bytes 1024 | tf_op jit(solution)/shard_map/first/pallas_call | solution.py:586
  16.4 1.9 %collective-permute-start.6 = (bf16[2,256,512]{2,1,0:T(8,128)(2,1)S(1)}, bf16[2,256,512]{2,1,0:T(8,128)(2,1)S(1)}, u32[]{:S(2)}, u32[]{:S(2)}) collective-permute-start(bf16[2,256,512]{2,1,0:T(8,128)(2,1)S(1)} %get-tuple-element.124), channel_id=1, source_target_pairs={{0,2},{1,3},{2,0},{3,1},{4,6},{5,7},{6,4},{7,5},{8,10},{9,11},{10,... | collective-permute-start | bytes 1572872 | tf_op jit(solution)/shard_map/ppermute | solution.py:641
  18.4 9.6 %second.1 = (f32[512,512]{1,0:T(8,128)S(1)}, bf16[512,512]{1,0:T(8,128)(2,1)S(1)}, bf16[512,512]{1,0:T(8,128)(2,1)S(1)}, f32[512,512]{1,0:T(8,128)S(1)}, bf16[4,...) custom-call(s32[2]{0:T(128)S(1)} %copy-done.3, ...), custom_call_target="tpu_custom_call" | custom-call | flops 32212254720 | bytes 1024 | tf_op jit(solution)/shard_map/second/pallas_call | solution.py:586
  28.0 0.3 collective-permute-start.8
  28.3 1.5 %collective-permute-start.9 = (bf16[4,256,256]{2,1,0:T(8,128)(2,1)S(1)}, bf16[4,256,256]{2,1,0:T(8,128)(2,1)S(1)}, u32[]{:S(2)}, u32[]{:S(2)}) collective-permute-start(bf16[4,256,256]{2,1,0:T(8,128)(2,1)S(1)} %get-tuple-element.134), channel_id=1, source_target_pairs={{0,4},{4,0},{8,12},{12,8},{16,20},{20,16},{24,28},{28,24},{1,5},{5... | collective-permute-start | bytes 1572872 | tf_op jit(solution)/shard_map/ppermute | solution.py:644
  29.8 1.1 %collective-permute-done.6.half_t = bf16[2,256,512]{2,1,0:T(8,128)(2,1)S(1)} collective-permute-done((bf16[2,256,512]{2,1,0:T(8,128)(2,1)S(1)}, bf16[2,256,512]{2,1,0:T(8,128)(2,1)S(1)}, u32[]{:S(2)}, u32[]{:S(2)}) %collective-permute-start.6) | collective-permute-done | bytes 524320 | tf_op jit(solution)/shard_map/ppermute | solution.py:641
  30.8 4.3 %third.1 = (bf16[512,512]{1,0:T(8,128)(2,1)S(1)}, bf16[512,128]{1,0:T(8,128)(2,1)S(1)}, bf16[512,128]{1,0:T(8,128)(2,1)S(1)}, f32[8,512]{1,0:T(8,128)S(1)}) custom-call(s32[2]{0:T(128)S(1)} %copy-done.3, bf16[512,512]{1,0:T(8,128)(2,1)S(1)} %get-tuple-element.119.grad2_ref, f32[512,512]{1,0:T(8,128)S(1)} %get-tuple-element.120.conv_ref, ...), custom_call_target="tpu_custom_call" | custom-call | flops 21474836480 | bytes 1024 | tf_op jit(solution)/shard_map/third/pallas_call | solution.py:586
  35.2 3.3 %weight2.5 = (bf16[4,576,128]{2,1,0:T(8,128)(2,1)S(1)}, bf16[4,576,128]{2,1,0:T(8,128)(2,1)S(1)}) custom-call(s32[2]{0:T(128)S(1)} %copy-done.3, bf16[512,512]{1,0:T(8,128)(2,1)S(1)} %get-tuple-element.123.act_t, bf16[2,256,512]{2,1,0:T(8,128)(2,1)S(1)} %collective-permute-done.6.half_t, bf16[2,256,512]{2,1,0:T(8,128)(2,1)S(1)} %collective-permute-done.7.partner_half_t, ...), custom_call_target="tpu_custom_call" | custom-call | flops 1073741824 | bytes 1024 | tf_op jit(solution)/shard_map/weight2/pallas_call | solution.py:586
  38.5 1.8 %collective-permute-start.14 = (bf16[4,576,128]{2,1,0:T(8,128)(2,1)S(1)}, bf16[4,576,128]{2,1,0:T(8,128)(2,1)S(1)}, u32[]{:S(2)}, u32[]{:S(2)}) collective-permute-start(bf16[4,576,128]{2,1,0:T(8,128)(2,1)S(1)} %get-tuple-element.132), channel_id=1, source_target_pairs={{0,4},{4,0},{8,12},{12,8},{16,20},{20,16},{24,28},{28,24},{1,5},{5... | collective-permute-start | bytes 1769480 | tf_op jit(solution)/shard_map/ppermute | solution.py:644
  40.3 1.8 %collective-permute-start.10 = (bf16[512,128]{1,0:T(8,128)(2,1)S(1)}, bf16[512,128]{1,0:T(8,128)(2,1)S(1)}, u32[]{:S(2)}, u32[]{:S(2)}) collective-permute-start(bf16[512,128]{1,0:T(8,128)(2,1)S(1)} %get-tuple-element.140), channel_id=1, source_target_pairs={{0,2},{1,3},{2,0},{3,1},{4,6},{5,7},{6,4},{7,5},{8,10},{9,11},{10,... | collective-permute-start | bytes 393224 | tf_op jit(solution)/shard_map/ppermute | solution.py:641
  42.1 0.1 routea1.1
  42.2 3.7 %collective-permute-start.13 = (bf16[1,256,256]{2,1,0:T(8,128)(2,1)S(1)}, bf16[1,256,256]{2,1,0:T(8,128)(2,1)S(1)}, u32[]{:S(2)}, u32[]{:S(2)}) collective-permute-start(bf16[1,256,256]{2,1,0:T(8,128)(2,1)S(1)} %get-tuple-element.138), channel_id=1, source_target_pairs={{0,24},{4,28},{8,16},{12,20},{16,8},{20,12},{24,0},{28,4},{1,25},{... | collective-permute-start | bytes 393224 | tf_op jit(solution)/shard_map/ppermute | solution.py:644
  45.9 0.8 collective-permute-start.11
  46.7 3.1 %weight1.4 = (bf16[4,576,128]{2,1,0:T(8,128)(2,1)S(1)}, bf16[4,576,128]{2,1,0:T(8,128)(2,1)S(1)}) custom-call(s32[2]{0:T(128)S(1)} %copy-done.3, bf16[512,512]{1,0:T(8,128)(2,1)S(1)} %get-tuple-element.130.act_t, bf16[2,256,512]{2,1,0:T(8,128)(2,1)S(1)} %collective-permute-done.6.half_t, bf16[2,256,512]{2,1,0:T(8,128)(2,1)S(1)} %collective-permute-done.7.partner_half_t, ...), custom_call_target="tpu_custom_call" | custom-call | flops 3221225472 | bytes 1024 | tf_op jit(solution)/shard_map/weight1/pallas_call | solution.py:586
  49.7 1.4 %collective-permute-start.17 = (bf16[4,576,128]{2,1,0:T(8,128)(2,1)S(1)}, bf16[4,576,128]{2,1,0:T(8,128)(2,1)S(1)}, u32[]{:S(2)}, u32[]{:S(2)}) collective-permute-start(bf16[4,576,128]{2,1,0:T(8,128)(2,1)S(1)} %get-tuple-element.141), channel_id=1, source_target_pairs={{0,4},{4,0},{8,12},{12,8},{16,20},{20,16},{24,28},{28,24},{1,5},{5... | collective-permute-start | bytes 1769480 | tf_op jit(solution)/shard_map/ppermute | solution.py:644
  51.2 5.9 %collective-permute-done.12.refs_2_ = bf16[1,256,256]{2,1,0:T(8,128)(2,1)S(1)} collective-permute-done((bf16[1,256,256]{2,1,0:T(8,128)(2,1)S(1)}, bf16[1,256,256]{2,1,0:T(8,128)(2,1)S(1)}, u32[]{:S(2)}, u32[]{:S(2)}) %collective-permute-start.12) | collective-permute-done | bytes 131104 | tf_op jit(solution)/shard_map/ppermute | solution.py:644
  57.1 0.1 sumroutea.1.own_ref
  57.1 0.1 routeb1.1
  57.3 0.1 collective-permute-start.18
  57.4 3.0 %collective-permute-start.19 = (bf16[1,576,128]{2,1,0:T(8,128)(2,1)S(1)}, bf16[1,576,128]{2,1,0:T(8,128)(2,1)S(1)}, u32[]{:S(2)}, u32[]{:S(2)}) collective-permute-start(bf16[1,576,128]{2,1,0:T(8,128)(2,1)S(1)} %get-tuple-element.148), channel_id=1, source_target_pairs={{0,16},{4,20},{8,24},{12,28},{16,0},{20,4},{24,8},{28,12},{1,17},{... | collective-permute-start | bytes 442376 | tf_op jit(solution)/shard_map/ppermute | solution.py:644
  60.4 1.3 %collective-permute-start.20 = (bf16[1,576,128]{2,1,0:T(8,128)(2,1)S(1)}, bf16[1,576,128]{2,1,0:T(8,128)(2,1)S(1)}, u32[]{:S(2)}, u32[]{:S(2)}) collective-permute-start(bf16[1,576,128]{2,1,0:T(8,128)(2,1)S(1)} %get-tuple-element.149), channel_id=1, source_target_pairs={{0,24},{4,28},{8,16},{12,20},{16,8},{20,12},{24,0},{28,4},{1,25},{... | collective-permute-start | bytes 442376 | tf_op jit(solution)/shard_map/ppermute | solution.py:644
  61.8 0.3 collective-permute-start.23
  62.0 5.0 %fourth.1 = (bf16[192,512]{1,0:T(8,128)(2,1)S(1)}, bf16[192,512]{1,0:T(8,128)(2,1)S(1)}, bf16[2,128,512]{2,1,0:T(8,128)(2,1)S(1)}, bf16[4,16,128]{2,1,0:T(8,128)(2,1)S(1)}, bf16[4,16,128]{2,1,0:T(8,128)(2,1)S(1)}) custom-call(s32[2]{0:T(128)S(1)} %copy-done.3, bf16[512,512]{1,0:T(8,128)(2,1)S(1)} %get-tuple-element.150.grad1_ref, ...), custom_call_target="tpu_custom_call" | custom-call | flops 21474836 | bytes 1024 | tf_op jit(solution)/shard_map/fourth/pallas_call | solution.py:586
  67.1 0.1 collective-permute-done.17.got_ref
  67.2 1.5 %collective-permute-start.16 = (bf16[4,16,128]{2,1,0:T(8,128)(2,1)S(1)}, bf16[4,16,128]{2,1,0:T(8,128)(2,1)S(1)}, u32[]{:S(2)}, u32[]{:S(2)}) collective-permute-start(bf16[4,16,128]{2,1,0:T(8,128)(2,1)S(1)} %get-tuple-element.160), channel_id=1, source_target_pairs={{0,4},{4,0},{8,12},{12,8},{16,20},{20,16},{24,28},{28,24},{1,5},{5... | collective-permute-start | bytes 49160 | tf_op jit(solution)/shard_map/ppermute | solution.py:644
  68.7 2.2 %collective-permute-done.16.got_ref = bf16[4,16,128]{2,1,0:T(8,128)(2,1)S(1)} collective-permute-done((bf16[4,16,128]{2,1,0:T(8,128)(2,1)S(1)}, bf16[4,16,128]{2,1,0:T(8,128)(2,1)S(1)}, u32[]{:S(2)}, u32[]{:S(2)}) %collective-permute-start.16) | collective-permute-done | bytes 16416 | tf_op jit(solution)/shard_map/ppermute | solution.py:644
  70.9 2.0 %collective-permute-start.15 = (bf16[2,128,512]{2,1,0:T(8,128)(2,1)S(1)}, bf16[2,128,512]{2,1,0:T(8,128)(2,1)S(1)}, u32[]{:S(2)}, u32[]{:S(2)}) collective-permute-start(bf16[2,128,512]{2,1,0:T(8,128)(2,1)S(1)} %get-tuple-element.158), channel_id=1, source_target_pairs={{0,2},{1,3},{2,0},{3,1},{4,6},{5,7},{6,4},{7,5},{8,10},{9,11},{10,... | collective-permute-start | bytes 786440 | tf_op jit(solution)/shard_map/ppermute | solution.py:641
  72.9 0.1 routec1.1
  73.1 3.4 %collective-permute-start.25 = (bf16[1,592,128]{2,1,0:T(8,128)(2,1)S(1)}, bf16[1,592,128]{2,1,0:T(8,128)(2,1)S(1)}, u32[]{:S(2)}, u32[]{:S(2)}) collective-permute-start(bf16[1,592,128]{2,1,0:T(8,128)(2,1)S(1)} %get-tuple-element.177), channel_id=1, source_target_pairs={{0,24},{4,28},{8,16},{12,20},{16,8},{20,12},{24,0},{28,4},{1,25},{... | collective-permute-start | bytes 454664 | tf_op jit(solution)/shard_map/ppermute | solution.py:644
  76.6 1.0 %collective-permute-start.21 = (bf16[1,592,128]{2,1,0:T(8,128)(2,1)S(1)}, bf16[1,592,128]{2,1,0:T(8,128)(2,1)S(1)}, u32[]{:S(2)}, u32[]{:S(2)}) collective-permute-start(bf16[1,592,128]{2,1,0:T(8,128)(2,1)S(1)} %get-tuple-element.168), channel_id=1, source_target_pairs={{0,8},{4,12},{8,0},{12,4},{16,24},{20,28},{24,16},{28,20},{1,9},{5... | collective-permute-start | bytes 454664 | tf_op jit(solution)/shard_map/ppermute | solution.py:644
  77.6 0.1 sumrouteb.1.own_ref
  77.7 0.1 collective-permute-start.22
  77.8 5.1 %collective-permute-done.22.far_ref = bf16[576,128]{1,0:T(8,128)(2,1)S(1)} collective-permute-done((bf16[576,128]{1,0:T(8,128)(2,1)S(1)}, bf16[576,128]{1,0:T(8,128)(2,1)S(1)}, u32[]{:S(2)}, u32[]{:S(2)}) %collective-permute-start.22) | collective-permute-done | bytes 147488 | tf_op jit(solution)/shard_map/ppermute | solution.py:641
  82.9 5.2 %collective-permute-done.24.refs_2_ = bf16[1,592,128]{2,1,0:T(8,128)(2,1)S(1)} collective-permute-done((bf16[1,592,128]{2,1,0:T(8,128)(2,1)S(1)}, bf16[1,592,128]{2,1,0:T(8,128)(2,1)S(1)}, u32[]{:S(2)}, u32[]{:S(2)}) %collective-permute-start.24) | collective-permute-done | bytes 151584 | tf_op jit(solution)/shard_map/ppermute | solution.py:644
  88.1 0.1 sumroutec.1.own_ref
  88.2 0.3 collective-permute-start.26
  88.6 0.5 collective-permute-start.29
  89.1 0.5 collective-permute-start.31
  89.6 1.5 %unpack.1 = (bf16[2,6,32,512]{3,2,1,0:T(8,128)(2,1)}, bf16[2,6,32,512]{3,2,1,0:T(8,128)(2,1)}) custom-call(s32[2]{0:T(128)S(1)} %copy-done.3, bf16[192,512]{1,0:T(8,128)(2,1)S(1)} %get-tuple-element.156.out_own, bf16[192,512]{1,0:T(8,128)(2,1)S(1)} %get-tuple-element.157.grad_own, bf16[2,128,512]{2,1,0:T(8,128)(2,1)S(1)} %collective-permute-done.15.away_ref), custom_call_target="tpu_custom_call" | custom-call | flops 21474836 | bytes 1024 | tf_op jit(solution)/shard_map/unpack/pallas_call | solution.py:586
  91.1 0.0 collective-permute-start.27
  91.1 0.9 joina.1
  92.0 1.2 %joinb.1 = f32[576,512]{1,0:T(8,128)} custom-call(bf16[576,128]{1,0:T(8,128)(2,1)S(1)} %sumrouteb.1.own_ref, bf16[576,128]{1,0:T(8,128)(2,1)S(1)} %collective-permute-done.22.far_ref, bf16[576,128]{1,0:T(8,128)(2,1)S(1)} %collective-permute-done.28.near_ref, bf16[576,128]{1,0:T(8,128)(2,1)S(1)} %collective-permute-done.29.diagonal_ref), custom_call_target="tpu_custom_call" | custom-call | flops 21474836 | bytes 1024 | tf_op jit(solution)/shard_map/joinb/pallas_call | solution.py:586
  93.2 0.3 collective-permute-done.26.far_ref
  93.5 0.2 collective-permute-start.32
  93.7 1.2 %collective-permute-done.32.diagonal_ref = bf16[592,128]{1,0:T(8,128)(2,1)S(1)} collective-permute-done((bf16[592,128]{1,0:T(8,128)(2,1)S(1)}, bf16[592,128]{1,0:T(8,128)(2,1)S(1)}, u32[]{:S(2)}, u32[]{:S(2)}) %collective-permute-start.32) | collective-permute-done | bytes 151584 | tf_op jit(solution)/shard_map/ppermute | solution.py:638
  94.8 1.2 %joinc.1 = (f32[576,512]{1,0:T(8,128)}, f32[1,64]{1,0:T(1,128)}, f32[1,64]{1,0:T(1,128)}, f32[1,64]{1,0:T(1,128)}, f32[1,64]{1,0:T(1,128)}, /*index=5*/f32[1,64]...) custom-call(bf16[592,128]{1,0:T(8,128)(2,1)S(1)} %sumroutec.1.own_re, ...), custom_call_target="tpu_custom_call" | custom-call | flops 21474836 | bytes 1024 | tf_op jit(solution)/shard_map/joinc/pallas_call | solution.py:586
  (69 shorter events, 0.2 us)
Async XLA Ops:
  0.7 5.1 %copy-start.8 = (f32[512]{0:T(512)S(1)}, f32[512]{0:T(512)}, u32[]{:S(2)}) copy-start(f32[512]{0:T(512)} %param.22) | copy-start | bytes 6148
  0.7 5.1 %copy-start.9 = (f32[512]{0:T(512)S(1)}, f32[512]{0:T(512)}, u32[]{:S(2)}) copy-start(f32[512]{0:T(512)} %param.23) | copy-start | bytes 6148
  0.7 5.1 %copy-start.18 = (f32[512]{0:T(512)S(1)}, f32[512]{0:T(512)}, u32[]{:S(2)}) copy-start(f32[512]{0:T(512)} %param.38) | copy-start | bytes 6148
  0.7 5.1 %copy-start.10 = (f32[512]{0:T(512)S(1)}, f32[512]{0:T(512)}, u32[]{:S(2)}) copy-start(f32[512]{0:T(512)} %param.25) | copy-start | bytes 6148
  0.7 5.1 %copy-start.11 = (f32[512]{0:T(512)S(1)}, f32[512]{0:T(512)}, u32[]{:S(2)}) copy-start(f32[512]{0:T(512)} %param.26) | copy-start | bytes 6148
  0.7 5.1 %copy-start.12 = (f32[512]{0:T(512)S(1)}, f32[512]{0:T(512)}, u32[]{:S(2)}) copy-start(f32[512]{0:T(512)} %param.27) | copy-start | bytes 6148
  0.7 5.1 %copy-start.13 = (f32[512]{0:T(512)S(1)}, f32[512]{0:T(512)}, u32[]{:S(2)}) copy-start(f32[512]{0:T(512)} %param.29) | copy-start | bytes 6148
  0.7 5.1 %copy-start.14 = (f32[512]{0:T(512)S(1)}, f32[512]{0:T(512)}, u32[]{:S(2)}) copy-start(f32[512]{0:T(512)} %param.30) | copy-start | bytes 6148
  0.7 5.1 %copy-start.15 = (f32[512]{0:T(512)S(1)}, f32[512]{0:T(512)}, u32[]{:S(2)}) copy-start(f32[512]{0:T(512)} %param.31) | copy-start | bytes 6148
  0.8 5.1 %copy-start.16 = (f32[512]{0:T(512)S(1)}, f32[512]{0:T(512)}, u32[]{:S(2)}) copy-start(f32[512]{0:T(512)} %param.33) | copy-start | bytes 6148
  0.8 5.1 %copy-start.17 = (f32[512]{0:T(512)S(1)}, f32[512]{0:T(512)}, u32[]{:S(2)}) copy-start(f32[512]{0:T(512)} %param.36) | copy-start | bytes 6148
  0.8 5.1 %copy-start.7 = (bf16[2,6,32,512]{3,2,1,0:T(8,128)(2,1)S(1)}, bf16[2,6,32,512]{3,2,1,0:T(8,128)(2,1)}, u32[]{:S(2)}) copy-start(bf16[2,6,32,512]{3,2,1,0:T(8,128)(2,1)} %cot_ref.1) | copy-start | bytes 1179652
  0.8 10.3 %slice-start = ((s8[4718592]{0:T(1024)(128)(4,1)}), s8[524288]{0:T(1024)(128)(4,1)S(1)}, s32[]{:S(2)}) async-start(s8[4718592]{0:T(1024)(128)(4,1)} %bitcast.22), calls=%async_computation | async-start | bytes 1048576
  0.8 17.5 %slice-start.2 = ((s8[4718592]{0:T(1024)(128)(4,1)}), s8[4194304]{0:T(1024)(128)(4,1)S(1)}, s32[]{:S(2)}) async-start(s8[4718592]{0:T(1024)(128)(4,1)} %bitcast.24), calls=%async_computation.2 | async-start | bytes 8388608
  2.7 6.7 %collective-permute-start.1 = (bf16[128,512]{1,0:T(8,128)(2,1)}, bf16[128,512]{1,0:T(8,128)(2,1)S(1)}, u32[]{:S(2)}, u32[]{:S(2)}) collective-permute-start(bf16[128,512]{1,0:T(8,128)(2,1)} %get-tuple-element.112), channel_id=1, source_target_pairs={{0,2},{1,3},{2,0},{3,1},{4,6},{5,7},{6,4},{7,5},{8,10},{9,11},{10,... | collective-permute-start | bytes 393224 | tf_op jit(solution)/shard_map/ppermute | solution.py:641
  5.8 4.3 %collective-permute-start = (bf16[192,512]{1,0:T(8,128)(2,1)}, bf16[192,512]{1,0:T(8,128)(2,1)S(1)}, u32[]{:S(2)}, u32[]{:S(2)}) collective-permute-start(bf16[192,512]{1,0:T(8,128)(2,1)} %get-tuple-element.111.own), channel_id=1, source_target_pairs={{0,1},{1,0},{2,3},{3,2},{4,5},{5,4},{6,7},{7,6},{8,9},{9,8},{10,11... | collective-permute-start | bytes 589832 | tf_op jit(solution)/shard_map/ppermute | solution.py:638
  5.8 5.3 %slice-start.1 = ((s8[4718592]{0:T(1024)(128)(4,1)}), s8[4194304]{0:T(1024)(128)(4,1)S(1)}, s32[]{:S(2)}) async-start(s8[4718592]{0:T(1024)(128)(4,1)} %bitcast.22), calls=%async_computation.1 | async-start | bytes 8388608
  5.9 0.8 copy-start.2
  6.7 4.4 %copy-start.1 = (bf16[192,512]{1,0:T(8,128)(2,1)S(1)}, bf16[192,512]{1,0:T(8,128)(2,1)}, u32[]{:S(2)}) copy-start(bf16[192,512]{1,0:T(8,128)(2,1)} %get-tuple-element.111.own) | copy-start | bytes 589828
  6.7 4.4 %copy-start.3 = (s32[2]{0:T(128)S(1)}, s32[2]{0:T(128)}, u32[]{:S(2)}) copy-start(s32[2]{0:T(128)} %get-tuple-element.110.kinds.bucket_ref) | copy-start | bytes 28
  6.7 11.6 %slice-start.3 = ((s8[4718592]{0:T(1024)(128)(4,1)}), s8[524288]{0:T(1024)(128)(4,1)S(1)}, s32[]{:S(2)}) async-start(s8[4718592]{0:T(1024)(128)(4,1)} %bitcast.24), calls=%async_computation.3 | async-start | bytes 1048576
  7.3 11.1 %copy-start = (bf16[512,512]{1,0:T(8,128)(2,1)S(1)}, bf16[512,512]{1,0:T(8,128)(2,1)}, u32[]{:S(2)}) copy-start(bf16[512,512]{1,0:T(8,128)(2,1)} %wp.3) | copy-start | bytes 1572868
  7.3 11.0 %copy-start.4 = (bf16[512,512]{1,0:T(8,128)(2,1)S(1)}, bf16[512,512]{1,0:T(8,128)(2,1)}, u32[]{:S(2)}) copy-start(bf16[512,512]{1,0:T(8,128)(2,1)} %wq.1) | copy-start | bytes 1572868
  7.3 11.0 %copy-start.5 = (bf16[512,512]{1,0:T(8,128)(2,1)S(1)}, bf16[512,512]{1,0:T(8,128)(2,1)}, u32[]{:S(2)}) copy-start(bf16[512,512]{1,0:T(8,128)(2,1)} %wk.1) | copy-start | bytes 1572868
  7.3 11.0 %copy-start.6 = (bf16[512,512]{1,0:T(8,128)(2,1)S(1)}, bf16[512,512]{1,0:T(8,128)(2,1)}, u32[]{:S(2)}) copy-start(bf16[512,512]{1,0:T(8,128)(2,1)} %wv.1) | copy-start | bytes 1572868
  7.3 11.0 %collective-permute-start.3 = (bf16[192,512]{1,0:T(8,128)(2,1)S(1)}, bf16[192,512]{1,0:T(8,128)(2,1)S(1)}, u32[]{:S(2)}, u32[]{:S(2)}) collective-permute-start(bf16[192,512]{1,0:T(8,128)(2,1)S(1)} %get-tuple-element.117.own), channel_id=1, source_target_pairs={{0,1},{1,0},{2,3},{3,2},{4,5},{5,4},{6,7},{7,6},{8,9},{9,8},{10,11... | collective-permute-start | bytes 589832 | tf_op jit(solution)/shard_map/ppermute | solution.py:638
  7.9 10.4 %collective-permute-start.4 = (bf16[160,512]{1,0:T(8,128)(2,1)S(1)}, bf16[160,512]{1,0:T(8,128)(2,1)S(1)}, u32[]{:S(2)}, u32[]{:S(2)}) collective-permute-start(bf16[160,512]{1,0:T(8,128)(2,1)S(1)} %get-tuple-element.118), channel_id=1, source_target_pairs={{0,2},{1,3},{2,0},{3,1},{4,6},{5,7},{6,4},{7,5},{8,10},{9,11},{10,... | collective-permute-start | bytes 491528 | tf_op jit(solution)/shard_map/ppermute | solution.py:641
  8.0 10.3 %collective-permute-start.5 = (bf16[160,512]{1,0:T(8,128)(2,1)S(1)}, bf16[160,512]{1,0:T(8,128)(2,1)S(1)}, u32[]{:S(2)}, u32[]{:S(2)}) collective-permute-start(bf16[160,512]{1,0:T(8,128)(2,1)S(1)} %get-tuple-element.118), channel_id=1, source_target_pairs={{0,3},{1,2},{2,1},{3,0},{4,7},{5,6},{6,5},{7,4},{8,11},{9,10},{10,... | collective-permute-start | bytes 491528 | tf_op jit(solution)/shard_map/ppermute | solution.py:674
  9.5 1.6 %collective-permute-start.2 = (bf16[128,512]{1,0:T(8,128)(2,1)S(1)}, bf16[128,512]{1,0:T(8,128)(2,1)S(1)}, u32[]{:S(2)}, u32[]{:S(2)}) collective-permute-start(bf16[128,512]{1,0:T(8,128)(2,1)S(1)} %collective-permute-done.1.received), channel_id=1, source_target_pairs={{0,1},{1,0},{2,3},{3,2},{4,5},{5,4},{6,7},{7,6},{8,9},{9,8},{10,11... | collective-permute-start | bytes 393224 | tf_op jit(solution)/shard_map/ppermute | solution.py:638
  16.4 14.4 %collective-permute-start.6 = (bf16[2,256,512]{2,1,0:T(8,128)(2,1)S(1)}, bf16[2,256,512]{2,1,0:T(8,128)(2,1)S(1)}, u32[]{:S(2)}, u32[]{:S(2)}) collective-permute-start(bf16[2,256,512]{2,1,0:T(8,128)(2,1)S(1)} %get-tuple-element.124), channel_id=1, source_target_pairs={{0,2},{1,3},{2,0},{3,1},{4,6},{5,7},{6,4},{7,5},{8,10},{9,11},{10,... | collective-permute-start | bytes 1572872 | tf_op jit(solution)/shard_map/ppermute | solution.py:641
  28.0 7.2 %collective-permute-start.8 = (bf16[512,128]{1,0:T(8,128)(2,1)S(1)}, bf16[512,128]{1,0:T(8,128)(2,1)S(1)}, u32[]{:S(2)}, u32[]{:S(2)}) collective-permute-start(bf16[512,128]{1,0:T(8,128)(2,1)S(1)} %get-tuple-element.128), channel_id=1, source_target_pairs={{0,2},{1,3},{2,0},{3,1},{4,6},{5,7},{6,4},{7,5},{8,10},{9,11},{10,... | collective-permute-start | bytes 393224 | tf_op jit(solution)/shard_map/ppermute | solution.py:641
  28.3 13.8 %collective-permute-start.9 = (bf16[4,256,256]{2,1,0:T(8,128)(2,1)S(1)}, bf16[4,256,256]{2,1,0:T(8,128)(2,1)S(1)}, u32[]{:S(2)}, u32[]{:S(2)}) collective-permute-start(bf16[4,256,256]{2,1,0:T(8,128)(2,1)S(1)} %get-tuple-element.134), channel_id=1, source_target_pairs={{0,4},{4,0},{8,12},{12,8},{16,20},{20,16},{24,28},{28,24},{1,5},{5... | collective-permute-start | bytes 1572872 | tf_op jit(solution)/shard_map/ppermute | solution.py:644
  30.8 4.3 %collective-permute-start.7 = (bf16[2,256,512]{2,1,0:T(8,128)(2,1)S(1)}, bf16[2,256,512]{2,1,0:T(8,128)(2,1)S(1)}, u32[]{:S(2)}, u32[]{:S(2)}) collective-permute-start(bf16[2,256,512]{2,1,0:T(8,128)(2,1)S(1)} %collective-permute-done.6.half_t), channel_id=1, source_target_pairs={{0,1},{1,0},{2,3},{3,2},{4,5},{5,4},{6,7},{7,6},{8,9},{9,8},{10,11... | collective-permute-start | bytes 1572872 | tf_op jit(solution)/shard_map/ppermute | solution.py:638
  38.5 18.6 %collective-permute-start.14 = (bf16[4,576,128]{2,1,0:T(8,128)(2,1)S(1)}, bf16[4,576,128]{2,1,0:T(8,128)(2,1)S(1)}, u32[]{:S(2)}, u32[]{:S(2)}) collective-permute-start(bf16[4,576,128]{2,1,0:T(8,128)(2,1)S(1)} %get-tuple-element.132), channel_id=1, source_target_pairs={{0,4},{4,0},{8,12},{12,8},{16,20},{20,16},{24,28},{28,24},{1,5},{5... | collective-permute-start | bytes 1769480 | tf_op jit(solution)/shard_map/ppermute | solution.py:644
  40.3 6.4 %collective-permute-start.10 = (bf16[512,128]{1,0:T(8,128)(2,1)S(1)}, bf16[512,128]{1,0:T(8,128)(2,1)S(1)}, u32[]{:S(2)}, u32[]{:S(2)}) collective-permute-start(bf16[512,128]{1,0:T(8,128)(2,1)S(1)} %get-tuple-element.140), channel_id=1, source_target_pairs={{0,2},{1,3},{2,0},{3,1},{4,6},{5,7},{6,4},{7,5},{8,10},{9,11},{10,... | collective-permute-start | bytes 393224 | tf_op jit(solution)/shard_map/ppermute | solution.py:641
  42.2 9.0 %collective-permute-start.13 = (bf16[1,256,256]{2,1,0:T(8,128)(2,1)S(1)}, bf16[1,256,256]{2,1,0:T(8,128)(2,1)S(1)}, u32[]{:S(2)}, u32[]{:S(2)}) collective-permute-start(bf16[1,256,256]{2,1,0:T(8,128)(2,1)S(1)} %get-tuple-element.138), channel_id=1, source_target_pairs={{0,24},{4,28},{8,16},{12,20},{16,8},{20,12},{24,0},{28,4},{1,25},{... | collective-permute-start | bytes 393224 | tf_op jit(solution)/shard_map/ppermute | solution.py:644
  45.9 11.2 %collective-permute-start.12 = (bf16[1,256,256]{2,1,0:T(8,128)(2,1)S(1)}, bf16[1,256,256]{2,1,0:T(8,128)(2,1)S(1)}, u32[]{:S(2)}, u32[]{:S(2)}) collective-permute-start(bf16[1,256,256]{2,1,0:T(8,128)(2,1)S(1)} %get-tuple-element.137), channel_id=1, source_target_pairs={{0,16},{4,20},{8,24},{12,28},{16,0},{20,4},{24,8},{28,12},{1,17},{... | collective-permute-start | bytes 393224 | tf_op jit(solution)/shard_map/ppermute | solution.py:644
  45.9 11.2 %collective-permute-start.11 = (bf16[1,256,256]{2,1,0:T(8,128)(2,1)S(1)}, bf16[1,256,256]{2,1,0:T(8,128)(2,1)S(1)}, u32[]{:S(2)}, u32[]{:S(2)}) collective-permute-start(bf16[1,256,256]{2,1,0:T(8,128)(2,1)S(1)} %get-tuple-element.136), channel_id=1, source_target_pairs={{0,8},{4,12},{8,0},{12,4},{16,24},{20,28},{24,16},{28,20},{1,9},{5... | collective-permute-start | bytes 393224 | tf_op jit(solution)/shard_map/ppermute | solution.py:644
  49.7 17.4 %collective-permute-start.17 = (bf16[4,576,128]{2,1,0:T(8,128)(2,1)S(1)}, bf16[4,576,128]{2,1,0:T(8,128)(2,1)S(1)}, u32[]{:S(2)}, u32[]{:S(2)}) collective-permute-start(bf16[4,576,128]{2,1,0:T(8,128)(2,1)S(1)} %get-tuple-element.141), channel_id=1, source_target_pairs={{0,4},{4,0},{8,12},{12,8},{16,20},{20,16},{24,28},{28,24},{1,5},{5... | collective-permute-start | bytes 1769480 | tf_op jit(solution)/shard_map/ppermute | solution.py:644
  57.3 15.8 %collective-permute-start.18 = (bf16[1,576,128]{2,1,0:T(8,128)(2,1)S(1)}, bf16[1,576,128]{2,1,0:T(8,128)(2,1)S(1)}, u32[]{:S(2)}, u32[]{:S(2)}) collective-permute-start(bf16[1,576,128]{2,1,0:T(8,128)(2,1)S(1)} %get-tuple-element.147), channel_id=1, source_target_pairs={{0,8},{4,12},{8,0},{12,4},{16,24},{20,28},{24,16},{28,20},{1,9},{5... | collective-permute-start | bytes 442376 | tf_op jit(solution)/shard_map/ppermute | solution.py:644
  57.4 15.7 %collective-permute-start.19 = (bf16[1,576,128]{2,1,0:T(8,128)(2,1)S(1)}, bf16[1,576,128]{2,1,0:T(8,128)(2,1)S(1)}, u32[]{:S(2)}, u32[]{:S(2)}) collective-permute-start(bf16[1,576,128]{2,1,0:T(8,128)(2,1)S(1)} %get-tuple-element.148), channel_id=1, source_target_pairs={{0,16},{4,20},{8,24},{12,28},{16,0},{20,4},{24,8},{28,12},{1,17},{... | collective-permute-start | bytes 442376 | tf_op jit(solution)/shard_map/ppermute | solution.py:644
  60.4 12.7 %collective-permute-start.20 = (bf16[1,576,128]{2,1,0:T(8,128)(2,1)S(1)}, bf16[1,576,128]{2,1,0:T(8,128)(2,1)S(1)}, u32[]{:S(2)}, u32[]{:S(2)}) collective-permute-start(bf16[1,576,128]{2,1,0:T(8,128)(2,1)S(1)} %get-tuple-element.149), channel_id=1, source_target_pairs={{0,24},{4,28},{8,16},{12,20},{16,8},{20,12},{24,0},{28,4},{1,25},{... | collective-permute-start | bytes 442376 | tf_op jit(solution)/shard_map/ppermute | solution.py:644
  61.8 15.9 %collective-permute-start.23 = (bf16[256,256]{1,0:T(8,128)(2,1)S(1)}, bf16[256,256]{1,0:T(8,128)(2,1)S(1)}, u32[]{:S(2)}, u32[]{:S(2)}) collective-permute-start(bf16[256,256]{1,0:T(8,128)(2,1)S(1)} %sumroutea.1.own_ref), channel_id=1, source_target_pairs={{0,2},{1,3},{2,0},{3,1},{4,6},{5,7},{6,4},{7,5},{8,10},{9,11},{10,... | collective-permute-start | bytes 393224 | tf_op jit(solution)/shard_map/ppermute | solution.py:641
  67.2 3.7 %collective-permute-start.16 = (bf16[4,16,128]{2,1,0:T(8,128)(2,1)S(1)}, bf16[4,16,128]{2,1,0:T(8,128)(2,1)S(1)}, u32[]{:S(2)}, u32[]{:S(2)}) collective-permute-start(bf16[4,16,128]{2,1,0:T(8,128)(2,1)S(1)} %get-tuple-element.160), channel_id=1, source_target_pairs={{0,4},{4,0},{8,12},{12,8},{16,20},{20,16},{24,28},{28,24},{1,5},{5... | collective-permute-start | bytes 49160 | tf_op jit(solution)/shard_map/ppermute | solution.py:644
  70.9 18.2 %collective-permute-start.15 = (bf16[2,128,512]{2,1,0:T(8,128)(2,1)S(1)}, bf16[2,128,512]{2,1,0:T(8,128)(2,1)S(1)}, u32[]{:S(2)}, u32[]{:S(2)}) collective-permute-start(bf16[2,128,512]{2,1,0:T(8,128)(2,1)S(1)} %get-tuple-element.158), channel_id=1, source_target_pairs={{0,2},{1,3},{2,0},{3,1},{4,6},{5,7},{6,4},{7,5},{8,10},{9,11},{10,... | collective-permute-start | bytes 786440 | tf_op jit(solution)/shard_map/ppermute | solution.py:641
  73.1 9.8 %collective-permute-start.25 = (bf16[1,592,128]{2,1,0:T(8,128)(2,1)S(1)}, bf16[1,592,128]{2,1,0:T(8,128)(2,1)S(1)}, u32[]{:S(2)}, u32[]{:S(2)}) collective-permute-start(bf16[1,592,128]{2,1,0:T(8,128)(2,1)S(1)} %get-tuple-element.177), channel_id=1, source_target_pairs={{0,24},{4,28},{8,16},{12,20},{16,8},{20,12},{24,0},{28,4},{1,25},{... | collective-permute-start | bytes 454664 | tf_op jit(solution)/shard_map/ppermute | solution.py:644
  76.6 11.6 %collective-permute-start.24 = (bf16[1,592,128]{2,1,0:T(8,128)(2,1)S(1)}, bf16[1,592,128]{2,1,0:T(8,128)(2,1)S(1)}, u32[]{:S(2)}, u32[]{:S(2)}) collective-permute-start(bf16[1,592,128]{2,1,0:T(8,128)(2,1)S(1)} %get-tuple-element.174), channel_id=1, source_target_pairs={{0,16},{4,20},{8,24},{12,28},{16,0},{20,4},{24,8},{28,12},{1,17},{... | collective-permute-start | bytes 454664 | tf_op jit(solution)/shard_map/ppermute | solution.py:644
  76.6 11.6 %collective-permute-start.21 = (bf16[1,592,128]{2,1,0:T(8,128)(2,1)S(1)}, bf16[1,592,128]{2,1,0:T(8,128)(2,1)S(1)}, u32[]{:S(2)}, u32[]{:S(2)}) collective-permute-start(bf16[1,592,128]{2,1,0:T(8,128)(2,1)S(1)} %get-tuple-element.168), channel_id=1, source_target_pairs={{0,8},{4,12},{8,0},{12,4},{16,24},{20,28},{24,16},{28,20},{1,9},{5... | collective-permute-start | bytes 454664 | tf_op jit(solution)/shard_map/ppermute | solution.py:644
  77.7 5.2 %collective-permute-start.22 = (bf16[576,128]{1,0:T(8,128)(2,1)S(1)}, bf16[576,128]{1,0:T(8,128)(2,1)S(1)}, u32[]{:S(2)}, u32[]{:S(2)}) collective-permute-start(bf16[576,128]{1,0:T(8,128)(2,1)S(1)} %sumrouteb.1.own_ref), channel_id=1, source_target_pairs={{0,2},{1,3},{2,0},{3,1},{4,6},{5,7},{6,4},{7,5},{8,10},{9,11},{10,... | collective-permute-start | bytes 442376 | tf_op jit(solution)/shard_map/ppermute | solution.py:641
  88.2 5.3 %collective-permute-start.26 = (bf16[592,128]{1,0:T(8,128)(2,1)S(1)}, bf16[592,128]{1,0:T(8,128)(2,1)S(1)}, u32[]{:S(2)}, u32[]{:S(2)}) collective-permute-start(bf16[592,128]{1,0:T(8,128)(2,1)S(1)} %sumroutec.1.own_ref), channel_id=1, source_target_pairs={{0,2},{1,3},{2,0},{3,1},{4,6},{5,7},{6,4},{7,5},{8,10},{9,11},{10,... | collective-permute-start | bytes 454664 | tf_op jit(solution)/shard_map/ppermute | solution.py:641
  88.6 3.4 %collective-permute-start.28 = (bf16[576,128]{1,0:T(8,128)(2,1)S(1)}, bf16[576,128]{1,0:T(8,128)(2,1)S(1)}, u32[]{:S(2)}, u32[]{:S(2)}) collective-permute-start(bf16[576,128]{1,0:T(8,128)(2,1)S(1)} %sumrouteb.1.own_ref), channel_id=1, source_target_pairs={{0,1},{1,0},{2,3},{3,2},{4,5},{5,4},{6,7},{7,6},{8,9},{9,8},{10,11... | collective-permute-start | bytes 442376 | tf_op jit(solution)/shard_map/ppermute | solution.py:638
  88.6 3.4 %collective-permute-start.29 = (bf16[576,128]{1,0:T(8,128)(2,1)S(1)}, bf16[576,128]{1,0:T(8,128)(2,1)S(1)}, u32[]{:S(2)}, u32[]{:S(2)}) collective-permute-start(bf16[576,128]{1,0:T(8,128)(2,1)S(1)} %collective-permute-done.22.far_ref), channel_id=1, source_target_pairs={{0,1},{1,0},{2,3},{3,2},{4,5},{5,4},{6,7},{7,6},{8,9},{9,8},{10,11... | collective-permute-start | bytes 442376 | tf_op jit(solution)/shard_map/ppermute | solution.py:638
  89.1 2.0 %collective-permute-start.30 = (bf16[256,256]{1,0:T(8,128)(2,1)S(1)}, bf16[256,256]{1,0:T(8,128)(2,1)S(1)}, u32[]{:S(2)}, u32[]{:S(2)}) collective-permute-start(bf16[256,256]{1,0:T(8,128)(2,1)S(1)} %sumroutea.1.own_ref), channel_id=1, source_target_pairs={{0,1},{1,0},{2,3},{3,2},{4,5},{5,4},{6,7},{7,6},{8,9},{9,8},{10,11... | collective-permute-start | bytes 393224 | tf_op jit(solution)/shard_map/ppermute | solution.py:638
  89.1 2.0 %collective-permute-start.31 = (bf16[256,256]{1,0:T(8,128)(2,1)S(1)}, bf16[256,256]{1,0:T(8,128)(2,1)S(1)}, u32[]{:S(2)}, u32[]{:S(2)}) collective-permute-start(bf16[256,256]{1,0:T(8,128)(2,1)S(1)} %collective-permute-done.23.far_ref), channel_id=1, source_target_pairs={{0,1},{1,0},{2,3},{3,2},{4,5},{5,4},{6,7},{7,6},{8,9},{9,8},{10,11... | collective-permute-start | bytes 393224 | tf_op jit(solution)/shard_map/ppermute | solution.py:638
  91.1 2.6 %collective-permute-start.27 = (bf16[592,128]{1,0:T(8,128)(2,1)S(1)}, bf16[592,128]{1,0:T(8,128)(2,1)S(1)}, u32[]{:S(2)}, u32[]{:S(2)}) collective-permute-start(bf16[592,128]{1,0:T(8,128)(2,1)S(1)} %sumroutec.1.own_ref), channel_id=1, source_target_pairs={{0,1},{1,0},{2,3},{3,2},{4,5},{5,4},{6,7},{7,6},{8,9},{9,8},{10,11... | collective-permute-start | bytes 454664 | tf_op jit(solution)/shard_map/ppermute | solution.py:638
  93.5 1.4 %collective-permute-start.32 = (bf16[592,128]{1,0:T(8,128)(2,1)S(1)}, bf16[592,128]{1,0:T(8,128)(2,1)S(1)}, u32[]{:S(2)}, u32[]{:S(2)}) collective-permute-start(bf16[592,128]{1,0:T(8,128)(2,1)S(1)} %collective-permute-done.26.far_ref), channel_id=1, source_target_pairs={{0,1},{1,0},{2,3},{3,2},{4,5},{5,4},{6,7},{7,6},{8,9},{9,8},{10,11... | collective-permute-start | bytes 454664 | tf_op jit(solution)/shard_map/ppermute | solution.py:638
